TPU v7x, 32 devices: a whole 2x2x4 slice. The times are simulated.
32 devices in a mesh: dp: 8 (over y, x, core), tensor: 4 (over z).
Axes of the slice: x: 2, y: 2, z: 4, core: 2. Of those that a mesh axis runs over, the one named last changes fastest.
Arguments:
- queries: bfloat16 [2048, 6144], P(('dp', 'tensor')), may hold values from -24 to 24
- key_vectors: bfloat16 [2048, 6144], P(('dp', 'tensor')), may hold values from -24 to 24
- value_vectors: bfloat16 [2048, 6144], P(('dp', 'tensor')), may hold values from -6 to 6
- grad_output: bfloat16 [2048, 6144], P(('dp', 'tensor')), may hold values from -6 to 6
- image_ids: int32 [2048], replicated, may hold values from 0 to 31, as said below
Outputs:
- attended: bfloat16 [2048, 6144], P('dp', 'tensor')
- grad_queries: bfloat16 [2048, 6144], P('dp', 'tensor')
- grad_keys: bfloat16 [2048, 6144], P('dp', 'tensor')
- grad_values: bfloat16 [2048, 6144], P('dp', 'tensor')
Inputs may be any that keep to these rules, and one draw needn't show every extreme that they name: `image_ids`: A patch's id is the index of its image's last block of 64 rows, so ids never fall along the rows; every image covers whole blocks of 64 rows and lies within one aligned block of 256 rows or two consecutive ones; images have 64 to 384 rows, and both ends are reached in every draw.
All inputs are finite; a program needn't handle non-finite values.
Results may differ from a plain program's by a relative error of at most 0.0068.
Values may be sent and summed in bfloat16 or wider, within the bound.
No kernel may reach another device: no remote copies, remote signals or barrier semaphores. Data moves between devices by JAX's collectives and lax.ppermute only.
A program may use at most 64 MiB of HBM per device.

v0:
```python
import math

import jax
import jax.numpy as jnp
from jax import lax
from jax.sharding import PartitionSpec as P

HD = 128


def from_behind(block, axis, distance):
    devices = range(lax.axis_size(axis))
    route = [(i - distance, i) for i in devices if i - distance in devices]
    return lax.ppermute(block, axis, route)


def split_heads(array, head_count):
    return jnp.transpose(array.reshape(array.shape[0], head_count, HD), (1, 0, 2))


def merge_heads(array):
    return jnp.transpose(array, (1, 0, 2)).reshape(array.shape[1], -1)


def attend(queries, key_vectors, value_vectors, grad_output, query_ids, key_ids):
    head_count = queries.shape[1] // HD
    score_scale = 1.0 / math.sqrt(HD)
    same_image = query_ids[:, None] == key_ids[None, :]

    def one_head(operands):
        query_head, key_head, value_head, grad_head = operands
        scores = jnp.dot(query_head, key_head.T, preferred_element_type=jnp.float32) * score_scale
        scores = jnp.where(same_image, scores, -1e30)
        row_max = jnp.max(scores, axis=1, keepdims=True)
        weights = jnp.exp(scores - row_max)
        probs = weights / jnp.sum(weights, axis=1, keepdims=True)
        probs_low = probs.astype(jnp.bfloat16)
        attended = jnp.dot(probs_low, value_head, preferred_element_type=jnp.float32).astype(
            jnp.bfloat16
        )
        grad_probs = jnp.dot(grad_head, value_head.T, preferred_element_type=jnp.float32)
        inner = jnp.sum(probs * grad_probs, axis=1, keepdims=True)
        grad_scores = (probs * (grad_probs - inner)).astype(jnp.bfloat16)
        grad_query = (
            jnp.dot(grad_scores, key_head, preferred_element_type=jnp.float32) * score_scale
        ).astype(jnp.bfloat16)
        grad_key = (
            jnp.dot(grad_scores.T, query_head, preferred_element_type=jnp.float32) * score_scale
        )
        grad_value = jnp.dot(probs_low.T, grad_head, preferred_element_type=jnp.float32)
        return (attended, grad_query, grad_key, grad_value)

    results = lax.map(
        one_head,
        (
            split_heads(queries, head_count),
            split_heads(key_vectors, head_count),
            split_heads(value_vectors, head_count),
            split_heads(grad_output, head_count),
        ),
    )
    return tuple((merge_heads(result_part) for result_part in results))


def shards(queries, key_vectors, value_vectors, grad_output, image_ids):
    query_rows, key_rows, value_rows, grad_rows = (
        lax.all_to_all(queries, "tensor", split_axis=1, concat_axis=0, tiled=True),
        lax.all_to_all(key_vectors, "tensor", split_axis=1, concat_axis=0, tiled=True),
        lax.all_to_all(value_vectors, "tensor", split_axis=1, concat_axis=0, tiled=True),
        lax.all_to_all(grad_output, "tensor", split_axis=1, concat_axis=0, tiled=True),
    )
    row_count = query_rows.shape[0]
    shard_index = lax.axis_index("dp")
    padded_ids = jnp.pad(image_ids, (row_count, row_count), constant_values=-1)
    nearby_ids = lax.dynamic_slice_in_dim(padded_ids, shard_index * row_count, 3 * row_count)
    own_ids = nearby_ids[row_count : 2 * row_count]
    later = from_behind((query_rows, key_rows, value_rows, grad_rows), "dp", -1)
    next_ids = nearby_ids[2 * row_count :]
    tail_ids = jnp.where(next_ids == own_ids[row_count - 1], next_ids, -2)
    joined_ids = jnp.concatenate((own_ids, tail_ids))
    attended, grad_query, grad_key, grad_value = attend(
        jnp.concatenate((query_rows, later[0])),
        jnp.concatenate((key_rows, later[1])),
        jnp.concatenate((value_rows, later[2])),
        jnp.concatenate((grad_rows, later[3])),
        joined_ids,
        joined_ids,
    )
    grad_key = grad_key.astype(jnp.bfloat16)
    grad_value = grad_value.astype(jnp.bfloat16)
    earlier = from_behind(
        (
            attended[row_count:],
            grad_query[row_count:],
            grad_key[row_count:],
            grad_value[row_count:],
        ),
        "dp",
        1,
    )
    borrowed = ((own_ids == own_ids[0]) & (nearby_ids[row_count - 1] == own_ids[0]))[:, None]
    return (
        jnp.where(borrowed, earlier[0], attended[:row_count]),
        jnp.where(borrowed, earlier[1], grad_query[:row_count]),
        jnp.where(borrowed, earlier[2], grad_key[:row_count]),
        jnp.where(borrowed, earlier[3], grad_value[:row_count]),
    )


def solution(mesh):
    return jax.shard_map(
        shards,
        mesh=mesh,
        in_specs=(
            P(("dp", "tensor"), None),
            P(("dp", "tensor"), None),
            P(("dp", "tensor"), None),
            P(("dp", "tensor"), None),
            P(),
        ),
        out_specs=(P("dp", "tensor"), P("dp", "tensor"), P("dp", "tensor"), P("dp", "tensor")),
        check_vma=False,
    )
```

profile of v0, /device:TPU:3, one launch (start us, length us, event | category | flops | bytes accessed | tf_op | source)
XLA Modules:
  0.0 303.8 jit_solution(3174069633491496927)
XLA Ops:
  0.6 2.1 copy.107
  2.8 4.6 %all-to-all-start.1 = ((bf16[64,4,1536]{2,0,1:T(8,128)(2,1)}), bf16[64,4,1536]{2,0,1:T(8,128)(2,1)}, u32[]{:S(2)}, u32[]{:S(2)}) async-start(bf16[64,4,1536]{2,0,1:T(8,128)(2,1)} %bitcast.102), calls=%async_computation.1 | async-start | bytes 1572864 | tf_op jit(solution)/shard_map/all_to_all | solution.py:68
  8.3 18.8 %all-to-all-done.1 = bf16[64,4,1536]{2,0,1:T(8,128)(2,1)} async-done(((bf16[64,4,1536]{2,0,1:T(8,128)(2,1)}), bf16[64,4,1536]{2,0,1:T(8,128)(2,1)}, u32[]{:S(2)}, u32[]{:S(2)}) %all-to-all-start.1) | async-done | bytes 786464 | tf_op jit(solution)/shard_map/all_to_all | solution.py:68
  27.1 4.2 %all-to-all-start.2 = ((bf16[64,4,1536]{2,0,1:T(8,128)(2,1)}), bf16[64,4,1536]{2,0,1:T(8,128)(2,1)}, u32[]{:S(2)}, u32[]{:S(2)}) async-start(bf16[64,4,1536]{2,0,1:T(8,128)(2,1)} %bitcast.101), calls=%async_computation.2 | async-start | bytes 1572864 | tf_op jit(solution)/shard_map/all_to_all | solution.py:69
  32.3 18.7 %all-to-all-done.2 = bf16[64,4,1536]{2,0,1:T(8,128)(2,1)} async-done(((bf16[64,4,1536]{2,0,1:T(8,128)(2,1)}), bf16[64,4,1536]{2,0,1:T(8,128)(2,1)}, u32[]{:S(2)}, u32[]{:S(2)}) %all-to-all-start.2) | async-done | bytes 786464 | tf_op jit(solution)/shard_map/all_to_all | solution.py:69
  51.0 4.2 %all-to-all-start.3 = ((bf16[64,4,1536]{2,0,1:T(8,128)(2,1)}), bf16[64,4,1536]{2,0,1:T(8,128)(2,1)}, u32[]{:S(2)}, u32[]{:S(2)}) async-start(bf16[64,4,1536]{2,0,1:T(8,128)(2,1)} %bitcast.100), calls=%async_computation.3 | async-start | bytes 1572864 | tf_op jit(solution)/shard_map/all_to_all | solution.py:70
  56.1 18.7 %all-to-all-done.3 = bf16[64,4,1536]{2,0,1:T(8,128)(2,1)} async-done(((bf16[64,4,1536]{2,0,1:T(8,128)(2,1)}), bf16[64,4,1536]{2,0,1:T(8,128)(2,1)}, u32[]{:S(2)}, u32[]{:S(2)}) %all-to-all-start.3) | async-done | bytes 786464 | tf_op jit(solution)/shard_map/all_to_all | solution.py:70
  74.8 4.2 %all-to-all-start = ((bf16[64,4,1536]{2,0,1:T(8,128)(2,1)}), bf16[64,4,1536]{2,0,1:T(8,128)(2,1)}, u32[]{:S(2)}, u32[]{:S(2)}) async-start(bf16[64,4,1536]{2,0,1:T(8,128)(2,1)} %bitcast.103), calls=%async_computation | async-start | bytes 1572864 | tf_op jit(solution)/shard_map/all_to_all | solution.py:67
  79.0 3.4 %collective-permute-start.3 = (bf16[256,1536]{1,0:T(8,128)(2,1)}, bf16[256,1536]{1,0:T(8,128)(2,1)}, u32[]{:S(2)}, u32[]{:S(2)}) collective-permute-start(bf16[256,1536]{1,0:T(8,128)(2,1)} %bitcast.15), channel_id=1, source_target_pairs={{4,0},{8,4},{12,8},{16,12},{20,16},{24,20},{28,24},{5,1},{9,5},{13... | collective-permute-start | bytes 2359304 | tf_op jit(solution)/shard_map/ppermute | solution.py:14
  84.4 2.5 collective-permute-start.1
  86.9 11.8 %all-to-all-done = bf16[64,4,1536]{2,0,1:T(8,128)(2,1)} async-done(((bf16[64,4,1536]{2,0,1:T(8,128)(2,1)}), bf16[64,4,1536]{2,0,1:T(8,128)(2,1)}, u32[]{:S(2)}, u32[]{:S(2)}) %all-to-all-start) | async-done | bytes 786464 | tf_op jit(solution)/shard_map/all_to_all | solution.py:67
  98.7 3.4 %collective-permute-start = (bf16[256,1536]{1,0:T(8,128)(2,1)}, bf16[256,1536]{1,0:T(8,128)(2,1)}, u32[]{:S(2)}, u32[]{:S(2)}) collective-permute-start(bf16[256,1536]{1,0:T(8,128)(2,1)} %bitcast.3), channel_id=1, source_target_pairs={{4,0},{8,4},{12,8},{16,12},{20,16},{24,20},{28,24},{5,1},{9,5},{13... | collective-permute-start | bytes 2359304 | tf_op jit(solution)/shard_map/ppermute | solution.py:14
  103.5 2.4 concatenate.45
  110.9 2.3 copy.75
  113.1 2.6 copy.76
  115.7 2.3 copy.72
  118.0 2.6 copy.73
  120.6 2.3 copy.69
  122.9 2.6 copy.70
  125.5 2.3 copy.66
  127.8 2.6 copy.67
  139.3 114.2 %while.17 = (s32[]{:T(128)}, bf16[12,512,128]{1,2,0:T(8,128)(2,1)}, bf16[12,512,128]{1,2,0:T(8,128)(2,1)}, bf16[12,512,128]{1,2,0:T(8,128)(2,1)}, bf16[12,512,12...) while((s32[]{:T(128)}, bf16[12,512,128]{1,2,0:T(8,128)(2,1)}, ...), condition=%wide.region_4.5_spmd.clone, body=%wide.region_0.4_spmd.clone.sunk | while | flops 408484352 | bytes 13272201 | solution.py:53
  202.5 1.9 fusion.73
  253.5 2.8 fusion.41
  257.6 3.1 %collective-permute-start.7 = (bf16[256,1536]{0,1:T(8,128)(2,1)}, bf16[256,1536]{0,1:T(8,128)(2,1)S(1)}, u32[]{:S(2)}, u32[]{:S(2)}) collective-permute-start(bf16[256,1536]{0,1:T(8,128)(2,1)} %bitcast.29), channel_id=1, source_target_pairs={{0,4},{4,8},{8,12},{12,16},{16,20},{20,24},{24,28},{1,5},{5,9},{9,... | collective-permute-start | bytes 2359304 | tf_op jit(solution)/shard_map/ppermute | solution.py:14
  260.7 2.3 collective-permute-start.4
  264.4 3.0 %collective-permute-start.5 = (bf16[256,1536]{0,1:T(8,128)(2,1)}, bf16[256,1536]{0,1:T(8,128)(2,1)S(1)}, u32[]{:S(2)}, u32[]{:S(2)}) collective-permute-start(bf16[256,1536]{0,1:T(8,128)(2,1)} %bitcast.23), channel_id=1, source_target_pairs={{0,4},{4,8},{8,12},{12,16},{16,20},{20,24},{24,28},{1,5},{5,9},{9,... | collective-permute-start | bytes 2359304 | tf_op jit(solution)/shard_map/ppermute | solution.py:14
  268.8 3.2 %collective-permute-start.6 = (bf16[256,1536]{0,1:T(8,128)(2,1)}, bf16[256,1536]{0,1:T(8,128)(2,1)S(1)}, u32[]{:S(2)}, u32[]{:S(2)}) collective-permute-start(bf16[256,1536]{0,1:T(8,128)(2,1)} %bitcast.26), channel_id=1, source_target_pairs={{0,4},{4,8},{8,12},{12,16},{16,20},{20,24},{24,28},{1,5},{5,9},{9,... | collective-permute-start | bytes 2359304 | tf_op jit(solution)/shard_map/ppermute | solution.py:14
  273.8 4.6 %collective-permute-done.4 = bf16[256,1536]{0,1:T(8,128)(2,1)S(1)} collective-permute-done((bf16[256,1536]{0,1:T(8,128)(2,1)}, bf16[256,1536]{0,1:T(8,128)(2,1)S(1)}, u32[]{:S(2)}, u32[]{:S(2)}) %collective-permute-start.4) | collective-permute-done | bytes 786464 | tf_op jit(solution)/shard_map/ppermute | solution.py:14
  278.4 8.4 %collective-permute-done.5 = bf16[256,1536]{0,1:T(8,128)(2,1)S(1)} collective-permute-done((bf16[256,1536]{0,1:T(8,128)(2,1)}, bf16[256,1536]{0,1:T(8,128)(2,1)S(1)}, u32[]{:S(2)}, u32[]{:S(2)}) %collective-permute-start.5) | collective-permute-done | bytes 786464 | tf_op jit(solution)/shard_map/ppermute | solution.py:14
  286.8 8.4 %collective-permute-done.6 = bf16[256,1536]{0,1:T(8,128)(2,1)S(1)} collective-permute-done((bf16[256,1536]{0,1:T(8,128)(2,1)}, bf16[256,1536]{0,1:T(8,128)(2,1)S(1)}, u32[]{:S(2)}, u32[]{:S(2)}) %collective-permute-start.6) | collective-permute-done | bytes 786464 | tf_op jit(solution)/shard_map/ppermute | solution.py:14
  296.1 3.1 %bitcast_select_fusion = (bf16[256,1536]{0,1:T(8,128)(2,1)S(1)}, bf16[256,1536]{0,1:T(8,128)(2,1)S(1)}, bf16[256,1536]{0,1:T(8,128)(2,1)S(1)}, bf16[256,1536]{0,1:T(8,128)(2,1)S(1)}) fusion(bf16[256,1536]{0,1:T(8,128)(2,1)} %copy-done.6, bf16[256,12,128]{0,2,1:T(8,128)(2,1)} %get-tuple-element.154, pred[256]{0:T(512)(128)(4,1)S(1)} %compare_and_fusion, ...), kind=kLoop, calls=%fused_computation.55 | loop fusion | flops 1572864 | bytes 9437440 | tf_op jit(solution)/shard_map/jit(_where)/select_n | solution.py:106
  (219 shorter events, 141.6 us)
Async XLA Ops:
  0.6 6.8 %copy-start.10 = (bf16[64,6144]{1,0:T(8,128)(2,1)S(1)}, bf16[64,6144]{1,0:T(8,128)(2,1)}, u32[]{:S(2)}) copy-start(bf16[64,6144]{1,0:T(8,128)(2,1)} %param.9) | copy-start | bytes 2359300
  2.8 24.3 %all-to-all-start.1 = ((bf16[64,4,1536]{2,0,1:T(8,128)(2,1)}), bf16[64,4,1536]{2,0,1:T(8,128)(2,1)}, u32[]{:S(2)}, u32[]{:S(2)}) async-start(bf16[64,4,1536]{2,0,1:T(8,128)(2,1)} %bitcast.102), calls=%async_computation.1 | async-start | bytes 1572864 | tf_op jit(solution)/shard_map/all_to_all | solution.py:68
  7.4 23.9 %copy-start.11 = (bf16[64,6144]{1,0:T(8,128)(2,1)S(1)}, bf16[64,6144]{1,0:T(8,128)(2,1)}, u32[]{:S(2)}) copy-start(bf16[64,6144]{1,0:T(8,128)(2,1)} %param.10) | copy-start | bytes 2359300
  27.1 23.9 %all-to-all-start.2 = ((bf16[64,4,1536]{2,0,1:T(8,128)(2,1)}), bf16[64,4,1536]{2,0,1:T(8,128)(2,1)}, u32[]{:S(2)}, u32[]{:S(2)}) async-start(bf16[64,4,1536]{2,0,1:T(8,128)(2,1)} %bitcast.101), calls=%async_computation.2 | async-start | bytes 1572864 | tf_op jit(solution)/shard_map/all_to_all | solution.py:69
  31.3 23.9 %copy-start.12 = (bf16[64,6144]{1,0:T(8,128)(2,1)S(1)}, bf16[64,6144]{1,0:T(8,128)(2,1)}, u32[]{:S(2)}) copy-start(bf16[64,6144]{1,0:T(8,128)(2,1)} %param.7) | copy-start | bytes 2359300
  51.0 23.9 %all-to-all-start.3 = ((bf16[64,4,1536]{2,0,1:T(8,128)(2,1)}), bf16[64,4,1536]{2,0,1:T(8,128)(2,1)}, u32[]{:S(2)}, u32[]{:S(2)}) async-start(bf16[64,4,1536]{2,0,1:T(8,128)(2,1)} %bitcast.100), calls=%async_computation.3 | async-start | bytes 1572864 | tf_op jit(solution)/shard_map/all_to_all | solution.py:70
  55.2 46.9 %copy-start.13 = (s32[2048]{0:T(1024)S(1)}, s32[2048]{0:T(1024)}, u32[]{:S(2)}) copy-start(s32[2048]{0:T(1024)} %param.11) | copy-start | bytes 24580
  74.8 23.9 %all-to-all-start = ((bf16[64,4,1536]{2,0,1:T(8,128)(2,1)}), bf16[64,4,1536]{2,0,1:T(8,128)(2,1)}, u32[]{:S(2)}, u32[]{:S(2)}) async-start(bf16[64,4,1536]{2,0,1:T(8,128)(2,1)} %bitcast.103), calls=%async_computation | async-start | bytes 1572864 | tf_op jit(solution)/shard_map/all_to_all | solution.py:67
  79.0 31.8 %collective-permute-start.3 = (bf16[256,1536]{1,0:T(8,128)(2,1)}, bf16[256,1536]{1,0:T(8,128)(2,1)}, u32[]{:S(2)}, u32[]{:S(2)}) collective-permute-start(bf16[256,1536]{1,0:T(8,128)(2,1)} %bitcast.15), channel_id=1, source_target_pairs={{4,0},{8,4},{12,8},{16,12},{20,16},{24,20},{28,24},{5,1},{9,5},{13... | collective-permute-start | bytes 2359304 | tf_op jit(solution)/shard_map/ppermute | solution.py:14
  82.4 33.3 %collective-permute-start.2 = (bf16[256,1536]{1,0:T(8,128)(2,1)}, bf16[256,1536]{1,0:T(8,128)(2,1)}, u32[]{:S(2)}, u32[]{:S(2)}) collective-permute-start(bf16[256,1536]{1,0:T(8,128)(2,1)} %bitcast.11), channel_id=1, source_target_pairs={{4,0},{8,4},{12,8},{16,12},{20,16},{24,20},{28,24},{5,1},{9,5},{13... | collective-permute-start | bytes 2359304 | tf_op jit(solution)/shard_map/ppermute | solution.py:14
  84.4 36.3 %collective-permute-start.1 = (bf16[256,1536]{1,0:T(8,128)(2,1)}, bf16[256,1536]{1,0:T(8,128)(2,1)}, u32[]{:S(2)}, u32[]{:S(2)}) collective-permute-start(bf16[256,1536]{1,0:T(8,128)(2,1)} %bitcast.7), channel_id=1, source_target_pairs={{4,0},{8,4},{12,8},{16,12},{20,16},{24,20},{28,24},{5,1},{9,5},{13... | collective-permute-start | bytes 2359304 | tf_op jit(solution)/shard_map/ppermute | solution.py:14
  98.7 26.8 %collective-permute-start = (bf16[256,1536]{1,0:T(8,128)(2,1)}, bf16[256,1536]{1,0:T(8,128)(2,1)}, u32[]{:S(2)}, u32[]{:S(2)}) collective-permute-start(bf16[256,1536]{1,0:T(8,128)(2,1)} %bitcast.3), channel_id=1, source_target_pairs={{4,0},{8,4},{12,8},{16,12},{20,16},{24,20},{28,24},{5,1},{9,5},{13... | collective-permute-start | bytes 2359304 | tf_op jit(solution)/shard_map/ppermute | solution.py:14
  132.3 1.6 copy-start
  134.2 1.6 copy-start.1
  136.1 1.2 copy-start.2
  253.5 2.8 copy-start.3
  256.3 6.8 %copy-start.5 = (bf16[12,512,128]{1,2,0:T(8,128)(2,1)S(1)}, bf16[12,512,128]{1,2,0:T(8,128)(2,1)}, u32[]{:S(2)}) copy-start(bf16[12,512,128]{1,2,0:T(8,128)(2,1)} %get-tuple-element.60) | copy-start | bytes 4718596
  257.6 16.1 %collective-permute-start.7 = (bf16[256,1536]{0,1:T(8,128)(2,1)}, bf16[256,1536]{0,1:T(8,128)(2,1)S(1)}, u32[]{:S(2)}, u32[]{:S(2)}) collective-permute-start(bf16[256,1536]{0,1:T(8,128)(2,1)} %bitcast.29), channel_id=1, source_target_pairs={{0,4},{4,8},{8,12},{12,16},{16,20},{20,24},{24,28},{1,5},{5,9},{9,... | collective-permute-start | bytes 2359304 | tf_op jit(solution)/shard_map/ppermute | solution.py:14
  260.7 17.7 %collective-permute-start.4 = (bf16[256,1536]{0,1:T(8,128)(2,1)}, bf16[256,1536]{0,1:T(8,128)(2,1)S(1)}, u32[]{:S(2)}, u32[]{:S(2)}) collective-permute-start(bf16[256,1536]{0,1:T(8,128)(2,1)} %bitcast.20), channel_id=1, source_target_pairs={{0,4},{4,8},{8,12},{12,16},{16,20},{20,24},{24,28},{1,5},{5,9},{9,... | collective-permute-start | bytes 2359304 | tf_op jit(solution)/shard_map/ppermute | solution.py:14
  263.1 4.4 %copy-start.4 = (bf16[12,512,128]{1,2,0:T(8,128)(2,1)S(1)}, bf16[12,512,128]{1,2,0:T(8,128)(2,1)}, u32[]{:S(2)}) copy-start(bf16[12,512,128]{1,2,0:T(8,128)(2,1)} %get-tuple-element.61) | copy-start | bytes 4718596
  264.4 22.4 %collective-permute-start.5 = (bf16[256,1536]{0,1:T(8,128)(2,1)}, bf16[256,1536]{0,1:T(8,128)(2,1)S(1)}, u32[]{:S(2)}, u32[]{:S(2)}) collective-permute-start(bf16[256,1536]{0,1:T(8,128)(2,1)} %bitcast.23), channel_id=1, source_target_pairs={{0,4},{4,8},{8,12},{12,16},{16,20},{20,24},{24,28},{1,5},{5,9},{9,... | collective-permute-start | bytes 2359304 | tf_op jit(solution)/shard_map/ppermute | solution.py:14
  268.8 26.4 %collective-permute-start.6 = (bf16[256,1536]{0,1:T(8,128)(2,1)}, bf16[256,1536]{0,1:T(8,128)(2,1)S(1)}, u32[]{:S(2)}, u32[]{:S(2)}) collective-permute-start(bf16[256,1536]{0,1:T(8,128)(2,1)} %bitcast.26), channel_id=1, source_target_pairs={{0,4},{4,8},{8,12},{12,16},{16,20},{20,24},{24,28},{1,5},{5,9},{9,... | collective-permute-start | bytes 2359304 | tf_op jit(solution)/shard_map/ppermute | solution.py:14
  273.8 21.5 %copy-start.6 = (bf16[256,1536]{0,1:T(8,128)(2,1)}, bf16[256,1536]{0,1:T(8,128)(2,1)S(1)}, u32[]{:S(2)}) copy-start(bf16[256,1536]{0,1:T(8,128)(2,1)S(1)} %collective-permute-done.7) | copy-start | bytes 2359300
  278.4 16.9 %copy-start.7 = (bf16[256,1536]{0,1:T(8,128)(2,1)}, bf16[256,1536]{0,1:T(8,128)(2,1)S(1)}, u32[]{:S(2)}) copy-start(bf16[256,1536]{0,1:T(8,128)(2,1)S(1)} %collective-permute-done.4) | copy-start | bytes 2359300
  286.8 8.4 %copy-start.8 = (bf16[256,1536]{0,1:T(8,128)(2,1)}, bf16[256,1536]{0,1:T(8,128)(2,1)S(1)}, u32[]{:S(2)}) copy-start(bf16[256,1536]{0,1:T(8,128)(2,1)S(1)} %collective-permute-done.5) | copy-start | bytes 2359300
  295.2 0.9 copy-start.9
where the time goes:
time: 307 us; the launch traced here: 304 us
  waiting for transfers between devices  89.4 us (29%)
  matrix products  87.1 us (28%)
  local copies, waits for them, and re-layouts  71.6 us (23%)
  starting transfers between devices  40 us (13%)
  other arithmetic  12.9 us (4%)
    dot_general x12, matrix products, one_head(): jnp.dot(probs_low.T, grad_head, preferred_element_type=jnp.float32)  23 us
    ppermute x8, starting transfers between devices, from_behind(): return lax.ppermute(block, axis, route)  22.9 us
    ppermute x8, waiting for transfers between devices, from_behind(): return lax.ppermute(block, axis, route)  21.4 us
    dynamic_update_slice x60, local copies, waits for them, and re-layouts, attend(): lax.map(one_head, (split_heads(queries, head_count), split_heads(key_vect...  20.8 us
    all_to_all x1, waiting for transfers between devices, shards(): lax.all_to_all(key_vectors, 'tensor', split_axis=1, concat_axis=0, tiled=...  18.8 us
    all_to_all x1, waiting for transfers between devices, shards(): lax.all_to_all(value_vectors, 'tensor', split_axis=1, concat_axis=0, tile...  18.7 us
    all_to_all x1, waiting for transfers between devices, shards(): lax.all_to_all(grad_output, 'tensor', split_axis=1, concat_axis=0, tiled=...  18.7 us
    dot_general x12, matrix products, one_head(): jnp.dot(grad_head, value_head.T, preferred_element_type=jnp.float32)  15.4 us
  transfers between devices with their start and end apart: 12, of which 7 were waited for; matrix products, arithmetic and copies ran while one was open for 10% of the time, Pallas kernels for 0%

commit v1 on v0

v1 whole, which is shorter than its diff:
```python
import functools
import math

import jax
import jax.numpy as jnp
from jax import lax
from jax.experimental import pallas as pl
from jax.experimental.pallas import tpu as pltpu
from jax.sharding import PartitionSpec as P

HD = 128
SCALE = 1.0 / math.sqrt(HD)
EXP2_SCALE = SCALE * math.log2(math.e)
MASKED = -1e30
CHUNK_SHARES = (4, 4, 4)
VMEM_LIMIT = 48 * 1024 * 1024


def split_counts(total, shares):
    whole = sum(shares)
    edges = [round(total * sum(shares[:i]) / whole) for i in range(len(shares) + 1)]
    return [(a, b - a) for a, b in zip(edges[:-1], edges[1:]) if b > a]


def shift(block, axis, distance):
    count = lax.axis_size(axis)
    route = [(i, i + distance) for i in range(count) if 0 <= i + distance < count]
    return lax.ppermute(block, axis, route)


def pack_kernel(parts, first, width, stride, *refs):
    arrays, packed, sems = refs[:4], refs[4], refs[5]
    copies = []
    for part in range(parts):
        for index, array in enumerate(arrays):
            copy = pltpu.make_async_copy(
                array.at[:, pl.ds(part * stride + first, width)],
                packed.at[part, index],
                sems.at[part * 4 + index],
            )
            copy.start()
            copies.append(copy)
    for copy in copies:
        copy.wait()


def pack(arrays, parts, first, width):
    rows, total = arrays[0].shape
    return pl.pallas_call(
        functools.partial(pack_kernel, parts, first, width, total // parts),
        out_shape=jax.ShapeDtypeStruct((parts, 4, rows, width), jnp.bfloat16),
        in_specs=[pl.BlockSpec(memory_space=pl.ANY)] * 4,
        out_specs=pl.BlockSpec(memory_space=pl.ANY),
        scratch_shapes=[pltpu.SemaphoreType.DMA((parts * 4,))],
        cost_estimate=pl.CostEstimate(
            flops=0, bytes_accessed=parts * 16 * rows * width, transcendentals=0
        ),
    )(*arrays)


def dot_nt(a, b):
    return lax.dot_general(a, b, (((1,), (1,)), ((), ())), preferred_element_type=jnp.float32)


def dot_tn(a, b):
    return lax.dot_general(a, b, (((0,), (0,)), ((), ())), preferred_element_type=jnp.float32)


def dot_nn(a, b):
    return jnp.dot(a, b, preferred_element_type=jnp.float32)


def probs_and_grads(queries, grads, keys, values, bias):
    scores = dot_nt(queries, keys) + bias
    row_max = jnp.max(scores, axis=1, keepdims=True)
    weights = jnp.exp2((scores - row_max) * EXP2_SCALE)
    probs = weights * (1.0 / jnp.sum(weights, axis=1, keepdims=True))
    grad_probs = dot_nt(grads, values)
    inner = jnp.sum(probs * grad_probs, axis=1, keepdims=True)
    grad_scores = probs * (grad_probs - inner)
    return probs.astype(jnp.bfloat16), grad_scores.astype(jnp.bfloat16)


def attend_kernel(rows, has_outs, *refs):
    row_ids, col_ids, own, left, right = refs[:5]
    refs = refs[5 + (4 if has_outs else 0) :]
    attended, grad_q, grad_k, grad_v, bias_own, bias_left, bias_right = refs

    @pl.when(pl.program_id(0) == 0)
    def _():
        def bias(row_start, col_start, col_count):
            same = (
                row_ids[row_start : row_start + rows, :]
                == col_ids[:, col_start : col_start + col_count]
            )
            return jnp.where(same, 0.0, MASKED)

        bias_own[...] = bias(rows, 0, 3 * rows)
        bias_left[...] = bias(0, 0, 2 * rows)
        bias_right[...] = bias(2 * rows, rows, 2 * rows)

    def load(ref, index):
        return ref[:, index].reshape(rows, HD)

    q_l, k_l, v_l, g_l = (load(left, i) for i in range(4))
    q_o, k_o, v_o, g_o = (load(own, i) for i in range(4))
    q_r, k_r, v_r, g_r = (load(right, i) for i in range(4))

    k_all = jnp.concatenate((k_l, k_o, k_r))
    v_all = jnp.concatenate((v_l, v_o, v_r))
    p, s = probs_and_grads(q_o, g_o, k_all, v_all, bias_own[...])
    attended[...] = dot_nn(p, v_all).astype(jnp.bfloat16)
    grad_q[...] = (dot_nn(s, k_all) * SCALE).astype(jnp.bfloat16)
    p_o, s_o = p[:, rows : 2 * rows], s[:, rows : 2 * rows]
    p_l, s_l = probs_and_grads(
        q_l, g_l, k_all[: 2 * rows], v_all[: 2 * rows], bias_left[...]
    )
    p_r, s_r = probs_and_grads(q_r, g_r, k_all[rows:], v_all[rows:], bias_right[...])
    p_l, s_l = p_l[:, rows:], s_l[:, rows:]
    p_r, s_r = p_r[:, :rows], s_r[:, :rows]
    grad_v[...] = (dot_tn(p_l, g_l) + dot_tn(p_o, g_o) + dot_tn(p_r, g_r)).astype(jnp.bfloat16)
    grad_k[...] = (
        (dot_tn(s_l, q_l) + dot_tn(s_o, q_o) + dot_tn(s_r, q_r)) * SCALE
    ).astype(jnp.bfloat16)


def attend(ids, own, left, right, outs, first_head, head_total):
    parts, _, part_rows, width = own.shape
    rows = parts * part_rows
    heads = width // HD
    block = pl.BlockSpec((parts, 4, part_rows, HD), lambda h: (0, 0, 0, h))
    whole = pl.BlockSpec(memory_space=pltpu.VMEM)
    out_spec = pl.BlockSpec((rows, HD), lambda h: (0, h + first_head))
    has_outs = outs is not None
    aliases = {5 + i: i for i in range(4)} if has_outs else {}
    return pl.pallas_call(
        functools.partial(attend_kernel, rows, has_outs),
        grid=(heads,),
        out_shape=[jax.ShapeDtypeStruct((rows, head_total * HD), jnp.bfloat16)] * 4,
        in_specs=[whole, whole, block, block, block]
        + ([pl.BlockSpec(memory_space=pl.ANY)] * 4 if has_outs else []),
        out_specs=[out_spec] * 4,
        scratch_shapes=[
            pltpu.VMEM((rows, 3 * rows), jnp.float32),
            pltpu.VMEM((rows, 2 * rows), jnp.float32),
            pltpu.VMEM((rows, 2 * rows), jnp.float32),
        ],
        input_output_aliases=aliases,
        compiler_params=pltpu.CompilerParams(
            dimension_semantics=("arbitrary",), vmem_limit_bytes=VMEM_LIMIT
        ),
        cost_estimate=pl.CostEstimate(
            flops=heads * 26 * 2 * rows * rows * HD,
            bytes_accessed=heads * 16 * 2 * rows * HD,
            transcendentals=heads * 7 * rows * rows,
        ),
    )(ids[:, None], ids[None, :], own, left, right, *(outs or ()))


def shards(queries, key_vectors, value_vectors, grad_output, image_ids):
    arrays = (queries, key_vectors, value_vectors, grad_output)
    parts = lax.axis_size("tensor")
    rows = queries.shape[0] * parts
    head_total = queries.shape[1] // HD // parts
    padded_ids = jnp.pad(image_ids, (rows, rows), constant_values=-1)
    ids = lax.dynamic_slice_in_dim(padded_ids, lax.axis_index("dp") * rows, 3 * rows)
    outs = None
    for first, count in split_counts(head_total, CHUNK_SHARES):
        packed = pack(arrays, parts, first * HD, count * HD)
        own = lax.all_to_all(packed, "tensor", split_axis=0, concat_axis=0, tiled=True)
        left = shift(own, "dp", 1)
        right = shift(own, "dp", -1)
        outs = attend(ids, own, left, right, outs, first, head_total)
    return tuple(outs)


def solution(mesh):
    return jax.shard_map(
        shards,
        mesh=mesh,
        in_specs=(
            P(("dp", "tensor"), None),
            P(("dp", "tensor"), None),
            P(("dp", "tensor"), None),
            P(("dp", "tensor"), None),
            P(),
        ),
        out_specs=(P("dp", "tensor"), P("dp", "tensor"), P("dp", "tensor"), P("dp", "tensor")),
        check_vma=False,
    )
```

time: 307 us -> 199 us (0.65)
  Pallas kernels: 0 us -> 126 us
  matrix products: 87.1 us -> 0 us
  local copies, waits for them, and re-layouts: 71.6 us -> 0.25 us
  waiting for transfers between devices: 89.4 us -> 36.7 us
  other arithmetic: 12.9 us -> 0 us
  starting transfers between devices: 40 us -> 33.6 us
    pallas_call x0 -> x6, Pallas kernels: none -> 126 us  [the longest x3 99 us: pack(): pl.pallas_call(functools.partial(pack_kernel, parts, first, width, total...]
    dot_general x72 -> x0, matrix products: 87.1 us -> none  [the longest x12 23 us: one_head(): jnp.dot(probs_low.T, grad_head, preferred_element_type=jnp.float32)]
    all_to_all x4 -> x3, waiting for transfers between devices: 67.9 us -> 11.6 us  [shards(): lax.all_to_all(packed, 'tensor', split_axis=0, concat_axis=0, tiled=True)]
    dynamic_update_slice x60 -> x0, local copies, waits for them, and re-layouts: 20.8 us -> none  [attend(): lax.map(one_head, (split_heads(queries, head_count), split_heads(key_vect...]
    concatenate x8 -> x0, local copies, waits for them, and re-layouts: 17.7 us -> none  [the longest x2 5 us: shards(): jnp.concatenate((grad_rows, later[3]))]
    unnamed x36 -> x2, local copies, waits for them, and re-layouts: 11.5 us -> 0.01 us
    ppermute x4 -> x0, local copies, waits for them, and re-layouts: 9.14 us -> none  [from_behind(): return lax.ppermute(block, axis, route)]
    slice x5 -> x0, local copies, waits for them, and re-layouts: 7.46 us -> none  [the longest x1 2.83 us: shards(): attended[:row_count]]
  transfers between devices with their start and end apart: 12 -> 9, of which waited for: 7 -> 6; matrix products, arithmetic and copies ran while one was open for 10% -> 0% of each run, Pallas kernels for 0% -> 43%
where the time goes in v1:
time: 199 us; the launch traced here: 197 us
  Pallas kernels  126 us (63%)
  waiting for transfers between devices  36.7 us (18%)
  starting transfers between devices  33.6 us (17%)
    pallas_call x3, Pallas kernels, pack(): pl.pallas_call(functools.partial(pack_kernel, parts, first, width, total...  99 us
    pallas_call x3, Pallas kernels, attend(): pl.pallas_call(functools.partial(attend_kernel, rows, has_outs), grid=(he...  26.8 us
    ppermute x6, waiting for transfers between devices, shift(): return lax.ppermute(block, axis, route)  25.1 us
    ppermute x6, starting transfers between devices, shift(): return lax.ppermute(block, axis, route)  20 us
    all_to_all x3, starting transfers between devices, shards(): lax.all_to_all(packed, 'tensor', split_axis=0, concat_axis=0, tiled=True)  13.7 us
    all_to_all x3, waiting for transfers between devices, shards(): lax.all_to_all(packed, 'tensor', split_axis=0, concat_axis=0, tiled=True)  11.6 us
  transfers between devices with their start and end apart: 9, of which 6 were waited for; matrix products, arithmetic and copies ran while one was open for 0% of the time, Pallas kernels for 43%

profile of v1, /device:TPU:3, one launch (start us, length us, event | category | flops | bytes accessed | tf_op | source)
XLA Modules:
  0.0 197.2 jit_solution(15840502950657347397)
XLA Ops:
  0.6 33.0 %shard_map.86 = bf16[4,4,64,512]{3,2,1,0:T(8,128)(2,1)} custom-call(bf16[64,6144]{1,0:T(8,128)(2,1)} %refs_0_.5, bf16[64,6144]{1,0:T(8,128)(2,1)} %refs_1_.5, bf16[64,6144]{1,0:T(8,128)(2,1)} %refs_2_.5, bf16[64,6144]{1,0:T(8,128)(2,1)} %refs_3_.5), custom_call_target="tpu_custom_call" | custom-call | bytes 2097152 | tf_op jit(solution)/shard_map/pallas_call | solution.py:49
  33.6 4.6 %all-to-all-start.2 = ((bf16[4,4,64,512]{3,2,1,0:T(8,128)(2,1)}), bf16[4,4,64,512]{3,2,1,0:T(8,128)(2,1)S(1)}, u32[]{:S(2)}, u32[]{:S(2)}) async-start(bf16[4,4,64,512]{3,2,1,0:T(8,128)(2,1)} %shard_map.86), calls=%async_computation.2 | async-start | bytes 2097152 | tf_op jit(solution)/shard_map/all_to_all | solution.py:170
  38.3 33.0 %shard_map.85 = bf16[4,4,64,512]{3,2,1,0:T(8,128)(2,1)} custom-call(bf16[64,6144]{1,0:T(8,128)(2,1)} %refs_0_.5, bf16[64,6144]{1,0:T(8,128)(2,1)} %refs_1_.5, bf16[64,6144]{1,0:T(8,128)(2,1)} %refs_2_.5, bf16[64,6144]{1,0:T(8,128)(2,1)} %refs_3_.5), custom_call_target="tpu_custom_call" | custom-call | bytes 2097152 | tf_op jit(solution)/shard_map/pallas_call | solution.py:49
  71.3 0.0 all-to-all-done.2.refs_2_
  71.3 4.5 %all-to-all-start.1 = ((bf16[4,4,64,512]{3,2,1,0:T(8,128)(2,1)}), bf16[4,4,64,512]{3,2,1,0:T(8,128)(2,1)S(1)}, u32[]{:S(2)}, u32[]{:S(2)}) async-start(bf16[4,4,64,512]{3,2,1,0:T(8,128)(2,1)} %shard_map.85), calls=%async_computation.1 | async-start | bytes 2097152 | tf_op jit(solution)/shard_map/all_to_all | solution.py:170
  75.8 33.0 %shard_map.84 = bf16[4,4,64,512]{3,2,1,0:T(8,128)(2,1)} custom-call(bf16[64,6144]{1,0:T(8,128)(2,1)} %refs_0_.5, bf16[64,6144]{1,0:T(8,128)(2,1)} %refs_1_.5, bf16[64,6144]{1,0:T(8,128)(2,1)} %refs_2_.5, bf16[64,6144]{1,0:T(8,128)(2,1)} %refs_3_.5), custom_call_target="tpu_custom_call" | custom-call | bytes 2097152 | tf_op jit(solution)/shard_map/pallas_call | solution.py:49
  108.8 0.0 all-to-all-done.1.refs_2_
  108.8 4.5 %all-to-all-start = ((bf16[4,4,64,512]{3,2,1,0:T(8,128)(2,1)}), bf16[4,4,64,512]{3,2,1,0:T(8,128)(2,1)S(1)}, u32[]{:S(2)}, u32[]{:S(2)}) async-start(bf16[4,4,64,512]{3,2,1,0:T(8,128)(2,1)} %shard_map.84), calls=%async_computation | async-start | bytes 2097152 | tf_op jit(solution)/shard_map/all_to_all | solution.py:170
  113.4 0.0 copy-start
  113.4 5.2 %collective-permute-start.4 = (bf16[4,4,64,512]{3,2,1,0:T(8,128)(2,1)S(1)}, bf16[4,4,64,512]{3,2,1,0:T(8,128)(2,1)}, u32[]{:S(2)}, u32[]{:S(2)}) collective-permute-start(bf16[4,4,64,512]{3,2,1,0:T(8,128)(2,1)S(1)} %all-to-all-done.2.refs_2_), channel_id=1, source_target_pairs={{0,4},{4,8},{8,12},{12,16},{16,20},{20,24},{24,28},{1,5},{5,9},{9,... | collective-permute-start | bytes 3145736 | tf_op jit(solution)/shard_map/ppermute | solution.py:28
  118.6 1.9 collective-permute-start.5
  120.5 4.5 %collective-permute-start.2 = (bf16[4,4,64,512]{3,2,1,0:T(8,128)(2,1)S(1)}, bf16[4,4,64,512]{3,2,1,0:T(8,128)(2,1)}, u32[]{:S(2)}, u32[]{:S(2)}) collective-permute-start(bf16[4,4,64,512]{3,2,1,0:T(8,128)(2,1)S(1)} %all-to-all-done.1.refs_2_), channel_id=1, source_target_pairs={{0,4},{4,8},{8,12},{12,16},{16,20},{20,24},{24,28},{1,5},{5,9},{9,... | collective-permute-start | bytes 3145736 | tf_op jit(solution)/shard_map/ppermute | solution.py:28
  125.1 1.9 collective-permute-start.3
  127.0 11.6 %all-to-all-done.refs_2_ = bf16[4,4,64,512]{3,2,1,0:T(8,128)(2,1)S(1)} async-done(((bf16[4,4,64,512]{3,2,1,0:T(8,128)(2,1)}), bf16[4,4,64,512]{3,2,1,0:T(8,128)(2,1)S(1)}, u32[]{:S(2)}, u32[]{:S(2)}) %all-to-all-start) | async-done | bytes 1048608 | tf_op jit(solution)/shard_map/all_to_all | solution.py:170
  138.6 4.5 %collective-permute-start = (bf16[4,4,64,512]{3,2,1,0:T(8,128)(2,1)S(1)}, bf16[4,4,64,512]{3,2,1,0:T(8,128)(2,1)}, u32[]{:S(2)}, u32[]{:S(2)}) collective-permute-start(bf16[4,4,64,512]{3,2,1,0:T(8,128)(2,1)S(1)} %all-to-all-done.refs_2_), channel_id=1, source_target_pairs={{0,4},{4,8},{8,12},{12,16},{16,20},{20,24},{24,28},{1,5},{5,9},{9,... | collective-permute-start | bytes 3145736 | tf_op jit(solution)/shard_map/ppermute | solution.py:28
  143.1 0.0 collective-permute-done.4.refs_3_
  143.1 1.9 collective-permute-start.1
  145.0 0.0 copy-done
  145.0 0.1 pad_dynamic-slice_fusion
  145.1 0.2 broadcast_in_dim.12.refs_0_
  145.3 1.7 collective-permute-done.5.refs_4_
  147.0 8.9 %shard_map.87 = (bf16[256,1536]{1,0:T(8,128)(2,1)}, bf16[256,1536]{1,0:T(8,128)(2,1)}, bf16[256,1536]{1,0:T(8,128)(2,1)}, bf16[256,1536]{1,0:T(8,128)(2,1)}) custom-call(s32[768,1]{1,0:T(8,128)S(1)} %broadcast_in_dim.12.refs_0_, s32[1,768]{1,0:T(1,128)S(1)} %broadcast_in_dim.5.refs_1_, bf16[4,4,64,512]{3,2,1,0:T(8,128)(2,1)S(1)} %all-to-all-done.2.refs_2_, ...), custom_call_target="tpu_custom_call" | custom-call | flops 1744830464 | bytes 4194304 | tf_op jit(solution)/shard_map/pallas_call | solution.py:136
  155.9 5.3 %collective-permute-done.2.refs_3_ = bf16[4,4,64,512]{3,2,1,0:T(8,128)(2,1)} collective-permute-done((bf16[4,4,64,512]{3,2,1,0:T(8,128)(2,1)S(1)}, bf16[4,4,64,512]{3,2,1,0:T(8,128)(2,1)}, u32[]{:S(2)}, u32[]{:S(2)}) %collective-permute-start.2) | collective-permute-done | bytes 1048608 | tf_op jit(solution)/shard_map/ppermute | solution.py:28
  161.2 8.3 %collective-permute-done.3.refs_4_ = bf16[4,4,64,512]{3,2,1,0:T(8,128)(2,1)} collective-permute-done((bf16[4,4,64,512]{3,2,1,0:T(8,128)(2,1)S(1)}, bf16[4,4,64,512]{3,2,1,0:T(8,128)(2,1)}, u32[]{:S(2)}, u32[]{:S(2)}) %collective-permute-start.3) | collective-permute-done | bytes 1048608 | tf_op jit(solution)/shard_map/ppermute | solution.py:28
  169.5 8.9 %shard_map.88 = (bf16[256,1536]{1,0:T(8,128)(2,1)}, bf16[256,1536]{1,0:T(8,128)(2,1)}, bf16[256,1536]{1,0:T(8,128)(2,1)}, bf16[256,1536]{1,0:T(8,128)(2,1)}) custom-call(s32[768,1]{1,0:T(8,128)S(1)} %broadcast_in_dim.12.refs_0_, s32[1,768]{1,0:T(1,128)S(1)} %broadcast_in_dim.5.refs_1_, ...), custom_call_target="tpu_custom_call", output_to_operand_aliasing={{0}: (5, {}), {1}: (6, {}), {2}: (7, {}), {3}: (8, {})} | custom-call | flops 1744830464 | bytes 4194304 | tf_op jit(solution)/shard_map/pallas_call | solution.py:136
  178.4 5.3 %collective-permute-done.refs_3_ = bf16[4,4,64,512]{3,2,1,0:T(8,128)(2,1)} collective-permute-done((bf16[4,4,64,512]{3,2,1,0:T(8,128)(2,1)S(1)}, bf16[4,4,64,512]{3,2,1,0:T(8,128)(2,1)}, u32[]{:S(2)}, u32[]{:S(2)}) %collective-permute-start) | collective-permute-done | bytes 1048608 | tf_op jit(solution)/shard_map/ppermute | solution.py:28
  183.7 4.6 %collective-permute-done.1.refs_4_ = bf16[4,4,64,512]{3,2,1,0:T(8,128)(2,1)} collective-permute-done((bf16[4,4,64,512]{3,2,1,0:T(8,128)(2,1)S(1)}, bf16[4,4,64,512]{3,2,1,0:T(8,128)(2,1)}, u32[]{:S(2)}, u32[]{:S(2)}) %collective-permute-start.1) | collective-permute-done | bytes 1048608 | tf_op jit(solution)/shard_map/ppermute | solution.py:28
  188.3 8.9 %shard_map.89 = (bf16[256,1536]{1,0:T(8,128)(2,1)}, bf16[256,1536]{1,0:T(8,128)(2,1)}, bf16[256,1536]{1,0:T(8,128)(2,1)}, bf16[256,1536]{1,0:T(8,128)(2,1)}) custom-call(s32[768,1]{1,0:T(8,128)S(1)} %broadcast_in_dim.12.refs_0_, s32[1,768]{1,0:T(1,128)S(1)} %broadcast_in_dim.5.refs_1_, ...), custom_call_target="tpu_custom_call", output_to_operand_aliasing={{0}: (5, {}), {1}: (6, {}), {2}: (7, {}), {3}: (8, {})} | custom-call | flops 1744830464 | bytes 4194304 | tf_op jit(solution)/shard_map/pallas_call | solution.py:136
  (1 shorter events, 0.0 us)
Async XLA Ops:
  33.6 37.6 %all-to-all-start.2 = ((bf16[4,4,64,512]{3,2,1,0:T(8,128)(2,1)}), bf16[4,4,64,512]{3,2,1,0:T(8,128)(2,1)S(1)}, u32[]{:S(2)}, u32[]{:S(2)}) async-start(bf16[4,4,64,512]{3,2,1,0:T(8,128)(2,1)} %shard_map.86), calls=%async_computation.2 | async-start | bytes 2097152 | tf_op jit(solution)/shard_map/all_to_all | solution.py:170
  71.3 37.6 %all-to-all-start.1 = ((bf16[4,4,64,512]{3,2,1,0:T(8,128)(2,1)}), bf16[4,4,64,512]{3,2,1,0:T(8,128)(2,1)S(1)}, u32[]{:S(2)}, u32[]{:S(2)}) async-start(bf16[4,4,64,512]{3,2,1,0:T(8,128)(2,1)} %shard_map.85), calls=%async_computation.1 | async-start | bytes 2097152 | tf_op jit(solution)/shard_map/all_to_all | solution.py:170
  108.8 29.8 %all-to-all-start = ((bf16[4,4,64,512]{3,2,1,0:T(8,128)(2,1)}), bf16[4,4,64,512]{3,2,1,0:T(8,128)(2,1)S(1)}, u32[]{:S(2)}, u32[]{:S(2)}) async-start(bf16[4,4,64,512]{3,2,1,0:T(8,128)(2,1)} %shard_map.84), calls=%async_computation | async-start | bytes 2097152 | tf_op jit(solution)/shard_map/all_to_all | solution.py:170
  113.4 31.6 %copy-start = (s32[2048]{0:T(1024)S(1)}, s32[2048]{0:T(1024)}, u32[]{:S(2)}) copy-start(s32[2048]{0:T(1024)} %param.9) | copy-start | bytes 24580
  113.4 29.7 %collective-permute-start.4 = (bf16[4,4,64,512]{3,2,1,0:T(8,128)(2,1)S(1)}, bf16[4,4,64,512]{3,2,1,0:T(8,128)(2,1)}, u32[]{:S(2)}, u32[]{:S(2)}) collective-permute-start(bf16[4,4,64,512]{3,2,1,0:T(8,128)(2,1)S(1)} %all-to-all-done.2.refs_2_), channel_id=1, source_target_pairs={{0,4},{4,8},{8,12},{12,16},{16,20},{20,24},{24,28},{1,5},{5,9},{9,... | collective-permute-start | bytes 3145736 | tf_op jit(solution)/shard_map/ppermute | solution.py:28
  118.6 28.4 %collective-permute-start.5 = (bf16[4,4,64,512]{3,2,1,0:T(8,128)(2,1)S(1)}, bf16[4,4,64,512]{3,2,1,0:T(8,128)(2,1)}, u32[]{:S(2)}, u32[]{:S(2)}) collective-permute-start(bf16[4,4,64,512]{3,2,1,0:T(8,128)(2,1)S(1)} %all-to-all-done.2.refs_2_), channel_id=1, source_target_pairs={{4,0},{8,4},{12,8},{16,12},{20,16},{24,20},{28,24},{5,1},{9,5},{13... | collective-permute-start | bytes 3145736 | tf_op jit(solution)/shard_map/ppermute | solution.py:28
  120.5 40.7 %collective-permute-start.2 = (bf16[4,4,64,512]{3,2,1,0:T(8,128)(2,1)S(1)}, bf16[4,4,64,512]{3,2,1,0:T(8,128)(2,1)}, u32[]{:S(2)}, u32[]{:S(2)}) collective-permute-start(bf16[4,4,64,512]{3,2,1,0:T(8,128)(2,1)S(1)} %all-to-all-done.1.refs_2_), channel_id=1, source_target_pairs={{0,4},{4,8},{8,12},{12,16},{16,20},{20,24},{24,28},{1,5},{5,9},{9,... | collective-permute-start | bytes 3145736 | tf_op jit(solution)/shard_map/ppermute | solution.py:28
  125.1 44.4 %collective-permute-start.3 = (bf16[4,4,64,512]{3,2,1,0:T(8,128)(2,1)S(1)}, bf16[4,4,64,512]{3,2,1,0:T(8,128)(2,1)}, u32[]{:S(2)}, u32[]{:S(2)}) collective-permute-start(bf16[4,4,64,512]{3,2,1,0:T(8,128)(2,1)S(1)} %all-to-all-done.1.refs_2_), channel_id=1, source_target_pairs={{4,0},{8,4},{12,8},{16,12},{20,16},{24,20},{28,24},{5,1},{9,5},{13... | collective-permute-start | bytes 3145736 | tf_op jit(solution)/shard_map/ppermute | solution.py:28
  138.6 45.1 %collective-permute-start = (bf16[4,4,64,512]{3,2,1,0:T(8,128)(2,1)S(1)}, bf16[4,4,64,512]{3,2,1,0:T(8,128)(2,1)}, u32[]{:S(2)}, u32[]{:S(2)}) collective-permute-start(bf16[4,4,64,512]{3,2,1,0:T(8,128)(2,1)S(1)} %all-to-all-done.refs_2_), channel_id=1, source_target_pairs={{0,4},{4,8},{8,12},{12,16},{16,20},{20,24},{24,28},{1,5},{5,9},{9,... | collective-permute-start | bytes 3145736 | tf_op jit(solution)/shard_map/ppermute | solution.py:28
  143.1 45.2 %collective-permute-start.1 = (bf16[4,4,64,512]{3,2,1,0:T(8,128)(2,1)S(1)}, bf16[4,4,64,512]{3,2,1,0:T(8,128)(2,1)}, u32[]{:S(2)}, u32[]{:S(2)}) collective-permute-start(bf16[4,4,64,512]{3,2,1,0:T(8,128)(2,1)S(1)} %all-to-all-done.refs_2_), channel_id=1, source_target_pairs={{4,0},{8,4},{12,8},{16,12},{20,16},{24,20},{28,24},{5,1},{9,5},{13... | collective-permute-start | bytes 3145736 | tf_op jit(solution)/shard_map/ppermute | solution.py:28

commit v2 on v1

--- a/solution.py
+++ b/solution.py
@@ -28,32 +28,31 @@
     return lax.ppermute(block, axis, route)
 
 
-def pack_kernel(parts, first, width, stride, *refs):
-    arrays, packed, sems = refs[:4], refs[4], refs[5]
-    copies = []
-    for part in range(parts):
-        for index, array in enumerate(arrays):
-            copy = pltpu.make_async_copy(
-                array.at[:, pl.ds(part * stride + first, width)],
-                packed.at[part, index],
-                sems.at[part * 4 + index],
-            )
-            copy.start()
-            copies.append(copy)
-    for copy in copies:
-        copy.wait()
+def pack_kernel(*refs):
+    packed = refs[4]
+    for index, array in enumerate(refs[:4]):
+        packed[0, index] = array[...]
 
 
-def pack(arrays, parts, first, width):
+def pack(arrays, parts, first, count):
     rows, total = arrays[0].shape
+    heads = total // parts // HD
+    width = math.gcd(first, math.gcd(count, heads)) * HD
+    steps = count * HD // width
+    in_spec = pl.BlockSpec(
+        (rows, width), lambda p, s: (0, p * (heads * HD // width) + first * HD // width + s)
+    )
     return pl.pallas_call(
-        functools.partial(pack_kernel, parts, first, width, total // parts),
-        out_shape=jax.ShapeDtypeStruct((parts, 4, rows, width), jnp.bfloat16),
-        in_specs=[pl.BlockSpec(memory_space=pl.ANY)] * 4,
-        out_specs=pl.BlockSpec(memory_space=pl.ANY),
-        scratch_shapes=[pltpu.SemaphoreType.DMA((parts * 4,))],
+        pack_kernel,
+        grid=(parts, steps),
+        out_shape=jax.ShapeDtypeStruct((parts, 4, rows, count * HD), jnp.bfloat16),
+        in_specs=[in_spec] * 4,
+        out_specs=pl.BlockSpec((1, 4, rows, width), lambda p, s: (p, 0, 0, s)),
+        compiler_params=pltpu.CompilerParams(
+            dimension_semantics=("arbitrary", "arbitrary"), vmem_limit_bytes=VMEM_LIMIT
+        ),
         cost_estimate=pl.CostEstimate(
-            flops=0, bytes_accessed=parts * 16 * rows * width, transcendentals=0
+            flops=0, bytes_accessed=parts * 16 * rows * count * HD, transcendentals=0
         ),
     )(*arrays)
 
@@ -166,7 +165,7 @@
     ids = lax.dynamic_slice_in_dim(padded_ids, lax.axis_index("dp") * rows, 3 * rows)
     outs = None
     for first, count in split_counts(head_total, CHUNK_SHARES):
-        packed = pack(arrays, parts, first * HD, count * HD)
+        packed = pack(arrays, parts, first, count)
         own = lax.all_to_all(packed, "tensor", split_axis=0, concat_axis=0, tiled=True)
         left = shift(own, "dp", 1)
         right = shift(own, "dp", -1)

time: 199 us -> 154 us (0.77)
  Pallas kernels: 126 us -> 27.7 us
  waiting for transfers between devices: 36.7 us -> 85 us
  local copies, waits for them, and re-layouts: 0.25 us -> 7.73 us
    pallas_call x3, Pallas kernels: 99 us -> 0.86 us  [pack(): pl.pallas_call(pack_kernel, grid=(parts, steps), out_shape=jax.ShapeDtype...]
    all_to_all x3, waiting for transfers between devices: 11.6 us -> 60.3 us  [shards(): lax.all_to_all(packed, 'tensor', split_axis=0, concat_axis=0, tiled=True)]
    unnamed x2 -> x24, local copies, waits for them, and re-layouts: 0.01 us -> 7.48 us
  transfers between devices with their start and end apart: 9 -> 9, of which waited for: 6 -> 8; matrix products, arithmetic and copies ran while one was open for 0% -> 0% of each run, Pallas kernels for 43% -> 12%
where the time goes in v2:
time: 154 us; the launch traced here: 153 us
  waiting for transfers between devices  85 us (55%)
  starting transfers between devices  31.7 us (21%)
  Pallas kernels  27.7 us (18%)
  local copies, waits for them, and re-layouts  7.73 us (5%)
    all_to_all x3, waiting for transfers between devices, shards(): lax.all_to_all(packed, 'tensor', split_axis=0, concat_axis=0, tiled=True)  60.3 us
    pallas_call x3, Pallas kernels, attend(): pl.pallas_call(functools.partial(attend_kernel, rows, has_outs), grid=(he...  26.8 us
    ppermute x6, waiting for transfers between devices, shift(): return lax.ppermute(block, axis, route)  24.7 us
    ppermute x6, starting transfers between devices, shift(): return lax.ppermute(block, axis, route)  19.2 us
    all_to_all x3, starting transfers between devices, shards(): lax.all_to_all(packed, 'tensor', split_axis=0, concat_axis=0, tiled=True)  12.5 us
    unnamed x24, local copies, waits for them, and re-layouts  7.48 us
  transfers between devices with their start and end apart: 9, of which 8 were waited for; matrix products, arithmetic and copies ran while one was open for 0% of the time, Pallas kernels for 12%

profile of v2, /device:TPU:3, one launch (start us, length us, event | category | flops | bytes accessed | tf_op | source)
XLA Modules:
  0.0 152.9 jit_solution(16608549959990906322)
XLA Ops:
  0.6 1.1 copy-done
  1.8 1.1 copy-done.2
  2.9 1.1 copy-done.4
  4.0 1.1 copy-done.6
  5.2 0.3 shard_map.86
  5.5 1.0 copy-done.10
  6.5 4.7 %all-to-all-start.2 = ((bf16[4,4,64,512]{3,2,1,0:T(8,128)(2,1)}), bf16[4,4,64,512]{3,2,1,0:T(8,128)(2,1)}, u32[]{:S(2)}, u32[]{:S(2)}) async-start(bf16[4,4,64,512]{3,2,1,0:T(8,128)(2,1)} %copy-done.10), calls=%async_computation.2 | async-start | bytes 2097152 | tf_op jit(solution)/shard_map/all_to_all | solution.py:169
  11.2 0.3 shard_map.85
  11.5 1.0 copy-done.9
  12.5 24.0 %all-to-all-done.2.refs_2_ = bf16[4,4,64,512]{3,2,1,0:T(8,128)(2,1)} async-done(((bf16[4,4,64,512]{3,2,1,0:T(8,128)(2,1)}), bf16[4,4,64,512]{3,2,1,0:T(8,128)(2,1)}, u32[]{:S(2)}, u32[]{:S(2)}) %all-to-all-start.2) | async-done | bytes 1048608 | tf_op jit(solution)/shard_map/all_to_all | solution.py:169
  36.5 4.2 %all-to-all-start.1 = ((bf16[4,4,64,512]{3,2,1,0:T(8,128)(2,1)}), bf16[4,4,64,512]{3,2,1,0:T(8,128)(2,1)}, u32[]{:S(2)}, u32[]{:S(2)}) async-start(bf16[4,4,64,512]{3,2,1,0:T(8,128)(2,1)} %copy-done.9), calls=%async_computation.1 | async-start | bytes 2097152 | tf_op jit(solution)/shard_map/all_to_all | solution.py:169
  40.8 0.3 shard_map.84
  41.1 1.0 copy-done.8
  42.0 24.0 %all-to-all-done.1.refs_2_ = bf16[4,4,64,512]{3,2,1,0:T(8,128)(2,1)} async-done(((bf16[4,4,64,512]{3,2,1,0:T(8,128)(2,1)}), bf16[4,4,64,512]{3,2,1,0:T(8,128)(2,1)}, u32[]{:S(2)}, u32[]{:S(2)}) %all-to-all-start.1) | async-done | bytes 1048608 | tf_op jit(solution)/shard_map/all_to_all | solution.py:169
  66.1 3.5 %all-to-all-start = ((bf16[4,4,64,512]{3,2,1,0:T(8,128)(2,1)}), bf16[4,4,64,512]{3,2,1,0:T(8,128)(2,1)S(1)}, u32[]{:S(2)}, u32[]{:S(2)}) async-start(bf16[4,4,64,512]{3,2,1,0:T(8,128)(2,1)} %copy-done.8), calls=%async_computation | async-start | bytes 2097152 | tf_op jit(solution)/shard_map/all_to_all | solution.py:169
  69.6 4.5 %collective-permute-start.4 = (bf16[4,4,64,512]{3,2,1,0:T(8,128)(2,1)}, bf16[4,4,64,512]{3,2,1,0:T(8,128)(2,1)}, u32[]{:S(2)}, u32[]{:S(2)}) collective-permute-start(bf16[4,4,64,512]{3,2,1,0:T(8,128)(2,1)} %all-to-all-done.2.refs_2_), channel_id=1, source_target_pairs={{0,4},{4,8},{8,12},{12,16},{16,20},{20,24},{24,28},{1,5},{5,9},{9,... | collective-permute-start | bytes 3145736 | tf_op jit(solution)/shard_map/ppermute | solution.py:28
  74.1 1.9 %collective-permute-start.5 = (bf16[4,4,64,512]{3,2,1,0:T(8,128)(2,1)}, bf16[4,4,64,512]{3,2,1,0:T(8,128)(2,1)}, u32[]{:S(2)}, u32[]{:S(2)}) collective-permute-start(bf16[4,4,64,512]{3,2,1,0:T(8,128)(2,1)} %all-to-all-done.2.refs_2_), channel_id=1, source_target_pairs={{4,0},{8,4},{12,8},{16,12},{20,16},{24,20},{28,24},{5,1},{9,5},{13... | collective-permute-start | bytes 3145736 | tf_op jit(solution)/shard_map/ppermute | solution.py:28
  76.0 4.5 %collective-permute-start.2 = (bf16[4,4,64,512]{3,2,1,0:T(8,128)(2,1)}, bf16[4,4,64,512]{3,2,1,0:T(8,128)(2,1)S(1)}, u32[]{:S(2)}, u32[]{:S(2)}) collective-permute-start(bf16[4,4,64,512]{3,2,1,0:T(8,128)(2,1)} %all-to-all-done.1.refs_2_), channel_id=1, source_target_pairs={{0,4},{4,8},{8,12},{12,16},{16,20},{20,24},{24,28},{1,5},{5,9},{9,... | collective-permute-start | bytes 3145736 | tf_op jit(solution)/shard_map/ppermute | solution.py:28
  80.5 1.9 %collective-permute-start.3 = (bf16[4,4,64,512]{3,2,1,0:T(8,128)(2,1)}, bf16[4,4,64,512]{3,2,1,0:T(8,128)(2,1)}, u32[]{:S(2)}, u32[]{:S(2)}) collective-permute-start(bf16[4,4,64,512]{3,2,1,0:T(8,128)(2,1)} %all-to-all-done.1.refs_2_), channel_id=1, source_target_pairs={{4,0},{8,4},{12,8},{16,12},{20,16},{24,20},{28,24},{5,1},{9,5},{13... | collective-permute-start | bytes 3145736 | tf_op jit(solution)/shard_map/ppermute | solution.py:28
  82.5 12.3 %all-to-all-done.refs_2_ = bf16[4,4,64,512]{3,2,1,0:T(8,128)(2,1)S(1)} async-done(((bf16[4,4,64,512]{3,2,1,0:T(8,128)(2,1)}), bf16[4,4,64,512]{3,2,1,0:T(8,128)(2,1)S(1)}, u32[]{:S(2)}, u32[]{:S(2)}) %all-to-all-start) | async-done | bytes 1048608 | tf_op jit(solution)/shard_map/all_to_all | solution.py:169
  94.8 4.5 %collective-permute-start = (bf16[4,4,64,512]{3,2,1,0:T(8,128)(2,1)S(1)}, bf16[4,4,64,512]{3,2,1,0:T(8,128)(2,1)S(1)}, u32[]{:S(2)}, u32[]{:S(2)}) collective-permute-start(bf16[4,4,64,512]{3,2,1,0:T(8,128)(2,1)S(1)} %all-to-all-done.refs_2_), channel_id=1, source_target_pairs={{0,4},{4,8},{8,12},{12,16},{16,20},{20,24},{24,28},{1,5},{5,9},{9,... | collective-permute-start | bytes 3145736 | tf_op jit(solution)/shard_map/ppermute | solution.py:28
  99.2 1.9 %collective-permute-start.1 = (bf16[4,4,64,512]{3,2,1,0:T(8,128)(2,1)S(1)}, bf16[4,4,64,512]{3,2,1,0:T(8,128)(2,1)}, u32[]{:S(2)}, u32[]{:S(2)}) collective-permute-start(bf16[4,4,64,512]{3,2,1,0:T(8,128)(2,1)S(1)} %all-to-all-done.refs_2_), channel_id=1, source_target_pairs={{4,0},{8,4},{12,8},{16,12},{20,16},{24,20},{28,24},{5,1},{9,5},{13... | collective-permute-start | bytes 3145736 | tf_op jit(solution)/shard_map/ppermute | solution.py:28
  101.2 0.1 pad_dynamic-slice_fusion
  101.3 0.2 broadcast_in_dim.12.refs_0_
  101.4 1.3 collective-permute-done.5.refs_4_
  102.7 8.9 %shard_map.87 = (bf16[256,1536]{1,0:T(8,128)(2,1)}, bf16[256,1536]{1,0:T(8,128)(2,1)}, bf16[256,1536]{1,0:T(8,128)(2,1)}, bf16[256,1536]{1,0:T(8,128)(2,1)}) custom-call(s32[768,1]{1,0:T(8,128)S(1)} %broadcast_in_dim.12.refs_0_, s32[1,768]{1,0:T(1,128)S(1)} %broadcast_in_dim.5.refs_1_, bf16[4,4,64,512]{3,2,1,0:T(8,128)(2,1)} %all-to-all-done.2.refs_2_, ...), custom_call_target="tpu_custom_call" | custom-call | flops 1744830464 | bytes 4194304 | tf_op jit(solution)/shard_map/pallas_call | solution.py:135
  111.6 5.4 %collective-permute-done.2.refs_3_ = bf16[4,4,64,512]{3,2,1,0:T(8,128)(2,1)S(1)} collective-permute-done((bf16[4,4,64,512]{3,2,1,0:T(8,128)(2,1)}, bf16[4,4,64,512]{3,2,1,0:T(8,128)(2,1)S(1)}, u32[]{:S(2)}, u32[]{:S(2)}) %collective-permute-start.2) | collective-permute-done | bytes 1048608 | tf_op jit(solution)/shard_map/ppermute | solution.py:28
  117.0 8.2 %collective-permute-done.3.refs_4_ = bf16[4,4,64,512]{3,2,1,0:T(8,128)(2,1)} collective-permute-done((bf16[4,4,64,512]{3,2,1,0:T(8,128)(2,1)}, bf16[4,4,64,512]{3,2,1,0:T(8,128)(2,1)}, u32[]{:S(2)}, u32[]{:S(2)}) %collective-permute-start.3) | collective-permute-done | bytes 1048608 | tf_op jit(solution)/shard_map/ppermute | solution.py:28
  125.2 8.9 %shard_map.88 = (bf16[256,1536]{1,0:T(8,128)(2,1)}, bf16[256,1536]{1,0:T(8,128)(2,1)}, bf16[256,1536]{1,0:T(8,128)(2,1)}, bf16[256,1536]{1,0:T(8,128)(2,1)}) custom-call(s32[768,1]{1,0:T(8,128)S(1)} %broadcast_in_dim.12.refs_0_, s32[1,768]{1,0:T(1,128)S(1)} %broadcast_in_dim.5.refs_1_, ...), custom_call_target="tpu_custom_call", output_to_operand_aliasing={{0}: (5, {}), {1}: (6, {}), {2}: (7, {}), {3}: (8, {})} | custom-call | flops 1744830464 | bytes 4194304 | tf_op jit(solution)/shard_map/pallas_call | solution.py:135
  134.1 5.3 %collective-permute-done.refs_3_ = bf16[4,4,64,512]{3,2,1,0:T(8,128)(2,1)S(1)} collective-permute-done((bf16[4,4,64,512]{3,2,1,0:T(8,128)(2,1)S(1)}, bf16[4,4,64,512]{3,2,1,0:T(8,128)(2,1)S(1)}, u32[]{:S(2)}, u32[]{:S(2)}) %collective-permute-start) | collective-permute-done | bytes 1048608 | tf_op jit(solution)/shard_map/ppermute | solution.py:28
  139.4 4.6 %collective-permute-done.1.refs_4_ = bf16[4,4,64,512]{3,2,1,0:T(8,128)(2,1)} collective-permute-done((bf16[4,4,64,512]{3,2,1,0:T(8,128)(2,1)S(1)}, bf16[4,4,64,512]{3,2,1,0:T(8,128)(2,1)}, u32[]{:S(2)}, u32[]{:S(2)}) %collective-permute-start.1) | collective-permute-done | bytes 1048608 | tf_op jit(solution)/shard_map/ppermute | solution.py:28
  143.9 9.0 %shard_map.89 = (bf16[256,1536]{1,0:T(8,128)(2,1)}, bf16[256,1536]{1,0:T(8,128)(2,1)}, bf16[256,1536]{1,0:T(8,128)(2,1)}, bf16[256,1536]{1,0:T(8,128)(2,1)}) custom-call(s32[768,1]{1,0:T(8,128)S(1)} %broadcast_in_dim.12.refs_0_, s32[1,768]{1,0:T(1,128)S(1)} %broadcast_in_dim.5.refs_1_, ...), custom_call_target="tpu_custom_call", output_to_operand_aliasing={{0}: (5, {}), {1}: (6, {}), {2}: (7, {}), {3}: (8, {})} | custom-call | flops 1744830464 | bytes 4194304 | tf_op jit(solution)/shard_map/pallas_call | solution.py:135
  (19 shorter events, 0.0 us)
Async XLA Ops:
  0.6 1.1 copy-start
  1.8 1.1 copy-start.2
  2.9 1.1 copy-start.4
  4.0 1.1 copy-start.6
  5.2 6.0 %copy-start.5 = (bf16[64,6144]{1,0:T(8,128)(2,1)S(1)}, bf16[64,6144]{1,0:T(8,128)(2,1)}, u32[]{:S(2)}) copy-start(bf16[64,6144]{1,0:T(8,128)(2,1)} %refs_2_.5) | copy-start | bytes 2359300
  5.2 6.0 %copy-start.7 = (bf16[64,6144]{1,0:T(8,128)(2,1)S(1)}, bf16[64,6144]{1,0:T(8,128)(2,1)}, u32[]{:S(2)}) copy-start(bf16[64,6144]{1,0:T(8,128)(2,1)} %refs_3_.5) | copy-start | bytes 2359300
  5.5 1.0 copy-start.10
  6.5 4.7 %copy-start.1 = (bf16[64,6144]{1,0:T(8,128)(2,1)S(1)}, bf16[64,6144]{1,0:T(8,128)(2,1)}, u32[]{:S(2)}) copy-start(bf16[64,6144]{1,0:T(8,128)(2,1)} %refs_0_.5) | copy-start | bytes 2359300
  6.5 4.7 %copy-start.3 = (bf16[64,6144]{1,0:T(8,128)(2,1)S(1)}, bf16[64,6144]{1,0:T(8,128)(2,1)}, u32[]{:S(2)}) copy-start(bf16[64,6144]{1,0:T(8,128)(2,1)} %refs_1_.5) | copy-start | bytes 2359300
  6.5 30.1 %all-to-all-start.2 = ((bf16[4,4,64,512]{3,2,1,0:T(8,128)(2,1)}), bf16[4,4,64,512]{3,2,1,0:T(8,128)(2,1)}, u32[]{:S(2)}, u32[]{:S(2)}) async-start(bf16[4,4,64,512]{3,2,1,0:T(8,128)(2,1)} %copy-done.10), calls=%async_computation.2 | async-start | bytes 2097152 | tf_op jit(solution)/shard_map/all_to_all | solution.py:169
  11.5 1.0 copy-start.9
  36.5 29.5 %all-to-all-start.1 = ((bf16[4,4,64,512]{3,2,1,0:T(8,128)(2,1)}), bf16[4,4,64,512]{3,2,1,0:T(8,128)(2,1)}, u32[]{:S(2)}, u32[]{:S(2)}) async-start(bf16[4,4,64,512]{3,2,1,0:T(8,128)(2,1)} %copy-done.9), calls=%async_computation.1 | async-start | bytes 2097152 | tf_op jit(solution)/shard_map/all_to_all | solution.py:169
  41.1 1.0 copy-start.8
  66.1 28.7 %all-to-all-start = ((bf16[4,4,64,512]{3,2,1,0:T(8,128)(2,1)}), bf16[4,4,64,512]{3,2,1,0:T(8,128)(2,1)S(1)}, u32[]{:S(2)}, u32[]{:S(2)}) async-start(bf16[4,4,64,512]{3,2,1,0:T(8,128)(2,1)} %copy-done.8), calls=%async_computation | async-start | bytes 2097152 | tf_op jit(solution)/shard_map/all_to_all | solution.py:169
  69.6 31.6 %copy-start.11 = (s32[2048]{0:T(1024)S(1)}, s32[2048]{0:T(1024)}, u32[]{:S(2)}) copy-start(s32[2048]{0:T(1024)} %param.9) | copy-start | bytes 24580
  69.6 29.6 %collective-permute-start.4 = (bf16[4,4,64,512]{3,2,1,0:T(8,128)(2,1)}, bf16[4,4,64,512]{3,2,1,0:T(8,128)(2,1)}, u32[]{:S(2)}, u32[]{:S(2)}) collective-permute-start(bf16[4,4,64,512]{3,2,1,0:T(8,128)(2,1)} %all-to-all-done.2.refs_2_), channel_id=1, source_target_pairs={{0,4},{4,8},{8,12},{12,16},{16,20},{20,24},{24,28},{1,5},{5,9},{9,... | collective-permute-start | bytes 3145736 | tf_op jit(solution)/shard_map/ppermute | solution.py:28
  74.1 28.6 %collective-permute-start.5 = (bf16[4,4,64,512]{3,2,1,0:T(8,128)(2,1)}, bf16[4,4,64,512]{3,2,1,0:T(8,128)(2,1)}, u32[]{:S(2)}, u32[]{:S(2)}) collective-permute-start(bf16[4,4,64,512]{3,2,1,0:T(8,128)(2,1)} %all-to-all-done.2.refs_2_), channel_id=1, source_target_pairs={{4,0},{8,4},{12,8},{16,12},{20,16},{24,20},{28,24},{5,1},{9,5},{13... | collective-permute-start | bytes 3145736 | tf_op jit(solution)/shard_map/ppermute | solution.py:28
  76.0 41.0 %collective-permute-start.2 = (bf16[4,4,64,512]{3,2,1,0:T(8,128)(2,1)}, bf16[4,4,64,512]{3,2,1,0:T(8,128)(2,1)S(1)}, u32[]{:S(2)}, u32[]{:S(2)}) collective-permute-start(bf16[4,4,64,512]{3,2,1,0:T(8,128)(2,1)} %all-to-all-done.1.refs_2_), channel_id=1, source_target_pairs={{0,4},{4,8},{8,12},{12,16},{16,20},{20,24},{24,28},{1,5},{5,9},{9,... | collective-permute-start | bytes 3145736 | tf_op jit(solution)/shard_map/ppermute | solution.py:28
  80.5 44.6 %collective-permute-start.3 = (bf16[4,4,64,512]{3,2,1,0:T(8,128)(2,1)}, bf16[4,4,64,512]{3,2,1,0:T(8,128)(2,1)}, u32[]{:S(2)}, u32[]{:S(2)}) collective-permute-start(bf16[4,4,64,512]{3,2,1,0:T(8,128)(2,1)} %all-to-all-done.1.refs_2_), channel_id=1, source_target_pairs={{4,0},{8,4},{12,8},{16,12},{20,16},{24,20},{28,24},{5,1},{9,5},{13... | collective-permute-start | bytes 3145736 | tf_op jit(solution)/shard_map/ppermute | solution.py:28
  94.8 44.6 %collective-permute-start = (bf16[4,4,64,512]{3,2,1,0:T(8,128)(2,1)S(1)}, bf16[4,4,64,512]{3,2,1,0:T(8,128)(2,1)S(1)}, u32[]{:S(2)}, u32[]{:S(2)}) collective-permute-start(bf16[4,4,64,512]{3,2,1,0:T(8,128)(2,1)S(1)} %all-to-all-done.refs_2_), channel_id=1, source_target_pairs={{0,4},{4,8},{8,12},{12,16},{16,20},{20,24},{24,28},{1,5},{5,9},{9,... | collective-permute-start | bytes 3145736 | tf_op jit(solution)/shard_map/ppermute | solution.py:28
  99.2 44.7 %collective-permute-start.1 = (bf16[4,4,64,512]{3,2,1,0:T(8,128)(2,1)S(1)}, bf16[4,4,64,512]{3,2,1,0:T(8,128)(2,1)}, u32[]{:S(2)}, u32[]{:S(2)}) collective-permute-start(bf16[4,4,64,512]{3,2,1,0:T(8,128)(2,1)S(1)} %all-to-all-done.refs_2_), channel_id=1, source_target_pairs={{4,0},{8,4},{12,8},{16,12},{20,16},{24,20},{28,24},{5,1},{9,5},{13... | collective-permute-start | bytes 3145736 | tf_op jit(solution)/shard_map/ppermute | solution.py:28

commit v3 on v1

--- a/solution.py
+++ b/solution.py
@@ -12,8 +12,9 @@
 SCALE = 1.0 / math.sqrt(HD)
 EXP2_SCALE = SCALE * math.log2(math.e)
 MASKED = -1e30
-CHUNK_SHARES = (4, 4, 4)
-VMEM_LIMIT = 48 * 1024 * 1024
+CHUNKS = (("all", 4), ("pairs", 2), ("all", 4), ("pairs", 2))
+VMEM_LIMIT = 60 * 1024 * 1024
+SMALL_COST = pl.CostEstimate(flops=1, bytes_accessed=1, transcendentals=0)
 
 
 def split_counts(total, shares):
@@ -28,34 +29,150 @@
     return lax.ppermute(block, axis, route)
 
 
-def pack_kernel(parts, first, width, stride, *refs):
-    arrays, packed, sems = refs[:4], refs[4], refs[5]
-    copies = []
+def swap(block, axis, flip):
+    route = [(i, i ^ flip) for i in range(lax.axis_size(axis))]
+    return lax.ppermute(block, axis, route)
+
+
+def columns(array, part, stride, first, width):
+    start = pl.multiple_of(part * stride + first, HD)
+    return array.at[:, pl.ds(start, width)]
+
+
+def pack_kernel(parts, stride, first, width, deps, *refs):
+    arrays, refs = refs[:4], refs[4 + deps :]
+    packed, (stage, in_sems, out_sems) = refs[: parts - 1], refs[parts - 1 :]
+    me = lax.axis_index("tensor")
+    loads, stores = [], []
+    for flip in range(1, parts):
+        for index, array in enumerate(arrays):
+            load = pltpu.make_async_copy(
+                columns(array, me ^ flip, stride, first, width),
+                stage.at[flip - 1, index],
+                in_sems.at[(flip - 1) * 4 + index],
+            )
+            load.start()
+            loads.append(load)
+    for flip in range(1, parts):
+        for load in loads[(flip - 1) * 4 : flip * 4]:
+            load.wait()
+        store = pltpu.make_async_copy(
+            stage.at[flip - 1], packed[flip - 1], out_sems.at[flip - 1]
+        )
+        store.start()
+        stores.append(store)
+    for store in stores:
+        store.wait()
+
+
+def pack(arrays, parts, first, count, after):
+    rows, total = arrays[0].shape
+    width = count * HD
+    return pl.pallas_call(
+        functools.partial(
+            pack_kernel, parts, total // parts, first * HD, width, len(after)
+        ),
+        out_shape=[jax.ShapeDtypeStruct((4, rows, width), jnp.bfloat16)] * (parts - 1),
+        in_specs=[pl.BlockSpec(memory_space=pl.ANY)] * (4 + len(after)),
+        out_specs=[pl.BlockSpec(memory_space=pl.ANY)] * (parts - 1),
+        scratch_shapes=[
+            pltpu.VMEM((parts - 1, 4, rows, width), jnp.bfloat16),
+            pltpu.SemaphoreType.DMA(((parts - 1) * 4,)),
+            pltpu.SemaphoreType.DMA((parts - 1,)),
+        ],
+        compiler_params=pltpu.CompilerParams(vmem_limit_bytes=VMEM_LIMIT),
+        cost_estimate=SMALL_COST,
+    )(*arrays, *after)
+
+
+def pack_all_kernel(parts, stride, first, width, deps, *refs):
+    arrays, (packed, stage, in_sems, out_sems) = refs[:4], refs[4 + deps :]
+    loads, stores = [], []
     for part in range(parts):
         for index, array in enumerate(arrays):
-            copy = pltpu.make_async_copy(
-                array.at[:, pl.ds(part * stride + first, width)],
-                packed.at[part, index],
-                sems.at[part * 4 + index],
+            load = pltpu.make_async_copy(
+                columns(array, part, stride, first, width),
+                stage.at[part, index],
+                in_sems.at[part * 4 + index],
             )
-            copy.start()
-            copies.append(copy)
-    for copy in copies:
-        copy.wait()
-
-
-def pack(arrays, parts, first, width):
+            load.start()
+            loads.append(load)
+    for part in range(parts):
+        for load in loads[part * 4 : part * 4 + 4]:
+            load.wait()
+        store = pltpu.make_async_copy(stage.at[part], packed.at[part], out_sems.at[part])
+        store.start()
+        stores.append(store)
+    for store in stores:
+        store.wait()
+
+
+def pack_all(arrays, parts, first, count, after):
     rows, total = arrays[0].shape
+    width = count * HD
     return pl.pallas_call(
-        functools.partial(pack_kernel, parts, first, width, total // parts),
+        functools.partial(
+            pack_all_kernel, parts, total // parts, first * HD, width, len(after)
+        ),
         out_shape=jax.ShapeDtypeStruct((parts, 4, rows, width), jnp.bfloat16),
-        in_specs=[pl.BlockSpec(memory_space=pl.ANY)] * 4,
+        in_specs=[pl.BlockSpec(memory_space=pl.ANY)] * (4 + len(after)),
         out_specs=pl.BlockSpec(memory_space=pl.ANY),
-        scratch_shapes=[pltpu.SemaphoreType.DMA((parts * 4,))],
-        cost_estimate=pl.CostEstimate(
-            flops=0, bytes_accessed=parts * 16 * rows * width, transcendentals=0
-        ),
-    )(*arrays)
+        scratch_shapes=[
+            pltpu.VMEM((parts, 4, rows, width), jnp.bfloat16),
+            pltpu.SemaphoreType.DMA((parts * 4,)),
+            pltpu.SemaphoreType.DMA((parts,)),
+        ],
+        compiler_params=pltpu.CompilerParams(vmem_limit_bytes=VMEM_LIMIT),
+        cost_estimate=SMALL_COST,
+    )(*arrays, *after)
+
+
+def join_kernel(parts, stride, first, width, deps, *refs):
+    arrays, received, refs = refs[:4], refs[4 : 3 + parts], refs[3 + parts + deps :]
+    joined, stage, in_sems, out_sems = refs
+    me = lax.axis_index("tensor")
+    loads, stores = [], []
+    for flip in range(1, parts):
+        load = pltpu.make_async_copy(received[flip - 1], stage.at[flip], in_sems.at[3 + flip])
+        load.start()
+        loads.append([load])
+    own = []
+    for index, array in enumerate(arrays):
+        load = pltpu.make_async_copy(
+            columns(array, me, stride, first, width), stage.at[0, index], in_sems.at[index]
+        )
+        load.start()
+        own.append(load)
+    loads = [own] + loads
+    for flip in range(parts):
+        for load in loads[flip]:
+            load.wait()
+        store = pltpu.make_async_copy(stage.at[flip], joined.at[me ^ flip], out_sems.at[flip])
+        store.start()
+        stores.append(store)
+    for store in stores:
+        store.wait()
+
+
+def join(arrays, received, first, after):
+    parts = len(received) + 1
+    rows, total = arrays[0].shape
+    width = received[0].shape[2]
+    return pl.pallas_call(
+        functools.partial(
+            join_kernel, parts, total // parts, first * HD, width, len(after)
+        ),
+        out_shape=jax.ShapeDtypeStruct((parts, 4, rows, width), jnp.bfloat16),
+        in_specs=[pl.BlockSpec(memory_space=pl.ANY)] * (3 + parts + len(after)),
+        out_specs=pl.BlockSpec(memory_space=pl.ANY),
+        scratch_shapes=[
+            pltpu.VMEM((parts, 4, rows, width), jnp.bfloat16),
+            pltpu.SemaphoreType.DMA((parts + 3,)),
+            pltpu.SemaphoreType.DMA((parts,)),
+        ],
+        compiler_params=pltpu.CompilerParams(vmem_limit_bytes=VMEM_LIMIT),
+        cost_estimate=SMALL_COST,
+    )(*arrays, *received, *after)
 
 
 def dot_nt(a, b):
@@ -149,11 +266,7 @@
         compiler_params=pltpu.CompilerParams(
             dimension_semantics=("arbitrary",), vmem_limit_bytes=VMEM_LIMIT
         ),
-        cost_estimate=pl.CostEstimate(
-            flops=heads * 26 * 2 * rows * rows * HD,
-            bytes_accessed=heads * 16 * 2 * rows * HD,
-            transcendentals=heads * 7 * rows * rows,
-        ),
+        cost_estimate=SMALL_COST,
     )(ids[:, None], ids[None, :], own, left, right, *(outs or ()))
 
 
@@ -164,13 +277,34 @@
     head_total = queries.shape[1] // HD // parts
     padded_ids = jnp.pad(image_ids, (rows, rows), constant_values=-1)
     ids = lax.dynamic_slice_in_dim(padded_ids, lax.axis_index("dp") * rows, 3 * rows)
-    outs = None
-    for first, count in split_counts(head_total, CHUNK_SHARES):
-        packed = pack(arrays, parts, first * HD, count * HD)
-        own = lax.all_to_all(packed, "tensor", split_axis=0, concat_axis=0, tiled=True)
+    chunks = split_counts(head_total, [share for _, share in CHUNKS])
+    outs, owns, out_history, sent = None, [], [], []
+
+    def send(number):
+        first, count = chunks[number]
+        after = owns[number - 2 : number - 1] if number >= 2 else []
+        if CHUNKS[number][0] == "all":
+            sent.append([pack_all(arrays, parts, first, count, after)])
+        else:
+            sent.append(pack(arrays, parts, first, count, after))
+
+    send(0)
+    send(1)
+    for number, (first, count) in enumerate(chunks):
+        packed = sent[number]
+        if CHUNKS[number][0] == "all":
+            own = lax.all_to_all(packed[0], "tensor", split_axis=0, concat_axis=0, tiled=True)
+        else:
+            received = [swap(packed[flip - 1], "tensor", flip) for flip in range(1, parts)]
+            after = [later[0] for later in sent[number + 1 : number + 2]]
+            own = join(arrays, received, first, after)
+        owns.append(own)
+        if number + 2 < len(chunks):
+            send(number + 2)
         left = shift(own, "dp", 1)
         right = shift(own, "dp", -1)
         outs = attend(ids, own, left, right, outs, first, head_total)
+        out_history.append(outs)
     return tuple(outs)
 
 

time: 199 us -> 155 us (0.78)
  Pallas kernels: 126 us -> 41.1 us
  blocking collectives: 0 us -> 29.6 us
  starting transfers between devices: 33.6 us -> 40.7 us
  local copies, waits for them, and re-layouts: 0.25 us -> 3.93 us
    pallas_call x3 -> x6, Pallas kernels: 99 us -> 11.5 us  [the longest x2 4.26 us: pack_all(): pl.pallas_call(functools.partial(pack_all_kernel, parts, total // parts,...]
    all_to_all x0 -> x1, blocking collectives: none -> 29.6 us  [shards(): lax.all_to_all(packed[0], 'tensor', split_axis=0, concat_axis=0, tiled=True)]
    ppermute x0 -> x6, waiting for transfers between devices: none -> 23.8 us  [swap(): return lax.ppermute(block, axis, route)]
    ppermute x6 -> x8, waiting for transfers between devices: 25.1 us -> 12.8 us  [shift(): return lax.ppermute(block, axis, route)]
    all_to_all x3 -> x1, waiting for transfers between devices: 11.6 us -> 0.01 us  [shards(): lax.all_to_all(packed[0], 'tensor', split_axis=0, concat_axis=0, tiled=True)]
    all_to_all x3 -> x1, starting transfers between devices: 13.7 us -> 3.66 us  [shards(): lax.all_to_all(packed[0], 'tensor', split_axis=0, concat_axis=0, tiled=True)]
    ppermute x0 -> x6, starting transfers between devices: none -> 8.59 us  [swap(): return lax.ppermute(block, axis, route)]
    ppermute x6 -> x8, starting transfers between devices: 20 us -> 28.5 us  [shift(): return lax.ppermute(block, axis, route)]
  transfers between devices with their start and end apart: 9 -> 15, of which waited for: 6 -> 5; matrix products, arithmetic and copies ran while one was open for 0% -> 1% of each run, Pallas kernels for 43% -> 20%
where the time goes in v3:
time: 155 us; the launch traced here: 153 us
  Pallas kernels  41.1 us (27%)
  starting transfers between devices  40.7 us (26%)
  waiting for transfers between devices  36.6 us (24%)
  blocking collectives  29.6 us (19%)
  local copies, waits for them, and re-layouts  3.93 us (3%)
    all_to_all x1, blocking collectives, shards(): lax.all_to_all(packed[0], 'tensor', split_axis=0, concat_axis=0, tiled=True)  29.6 us
    pallas_call x4, Pallas kernels, attend(): pl.pallas_call(functools.partial(attend_kernel, rows, has_outs), grid=(he...  29.5 us
    ppermute x8, starting transfers between devices, shift(): return lax.ppermute(block, axis, route)  28.5 us
    ppermute x6, waiting for transfers between devices, swap(): return lax.ppermute(block, axis, route)  23.8 us
    ppermute x8, waiting for transfers between devices, shift(): return lax.ppermute(block, axis, route)  12.8 us
    ppermute x6, starting transfers between devices, swap(): return lax.ppermute(block, axis, route)  8.59 us
    pallas_call x2, Pallas kernels, pack_all(): pl.pallas_call(functools.partial(pack_all_kernel, parts, total // parts,...  4.26 us
    pallas_call x2, Pallas kernels, join(): pl.pallas_call(functools.partial(join_kernel, parts, total // parts, firs...  3.77 us
  transfers between devices with their start and end apart: 15, of which 5 were waited for; matrix products, arithmetic and copies ran while one was open for 1% of the time, Pallas kernels for 20%

profile of v3, /device:TPU:3, one launch (start us, length us, event | category | flops | bytes accessed | tf_op | source)
XLA Modules:
  0.0 152.9 jit_solution(1117128844144975406)
XLA Ops:
  0.6 2.1 %shard_map.85 = bf16[4,4,64,512]{3,2,1,0:T(8,128)(2,1)} custom-call(bf16[64,6144]{1,0:T(8,128)(2,1)} %refs_0_.11, bf16[64,6144]{1,0:T(8,128)(2,1)} %refs_1_.11, bf16[64,6144]{1,0:T(8,128)(2,1)} %refs_2_.11, bf16[64,6144]{1,0:T(8,128)(2,1)} %refs_3_.11), custom_call_target="tpu_custom_call" | custom-call | flops 1 | bytes 1 | tf_op jit(solution)/shard_map/pallas_call | solution.py:113
  2.8 29.6 %all_to_all.10.refs_4_.refs_2_ = bf16[4,4,64,512]{3,2,1,0:T(8,128)(2,1)} all-to-all(bf16[4,4,64,512]{3,2,1,0:T(8,128)(2,1)} %shard_map.85), channel_id=1, replica_groups=mesh['dp'=8,'tensor'=4] {'tensor'}, dimensions={0} | all-to-all | bytes 2097152 | tf_op jit(solution)/shard_map/all_to_all | solution.py:296
  32.3 2.1 %shard_map.86.refs_7_ = bf16[4,4,64,512]{3,2,1,0:T(8,128)(2,1)} custom-call(bf16[64,6144]{1,0:T(8,128)(2,1)} %refs_0_.11, bf16[64,6144]{1,0:T(8,128)(2,1)} %refs_1_.11, bf16[64,6144]{1,0:T(8,128)(2,1)} %refs_2_.11, bf16[64,6144]{1,0:T(8,128)(2,1)} %refs_3_.11, bf16[4,4,64,512]{3,2,1,0:T(8,128)(2,1)} %all_to_all.10.refs_4_.refs_2_), custom_call_target="tpu_custom_call" | custom-call | flops 1 | bytes 1 | tf_op jit(solution)/shard_map/pallas_call | solution.py:113
  34.5 3.7 %all-to-all-start.1 = ((bf16[4,4,64,512]{3,2,1,0:T(8,128)(2,1)}), bf16[4,4,64,512]{3,2,1,0:T(8,128)(2,1)S(1)}, u32[]{:S(2)}, u32[]{:S(2)}) async-start(bf16[4,4,64,512]{3,2,1,0:T(8,128)(2,1)} %shard_map.86.refs_7_), calls=%async_computation.1 | async-start | bytes 2097152 | tf_op jit(solution)/shard_map/all_to_all | solution.py:296
  38.2 4.8 %collective-permute-start.12 = (bf16[4,4,64,512]{3,2,1,0:T(8,128)(2,1)S(1)}, bf16[4,4,64,512]{3,2,1,0:T(8,128)(2,1)}, u32[]{:S(2)}, u32[]{:S(2)}) collective-permute-start(bf16[4,4,64,512]{3,2,1,0:T(8,128)(2,1)S(1)} %copy-done), channel_id=1, source_target_pairs={{0,4},{4,8},{8,12},{12,16},{16,20},{20,24},{24,28},{1,5},{5,9},{9,... | collective-permute-start | bytes 3145736 | tf_op jit(solution)/shard_map/ppermute | solution.py:29
  43.0 1.9 %collective-permute-start.13 = (bf16[4,4,64,512]{3,2,1,0:T(8,128)(2,1)S(1)}, bf16[4,4,64,512]{3,2,1,0:T(8,128)(2,1)}, u32[]{:S(2)}, u32[]{:S(2)}) collective-permute-start(bf16[4,4,64,512]{3,2,1,0:T(8,128)(2,1)S(1)} %copy-done), channel_id=1, source_target_pairs={{4,0},{8,4},{12,8},{16,12},{20,16},{24,20},{28,24},{5,1},{9,5},{13... | collective-permute-start | bytes 3145736 | tf_op jit(solution)/shard_map/ppermute | solution.py:29
  44.9 1.7 %shard_map.84 = (bf16[4,64,256]{2,1,0:T(8,128)(2,1)}, bf16[4,64,256]{2,1,0:T(8,128)(2,1)}, bf16[4,64,256]{2,1,0:T(8,128)(2,1)}) custom-call(bf16[64,6144]{1,0:T(8,128)(2,1)} %refs_0_.11, bf16[64,6144]{1,0:T(8,128)(2,1)} %refs_1_.11, bf16[64,6144]{1,0:T(8,128)(2,1)} %refs_2_.11, bf16[64,6144]{1,0:T(8,128)(2,1)} %refs_3_.11), custom_call_target="tpu_custom_call" | custom-call | flops 1 | bytes 1 | tf_op jit(solution)/shard_map/pallas_call | solution.py:71
  46.7 1.8 %collective-permute-start = (bf16[4,64,256]{2,1,0:T(8,128)(2,1)}, bf16[4,64,256]{2,1,0:T(8,128)(2,1)S(1)}, u32[]{:S(2)}, u32[]{:S(2)}) collective-permute-start(bf16[4,64,256]{2,1,0:T(8,128)(2,1)} %get-tuple-element.22), channel_id=1, source_target_pairs={{0,1},{1,0},{2,3},{3,2},{4,5},{5,4},{6,7},{7,6},{8,9},{9,8},{10,11... | collective-permute-start | bytes 393224 | tf_op jit(solution)/shard_map/ppermute | solution.py:34
  48.4 2.1 %collective-permute-start.1 = (bf16[4,64,256]{2,1,0:T(8,128)(2,1)}, bf16[4,64,256]{2,1,0:T(8,128)(2,1)S(1)}, u32[]{:S(2)}, u32[]{:S(2)}) collective-permute-start(bf16[4,64,256]{2,1,0:T(8,128)(2,1)} %get-tuple-element.23), channel_id=1, source_target_pairs={{0,2},{1,3},{2,0},{3,1},{4,6},{5,7},{6,4},{7,5},{8,10},{9,11},{10,... | collective-permute-start | bytes 393224 | tf_op jit(solution)/shard_map/ppermute | solution.py:34
  50.6 6.0 %collective-permute-done.refs_4_ = bf16[4,64,256]{2,1,0:T(8,128)(2,1)S(1)} collective-permute-done((bf16[4,64,256]{2,1,0:T(8,128)(2,1)}, bf16[4,64,256]{2,1,0:T(8,128)(2,1)S(1)}, u32[]{:S(2)}, u32[]{:S(2)}) %collective-permute-start) | collective-permute-done | bytes 131104 | tf_op jit(solution)/shard_map/ppermute | solution.py:34
  56.6 15.2 %collective-permute-done.1.refs_5_ = bf16[4,64,256]{2,1,0:T(8,128)(2,1)S(1)} collective-permute-done((bf16[4,64,256]{2,1,0:T(8,128)(2,1)}, bf16[4,64,256]{2,1,0:T(8,128)(2,1)S(1)}, u32[]{:S(2)}, u32[]{:S(2)}) %collective-permute-start.1) | collective-permute-done | bytes 131104 | tf_op jit(solution)/shard_map/ppermute | solution.py:34
  71.8 0.6 copy-done.10
  72.4 0.7 copy-done.11
  73.1 1.9 %shard_map.87.refs_4_.refs_2_ = bf16[4,4,64,256]{3,2,1,0:T(8,128)(2,1)} custom-call(bf16[64,6144]{1,0:T(8,128)(2,1)} %refs_0_.11, bf16[64,6144]{1,0:T(8,128)(2,1)} %refs_1_.11, bf16[64,6144]{1,0:T(8,128)(2,1)} %refs_2_.11, bf16[64,6144]{1,0:T(8,128)(2,1)} %refs_3_.11, bf16[4,64,256]{2,1,0:T(8,128)(2,1)} %copy-done.9, bf16[4,64,256]{2,1,0:T(8,128)(2,1)} %copy-done.10, ...), custom_call_target="tpu_custom_call" | custom-call | flops 1 | bytes 1 | tf_op jit(solution)/shard_map/pallas_call | solution.py:161
  75.0 1.8 %shard_map.88 = (bf16[4,64,256]{2,1,0:T(8,128)(2,1)}, bf16[4,64,256]{2,1,0:T(8,128)(2,1)}, bf16[4,64,256]{2,1,0:T(8,128)(2,1)}) custom-call(bf16[64,6144]{1,0:T(8,128)(2,1)} %refs_0_.11, bf16[64,6144]{1,0:T(8,128)(2,1)} %refs_1_.11, bf16[64,6144]{1,0:T(8,128)(2,1)} %refs_2_.11, bf16[64,6144]{1,0:T(8,128)(2,1)} %refs_3_.11, ...), custom_call_target="tpu_custom_call" | custom-call | flops 1 | bytes 1 | tf_op jit(solution)/shard_map/pallas_call | solution.py:71
  76.8 2.5 %collective-permute-start.3 = (bf16[4,64,256]{2,1,0:T(8,128)(2,1)}, bf16[4,64,256]{2,1,0:T(8,128)(2,1)S(1)}, u32[]{:S(2)}, u32[]{:S(2)}) collective-permute-start(bf16[4,64,256]{2,1,0:T(8,128)(2,1)} %get-tuple-element.25), channel_id=1, source_target_pairs={{0,1},{1,0},{2,3},{3,2},{4,5},{5,4},{6,7},{7,6},{8,9},{9,8},{10,11... | collective-permute-start | bytes 393224 | tf_op jit(solution)/shard_map/ppermute | solution.py:34
  79.3 2.2 %collective-permute-start.5 = (bf16[4,64,256]{2,1,0:T(8,128)(2,1)}, bf16[4,64,256]{2,1,0:T(8,128)(2,1)S(1)}, u32[]{:S(2)}, u32[]{:S(2)}) collective-permute-start(bf16[4,64,256]{2,1,0:T(8,128)(2,1)} %get-tuple-element.27), channel_id=1, source_target_pairs={{0,3},{1,2},{2,1},{3,0},{4,7},{5,6},{6,5},{7,4},{8,11},{9,10},{10,... | collective-permute-start | bytes 393224 | tf_op jit(solution)/shard_map/ppermute | solution.py:34
  81.8 6.4 %collective-permute-start.10 = (bf16[4,4,64,256]{3,2,1,0:T(8,128)(2,1)S(1)}, bf16[4,4,64,256]{3,2,1,0:T(8,128)(2,1)S(1)}, u32[]{:S(2)}, u32[]{:S(2)}) collective-permute-start(bf16[4,4,64,256]{3,2,1,0:T(8,128)(2,1)S(1)} %copy-done.1), channel_id=1, source_target_pairs={{0,4},{4,8},{8,12},{12,16},{16,20},{20,24},{24,28},{1,5},{5,9},{9,... | collective-permute-start | bytes 1572872 | tf_op jit(solution)/shard_map/ppermute | solution.py:29
  88.3 2.2 %collective-permute-done.4.refs_5_ = bf16[4,64,256]{2,1,0:T(8,128)(2,1)S(1)} collective-permute-done((bf16[4,64,256]{2,1,0:T(8,128)(2,1)}, bf16[4,64,256]{2,1,0:T(8,128)(2,1)S(1)}, u32[]{:S(2)}, u32[]{:S(2)}) %collective-permute-start.4) | collective-permute-done | bytes 131104 | tf_op jit(solution)/shard_map/ppermute | solution.py:34
  90.5 5.0 %collective-permute-start.8 = (bf16[4,4,64,512]{3,2,1,0:T(8,128)(2,1)S(1)}, bf16[4,4,64,512]{3,2,1,0:T(8,128)(2,1)}, u32[]{:S(2)}, u32[]{:S(2)}) collective-permute-start(bf16[4,4,64,512]{3,2,1,0:T(8,128)(2,1)S(1)} %all-to-all-done.1.refs_2_), channel_id=1, source_target_pairs={{0,4},{4,8},{8,12},{12,16},{16,20},{20,24},{24,28},{1,5},{5,9},{9,... | collective-permute-start | bytes 3145736 | tf_op jit(solution)/shard_map/ppermute | solution.py:29
  95.5 1.9 %collective-permute-start.9 = (bf16[4,4,64,512]{3,2,1,0:T(8,128)(2,1)S(1)}, bf16[4,4,64,512]{3,2,1,0:T(8,128)(2,1)}, u32[]{:S(2)}, u32[]{:S(2)}) collective-permute-start(bf16[4,4,64,512]{3,2,1,0:T(8,128)(2,1)S(1)} %all-to-all-done.1.refs_2_), channel_id=1, source_target_pairs={{4,0},{8,4},{12,8},{16,12},{20,16},{24,20},{28,24},{5,1},{9,5},{13... | collective-permute-start | bytes 3145736 | tf_op jit(solution)/shard_map/ppermute | solution.py:29
  97.5 2.5 %collective-permute-start.11 = (bf16[4,4,64,256]{3,2,1,0:T(8,128)(2,1)S(1)}, bf16[4,4,64,256]{3,2,1,0:T(8,128)(2,1)}, u32[]{:S(2)}, u32[]{:S(2)}) collective-permute-start(bf16[4,4,64,256]{3,2,1,0:T(8,128)(2,1)S(1)} %copy-done.1), channel_id=1, source_target_pairs={{4,0},{8,4},{12,8},{16,12},{20,16},{24,20},{28,24},{5,1},{9,5},{13... | collective-permute-start | bytes 1572872 | tf_op jit(solution)/shard_map/ppermute | solution.py:29
  100.1 1.9 %shard_map.89.refs_2_ = bf16[4,4,64,256]{3,2,1,0:T(8,128)(2,1)} custom-call(bf16[64,6144]{1,0:T(8,128)(2,1)} %refs_0_.11, bf16[64,6144]{1,0:T(8,128)(2,1)} %refs_1_.11, bf16[64,6144]{1,0:T(8,128)(2,1)} %refs_2_.11, bf16[64,6144]{1,0:T(8,128)(2,1)} %refs_3_.11, bf16[4,64,256]{2,1,0:T(8,128)(2,1)} %copy-done.6, bf16[4,64,256]{2,1,0:T(8,128)(2,1)} %copy-done.7, ...), custom_call_target="tpu_custom_call" | custom-call | flops 1 | bytes 1 | tf_op jit(solution)/shard_map/pallas_call | solution.py:161
  102.0 3.9 %collective-permute-start.6 = (bf16[4,4,64,256]{3,2,1,0:T(8,128)(2,1)}, bf16[4,4,64,256]{3,2,1,0:T(8,128)(2,1)S(1)}, u32[]{:S(2)}, u32[]{:S(2)}) collective-permute-start(bf16[4,4,64,256]{3,2,1,0:T(8,128)(2,1)} %shard_map.89.refs_2_), channel_id=1, source_target_pairs={{0,4},{4,8},{8,12},{12,16},{16,20},{20,24},{24,28},{1,5},{5,9},{9,... | collective-permute-start | bytes 1572872 | tf_op jit(solution)/shard_map/ppermute | solution.py:29
  106.0 1.9 %collective-permute-start.7 = (bf16[4,4,64,256]{3,2,1,0:T(8,128)(2,1)}, bf16[4,4,64,256]{3,2,1,0:T(8,128)(2,1)S(1)}, u32[]{:S(2)}, u32[]{:S(2)}) collective-permute-start(bf16[4,4,64,256]{3,2,1,0:T(8,128)(2,1)} %shard_map.89.refs_2_), channel_id=1, source_target_pairs={{4,0},{8,4},{12,8},{16,12},{20,16},{24,20},{28,24},{5,1},{9,5},{13... | collective-permute-start | bytes 1572872 | tf_op jit(solution)/shard_map/ppermute | solution.py:29
  108.0 1.0 broadcast_in_dim.6.refs_0_
  109.5 9.1 %shard_map.90 = (bf16[256,1536]{1,0:T(8,128)(2,1)}, bf16[256,1536]{1,0:T(8,128)(2,1)}, bf16[256,1536]{1,0:T(8,128)(2,1)}, bf16[256,1536]{1,0:T(8,128)(2,1)}) custom-call(s32[768,1]{1,0:T(8,128)} %broadcast_in_dim.6.refs_0_, s32[1,768]{1,0:T(1,128)} %broadcast_in_dim.5.refs_1_, bf16[4,4,64,512]{3,2,1,0:T(8,128)(2,1)} %all_to_all.10.refs_4_.refs_2_, ...), custom_call_target="tpu_custom_call" | custom-call | flops 1 | bytes 1 | tf_op jit(solution)/shard_map/pallas_call | solution.py:253
  118.7 12.8 %collective-permute-done.11.refs_4_ = bf16[4,4,64,256]{3,2,1,0:T(8,128)(2,1)} collective-permute-done((bf16[4,4,64,256]{3,2,1,0:T(8,128)(2,1)S(1)}, bf16[4,4,64,256]{3,2,1,0:T(8,128)(2,1)}, u32[]{:S(2)}, u32[]{:S(2)}) %collective-permute-start.11) | collective-permute-done | bytes 524320 | tf_op jit(solution)/shard_map/ppermute | solution.py:29
  131.5 5.6 %shard_map.91 = (bf16[256,1536]{1,0:T(8,128)(2,1)}, bf16[256,1536]{1,0:T(8,128)(2,1)}, bf16[256,1536]{1,0:T(8,128)(2,1)}, bf16[256,1536]{1,0:T(8,128)(2,1)}) custom-call(s32[768,1]{1,0:T(8,128)} %broadcast_in_dim.6.refs_0_, s32[1,768]{1,0:T(1,128)} %broadcast_in_dim.5.refs_1_, ...), custom_call_target="tpu_custom_call", output_to_operand_aliasing={{0}: (5, {}), {1}: (6, {}), {2}: (7, {}), {3}: (8, {})} | custom-call | flops 1 | bytes 1 | tf_op jit(solution)/shard_map/pallas_call | solution.py:253
  137.1 9.2 %shard_map.92 = (bf16[256,1536]{1,0:T(8,128)(2,1)}, bf16[256,1536]{1,0:T(8,128)(2,1)}, bf16[256,1536]{1,0:T(8,128)(2,1)}, bf16[256,1536]{1,0:T(8,128)(2,1)}) custom-call(s32[768,1]{1,0:T(8,128)} %broadcast_in_dim.6.refs_0_, s32[1,768]{1,0:T(1,128)} %broadcast_in_dim.5.refs_1_, ...), custom_call_target="tpu_custom_call", output_to_operand_aliasing={{0}: (5, {}), {1}: (6, {}), {2}: (7, {}), {3}: (8, {})} | custom-call | flops 1 | bytes 1 | tf_op jit(solution)/shard_map/pallas_call | solution.py:253
  146.3 0.8 copy-done.4
  147.3 5.6 %shard_map.93 = (bf16[256,1536]{1,0:T(8,128)(2,1)}, bf16[256,1536]{1,0:T(8,128)(2,1)}, bf16[256,1536]{1,0:T(8,128)(2,1)}, bf16[256,1536]{1,0:T(8,128)(2,1)}) custom-call(s32[768,1]{1,0:T(8,128)} %broadcast_in_dim.6.refs_0_, s32[1,768]{1,0:T(1,128)} %broadcast_in_dim.5.refs_1_, ...), custom_call_target="tpu_custom_call", output_to_operand_aliasing={{0}: (5, {}), {1}: (6, {}), {2}: (7, {}), {3}: (8, {})} | custom-call | flops 1 | bytes 1 | tf_op jit(solution)/shard_map/pallas_call | solution.py:253
  (38 shorter events, 1.4 us)
Async XLA Ops:
  34.5 3.7 %copy-start = (bf16[4,4,64,512]{3,2,1,0:T(8,128)(2,1)S(1)}, bf16[4,4,64,512]{3,2,1,0:T(8,128)(2,1)}, u32[]{:S(2)}) copy-start(bf16[4,4,64,512]{3,2,1,0:T(8,128)(2,1)} %all_to_all.10.refs_4_.refs_2_) | copy-start | bytes 3145732
  34.5 56.0 %all-to-all-start.1 = ((bf16[4,4,64,512]{3,2,1,0:T(8,128)(2,1)}), bf16[4,4,64,512]{3,2,1,0:T(8,128)(2,1)S(1)}, u32[]{:S(2)}, u32[]{:S(2)}) async-start(bf16[4,4,64,512]{3,2,1,0:T(8,128)(2,1)} %shard_map.86.refs_7_), calls=%async_computation.1 | async-start | bytes 2097152 | tf_op jit(solution)/shard_map/all_to_all | solution.py:296
  38.2 63.9 %collective-permute-start.12 = (bf16[4,4,64,512]{3,2,1,0:T(8,128)(2,1)S(1)}, bf16[4,4,64,512]{3,2,1,0:T(8,128)(2,1)}, u32[]{:S(2)}, u32[]{:S(2)}) collective-permute-start(bf16[4,4,64,512]{3,2,1,0:T(8,128)(2,1)S(1)} %copy-done), channel_id=1, source_target_pairs={{0,4},{4,8},{8,12},{12,16},{16,20},{20,24},{24,28},{1,5},{5,9},{9,... | collective-permute-start | bytes 3145736 | tf_op jit(solution)/shard_map/ppermute | solution.py:29
  43.0 63.0 %collective-permute-start.13 = (bf16[4,4,64,512]{3,2,1,0:T(8,128)(2,1)S(1)}, bf16[4,4,64,512]{3,2,1,0:T(8,128)(2,1)}, u32[]{:S(2)}, u32[]{:S(2)}) collective-permute-start(bf16[4,4,64,512]{3,2,1,0:T(8,128)(2,1)S(1)} %copy-done), channel_id=1, source_target_pairs={{4,0},{8,4},{12,8},{16,12},{20,16},{24,20},{28,24},{5,1},{9,5},{13... | collective-permute-start | bytes 3145736 | tf_op jit(solution)/shard_map/ppermute | solution.py:29
  46.7 9.9 %collective-permute-start = (bf16[4,64,256]{2,1,0:T(8,128)(2,1)}, bf16[4,64,256]{2,1,0:T(8,128)(2,1)S(1)}, u32[]{:S(2)}, u32[]{:S(2)}) collective-permute-start(bf16[4,64,256]{2,1,0:T(8,128)(2,1)} %get-tuple-element.22), channel_id=1, source_target_pairs={{0,1},{1,0},{2,3},{3,2},{4,5},{5,4},{6,7},{7,6},{8,9},{9,8},{10,11... | collective-permute-start | bytes 393224 | tf_op jit(solution)/shard_map/ppermute | solution.py:34
  48.4 23.4 %collective-permute-start.1 = (bf16[4,64,256]{2,1,0:T(8,128)(2,1)}, bf16[4,64,256]{2,1,0:T(8,128)(2,1)S(1)}, u32[]{:S(2)}, u32[]{:S(2)}) collective-permute-start(bf16[4,64,256]{2,1,0:T(8,128)(2,1)} %get-tuple-element.23), channel_id=1, source_target_pairs={{0,2},{1,3},{2,0},{3,1},{4,6},{5,7},{6,4},{7,5},{8,10},{9,11},{10,... | collective-permute-start | bytes 393224 | tf_op jit(solution)/shard_map/ppermute | solution.py:34
  50.5 21.3 %collective-permute-start.2 = (bf16[4,64,256]{2,1,0:T(8,128)(2,1)}, bf16[4,64,256]{2,1,0:T(8,128)(2,1)S(1)}, u32[]{:S(2)}, u32[]{:S(2)}) collective-permute-start(bf16[4,64,256]{2,1,0:T(8,128)(2,1)} %get-tuple-element.24), channel_id=1, source_target_pairs={{0,3},{1,2},{2,1},{3,0},{4,7},{5,6},{6,5},{7,4},{8,11},{9,10},{10,... | collective-permute-start | bytes 393224 | tf_op jit(solution)/shard_map/ppermute | solution.py:34
  56.6 15.2 %copy-start.9 = (bf16[4,64,256]{2,1,0:T(8,128)(2,1)}, bf16[4,64,256]{2,1,0:T(8,128)(2,1)S(1)}, u32[]{:S(2)}) copy-start(bf16[4,64,256]{2,1,0:T(8,128)(2,1)S(1)} %collective-permute-done.refs_4_) | copy-start | bytes 393220
  71.8 0.7 copy-start.10
  72.4 0.7 copy-start.11
  75.0 6.9 %copy-start.1 = (bf16[4,4,64,256]{3,2,1,0:T(8,128)(2,1)S(1)}, bf16[4,4,64,256]{3,2,1,0:T(8,128)(2,1)}, u32[]{:S(2)}) copy-start(bf16[4,4,64,256]{3,2,1,0:T(8,128)(2,1)} %shard_map.87.refs_4_.refs_2_) | copy-start | bytes 1572868
  76.8 5.1 %collective-permute-start.3 = (bf16[4,64,256]{2,1,0:T(8,128)(2,1)}, bf16[4,64,256]{2,1,0:T(8,128)(2,1)S(1)}, u32[]{:S(2)}, u32[]{:S(2)}) collective-permute-start(bf16[4,64,256]{2,1,0:T(8,128)(2,1)} %get-tuple-element.25), channel_id=1, source_target_pairs={{0,1},{1,0},{2,3},{3,2},{4,5},{5,4},{6,7},{7,6},{8,9},{9,8},{10,11... | collective-permute-start | bytes 393224 | tf_op jit(solution)/shard_map/ppermute | solution.py:34
  79.3 11.2 %collective-permute-start.4 = (bf16[4,64,256]{2,1,0:T(8,128)(2,1)}, bf16[4,64,256]{2,1,0:T(8,128)(2,1)S(1)}, u32[]{:S(2)}, u32[]{:S(2)}) collective-permute-start(bf16[4,64,256]{2,1,0:T(8,128)(2,1)} %get-tuple-element.26), channel_id=1, source_target_pairs={{0,2},{1,3},{2,0},{3,1},{4,6},{5,7},{6,4},{7,5},{8,10},{9,11},{10,... | collective-permute-start | bytes 393224 | tf_op jit(solution)/shard_map/ppermute | solution.py:34
  79.3 16.3 %collective-permute-start.5 = (bf16[4,64,256]{2,1,0:T(8,128)(2,1)}, bf16[4,64,256]{2,1,0:T(8,128)(2,1)S(1)}, u32[]{:S(2)}, u32[]{:S(2)}) collective-permute-start(bf16[4,64,256]{2,1,0:T(8,128)(2,1)} %get-tuple-element.27), channel_id=1, source_target_pairs={{0,3},{1,2},{2,1},{3,0},{4,7},{5,6},{6,5},{7,4},{8,11},{9,10},{10,... | collective-permute-start | bytes 393224 | tf_op jit(solution)/shard_map/ppermute | solution.py:34
  81.8 18.2 %copy-start.6 = (bf16[4,64,256]{2,1,0:T(8,128)(2,1)}, bf16[4,64,256]{2,1,0:T(8,128)(2,1)S(1)}, u32[]{:S(2)}) copy-start(bf16[4,64,256]{2,1,0:T(8,128)(2,1)S(1)} %collective-permute-done.3.refs_4_) | copy-start | bytes 393220
  81.8 15.6 %collective-permute-start.10 = (bf16[4,4,64,256]{3,2,1,0:T(8,128)(2,1)S(1)}, bf16[4,4,64,256]{3,2,1,0:T(8,128)(2,1)S(1)}, u32[]{:S(2)}, u32[]{:S(2)}) collective-permute-start(bf16[4,4,64,256]{3,2,1,0:T(8,128)(2,1)S(1)} %copy-done.1), channel_id=1, source_target_pairs={{0,4},{4,8},{8,12},{12,16},{16,20},{20,24},{24,28},{1,5},{5,9},{9,... | collective-permute-start | bytes 1572872 | tf_op jit(solution)/shard_map/ppermute | solution.py:29
  90.5 9.6 %copy-start.7 = (bf16[4,64,256]{2,1,0:T(8,128)(2,1)}, bf16[4,64,256]{2,1,0:T(8,128)(2,1)S(1)}, u32[]{:S(2)}) copy-start(bf16[4,64,256]{2,1,0:T(8,128)(2,1)S(1)} %collective-permute-done.4.refs_5_) | copy-start | bytes 393220
  90.5 11.5 %copy-start.2 = (bf16[4,4,64,512]{3,2,1,0:T(8,128)(2,1)}, bf16[4,4,64,512]{3,2,1,0:T(8,128)(2,1)S(1)}, u32[]{:S(2)}) copy-start(bf16[4,4,64,512]{3,2,1,0:T(8,128)(2,1)S(1)} %all-to-all-done.1.refs_2_) | copy-start | bytes 3145732
  90.5 46.6 %collective-permute-start.8 = (bf16[4,4,64,512]{3,2,1,0:T(8,128)(2,1)S(1)}, bf16[4,4,64,512]{3,2,1,0:T(8,128)(2,1)}, u32[]{:S(2)}, u32[]{:S(2)}) collective-permute-start(bf16[4,4,64,512]{3,2,1,0:T(8,128)(2,1)S(1)} %all-to-all-done.1.refs_2_), channel_id=1, source_target_pairs={{0,4},{4,8},{8,12},{12,16},{16,20},{20,24},{24,28},{1,5},{5,9},{9,... | collective-permute-start | bytes 3145736 | tf_op jit(solution)/shard_map/ppermute | solution.py:29
  95.5 4.5 %copy-start.8 = (bf16[4,64,256]{2,1,0:T(8,128)(2,1)}, bf16[4,64,256]{2,1,0:T(8,128)(2,1)S(1)}, u32[]{:S(2)}) copy-start(bf16[4,64,256]{2,1,0:T(8,128)(2,1)S(1)} %collective-permute-done.5.refs_6_) | copy-start | bytes 393220
  95.5 41.6 %collective-permute-start.9 = (bf16[4,4,64,512]{3,2,1,0:T(8,128)(2,1)S(1)}, bf16[4,4,64,512]{3,2,1,0:T(8,128)(2,1)}, u32[]{:S(2)}, u32[]{:S(2)}) collective-permute-start(bf16[4,4,64,512]{3,2,1,0:T(8,128)(2,1)S(1)} %all-to-all-done.1.refs_2_), channel_id=1, source_target_pairs={{4,0},{8,4},{12,8},{16,12},{20,16},{24,20},{28,24},{5,1},{9,5},{13... | collective-permute-start | bytes 3145736 | tf_op jit(solution)/shard_map/ppermute | solution.py:29
  97.5 4.5 %copy-start.3 = (bf16[4,4,64,256]{3,2,1,0:T(8,128)(2,1)}, bf16[4,4,64,256]{3,2,1,0:T(8,128)(2,1)S(1)}, u32[]{:S(2)}) copy-start(bf16[4,4,64,256]{3,2,1,0:T(8,128)(2,1)S(1)} %collective-permute-done.10.refs_3_) | copy-start | bytes 1572868
  97.5 34.0 %collective-permute-start.11 = (bf16[4,4,64,256]{3,2,1,0:T(8,128)(2,1)S(1)}, bf16[4,4,64,256]{3,2,1,0:T(8,128)(2,1)}, u32[]{:S(2)}, u32[]{:S(2)}) collective-permute-start(bf16[4,4,64,256]{3,2,1,0:T(8,128)(2,1)S(1)} %copy-done.1), channel_id=1, source_target_pairs={{4,0},{8,4},{12,8},{16,12},{20,16},{24,20},{28,24},{5,1},{9,5},{13... | collective-permute-start | bytes 1572872 | tf_op jit(solution)/shard_map/ppermute | solution.py:29
  102.0 5.9 %copy-start.12 = (s32[2048]{0:T(1024)S(1)}, s32[2048]{0:T(1024)}, u32[]{:S(2)}) copy-start(s32[2048]{0:T(1024)} %param.9) | copy-start | bytes 24580
  102.0 44.3 %collective-permute-start.6 = (bf16[4,4,64,256]{3,2,1,0:T(8,128)(2,1)}, bf16[4,4,64,256]{3,2,1,0:T(8,128)(2,1)S(1)}, u32[]{:S(2)}, u32[]{:S(2)}) collective-permute-start(bf16[4,4,64,256]{3,2,1,0:T(8,128)(2,1)} %shard_map.89.refs_2_), channel_id=1, source_target_pairs={{0,4},{4,8},{8,12},{12,16},{16,20},{20,24},{24,28},{1,5},{5,9},{9,... | collective-permute-start | bytes 1572872 | tf_op jit(solution)/shard_map/ppermute | solution.py:29
  106.0 40.3 %collective-permute-start.7 = (bf16[4,4,64,256]{3,2,1,0:T(8,128)(2,1)}, bf16[4,4,64,256]{3,2,1,0:T(8,128)(2,1)S(1)}, u32[]{:S(2)}, u32[]{:S(2)}) collective-permute-start(bf16[4,4,64,256]{3,2,1,0:T(8,128)(2,1)} %shard_map.89.refs_2_), channel_id=1, source_target_pairs={{4,0},{8,4},{12,8},{16,12},{20,16},{24,20},{28,24},{5,1},{9,5},{13... | collective-permute-start | bytes 1572872 | tf_op jit(solution)/shard_map/ppermute | solution.py:29
  146.3 0.8 copy-start.4
  146.3 1.0 copy-start.5

commit v4 on v3

--- a/solution.py
+++ b/solution.py
@@ -12,8 +12,9 @@
 SCALE = 1.0 / math.sqrt(HD)
 EXP2_SCALE = SCALE * math.log2(math.e)
 MASKED = -1e30
-CHUNKS = (("all", 4), ("pairs", 2), ("all", 4), ("pairs", 2))
+CHUNK_SHARES = (4, 4, 3, 1)
 VMEM_LIMIT = 60 * 1024 * 1024
+ATTEND_FLOPS = 2_500_000_000
 SMALL_COST = pl.CostEstimate(flops=1, bytes_accessed=1, transcendentals=0)
 
 
@@ -23,15 +24,25 @@
     return [(a, b - a) for a, b in zip(edges[:-1], edges[1:]) if b > a]
 
 
-def shift(block, axis, distance):
+def swap_pairs(block, axis, first):
     count = lax.axis_size(axis)
-    route = [(i, i + distance) for i in range(count) if 0 <= i + distance < count]
+    route = []
+    for low in range(first, count - 1, 2):
+        route += [(low, low + 1), (low + 1, low)]
     return lax.ppermute(block, axis, route)
 
 
-def swap(block, axis, flip):
-    route = [(i, i ^ flip) for i in range(lax.axis_size(axis))]
-    return lax.ppermute(block, axis, route)
+def nearby_ids(image_ids, rows):
+    shard = lax.axis_index("dp")
+    padded = jnp.pad(image_ids, (rows, rows), constant_values=-1)
+    odd = lax.rem(shard, 2)
+
+    def ids_of(other):
+        return lax.dynamic_slice_in_dim(padded, (other + 1) * rows, rows)
+
+    return jnp.concatenate(
+        (ids_of(shard + 1 - 2 * odd), ids_of(shard), ids_of(shard - 1 + 2 * odd))
+    )
 
 
 def columns(array, part, stride, first, width):
@@ -40,52 +51,6 @@
 
 
 def pack_kernel(parts, stride, first, width, deps, *refs):
-    arrays, refs = refs[:4], refs[4 + deps :]
-    packed, (stage, in_sems, out_sems) = refs[: parts - 1], refs[parts - 1 :]
-    me = lax.axis_index("tensor")
-    loads, stores = [], []
-    for flip in range(1, parts):
-        for index, array in enumerate(arrays):
-            load = pltpu.make_async_copy(
-                columns(array, me ^ flip, stride, first, width),
-                stage.at[flip - 1, index],
-                in_sems.at[(flip - 1) * 4 + index],
-            )
-            load.start()
-            loads.append(load)
-    for flip in range(1, parts):
-        for load in loads[(flip - 1) * 4 : flip * 4]:
-            load.wait()
-        store = pltpu.make_async_copy(
-            stage.at[flip - 1], packed[flip - 1], out_sems.at[flip - 1]
-        )
-        store.start()
-        stores.append(store)
-    for store in stores:
-        store.wait()
-
-
-def pack(arrays, parts, first, count, after):
-    rows, total = arrays[0].shape
-    width = count * HD
-    return pl.pallas_call(
-        functools.partial(
-            pack_kernel, parts, total // parts, first * HD, width, len(after)
-        ),
-        out_shape=[jax.ShapeDtypeStruct((4, rows, width), jnp.bfloat16)] * (parts - 1),
-        in_specs=[pl.BlockSpec(memory_space=pl.ANY)] * (4 + len(after)),
-        out_specs=[pl.BlockSpec(memory_space=pl.ANY)] * (parts - 1),
-        scratch_shapes=[
-            pltpu.VMEM((parts - 1, 4, rows, width), jnp.bfloat16),
-            pltpu.SemaphoreType.DMA(((parts - 1) * 4,)),
-            pltpu.SemaphoreType.DMA((parts - 1,)),
-        ],
-        compiler_params=pltpu.CompilerParams(vmem_limit_bytes=VMEM_LIMIT),
-        cost_estimate=SMALL_COST,
-    )(*arrays, *after)
-
-
-def pack_all_kernel(parts, stride, first, width, deps, *refs):
     arrays, (packed, stage, in_sems, out_sems) = refs[:4], refs[4 + deps :]
     loads, stores = [], []
     for part in range(parts):
@@ -107,12 +72,12 @@
         store.wait()
 
 
-def pack_all(arrays, parts, first, count, after):
+def pack(arrays, parts, first, count, after):
     rows, total = arrays[0].shape
     width = count * HD
     return pl.pallas_call(
         functools.partial(
-            pack_all_kernel, parts, total // parts, first * HD, width, len(after)
+            pack_kernel, parts, total // parts, first * HD, width, len(after)
         ),
         out_shape=jax.ShapeDtypeStruct((parts, 4, rows, width), jnp.bfloat16),
         in_specs=[pl.BlockSpec(memory_space=pl.ANY)] * (4 + len(after)),
@@ -175,6 +140,18 @@
     )(*arrays, *received, *after)
 
 
+def hold(array, after):
+    return pl.pallas_call(
+        lambda *refs: None,
+        out_shape=jax.ShapeDtypeStruct(array.shape, array.dtype),
+        in_specs=[pl.BlockSpec(memory_space=pl.ANY)] * (1 + len(after)),
+        out_specs=pl.BlockSpec(memory_space=pl.ANY),
+        input_output_aliases={0: 0},
+        compiler_params=pltpu.CompilerParams(vmem_limit_bytes=VMEM_LIMIT),
+        cost_estimate=SMALL_COST,
+    )(array, *after)
+
+
 def dot_nt(a, b):
     return lax.dot_general(a, b, (((1,), (1,)), ((), ())), preferred_element_type=jnp.float32)
 
@@ -266,7 +243,9 @@
         compiler_params=pltpu.CompilerParams(
             dimension_semantics=("arbitrary",), vmem_limit_bytes=VMEM_LIMIT
         ),
-        cost_estimate=SMALL_COST,
+        cost_estimate=pl.CostEstimate(
+            flops=heads * ATTEND_FLOPS, bytes_accessed=1, transcendentals=0
+        ),
     )(ids[:, None], ids[None, :], own, left, right, *(outs or ()))
 
 
@@ -275,35 +254,22 @@
     parts = lax.axis_size("tensor")
     rows = queries.shape[0] * parts
     head_total = queries.shape[1] // HD // parts
-    padded_ids = jnp.pad(image_ids, (rows, rows), constant_values=-1)
-    ids = lax.dynamic_slice_in_dim(padded_ids, lax.axis_index("dp") * rows, 3 * rows)
-    chunks = split_counts(head_total, [share for _, share in CHUNKS])
-    outs, owns, out_history, sent = None, [], [], []
-
-    def send(number):
-        first, count = chunks[number]
-        after = owns[number - 2 : number - 1] if number >= 2 else []
-        if CHUNKS[number][0] == "all":
-            sent.append([pack_all(arrays, parts, first, count, after)])
-        else:
-            sent.append(pack(arrays, parts, first, count, after))
-
-    send(0)
-    send(1)
+    ids = nearby_ids(image_ids, rows)
+    chunks = split_counts(head_total, CHUNK_SHARES)
+    outs, out_history, packed = None, [], []
+    for first, count in chunks[:2]:
+        packed.append(pack(arrays, parts, first, count, []))
     for number, (first, count) in enumerate(chunks):
-        packed = sent[number]
-        if CHUNKS[number][0] == "all":
-            own = lax.all_to_all(packed[0], "tensor", split_axis=0, concat_axis=0, tiled=True)
-        else:
-            received = [swap(packed[flip - 1], "tensor", flip) for flip in range(1, parts)]
-            after = [later[0] for later in sent[number + 1 : number + 2]]
-            own = join(arrays, received, first, after)
-        owns.append(own)
+        own = lax.all_to_all(packed[number], "tensor", split_axis=0, concat_axis=0, tiled=True)
+        after = packed[number + 1 : number + 2]
+        if number >= 2:
+            after.append(out_history[number - 2][0])
+        own = hold(own, after)
         if number + 2 < len(chunks):
-            send(number + 2)
-        left = shift(own, "dp", 1)
-        right = shift(own, "dp", -1)
-        outs = attend(ids, own, left, right, outs, first, head_total)
+            packed.append(pack(arrays, parts, *chunks[number + 2], [own]))
+        near = swap_pairs(own, "dp", 0)
+        far = swap_pairs(own, "dp", 1)
+        outs = attend(ids, own, near, far, outs, first, head_total)
         out_history.append(outs)
     return tuple(outs)
 

time: 155 us -> 126 us (0.81)
  blocking collectives: 29.6 us -> 0 us
  waiting for transfers between devices: 36.6 us -> 49.2 us
  starting transfers between devices: 40.7 us -> 31.9 us
  Pallas kernels: 41.1 us -> 37.3 us
  local copies, waits for them, and re-layouts: 3.93 us -> 5.65 us
    all_to_all x1 -> x4, waiting for transfers between devices: 0.01 us -> 42.6 us  [shards(): lax.all_to_all(packed[number], 'tensor', split_axis=0, concat_axis=0, til...]
    ppermute x14 -> x8, waiting for transfers between devices: 36.6 us -> 6.6 us  [swap_pairs(): return lax.ppermute(block, axis, route)]
    all_to_all x1 -> x0, blocking collectives: 29.6 us -> none  [shards(): lax.all_to_all(packed[0], 'tensor', split_axis=0, concat_axis=0, tiled=True)]
    ppermute x14 -> x8, starting transfers between devices: 37.1 us -> 16.4 us  [swap_pairs(): return lax.ppermute(block, axis, route)]
    all_to_all x1 -> x4, starting transfers between devices: 3.66 us -> 15.5 us  [shards(): lax.all_to_all(packed[number], 'tensor', split_axis=0, concat_axis=0, til...]
    pallas_call x4, Pallas kernels: 8.02 us -> 0.01 us  [hold(): pl.pallas_call(lambda *refs: None, out_shape=jax.ShapeDtypeStruct(array.s...]
    pallas_call x2 -> x4, Pallas kernels: 3.52 us -> 7.97 us  [pack(): pl.pallas_call(functools.partial(pack_kernel, parts, total // parts, firs...]
    unnamed x26 -> x20, local copies, waits for them, and re-layouts: 2.29 us -> 4.07 us
  transfers between devices with their start and end apart: 15 -> 12, of which waited for: 5 -> 5; matrix products, arithmetic and copies ran while one was open for 1% -> 1% of each run, Pallas kernels for 20% -> 25%
where the time goes in v4:
time: 126 us; the launch traced here: 125 us
  waiting for transfers between devices  49.2 us (39%)
  Pallas kernels  37.3 us (30%)
  starting transfers between devices  31.9 us (25%)
  local copies, waits for them, and re-layouts  5.65 us (4%)
    all_to_all x4, waiting for transfers between devices, shards(): lax.all_to_all(packed[number], 'tensor', split_axis=0, concat_axis=0, til...  42.6 us
    pallas_call x4, Pallas kernels, attend(): pl.pallas_call(functools.partial(attend_kernel, rows, has_outs), grid=(he...  29.3 us
    ppermute x8, starting transfers between devices, swap_pairs(): return lax.ppermute(block, axis, route)  16.4 us
    all_to_all x4, starting transfers between devices, shards(): lax.all_to_all(packed[number], 'tensor', split_axis=0, concat_axis=0, til...  15.5 us
    pallas_call x4, Pallas kernels, pack(): pl.pallas_call(functools.partial(pack_kernel, parts, total // parts, firs...  7.97 us
    ppermute x8, waiting for transfers between devices, swap_pairs(): return lax.ppermute(block, axis, route)  6.6 us
    unnamed x20, local copies, waits for them, and re-layouts  4.07 us
  transfers between devices with their start and end apart: 12, of which 5 were waited for; matrix products, arithmetic and copies ran while one was open for 1% of the time, Pallas kernels for 25%

profile of v4, /device:TPU:3, one launch (start us, length us, event | category | flops | bytes accessed | tf_op | source)
XLA Modules:
  0.0 124.9 jit_solution(16115821902323907969)
XLA Ops:
  0.6 2.1 %shard_map.85 = bf16[4,4,64,512]{3,2,1,0:T(8,128)(2,1)} custom-call(bf16[64,6144]{1,0:T(8,128)(2,1)} %refs_0_.7, bf16[64,6144]{1,0:T(8,128)(2,1)} %refs_1_.7, bf16[64,6144]{1,0:T(8,128)(2,1)} %refs_2_.7, bf16[64,6144]{1,0:T(8,128)(2,1)} %refs_3_.7), custom_call_target="tpu_custom_call" | custom-call | flops 1 | bytes 1 | tf_op jit(solution)/shard_map/pallas_call | solution.py:78
  2.8 4.6 %all-to-all-start.1 = ((bf16[4,4,64,512]{3,2,1,0:T(8,128)(2,1)}), bf16[4,4,64,512]{3,2,1,0:T(8,128)(2,1)S(1)}, u32[]{:S(2)}, u32[]{:S(2)}) async-start(bf16[4,4,64,512]{3,2,1,0:T(8,128)(2,1)} %shard_map.85), calls=%async_computation.1 | async-start | bytes 2097152 | tf_op jit(solution)/shard_map/all_to_all | solution.py:263
  7.4 2.1 %shard_map.84.refs_1_ = bf16[4,4,64,512]{3,2,1,0:T(8,128)(2,1)} custom-call(bf16[64,6144]{1,0:T(8,128)(2,1)} %refs_0_.7, bf16[64,6144]{1,0:T(8,128)(2,1)} %refs_1_.7, bf16[64,6144]{1,0:T(8,128)(2,1)} %refs_2_.7, bf16[64,6144]{1,0:T(8,128)(2,1)} %refs_3_.7), custom_call_target="tpu_custom_call" | custom-call | flops 1 | bytes 1 | tf_op jit(solution)/shard_map/pallas_call | solution.py:78
  9.5 23.1 %all-to-all-done.1.refs_0_ = bf16[4,4,64,512]{3,2,1,0:T(8,128)(2,1)S(1)} async-done(((bf16[4,4,64,512]{3,2,1,0:T(8,128)(2,1)}), bf16[4,4,64,512]{3,2,1,0:T(8,128)(2,1)S(1)}, u32[]{:S(2)}, u32[]{:S(2)}) %all-to-all-start.1) | async-done | bytes 1048608 | tf_op jit(solution)/shard_map/all_to_all | solution.py:263
  32.6 3.5 %all-to-all-start = ((bf16[4,4,64,512]{3,2,1,0:T(8,128)(2,1)}), bf16[4,4,64,512]{3,2,1,0:T(8,128)(2,1)S(1)}, u32[]{:S(2)}, u32[]{:S(2)}) async-start(bf16[4,4,64,512]{3,2,1,0:T(8,128)(2,1)} %shard_map.84.refs_1_), calls=%async_computation | async-start | bytes 2097152 | tf_op jit(solution)/shard_map/all_to_all | solution.py:263
  36.2 1.5 %collective-permute-start.2 = (bf16[4,4,64,512]{3,2,1,0:T(8,128)(2,1)}, bf16[4,4,64,512]{3,2,1,0:T(8,128)(2,1)S(1)}, u32[]{:S(2)}, u32[]{:S(2)}) collective-permute-start(bf16[4,4,64,512]{3,2,1,0:T(8,128)(2,1)} %shard_map.86.refs_4_.refs_2_), channel_id=1, source_target_pairs={{0,4},{4,0},{8,12},{12,8},{16,20},{20,16},{24,28},{28,24},{1,5},{5... | collective-permute-start | bytes 3145736 | tf_op jit(solution)/shard_map/ppermute | solution.py:32
  37.7 3.0 %collective-permute-start.3 = (bf16[4,4,64,512]{3,2,1,0:T(8,128)(2,1)}, bf16[4,4,64,512]{3,2,1,0:T(8,128)(2,1)}, u32[]{:S(2)}, u32[]{:S(2)}) collective-permute-start(bf16[4,4,64,512]{3,2,1,0:T(8,128)(2,1)} %shard_map.86.refs_4_.refs_2_), channel_id=1, source_target_pairs={{4,8},{8,4},{12,16},{16,12},{20,24},{24,20},{5,9},{9,5},{13,17},{1... | collective-permute-start | bytes 3145736 | tf_op jit(solution)/shard_map/ppermute | solution.py:32
  40.7 2.0 %shard_map.87.refs_1_ = bf16[4,4,64,384]{3,2,1,0:T(8,128)(2,1)} custom-call(bf16[64,6144]{1,0:T(8,128)(2,1)} %refs_0_.7, bf16[64,6144]{1,0:T(8,128)(2,1)} %refs_1_.7, bf16[64,6144]{1,0:T(8,128)(2,1)} %refs_2_.7, bf16[64,6144]{1,0:T(8,128)(2,1)} %refs_3_.7, bf16[4,4,64,512]{3,2,1,0:T(8,128)(2,1)} %shard_map.86.refs_4_.refs_2_), custom_call_target="tpu_custom_call" | custom-call | flops 1 | bytes 1 | tf_op jit(solution)/shard_map/pallas_call | solution.py:78
  42.7 18.6 %all-to-all-done.refs_0_ = bf16[4,4,64,512]{3,2,1,0:T(8,128)(2,1)S(1)} async-done(((bf16[4,4,64,512]{3,2,1,0:T(8,128)(2,1)}), bf16[4,4,64,512]{3,2,1,0:T(8,128)(2,1)S(1)}, u32[]{:S(2)}, u32[]{:S(2)}) %all-to-all-start) | async-done | bytes 1048608 | tf_op jit(solution)/shard_map/all_to_all | solution.py:263
  61.3 3.5 %all-to-all-start.3 = ((bf16[4,4,64,384]{3,2,1,0:T(8,128)(2,1)}), bf16[4,4,64,384]{3,2,1,0:T(8,128)(2,1)S(1)}, u32[]{:S(2)}, u32[]{:S(2)}) async-start(bf16[4,4,64,384]{3,2,1,0:T(8,128)(2,1)} %shard_map.87.refs_1_), calls=%async_computation.3 | async-start | bytes 1572864 | tf_op jit(solution)/shard_map/all_to_all | solution.py:263
  64.8 0.7 copy-done.4
  65.6 1.5 %collective-permute-start = (bf16[4,4,64,512]{3,2,1,0:T(8,128)(2,1)}, bf16[4,4,64,512]{3,2,1,0:T(8,128)(2,1)}, u32[]{:S(2)}, u32[]{:S(2)}) collective-permute-start(bf16[4,4,64,512]{3,2,1,0:T(8,128)(2,1)} %shard_map.88.refs_4_.refs_2_), channel_id=1, source_target_pairs={{0,4},{4,0},{8,12},{12,8},{16,20},{20,16},{24,28},{28,24},{1,5},{5... | collective-permute-start | bytes 3145736 | tf_op jit(solution)/shard_map/ppermute | solution.py:32
  67.1 3.0 %collective-permute-start.1 = (bf16[4,4,64,512]{3,2,1,0:T(8,128)(2,1)}, bf16[4,4,64,512]{3,2,1,0:T(8,128)(2,1)}, u32[]{:S(2)}, u32[]{:S(2)}) collective-permute-start(bf16[4,4,64,512]{3,2,1,0:T(8,128)(2,1)} %shard_map.88.refs_4_.refs_2_), channel_id=1, source_target_pairs={{4,8},{8,4},{12,16},{16,12},{20,24},{24,20},{5,9},{9,5},{13,17},{1... | collective-permute-start | bytes 3145736 | tf_op jit(solution)/shard_map/ppermute | solution.py:32
  70.2 0.9 broadcast_in_dim.6.refs_0_
  71.1 0.6 broadcast_in_dim.5.refs_1_
  71.6 1.7 %shard_map.89.refs_1_ = bf16[4,4,64,128]{3,2,1,0:T(8,128)(2,1)} custom-call(bf16[64,6144]{1,0:T(8,128)(2,1)} %refs_0_.7, bf16[64,6144]{1,0:T(8,128)(2,1)} %refs_1_.7, bf16[64,6144]{1,0:T(8,128)(2,1)} %refs_2_.7, bf16[64,6144]{1,0:T(8,128)(2,1)} %refs_3_.7, bf16[4,4,64,512]{3,2,1,0:T(8,128)(2,1)} %shard_map.88.refs_4_.refs_2_), custom_call_target="tpu_custom_call" | custom-call | flops 1 | bytes 1 | tf_op jit(solution)/shard_map/pallas_call | solution.py:78
  73.4 0.9 copy-done.5
  74.3 9.1 %shard_map.90 = (bf16[256,1536]{1,0:T(8,128)(2,1)}, bf16[256,1536]{1,0:T(8,128)(2,1)}, bf16[256,1536]{1,0:T(8,128)(2,1)}, bf16[256,1536]{1,0:T(8,128)(2,1)}) custom-call(s32[768,1]{1,0:T(8,128)} %broadcast_in_dim.6.refs_0_, s32[1,768]{1,0:T(1,128)} %broadcast_in_dim.5.refs_1_, bf16[4,4,64,512]{3,2,1,0:T(8,128)(2,1)} %shard_map.86.refs_4_.refs_2_, ...), custom_call_target="tpu_custom_call" | custom-call | flops 10000000000 | bytes 1 | tf_op jit(solution)/shard_map/pallas_call | solution.py:230
  83.5 0.9 all-to-all-done.3.refs_0_
  84.4 3.9 %all-to-all-start.2 = ((bf16[4,4,64,128]{3,2,1,0:T(8,128)(2,1)}), bf16[4,4,64,128]{3,2,1,0:T(8,128)(2,1)S(1)}, u32[]{:S(2)}, u32[]{:S(2)}) async-start(bf16[4,4,64,128]{3,2,1,0:T(8,128)(2,1)} %shard_map.89.refs_1_), calls=%async_computation.2 | async-start | bytes 524288 | tf_op jit(solution)/shard_map/all_to_all | solution.py:263
  88.3 1.1 collective-permute-start.6
  89.3 3.1 %collective-permute-start.7 = (bf16[4,4,64,384]{3,2,1,0:T(8,128)(2,1)}, bf16[4,4,64,384]{3,2,1,0:T(8,128)(2,1)S(1)}, u32[]{:S(2)}, u32[]{:S(2)}) collective-permute-start(bf16[4,4,64,384]{3,2,1,0:T(8,128)(2,1)} %shard_map.93.refs_2_), channel_id=1, source_target_pairs={{4,8},{8,4},{12,16},{16,12},{20,24},{24,20},{5,9},{9,5},{13,17},{1... | collective-permute-start | bytes 2359304 | tf_op jit(solution)/shard_map/ppermute | solution.py:32
  92.5 2.9 %collective-permute-done.1.refs_4_ = bf16[4,4,64,512]{3,2,1,0:T(8,128)(2,1)} collective-permute-done((bf16[4,4,64,512]{3,2,1,0:T(8,128)(2,1)}, bf16[4,4,64,512]{3,2,1,0:T(8,128)(2,1)}, u32[]{:S(2)}, u32[]{:S(2)}) %collective-permute-start.1) | collective-permute-done | bytes 1048608 | tf_op jit(solution)/shard_map/ppermute | solution.py:32
  95.4 9.1 %shard_map.91 = (bf16[256,1536]{1,0:T(8,128)(2,1)}, bf16[256,1536]{1,0:T(8,128)(2,1)}, bf16[256,1536]{1,0:T(8,128)(2,1)}, bf16[256,1536]{1,0:T(8,128)(2,1)}) custom-call(s32[768,1]{1,0:T(8,128)} %broadcast_in_dim.6.refs_0_, s32[1,768]{1,0:T(1,128)} %broadcast_in_dim.5.refs_1_, ...), custom_call_target="tpu_custom_call", output_to_operand_aliasing={{0}: (5, {}), {1}: (6, {}), {2}: (7, {}), {3}: (8, {})} | custom-call | flops 10000000000 | bytes 1 | tf_op jit(solution)/shard_map/pallas_call | solution.py:230
  104.6 0.7 copy-done.3
  105.3 3.1 %collective-permute-start.5 = (bf16[4,4,64,128]{3,2,1,0:T(8,128)(2,1)}, bf16[4,4,64,128]{3,2,1,0:T(8,128)(2,1)S(1)}, u32[]{:S(2)}, u32[]{:S(2)}) collective-permute-start(bf16[4,4,64,128]{3,2,1,0:T(8,128)(2,1)} %shard_map.92.refs_2_), channel_id=1, source_target_pairs={{4,8},{8,4},{12,16},{16,12},{20,24},{24,20},{5,9},{9,5},{13,17},{1... | collective-permute-start | bytes 786440 | tf_op jit(solution)/shard_map/ppermute | solution.py:32
  108.5 3.6 %collective-permute-done.7.refs_4_ = bf16[4,4,64,384]{3,2,1,0:T(8,128)(2,1)S(1)} collective-permute-done((bf16[4,4,64,384]{3,2,1,0:T(8,128)(2,1)}, bf16[4,4,64,384]{3,2,1,0:T(8,128)(2,1)S(1)}, u32[]{:S(2)}, u32[]{:S(2)}) %collective-permute-start.7) | collective-permute-done | bytes 786464 | tf_op jit(solution)/shard_map/ppermute | solution.py:32
  112.1 0.9 copy-done.7
  113.1 7.4 %shard_map.94 = (bf16[256,1536]{1,0:T(8,128)(2,1)}, bf16[256,1536]{1,0:T(8,128)(2,1)}, bf16[256,1536]{1,0:T(8,128)(2,1)}, bf16[256,1536]{1,0:T(8,128)(2,1)}) custom-call(s32[768,1]{1,0:T(8,128)} %broadcast_in_dim.6.refs_0_, s32[1,768]{1,0:T(1,128)} %broadcast_in_dim.5.refs_1_, ...), custom_call_target="tpu_custom_call", output_to_operand_aliasing={{0}: (5, {}), {1}: (6, {}), {2}: (7, {}), {3}: (8, {})} | custom-call | flops 7500000256 | bytes 1 | tf_op jit(solution)/shard_map/pallas_call | solution.py:230
  120.5 0.7 copy-done.8
  121.1 0.1 copy-done.9
  121.2 3.6 %shard_map.95 = (bf16[256,1536]{1,0:T(8,128)(2,1)}, bf16[256,1536]{1,0:T(8,128)(2,1)}, bf16[256,1536]{1,0:T(8,128)(2,1)}, bf16[256,1536]{1,0:T(8,128)(2,1)}) custom-call(s32[768,1]{1,0:T(8,128)} %broadcast_in_dim.6.refs_0_, s32[1,768]{1,0:T(1,128)} %broadcast_in_dim.5.refs_1_, ...), custom_call_target="tpu_custom_call", output_to_operand_aliasing={{0}: (5, {}), {1}: (6, {}), {2}: (7, {}), {3}: (8, {})} | custom-call | flops 2500000000 | bytes 1 | tf_op jit(solution)/shard_map/pallas_call | solution.py:230
  (28 shorter events, 0.2 us)
Async XLA Ops:
  2.8 29.8 %all-to-all-start.1 = ((bf16[4,4,64,512]{3,2,1,0:T(8,128)(2,1)}), bf16[4,4,64,512]{3,2,1,0:T(8,128)(2,1)S(1)}, u32[]{:S(2)}, u32[]{:S(2)}) async-start(bf16[4,4,64,512]{3,2,1,0:T(8,128)(2,1)} %shard_map.85), calls=%async_computation.1 | async-start | bytes 2097152 | tf_op jit(solution)/shard_map/all_to_all | solution.py:263
  32.6 3.5 %copy-start = (bf16[4,4,64,512]{3,2,1,0:T(8,128)(2,1)}, bf16[4,4,64,512]{3,2,1,0:T(8,128)(2,1)S(1)}, u32[]{:S(2)}) copy-start(bf16[4,4,64,512]{3,2,1,0:T(8,128)(2,1)S(1)} %all-to-all-done.1.refs_0_) | copy-start | bytes 3145732
  32.6 28.7 %all-to-all-start = ((bf16[4,4,64,512]{3,2,1,0:T(8,128)(2,1)}), bf16[4,4,64,512]{3,2,1,0:T(8,128)(2,1)S(1)}, u32[]{:S(2)}, u32[]{:S(2)}) async-start(bf16[4,4,64,512]{3,2,1,0:T(8,128)(2,1)} %shard_map.84.refs_1_), calls=%async_computation | async-start | bytes 2097152 | tf_op jit(solution)/shard_map/all_to_all | solution.py:263
  36.2 37.2 %collective-permute-start.2 = (bf16[4,4,64,512]{3,2,1,0:T(8,128)(2,1)}, bf16[4,4,64,512]{3,2,1,0:T(8,128)(2,1)S(1)}, u32[]{:S(2)}, u32[]{:S(2)}) collective-permute-start(bf16[4,4,64,512]{3,2,1,0:T(8,128)(2,1)} %shard_map.86.refs_4_.refs_2_), channel_id=1, source_target_pairs={{0,4},{4,0},{8,12},{12,8},{16,20},{20,16},{24,28},{28,24},{1,5},{5... | collective-permute-start | bytes 3145736 | tf_op jit(solution)/shard_map/ppermute | solution.py:32
  37.7 35.7 %collective-permute-start.3 = (bf16[4,4,64,512]{3,2,1,0:T(8,128)(2,1)}, bf16[4,4,64,512]{3,2,1,0:T(8,128)(2,1)}, u32[]{:S(2)}, u32[]{:S(2)}) collective-permute-start(bf16[4,4,64,512]{3,2,1,0:T(8,128)(2,1)} %shard_map.86.refs_4_.refs_2_), channel_id=1, source_target_pairs={{4,8},{8,4},{12,16},{16,12},{20,24},{24,20},{5,9},{9,5},{13,17},{1... | collective-permute-start | bytes 3145736 | tf_op jit(solution)/shard_map/ppermute | solution.py:32
  61.3 4.3 %copy-start.1 = (bf16[4,4,64,512]{3,2,1,0:T(8,128)(2,1)}, bf16[4,4,64,512]{3,2,1,0:T(8,128)(2,1)S(1)}, u32[]{:S(2)}) copy-start(bf16[4,4,64,512]{3,2,1,0:T(8,128)(2,1)S(1)} %all-to-all-done.refs_0_) | copy-start | bytes 3145732
  61.3 23.1 %all-to-all-start.3 = ((bf16[4,4,64,384]{3,2,1,0:T(8,128)(2,1)}), bf16[4,4,64,384]{3,2,1,0:T(8,128)(2,1)S(1)}, u32[]{:S(2)}, u32[]{:S(2)}) async-start(bf16[4,4,64,384]{3,2,1,0:T(8,128)(2,1)} %shard_map.87.refs_1_), calls=%async_computation.3 | async-start | bytes 1572864 | tf_op jit(solution)/shard_map/all_to_all | solution.py:263
  64.8 0.7 copy-start.4
  65.6 26.9 %collective-permute-start = (bf16[4,4,64,512]{3,2,1,0:T(8,128)(2,1)}, bf16[4,4,64,512]{3,2,1,0:T(8,128)(2,1)}, u32[]{:S(2)}, u32[]{:S(2)}) collective-permute-start(bf16[4,4,64,512]{3,2,1,0:T(8,128)(2,1)} %shard_map.88.refs_4_.refs_2_), channel_id=1, source_target_pairs={{0,4},{4,0},{8,12},{12,8},{16,20},{20,16},{24,28},{28,24},{1,5},{5... | collective-permute-start | bytes 3145736 | tf_op jit(solution)/shard_map/ppermute | solution.py:32
  67.1 28.3 %collective-permute-start.1 = (bf16[4,4,64,512]{3,2,1,0:T(8,128)(2,1)}, bf16[4,4,64,512]{3,2,1,0:T(8,128)(2,1)}, u32[]{:S(2)}, u32[]{:S(2)}) collective-permute-start(bf16[4,4,64,512]{3,2,1,0:T(8,128)(2,1)} %shard_map.88.refs_4_.refs_2_), channel_id=1, source_target_pairs={{4,8},{8,4},{12,16},{16,12},{20,24},{24,20},{5,9},{9,5},{13,17},{1... | collective-permute-start | bytes 3145736 | tf_op jit(solution)/shard_map/ppermute | solution.py:32
  73.4 1.0 copy-start.5
  84.4 3.9 %copy-start.2 = (bf16[4,4,64,384]{3,2,1,0:T(8,128)(2,1)}, bf16[4,4,64,384]{3,2,1,0:T(8,128)(2,1)S(1)}, u32[]{:S(2)}) copy-start(bf16[4,4,64,384]{3,2,1,0:T(8,128)(2,1)S(1)} %all-to-all-done.3.refs_0_) | copy-start | bytes 2359300
  84.4 20.2 %all-to-all-start.2 = ((bf16[4,4,64,128]{3,2,1,0:T(8,128)(2,1)}), bf16[4,4,64,128]{3,2,1,0:T(8,128)(2,1)S(1)}, u32[]{:S(2)}, u32[]{:S(2)}) async-start(bf16[4,4,64,128]{3,2,1,0:T(8,128)(2,1)} %shard_map.89.refs_1_), calls=%async_computation.2 | async-start | bytes 524288 | tf_op jit(solution)/shard_map/all_to_all | solution.py:263
  88.3 20.2 %collective-permute-start.6 = (bf16[4,4,64,384]{3,2,1,0:T(8,128)(2,1)}, bf16[4,4,64,384]{3,2,1,0:T(8,128)(2,1)S(1)}, u32[]{:S(2)}, u32[]{:S(2)}) collective-permute-start(bf16[4,4,64,384]{3,2,1,0:T(8,128)(2,1)} %shard_map.93.refs_2_), channel_id=1, source_target_pairs={{0,4},{4,0},{8,12},{12,8},{16,20},{20,16},{24,28},{28,24},{1,5},{5... | collective-permute-start | bytes 2359304 | tf_op jit(solution)/shard_map/ppermute | solution.py:32
  89.3 22.8 %collective-permute-start.7 = (bf16[4,4,64,384]{3,2,1,0:T(8,128)(2,1)}, bf16[4,4,64,384]{3,2,1,0:T(8,128)(2,1)S(1)}, u32[]{:S(2)}, u32[]{:S(2)}) collective-permute-start(bf16[4,4,64,384]{3,2,1,0:T(8,128)(2,1)} %shard_map.93.refs_2_), channel_id=1, source_target_pairs={{4,8},{8,4},{12,16},{16,12},{20,24},{24,20},{5,9},{9,5},{13,17},{1... | collective-permute-start | bytes 2359304 | tf_op jit(solution)/shard_map/ppermute | solution.py:32
  104.6 0.7 copy-start.3
  105.3 15.1 %collective-permute-start.4 = (bf16[4,4,64,128]{3,2,1,0:T(8,128)(2,1)}, bf16[4,4,64,128]{3,2,1,0:T(8,128)(2,1)S(1)}, u32[]{:S(2)}, u32[]{:S(2)}) collective-permute-start(bf16[4,4,64,128]{3,2,1,0:T(8,128)(2,1)} %shard_map.92.refs_2_), channel_id=1, source_target_pairs={{0,4},{4,0},{8,12},{12,8},{16,20},{20,16},{24,28},{28,24},{1,5},{5... | collective-permute-start | bytes 786440 | tf_op jit(solution)/shard_map/ppermute | solution.py:32
  105.3 15.1 %collective-permute-start.5 = (bf16[4,4,64,128]{3,2,1,0:T(8,128)(2,1)}, bf16[4,4,64,128]{3,2,1,0:T(8,128)(2,1)S(1)}, u32[]{:S(2)}, u32[]{:S(2)}) collective-permute-start(bf16[4,4,64,128]{3,2,1,0:T(8,128)(2,1)} %shard_map.92.refs_2_), channel_id=1, source_target_pairs={{4,8},{8,4},{12,16},{16,12},{20,24},{24,20},{5,9},{9,5},{13,17},{1... | collective-permute-start | bytes 786440 | tf_op jit(solution)/shard_map/ppermute | solution.py:32
  108.5 3.7 %copy-start.6 = (bf16[4,4,64,384]{3,2,1,0:T(8,128)(2,1)}, bf16[4,4,64,384]{3,2,1,0:T(8,128)(2,1)S(1)}, u32[]{:S(2)}) copy-start(bf16[4,4,64,384]{3,2,1,0:T(8,128)(2,1)S(1)} %collective-permute-done.6.refs_3_) | copy-start | bytes 2359300
  112.1 0.9 copy-start.7
  120.4 0.7 copy-start.8
  120.5 0.8 copy-start.9

commit v5 on v4

--- a/solution.py
+++ b/solution.py
@@ -9,12 +9,14 @@
 from jax.sharding import PartitionSpec as P
 
 HD = 128
+BLOCK = 64
+WINDOW = 384
 SCALE = 1.0 / math.sqrt(HD)
 EXP2_SCALE = SCALE * math.log2(math.e)
 MASKED = -1e30
 CHUNK_SHARES = (4, 4, 3, 1)
 VMEM_LIMIT = 60 * 1024 * 1024
-ATTEND_FLOPS = 2_500_000_000
+ATTEND_FLOPS = 1_500_000_000
 SMALL_COST = pl.CostEstimate(flops=1, bytes_accessed=1, transcendentals=0)
 
 
@@ -40,9 +42,7 @@
     def ids_of(other):
         return lax.dynamic_slice_in_dim(padded, (other + 1) * rows, rows)
 
-    return jnp.concatenate(
-        (ids_of(shard + 1 - 2 * odd), ids_of(shard), ids_of(shard - 1 + 2 * odd))
-    )
+    return ids_of(shard), ids_of(shard + 1 - 2 * odd), ids_of(shard - 1 + 2 * odd)
 
 
 def columns(array, part, stride, first, width):
@@ -164,61 +164,87 @@
     return jnp.dot(a, b, preferred_element_type=jnp.float32)
 
 
-def probs_and_grads(queries, grads, keys, values, bias):
+def attention(queries, keys, values, grads, bias, count):
     scores = dot_nt(queries, keys) + bias
     row_max = jnp.max(scores, axis=1, keepdims=True)
     weights = jnp.exp2((scores - row_max) * EXP2_SCALE)
     probs = weights * (1.0 / jnp.sum(weights, axis=1, keepdims=True))
     grad_probs = dot_nt(grads, values)
     inner = jnp.sum(probs * grad_probs, axis=1, keepdims=True)
-    grad_scores = probs * (grad_probs - inner)
-    return probs.astype(jnp.bfloat16), grad_scores.astype(jnp.bfloat16)
+    low = probs.astype(jnp.bfloat16)
+    grad_scores = (probs * (grad_probs - inner)).astype(jnp.bfloat16)
+    results = (
+        dot_nn(low[:count], values),
+        dot_nn(grad_scores[:count], keys) * SCALE,
+        dot_tn(grad_scores[:, :count], queries) * SCALE,
+        dot_tn(low[:, :count], grads),
+    )
+    return [result.astype(jnp.bfloat16) for result in results]
 
 
 def attend_kernel(rows, has_outs, *refs):
-    row_ids, col_ids, own, left, right = refs[:5]
-    refs = refs[5 + (4 if has_outs else 0) :]
-    attended, grad_q, grad_k, grad_v, bias_own, bias_left, bias_right = refs
+    row_ids, col_ids, sides, own, near, far = refs[:6]
+    refs = refs[6 + (4 if has_outs else 0) :]
+    outs, (bias, gathered, results) = refs[:4], refs[4:]
+    parts_per_block = own.shape[0] * BLOCK // rows
+    most = WINDOW // BLOCK
 
     @pl.when(pl.program_id(0) == 0)
     def _():
-        def bias(row_start, col_start, col_count):
-            same = (
-                row_ids[row_start : row_start + rows, :]
-                == col_ids[:, col_start : col_start + col_count]
-            )
-            return jnp.where(same, 0.0, MASKED)
-
-        bias_own[...] = bias(rows, 0, 3 * rows)
-        bias_left[...] = bias(0, 0, 2 * rows)
-        bias_right[...] = bias(2 * rows, rows, 2 * rows)
-
-    def load(ref, index):
-        return ref[:, index].reshape(rows, HD)
-
-    q_l, k_l, v_l, g_l = (load(left, i) for i in range(4))
-    q_o, k_o, v_o, g_o = (load(own, i) for i in range(4))
-    q_r, k_r, v_r, g_r = (load(right, i) for i in range(4))
-
-    k_all = jnp.concatenate((k_l, k_o, k_r))
-    v_all = jnp.concatenate((v_l, v_o, v_r))
-    p, s = probs_and_grads(q_o, g_o, k_all, v_all, bias_own[...])
-    attended[...] = dot_nn(p, v_all).astype(jnp.bfloat16)
-    grad_q[...] = (dot_nn(s, k_all) * SCALE).astype(jnp.bfloat16)
-    p_o, s_o = p[:, rows : 2 * rows], s[:, rows : 2 * rows]
-    p_l, s_l = probs_and_grads(
-        q_l, g_l, k_all[: 2 * rows], v_all[: 2 * rows], bias_left[...]
-    )
-    p_r, s_r = probs_and_grads(q_r, g_r, k_all[rows:], v_all[rows:], bias_right[...])
-    p_l, s_l = p_l[:, rows:], s_l[:, rows:]
-    p_r, s_r = p_r[:, :rows], s_r[:, :rows]
-    grad_v[...] = (dot_tn(p_l, g_l) + dot_tn(p_o, g_o) + dot_tn(p_r, g_r)).astype(jnp.bfloat16)
-    grad_k[...] = (
-        (dot_tn(s_l, q_l) + dot_tn(s_o, q_o) + dot_tn(s_r, q_r)) * SCALE
-    ).astype(jnp.bfloat16)
-
-
-def attend(ids, own, left, right, outs, first_head, head_total):
+        bias[...] = jnp.where(row_ids[...] == col_ids[...], 0.0, MASKED)
+
+    whole = [own[:, index].reshape(rows, HD) for index in range(4)]
+    for out, result in zip(outs, attention(*whole, bias[...], rows)):
+        out[...] = result
+
+    def block_of(ref, block, index):
+        block = jnp.clip(block, 0, rows // BLOCK - 1)
+        taken = ref[pl.ds(block * parts_per_block, parts_per_block), index]
+        return taken.reshape(BLOCK, HD)
+
+    def one_side(side, other):
+        own_first, own_count = sides[side, 0], sides[side, 1]
+        other_first, other_count = sides[side, 2], sides[side, 3]
+        total = own_count + other_count
+
+        @pl.when(own_count > 0)
+        def _():
+            for slot in range(most):
+                for index in range(4):
+                    block = jnp.where(
+                        slot < own_count,
+                        block_of(own, own_first + slot, index),
+                        block_of(other, other_first + slot - own_count, index),
+                    )
+                    if index == 3:
+                        block = jnp.where(slot < total, block, jnp.zeros_like(block))
+                    gathered[index, slot * BLOCK : (slot + 1) * BLOCK] = block
+
+        for size in range(2 * BLOCK, WINDOW + 1, 2 * BLOCK):
+            blocks = size // BLOCK
+
+            @pl.when((own_count > 0) & (total > blocks - 2) & (total <= blocks))
+            def _():
+                lane = lax.broadcasted_iota(jnp.int32, (1, size), 1)
+                tail = jnp.where(lane < total * BLOCK, 0.0, MASKED)
+                count = min(size, rows)
+                image = [gathered[index, :size] for index in range(4)]
+                for index, result in enumerate(attention(*image, tail, count)):
+                    results[index, :count] = result
+
+        for slot in range(rows // BLOCK):
+
+            @pl.when(slot < own_count)
+            def _():
+                target = pl.ds(pl.multiple_of((own_first + slot) * BLOCK, BLOCK), BLOCK)
+                for index, out in enumerate(outs):
+                    out[target, :] = results[index, slot * BLOCK : (slot + 1) * BLOCK]
+
+    one_side(0, near)
+    one_side(1, far)
+
+
+def attend(ids, sides, own, near, far, outs, first_head, head_total):
     parts, _, part_rows, width = own.shape
     rows = parts * part_rows
     heads = width // HD
@@ -226,18 +252,18 @@
     whole = pl.BlockSpec(memory_space=pltpu.VMEM)
     out_spec = pl.BlockSpec((rows, HD), lambda h: (0, h + first_head))
     has_outs = outs is not None
-    aliases = {5 + i: i for i in range(4)} if has_outs else {}
+    aliases = {6 + i: i for i in range(4)} if has_outs else {}
     return pl.pallas_call(
         functools.partial(attend_kernel, rows, has_outs),
         grid=(heads,),
         out_shape=[jax.ShapeDtypeStruct((rows, head_total * HD), jnp.bfloat16)] * 4,
-        in_specs=[whole, whole, block, block, block]
+        in_specs=[whole, whole, pl.BlockSpec(memory_space=pltpu.SMEM), block, block, block]
         + ([pl.BlockSpec(memory_space=pl.ANY)] * 4 if has_outs else []),
         out_specs=[out_spec] * 4,
         scratch_shapes=[
-            pltpu.VMEM((rows, 3 * rows), jnp.float32),
-            pltpu.VMEM((rows, 2 * rows), jnp.float32),
-            pltpu.VMEM((rows, 2 * rows), jnp.float32),
+            pltpu.VMEM((rows, rows), jnp.float32),
+            pltpu.VMEM((4, WINDOW, HD), jnp.bfloat16),
+            pltpu.VMEM((4, rows, HD), jnp.bfloat16),
         ],
         input_output_aliases=aliases,
         compiler_params=pltpu.CompilerParams(
@@ -246,7 +272,16 @@
         cost_estimate=pl.CostEstimate(
             flops=heads * ATTEND_FLOPS, bytes_accessed=1, transcendentals=0
         ),
-    )(ids[:, None], ids[None, :], own, left, right, *(outs or ()))
+    )(ids[:, None], ids[None, :], sides, own, near, far, *(outs or ()))
+
+
+def side_blocks(own_ids, other_ids):
+    same = own_ids[:, None] == other_ids[None, :]
+
+    def span(shared):
+        return jnp.argmax(shared).astype(jnp.int32), jnp.sum(shared, dtype=jnp.int32)
+
+    return jnp.stack(span(jnp.any(same, axis=1)) + span(jnp.any(same, axis=0)))
 
 
 def shards(queries, key_vectors, value_vectors, grad_output, image_ids):
@@ -254,7 +289,8 @@
     parts = lax.axis_size("tensor")
     rows = queries.shape[0] * parts
     head_total = queries.shape[1] // HD // parts
-    ids = nearby_ids(image_ids, rows)
+    ids, *others = nearby_ids(image_ids, rows)
+    sides = jnp.stack([side_blocks(ids[::BLOCK], other[::BLOCK]) for other in others])
     chunks = split_counts(head_total, CHUNK_SHARES)
     outs, out_history, packed = None, [], []
     for first, count in chunks[:2]:
@@ -269,7 +305,7 @@
             packed.append(pack(arrays, parts, *chunks[number + 2], [own]))
         near = swap_pairs(own, "dp", 0)
         far = swap_pairs(own, "dp", 1)
-        outs = attend(ids, own, near, far, outs, first, head_total)
+        outs = attend(ids, sides, own, near, far, outs, first, head_total)
         out_history.append(outs)
     return tuple(outs)
 

time: 126 us -> 135 us (1.071)
  waiting for transfers between devices: 49.2 us -> 38.5 us
  other arithmetic: 0.01 us -> 10 us
  Pallas kernels: 37.3 us -> 44.9 us
    another operation x0 -> x7, other arithmetic: none -> 8.48 us  [the longest x3 5.81 us: shards(): jnp.stack([side_blocks(ids[::BLOCK], other[::BLOCK]) for other in others])]
    pallas_call x4, Pallas kernels: 29.3 us -> 36.9 us  [attend(): pl.pallas_call(functools.partial(attend_kernel, rows, has_outs), grid=(he...]
    ppermute x8, waiting for transfers between devices: 6.6 us -> 0.02 us  [swap_pairs(): return lax.ppermute(block, axis, route)]
    all_to_all x4, waiting for transfers between devices: 42.6 us -> 38.5 us  [shards(): lax.all_to_all(packed[number], 'tensor', split_axis=0, concat_axis=0, til...]
    reduce_sum x0 -> x2, other arithmetic: none -> 1.35 us  [span(): jnp.sum(shared, dtype=jnp.int32)]
    unnamed x20 -> x22, local copies, waits for them, and re-layouts: 4.07 us -> 5.15 us
  transfers between devices with their start and end apart: 12 -> 12, of which waited for: 5 -> 2; matrix products, arithmetic and copies ran while one was open for 1% -> 8% of each run, Pallas kernels for 25% -> 29%
where the time goes in v5:
time: 135 us; the launch traced here: 133 us
  Pallas kernels  44.9 us (33%)
  waiting for transfers between devices  38.5 us (29%)
  starting transfers between devices  32.2 us (24%)
  other arithmetic  10 us (7%)
  local copies, waits for them, and re-layouts  6.32 us (5%)
    all_to_all x4, waiting for transfers between devices, shards(): lax.all_to_all(packed[number], 'tensor', split_axis=0, concat_axis=0, til...  38.5 us
    pallas_call x4, Pallas kernels, attend(): pl.pallas_call(functools.partial(attend_kernel, rows, has_outs), grid=(he...  36.9 us
    all_to_all x4, starting transfers between devices, shards(): lax.all_to_all(packed[number], 'tensor', split_axis=0, concat_axis=0, til...  16.4 us
    ppermute x8, starting transfers between devices, swap_pairs(): return lax.ppermute(block, axis, route)  15.8 us
    pallas_call x4, Pallas kernels, pack(): pl.pallas_call(functools.partial(pack_kernel, parts, total // parts, firs...  8.02 us
    another operation x3, other arithmetic, shards(): jnp.stack([side_blocks(ids[::BLOCK], other[::BLOCK]) for other in others])  5.81 us
    unnamed x22, local copies, waits for them, and re-layouts  5.15 us
  transfers between devices with their start and end apart: 12, of which 2 were waited for; matrix products, arithmetic and copies ran while one was open for 8% of the time, Pallas kernels for 29%

profile of v5, /device:TPU:3, one launch (start us, length us, event | category | flops | bytes accessed | tf_op | source)
XLA Modules:
  0.0 132.8 jit_solution(9440557565435589323)
XLA Ops:
  0.6 2.1 %shard_map.85 = bf16[4,4,64,512]{3,2,1,0:T(8,128)(2,1)} custom-call(bf16[64,6144]{1,0:T(8,128)(2,1)} %refs_0_.7, bf16[64,6144]{1,0:T(8,128)(2,1)} %refs_1_.7, bf16[64,6144]{1,0:T(8,128)(2,1)} %refs_2_.7, bf16[64,6144]{1,0:T(8,128)(2,1)} %refs_3_.7), custom_call_target="tpu_custom_call" | custom-call | flops 1 | bytes 1 | tf_op jit(solution)/shard_map/pallas_call | solution.py:78
  2.8 4.6 %all-to-all-start.1 = ((bf16[4,4,64,512]{3,2,1,0:T(8,128)(2,1)}), bf16[4,4,64,512]{3,2,1,0:T(8,128)(2,1)S(1)}, u32[]{:S(2)}, u32[]{:S(2)}) async-start(bf16[4,4,64,512]{3,2,1,0:T(8,128)(2,1)} %shard_map.85), calls=%async_computation.1 | async-start | bytes 2097152 | tf_op jit(solution)/shard_map/all_to_all | solution.py:299
  7.4 2.2 %shard_map.84.refs_1_ = bf16[4,4,64,512]{3,2,1,0:T(8,128)(2,1)} custom-call(bf16[64,6144]{1,0:T(8,128)(2,1)} %refs_0_.7, bf16[64,6144]{1,0:T(8,128)(2,1)} %refs_1_.7, bf16[64,6144]{1,0:T(8,128)(2,1)} %refs_2_.7, bf16[64,6144]{1,0:T(8,128)(2,1)} %refs_3_.7), custom_call_target="tpu_custom_call" | custom-call | flops 1 | bytes 1 | tf_op jit(solution)/shard_map/pallas_call | solution.py:78
  9.6 23.1 %all-to-all-done.1.refs_0_ = bf16[4,4,64,512]{3,2,1,0:T(8,128)(2,1)S(1)} async-done(((bf16[4,4,64,512]{3,2,1,0:T(8,128)(2,1)}), bf16[4,4,64,512]{3,2,1,0:T(8,128)(2,1)S(1)}, u32[]{:S(2)}, u32[]{:S(2)}) %all-to-all-start.1) | async-done | bytes 1048608 | tf_op jit(solution)/shard_map/all_to_all | solution.py:299
  32.6 3.5 %all-to-all-start = ((bf16[4,4,64,512]{3,2,1,0:T(8,128)(2,1)}), bf16[4,4,64,512]{3,2,1,0:T(8,128)(2,1)S(1)}, u32[]{:S(2)}, u32[]{:S(2)}) async-start(bf16[4,4,64,512]{3,2,1,0:T(8,128)(2,1)} %shard_map.84.refs_1_), calls=%async_computation | async-start | bytes 2097152 | tf_op jit(solution)/shard_map/all_to_all | solution.py:299
  36.2 0.7 copy-done.4
  37.4 0.7 iota_reduce_fusion.3
  38.1 1.4 %collective-permute-start.2 = (bf16[4,4,64,512]{3,2,1,0:T(8,128)(2,1)}, bf16[4,4,64,512]{3,2,1,0:T(8,128)(2,1)S(1)}, u32[]{:S(2)}, u32[]{:S(2)}) collective-permute-start(bf16[4,4,64,512]{3,2,1,0:T(8,128)(2,1)} %shard_map.86.refs_4_.refs_3_), channel_id=1, source_target_pairs={{0,4},{4,0},{8,12},{12,8},{16,20},{20,16},{24,28},{28,24},{1,5},{5... | collective-permute-start | bytes 3145736 | tf_op jit(solution)/shard_map/ppermute | solution.py:34
  39.6 3.0 %collective-permute-start.3 = (bf16[4,4,64,512]{3,2,1,0:T(8,128)(2,1)}, bf16[4,4,64,512]{3,2,1,0:T(8,128)(2,1)}, u32[]{:S(2)}, u32[]{:S(2)}) collective-permute-start(bf16[4,4,64,512]{3,2,1,0:T(8,128)(2,1)} %shard_map.86.refs_4_.refs_3_), channel_id=1, source_target_pairs={{4,8},{8,4},{12,16},{16,12},{20,24},{24,20},{5,9},{9,5},{13,17},{1... | collective-permute-start | bytes 3145736 | tf_op jit(solution)/shard_map/ppermute | solution.py:34
  42.6 0.7 iota_reduce_fusion.2
  43.9 2.0 %shard_map.87.refs_1_ = bf16[4,4,64,384]{3,2,1,0:T(8,128)(2,1)} custom-call(bf16[64,6144]{1,0:T(8,128)(2,1)} %refs_0_.7, bf16[64,6144]{1,0:T(8,128)(2,1)} %refs_1_.7, bf16[64,6144]{1,0:T(8,128)(2,1)} %refs_2_.7, bf16[64,6144]{1,0:T(8,128)(2,1)} %refs_3_.7, bf16[4,4,64,512]{3,2,1,0:T(8,128)(2,1)} %shard_map.86.refs_4_.refs_3_), custom_call_target="tpu_custom_call" | custom-call | flops 1 | bytes 1 | tf_op jit(solution)/shard_map/pallas_call | solution.py:78
  45.9 15.4 %all-to-all-done.refs_0_ = bf16[4,4,64,512]{3,2,1,0:T(8,128)(2,1)S(1)} async-done(((bf16[4,4,64,512]{3,2,1,0:T(8,128)(2,1)}), bf16[4,4,64,512]{3,2,1,0:T(8,128)(2,1)S(1)}, u32[]{:S(2)}, u32[]{:S(2)}) %all-to-all-start) | async-done | bytes 1048608 | tf_op jit(solution)/shard_map/all_to_all | solution.py:299
  61.3 3.5 %all-to-all-start.3 = ((bf16[4,4,64,384]{3,2,1,0:T(8,128)(2,1)}), bf16[4,4,64,384]{3,2,1,0:T(8,128)(2,1)S(1)}, u32[]{:S(2)}, u32[]{:S(2)}) async-start(bf16[4,4,64,384]{3,2,1,0:T(8,128)(2,1)} %shard_map.87.refs_1_), calls=%async_computation.3 | async-start | bytes 1572864 | tf_op jit(solution)/shard_map/all_to_all | solution.py:299
  65.5 0.7 convert_reduce_fusion.2
  66.8 1.5 %collective-permute-start = (bf16[4,4,64,512]{3,2,1,0:T(8,128)(2,1)}, bf16[4,4,64,512]{3,2,1,0:T(8,128)(2,1)}, u32[]{:S(2)}, u32[]{:S(2)}) collective-permute-start(bf16[4,4,64,512]{3,2,1,0:T(8,128)(2,1)} %shard_map.88.refs_4_.refs_3_), channel_id=1, source_target_pairs={{0,4},{4,0},{8,12},{12,8},{16,20},{20,16},{24,28},{28,24},{1,5},{5... | collective-permute-start | bytes 3145736 | tf_op jit(solution)/shard_map/ppermute | solution.py:34
  68.3 3.0 %collective-permute-start.1 = (bf16[4,4,64,512]{3,2,1,0:T(8,128)(2,1)}, bf16[4,4,64,512]{3,2,1,0:T(8,128)(2,1)}, u32[]{:S(2)}, u32[]{:S(2)}) collective-permute-start(bf16[4,4,64,512]{3,2,1,0:T(8,128)(2,1)} %shard_map.88.refs_4_.refs_3_), channel_id=1, source_target_pairs={{4,8},{8,4},{12,16},{16,12},{20,24},{24,20},{5,9},{9,5},{13,17},{1... | collective-permute-start | bytes 3145736 | tf_op jit(solution)/shard_map/ppermute | solution.py:34
  71.3 2.6 %add_bitcast_fusion = s32[1,4]{1,0:T(1,128)S(1)} fusion(s32[1]{0:T(128)} %bitcast.5, s32[1]{0:T(128)} %bitcast.4, s32[1]{0:T(128)} %bitcast.3, s32[1]{0:T(128)} %bitcast.2), kind=kLoop, calls=%fused_computation.8 | loop fusion | flops 12 | bytes 32 | tf_op jit(solution)/shard_map/stack | solution.py:293
  73.9 0.8 copy.32.refs_0_
  74.7 2.7 %add_bitcast_fusion.1 = s32[1,4]{1,0:T(1,128)S(1)} fusion(s32[1]{0:T(128)} %bitcast.10, s32[1]{0:T(128)} %bitcast.9, s32[1]{0:T(128)} %bitcast.8, s32[1]{0:T(128)} %bitcast.7), kind=kLoop, calls=%fused_computation.9 | loop fusion | flops 12 | bytes 32 | tf_op jit(solution)/shard_map/stack | solution.py:293
  77.9 1.7 %shard_map.89.refs_1_ = bf16[4,4,64,128]{3,2,1,0:T(8,128)(2,1)} custom-call(bf16[64,6144]{1,0:T(8,128)(2,1)} %refs_0_.7, bf16[64,6144]{1,0:T(8,128)(2,1)} %refs_1_.7, bf16[64,6144]{1,0:T(8,128)(2,1)} %refs_2_.7, bf16[64,6144]{1,0:T(8,128)(2,1)} %refs_3_.7, bf16[4,4,64,512]{3,2,1,0:T(8,128)(2,1)} %shard_map.88.refs_4_.refs_3_), custom_call_target="tpu_custom_call" | custom-call | flops 1 | bytes 1 | tf_op jit(solution)/shard_map/pallas_call | solution.py:78
  79.7 1.0 copy-done.6
  80.7 11.7 %shard_map.90 = (bf16[256,1536]{1,0:T(8,128)(2,1)}, bf16[256,1536]{1,0:T(8,128)(2,1)}, bf16[256,1536]{1,0:T(8,128)(2,1)}, bf16[256,1536]{1,0:T(8,128)(2,1)}) custom-call(s32[256,1]{1,0:T(8,128)} %copy.32.refs_0_, s32[1,256]{1,0:T(1,128)} %bitcast.15, s32[2,4]{1,0:T(2,128)} %pad_add_fusion.refs_2_, bf16[4,4,64,512]{3,2,1,0:T(8,128)(2,1)} %shard_map.86.refs_4_.refs_3_, ...), custom_call_target="tpu_custom_call" | custom-call | flops 6000000000 | bytes 1 | tf_op jit(solution)/shard_map/pallas_call | solution.py:256
  92.3 0.9 copy-done.2
  93.2 3.4 %collective-permute-start.7 = (bf16[4,4,64,384]{3,2,1,0:T(8,128)(2,1)}, bf16[4,4,64,384]{3,2,1,0:T(8,128)(2,1)S(1)}, u32[]{:S(2)}, u32[]{:S(2)}) collective-permute-start(bf16[4,4,64,384]{3,2,1,0:T(8,128)(2,1)} %shard_map.93.refs_3_), channel_id=1, source_target_pairs={{4,8},{8,4},{12,16},{16,12},{20,24},{24,20},{5,9},{9,5},{13,17},{1... | collective-permute-start | bytes 2359304 | tf_op jit(solution)/shard_map/ppermute | solution.py:34
  96.7 4.8 %all-to-all-start.2 = ((bf16[4,4,64,128]{3,2,1,0:T(8,128)(2,1)}), bf16[4,4,64,128]{3,2,1,0:T(8,128)(2,1)S(1)}, u32[]{:S(2)}, u32[]{:S(2)}) async-start(bf16[4,4,64,128]{3,2,1,0:T(8,128)(2,1)} %shard_map.89.refs_1_), calls=%async_computation.2 | async-start | bytes 524288 | tf_op jit(solution)/shard_map/all_to_all | solution.py:299
  101.5 11.7 %shard_map.91 = (bf16[256,1536]{1,0:T(8,128)(2,1)}, bf16[256,1536]{1,0:T(8,128)(2,1)}, bf16[256,1536]{1,0:T(8,128)(2,1)}, bf16[256,1536]{1,0:T(8,128)(2,1)}) custom-call(s32[256,1]{1,0:T(8,128)} %copy.32.refs_0_, s32[1,256]{1,0:T(1,128)} %bitcast.16, ...), custom_call_target="tpu_custom_call", output_to_operand_aliasing={{0}: (6, {}), {1}: (7, {}), {2}: (8, {}), {3}: (9, {})} | custom-call | flops 6000000000 | bytes 1 | tf_op jit(solution)/shard_map/pallas_call | solution.py:256
  113.2 0.7 copy-done.3
  113.9 3.5 %collective-permute-start.5 = (bf16[4,4,64,128]{3,2,1,0:T(8,128)(2,1)}, bf16[4,4,64,128]{3,2,1,0:T(8,128)(2,1)S(1)}, u32[]{:S(2)}, u32[]{:S(2)}) collective-permute-start(bf16[4,4,64,128]{3,2,1,0:T(8,128)(2,1)} %shard_map.92.refs_3_), channel_id=1, source_target_pairs={{4,8},{8,4},{12,16},{16,12},{20,24},{24,20},{5,9},{9,5},{13,17},{1... | collective-permute-start | bytes 786440 | tf_op jit(solution)/shard_map/ppermute | solution.py:34
  117.4 0.8 copy-done.7
  118.5 9.2 %shard_map.94 = (bf16[256,1536]{1,0:T(8,128)(2,1)}, bf16[256,1536]{1,0:T(8,128)(2,1)}, bf16[256,1536]{1,0:T(8,128)(2,1)}, bf16[256,1536]{1,0:T(8,128)(2,1)}) custom-call(s32[256,1]{1,0:T(8,128)} %copy.32.refs_0_, s32[1,256]{1,0:T(1,128)} %bitcast.17, ...), custom_call_target="tpu_custom_call", output_to_operand_aliasing={{0}: (6, {}), {1}: (7, {}), {2}: (8, {}), {3}: (9, {})} | custom-call | flops 4499999744 | bytes 1 | tf_op jit(solution)/shard_map/pallas_call | solution.py:256
  127.8 0.7 copy-done.9
  128.6 4.2 %shard_map.95 = (bf16[256,1536]{1,0:T(8,128)(2,1)}, bf16[256,1536]{1,0:T(8,128)(2,1)}, bf16[256,1536]{1,0:T(8,128)(2,1)}, bf16[256,1536]{1,0:T(8,128)(2,1)}) custom-call(s32[256,1]{1,0:T(8,128)} %copy.32.refs_0_, s32[1,256]{1,0:T(1,128)} %bitcast.18, ...), custom_call_target="tpu_custom_call", output_to_operand_aliasing={{0}: (6, {}), {1}: (7, {}), {2}: (8, {}), {3}: (9, {})} | custom-call | flops 1500000000 | bytes 1 | tf_op jit(solution)/shard_map/pallas_call | solution.py:256
  (41 shorter events, 3.5 us)
Async XLA Ops:
  2.8 29.8 %all-to-all-start.1 = ((bf16[4,4,64,512]{3,2,1,0:T(8,128)(2,1)}), bf16[4,4,64,512]{3,2,1,0:T(8,128)(2,1)S(1)}, u32[]{:S(2)}, u32[]{:S(2)}) async-start(bf16[4,4,64,512]{3,2,1,0:T(8,128)(2,1)} %shard_map.85), calls=%async_computation.1 | async-start | bytes 2097152 | tf_op jit(solution)/shard_map/all_to_all | solution.py:299
  32.6 3.5 %copy-start = (bf16[4,4,64,512]{3,2,1,0:T(8,128)(2,1)}, bf16[4,4,64,512]{3,2,1,0:T(8,128)(2,1)S(1)}, u32[]{:S(2)}) copy-start(bf16[4,4,64,512]{3,2,1,0:T(8,128)(2,1)S(1)} %all-to-all-done.1.refs_0_) | copy-start | bytes 3145732
  32.6 28.7 %all-to-all-start = ((bf16[4,4,64,512]{3,2,1,0:T(8,128)(2,1)}), bf16[4,4,64,512]{3,2,1,0:T(8,128)(2,1)S(1)}, u32[]{:S(2)}, u32[]{:S(2)}) async-start(bf16[4,4,64,512]{3,2,1,0:T(8,128)(2,1)} %shard_map.84.refs_1_), calls=%async_computation | async-start | bytes 2097152 | tf_op jit(solution)/shard_map/all_to_all | solution.py:299
  36.2 0.7 copy-start.4
  37.0 36.9 %copy-start.5 = (s32[256]{0:T(256)}, s32[256]{0:T(256)S(1)}, u32[]{:S(2)}) copy-start(s32[256]{0:T(256)S(1)} %get-tuple-element.44) | copy-start | bytes 3076
  38.1 41.5 %collective-permute-start.2 = (bf16[4,4,64,512]{3,2,1,0:T(8,128)(2,1)}, bf16[4,4,64,512]{3,2,1,0:T(8,128)(2,1)S(1)}, u32[]{:S(2)}, u32[]{:S(2)}) collective-permute-start(bf16[4,4,64,512]{3,2,1,0:T(8,128)(2,1)} %shard_map.86.refs_4_.refs_3_), channel_id=1, source_target_pairs={{0,4},{4,0},{8,12},{12,8},{16,20},{20,16},{24,28},{28,24},{1,5},{5... | collective-permute-start | bytes 3145736 | tf_op jit(solution)/shard_map/ppermute | solution.py:34
  39.6 40.1 %collective-permute-start.3 = (bf16[4,4,64,512]{3,2,1,0:T(8,128)(2,1)}, bf16[4,4,64,512]{3,2,1,0:T(8,128)(2,1)}, u32[]{:S(2)}, u32[]{:S(2)}) collective-permute-start(bf16[4,4,64,512]{3,2,1,0:T(8,128)(2,1)} %shard_map.86.refs_4_.refs_3_), channel_id=1, source_target_pairs={{4,8},{8,4},{12,16},{16,12},{20,24},{24,20},{5,9},{9,5},{13,17},{1... | collective-permute-start | bytes 3145736 | tf_op jit(solution)/shard_map/ppermute | solution.py:34
  61.3 5.5 %copy-start.1 = (bf16[4,4,64,512]{3,2,1,0:T(8,128)(2,1)}, bf16[4,4,64,512]{3,2,1,0:T(8,128)(2,1)S(1)}, u32[]{:S(2)}) copy-start(bf16[4,4,64,512]{3,2,1,0:T(8,128)(2,1)S(1)} %all-to-all-done.refs_0_) | copy-start | bytes 3145732
  61.3 31.0 %all-to-all-start.3 = ((bf16[4,4,64,384]{3,2,1,0:T(8,128)(2,1)}), bf16[4,4,64,384]{3,2,1,0:T(8,128)(2,1)S(1)}, u32[]{:S(2)}, u32[]{:S(2)}) async-start(bf16[4,4,64,384]{3,2,1,0:T(8,128)(2,1)} %shard_map.87.refs_1_), calls=%async_computation.3 | async-start | bytes 1572864 | tf_op jit(solution)/shard_map/all_to_all | solution.py:299
  66.8 34.6 %collective-permute-start = (bf16[4,4,64,512]{3,2,1,0:T(8,128)(2,1)}, bf16[4,4,64,512]{3,2,1,0:T(8,128)(2,1)}, u32[]{:S(2)}, u32[]{:S(2)}) collective-permute-start(bf16[4,4,64,512]{3,2,1,0:T(8,128)(2,1)} %shard_map.88.refs_4_.refs_3_), channel_id=1, source_target_pairs={{0,4},{4,0},{8,12},{12,8},{16,20},{20,16},{24,28},{28,24},{1,5},{5... | collective-permute-start | bytes 3145736 | tf_op jit(solution)/shard_map/ppermute | solution.py:34
  68.3 33.1 %collective-permute-start.1 = (bf16[4,4,64,512]{3,2,1,0:T(8,128)(2,1)}, bf16[4,4,64,512]{3,2,1,0:T(8,128)(2,1)}, u32[]{:S(2)}, u32[]{:S(2)}) collective-permute-start(bf16[4,4,64,512]{3,2,1,0:T(8,128)(2,1)} %shard_map.88.refs_4_.refs_3_), channel_id=1, source_target_pairs={{4,8},{8,4},{12,16},{16,12},{20,24},{24,20},{5,9},{9,5},{13,17},{1... | collective-permute-start | bytes 3145736 | tf_op jit(solution)/shard_map/ppermute | solution.py:34
  79.6 1.0 copy-start.6
  92.3 0.9 copy-start.2
  93.2 24.1 %collective-permute-start.6 = (bf16[4,4,64,384]{3,2,1,0:T(8,128)(2,1)}, bf16[4,4,64,384]{3,2,1,0:T(8,128)(2,1)S(1)}, u32[]{:S(2)}, u32[]{:S(2)}) collective-permute-start(bf16[4,4,64,384]{3,2,1,0:T(8,128)(2,1)} %shard_map.93.refs_3_), channel_id=1, source_target_pairs={{0,4},{4,0},{8,12},{12,8},{16,20},{20,16},{24,28},{28,24},{1,5},{5... | collective-permute-start | bytes 2359304 | tf_op jit(solution)/shard_map/ppermute | solution.py:34
  93.2 24.2 %collective-permute-start.7 = (bf16[4,4,64,384]{3,2,1,0:T(8,128)(2,1)}, bf16[4,4,64,384]{3,2,1,0:T(8,128)(2,1)S(1)}, u32[]{:S(2)}, u32[]{:S(2)}) collective-permute-start(bf16[4,4,64,384]{3,2,1,0:T(8,128)(2,1)} %shard_map.93.refs_3_), channel_id=1, source_target_pairs={{4,8},{8,4},{12,16},{16,12},{20,24},{24,20},{5,9},{9,5},{13,17},{1... | collective-permute-start | bytes 2359304 | tf_op jit(solution)/shard_map/ppermute | solution.py:34
  96.7 16.5 %all-to-all-start.2 = ((bf16[4,4,64,128]{3,2,1,0:T(8,128)(2,1)}), bf16[4,4,64,128]{3,2,1,0:T(8,128)(2,1)S(1)}, u32[]{:S(2)}, u32[]{:S(2)}) async-start(bf16[4,4,64,128]{3,2,1,0:T(8,128)(2,1)} %shard_map.89.refs_1_), calls=%async_computation.2 | async-start | bytes 524288 | tf_op jit(solution)/shard_map/all_to_all | solution.py:299
  113.2 0.7 copy-start.3
  113.9 13.9 %collective-permute-start.4 = (bf16[4,4,64,128]{3,2,1,0:T(8,128)(2,1)}, bf16[4,4,64,128]{3,2,1,0:T(8,128)(2,1)S(1)}, u32[]{:S(2)}, u32[]{:S(2)}) collective-permute-start(bf16[4,4,64,128]{3,2,1,0:T(8,128)(2,1)} %shard_map.92.refs_3_), channel_id=1, source_target_pairs={{0,4},{4,0},{8,12},{12,8},{16,20},{20,16},{24,28},{28,24},{1,5},{5... | collective-permute-start | bytes 786440 | tf_op jit(solution)/shard_map/ppermute | solution.py:34
  113.9 13.9 %collective-permute-start.5 = (bf16[4,4,64,128]{3,2,1,0:T(8,128)(2,1)}, bf16[4,4,64,128]{3,2,1,0:T(8,128)(2,1)S(1)}, u32[]{:S(2)}, u32[]{:S(2)}) collective-permute-start(bf16[4,4,64,128]{3,2,1,0:T(8,128)(2,1)} %shard_map.92.refs_3_), channel_id=1, source_target_pairs={{4,8},{8,4},{12,16},{16,12},{20,24},{24,20},{5,9},{9,5},{13,17},{1... | collective-permute-start | bytes 786440 | tf_op jit(solution)/shard_map/ppermute | solution.py:34
  117.4 0.9 copy-start.7
  117.4 1.1 copy-start.8
  127.8 0.7 copy-start.9
  127.8 0.8 copy-start.10

commit v6 on v4

--- a/solution.py
+++ b/solution.py
@@ -9,12 +9,13 @@
 from jax.sharding import PartitionSpec as P
 
 HD = 128
+BLOCK = 64
 SCALE = 1.0 / math.sqrt(HD)
 EXP2_SCALE = SCALE * math.log2(math.e)
 MASKED = -1e30
 CHUNK_SHARES = (4, 4, 3, 1)
 VMEM_LIMIT = 60 * 1024 * 1024
-ATTEND_FLOPS = 2_500_000_000
+ATTEND_FLOPS = 1_500_000_000
 SMALL_COST = pl.CostEstimate(flops=1, bytes_accessed=1, transcendentals=0)
 
 
@@ -32,17 +33,16 @@
     return lax.ppermute(block, axis, route)
 
 
-def nearby_ids(image_ids, rows):
+def nearby_block_ids(image_ids, rows):
     shard = lax.axis_index("dp")
-    padded = jnp.pad(image_ids, (rows, rows), constant_values=-1)
+    blocks = rows // BLOCK
+    padded = jnp.pad(image_ids[::BLOCK], (blocks, blocks), constant_values=-1)
     odd = lax.rem(shard, 2)
 
     def ids_of(other):
-        return lax.dynamic_slice_in_dim(padded, (other + 1) * rows, rows)
-
-    return jnp.concatenate(
-        (ids_of(shard + 1 - 2 * odd), ids_of(shard), ids_of(shard - 1 + 2 * odd))
-    )
+        return lax.dynamic_slice_in_dim(padded, (other + 1) * blocks, blocks)
+
+    return jnp.stack((ids_of(shard), ids_of(shard + 1 - 2 * odd), ids_of(shard - 1 + 2 * odd)))
 
 
 def columns(array, part, stride, first, width):
@@ -164,80 +164,112 @@
     return jnp.dot(a, b, preferred_element_type=jnp.float32)
 
 
-def probs_and_grads(queries, grads, keys, values, bias):
-    scores = dot_nt(queries, keys) + bias
-    row_max = jnp.max(scores, axis=1, keepdims=True)
-    weights = jnp.exp2((scores - row_max) * EXP2_SCALE)
-    probs = weights * (1.0 / jnp.sum(weights, axis=1, keepdims=True))
-    grad_probs = dot_nt(grads, values)
-    inner = jnp.sum(probs * grad_probs, axis=1, keepdims=True)
-    grad_scores = probs * (grad_probs - inner)
-    return probs.astype(jnp.bfloat16), grad_scores.astype(jnp.bfloat16)
+def attend_head(values_of, bias, size, rows):
+    queries, keys, values, grads = values_of
+    grad_k = grad_v = None
+    for start in range(0, size, rows):
+        tile = slice(start, start + rows)
+        scores = dot_nt(keys, queries[tile]) + bias[:size, tile]
+        weights = jnp.exp2((scores - jnp.max(scores, axis=0, keepdims=True)) * EXP2_SCALE)
+        probs = weights * (1.0 / jnp.sum(weights, axis=0, keepdims=True))
+        grad_probs = dot_nt(values, grads[tile])
+        inner = jnp.sum(probs * grad_probs, axis=0, keepdims=True)
+        low = probs.astype(jnp.bfloat16)
+        grad_scores = (probs * (grad_probs - inner)).astype(jnp.bfloat16)
+        tile_v = dot_nn(low[:rows], grads[tile])
+        tile_k = dot_nn(grad_scores[:rows], queries[tile])
+        if start == 0:
+            attended = dot_tn(low, values)
+            grad_q = dot_tn(grad_scores, keys)
+            grad_k, grad_v = tile_k, tile_v
+        else:
+            grad_k, grad_v = grad_k + tile_k, grad_v + tile_v
+    return attended, grad_q * SCALE, grad_k * SCALE, grad_v
 
 
 def attend_kernel(rows, has_outs, *refs):
-    row_ids, col_ids, own, left, right = refs[:5]
-    refs = refs[5 + (4 if has_outs else 0) :]
-    attended, grad_q, grad_k, grad_v, bias_own, bias_left, bias_right = refs
+    block_ids, own, near, far = refs[:4]
+    refs = refs[4 + (4 if has_outs else 0) :]
+    outs, (bias, gathered, table) = refs[:4], refs[4:]
+    blocks = rows // BLOCK
+    parts_per_block = own.shape[0] * BLOCK // rows
+    most = 3 * rows
 
     @pl.when(pl.program_id(0) == 0)
     def _():
-        def bias(row_start, col_start, col_count):
-            same = (
-                row_ids[row_start : row_start + rows, :]
-                == col_ids[:, col_start : col_start + col_count]
-            )
-            return jnp.where(same, 0.0, MASKED)
-
-        bias_own[...] = bias(rows, 0, 3 * rows)
-        bias_left[...] = bias(0, 0, 2 * rows)
-        bias_right[...] = bias(2 * rows, rows, 2 * rows)
-
-    def load(ref, index):
-        return ref[:, index].reshape(rows, HD)
-
-    q_l, k_l, v_l, g_l = (load(left, i) for i in range(4))
-    q_o, k_o, v_o, g_o = (load(own, i) for i in range(4))
-    q_r, k_r, v_r, g_r = (load(right, i) for i in range(4))
-
-    k_all = jnp.concatenate((k_l, k_o, k_r))
-    v_all = jnp.concatenate((v_l, v_o, v_r))
-    p, s = probs_and_grads(q_o, g_o, k_all, v_all, bias_own[...])
-    attended[...] = dot_nn(p, v_all).astype(jnp.bfloat16)
-    grad_q[...] = (dot_nn(s, k_all) * SCALE).astype(jnp.bfloat16)
-    p_o, s_o = p[:, rows : 2 * rows], s[:, rows : 2 * rows]
-    p_l, s_l = probs_and_grads(
-        q_l, g_l, k_all[: 2 * rows], v_all[: 2 * rows], bias_left[...]
-    )
-    p_r, s_r = probs_and_grads(q_r, g_r, k_all[rows:], v_all[rows:], bias_right[...])
-    p_l, s_l = p_l[:, rows:], s_l[:, rows:]
-    p_r, s_r = p_r[:, :rows], s_r[:, :rows]
-    grad_v[...] = (dot_tn(p_l, g_l) + dot_tn(p_o, g_o) + dot_tn(p_r, g_r)).astype(jnp.bfloat16)
-    grad_k[...] = (
-        (dot_tn(s_l, q_l) + dot_tn(s_o, q_o) + dot_tn(s_r, q_r)) * SCALE
-    ).astype(jnp.bfloat16)
-
-
-def attend(ids, own, left, right, outs, first_head, head_total):
+        count = jnp.int32(0)
+        for other in range(2 * blocks):
+            other_id = block_ids[1 + other // blocks, other % blocks]
+            shared = other_id == block_ids[0, 0]
+            for block in range(1, blocks):
+                shared = shared | (other_id == block_ids[0, block])
+            table[count] = other
+            count = count + shared.astype(jnp.int32)
+        table[2 * blocks] = count
+
+        def ids_along(axis):
+            shape = (most, 1) if axis == 0 else (1, most)
+            place = lax.broadcasted_iota(jnp.int32, shape, axis)
+            ids = jnp.full(shape, -2, jnp.int32)
+            for block in range(3 * blocks):
+                if block < blocks:
+                    block_id = block_ids[0, block]
+                else:
+                    source = table[jnp.minimum(block - blocks, 2 * blocks - 1)]
+                    source = jnp.clip(source, 0, 2 * blocks - 1)
+                    block_id = block_ids[1 + source // blocks, lax.rem(source, blocks)]
+                    block_id = jnp.where(block - blocks < count, block_id, -2)
+                inside = (place >= block * BLOCK) & (place < (block + 1) * BLOCK)
+                ids = jnp.where(inside, block_id, ids)
+            return ids
+
+        bias[...] = jnp.where(ids_along(0) == ids_along(1), 0.0, MASKED)
+
+    count = table[2 * blocks]
+
+    def other_block(slot, index):
+        source = jnp.where(slot < count, table[slot], 0)
+        place = lax.rem(source, blocks) * parts_per_block
+        taken = [ref[pl.ds(place, parts_per_block), index] for ref in (near, far)]
+        return jnp.where(source < blocks, *taken).reshape(BLOCK, HD)
+
+    for size in range(rows, most + 1, rows):
+        slots = size // BLOCK - blocks
+
+        @pl.when((count <= slots) & (count > slots - blocks))
+        def _():
+            for slot in range(slots):
+                for index in range(4):
+                    gathered[index, slot * BLOCK : (slot + 1) * BLOCK] = other_block(slot, index)
+            values_of = []
+            for index in range(4):
+                mine = own[:, index].reshape(rows, HD)
+                if slots:
+                    mine = jnp.concatenate((mine, gathered[index, : slots * BLOCK]))
+                values_of.append(mine)
+            for out, result in zip(outs, attend_head(values_of, bias, size, rows)):
+                out[...] = result.astype(jnp.bfloat16)
+
+
+def attend(block_ids, own, near, far, outs, first_head, head_total):
     parts, _, part_rows, width = own.shape
     rows = parts * part_rows
     heads = width // HD
     block = pl.BlockSpec((parts, 4, part_rows, HD), lambda h: (0, 0, 0, h))
-    whole = pl.BlockSpec(memory_space=pltpu.VMEM)
     out_spec = pl.BlockSpec((rows, HD), lambda h: (0, h + first_head))
     has_outs = outs is not None
-    aliases = {5 + i: i for i in range(4)} if has_outs else {}
+    aliases = {4 + i: i for i in range(4)} if has_outs else {}
     return pl.pallas_call(
         functools.partial(attend_kernel, rows, has_outs),
         grid=(heads,),
         out_shape=[jax.ShapeDtypeStruct((rows, head_total * HD), jnp.bfloat16)] * 4,
-        in_specs=[whole, whole, block, block, block]
+        in_specs=[pl.BlockSpec(memory_space=pltpu.SMEM), block, block, block]
         + ([pl.BlockSpec(memory_space=pl.ANY)] * 4 if has_outs else []),
         out_specs=[out_spec] * 4,
         scratch_shapes=[
-            pltpu.VMEM((rows, 3 * rows), jnp.float32),
-            pltpu.VMEM((rows, 2 * rows), jnp.float32),
-            pltpu.VMEM((rows, 2 * rows), jnp.float32),
+            pltpu.VMEM((3 * rows, 3 * rows), jnp.float32),
+            pltpu.VMEM((4, 2 * rows, HD), jnp.bfloat16),
+            pltpu.SMEM((2 * rows // BLOCK + 1,), jnp.int32),
         ],
         input_output_aliases=aliases,
         compiler_params=pltpu.CompilerParams(
@@ -246,7 +278,7 @@
         cost_estimate=pl.CostEstimate(
             flops=heads * ATTEND_FLOPS, bytes_accessed=1, transcendentals=0
         ),
-    )(ids[:, None], ids[None, :], own, left, right, *(outs or ()))
+    )(block_ids, own, near, far, *(outs or ()))
 
 
 def shards(queries, key_vectors, value_vectors, grad_output, image_ids):
@@ -254,7 +286,7 @@
     parts = lax.axis_size("tensor")
     rows = queries.shape[0] * parts
     head_total = queries.shape[1] // HD // parts
-    ids = nearby_ids(image_ids, rows)
+    block_ids = nearby_block_ids(image_ids, rows)
     chunks = split_counts(head_total, CHUNK_SHARES)
     outs, out_history, packed = None, [], []
     for first, count in chunks[:2]:
@@ -269,7 +301,7 @@
             packed.append(pack(arrays, parts, *chunks[number + 2], [own]))
         near = swap_pairs(own, "dp", 0)
         far = swap_pairs(own, "dp", 1)
-        outs = attend(ids, own, near, far, outs, first, head_total)
+        outs = attend(block_ids, own, near, far, outs, first, head_total)
         out_history.append(outs)
     return tuple(outs)
 

time: 126 us -> 124 us (0.984)
  Pallas kernels: 37.3 us -> 33.3 us
  waiting for transfers between devices: 49.2 us -> 51.9 us
  local copies, waits for them, and re-layouts: 5.65 us -> 4.24 us
    pallas_call x4, Pallas kernels: 29.3 us -> 25.3 us  [attend(): pl.pallas_call(functools.partial(attend_kernel, rows, has_outs), grid=(he...]
    all_to_all x4, waiting for transfers between devices: 42.6 us -> 45.6 us  [shards(): lax.all_to_all(packed[number], 'tensor', split_axis=0, concat_axis=0, til...]
    broadcast_in_dim x2 -> x0, local copies, waits for them, and re-layouts: 1.49 us -> none  [the longest x1 0.9 us: attend(): ids[:, None]]
    unnamed x20 -> x18, local copies, waits for them, and re-layouts: 4.07 us -> 3.33 us
  transfers between devices with their start and end apart: 12 -> 12, of which waited for: 5 -> 5; matrix products, arithmetic and copies ran while one was open for 1% -> 1% of each run, Pallas kernels for 25% -> 23%
where the time goes in v6:
time: 124 us; the launch traced here: 123 us
  waiting for transfers between devices  51.9 us (42%)
  Pallas kernels  33.3 us (27%)
  starting transfers between devices  32.1 us (26%)
  local copies, waits for them, and re-layouts  4.24 us (3%)
    all_to_all x4, waiting for transfers between devices, shards(): lax.all_to_all(packed[number], 'tensor', split_axis=0, concat_axis=0, til...  45.6 us
    pallas_call x4, Pallas kernels, attend(): pl.pallas_call(functools.partial(attend_kernel, rows, has_outs), grid=(he...  25.3 us
    ppermute x8, starting transfers between devices, swap_pairs(): return lax.ppermute(block, axis, route)  17.1 us
    all_to_all x4, starting transfers between devices, shards(): lax.all_to_all(packed[number], 'tensor', split_axis=0, concat_axis=0, til...  15 us
    pallas_call x4, Pallas kernels, pack(): pl.pallas_call(functools.partial(pack_kernel, parts, total // parts, firs...  7.98 us
    ppermute x8, waiting for transfers between devices, swap_pairs(): return lax.ppermute(block, axis, route)  6.31 us
    unnamed x18, local copies, waits for them, and re-layouts  3.33 us
  transfers between devices with their start and end apart: 12, of which 5 were waited for; matrix products, arithmetic and copies ran while one was open for 1% of the time, Pallas kernels for 23%

profile of v6, /device:TPU:3, one launch (start us, length us, event | category | flops | bytes accessed | tf_op | source)
XLA Modules:
  0.0 123.0 jit_solution(16093578852767753112)
XLA Ops:
  0.6 2.1 %shard_map.85 = bf16[4,4,64,512]{3,2,1,0:T(8,128)(2,1)} custom-call(bf16[64,6144]{1,0:T(8,128)(2,1)} %refs_0_.7, bf16[64,6144]{1,0:T(8,128)(2,1)} %refs_1_.7, bf16[64,6144]{1,0:T(8,128)(2,1)} %refs_2_.7, bf16[64,6144]{1,0:T(8,128)(2,1)} %refs_3_.7), custom_call_target="tpu_custom_call" | custom-call | flops 1 | bytes 1 | tf_op jit(solution)/shard_map/pallas_call | solution.py:78
  2.8 4.6 %all-to-all-start.1 = ((bf16[4,4,64,512]{3,2,1,0:T(8,128)(2,1)}), bf16[4,4,64,512]{3,2,1,0:T(8,128)(2,1)S(1)}, u32[]{:S(2)}, u32[]{:S(2)}) async-start(bf16[4,4,64,512]{3,2,1,0:T(8,128)(2,1)} %shard_map.85), calls=%async_computation.1 | async-start | bytes 2097152 | tf_op jit(solution)/shard_map/all_to_all | solution.py:295
  7.4 2.1 %shard_map.84.refs_1_ = bf16[4,4,64,512]{3,2,1,0:T(8,128)(2,1)} custom-call(bf16[64,6144]{1,0:T(8,128)(2,1)} %refs_0_.7, bf16[64,6144]{1,0:T(8,128)(2,1)} %refs_1_.7, bf16[64,6144]{1,0:T(8,128)(2,1)} %refs_2_.7, bf16[64,6144]{1,0:T(8,128)(2,1)} %refs_3_.7), custom_call_target="tpu_custom_call" | custom-call | flops 1 | bytes 1 | tf_op jit(solution)/shard_map/pallas_call | solution.py:78
  9.5 23.1 %all-to-all-done.1.refs_0_ = bf16[4,4,64,512]{3,2,1,0:T(8,128)(2,1)S(1)} async-done(((bf16[4,4,64,512]{3,2,1,0:T(8,128)(2,1)}), bf16[4,4,64,512]{3,2,1,0:T(8,128)(2,1)S(1)}, u32[]{:S(2)}, u32[]{:S(2)}) %all-to-all-start.1) | async-done | bytes 1048608 | tf_op jit(solution)/shard_map/all_to_all | solution.py:295
  32.6 3.5 %all-to-all-start = ((bf16[4,4,64,512]{3,2,1,0:T(8,128)(2,1)}), bf16[4,4,64,512]{3,2,1,0:T(8,128)(2,1)S(1)}, u32[]{:S(2)}, u32[]{:S(2)}) async-start(bf16[4,4,64,512]{3,2,1,0:T(8,128)(2,1)} %shard_map.84.refs_1_), calls=%async_computation | async-start | bytes 2097152 | tf_op jit(solution)/shard_map/all_to_all | solution.py:295
  36.1 1.5 %collective-permute-start.2 = (bf16[4,4,64,512]{3,2,1,0:T(8,128)(2,1)}, bf16[4,4,64,512]{3,2,1,0:T(8,128)(2,1)}, u32[]{:S(2)}, u32[]{:S(2)}) collective-permute-start(bf16[4,4,64,512]{3,2,1,0:T(8,128)(2,1)} %shard_map.86.refs_4_.refs_1_), channel_id=1, source_target_pairs={{0,4},{4,0},{8,12},{12,8},{16,20},{20,16},{24,28},{28,24},{1,5},{5... | collective-permute-start | bytes 3145736 | tf_op jit(solution)/shard_map/ppermute | solution.py:33
  37.7 3.0 %collective-permute-start.3 = (bf16[4,4,64,512]{3,2,1,0:T(8,128)(2,1)}, bf16[4,4,64,512]{3,2,1,0:T(8,128)(2,1)}, u32[]{:S(2)}, u32[]{:S(2)}) collective-permute-start(bf16[4,4,64,512]{3,2,1,0:T(8,128)(2,1)} %shard_map.86.refs_4_.refs_1_), channel_id=1, source_target_pairs={{4,8},{8,4},{12,16},{16,12},{20,24},{24,20},{5,9},{9,5},{13,17},{1... | collective-permute-start | bytes 3145736 | tf_op jit(solution)/shard_map/ppermute | solution.py:33
  40.7 2.0 %shard_map.87.refs_1_ = bf16[4,4,64,384]{3,2,1,0:T(8,128)(2,1)} custom-call(bf16[64,6144]{1,0:T(8,128)(2,1)} %refs_0_.7, bf16[64,6144]{1,0:T(8,128)(2,1)} %refs_1_.7, bf16[64,6144]{1,0:T(8,128)(2,1)} %refs_2_.7, bf16[64,6144]{1,0:T(8,128)(2,1)} %refs_3_.7, bf16[4,4,64,512]{3,2,1,0:T(8,128)(2,1)} %shard_map.86.refs_4_.refs_1_), custom_call_target="tpu_custom_call" | custom-call | flops 1 | bytes 1 | tf_op jit(solution)/shard_map/pallas_call | solution.py:78
  42.7 18.6 %all-to-all-done.refs_0_ = bf16[4,4,64,512]{3,2,1,0:T(8,128)(2,1)S(1)} async-done(((bf16[4,4,64,512]{3,2,1,0:T(8,128)(2,1)}), bf16[4,4,64,512]{3,2,1,0:T(8,128)(2,1)S(1)}, u32[]{:S(2)}, u32[]{:S(2)}) %all-to-all-start) | async-done | bytes 1048608 | tf_op jit(solution)/shard_map/all_to_all | solution.py:295
  61.3 3.5 %all-to-all-start.3 = ((bf16[4,4,64,384]{3,2,1,0:T(8,128)(2,1)}), bf16[4,4,64,384]{3,2,1,0:T(8,128)(2,1)S(1)}, u32[]{:S(2)}, u32[]{:S(2)}) async-start(bf16[4,4,64,384]{3,2,1,0:T(8,128)(2,1)} %shard_map.87.refs_1_), calls=%async_computation.3 | async-start | bytes 1572864 | tf_op jit(solution)/shard_map/all_to_all | solution.py:295
  64.8 1.5 %collective-permute-start = (bf16[4,4,64,512]{3,2,1,0:T(8,128)(2,1)}, bf16[4,4,64,512]{3,2,1,0:T(8,128)(2,1)S(1)}, u32[]{:S(2)}, u32[]{:S(2)}) collective-permute-start(bf16[4,4,64,512]{3,2,1,0:T(8,128)(2,1)} %shard_map.88.refs_4_.refs_1_), channel_id=1, source_target_pairs={{0,4},{4,0},{8,12},{12,8},{16,20},{20,16},{24,28},{28,24},{1,5},{5... | collective-permute-start | bytes 3145736 | tf_op jit(solution)/shard_map/ppermute | solution.py:33
  66.4 3.0 %collective-permute-start.1 = (bf16[4,4,64,512]{3,2,1,0:T(8,128)(2,1)}, bf16[4,4,64,512]{3,2,1,0:T(8,128)(2,1)}, u32[]{:S(2)}, u32[]{:S(2)}) collective-permute-start(bf16[4,4,64,512]{3,2,1,0:T(8,128)(2,1)} %shard_map.88.refs_4_.refs_1_), channel_id=1, source_target_pairs={{4,8},{8,4},{12,16},{16,12},{20,24},{24,20},{5,9},{9,5},{13,17},{1... | collective-permute-start | bytes 3145736 | tf_op jit(solution)/shard_map/ppermute | solution.py:33
  69.4 0.8 slice.3
  70.2 0.1 dynamic-slice_bitcast_fusion.2
  70.3 0.6 pad_add_fusion.refs_0_
  70.9 1.7 %shard_map.89.refs_1_ = bf16[4,4,64,128]{3,2,1,0:T(8,128)(2,1)} custom-call(bf16[64,6144]{1,0:T(8,128)(2,1)} %refs_0_.7, bf16[64,6144]{1,0:T(8,128)(2,1)} %refs_1_.7, bf16[64,6144]{1,0:T(8,128)(2,1)} %refs_2_.7, bf16[64,6144]{1,0:T(8,128)(2,1)} %refs_3_.7, bf16[4,4,64,512]{3,2,1,0:T(8,128)(2,1)} %shard_map.88.refs_4_.refs_1_), custom_call_target="tpu_custom_call" | custom-call | flops 1 | bytes 1 | tf_op jit(solution)/shard_map/pallas_call | solution.py:78
  72.6 7.8 %shard_map.90 = (bf16[256,1536]{1,0:T(8,128)(2,1)}, bf16[256,1536]{1,0:T(8,128)(2,1)}, bf16[256,1536]{1,0:T(8,128)(2,1)}, bf16[256,1536]{1,0:T(8,128)(2,1)}) custom-call(s32[3,4]{1,0:T(4,128)} %pad_add_fusion.refs_0_, bf16[4,4,64,512]{3,2,1,0:T(8,128)(2,1)} %shard_map.86.refs_4_.refs_1_, bf16[4,4,64,512]{3,2,1,0:T(8,128)(2,1)} %collective-permute-done.2.refs_2_, ...), custom_call_target="tpu_custom_call" | custom-call | flops 6000000000 | bytes 1 | tf_op jit(solution)/shard_map/pallas_call | solution.py:262
  80.4 3.9 %all-to-all-done.3.refs_0_ = bf16[4,4,64,384]{3,2,1,0:T(8,128)(2,1)S(1)} async-done(((bf16[4,4,64,384]{3,2,1,0:T(8,128)(2,1)}), bf16[4,4,64,384]{3,2,1,0:T(8,128)(2,1)S(1)}, u32[]{:S(2)}, u32[]{:S(2)}) %all-to-all-start.3) | async-done | bytes 786464 | tf_op jit(solution)/shard_map/all_to_all | solution.py:295
  84.4 0.9 copy-done.2
  85.3 1.5 %collective-permute-start.6 = (bf16[4,4,64,384]{3,2,1,0:T(8,128)(2,1)}, bf16[4,4,64,384]{3,2,1,0:T(8,128)(2,1)S(1)}, u32[]{:S(2)}, u32[]{:S(2)}) collective-permute-start(bf16[4,4,64,384]{3,2,1,0:T(8,128)(2,1)} %shard_map.93.refs_1_), channel_id=1, source_target_pairs={{0,4},{4,0},{8,12},{12,8},{16,20},{20,16},{24,28},{28,24},{1,5},{5... | collective-permute-start | bytes 2359304 | tf_op jit(solution)/shard_map/ppermute | solution.py:33
  86.7 3.1 %collective-permute-start.7 = (bf16[4,4,64,384]{3,2,1,0:T(8,128)(2,1)}, bf16[4,4,64,384]{3,2,1,0:T(8,128)(2,1)S(1)}, u32[]{:S(2)}, u32[]{:S(2)}) collective-permute-start(bf16[4,4,64,384]{3,2,1,0:T(8,128)(2,1)} %shard_map.93.refs_1_), channel_id=1, source_target_pairs={{4,8},{8,4},{12,16},{16,12},{20,24},{24,20},{5,9},{9,5},{13,17},{1... | collective-permute-start | bytes 2359304 | tf_op jit(solution)/shard_map/ppermute | solution.py:33
  89.8 3.4 %all-to-all-start.2 = ((bf16[4,4,64,128]{3,2,1,0:T(8,128)(2,1)}), bf16[4,4,64,128]{3,2,1,0:T(8,128)(2,1)S(1)}, u32[]{:S(2)}, u32[]{:S(2)}) async-start(bf16[4,4,64,128]{3,2,1,0:T(8,128)(2,1)} %shard_map.89.refs_1_), calls=%async_computation.2 | async-start | bytes 524288 | tf_op jit(solution)/shard_map/all_to_all | solution.py:295
  93.3 1.6 %collective-permute-done.1.refs_3_ = bf16[4,4,64,512]{3,2,1,0:T(8,128)(2,1)} collective-permute-done((bf16[4,4,64,512]{3,2,1,0:T(8,128)(2,1)}, bf16[4,4,64,512]{3,2,1,0:T(8,128)(2,1)}, u32[]{:S(2)}, u32[]{:S(2)}) %collective-permute-start.1) | collective-permute-done | bytes 1048608 | tf_op jit(solution)/shard_map/ppermute | solution.py:33
  94.9 7.8 %shard_map.91 = (bf16[256,1536]{1,0:T(8,128)(2,1)}, bf16[256,1536]{1,0:T(8,128)(2,1)}, bf16[256,1536]{1,0:T(8,128)(2,1)}, bf16[256,1536]{1,0:T(8,128)(2,1)}) custom-call(s32[3,4]{1,0:T(4,128)} %pad_add_fusion.refs_0_, bf16[4,4,64,512]{3,2,1,0:T(8,128)(2,1)} %shard_map.88.refs_4_.refs_1_, ...), custom_call_target="tpu_custom_call", output_to_operand_aliasing={{0}: (4, {}), {1}: (5, {}), {2}: (6, {}), {3}: (7, {})} | custom-call | flops 6000000000 | bytes 1 | tf_op jit(solution)/shard_map/pallas_call | solution.py:262
  102.7 0.7 copy-done.3
  103.4 0.2 collective-permute-start.4
  103.6 3.3 %collective-permute-start.5 = (bf16[4,4,64,128]{3,2,1,0:T(8,128)(2,1)}, bf16[4,4,64,128]{3,2,1,0:T(8,128)(2,1)S(1)}, u32[]{:S(2)}, u32[]{:S(2)}) collective-permute-start(bf16[4,4,64,128]{3,2,1,0:T(8,128)(2,1)} %shard_map.92.refs_1_), channel_id=1, source_target_pairs={{4,8},{8,4},{12,16},{16,12},{20,24},{24,20},{5,9},{9,5},{13,17},{1... | collective-permute-start | bytes 786440 | tf_op jit(solution)/shard_map/ppermute | solution.py:33
  106.9 4.7 %collective-permute-done.7.refs_3_ = bf16[4,4,64,384]{3,2,1,0:T(8,128)(2,1)S(1)} collective-permute-done((bf16[4,4,64,384]{3,2,1,0:T(8,128)(2,1)}, bf16[4,4,64,384]{3,2,1,0:T(8,128)(2,1)S(1)}, u32[]{:S(2)}, u32[]{:S(2)}) %collective-permute-start.7) | collective-permute-done | bytes 786464 | tf_op jit(solution)/shard_map/ppermute | solution.py:33
  111.6 0.9 copy-done.6
  112.5 6.3 %shard_map.94 = (bf16[256,1536]{1,0:T(8,128)(2,1)}, bf16[256,1536]{1,0:T(8,128)(2,1)}, bf16[256,1536]{1,0:T(8,128)(2,1)}, bf16[256,1536]{1,0:T(8,128)(2,1)}) custom-call(s32[3,4]{1,0:T(4,128)} %pad_add_fusion.refs_0_, bf16[4,4,64,384]{3,2,1,0:T(8,128)(2,1)} %shard_map.93.refs_1_, ...), custom_call_target="tpu_custom_call", output_to_operand_aliasing={{0}: (4, {}), {1}: (5, {}), {2}: (6, {}), {3}: (7, {})} | custom-call | flops 4499999744 | bytes 1 | tf_op jit(solution)/shard_map/pallas_call | solution.py:262
  118.9 0.7 copy-done.7
  119.7 3.4 %shard_map.95 = (bf16[256,1536]{1,0:T(8,128)(2,1)}, bf16[256,1536]{1,0:T(8,128)(2,1)}, bf16[256,1536]{1,0:T(8,128)(2,1)}, bf16[256,1536]{1,0:T(8,128)(2,1)}) custom-call(s32[3,4]{1,0:T(4,128)} %pad_add_fusion.refs_0_, bf16[4,4,64,128]{3,2,1,0:T(8,128)(2,1)} %shard_map.92.refs_1_, ...), custom_call_target="tpu_custom_call", output_to_operand_aliasing={{0}: (4, {}), {1}: (5, {}), {2}: (6, {}), {3}: (7, {})} | custom-call | flops 1500000000 | bytes 1 | tf_op jit(solution)/shard_map/pallas_call | solution.py:262
  (25 shorter events, 0.1 us)
Async XLA Ops:
  2.8 29.8 %all-to-all-start.1 = ((bf16[4,4,64,512]{3,2,1,0:T(8,128)(2,1)}), bf16[4,4,64,512]{3,2,1,0:T(8,128)(2,1)S(1)}, u32[]{:S(2)}, u32[]{:S(2)}) async-start(bf16[4,4,64,512]{3,2,1,0:T(8,128)(2,1)} %shard_map.85), calls=%async_computation.1 | async-start | bytes 2097152 | tf_op jit(solution)/shard_map/all_to_all | solution.py:295
  32.6 3.5 %copy-start = (bf16[4,4,64,512]{3,2,1,0:T(8,128)(2,1)}, bf16[4,4,64,512]{3,2,1,0:T(8,128)(2,1)S(1)}, u32[]{:S(2)}) copy-start(bf16[4,4,64,512]{3,2,1,0:T(8,128)(2,1)S(1)} %all-to-all-done.1.refs_0_) | copy-start | bytes 3145732
  32.6 28.7 %all-to-all-start = ((bf16[4,4,64,512]{3,2,1,0:T(8,128)(2,1)}), bf16[4,4,64,512]{3,2,1,0:T(8,128)(2,1)S(1)}, u32[]{:S(2)}, u32[]{:S(2)}) async-start(bf16[4,4,64,512]{3,2,1,0:T(8,128)(2,1)} %shard_map.84.refs_1_), calls=%async_computation | async-start | bytes 2097152 | tf_op jit(solution)/shard_map/all_to_all | solution.py:295
  36.1 36.5 %collective-permute-start.2 = (bf16[4,4,64,512]{3,2,1,0:T(8,128)(2,1)}, bf16[4,4,64,512]{3,2,1,0:T(8,128)(2,1)}, u32[]{:S(2)}, u32[]{:S(2)}) collective-permute-start(bf16[4,4,64,512]{3,2,1,0:T(8,128)(2,1)} %shard_map.86.refs_4_.refs_1_), channel_id=1, source_target_pairs={{0,4},{4,0},{8,12},{12,8},{16,20},{20,16},{24,28},{28,24},{1,5},{5... | collective-permute-start | bytes 3145736 | tf_op jit(solution)/shard_map/ppermute | solution.py:33
  37.7 35.0 %collective-permute-start.3 = (bf16[4,4,64,512]{3,2,1,0:T(8,128)(2,1)}, bf16[4,4,64,512]{3,2,1,0:T(8,128)(2,1)}, u32[]{:S(2)}, u32[]{:S(2)}) collective-permute-start(bf16[4,4,64,512]{3,2,1,0:T(8,128)(2,1)} %shard_map.86.refs_4_.refs_1_), channel_id=1, source_target_pairs={{4,8},{8,4},{12,16},{16,12},{20,24},{24,20},{5,9},{9,5},{13,17},{1... | collective-permute-start | bytes 3145736 | tf_op jit(solution)/shard_map/ppermute | solution.py:33
  61.3 3.5 %copy-start.1 = (bf16[4,4,64,512]{3,2,1,0:T(8,128)(2,1)}, bf16[4,4,64,512]{3,2,1,0:T(8,128)(2,1)S(1)}, u32[]{:S(2)}) copy-start(bf16[4,4,64,512]{3,2,1,0:T(8,128)(2,1)S(1)} %all-to-all-done.refs_0_) | copy-start | bytes 3145732
  61.3 23.1 %all-to-all-start.3 = ((bf16[4,4,64,384]{3,2,1,0:T(8,128)(2,1)}), bf16[4,4,64,384]{3,2,1,0:T(8,128)(2,1)S(1)}, u32[]{:S(2)}, u32[]{:S(2)}) async-start(bf16[4,4,64,384]{3,2,1,0:T(8,128)(2,1)} %shard_map.87.refs_1_), calls=%async_computation.3 | async-start | bytes 1572864 | tf_op jit(solution)/shard_map/all_to_all | solution.py:295
  64.8 28.4 %collective-permute-start = (bf16[4,4,64,512]{3,2,1,0:T(8,128)(2,1)}, bf16[4,4,64,512]{3,2,1,0:T(8,128)(2,1)S(1)}, u32[]{:S(2)}, u32[]{:S(2)}) collective-permute-start(bf16[4,4,64,512]{3,2,1,0:T(8,128)(2,1)} %shard_map.88.refs_4_.refs_1_), channel_id=1, source_target_pairs={{0,4},{4,0},{8,12},{12,8},{16,20},{20,16},{24,28},{28,24},{1,5},{5... | collective-permute-start | bytes 3145736 | tf_op jit(solution)/shard_map/ppermute | solution.py:33
  66.4 28.5 %collective-permute-start.1 = (bf16[4,4,64,512]{3,2,1,0:T(8,128)(2,1)}, bf16[4,4,64,512]{3,2,1,0:T(8,128)(2,1)}, u32[]{:S(2)}, u32[]{:S(2)}) collective-permute-start(bf16[4,4,64,512]{3,2,1,0:T(8,128)(2,1)} %shard_map.88.refs_4_.refs_1_), channel_id=1, source_target_pairs={{4,8},{8,4},{12,16},{16,12},{20,24},{24,20},{5,9},{9,5},{13,17},{1... | collective-permute-start | bytes 3145736 | tf_op jit(solution)/shard_map/ppermute | solution.py:33
  84.4 0.9 copy-start.2
  85.3 21.6 %collective-permute-start.6 = (bf16[4,4,64,384]{3,2,1,0:T(8,128)(2,1)}, bf16[4,4,64,384]{3,2,1,0:T(8,128)(2,1)S(1)}, u32[]{:S(2)}, u32[]{:S(2)}) collective-permute-start(bf16[4,4,64,384]{3,2,1,0:T(8,128)(2,1)} %shard_map.93.refs_1_), channel_id=1, source_target_pairs={{0,4},{4,0},{8,12},{12,8},{16,20},{20,16},{24,28},{28,24},{1,5},{5... | collective-permute-start | bytes 2359304 | tf_op jit(solution)/shard_map/ppermute | solution.py:33
  86.7 24.9 %collective-permute-start.7 = (bf16[4,4,64,384]{3,2,1,0:T(8,128)(2,1)}, bf16[4,4,64,384]{3,2,1,0:T(8,128)(2,1)S(1)}, u32[]{:S(2)}, u32[]{:S(2)}) collective-permute-start(bf16[4,4,64,384]{3,2,1,0:T(8,128)(2,1)} %shard_map.93.refs_1_), channel_id=1, source_target_pairs={{4,8},{8,4},{12,16},{16,12},{20,24},{24,20},{5,9},{9,5},{13,17},{1... | collective-permute-start | bytes 2359304 | tf_op jit(solution)/shard_map/ppermute | solution.py:33
  89.8 12.8 %all-to-all-start.2 = ((bf16[4,4,64,128]{3,2,1,0:T(8,128)(2,1)}), bf16[4,4,64,128]{3,2,1,0:T(8,128)(2,1)S(1)}, u32[]{:S(2)}, u32[]{:S(2)}) async-start(bf16[4,4,64,128]{3,2,1,0:T(8,128)(2,1)} %shard_map.89.refs_1_), calls=%async_computation.2 | async-start | bytes 524288 | tf_op jit(solution)/shard_map/all_to_all | solution.py:295
  93.3 1.6 %copy-start.4 = (bf16[4,4,64,512]{3,2,1,0:T(8,128)(2,1)}, bf16[4,4,64,512]{3,2,1,0:T(8,128)(2,1)S(1)}, u32[]{:S(2)}) copy-start(bf16[4,4,64,512]{3,2,1,0:T(8,128)(2,1)S(1)} %collective-permute-done.refs_2_) | copy-start | bytes 3145732
  102.7 0.7 copy-start.3
  103.4 15.4 %collective-permute-start.4 = (bf16[4,4,64,128]{3,2,1,0:T(8,128)(2,1)}, bf16[4,4,64,128]{3,2,1,0:T(8,128)(2,1)S(1)}, u32[]{:S(2)}, u32[]{:S(2)}) collective-permute-start(bf16[4,4,64,128]{3,2,1,0:T(8,128)(2,1)} %shard_map.92.refs_1_), channel_id=1, source_target_pairs={{0,4},{4,0},{8,12},{12,8},{16,20},{20,16},{24,28},{28,24},{1,5},{5... | collective-permute-start | bytes 786440 | tf_op jit(solution)/shard_map/ppermute | solution.py:33
  103.6 15.3 %collective-permute-start.5 = (bf16[4,4,64,128]{3,2,1,0:T(8,128)(2,1)}, bf16[4,4,64,128]{3,2,1,0:T(8,128)(2,1)S(1)}, u32[]{:S(2)}, u32[]{:S(2)}) collective-permute-start(bf16[4,4,64,128]{3,2,1,0:T(8,128)(2,1)} %shard_map.92.refs_1_), channel_id=1, source_target_pairs={{4,8},{8,4},{12,16},{16,12},{20,24},{24,20},{5,9},{9,5},{13,17},{1... | collective-permute-start | bytes 786440 | tf_op jit(solution)/shard_map/ppermute | solution.py:33
  106.9 4.7 %copy-start.5 = (bf16[4,4,64,384]{3,2,1,0:T(8,128)(2,1)}, bf16[4,4,64,384]{3,2,1,0:T(8,128)(2,1)S(1)}, u32[]{:S(2)}) copy-start(bf16[4,4,64,384]{3,2,1,0:T(8,128)(2,1)S(1)} %collective-permute-done.6.refs_2_) | copy-start | bytes 2359300
  111.6 0.9 copy-start.6
  118.8 0.7 copy-start.7
  118.9 0.8 copy-start.8

commit v7 on v6

v7 whole, which is shorter than its diff:
```python
import functools
import math

import jax
import jax.numpy as jnp
from jax import lax
from jax.experimental import pallas as pl
from jax.experimental.pallas import tpu as pltpu
from jax.sharding import PartitionSpec as P

HD = 128
SCALE = 1.0 / math.sqrt(HD)
EXP2_SCALE = SCALE * math.log2(math.e)
MASKED = -1e30
CHUNK_SHARES = (6, 4, 2)
VMEM_LIMIT = 63 * 1024 * 1024
ATTEND_FLOPS = 1_500_000_000
SMALL_COST = pl.CostEstimate(flops=1, bytes_accessed=1, transcendentals=0)


def split_counts(total, shares):
    whole = sum(shares)
    edges = [round(total * sum(shares[:i]) / whole) for i in range(len(shares) + 1)]
    return [(a, b - a) for a, b in zip(edges[:-1], edges[1:]) if b > a]


def swap_pairs(block, axis, first):
    count = lax.axis_size(axis)
    route = []
    for low in range(first, count - 1, 2):
        route += [(low, low + 1), (low + 1, low)]
    return lax.ppermute(block, axis, route)


def swap_flipped(block, axis, flip):
    return lax.ppermute(block, axis, [(i, i ^ flip) for i in range(lax.axis_size(axis))])


def nearby_ids(image_ids, parts, part_rows):
    shard = lax.axis_index("dp")
    padded = jnp.pad(image_ids[::part_rows], (parts, parts), constant_values=-1)
    odd = lax.rem(shard, 2)

    def ids_of(other):
        return lax.dynamic_slice_in_dim(padded, (other + 1) * parts, parts)

    return jnp.stack((ids_of(shard), ids_of(shard + 1 - 2 * odd), ids_of(shard - 1 + 2 * odd)))


def columns(array, part, stride, first, width):
    start = pl.multiple_of(part * stride + first, HD)
    return array.at[:, pl.ds(start, width)]


def pack_kernel(parts, stride, chunks, *refs):
    arrays, refs = refs[:4], refs[4:]
    own, packed, (stage, in_sems, out_sems) = refs[0], refs[1:-3], refs[-3:]
    me = lax.axis_index("tensor")
    jobs = [(0, 0, stride, own)]
    for number, (first, count) in enumerate(chunks):
        for flip in range(1, parts):
            target = packed[number * (parts - 1) + flip - 1]
            jobs.append((flip, first * HD, count * HD, target))
    jobs = jobs[1:parts] + jobs[:1] + jobs[parts:]
    loads, stores = [], []
    for number, (flip, first, width, _) in enumerate(jobs):
        for index, array in enumerate(arrays):
            load = pltpu.make_async_copy(
                columns(array, me ^ flip, stride, first, width),
                stage.at[flip, index, :, pl.ds(first, width)],
                in_sems.at[number * 4 + index],
            )
            load.start()
            loads.append(load)
    for number, (flip, first, width, target) in enumerate(jobs):
        for load in loads[number * 4 : number * 4 + 4]:
            load.wait()
        store = pltpu.make_async_copy(
            stage.at[flip, :, :, pl.ds(first, width)], target, out_sems.at[number]
        )
        store.start()
        stores.append(store)
    for store in stores:
        store.wait()


def pack(arrays, parts, chunks):
    rows, total = arrays[0].shape
    stride = total // parts
    widths = [stride] + [count * HD for _, count in chunks for _ in range(1, parts)]
    results = pl.pallas_call(
        functools.partial(pack_kernel, parts, stride, chunks),
        out_shape=[jax.ShapeDtypeStruct((4, rows, width), jnp.bfloat16) for width in widths],
        in_specs=[pl.BlockSpec(memory_space=pl.ANY)] * 4,
        out_specs=[pl.BlockSpec(memory_space=pl.ANY)] * len(widths),
        scratch_shapes=[
            pltpu.VMEM((parts, 4, rows, stride), jnp.bfloat16),
            pltpu.SemaphoreType.DMA((4 * len(widths),)),
            pltpu.SemaphoreType.DMA((len(widths),)),
        ],
        compiler_params=pltpu.CompilerParams(vmem_limit_bytes=VMEM_LIMIT),
        cost_estimate=SMALL_COST,
    )(*arrays)
    pieces = results[1:]
    return results[0], [
        pieces[start : start + parts - 1] for start in range(0, len(pieces), parts - 1)
    ]


def join_kernel(pieces, *refs):
    received, (joined, stage, in_sems, out_sems) = refs[:pieces], refs[-4:]
    loads, stores = [], []
    for piece in range(pieces):
        load = pltpu.make_async_copy(received[piece], stage.at[piece], in_sems.at[piece])
        load.start()
        loads.append(load)
    for piece in range(pieces):
        loads[piece].wait()
        store = pltpu.make_async_copy(stage.at[piece], joined.at[piece], out_sems.at[piece])
        store.start()
        stores.append(store)
    for store in stores:
        store.wait()


def join(received, after):
    pieces = len(received)
    shape = (pieces,) + received[0].shape
    return pl.pallas_call(
        functools.partial(join_kernel, pieces),
        out_shape=jax.ShapeDtypeStruct(shape, jnp.bfloat16),
        in_specs=[pl.BlockSpec(memory_space=pl.ANY)] * (pieces + len(after)),
        out_specs=pl.BlockSpec(memory_space=pl.ANY),
        scratch_shapes=[
            pltpu.VMEM(shape, jnp.bfloat16),
            pltpu.SemaphoreType.DMA((pieces,)),
            pltpu.SemaphoreType.DMA((pieces,)),
        ],
        compiler_params=pltpu.CompilerParams(vmem_limit_bytes=VMEM_LIMIT),
        cost_estimate=SMALL_COST,
    )(*received, *after)


def hold(array, after):
    return pl.pallas_call(
        lambda *refs: None,
        out_shape=jax.ShapeDtypeStruct(array.shape, array.dtype),
        in_specs=[pl.BlockSpec(memory_space=pl.ANY)] * (1 + len(after)),
        out_specs=pl.BlockSpec(memory_space=pl.ANY),
        input_output_aliases={0: 0},
        compiler_params=pltpu.CompilerParams(vmem_limit_bytes=VMEM_LIMIT),
        cost_estimate=SMALL_COST,
    )(array, *after)


def dot_nt(a, b):
    return lax.dot_general(a, b, (((1,), (1,)), ((), ())), preferred_element_type=jnp.float32)


def dot_tn(a, b):
    return lax.dot_general(a, b, (((0,), (0,)), ((), ())), preferred_element_type=jnp.float32)


def dot_nn(a, b):
    return jnp.dot(a, b, preferred_element_type=jnp.float32)


def attend_head(values_of, bias, size, rows):
    queries, keys, values, grads = values_of
    grad_k = grad_v = None
    for start in range(0, size, rows):
        tile = slice(start, start + rows)
        scores = dot_nt(keys, queries[tile]) + bias[:size, tile]
        weights = jnp.exp2((scores - jnp.max(scores, axis=0, keepdims=True)) * EXP2_SCALE)
        probs = weights * (1.0 / jnp.sum(weights, axis=0, keepdims=True))
        grad_probs = dot_nt(values, grads[tile])
        inner = jnp.sum(probs * grad_probs, axis=0, keepdims=True)
        low = probs.astype(jnp.bfloat16)
        grad_scores = (probs * (grad_probs - inner)).astype(jnp.bfloat16)
        tile_v = dot_nn(low[:rows], grads[tile])
        tile_k = dot_nn(grad_scores[:rows], queries[tile])
        if start == 0:
            attended = dot_tn(low, values)
            grad_q = dot_tn(grad_scores, keys)
            grad_k, grad_v = tile_k, tile_v
        else:
            grad_k, grad_v = grad_k + tile_k, grad_v + tile_v
    return attended, grad_q * SCALE, grad_k * SCALE, grad_v


def attend_kernel(parts, has_outs, *refs):
    image_ids, groups = refs[0], (refs[1:3], refs[3:5], refs[5:7])
    refs = refs[7 + (4 if has_outs else 0) :]
    outs, (bias, gathered, table) = refs[:4], refs[4:]
    part_rows = groups[0][0].shape[1]
    rows = parts * part_rows
    most = 3 * rows
    me = lax.axis_index("tensor")

    def id_of(group, slot):
        return image_ids[group, me ^ slot]

    @pl.when(pl.program_id(0) == 0)
    def _():
        count = jnp.int32(0)
        for other in range(2 * parts):
            other_id = id_of(1 + other // parts, other % parts)
            shared = other_id == id_of(0, 0)
            for slot in range(1, parts):
                shared = shared | (other_id == id_of(0, slot))
            table[count] = other
            count = count + shared.astype(jnp.int32)
        table[2 * parts] = count

        def ids_along(axis):
            shape = (most, 1) if axis == 0 else (1, most)
            place = lax.broadcasted_iota(jnp.int32, shape, axis)
            ids = jnp.full(shape, -2, jnp.int32)
            for slot in range(3 * parts):
                if slot < parts:
                    slot_id = id_of(0, slot)
                else:
                    used = slot - parts < count
                    source = jnp.where(used, table[slot - parts], 0)
                    slot_id = id_of(1 + source // parts, lax.rem(source, parts))
                    slot_id = jnp.where(used, slot_id, -2)
                inside = (place >= slot * part_rows) & (place < (slot + 1) * part_rows)
                ids = jnp.where(inside, slot_id, ids)
            return ids

        bias[...] = jnp.where(ids_along(0) == ids_along(1), 0.0, MASKED)

    count = table[2 * parts]

    def other_part(slot, index):
        source = jnp.where(slot < count, table[slot], 0)
        place = lax.rem(source, parts)
        taken = [
            jnp.where(place == 0, first[index], rest[jnp.maximum(place - 1, 0), index])
            for first, rest in groups[1:]
        ]
        return jnp.where(source < parts, *taken)

    for size in range(rows, most + 1, rows):
        slots = (size - rows) // part_rows

        @pl.when((count <= slots) & (count > slots - parts))
        def _():
            for slot in range(slots):
                for index in range(4):
                    place = slice(slot * part_rows, (slot + 1) * part_rows)
                    gathered[index, place] = other_part(slot, index)
            values_of = []
            for index in range(4):
                first, rest = groups[0]
                mine = [first[index], rest[:, index].reshape(rows - part_rows, HD)]
                if slots:
                    mine.append(gathered[index, : size - rows])
                values_of.append(jnp.concatenate(mine))
            for out, result in zip(outs, attend_head(values_of, bias, size, rows)):
                result = result.astype(jnp.bfloat16)
                for slot in range(parts):
                    target = pl.multiple_of((me ^ slot) * part_rows, part_rows)
                    out[pl.ds(target, part_rows), :] = result[
                        slot * part_rows : (slot + 1) * part_rows
                    ]


def attend(image_ids, groups, outs, first_head):
    (first, rest) = groups[0]
    others, _, part_rows, width = rest.shape
    parts = others + 1
    rows = parts * part_rows
    heads = width // HD
    first_block = pl.BlockSpec((4, part_rows, HD), lambda h: (0, 0, h + first_head))
    rest_block = pl.BlockSpec((others, 4, part_rows, HD), lambda h: (0, 0, 0, h))
    out_spec = pl.BlockSpec((rows, HD), lambda h: (0, h + first_head))
    has_outs = outs is not None
    aliases = {7 + i: i for i in range(4)} if has_outs else {}
    return pl.pallas_call(
        functools.partial(attend_kernel, parts, has_outs),
        grid=(heads,),
        out_shape=[jax.ShapeDtypeStruct((rows, first.shape[2]), jnp.bfloat16)] * 4,
        in_specs=[pl.BlockSpec(memory_space=pltpu.SMEM)]
        + [first_block, rest_block] * 3
        + ([pl.BlockSpec(memory_space=pl.ANY)] * 4 if has_outs else []),
        out_specs=[out_spec] * 4,
        scratch_shapes=[
            pltpu.VMEM((3 * rows, 3 * rows), jnp.float32),
            pltpu.VMEM((4, 2 * rows, HD), jnp.bfloat16),
            pltpu.SMEM((2 * parts + 1,), jnp.int32),
        ],
        input_output_aliases=aliases,
        compiler_params=pltpu.CompilerParams(
            dimension_semantics=("arbitrary",), vmem_limit_bytes=VMEM_LIMIT
        ),
        cost_estimate=pl.CostEstimate(
            flops=heads * ATTEND_FLOPS, bytes_accessed=1, transcendentals=0
        ),
    )(image_ids, *groups[0], *groups[1], *groups[2], *(outs or ()))


def shards(queries, key_vectors, value_vectors, grad_output, image_ids):
    arrays = (queries, key_vectors, value_vectors, grad_output)
    parts = lax.axis_size("tensor")
    part_rows = queries.shape[0]
    head_total = queries.shape[1] // HD // parts
    near_ids = nearby_ids(image_ids, parts, part_rows)
    chunks = split_counts(head_total, CHUNK_SHARES)

    def cross(packed):
        return [
            swap_flipped(piece, "tensor", flip) for flip, piece in enumerate(packed, start=1)
        ]

    first, packed = pack(arrays, parts, chunks)
    received = [cross(packed[0])]
    near_first = swap_pairs(first, "dp", 0)
    far_first = swap_pairs(first, "dp", 1)
    firsts = [near_first, far_first]
    outs, out_history = None, []
    for number, (first_head, _) in enumerate(chunks):
        if number + 1 < len(chunks):
            held = [
                hold(piece, [done] + (firsts if number == 0 else []))
                for piece, done in zip(packed[number + 1], received[number])
            ]
            received.append(cross(held))
        after = [out_history[number - 2][0]] if number >= 2 else []
        after += firsts if number == 0 else []
        rest = join(received[number], after)
        near_rest = swap_pairs(rest, "dp", 0)
        far_rest = swap_pairs(rest, "dp", 1)
        groups = ((first, rest), (near_first, near_rest), (far_first, far_rest))
        outs = attend(near_ids, groups, outs, first_head)
        out_history.append(outs)
    return tuple(outs)


def solution(mesh):
    return jax.shard_map(
        shards,
        mesh=mesh,
        in_specs=(
            P(("dp", "tensor"), None),
            P(("dp", "tensor"), None),
            P(("dp", "tensor"), None),
            P(("dp", "tensor"), None),
            P(),
        ),
        out_specs=(P("dp", "tensor"), P("dp", "tensor"), P("dp", "tensor"), P("dp", "tensor")),
        check_vma=False,
    )
```

time: 124 us -> 123 us (level)
  the two profiles are of different devices: /device:TPU:3 before, /device:TPU:1 now
where the time goes in v7:
time: 123 us
  waiting for transfers between devices  44 us (36%)
  starting transfers between devices  39.6 us (32%)
  Pallas kernels  32.8 us (27%)
  local copies, waits for them, and re-layouts  4.84 us (4%)
    ppermute x9, waiting for transfers between devices, swap_flipped(): lax.ppermute(block, axis, [(i, i ^ flip) for i in range(lax.axis_size(axi...  41.8 us
    pallas_call x3, Pallas kernels, attend(): pl.pallas_call(functools.partial(attend_kernel, parts, has_outs), grid=(h...  23.8 us
    ppermute x8, starting transfers between devices, swap_pairs(): return lax.ppermute(block, axis, route)  19.8 us
    ppermute x9, starting transfers between devices, swap_flipped(): lax.ppermute(block, axis, [(i, i ^ flip) for i in range(lax.axis_size(axi...  19.8 us
    pallas_call x3, Pallas kernels, join(): pl.pallas_call(functools.partial(join_kernel, pieces), out_shape=jax.Shap...  5.71 us
    unnamed x24, local copies, waits for them, and re-layouts  3.94 us
    pallas_call x1, Pallas kernels, pack(): pl.pallas_call(functools.partial(pack_kernel, parts, stride, chunks), out...  3.29 us
  transfers between devices with their start and end apart: 17, of which 5 were waited for; matrix products, arithmetic and copies ran while one was open for 1% of the time, Pallas kernels for 18%

profile of v7, /device:TPU:1, one launch (start us, length us, event | category | flops | bytes accessed | tf_op | source)
XLA Modules:
  0.0 122.7 jit_solution(7943938694347315152)
XLA Ops:
  0.6 3.3 %shard_map.84 = (bf16[4,64,1536]{2,1,0:T(8,128)(2,1)}, bf16[4,64,768]{2,1,0:T(8,128)(2,1)}, bf16[4,64,768]{2,1,0:T(8,128)(2,1)}, bf16[4,64,768]{2,1,0:T(8,128)(2...) custom-call(bf16[64,6144]{1,0:T(8,128)(2,1)} %refs_0_.1, ...), custom_call_target="tpu_custom_call" | custom-call | flops 1 | bytes 1 | tf_op jit(solution)/shard_map/pallas_call | solution.py:91
  3.9 4.5 %collective-permute-start.2 = (bf16[4,64,1536]{2,1,0:T(8,128)(2,1)}, bf16[4,64,1536]{2,1,0:T(8,128)(2,1)S(1)}, u32[]{:S(2)}, u32[]{:S(2)}) collective-permute-start(bf16[4,64,1536]{2,1,0:T(8,128)(2,1)} %get-tuple-element.22.refs_1_), channel_id=1, source_target_pairs={{4,8},{8,4},{12,16},{16,12},{20,24},{24,20},{5,9},{9,5},{13,17},{1... | collective-permute-start | bytes 2359304 | tf_op jit(solution)/shard_map/ppermute | solution.py:32
  8.5 1.4 %collective-permute-start = (bf16[4,64,768]{2,1,0:T(8,128)(2,1)}, bf16[4,64,768]{2,1,0:T(8,128)(2,1)S(1)}, u32[]{:S(2)}, u32[]{:S(2)}) collective-permute-start(bf16[4,64,768]{2,1,0:T(8,128)(2,1)} %get-tuple-element.25), channel_id=1, source_target_pairs={{0,1},{1,0},{2,3},{3,2},{4,5},{5,4},{6,7},{7,6},{8,9},{9,8},{10,11... | collective-permute-start | bytes 1179656 | tf_op jit(solution)/shard_map/ppermute | solution.py:36
  9.9 2.3 %collective-permute-start.5 = (bf16[4,64,768]{2,1,0:T(8,128)(2,1)}, bf16[4,64,768]{2,1,0:T(8,128)(2,1)S(1)}, u32[]{:S(2)}, u32[]{:S(2)}) collective-permute-start(bf16[4,64,768]{2,1,0:T(8,128)(2,1)} %get-tuple-element.28), channel_id=1, source_target_pairs={{0,2},{1,3},{2,0},{3,1},{4,6},{5,7},{6,4},{7,5},{8,10},{9,11},{10,... | collective-permute-start | bytes 1179656 | tf_op jit(solution)/shard_map/ppermute | solution.py:36
  12.2 14.7 %collective-permute-done.refs_1_.refs_0_ = bf16[4,64,768]{2,1,0:T(8,128)(2,1)S(1)} collective-permute-done((bf16[4,64,768]{2,1,0:T(8,128)(2,1)}, bf16[4,64,768]{2,1,0:T(8,128)(2,1)S(1)}, u32[]{:S(2)}, u32[]{:S(2)}) %collective-permute-start) | collective-permute-done | bytes 393248 | tf_op jit(solution)/shard_map/ppermute | solution.py:36
  26.9 11.1 %collective-permute-done.8.refs_1_.refs_2_ = bf16[4,64,768]{2,1,0:T(8,128)(2,1)S(1)} collective-permute-done((bf16[4,64,768]{2,1,0:T(8,128)(2,1)}, bf16[4,64,768]{2,1,0:T(8,128)(2,1)S(1)}, u32[]{:S(2)}, u32[]{:S(2)}) %collective-permute-start.8) | collective-permute-done | bytes 393248 | tf_op jit(solution)/shard_map/ppermute | solution.py:36
  38.0 0.7 copy-done.1
  38.7 0.9 copy-done
  39.6 2.1 %shard_map.91.refs_2_ = bf16[3,4,64,768]{3,2,1,0:T(8,128)(2,1)} custom-call(bf16[4,64,768]{2,1,0:T(8,128)(2,1)} %copy-done.3, bf16[4,64,768]{2,1,0:T(8,128)(2,1)} %copy-done.2, bf16[4,64,768]{2,1,0:T(8,128)(2,1)} %copy-done.1, bf16[4,64,1536]{2,1,0:T(8,128)(2,1)} %collective-permute-done.1.refs_2_.refs_3_, bf16[4,64,1536]{2,1,0:T(8,128)(2,1)} %copy-done), custom_call_target="tpu_custom_call" | custom-call | flops 1 | bytes 1 | tf_op jit(solution)/shard_map/pallas_call | solution.py:129
  41.7 5.7 %collective-permute-start.12 = (bf16[3,4,64,768]{3,2,1,0:T(8,128)(2,1)}, bf16[3,4,64,768]{3,2,1,0:T(8,128)(2,1)}, u32[]{:S(2)}, u32[]{:S(2)}) collective-permute-start(bf16[3,4,64,768]{3,2,1,0:T(8,128)(2,1)} %shard_map.91.refs_2_), channel_id=1, source_target_pairs={{4,8},{8,4},{12,16},{16,12},{20,24},{24,20},{5,9},{9,5},{13,17},{1... | collective-permute-start | bytes 3538952 | tf_op jit(solution)/shard_map/ppermute | solution.py:32
  47.5 7.5 %collective-permute-start.3 = (bf16[4,64,512]{2,1,0:T(8,128)(2,1)}, bf16[4,64,512]{2,1,0:T(8,128)(2,1)S(1)}, u32[]{:S(2)}, u32[]{:S(2)}) collective-permute-start(bf16[4,64,512]{2,1,0:T(8,128)(2,1)} %shard_map.85), channel_id=1, source_target_pairs={{0,1},{1,0},{2,3},{3,2},{4,5},{5,4},{6,7},{7,6},{8,9},{9,8},{10,11... | collective-permute-start | bytes 786440 | tf_op jit(solution)/shard_map/ppermute | solution.py:36
  55.0 1.1 collective-permute-start.6
  56.1 1.1 collective-permute-start.9
  57.2 0.8 slice.3
  58.1 0.6 pad_add_fusion.refs_0_
  58.7 7.9 %collective-permute-done.3.refs_1_.refs_0_ = bf16[4,64,512]{2,1,0:T(8,128)(2,1)S(1)} collective-permute-done((bf16[4,64,512]{2,1,0:T(8,128)(2,1)}, bf16[4,64,512]{2,1,0:T(8,128)(2,1)S(1)}, u32[]{:S(2)}, u32[]{:S(2)}) %collective-permute-start.3) | collective-permute-done | bytes 262176 | tf_op jit(solution)/shard_map/ppermute | solution.py:36
  66.6 8.1 %collective-permute-done.9.refs_1_.refs_2_ = bf16[4,64,512]{2,1,0:T(8,128)(2,1)S(1)} collective-permute-done((bf16[4,64,512]{2,1,0:T(8,128)(2,1)}, bf16[4,64,512]{2,1,0:T(8,128)(2,1)S(1)}, u32[]{:S(2)}, u32[]{:S(2)}) %collective-permute-start.9) | collective-permute-done | bytes 262176 | tf_op jit(solution)/shard_map/ppermute | solution.py:36
  74.7 0.7 copy-done.6
  75.4 1.9 %shard_map.94.refs_2_ = bf16[3,4,64,512]{3,2,1,0:T(8,128)(2,1)} custom-call(bf16[4,64,512]{2,1,0:T(8,128)(2,1)} %copy-done.4, bf16[4,64,512]{2,1,0:T(8,128)(2,1)} %copy-done.5, bf16[4,64,512]{2,1,0:T(8,128)(2,1)} %copy-done.6), custom_call_target="tpu_custom_call" | custom-call | flops 1 | bytes 1 | tf_op jit(solution)/shard_map/pallas_call | solution.py:129
  77.3 6.3 %collective-permute-start.16 = (bf16[3,4,64,512]{3,2,1,0:T(8,128)(2,1)}, bf16[3,4,64,512]{3,2,1,0:T(8,128)(2,1)}, u32[]{:S(2)}, u32[]{:S(2)}) collective-permute-start(bf16[3,4,64,512]{3,2,1,0:T(8,128)(2,1)} %shard_map.94.refs_2_), channel_id=1, source_target_pairs={{4,8},{8,4},{12,16},{16,12},{20,24},{24,20},{5,9},{9,5},{13,17},{1... | collective-permute-start | bytes 2359304 | tf_op jit(solution)/shard_map/ppermute | solution.py:32
  83.7 4.1 %collective-permute-start.4 = (bf16[4,64,256]{2,1,0:T(8,128)(2,1)}, bf16[4,64,256]{2,1,0:T(8,128)(2,1)S(1)}, u32[]{:S(2)}, u32[]{:S(2)}) collective-permute-start(bf16[4,64,256]{2,1,0:T(8,128)(2,1)} %shard_map.86), channel_id=1, source_target_pairs={{0,1},{1,0},{2,3},{3,2},{4,5},{5,4},{6,7},{7,6},{8,9},{9,8},{10,11... | collective-permute-start | bytes 393224 | tf_op jit(solution)/shard_map/ppermute | solution.py:36
  87.8 1.1 collective-permute-start.7
  88.9 1.2 collective-permute-start.10
  90.1 10.8 %shard_map.92 = (bf16[256,1536]{1,0:T(8,128)(2,1)}, bf16[256,1536]{1,0:T(8,128)(2,1)}, bf16[256,1536]{1,0:T(8,128)(2,1)}, bf16[256,1536]{1,0:T(8,128)(2,1)}) custom-call(s32[3,4]{1,0:T(4,128)} %pad_add_fusion.refs_0_, bf16[4,64,1536]{2,1,0:T(8,128)(2,1)} %get-tuple-element.22.refs_1_, bf16[3,4,64,768]{3,2,1,0:T(8,128)(2,1)} %shard_map.91.refs_2_, ...), custom_call_target="tpu_custom_call" | custom-call | flops 8999999488 | bytes 1 | tf_op jit(solution)/shard_map/pallas_call | solution.py:280
  101.0 0.6 copy-done.7
  101.7 1.7 %shard_map.93.refs_2_ = bf16[3,4,64,256]{3,2,1,0:T(8,128)(2,1)} custom-call(bf16[4,64,256]{2,1,0:T(8,128)(2,1)} %copy-done.7, bf16[4,64,256]{2,1,0:T(8,128)(2,1)} %copy-done.8, bf16[4,64,256]{2,1,0:T(8,128)(2,1)} %copy-done.9, bf16[256,1536]{1,0:T(8,128)(2,1)} %get-tuple-element.32.refs_3_.refs_7_), custom_call_target="tpu_custom_call" | custom-call | flops 1 | bytes 1 | tf_op jit(solution)/shard_map/pallas_call | solution.py:129
  103.4 3.0 %collective-permute-start.14 = (bf16[3,4,64,256]{3,2,1,0:T(8,128)(2,1)}, bf16[3,4,64,256]{3,2,1,0:T(8,128)(2,1)S(1)}, u32[]{:S(2)}, u32[]{:S(2)}) collective-permute-start(bf16[3,4,64,256]{3,2,1,0:T(8,128)(2,1)} %shard_map.93.refs_2_), channel_id=1, source_target_pairs={{4,8},{8,4},{12,16},{16,12},{20,24},{24,20},{5,9},{9,5},{13,17},{1... | collective-permute-start | bytes 1179656 | tf_op jit(solution)/shard_map/ppermute | solution.py:32
  106.6 8.0 %shard_map.95 = (bf16[256,1536]{1,0:T(8,128)(2,1)}, bf16[256,1536]{1,0:T(8,128)(2,1)}, bf16[256,1536]{1,0:T(8,128)(2,1)}, bf16[256,1536]{1,0:T(8,128)(2,1)}) custom-call(s32[3,4]{1,0:T(4,128)} %pad_add_fusion.refs_0_, bf16[4,64,1536]{2,1,0:T(8,128)(2,1)} %get-tuple-element.22.refs_1_, ...), custom_call_target="tpu_custom_call", output_to_operand_aliasing={{0}: (7, {}), {1}: (8, {}), {2}: (9, {}), {3}: (10, {})} | custom-call | flops 6000000000 | bytes 1 | tf_op jit(solution)/shard_map/pallas_call | solution.py:280
  114.5 2.2 %collective-permute-done.14.refs_6_ = bf16[3,4,64,256]{3,2,1,0:T(8,128)(2,1)S(1)} collective-permute-done((bf16[3,4,64,256]{3,2,1,0:T(8,128)(2,1)}, bf16[3,4,64,256]{3,2,1,0:T(8,128)(2,1)S(1)}, u32[]{:S(2)}, u32[]{:S(2)}) %collective-permute-start.14) | collective-permute-done | bytes 393248 | tf_op jit(solution)/shard_map/ppermute | solution.py:32
  116.7 0.8 copy-done.10
  117.5 0.1 copy-done.11
  117.6 5.0 %shard_map.96 = (bf16[256,1536]{1,0:T(8,128)(2,1)}, bf16[256,1536]{1,0:T(8,128)(2,1)}, bf16[256,1536]{1,0:T(8,128)(2,1)}, bf16[256,1536]{1,0:T(8,128)(2,1)}) custom-call(s32[3,4]{1,0:T(4,128)} %pad_add_fusion.refs_0_, bf16[4,64,1536]{2,1,0:T(8,128)(2,1)} %get-tuple-element.22.refs_1_, ...), custom_call_target="tpu_custom_call", output_to_operand_aliasing={{0}: (7, {}), {1}: (8, {}), {2}: (9, {}), {3}: (10, {})} | custom-call | flops 3000000000 | bytes 1 | tf_op jit(solution)/shard_map/pallas_call | solution.py:280
  (42 shorter events, 0.6 us)
Async XLA Ops:
  3.9 34.1 %collective-permute-start.2 = (bf16[4,64,1536]{2,1,0:T(8,128)(2,1)}, bf16[4,64,1536]{2,1,0:T(8,128)(2,1)S(1)}, u32[]{:S(2)}, u32[]{:S(2)}) collective-permute-start(bf16[4,64,1536]{2,1,0:T(8,128)(2,1)} %get-tuple-element.22.refs_1_), channel_id=1, source_target_pairs={{4,8},{8,4},{12,16},{16,12},{20,24},{24,20},{5,9},{9,5},{13,17},{1... | collective-permute-start | bytes 2359304 | tf_op jit(solution)/shard_map/ppermute | solution.py:32
  8.4 30.3 %collective-permute-start.1 = (bf16[4,64,1536]{2,1,0:T(8,128)(2,1)}, bf16[4,64,1536]{2,1,0:T(8,128)(2,1)}, u32[]{:S(2)}, u32[]{:S(2)}) collective-permute-start(bf16[4,64,1536]{2,1,0:T(8,128)(2,1)} %get-tuple-element.22.refs_1_), channel_id=1, source_target_pairs={{0,4},{4,0},{8,12},{12,8},{16,20},{20,16},{24,28},{28,24},{1,5},{5... | collective-permute-start | bytes 2359304 | tf_op jit(solution)/shard_map/ppermute | solution.py:32
  8.5 18.3 %collective-permute-start = (bf16[4,64,768]{2,1,0:T(8,128)(2,1)}, bf16[4,64,768]{2,1,0:T(8,128)(2,1)S(1)}, u32[]{:S(2)}, u32[]{:S(2)}) collective-permute-start(bf16[4,64,768]{2,1,0:T(8,128)(2,1)} %get-tuple-element.25), channel_id=1, source_target_pairs={{0,1},{1,0},{2,3},{3,2},{4,5},{5,4},{6,7},{7,6},{8,9},{9,8},{10,11... | collective-permute-start | bytes 1179656 | tf_op jit(solution)/shard_map/ppermute | solution.py:36
  9.9 17.0 %collective-permute-start.5 = (bf16[4,64,768]{2,1,0:T(8,128)(2,1)}, bf16[4,64,768]{2,1,0:T(8,128)(2,1)S(1)}, u32[]{:S(2)}, u32[]{:S(2)}) collective-permute-start(bf16[4,64,768]{2,1,0:T(8,128)(2,1)} %get-tuple-element.28), channel_id=1, source_target_pairs={{0,2},{1,3},{2,0},{3,1},{4,6},{5,7},{6,4},{7,5},{8,10},{9,11},{10,... | collective-permute-start | bytes 1179656 | tf_op jit(solution)/shard_map/ppermute | solution.py:36
  12.2 25.8 %collective-permute-start.8 = (bf16[4,64,768]{2,1,0:T(8,128)(2,1)}, bf16[4,64,768]{2,1,0:T(8,128)(2,1)S(1)}, u32[]{:S(2)}, u32[]{:S(2)}) collective-permute-start(bf16[4,64,768]{2,1,0:T(8,128)(2,1)} %get-tuple-element.31), channel_id=1, source_target_pairs={{0,3},{1,2},{2,1},{3,0},{4,7},{5,6},{6,5},{7,4},{8,11},{9,10},{10,... | collective-permute-start | bytes 1179656 | tf_op jit(solution)/shard_map/ppermute | solution.py:36
  26.9 11.1 %copy-start.3 = (bf16[4,64,768]{2,1,0:T(8,128)(2,1)}, bf16[4,64,768]{2,1,0:T(8,128)(2,1)S(1)}, u32[]{:S(2)}) copy-start(bf16[4,64,768]{2,1,0:T(8,128)(2,1)S(1)} %collective-permute-done.refs_1_.refs_0_) | copy-start | bytes 1179652
  26.9 11.1 %copy-start.2 = (bf16[4,64,768]{2,1,0:T(8,128)(2,1)}, bf16[4,64,768]{2,1,0:T(8,128)(2,1)S(1)}, u32[]{:S(2)}) copy-start(bf16[4,64,768]{2,1,0:T(8,128)(2,1)S(1)} %collective-permute-done.5.refs_1_) | copy-start | bytes 1179652
  38.0 0.7 copy-start.1
  38.7 0.9 copy-start
  41.7 46.1 %collective-permute-start.12 = (bf16[3,4,64,768]{3,2,1,0:T(8,128)(2,1)}, bf16[3,4,64,768]{3,2,1,0:T(8,128)(2,1)}, u32[]{:S(2)}, u32[]{:S(2)}) collective-permute-start(bf16[3,4,64,768]{3,2,1,0:T(8,128)(2,1)} %shard_map.91.refs_2_), channel_id=1, source_target_pairs={{4,8},{8,4},{12,16},{16,12},{20,24},{24,20},{5,9},{9,5},{13,17},{1... | collective-permute-start | bytes 3538952 | tf_op jit(solution)/shard_map/ppermute | solution.py:32
  47.4 41.5 %collective-permute-start.11 = (bf16[3,4,64,768]{3,2,1,0:T(8,128)(2,1)}, bf16[3,4,64,768]{3,2,1,0:T(8,128)(2,1)}, u32[]{:S(2)}, u32[]{:S(2)}) collective-permute-start(bf16[3,4,64,768]{3,2,1,0:T(8,128)(2,1)} %shard_map.91.refs_2_), channel_id=1, source_target_pairs={{0,4},{4,0},{8,12},{12,8},{16,20},{20,16},{24,28},{28,24},{1,5},{5... | collective-permute-start | bytes 3538952 | tf_op jit(solution)/shard_map/ppermute | solution.py:32
  47.5 19.0 %collective-permute-start.3 = (bf16[4,64,512]{2,1,0:T(8,128)(2,1)}, bf16[4,64,512]{2,1,0:T(8,128)(2,1)S(1)}, u32[]{:S(2)}, u32[]{:S(2)}) collective-permute-start(bf16[4,64,512]{2,1,0:T(8,128)(2,1)} %shard_map.85), channel_id=1, source_target_pairs={{0,1},{1,0},{2,3},{3,2},{4,5},{5,4},{6,7},{7,6},{8,9},{9,8},{10,11... | collective-permute-start | bytes 786440 | tf_op jit(solution)/shard_map/ppermute | solution.py:36
  55.0 11.5 %collective-permute-start.6 = (bf16[4,64,512]{2,1,0:T(8,128)(2,1)}, bf16[4,64,512]{2,1,0:T(8,128)(2,1)S(1)}, u32[]{:S(2)}, u32[]{:S(2)}) collective-permute-start(bf16[4,64,512]{2,1,0:T(8,128)(2,1)} %shard_map.87), channel_id=1, source_target_pairs={{0,2},{1,3},{2,0},{3,1},{4,6},{5,7},{6,4},{7,5},{8,10},{9,11},{10,... | collective-permute-start | bytes 786440 | tf_op jit(solution)/shard_map/ppermute | solution.py:36
  56.1 18.6 %collective-permute-start.9 = (bf16[4,64,512]{2,1,0:T(8,128)(2,1)}, bf16[4,64,512]{2,1,0:T(8,128)(2,1)S(1)}, u32[]{:S(2)}, u32[]{:S(2)}) collective-permute-start(bf16[4,64,512]{2,1,0:T(8,128)(2,1)} %shard_map.89), channel_id=1, source_target_pairs={{0,3},{1,2},{2,1},{3,0},{4,7},{5,6},{6,5},{7,4},{8,11},{9,10},{10,... | collective-permute-start | bytes 786440 | tf_op jit(solution)/shard_map/ppermute | solution.py:36
  66.6 8.2 %copy-start.4 = (bf16[4,64,512]{2,1,0:T(8,128)(2,1)}, bf16[4,64,512]{2,1,0:T(8,128)(2,1)S(1)}, u32[]{:S(2)}) copy-start(bf16[4,64,512]{2,1,0:T(8,128)(2,1)S(1)} %collective-permute-done.3.refs_1_.refs_0_) | copy-start | bytes 786436
  66.6 8.2 %copy-start.5 = (bf16[4,64,512]{2,1,0:T(8,128)(2,1)}, bf16[4,64,512]{2,1,0:T(8,128)(2,1)S(1)}, u32[]{:S(2)}) copy-start(bf16[4,64,512]{2,1,0:T(8,128)(2,1)S(1)} %collective-permute-done.6.refs_1_) | copy-start | bytes 786436
  74.7 0.7 copy-start.6
  77.3 29.2 %collective-permute-start.16 = (bf16[3,4,64,512]{3,2,1,0:T(8,128)(2,1)}, bf16[3,4,64,512]{3,2,1,0:T(8,128)(2,1)}, u32[]{:S(2)}, u32[]{:S(2)}) collective-permute-start(bf16[3,4,64,512]{3,2,1,0:T(8,128)(2,1)} %shard_map.94.refs_2_), channel_id=1, source_target_pairs={{4,8},{8,4},{12,16},{16,12},{20,24},{24,20},{5,9},{9,5},{13,17},{1... | collective-permute-start | bytes 2359304 | tf_op jit(solution)/shard_map/ppermute | solution.py:32
  83.6 23.0 %collective-permute-start.15 = (bf16[3,4,64,512]{3,2,1,0:T(8,128)(2,1)}, bf16[3,4,64,512]{3,2,1,0:T(8,128)(2,1)}, u32[]{:S(2)}, u32[]{:S(2)}) collective-permute-start(bf16[3,4,64,512]{3,2,1,0:T(8,128)(2,1)} %shard_map.94.refs_2_), channel_id=1, source_target_pairs={{0,4},{4,0},{8,12},{12,8},{16,20},{20,16},{24,28},{28,24},{1,5},{5... | collective-permute-start | bytes 2359304 | tf_op jit(solution)/shard_map/ppermute | solution.py:32
  83.7 17.2 %collective-permute-start.4 = (bf16[4,64,256]{2,1,0:T(8,128)(2,1)}, bf16[4,64,256]{2,1,0:T(8,128)(2,1)S(1)}, u32[]{:S(2)}, u32[]{:S(2)}) collective-permute-start(bf16[4,64,256]{2,1,0:T(8,128)(2,1)} %shard_map.86), channel_id=1, source_target_pairs={{0,1},{1,0},{2,3},{3,2},{4,5},{5,4},{6,7},{7,6},{8,9},{9,8},{10,11... | collective-permute-start | bytes 393224 | tf_op jit(solution)/shard_map/ppermute | solution.py:36
  87.8 13.1 %collective-permute-start.7 = (bf16[4,64,256]{2,1,0:T(8,128)(2,1)}, bf16[4,64,256]{2,1,0:T(8,128)(2,1)S(1)}, u32[]{:S(2)}, u32[]{:S(2)}) collective-permute-start(bf16[4,64,256]{2,1,0:T(8,128)(2,1)} %shard_map.88), channel_id=1, source_target_pairs={{0,2},{1,3},{2,0},{3,1},{4,6},{5,7},{6,4},{7,5},{8,10},{9,11},{10,... | collective-permute-start | bytes 393224 | tf_op jit(solution)/shard_map/ppermute | solution.py:36
  88.9 12.0 %collective-permute-start.10 = (bf16[4,64,256]{2,1,0:T(8,128)(2,1)}, bf16[4,64,256]{2,1,0:T(8,128)(2,1)S(1)}, u32[]{:S(2)}, u32[]{:S(2)}) collective-permute-start(bf16[4,64,256]{2,1,0:T(8,128)(2,1)} %shard_map.90), channel_id=1, source_target_pairs={{0,3},{1,2},{2,1},{3,0},{4,7},{5,6},{6,5},{7,4},{8,11},{9,10},{10,... | collective-permute-start | bytes 393224 | tf_op jit(solution)/shard_map/ppermute | solution.py:36
  100.9 0.7 copy-start.7
  100.9 0.7 copy-start.8
  101.0 0.7 copy-start.9
  103.4 13.3 %collective-permute-start.14 = (bf16[3,4,64,256]{3,2,1,0:T(8,128)(2,1)}, bf16[3,4,64,256]{3,2,1,0:T(8,128)(2,1)S(1)}, u32[]{:S(2)}, u32[]{:S(2)}) collective-permute-start(bf16[3,4,64,256]{3,2,1,0:T(8,128)(2,1)} %shard_map.93.refs_2_), channel_id=1, source_target_pairs={{4,8},{8,4},{12,16},{16,12},{20,24},{24,20},{5,9},{9,5},{13,17},{1... | collective-permute-start | bytes 1179656 | tf_op jit(solution)/shard_map/ppermute | solution.py:32
  106.5 10.2 %collective-permute-start.13 = (bf16[3,4,64,256]{3,2,1,0:T(8,128)(2,1)}, bf16[3,4,64,256]{3,2,1,0:T(8,128)(2,1)S(1)}, u32[]{:S(2)}, u32[]{:S(2)}) collective-permute-start(bf16[3,4,64,256]{3,2,1,0:T(8,128)(2,1)} %shard_map.93.refs_2_), channel_id=1, source_target_pairs={{0,4},{4,0},{8,12},{12,8},{16,20},{20,16},{24,28},{28,24},{1,5},{5... | collective-permute-start | bytes 1179656 | tf_op jit(solution)/shard_map/ppermute | solution.py:32
  116.7 0.8 copy-start.10
  116.7 0.9 copy-start.11

commit v8 on v7

--- a/solution.py
+++ b/solution.py
@@ -12,9 +12,9 @@
 SCALE = 1.0 / math.sqrt(HD)
 EXP2_SCALE = SCALE * math.log2(math.e)
 MASKED = -1e30
-CHUNK_SHARES = (6, 4, 2)
+CHUNK_SHARES = (5, 4, 2, 1)
 VMEM_LIMIT = 63 * 1024 * 1024
-ATTEND_FLOPS = 1_500_000_000
+ATTEND_FLOPS = 2_500_000_000
 SMALL_COST = pl.CostEstimate(flops=1, bytes_accessed=1, transcendentals=0)
 
 
@@ -32,10 +32,6 @@
     return lax.ppermute(block, axis, route)
 
 
-def swap_flipped(block, axis, flip):
-    return lax.ppermute(block, axis, [(i, i ^ flip) for i in range(lax.axis_size(axis))])
-
-
 def nearby_ids(image_ids, parts, part_rows):
     shard = lax.axis_index("dp")
     padded = jnp.pad(image_ids[::part_rows], (parts, parts), constant_values=-1)
@@ -52,105 +48,167 @@
     return array.at[:, pl.ds(start, width)]
 
 
-def pack_kernel(parts, stride, chunks, *refs):
-    arrays, refs = refs[:4], refs[4:]
-    own, packed, (stage, in_sems, out_sems) = refs[0], refs[1:-3], refs[-3:]
-    me = lax.axis_index("tensor")
-    jobs = [(0, 0, stride, own)]
-    for number, (first, count) in enumerate(chunks):
-        for flip in range(1, parts):
-            target = packed[number * (parts - 1) + flip - 1]
-            jobs.append((flip, first * HD, count * HD, target))
-    jobs = jobs[1:parts] + jobs[:1] + jobs[parts:]
+def pack_kernel(parts, stride, first, width, deps, *refs):
+    arrays, (packed, stage, in_sems, out_sems) = refs[:4], refs[4 + deps :]
     loads, stores = [], []
-    for number, (flip, first, width, _) in enumerate(jobs):
+    for part in range(parts):
         for index, array in enumerate(arrays):
             load = pltpu.make_async_copy(
-                columns(array, me ^ flip, stride, first, width),
-                stage.at[flip, index, :, pl.ds(first, width)],
-                in_sems.at[number * 4 + index],
+                columns(array, part, stride, first, width),
+                stage.at[part, index],
+                in_sems.at[part * 4 + index],
             )
             load.start()
             loads.append(load)
-    for number, (flip, first, width, target) in enumerate(jobs):
-        for load in loads[number * 4 : number * 4 + 4]:
+    for part in range(parts):
+        for load in loads[part * 4 : part * 4 + 4]:
             load.wait()
-        store = pltpu.make_async_copy(
-            stage.at[flip, :, :, pl.ds(first, width)], target, out_sems.at[number]
-        )
+        store = pltpu.make_async_copy(stage.at[part], packed.at[part], out_sems.at[part])
         store.start()
         stores.append(store)
     for store in stores:
         store.wait()
 
 
-def pack(arrays, parts, chunks):
+def pack(arrays, parts, first, count, after):
     rows, total = arrays[0].shape
-    stride = total // parts
-    widths = [stride] + [count * HD for _, count in chunks for _ in range(1, parts)]
-    results = pl.pallas_call(
-        functools.partial(pack_kernel, parts, stride, chunks),
-        out_shape=[jax.ShapeDtypeStruct((4, rows, width), jnp.bfloat16) for width in widths],
-        in_specs=[pl.BlockSpec(memory_space=pl.ANY)] * 4,
-        out_specs=[pl.BlockSpec(memory_space=pl.ANY)] * len(widths),
+    width = count * HD
+    return pl.pallas_call(
+        functools.partial(
+            pack_kernel, parts, total // parts, first * HD, width, len(after)
+        ),
+        out_shape=jax.ShapeDtypeStruct((parts, 4, rows, width), jnp.bfloat16),
+        in_specs=[pl.BlockSpec(memory_space=pl.ANY)] * (4 + len(after)),
+        out_specs=pl.BlockSpec(memory_space=pl.ANY),
         scratch_shapes=[
-            pltpu.VMEM((parts, 4, rows, stride), jnp.bfloat16),
-            pltpu.SemaphoreType.DMA((4 * len(widths),)),
-            pltpu.SemaphoreType.DMA((len(widths),)),
+            pltpu.VMEM((parts, 4, rows, width), jnp.bfloat16),
+            pltpu.SemaphoreType.DMA((parts * 4,)),
+            pltpu.SemaphoreType.DMA((parts,)),
         ],
         compiler_params=pltpu.CompilerParams(vmem_limit_bytes=VMEM_LIMIT),
         cost_estimate=SMALL_COST,
-    )(*arrays)
-    pieces = results[1:]
-    return results[0], [
-        pieces[start : start + parts - 1] for start in range(0, len(pieces), parts - 1)
-    ]
-
-
-def join_kernel(pieces, *refs):
-    received, (joined, stage, in_sems, out_sems) = refs[:pieces], refs[-4:]
+    )(*arrays, *after)
+
+
+def join_kernel(parts, stride, first, width, deps, *refs):
+    arrays, received, refs = refs[:4], refs[4 : 3 + parts], refs[3 + parts + deps :]
+    joined, stage, in_sems, out_sems = refs
+    me = lax.axis_index("tensor")
     loads, stores = [], []
-    for piece in range(pieces):
-        load = pltpu.make_async_copy(received[piece], stage.at[piece], in_sems.at[piece])
+    for flip in range(1, parts):
+        load = pltpu.make_async_copy(received[flip - 1], stage.at[flip], in_sems.at[3 + flip])
         load.start()
-        loads.append(load)
-    for piece in range(pieces):
-        loads[piece].wait()
-        store = pltpu.make_async_copy(stage.at[piece], joined.at[piece], out_sems.at[piece])
+        loads.append([load])
+    own = []
+    for index, array in enumerate(arrays):
+        load = pltpu.make_async_copy(
+            columns(array, me, stride, first, width), stage.at[0, index], in_sems.at[index]
+        )
+        load.start()
+        own.append(load)
+    loads = [own] + loads
+    for flip in range(parts):
+        for load in loads[flip]:
+            load.wait()
+        store = pltpu.make_async_copy(stage.at[flip], joined.at[me ^ flip], out_sems.at[flip])
         store.start()
         stores.append(store)
     for store in stores:
         store.wait()
 
 
-def join(received, after):
-    pieces = len(received)
-    shape = (pieces,) + received[0].shape
+def join(arrays, received, first, after):
+    parts = len(received) + 1
+    rows, total = arrays[0].shape
+    width = received[0].shape[2]
     return pl.pallas_call(
-        functools.partial(join_kernel, pieces),
+        functools.partial(
+            join_kernel, parts, total // parts, first * HD, width, len(after)
+        ),
+        out_shape=jax.ShapeDtypeStruct((parts, 4, rows, width), jnp.bfloat16),
+        in_specs=[pl.BlockSpec(memory_space=pl.ANY)] * (3 + parts + len(after)),
+        out_specs=pl.BlockSpec(memory_space=pl.ANY),
+        scratch_shapes=[
+            pltpu.VMEM((parts, 4, rows, width), jnp.bfloat16),
+            pltpu.SemaphoreType.DMA((parts + 3,)),
+            pltpu.SemaphoreType.DMA((parts,)),
+        ],
+        compiler_params=pltpu.CompilerParams(vmem_limit_bytes=VMEM_LIMIT),
+        cost_estimate=SMALL_COST,
+    )(*arrays, *received, *after)
+
+
+def own_kernel(stride, deps, *refs):
+    arrays, (packed, stage, in_sems, out_sems) = refs[:4], refs[4 + deps :]
+    me = lax.axis_index("tensor")
+    loads, stores = [], []
+    for index, array in enumerate(arrays):
+        load = pltpu.make_async_copy(
+            columns(array, me, stride, 0, stride), stage.at[index], in_sems.at[index]
+        )
+        load.start()
+        loads.append(load)
+    for index in range(4):
+        loads[index].wait()
+        store = pltpu.make_async_copy(stage.at[index], packed.at[index], out_sems.at[index])
+        store.start()
+        stores.append(store)
+    for store in stores:
+        store.wait()
+
+
+def own_columns(arrays, parts, after):
+    rows, total = arrays[0].shape
+    shape = (4, rows, total // parts)
+    return pl.pallas_call(
+        functools.partial(own_kernel, total // parts, len(after)),
         out_shape=jax.ShapeDtypeStruct(shape, jnp.bfloat16),
-        in_specs=[pl.BlockSpec(memory_space=pl.ANY)] * (pieces + len(after)),
+        in_specs=[pl.BlockSpec(memory_space=pl.ANY)] * (4 + len(after)),
         out_specs=pl.BlockSpec(memory_space=pl.ANY),
         scratch_shapes=[
             pltpu.VMEM(shape, jnp.bfloat16),
-            pltpu.SemaphoreType.DMA((pieces,)),
-            pltpu.SemaphoreType.DMA((pieces,)),
+            pltpu.SemaphoreType.DMA((4,)),
+            pltpu.SemaphoreType.DMA((4,)),
         ],
         compiler_params=pltpu.CompilerParams(vmem_limit_bytes=VMEM_LIMIT),
         cost_estimate=SMALL_COST,
-    )(*received, *after)
-
-
-def hold(array, after):
+    )(*arrays, *after)
+
+
+def others_kernel(others, *refs):
+    crossed, (rest, stage, in_sems, out_sems) = refs[0], refs[-4:]
+    me = lax.axis_index("tensor")
+    loads, stores = [], []
+    for other in range(others):
+        load = pltpu.make_async_copy(
+            crossed.at[me ^ (other + 1)], stage.at[other], in_sems.at[other]
+        )
+        load.start()
+        loads.append(load)
+    for other in range(others):
+        loads[other].wait()
+        store = pltpu.make_async_copy(stage.at[other], rest.at[other], out_sems.at[other])
+        store.start()
+        stores.append(store)
+    for store in stores:
+        store.wait()
+
+
+def take_others(crossed, after):
+    shape = (crossed.shape[0] - 1,) + crossed.shape[1:]
     return pl.pallas_call(
-        lambda *refs: None,
-        out_shape=jax.ShapeDtypeStruct(array.shape, array.dtype),
+        functools.partial(others_kernel, shape[0]),
+        out_shape=jax.ShapeDtypeStruct(shape, jnp.bfloat16),
         in_specs=[pl.BlockSpec(memory_space=pl.ANY)] * (1 + len(after)),
         out_specs=pl.BlockSpec(memory_space=pl.ANY),
-        input_output_aliases={0: 0},
+        scratch_shapes=[
+            pltpu.VMEM(shape, jnp.bfloat16),
+            pltpu.SemaphoreType.DMA((shape[0],)),
+            pltpu.SemaphoreType.DMA((shape[0],)),
+        ],
         compiler_params=pltpu.CompilerParams(vmem_limit_bytes=VMEM_LIMIT),
         cost_estimate=SMALL_COST,
-    )(array, *after)
+    )(crossed, *after)
 
 
 def dot_nt(a, b):
@@ -212,11 +270,11 @@
             count = count + shared.astype(jnp.int32)
         table[2 * parts] = count
 
-        def ids_along(axis):
-            shape = (most, 1) if axis == 0 else (1, most)
+        def ids_along(axis, size):
+            shape = (size, 1) if axis == 0 else (1, size)
             place = lax.broadcasted_iota(jnp.int32, shape, axis)
             ids = jnp.full(shape, -2, jnp.int32)
-            for slot in range(3 * parts):
+            for slot in range(size // part_rows):
                 if slot < parts:
                     slot_id = id_of(0, slot)
                 else:
@@ -228,7 +286,13 @@
                 ids = jnp.where(inside, slot_id, ids)
             return ids
 
-        bias[...] = jnp.where(ids_along(0) == ids_along(1), 0.0, MASKED)
+        for size in range(rows, most + 1, rows):
+            slots = (size - rows) // part_rows
+
+            @pl.when((count <= slots) & (count > slots - parts))
+            def _():
+                same = ids_along(0, size) == ids_along(1, size)
+                bias[:size, :size] = jnp.where(same, 0.0, MASKED)
 
     count = table[2 * parts]
 
@@ -308,27 +372,20 @@
     near_ids = nearby_ids(image_ids, parts, part_rows)
     chunks = split_counts(head_total, CHUNK_SHARES)
 
-    def cross(packed):
-        return [
-            swap_flipped(piece, "tensor", flip) for flip, piece in enumerate(packed, start=1)
-        ]
-
-    first, packed = pack(arrays, parts, chunks)
-    received = [cross(packed[0])]
+    packed = [pack(arrays, parts, *chunk, []) for chunk in chunks[:2]]
+    first = own_columns(arrays, parts, [packed[0]])
     near_first = swap_pairs(first, "dp", 0)
     far_first = swap_pairs(first, "dp", 1)
-    firsts = [near_first, far_first]
     outs, out_history = None, []
     for number, (first_head, _) in enumerate(chunks):
-        if number + 1 < len(chunks):
-            held = [
-                hold(piece, [done] + (firsts if number == 0 else []))
-                for piece, done in zip(packed[number + 1], received[number])
-            ]
-            received.append(cross(held))
-        after = [out_history[number - 2][0]] if number >= 2 else []
-        after += firsts if number == 0 else []
-        rest = join(received[number], after)
+        crossed = lax.all_to_all(packed[number], "tensor", split_axis=0, concat_axis=0, tiled=True)
+        after = packed[number + 1 : number + 2]
+        after += [near_first, far_first] if number == 0 else []
+        if number >= 2:
+            after.append(out_history[number - 2][0])
+        rest = take_others(crossed, after)
+        if number + 2 < len(chunks):
+            packed.append(pack(arrays, parts, *chunks[number + 2], [rest]))
         near_rest = swap_pairs(rest, "dp", 0)
         far_rest = swap_pairs(rest, "dp", 1)
         groups = ((first, rest), (near_first, near_rest), (far_first, far_rest))

time: 123 us -> 125 us (1.016)
  the two profiles are of different devices: /device:TPU:1 before, /device:TPU:3 now
where the time goes in v8:
time: 125 us; the launch traced here: 123 us
  Pallas kernels  42.8 us (34%)
  waiting for transfers between devices  38.4 us (31%)
  starting transfers between devices  37.7 us (30%)
  local copies, waits for them, and re-layouts  2.46 us (2%)
    all_to_all x4, waiting for transfers between devices, shards(): lax.all_to_all(packed[number], 'tensor', split_axis=0, concat_axis=0, til...  37.2 us
    pallas_call x4, Pallas kernels, attend(): pl.pallas_call(functools.partial(attend_kernel, parts, has_outs), grid=(h...  25.6 us
    ppermute x10, starting transfers between devices, swap_pairs(): return lax.ppermute(block, axis, route)  19.9 us
    all_to_all x4, starting transfers between devices, shards(): lax.all_to_all(packed[number], 'tensor', split_axis=0, concat_axis=0, til...  17.8 us
    pallas_call x4, Pallas kernels, pack(): pl.pallas_call(functools.partial(pack_kernel, parts, total // parts, firs...  8.1 us
    pallas_call x4, Pallas kernels, take_others(): pl.pallas_call(functools.partial(others_kernel, shape[0]), out_shape=jax....  7.2 us
  transfers between devices with their start and end apart: 14, of which 3 were waited for; matrix products, arithmetic and copies ran while one was open for 1% of the time, Pallas kernels for 30%

profile of v8, /device:TPU:3, one launch (start us, length us, event | category | flops | bytes accessed | tf_op | source)
XLA Modules:
  0.0 122.9 jit_solution(17072866156950746318)
XLA Ops:
  0.6 2.3 %shard_map.84.refs_4_ = bf16[4,4,64,640]{3,2,1,0:T(8,128)(2,1)} custom-call(bf16[64,6144]{1,0:T(8,128)(2,1)} %refs_0_.9, bf16[64,6144]{1,0:T(8,128)(2,1)} %refs_1_.9, bf16[64,6144]{1,0:T(8,128)(2,1)} %refs_2_.9, bf16[64,6144]{1,0:T(8,128)(2,1)} %refs_3_.9), custom_call_target="tpu_custom_call" | custom-call | flops 1 | bytes 1 | tf_op jit(solution)/shard_map/pallas_call | solution.py:76
  3.0 4.6 %all-to-all-start.1 = ((bf16[4,4,64,640]{3,2,1,0:T(8,128)(2,1)}), bf16[4,4,64,640]{3,2,1,0:T(8,128)(2,1)}, u32[]{:S(2)}, u32[]{:S(2)}) async-start(bf16[4,4,64,640]{3,2,1,0:T(8,128)(2,1)} %shard_map.84.refs_4_), calls=%async_computation.1 | async-start | bytes 2621440 | tf_op jit(solution)/shard_map/all_to_all | solution.py:381
  7.6 2.0 %shard_map.85.refs_1_ = bf16[4,64,1536]{2,1,0:T(8,128)(2,1)} custom-call(bf16[64,6144]{1,0:T(8,128)(2,1)} %refs_0_.9, bf16[64,6144]{1,0:T(8,128)(2,1)} %refs_1_.9, bf16[64,6144]{1,0:T(8,128)(2,1)} %refs_2_.9, bf16[64,6144]{1,0:T(8,128)(2,1)} %refs_3_.9, bf16[4,4,64,640]{3,2,1,0:T(8,128)(2,1)} %shard_map.84.refs_4_), custom_call_target="tpu_custom_call" | custom-call | flops 1 | bytes 1 | tf_op jit(solution)/shard_map/pallas_call | solution.py:163
  9.5 1.0 collective-permute-start
  10.6 3.0 %collective-permute-start.1 = (bf16[4,64,1536]{2,1,0:T(8,128)(2,1)}, bf16[4,64,1536]{2,1,0:T(8,128)(2,1)}, u32[]{:S(2)}, u32[]{:S(2)}) collective-permute-start(bf16[4,64,1536]{2,1,0:T(8,128)(2,1)} %shard_map.85.refs_1_), channel_id=1, source_target_pairs={{4,8},{8,4},{12,16},{16,12},{20,24},{24,20},{5,9},{9,5},{13,17},{1... | collective-permute-start | bytes 2359304 | tf_op jit(solution)/shard_map/ppermute | solution.py:32
  13.6 2.1 %shard_map.86.refs_1_ = bf16[4,4,64,512]{3,2,1,0:T(8,128)(2,1)} custom-call(bf16[64,6144]{1,0:T(8,128)(2,1)} %refs_0_.9, bf16[64,6144]{1,0:T(8,128)(2,1)} %refs_1_.9, bf16[64,6144]{1,0:T(8,128)(2,1)} %refs_2_.9, bf16[64,6144]{1,0:T(8,128)(2,1)} %refs_3_.9), custom_call_target="tpu_custom_call" | custom-call | flops 1 | bytes 1 | tf_op jit(solution)/shard_map/pallas_call | solution.py:76
  15.7 22.8 %all-to-all-done.1.refs_0_ = bf16[4,4,64,640]{3,2,1,0:T(8,128)(2,1)} async-done(((bf16[4,4,64,640]{3,2,1,0:T(8,128)(2,1)}), bf16[4,4,64,640]{3,2,1,0:T(8,128)(2,1)}, u32[]{:S(2)}, u32[]{:S(2)}) %all-to-all-start.1) | async-done | bytes 1310752 | tf_op jit(solution)/shard_map/all_to_all | solution.py:381
  38.5 4.2 %all-to-all-start = ((bf16[4,4,64,512]{3,2,1,0:T(8,128)(2,1)}), bf16[4,4,64,512]{3,2,1,0:T(8,128)(2,1)}, u32[]{:S(2)}, u32[]{:S(2)}) async-start(bf16[4,4,64,512]{3,2,1,0:T(8,128)(2,1)} %shard_map.86.refs_1_), calls=%async_computation | async-start | bytes 2097152 | tf_op jit(solution)/shard_map/all_to_all | solution.py:381
  42.8 0.9 copy-done.1
  43.7 2.0 %shard_map.87.refs_4_.refs_2_ = bf16[3,4,64,640]{3,2,1,0:T(8,128)(2,1)} custom-call(bf16[4,4,64,640]{3,2,1,0:T(8,128)(2,1)} %all-to-all-done.1.refs_0_, bf16[4,4,64,512]{3,2,1,0:T(8,128)(2,1)} %shard_map.86.refs_1_, bf16[4,64,1536]{2,1,0:T(8,128)(2,1)} %copy-done.1, bf16[4,64,1536]{2,1,0:T(8,128)(2,1)} %collective-permute-done.1.refs_3_.refs_5_), custom_call_target="tpu_custom_call" | custom-call | flops 1 | bytes 1 | tf_op jit(solution)/shard_map/pallas_call | solution.py:199
  45.7 1.5 %collective-permute-start.4 = (bf16[3,4,64,640]{3,2,1,0:T(8,128)(2,1)}, bf16[3,4,64,640]{3,2,1,0:T(8,128)(2,1)}, u32[]{:S(2)}, u32[]{:S(2)}) collective-permute-start(bf16[3,4,64,640]{3,2,1,0:T(8,128)(2,1)} %shard_map.87.refs_4_.refs_2_), channel_id=1, source_target_pairs={{0,4},{4,0},{8,12},{12,8},{16,20},{20,16},{24,28},{28,24},{1,5},{5... | collective-permute-start | bytes 2949128 | tf_op jit(solution)/shard_map/ppermute | solution.py:32
  47.2 3.0 %collective-permute-start.5 = (bf16[3,4,64,640]{3,2,1,0:T(8,128)(2,1)}, bf16[3,4,64,640]{3,2,1,0:T(8,128)(2,1)}, u32[]{:S(2)}, u32[]{:S(2)}) collective-permute-start(bf16[3,4,64,640]{3,2,1,0:T(8,128)(2,1)} %shard_map.87.refs_4_.refs_2_), channel_id=1, source_target_pairs={{4,8},{8,4},{12,16},{16,12},{20,24},{24,20},{5,9},{9,5},{13,17},{1... | collective-permute-start | bytes 2949128 | tf_op jit(solution)/shard_map/ppermute | solution.py:32
  50.2 0.8 slice.3
  51.1 0.6 pad_add_fusion.refs_0_
  51.7 1.9 %shard_map.88.refs_1_ = bf16[4,4,64,256]{3,2,1,0:T(8,128)(2,1)} custom-call(bf16[64,6144]{1,0:T(8,128)(2,1)} %refs_0_.9, bf16[64,6144]{1,0:T(8,128)(2,1)} %refs_1_.9, bf16[64,6144]{1,0:T(8,128)(2,1)} %refs_2_.9, bf16[64,6144]{1,0:T(8,128)(2,1)} %refs_3_.9, bf16[3,4,64,640]{3,2,1,0:T(8,128)(2,1)} %shard_map.87.refs_4_.refs_2_), custom_call_target="tpu_custom_call" | custom-call | flops 1 | bytes 1 | tf_op jit(solution)/shard_map/pallas_call | solution.py:76
  53.6 14.4 %all-to-all-done.refs_0_ = bf16[4,4,64,512]{3,2,1,0:T(8,128)(2,1)} async-done(((bf16[4,4,64,512]{3,2,1,0:T(8,128)(2,1)}), bf16[4,4,64,512]{3,2,1,0:T(8,128)(2,1)}, u32[]{:S(2)}, u32[]{:S(2)}) %all-to-all-start) | async-done | bytes 1048608 | tf_op jit(solution)/shard_map/all_to_all | solution.py:381
  68.1 1.9 %shard_map.89.refs_4_.refs_2_ = bf16[3,4,64,512]{3,2,1,0:T(8,128)(2,1)} custom-call(bf16[4,4,64,512]{3,2,1,0:T(8,128)(2,1)} %all-to-all-done.refs_0_, bf16[4,4,64,256]{3,2,1,0:T(8,128)(2,1)} %shard_map.88.refs_1_), custom_call_target="tpu_custom_call" | custom-call | flops 1 | bytes 1 | tf_op jit(solution)/shard_map/pallas_call | solution.py:199
  70.0 4.2 %all-to-all-start.3 = ((bf16[4,4,64,256]{3,2,1,0:T(8,128)(2,1)}), bf16[4,4,64,256]{3,2,1,0:T(8,128)(2,1)}, u32[]{:S(2)}, u32[]{:S(2)}) async-start(bf16[4,4,64,256]{3,2,1,0:T(8,128)(2,1)} %shard_map.88.refs_1_), calls=%async_computation.3 | async-start | bytes 1048576 | tf_op jit(solution)/shard_map/all_to_all | solution.py:381
  74.1 1.8 %shard_map.90.refs_1_ = bf16[4,4,64,128]{3,2,1,0:T(8,128)(2,1)} custom-call(bf16[64,6144]{1,0:T(8,128)(2,1)} %refs_0_.9, bf16[64,6144]{1,0:T(8,128)(2,1)} %refs_1_.9, bf16[64,6144]{1,0:T(8,128)(2,1)} %refs_2_.9, bf16[64,6144]{1,0:T(8,128)(2,1)} %refs_3_.9, bf16[3,4,64,512]{3,2,1,0:T(8,128)(2,1)} %shard_map.89.refs_4_.refs_2_), custom_call_target="tpu_custom_call" | custom-call | flops 1 | bytes 1 | tf_op jit(solution)/shard_map/pallas_call | solution.py:76
  75.9 1.5 %collective-permute-start.2 = (bf16[3,4,64,512]{3,2,1,0:T(8,128)(2,1)S(1)}, bf16[3,4,64,512]{3,2,1,0:T(8,128)(2,1)}, u32[]{:S(2)}, u32[]{:S(2)}) collective-permute-start(bf16[3,4,64,512]{3,2,1,0:T(8,128)(2,1)S(1)} %copy-done), channel_id=1, source_target_pairs={{0,4},{4,0},{8,12},{12,8},{16,20},{20,16},{24,28},{28,24},{1,5},{5... | collective-permute-start | bytes 2359304 | tf_op jit(solution)/shard_map/ppermute | solution.py:32
  77.5 3.0 %collective-permute-start.3 = (bf16[3,4,64,512]{3,2,1,0:T(8,128)(2,1)S(1)}, bf16[3,4,64,512]{3,2,1,0:T(8,128)(2,1)}, u32[]{:S(2)}, u32[]{:S(2)}) collective-permute-start(bf16[3,4,64,512]{3,2,1,0:T(8,128)(2,1)S(1)} %copy-done), channel_id=1, source_target_pairs={{4,8},{8,4},{12,16},{16,12},{20,24},{24,20},{5,9},{9,5},{13,17},{1... | collective-permute-start | bytes 2359304 | tf_op jit(solution)/shard_map/ppermute | solution.py:32
  80.5 9.3 %shard_map.91 = (bf16[256,1536]{1,0:T(8,128)(2,1)}, bf16[256,1536]{1,0:T(8,128)(2,1)}, bf16[256,1536]{1,0:T(8,128)(2,1)}, bf16[256,1536]{1,0:T(8,128)(2,1)}) custom-call(s32[3,4]{1,0:T(4,128)} %pad_add_fusion.refs_0_, bf16[4,64,1536]{2,1,0:T(8,128)(2,1)} %shard_map.85.refs_1_, bf16[3,4,64,640]{3,2,1,0:T(8,128)(2,1)} %shard_map.87.refs_4_.refs_2_, ...), custom_call_target="tpu_custom_call" | custom-call | flops 12499999744 | bytes 1 | tf_op jit(solution)/shard_map/pallas_call | solution.py:344
  89.8 4.8 %all-to-all-start.2 = ((bf16[4,4,64,128]{3,2,1,0:T(8,128)(2,1)}), bf16[4,4,64,128]{3,2,1,0:T(8,128)(2,1)}, u32[]{:S(2)}, u32[]{:S(2)}) async-start(bf16[4,4,64,128]{3,2,1,0:T(8,128)(2,1)} %shard_map.90.refs_1_), calls=%async_computation.2 | async-start | bytes 524288 | tf_op jit(solution)/shard_map/all_to_all | solution.py:381
  94.6 1.7 %shard_map.94.refs_2_ = bf16[3,4,64,256]{3,2,1,0:T(8,128)(2,1)} custom-call(bf16[4,4,64,256]{3,2,1,0:T(8,128)(2,1)} %all-to-all-done.3.refs_0_, bf16[4,4,64,128]{3,2,1,0:T(8,128)(2,1)} %shard_map.90.refs_1_, bf16[256,1536]{1,0:T(8,128)(2,1)} %get-tuple-element.16.refs_7_.refs_2_), custom_call_target="tpu_custom_call" | custom-call | flops 1 | bytes 1 | tf_op jit(solution)/shard_map/pallas_call | solution.py:199
  96.4 3.7 %collective-permute-start.9 = (bf16[3,4,64,256]{3,2,1,0:T(8,128)(2,1)}, bf16[3,4,64,256]{3,2,1,0:T(8,128)(2,1)}, u32[]{:S(2)}, u32[]{:S(2)}) collective-permute-start(bf16[3,4,64,256]{3,2,1,0:T(8,128)(2,1)} %shard_map.94.refs_2_), channel_id=1, source_target_pairs={{4,8},{8,4},{12,16},{16,12},{20,24},{24,20},{5,9},{9,5},{13,17},{1... | collective-permute-start | bytes 1179656 | tf_op jit(solution)/shard_map/ppermute | solution.py:32
  100.1 7.9 %shard_map.92 = (bf16[256,1536]{1,0:T(8,128)(2,1)}, bf16[256,1536]{1,0:T(8,128)(2,1)}, bf16[256,1536]{1,0:T(8,128)(2,1)}, bf16[256,1536]{1,0:T(8,128)(2,1)}) custom-call(s32[3,4]{1,0:T(4,128)} %pad_add_fusion.refs_0_, bf16[4,64,1536]{2,1,0:T(8,128)(2,1)} %shard_map.85.refs_1_, ...), custom_call_target="tpu_custom_call", output_to_operand_aliasing={{0}: (7, {}), {1}: (8, {}), {2}: (9, {}), {3}: (10, {})} | custom-call | flops 10000000000 | bytes 1 | tf_op jit(solution)/shard_map/pallas_call | solution.py:344
  108.0 1.6 %shard_map.93.refs_2_ = bf16[3,4,64,128]{3,2,1,0:T(8,128)(2,1)} custom-call(bf16[4,4,64,128]{3,2,1,0:T(8,128)(2,1)} %all-to-all-done.2.refs_0_, bf16[256,1536]{1,0:T(8,128)(2,1)} %get-tuple-element.20.refs_1_.refs_7_), custom_call_target="tpu_custom_call" | custom-call | flops 1 | bytes 1 | tf_op jit(solution)/shard_map/pallas_call | solution.py:199
  109.7 3.0 %collective-permute-start.7 = (bf16[3,4,64,128]{3,2,1,0:T(8,128)(2,1)}, bf16[3,4,64,128]{3,2,1,0:T(8,128)(2,1)S(1)}, u32[]{:S(2)}, u32[]{:S(2)}) collective-permute-start(bf16[3,4,64,128]{3,2,1,0:T(8,128)(2,1)} %shard_map.93.refs_2_), channel_id=1, source_target_pairs={{4,8},{8,4},{12,16},{16,12},{20,24},{24,20},{5,9},{9,5},{13,17},{1... | collective-permute-start | bytes 589832 | tf_op jit(solution)/shard_map/ppermute | solution.py:32
  112.7 4.9 %shard_map.95 = (bf16[256,1536]{1,0:T(8,128)(2,1)}, bf16[256,1536]{1,0:T(8,128)(2,1)}, bf16[256,1536]{1,0:T(8,128)(2,1)}, bf16[256,1536]{1,0:T(8,128)(2,1)}) custom-call(s32[3,4]{1,0:T(4,128)} %pad_add_fusion.refs_0_, bf16[4,64,1536]{2,1,0:T(8,128)(2,1)} %shard_map.85.refs_1_, ...), custom_call_target="tpu_custom_call", output_to_operand_aliasing={{0}: (7, {}), {1}: (8, {}), {2}: (9, {}), {3}: (10, {})} | custom-call | flops 5000000000 | bytes 1 | tf_op jit(solution)/shard_map/pallas_call | solution.py:344
  117.6 1.2 collective-permute-done.7.refs_6_
  118.8 0.7 copy-done.3
  119.5 3.4 %shard_map.96 = (bf16[256,1536]{1,0:T(8,128)(2,1)}, bf16[256,1536]{1,0:T(8,128)(2,1)}, bf16[256,1536]{1,0:T(8,128)(2,1)}, bf16[256,1536]{1,0:T(8,128)(2,1)}) custom-call(s32[3,4]{1,0:T(4,128)} %pad_add_fusion.refs_0_, bf16[4,64,1536]{2,1,0:T(8,128)(2,1)} %shard_map.85.refs_1_, ...), custom_call_target="tpu_custom_call", output_to_operand_aliasing={{0}: (7, {}), {1}: (8, {}), {2}: (9, {}), {3}: (10, {})} | custom-call | flops 2500000000 | bytes 1 | tf_op jit(solution)/shard_map/pallas_call | solution.py:344
  (20 shorter events, 0.3 us)
Async XLA Ops:
  3.0 35.6 %all-to-all-start.1 = ((bf16[4,4,64,640]{3,2,1,0:T(8,128)(2,1)}), bf16[4,4,64,640]{3,2,1,0:T(8,128)(2,1)}, u32[]{:S(2)}, u32[]{:S(2)}) async-start(bf16[4,4,64,640]{3,2,1,0:T(8,128)(2,1)} %shard_map.84.refs_4_), calls=%async_computation.1 | async-start | bytes 2621440 | tf_op jit(solution)/shard_map/all_to_all | solution.py:381
  9.5 33.2 %collective-permute-start = (bf16[4,64,1536]{2,1,0:T(8,128)(2,1)}, bf16[4,64,1536]{2,1,0:T(8,128)(2,1)S(1)}, u32[]{:S(2)}, u32[]{:S(2)}) collective-permute-start(bf16[4,64,1536]{2,1,0:T(8,128)(2,1)} %shard_map.85.refs_1_), channel_id=1, source_target_pairs={{0,4},{4,0},{8,12},{12,8},{16,20},{20,16},{24,28},{28,24},{1,5},{5... | collective-permute-start | bytes 2359304 | tf_op jit(solution)/shard_map/ppermute | solution.py:32
  10.6 32.2 %collective-permute-start.1 = (bf16[4,64,1536]{2,1,0:T(8,128)(2,1)}, bf16[4,64,1536]{2,1,0:T(8,128)(2,1)}, u32[]{:S(2)}, u32[]{:S(2)}) collective-permute-start(bf16[4,64,1536]{2,1,0:T(8,128)(2,1)} %shard_map.85.refs_1_), channel_id=1, source_target_pairs={{4,8},{8,4},{12,16},{16,12},{20,24},{24,20},{5,9},{9,5},{13,17},{1... | collective-permute-start | bytes 2359304 | tf_op jit(solution)/shard_map/ppermute | solution.py:32
  38.5 29.5 %all-to-all-start = ((bf16[4,4,64,512]{3,2,1,0:T(8,128)(2,1)}), bf16[4,4,64,512]{3,2,1,0:T(8,128)(2,1)}, u32[]{:S(2)}, u32[]{:S(2)}) async-start(bf16[4,4,64,512]{3,2,1,0:T(8,128)(2,1)} %shard_map.86.refs_1_), calls=%async_computation | async-start | bytes 2097152 | tf_op jit(solution)/shard_map/all_to_all | solution.py:381
  42.8 0.9 copy-start.1
  45.7 34.8 %collective-permute-start.4 = (bf16[3,4,64,640]{3,2,1,0:T(8,128)(2,1)}, bf16[3,4,64,640]{3,2,1,0:T(8,128)(2,1)}, u32[]{:S(2)}, u32[]{:S(2)}) collective-permute-start(bf16[3,4,64,640]{3,2,1,0:T(8,128)(2,1)} %shard_map.87.refs_4_.refs_2_), channel_id=1, source_target_pairs={{0,4},{4,0},{8,12},{12,8},{16,20},{20,16},{24,28},{28,24},{1,5},{5... | collective-permute-start | bytes 2949128 | tf_op jit(solution)/shard_map/ppermute | solution.py:32
  47.2 33.3 %collective-permute-start.5 = (bf16[3,4,64,640]{3,2,1,0:T(8,128)(2,1)}, bf16[3,4,64,640]{3,2,1,0:T(8,128)(2,1)}, u32[]{:S(2)}, u32[]{:S(2)}) collective-permute-start(bf16[3,4,64,640]{3,2,1,0:T(8,128)(2,1)} %shard_map.87.refs_4_.refs_2_), channel_id=1, source_target_pairs={{4,8},{8,4},{12,16},{16,12},{20,24},{24,20},{5,9},{9,5},{13,17},{1... | collective-permute-start | bytes 2949128 | tf_op jit(solution)/shard_map/ppermute | solution.py:32
  70.0 19.8 %all-to-all-start.3 = ((bf16[4,4,64,256]{3,2,1,0:T(8,128)(2,1)}), bf16[4,4,64,256]{3,2,1,0:T(8,128)(2,1)}, u32[]{:S(2)}, u32[]{:S(2)}) async-start(bf16[4,4,64,256]{3,2,1,0:T(8,128)(2,1)} %shard_map.88.refs_1_), calls=%async_computation.3 | async-start | bytes 1048576 | tf_op jit(solution)/shard_map/all_to_all | solution.py:381
  74.1 1.8 %copy-start = (bf16[3,4,64,512]{3,2,1,0:T(8,128)(2,1)S(1)}, bf16[3,4,64,512]{3,2,1,0:T(8,128)(2,1)}, u32[]{:S(2)}) copy-start(bf16[3,4,64,512]{3,2,1,0:T(8,128)(2,1)} %shard_map.89.refs_4_.refs_2_) | copy-start | bytes 2359300
  75.9 24.2 %collective-permute-start.2 = (bf16[3,4,64,512]{3,2,1,0:T(8,128)(2,1)S(1)}, bf16[3,4,64,512]{3,2,1,0:T(8,128)(2,1)}, u32[]{:S(2)}, u32[]{:S(2)}) collective-permute-start(bf16[3,4,64,512]{3,2,1,0:T(8,128)(2,1)S(1)} %copy-done), channel_id=1, source_target_pairs={{0,4},{4,0},{8,12},{12,8},{16,20},{20,16},{24,28},{28,24},{1,5},{5... | collective-permute-start | bytes 2359304 | tf_op jit(solution)/shard_map/ppermute | solution.py:32
  77.5 22.7 %collective-permute-start.3 = (bf16[3,4,64,512]{3,2,1,0:T(8,128)(2,1)S(1)}, bf16[3,4,64,512]{3,2,1,0:T(8,128)(2,1)}, u32[]{:S(2)}, u32[]{:S(2)}) collective-permute-start(bf16[3,4,64,512]{3,2,1,0:T(8,128)(2,1)S(1)} %copy-done), channel_id=1, source_target_pairs={{4,8},{8,4},{12,16},{16,12},{20,24},{24,20},{5,9},{9,5},{13,17},{1... | collective-permute-start | bytes 2359304 | tf_op jit(solution)/shard_map/ppermute | solution.py:32
  89.8 18.2 %all-to-all-start.2 = ((bf16[4,4,64,128]{3,2,1,0:T(8,128)(2,1)}), bf16[4,4,64,128]{3,2,1,0:T(8,128)(2,1)}, u32[]{:S(2)}, u32[]{:S(2)}) async-start(bf16[4,4,64,128]{3,2,1,0:T(8,128)(2,1)} %shard_map.90.refs_1_), calls=%async_computation.2 | async-start | bytes 524288 | tf_op jit(solution)/shard_map/all_to_all | solution.py:381
  96.3 16.3 %collective-permute-start.8 = (bf16[3,4,64,256]{3,2,1,0:T(8,128)(2,1)}, bf16[3,4,64,256]{3,2,1,0:T(8,128)(2,1)}, u32[]{:S(2)}, u32[]{:S(2)}) collective-permute-start(bf16[3,4,64,256]{3,2,1,0:T(8,128)(2,1)} %shard_map.94.refs_2_), channel_id=1, source_target_pairs={{0,4},{4,0},{8,12},{12,8},{16,20},{20,16},{24,28},{28,24},{1,5},{5... | collective-permute-start | bytes 1179656 | tf_op jit(solution)/shard_map/ppermute | solution.py:32
  96.4 16.3 %collective-permute-start.9 = (bf16[3,4,64,256]{3,2,1,0:T(8,128)(2,1)}, bf16[3,4,64,256]{3,2,1,0:T(8,128)(2,1)}, u32[]{:S(2)}, u32[]{:S(2)}) collective-permute-start(bf16[3,4,64,256]{3,2,1,0:T(8,128)(2,1)} %shard_map.94.refs_2_), channel_id=1, source_target_pairs={{4,8},{8,4},{12,16},{16,12},{20,24},{24,20},{5,9},{9,5},{13,17},{1... | collective-permute-start | bytes 1179656 | tf_op jit(solution)/shard_map/ppermute | solution.py:32
  109.6 8.0 %collective-permute-start.6 = (bf16[3,4,64,128]{3,2,1,0:T(8,128)(2,1)}, bf16[3,4,64,128]{3,2,1,0:T(8,128)(2,1)S(1)}, u32[]{:S(2)}, u32[]{:S(2)}) collective-permute-start(bf16[3,4,64,128]{3,2,1,0:T(8,128)(2,1)} %shard_map.93.refs_2_), channel_id=1, source_target_pairs={{0,4},{4,0},{8,12},{12,8},{16,20},{20,16},{24,28},{28,24},{1,5},{5... | collective-permute-start | bytes 589832 | tf_op jit(solution)/shard_map/ppermute | solution.py:32
  109.7 9.1 %collective-permute-start.7 = (bf16[3,4,64,128]{3,2,1,0:T(8,128)(2,1)}, bf16[3,4,64,128]{3,2,1,0:T(8,128)(2,1)S(1)}, u32[]{:S(2)}, u32[]{:S(2)}) collective-permute-start(bf16[3,4,64,128]{3,2,1,0:T(8,128)(2,1)} %shard_map.93.refs_2_), channel_id=1, source_target_pairs={{4,8},{8,4},{12,16},{16,12},{20,24},{24,20},{5,9},{9,5},{13,17},{1... | collective-permute-start | bytes 589832 | tf_op jit(solution)/shard_map/ppermute | solution.py:32
  117.6 1.2 copy-start.2
  118.8 0.7 copy-start.3

commit v9 on v7

v9 whole, which is shorter than its diff:
```python
import functools
import math

import jax
import jax.numpy as jnp
from jax import lax
from jax.experimental import pallas as pl
from jax.experimental.pallas import tpu as pltpu
from jax.sharding import PartitionSpec as P

HD = 128
SCALE = 1.0 / math.sqrt(HD)
EXP2_SCALE = SCALE * math.log2(math.e)
MASKED = -1e30
CHUNK_SHARES = (6, 4, 2)
VMEM_LIMIT = 63 * 1024 * 1024
ATTEND_FLOPS = 1_500_000_000
SMALL_COST = pl.CostEstimate(flops=1, bytes_accessed=1, transcendentals=0)


def split_counts(total, shares):
    whole = sum(shares)
    edges = [round(total * sum(shares[:i]) / whole) for i in range(len(shares) + 1)]
    return [(a, b - a) for a, b in zip(edges[:-1], edges[1:]) if b > a]


def swap_pairs(block, axis, first):
    count = lax.axis_size(axis)
    route = []
    for low in range(first, count - 1, 2):
        route += [(low, low + 1), (low + 1, low)]
    return lax.ppermute(block, axis, route)


def swap_flipped(block, axis, flip):
    return lax.ppermute(block, axis, [(i, i ^ flip) for i in range(lax.axis_size(axis))])


def nearby_ids(image_ids, parts, part_rows):
    shard = lax.axis_index("dp")
    padded = jnp.pad(image_ids[::part_rows], (parts, parts), constant_values=-1)
    odd = lax.rem(shard, 2)

    def ids_of(other):
        return lax.dynamic_slice_in_dim(padded, (other + 1) * parts, parts)

    return jnp.stack((ids_of(shard), ids_of(shard + 1 - 2 * odd), ids_of(shard - 1 + 2 * odd)))


def columns(array, part, stride, first, width):
    start = pl.multiple_of(part * stride + first, HD)
    return array.at[:, pl.ds(start, width)]


def pack_kernel(stride, jobs, *refs):
    arrays, packed, (stage, in_sems, out_sems) = refs[:4], refs[4:-3], refs[-3:]
    me = lax.axis_index("tensor")
    loads, stores = [], []
    for number, (flip, first, count) in enumerate(jobs):
        for index, array in enumerate(arrays):
            load = pltpu.make_async_copy(
                columns(array, me ^ flip, stride, first * HD, count * HD),
                stage.at[flip, index, :, pl.ds(first * HD, count * HD)],
                in_sems.at[number * 4 + index],
            )
            load.start()
            loads.append(load)
    for number, (flip, first, count) in enumerate(jobs):
        for load in loads[number * 4 : number * 4 + 4]:
            load.wait()
        store = pltpu.make_async_copy(
            stage.at[flip, :, :, pl.ds(first * HD, count * HD)],
            packed[number],
            out_sems.at[number],
        )
        store.start()
        stores.append(store)
    for store in stores:
        store.wait()


def pack(arrays, parts, jobs):
    rows, total = arrays[0].shape
    stride = total // parts
    return pl.pallas_call(
        functools.partial(pack_kernel, stride, jobs),
        out_shape=[
            jax.ShapeDtypeStruct((4, rows, count * HD), jnp.bfloat16) for _, _, count in jobs
        ],
        in_specs=[pl.BlockSpec(memory_space=pl.ANY)] * 4,
        out_specs=[pl.BlockSpec(memory_space=pl.ANY)] * len(jobs),
        scratch_shapes=[
            pltpu.VMEM((parts, 4, rows, stride), jnp.bfloat16),
            pltpu.SemaphoreType.DMA((4 * len(jobs),)),
            pltpu.SemaphoreType.DMA((len(jobs),)),
        ],
        compiler_params=pltpu.CompilerParams(vmem_limit_bytes=VMEM_LIMIT),
        cost_estimate=SMALL_COST,
    )(*arrays)


def hold(array, after):
    return pl.pallas_call(
        lambda *refs: None,
        out_shape=jax.ShapeDtypeStruct(array.shape, array.dtype),
        in_specs=[pl.BlockSpec(memory_space=pl.ANY)] * (1 + len(after)),
        out_specs=pl.BlockSpec(memory_space=pl.ANY),
        input_output_aliases={0: 0},
        compiler_params=pltpu.CompilerParams(vmem_limit_bytes=VMEM_LIMIT),
        cost_estimate=SMALL_COST,
    )(array, *after)


def dot_nt(a, b):
    return lax.dot_general(a, b, (((1,), (1,)), ((), ())), preferred_element_type=jnp.float32)


def dot_tn(a, b):
    return lax.dot_general(a, b, (((0,), (0,)), ((), ())), preferred_element_type=jnp.float32)


def dot_nn(a, b):
    return jnp.dot(a, b, preferred_element_type=jnp.float32)


def attend_head(values_of, bias, size, rows):
    queries, keys, values, grads = values_of
    grad_k = grad_v = None
    for start in range(0, size, rows):
        tile = slice(start, start + rows)
        scores = dot_nt(keys, queries[tile]) + bias[:size, tile]
        weights = jnp.exp2((scores - jnp.max(scores, axis=0, keepdims=True)) * EXP2_SCALE)
        probs = weights * (1.0 / jnp.sum(weights, axis=0, keepdims=True))
        grad_probs = dot_nt(values, grads[tile])
        inner = jnp.sum(probs * grad_probs, axis=0, keepdims=True)
        low = probs.astype(jnp.bfloat16)
        grad_scores = (probs * (grad_probs - inner)).astype(jnp.bfloat16)
        tile_v = dot_nn(low[:rows], grads[tile])
        tile_k = dot_nn(grad_scores[:rows], queries[tile])
        if start == 0:
            attended = dot_tn(low, values)
            grad_q = dot_tn(grad_scores, keys)
            grad_k, grad_v = tile_k, tile_v
        else:
            grad_k, grad_v = grad_k + tile_k, grad_v + tile_v
    return attended, grad_q * SCALE, grad_k * SCALE, grad_v


def attend_kernel(parts, part_rows, heads, first_head, has_outs, *refs):
    image_ids, refs = refs[0], refs[1:]
    mine, others = refs[:parts], refs[parts : 3 * parts]
    refs = refs[3 * parts + (4 if has_outs else 0) :]
    outs, (bias, window, table, sems) = refs[:4], refs[4:]
    rows = parts * part_rows
    most = 3 * rows
    me = lax.axis_index("tensor")
    head = pl.program_id(0)

    def head_columns(ref, number):
        if ref.shape[2] > heads * HD:
            number = number + first_head
        return ref.at[:, :, pl.ds(pl.multiple_of(number * HD, HD), HD)]

    def copy_of(ref, number, place, sem):
        buffer = lax.rem(number, 2)
        start = pl.multiple_of(place * part_rows, part_rows)
        return pltpu.make_async_copy(
            head_columns(ref, number),
            window.at[buffer, :, pl.ds(start, part_rows), :],
            sems.at[buffer, sem],
        )

    def fetch(number):
        for flip in range(parts):
            copy_of(mine[flip], number, me ^ flip, flip).start()
        for slot in range(2 * parts):

            @pl.when(slot < table[2 * parts])
            def _():
                for source in range(2 * parts):

                    @pl.when(table[slot] == source)
                    def _():
                        copy_of(others[source], number, parts + slot, parts + slot).start()

    def await_fetch(number):
        for flip in range(parts):
            copy_of(mine[flip], number, me ^ flip, flip).wait()
        for slot in range(2 * parts):

            @pl.when(slot < table[2 * parts])
            def _():
                copy_of(others[0], number, parts + slot, parts + slot).wait()

    @pl.when(head == 0)
    def _():
        window[...] = jnp.zeros_like(window)
        count = jnp.int32(0)
        for other in range(2 * parts):
            side, flip = 1 + other // parts, other % parts
            other_id = image_ids[side, me ^ flip]
            shared = other_id == image_ids[0, 0]
            for part in range(1, parts):
                shared = shared | (other_id == image_ids[0, part])
            table[count] = other
            count = count + shared.astype(jnp.int32)
        table[2 * parts] = count
        fetch(0)

        def ids_along(axis, size):
            shape = (size, 1) if axis == 0 else (1, size)
            place = lax.broadcasted_iota(jnp.int32, shape, axis)
            ids = jnp.full(shape, -2, jnp.int32)
            for slot in range(size // part_rows):
                if slot < parts:
                    slot_id = image_ids[0, slot]
                else:
                    used = slot - parts < count
                    source = jnp.where(used, table[slot - parts], 0)
                    slot_id = image_ids[1 + source // parts, me ^ lax.rem(source, parts)]
                    slot_id = jnp.where(used, slot_id, -2)
                inside = (place >= slot * part_rows) & (place < (slot + 1) * part_rows)
                ids = jnp.where(inside, slot_id, ids)
            return ids

        for size in range(rows, most + 1, rows):
            slots = (size - rows) // part_rows

            @pl.when((count <= slots) & (count > slots - parts))
            def _():
                same = ids_along(0, size) == ids_along(1, size)
                bias[:size, :size] = jnp.where(same, 0.0, MASKED)

    @pl.when(head + 1 < heads)
    def _():
        fetch(head + 1)

    await_fetch(head)
    count = table[2 * parts]
    buffer = lax.rem(head, 2)
    for size in range(rows, most + 1, rows):
        slots = (size - rows) // part_rows

        @pl.when((count <= slots) & (count > slots - parts))
        def _():
            values_of = [window[buffer, index, :size] for index in range(4)]
            for out, result in zip(outs, attend_head(values_of, bias, size, rows)):
                out[...] = result.astype(jnp.bfloat16)


def attend(image_ids, groups, outs, first_head, heads):
    parts = len(groups[0])
    _, part_rows, width = groups[0][0].shape
    rows = parts * part_rows
    out_spec = pl.BlockSpec((rows, HD), lambda h: (0, h + first_head))
    has_outs = outs is not None
    pieces = [piece for group in groups for piece in group]
    aliases = {1 + len(pieces) + i: i for i in range(4)} if has_outs else {}
    return pl.pallas_call(
        functools.partial(attend_kernel, parts, part_rows, heads, first_head, has_outs),
        grid=(heads,),
        out_shape=[jax.ShapeDtypeStruct((rows, width), jnp.bfloat16)] * 4,
        in_specs=[pl.BlockSpec(memory_space=pltpu.SMEM)]
        + [pl.BlockSpec(memory_space=pl.ANY)] * (len(pieces) + (4 if has_outs else 0)),
        out_specs=[out_spec] * 4,
        scratch_shapes=[
            pltpu.VMEM((3 * rows, 3 * rows), jnp.float32),
            pltpu.VMEM((2, 4, 3 * rows, HD), jnp.bfloat16),
            pltpu.SMEM((2 * parts + 1,), jnp.int32),
            pltpu.SemaphoreType.DMA((2, 3 * parts)),
        ],
        input_output_aliases=aliases,
        compiler_params=pltpu.CompilerParams(
            dimension_semantics=("arbitrary",), vmem_limit_bytes=VMEM_LIMIT
        ),
        cost_estimate=pl.CostEstimate(
            flops=heads * ATTEND_FLOPS, bytes_accessed=1, transcendentals=0
        ),
    )(image_ids, *pieces, *(outs or ()))


def shards(queries, key_vectors, value_vectors, grad_output, image_ids):
    arrays = (queries, key_vectors, value_vectors, grad_output)
    parts = lax.axis_size("tensor")
    part_rows = queries.shape[0]
    head_total = queries.shape[1] // HD // parts
    near_ids = nearby_ids(image_ids, parts, part_rows)
    chunks = split_counts(head_total, CHUNK_SHARES)
    last = parts - 1

    jobs = [(flip, 0, head_total) for flip in range(last)]
    jobs += [(last, first, count) for first, count in chunks]
    packed = pack(arrays, parts, jobs)

    def spread(piece):
        return piece, swap_pairs(piece, "dp", 0), swap_pairs(piece, "dp", 1)

    wide = [spread(packed[0])]
    for flip in range(1, last):
        wide.append(spread(swap_flipped(packed[flip], "tensor", flip)))
    outs, narrow = None, []
    for number, (first_head, count) in enumerate(chunks):
        piece = packed[last + number]
        if number < 2:
            piece = hold(piece, [wide[max(1, last - 2 + number)][0]])
        else:
            piece = hold(piece, [narrow[number - 2][0]])
        narrow.append(spread(swap_flipped(piece, "tensor", last)))
    for number, (first_head, count) in enumerate(chunks):
        groups = list(zip(*wide, narrow[number]))
        outs = attend(near_ids, groups, outs, first_head, count)
    return tuple(outs)


def solution(mesh):
    return jax.shard_map(
        shards,
        mesh=mesh,
        in_specs=(
            P(("dp", "tensor"), None),
            P(("dp", "tensor"), None),
            P(("dp", "tensor"), None),
            P(("dp", "tensor"), None),
            P(),
        ),
        out_specs=(P("dp", "tensor"), P("dp", "tensor"), P("dp", "tensor"), P("dp", "tensor")),
        check_vma=False,
    )
```

time: 123 us -> 148 us (1.20)
  the two profiles are of different devices: /device:TPU:1 before, /device:TPU:15 now
where the time goes in v9:
time: 148 us
  starting transfers between devices  57.5 us (39%)
  waiting for transfers between devices  53.7 us (36%)
  Pallas kernels  31.4 us (21%)
  local copies, waits for them, and re-layouts  3.65 us (2%)
    ppermute x5, waiting for transfers between devices, swap_flipped(): lax.ppermute(block, axis, [(i, i ^ flip) for i in range(lax.axis_size(axi...  53.6 us
    ppermute x12, starting transfers between devices, swap_pairs(): return lax.ppermute(block, axis, route)  52.2 us
    pallas_call x3, Pallas kernels, attend(): pl.pallas_call(functools.partial(attend_kernel, parts, part_rows, heads,...  28.2 us
    ppermute x5, starting transfers between devices, swap_flipped(): lax.ppermute(block, axis, [(i, i ^ flip) for i in range(lax.axis_size(axi...  5.31 us
    pallas_call x1, Pallas kernels, pack(): pl.pallas_call(functools.partial(pack_kernel, stride, jobs), out_shape=[j...  3.16 us
  transfers between devices with their start and end apart: 17, of which 4 were waited for; matrix products, arithmetic and copies ran while one was open for 1% of the time, Pallas kernels for 15%

profile of v9, /device:TPU:15, one launch (start us, length us, event | category | flops | bytes accessed | tf_op | source)
XLA Modules:
  0.0 147.8 jit_solution(15682258000797200198)
XLA Ops:
  0.6 3.2 %shard_map.84 = (bf16[4,64,1536]{2,1,0:T(8,128)(2,1)}, bf16[4,64,1536]{2,1,0:T(8,128)(2,1)}, bf16[4,64,1536]{2,1,0:T(8,128)(2,1)}, bf16[4,64,768]{2,1,0:T(8,128)...) custom-call(bf16[64,6144]{1,0:T(8,128)(2,1)} %refs_0_.1, bf16[64,6144]{1,0:T(8,128)(2,1)} %refs_1_.1, ...), custom_call_target="tpu_custom_call" | custom-call | flops 1 | bytes 1 | tf_op jit(solution)/shard_map/pallas_call | solution.py:85
  3.8 0.2 collective-permute-start
  4.0 2.3 %collective-permute-start.1 = (bf16[4,64,1536]{2,1,0:T(8,128)(2,1)}, bf16[4,64,1536]{2,1,0:T(8,128)(2,1)}, u32[]{:S(2)}, u32[]{:S(2)}) collective-permute-start(bf16[4,64,1536]{2,1,0:T(8,128)(2,1)} %get-tuple-element.20), channel_id=1, source_target_pairs={{0,2},{1,3},{2,0},{3,1},{4,6},{5,7},{6,4},{7,5},{8,10},{9,11},{10,... | collective-permute-start | bytes 2359304 | tf_op jit(solution)/shard_map/ppermute | solution.py:36
  6.3 1.5 %collective-permute-start.8 = (bf16[4,64,1536]{2,1,0:T(8,128)(2,1)}, bf16[4,64,1536]{2,1,0:T(8,128)(2,1)}, u32[]{:S(2)}, u32[]{:S(2)}) collective-permute-start(bf16[4,64,1536]{2,1,0:T(8,128)(2,1)} %get-tuple-element.18.refs_1_), channel_id=1, source_target_pairs={{4,8},{8,4},{12,16},{16,12},{20,24},{24,20},{5,9},{9,5},{13,17},{1... | collective-permute-start | bytes 2359304 | tf_op jit(solution)/shard_map/ppermute | solution.py:32
  7.9 1.7 %collective-permute-start.4 = (bf16[4,64,1536]{2,1,0:T(8,128)(2,1)}, bf16[4,64,1536]{2,1,0:T(8,128)(2,1)}, u32[]{:S(2)}, u32[]{:S(2)}) collective-permute-start(bf16[4,64,1536]{2,1,0:T(8,128)(2,1)} %get-tuple-element.18.refs_1_), channel_id=1, source_target_pairs={{0,4},{4,0},{8,12},{12,8},{16,20},{20,16},{24,28},{28,24},{1,5},{5... | collective-permute-start | bytes 2359304 | tf_op jit(solution)/shard_map/ppermute | solution.py:32
  9.6 27.7 %collective-permute-done.refs_1_.refs_2_ = bf16[4,64,1536]{2,1,0:T(8,128)(2,1)S(1)} collective-permute-done((bf16[4,64,1536]{2,1,0:T(8,128)(2,1)}, bf16[4,64,1536]{2,1,0:T(8,128)(2,1)S(1)}, u32[]{:S(2)}, u32[]{:S(2)}) %collective-permute-start) | collective-permute-done | bytes 786464 | tf_op jit(solution)/shard_map/ppermute | solution.py:36
  37.3 0.9 copy-done
  38.2 1.3 collective-permute-start.2
  39.5 1.0 collective-permute-done.1.refs_1_.refs_3_
  40.5 0.2 collective-permute-start.12
  40.7 24.9 %collective-permute-done.2.refs_1_.refs_4_ = bf16[4,64,768]{2,1,0:T(8,128)(2,1)} collective-permute-done((bf16[4,64,768]{2,1,0:T(8,128)(2,1)}, bf16[4,64,768]{2,1,0:T(8,128)(2,1)}, u32[]{:S(2)}, u32[]{:S(2)}) %collective-permute-start.2) | collective-permute-done | bytes 393248 | tf_op jit(solution)/shard_map/ppermute | solution.py:36
  65.6 1.3 collective-permute-start.3
  66.9 1.4 collective-permute-start.16
  68.3 0.7 collective-permute-start.9
  69.0 7.2 %collective-permute-start.5 = (bf16[4,64,1536]{2,1,0:T(8,128)(2,1)S(1)}, bf16[4,64,1536]{2,1,0:T(8,128)(2,1)S(1)}, u32[]{:S(2)}, u32[]{:S(2)}) collective-permute-start(bf16[4,64,1536]{2,1,0:T(8,128)(2,1)S(1)} %copy-done.1), channel_id=1, source_target_pairs={{0,4},{4,0},{8,12},{12,8},{16,20},{20,16},{24,28},{28,24},{1,5},{5... | collective-permute-start | bytes 2359304 | tf_op jit(solution)/shard_map/ppermute | solution.py:32
  76.3 0.7 collective-permute-start.10
  77.0 2.8 %collective-permute-start.6 = (bf16[4,64,1536]{2,1,0:T(8,128)(2,1)}, bf16[4,64,1536]{2,1,0:T(8,128)(2,1)}, u32[]{:S(2)}, u32[]{:S(2)}) collective-permute-start(bf16[4,64,1536]{2,1,0:T(8,128)(2,1)} %collective-permute-done.1.refs_1_.refs_3_), channel_id=1, source_target_pairs={{0,4},{4,0},{8,12},{12,8},{16,20},{20,16},{24,28},{28,24},{1,5},{5... | collective-permute-start | bytes 2359304 | tf_op jit(solution)/shard_map/ppermute | solution.py:32
  79.8 4.4 %collective-permute-start.15 = (bf16[4,64,768]{2,1,0:T(8,128)(2,1)}, bf16[4,64,768]{2,1,0:T(8,128)(2,1)S(1)}, u32[]{:S(2)}, u32[]{:S(2)}) collective-permute-start(bf16[4,64,768]{2,1,0:T(8,128)(2,1)} %collective-permute-done.2.refs_1_.refs_4_), channel_id=1, source_target_pairs={{0,4},{4,0},{8,12},{12,8},{16,20},{20,16},{24,28},{28,24},{1,5},{5... | collective-permute-start | bytes 1179656 | tf_op jit(solution)/shard_map/ppermute | solution.py:32
  84.2 0.8 slice.3
  85.0 0.1 dynamic-slice_bitcast_fusion.2
  85.1 0.6 pad_add_fusion.refs_0_
  85.7 0.1 collective-permute-done.15.refs_8_
  85.7 1.4 collective-permute-start.14
  87.1 13.8 %collective-permute-start.13 = (bf16[4,64,512]{2,1,0:T(8,128)(2,1)}, bf16[4,64,512]{2,1,0:T(8,128)(2,1)}, u32[]{:S(2)}, u32[]{:S(2)}) collective-permute-start(bf16[4,64,512]{2,1,0:T(8,128)(2,1)} %collective-permute-done.12.refs_4_), channel_id=1, source_target_pairs={{0,4},{4,0},{8,12},{12,8},{16,20},{20,16},{24,28},{28,24},{1,5},{5... | collective-permute-start | bytes 786440 | tf_op jit(solution)/shard_map/ppermute | solution.py:32
  100.9 0.7 collective-permute-start.11
  101.6 0.2 copy-done.3
  101.8 0.9 copy-done.4
  102.7 15.9 %collective-permute-start.7 = (bf16[4,64,256]{2,1,0:T(8,128)(2,1)}, bf16[4,64,256]{2,1,0:T(8,128)(2,1)S(1)}, u32[]{:S(2)}, u32[]{:S(2)}) collective-permute-start(bf16[4,64,256]{2,1,0:T(8,128)(2,1)} %copy-done.6), channel_id=1, source_target_pairs={{0,4},{4,0},{8,12},{12,8},{16,20},{20,16},{24,28},{28,24},{1,5},{5... | collective-permute-start | bytes 393224 | tf_op jit(solution)/shard_map/ppermute | solution.py:32
  118.7 13.0 %shard_map.88 = (bf16[256,1536]{1,0:T(8,128)(2,1)}, bf16[256,1536]{1,0:T(8,128)(2,1)}, bf16[256,1536]{1,0:T(8,128)(2,1)}, bf16[256,1536]{1,0:T(8,128)(2,1)}) custom-call(s32[3,4]{1,0:T(4,128)} %pad_add_fusion.refs_0_, bf16[4,64,1536]{2,1,0:T(8,128)(2,1)} %get-tuple-element.18.refs_1_, bf16[4,64,1536]{2,1,0:T(8,128)(2,1)} %copy-done, ...), custom_call_target="tpu_custom_call" | custom-call | flops 8999999488 | bytes 1 | tf_op jit(solution)/shard_map/pallas_call | solution.py:259
  131.7 9.4 %shard_map.89 = (bf16[256,1536]{1,0:T(8,128)(2,1)}, bf16[256,1536]{1,0:T(8,128)(2,1)}, bf16[256,1536]{1,0:T(8,128)(2,1)}, bf16[256,1536]{1,0:T(8,128)(2,1)}) custom-call(s32[3,4]{1,0:T(4,128)} %pad_add_fusion.refs_0_, bf16[4,64,1536]{2,1,0:T(8,128)(2,1)} %get-tuple-element.18.refs_1_, ...), custom_call_target="tpu_custom_call", output_to_operand_aliasing={{0}: (13, {}), {1}: (14, {}), {2}: (15, {}), {3}: (16, {})} | custom-call | flops 6000000000 | bytes 1 | tf_op jit(solution)/shard_map/pallas_call | solution.py:259
  141.2 0.6 copy-done.7
  141.9 5.8 %shard_map.90 = (bf16[256,1536]{1,0:T(8,128)(2,1)}, bf16[256,1536]{1,0:T(8,128)(2,1)}, bf16[256,1536]{1,0:T(8,128)(2,1)}, bf16[256,1536]{1,0:T(8,128)(2,1)}) custom-call(s32[3,4]{1,0:T(4,128)} %pad_add_fusion.refs_0_, bf16[4,64,1536]{2,1,0:T(8,128)(2,1)} %get-tuple-element.18.refs_1_, ...), custom_call_target="tpu_custom_call", output_to_operand_aliasing={{0}: (13, {}), {1}: (14, {}), {2}: (15, {}), {3}: (16, {})} | custom-call | flops 3000000000 | bytes 1 | tf_op jit(solution)/shard_map/pallas_call | solution.py:259
  (30 shorter events, 0.1 us)
Async XLA Ops:
  3.8 33.5 %collective-permute-start = (bf16[4,64,1536]{2,1,0:T(8,128)(2,1)}, bf16[4,64,1536]{2,1,0:T(8,128)(2,1)S(1)}, u32[]{:S(2)}, u32[]{:S(2)}) collective-permute-start(bf16[4,64,1536]{2,1,0:T(8,128)(2,1)} %get-tuple-element.19), channel_id=1, source_target_pairs={{0,1},{1,0},{2,3},{3,2},{4,5},{5,4},{6,7},{7,6},{8,9},{9,8},{10,11... | collective-permute-start | bytes 2359304 | tf_op jit(solution)/shard_map/ppermute | solution.py:36
  4.0 36.5 %collective-permute-start.1 = (bf16[4,64,1536]{2,1,0:T(8,128)(2,1)}, bf16[4,64,1536]{2,1,0:T(8,128)(2,1)}, u32[]{:S(2)}, u32[]{:S(2)}) collective-permute-start(bf16[4,64,1536]{2,1,0:T(8,128)(2,1)} %get-tuple-element.20), channel_id=1, source_target_pairs={{0,2},{1,3},{2,0},{3,1},{4,6},{5,7},{6,4},{7,5},{8,10},{9,11},{10,... | collective-permute-start | bytes 2359304 | tf_op jit(solution)/shard_map/ppermute | solution.py:36
  6.3 62.0 %collective-permute-start.8 = (bf16[4,64,1536]{2,1,0:T(8,128)(2,1)}, bf16[4,64,1536]{2,1,0:T(8,128)(2,1)}, u32[]{:S(2)}, u32[]{:S(2)}) collective-permute-start(bf16[4,64,1536]{2,1,0:T(8,128)(2,1)} %get-tuple-element.18.refs_1_), channel_id=1, source_target_pairs={{4,8},{8,4},{12,16},{16,12},{20,24},{24,20},{5,9},{9,5},{13,17},{1... | collective-permute-start | bytes 2359304 | tf_op jit(solution)/shard_map/ppermute | solution.py:32
  7.9 61.1 %collective-permute-start.4 = (bf16[4,64,1536]{2,1,0:T(8,128)(2,1)}, bf16[4,64,1536]{2,1,0:T(8,128)(2,1)}, u32[]{:S(2)}, u32[]{:S(2)}) collective-permute-start(bf16[4,64,1536]{2,1,0:T(8,128)(2,1)} %get-tuple-element.18.refs_1_), channel_id=1, source_target_pairs={{0,4},{4,0},{8,12},{12,8},{16,20},{20,16},{24,28},{28,24},{1,5},{5... | collective-permute-start | bytes 2359304 | tf_op jit(solution)/shard_map/ppermute | solution.py:32
  37.3 0.9 copy-start
  38.2 27.4 %collective-permute-start.2 = (bf16[4,64,768]{2,1,0:T(8,128)(2,1)}, bf16[4,64,768]{2,1,0:T(8,128)(2,1)}, u32[]{:S(2)}, u32[]{:S(2)}) collective-permute-start(bf16[4,64,768]{2,1,0:T(8,128)(2,1)} %shard_map.85), channel_id=1, source_target_pairs={{0,3},{1,2},{2,1},{3,0},{4,7},{5,6},{6,5},{7,4},{8,11},{9,10},{10,... | collective-permute-start | bytes 1179656 | tf_op jit(solution)/shard_map/ppermute | solution.py:36
  40.5 27.8 %copy-start.1 = (bf16[4,64,1536]{2,1,0:T(8,128)(2,1)S(1)}, bf16[4,64,1536]{2,1,0:T(8,128)(2,1)}, u32[]{:S(2)}) copy-start(bf16[4,64,1536]{2,1,0:T(8,128)(2,1)} %copy-done) | copy-start | bytes 2359300
  40.5 35.7 %collective-permute-start.12 = (bf16[4,64,512]{2,1,0:T(8,128)(2,1)}, bf16[4,64,512]{2,1,0:T(8,128)(2,1)}, u32[]{:S(2)}, u32[]{:S(2)}) collective-permute-start(bf16[4,64,512]{2,1,0:T(8,128)(2,1)} %shard_map.87), channel_id=1, source_target_pairs={{0,3},{1,2},{2,1},{3,0},{4,7},{5,6},{6,5},{7,4},{8,11},{9,10},{10,... | collective-permute-start | bytes 786440 | tf_op jit(solution)/shard_map/ppermute | solution.py:36
  65.6 11.4 %collective-permute-start.3 = (bf16[4,64,256]{2,1,0:T(8,128)(2,1)}, bf16[4,64,256]{2,1,0:T(8,128)(2,1)S(1)}, u32[]{:S(2)}, u32[]{:S(2)}) collective-permute-start(bf16[4,64,256]{2,1,0:T(8,128)(2,1)} %shard_map.86), channel_id=1, source_target_pairs={{0,3},{1,2},{2,1},{3,0},{4,7},{5,6},{6,5},{7,4},{8,11},{9,10},{10,... | collective-permute-start | bytes 393224 | tf_op jit(solution)/shard_map/ppermute | solution.py:36
  66.9 12.9 %collective-permute-start.16 = (bf16[4,64,768]{2,1,0:T(8,128)(2,1)}, bf16[4,64,768]{2,1,0:T(8,128)(2,1)}, u32[]{:S(2)}, u32[]{:S(2)}) collective-permute-start(bf16[4,64,768]{2,1,0:T(8,128)(2,1)} %collective-permute-done.2.refs_1_.refs_4_), channel_id=1, source_target_pairs={{4,8},{8,4},{12,16},{16,12},{20,24},{24,20},{5,9},{9,5},{13,17},{1... | collective-permute-start | bytes 1179656 | tf_op jit(solution)/shard_map/ppermute | solution.py:32
  68.3 18.8 %collective-permute-start.9 = (bf16[4,64,1536]{2,1,0:T(8,128)(2,1)S(1)}, bf16[4,64,1536]{2,1,0:T(8,128)(2,1)S(1)}, u32[]{:S(2)}, u32[]{:S(2)}) collective-permute-start(bf16[4,64,1536]{2,1,0:T(8,128)(2,1)S(1)} %copy-done.1), channel_id=1, source_target_pairs={{4,8},{8,4},{12,16},{16,12},{20,24},{24,20},{5,9},{9,5},{13,17},{1... | collective-permute-start | bytes 2359304 | tf_op jit(solution)/shard_map/ppermute | solution.py:32
  69.0 31.9 %collective-permute-start.5 = (bf16[4,64,1536]{2,1,0:T(8,128)(2,1)S(1)}, bf16[4,64,1536]{2,1,0:T(8,128)(2,1)S(1)}, u32[]{:S(2)}, u32[]{:S(2)}) collective-permute-start(bf16[4,64,1536]{2,1,0:T(8,128)(2,1)S(1)} %copy-done.1), channel_id=1, source_target_pairs={{0,4},{4,0},{8,12},{12,8},{16,20},{20,16},{24,28},{28,24},{1,5},{5... | collective-permute-start | bytes 2359304 | tf_op jit(solution)/shard_map/ppermute | solution.py:32
  76.3 25.6 %collective-permute-start.10 = (bf16[4,64,1536]{2,1,0:T(8,128)(2,1)}, bf16[4,64,1536]{2,1,0:T(8,128)(2,1)S(1)}, u32[]{:S(2)}, u32[]{:S(2)}) collective-permute-start(bf16[4,64,1536]{2,1,0:T(8,128)(2,1)} %collective-permute-done.1.refs_1_.refs_3_), channel_id=1, source_target_pairs={{4,8},{8,4},{12,16},{16,12},{20,24},{24,20},{5,9},{9,5},{13,17},{1... | collective-permute-start | bytes 2359304 | tf_op jit(solution)/shard_map/ppermute | solution.py:32
  77.0 2.8 %copy-start.6 = (bf16[4,64,256]{2,1,0:T(8,128)(2,1)}, bf16[4,64,256]{2,1,0:T(8,128)(2,1)S(1)}, u32[]{:S(2)}) copy-start(bf16[4,64,256]{2,1,0:T(8,128)(2,1)S(1)} %collective-permute-done.3.refs_4_) | copy-start | bytes 393220
  77.0 41.7 %collective-permute-start.6 = (bf16[4,64,1536]{2,1,0:T(8,128)(2,1)}, bf16[4,64,1536]{2,1,0:T(8,128)(2,1)}, u32[]{:S(2)}, u32[]{:S(2)}) collective-permute-start(bf16[4,64,1536]{2,1,0:T(8,128)(2,1)} %collective-permute-done.1.refs_1_.refs_3_), channel_id=1, source_target_pairs={{0,4},{4,0},{8,12},{12,8},{16,20},{20,16},{24,28},{28,24},{1,5},{5... | collective-permute-start | bytes 2359304 | tf_op jit(solution)/shard_map/ppermute | solution.py:32
  79.8 5.9 %collective-permute-start.15 = (bf16[4,64,768]{2,1,0:T(8,128)(2,1)}, bf16[4,64,768]{2,1,0:T(8,128)(2,1)S(1)}, u32[]{:S(2)}, u32[]{:S(2)}) collective-permute-start(bf16[4,64,768]{2,1,0:T(8,128)(2,1)} %collective-permute-done.2.refs_1_.refs_4_), channel_id=1, source_target_pairs={{0,4},{4,0},{8,12},{12,8},{16,20},{20,16},{24,28},{28,24},{1,5},{5... | collective-permute-start | bytes 1179656 | tf_op jit(solution)/shard_map/ppermute | solution.py:32
  85.7 32.9 %copy-start.5 = (bf16[4,64,768]{2,1,0:T(8,128)(2,1)}, bf16[4,64,768]{2,1,0:T(8,128)(2,1)S(1)}, u32[]{:S(2)}) copy-start(bf16[4,64,768]{2,1,0:T(8,128)(2,1)S(1)} %collective-permute-done.15.refs_8_) | copy-start | bytes 1179652
  85.7 46.0 %collective-permute-start.14 = (bf16[4,64,512]{2,1,0:T(8,128)(2,1)}, bf16[4,64,512]{2,1,0:T(8,128)(2,1)}, u32[]{:S(2)}, u32[]{:S(2)}) collective-permute-start(bf16[4,64,512]{2,1,0:T(8,128)(2,1)} %collective-permute-done.12.refs_4_), channel_id=1, source_target_pairs={{4,8},{8,4},{12,16},{16,12},{20,24},{24,20},{5,9},{9,5},{13,17},{1... | collective-permute-start | bytes 786440 | tf_op jit(solution)/shard_map/ppermute | solution.py:32
  87.1 13.8 %copy-start.2 = (bf16[4,64,1536]{2,1,0:T(8,128)(2,1)}, bf16[4,64,1536]{2,1,0:T(8,128)(2,1)S(1)}, u32[]{:S(2)}) copy-start(bf16[4,64,1536]{2,1,0:T(8,128)(2,1)S(1)} %collective-permute-done.9.refs_10_) | copy-start | bytes 2359300
  87.1 44.6 %collective-permute-start.13 = (bf16[4,64,512]{2,1,0:T(8,128)(2,1)}, bf16[4,64,512]{2,1,0:T(8,128)(2,1)}, u32[]{:S(2)}, u32[]{:S(2)}) collective-permute-start(bf16[4,64,512]{2,1,0:T(8,128)(2,1)} %collective-permute-done.12.refs_4_), channel_id=1, source_target_pairs={{0,4},{4,0},{8,12},{12,8},{16,20},{20,16},{24,28},{28,24},{1,5},{5... | collective-permute-start | bytes 786440 | tf_op jit(solution)/shard_map/ppermute | solution.py:32
  100.9 0.9 copy-start.3
  100.9 40.3 %collective-permute-start.11 = (bf16[4,64,256]{2,1,0:T(8,128)(2,1)}, bf16[4,64,256]{2,1,0:T(8,128)(2,1)S(1)}, u32[]{:S(2)}, u32[]{:S(2)}) collective-permute-start(bf16[4,64,256]{2,1,0:T(8,128)(2,1)} %copy-done.6), channel_id=1, source_target_pairs={{4,8},{8,4},{12,16},{16,12},{20,24},{24,20},{5,9},{9,5},{13,17},{1... | collective-permute-start | bytes 393224 | tf_op jit(solution)/shard_map/ppermute | solution.py:32
  101.8 0.9 copy-start.4
  102.7 38.5 %collective-permute-start.7 = (bf16[4,64,256]{2,1,0:T(8,128)(2,1)}, bf16[4,64,256]{2,1,0:T(8,128)(2,1)S(1)}, u32[]{:S(2)}, u32[]{:S(2)}) collective-permute-start(bf16[4,64,256]{2,1,0:T(8,128)(2,1)} %copy-done.6), channel_id=1, source_target_pairs={{0,4},{4,0},{8,12},{12,8},{16,20},{20,16},{24,28},{28,24},{1,5},{5... | collective-permute-start | bytes 393224 | tf_op jit(solution)/shard_map/ppermute | solution.py:32
  141.2 0.6 copy-start.7
  141.2 0.7 copy-start.8

commit v10 on v9

--- a/solution.py
+++ b/solution.py
@@ -12,8 +12,9 @@
 SCALE = 1.0 / math.sqrt(HD)
 EXP2_SCALE = SCALE * math.log2(math.e)
 MASKED = -1e30
+HALF_SHARES = (6, 6)
 CHUNK_SHARES = (6, 4, 2)
-VMEM_LIMIT = 63 * 1024 * 1024
+VMEM_LIMIT = 64 * 1024 * 1024 - 256 * 1024
 ATTEND_FLOPS = 1_500_000_000
 SMALL_COST = pl.CostEstimate(flops=1, bytes_accessed=1, transcendentals=0)
 
@@ -146,66 +147,51 @@
     return attended, grad_q * SCALE, grad_k * SCALE, grad_v
 
 
-def attend_kernel(parts, part_rows, heads, first_head, has_outs, *refs):
+def attend_kernel(parts, part_rows, heads, offsets, has_outs, *refs):
     image_ids, refs = refs[0], refs[1:]
     mine, others = refs[:parts], refs[parts : 3 * parts]
     refs = refs[3 * parts + (4 if has_outs else 0) :]
-    outs, (bias, window, table, sems) = refs[:4], refs[4:]
+    outs, (bias, window, slot_of, table, sems) = refs[:4], refs[4:]
     rows = parts * part_rows
     most = 3 * rows
     me = lax.axis_index("tensor")
     head = pl.program_id(0)
 
-    def head_columns(ref, number):
-        if ref.shape[2] > heads * HD:
-            number = number + first_head
-        return ref.at[:, :, pl.ds(pl.multiple_of(number * HD, HD), HD)]
-
-    def copy_of(ref, number, place, sem):
+    def copy_of(ref, flip, number, place, sem):
         buffer = lax.rem(number, 2)
         start = pl.multiple_of(place * part_rows, part_rows)
+        column = pl.multiple_of((number + offsets[flip]) * HD, HD)
         return pltpu.make_async_copy(
-            head_columns(ref, number),
+            ref.at[:, :, pl.ds(column, HD)],
             window.at[buffer, :, pl.ds(start, part_rows), :],
             sems.at[buffer, sem],
         )
 
-    def fetch(number):
+    def copies(number, act):
         for flip in range(parts):
-            copy_of(mine[flip], number, me ^ flip, flip).start()
-        for slot in range(2 * parts):
-
-            @pl.when(slot < table[2 * parts])
+            act(copy_of(mine[flip], flip, number, me ^ flip, flip))
+        for source in range(2 * parts):
+            slot = slot_of[source]
+
+            @pl.when(slot >= 0)
             def _():
-                for source in range(2 * parts):
-
-                    @pl.when(table[slot] == source)
-                    def _():
-                        copy_of(others[source], number, parts + slot, parts + slot).start()
-
-    def await_fetch(number):
-        for flip in range(parts):
-            copy_of(mine[flip], number, me ^ flip, flip).wait()
-        for slot in range(2 * parts):
-
-            @pl.when(slot < table[2 * parts])
-            def _():
-                copy_of(others[0], number, parts + slot, parts + slot).wait()
+                act(copy_of(others[source], source % parts, number, parts + slot, parts + source))
 
     @pl.when(head == 0)
     def _():
-        window[...] = jnp.zeros_like(window)
         count = jnp.int32(0)
-        for other in range(2 * parts):
-            side, flip = 1 + other // parts, other % parts
+        for source in range(2 * parts):
+            side, flip = 1 + source // parts, source % parts
             other_id = image_ids[side, me ^ flip]
             shared = other_id == image_ids[0, 0]
             for part in range(1, parts):
                 shared = shared | (other_id == image_ids[0, part])
-            table[count] = other
+            slot_of[source] = jnp.where(shared, count, -1)
+            table[count] = other_id
             count = count + shared.astype(jnp.int32)
         table[2 * parts] = count
-        fetch(0)
+        window[...] = jnp.zeros_like(window)
+        copies(0, lambda copy: copy.start())
 
         def ids_along(axis, size):
             shape = (size, 1) if axis == 0 else (1, size)
@@ -215,10 +201,7 @@
                 if slot < parts:
                     slot_id = image_ids[0, slot]
                 else:
-                    used = slot - parts < count
-                    source = jnp.where(used, table[slot - parts], 0)
-                    slot_id = image_ids[1 + source // parts, me ^ lax.rem(source, parts)]
-                    slot_id = jnp.where(used, slot_id, -2)
+                    slot_id = jnp.where(slot - parts < count, table[slot - parts], -2)
                 inside = (place >= slot * part_rows) & (place < (slot + 1) * part_rows)
                 ids = jnp.where(inside, slot_id, ids)
             return ids
@@ -233,9 +216,9 @@
 
     @pl.when(head + 1 < heads)
     def _():
-        fetch(head + 1)
-
-    await_fetch(head)
+        copies(head + 1, lambda copy: copy.start())
+
+    copies(head, lambda copy: copy.wait())
     count = table[2 * parts]
     buffer = lax.rem(head, 2)
     for size in range(rows, most + 1, rows):
@@ -248,7 +231,7 @@
                 out[...] = result.astype(jnp.bfloat16)
 
 
-def attend(image_ids, groups, outs, first_head, heads):
+def attend(image_ids, groups, offsets, outs, first_head, heads):
     parts = len(groups[0])
     _, part_rows, width = groups[0][0].shape
     rows = parts * part_rows
@@ -257,7 +240,7 @@
     pieces = [piece for group in groups for piece in group]
     aliases = {1 + len(pieces) + i: i for i in range(4)} if has_outs else {}
     return pl.pallas_call(
-        functools.partial(attend_kernel, parts, part_rows, heads, first_head, has_outs),
+        functools.partial(attend_kernel, parts, part_rows, heads, offsets, has_outs),
         grid=(heads,),
         out_shape=[jax.ShapeDtypeStruct((rows, width), jnp.bfloat16)] * 4,
         in_specs=[pl.BlockSpec(memory_space=pltpu.SMEM)]
@@ -266,6 +249,7 @@
         scratch_shapes=[
             pltpu.VMEM((3 * rows, 3 * rows), jnp.float32),
             pltpu.VMEM((2, 4, 3 * rows, HD), jnp.bfloat16),
+            pltpu.SMEM((2 * parts,), jnp.int32),
             pltpu.SMEM((2 * parts + 1,), jnp.int32),
             pltpu.SemaphoreType.DMA((2, 3 * parts)),
         ],
@@ -285,30 +269,54 @@
     part_rows = queries.shape[0]
     head_total = queries.shape[1] // HD // parts
     near_ids = nearby_ids(image_ids, parts, part_rows)
+    whole = [(0, head_total)]
+    halves = split_counts(head_total, HALF_SHARES)
     chunks = split_counts(head_total, CHUNK_SHARES)
-    last = parts - 1
-
-    jobs = [(flip, 0, head_total) for flip in range(last)]
-    jobs += [(last, first, count) for first, count in chunks]
-    packed = pack(arrays, parts, jobs)
-
-    def spread(piece):
-        return piece, swap_pairs(piece, "dp", 0), swap_pairs(piece, "dp", 1)
-
-    wide = [spread(packed[0])]
-    for flip in range(1, last):
-        wide.append(spread(swap_flipped(packed[flip], "tensor", flip)))
-    outs, narrow = None, []
-    for number, (first_head, count) in enumerate(chunks):
-        piece = packed[last + number]
-        if number < 2:
-            piece = hold(piece, [wide[max(1, last - 2 + number)][0]])
-        else:
-            piece = hold(piece, [narrow[number - 2][0]])
-        narrow.append(spread(swap_flipped(piece, "tensor", last)))
-    for number, (first_head, count) in enumerate(chunks):
-        groups = list(zip(*wide, narrow[number]))
-        outs = attend(near_ids, groups, outs, first_head, count)
+    last, middle = parts - 1, parts - 2
+
+    jobs = [(middle, *halves[0]), (0, *whole[0])]
+    jobs += [(flip, *whole[0]) for flip in range(1, middle)]
+    jobs += [(middle, *half) for half in halves[1:]]
+    jobs += [(last, *chunk) for chunk in chunks]
+    packed = dict(zip(jobs, pack(arrays, parts, jobs)))
+    crossed, spread = {(0, *whole[0]): packed[(0, *whole[0])]}, {}
+
+    def cross(job, after):
+        piece = hold(packed[job], after) if after else packed[job]
+        crossed[job] = swap_flipped(piece, "tensor", job[0])
+        return [piece]
+
+    def send(job, after):
+        held = hold(crossed[job], after) if after else crossed[job]
+        spread[job] = (held, swap_pairs(held, "dp", 0), swap_pairs(held, "dp", 1))
+
+    heavy = [(middle, *half) for half in halves] + [(last, *chunk) for chunk in chunks]
+    light = [(flip, *whole[0]) for flip in range(1, middle)]
+    order = [(0, *whole[0])] + heavy[:2] + light + heavy[2:]
+    cross(heavy[0], [])
+    for job in light:
+        cross(job, [])
+    for number, job in enumerate(order):
+        after = []
+        if number >= 1:
+            after.append(spread[order[number - 1]][1])
+        if number >= 2:
+            after.append(spread[order[number - 2]][2])
+        if job in heavy:
+            place = heavy.index(job)
+            if place + 1 < len(heavy) and heavy[place + 1] not in crossed:
+                after += cross(heavy[place + 1], [crossed[job]])
+        send(job, after)
+    outs = None
+    for first_head, count in chunks:
+        jobs_of = []
+        for flip in range(parts):
+            parts_of = halves if flip == middle else chunks if flip == last else whole
+            inside = [span for span in parts_of if span[0] <= first_head < sum(span)]
+            jobs_of.append((flip, *inside[0]))
+        groups = list(zip(*(spread[job] for job in jobs_of)))
+        offsets = [first_head - job[1] for job in jobs_of]
+        outs = attend(near_ids, groups, offsets, outs, first_head, count)
     return tuple(outs)
 
 

time: 148 us -> 130 us (0.88)
  the two profiles are of different devices: /device:TPU:15 before, /device:TPU:3 now
where the time goes in v10:
time: 130 us; the launch traced here: 129 us
  waiting for transfers between devices  57 us (44%)
  starting transfers between devices  38.3 us (29%)
  Pallas kernels  29.7 us (23%)
  local copies, waits for them, and re-layouts  2.17 us (2%)
    ppermute x6, waiting for transfers between devices, swap_flipped(): lax.ppermute(block, axis, [(i, i ^ flip) for i in range(lax.axis_size(axi...  44.8 us
    ppermute x14, starting transfers between devices, swap_pairs(): return lax.ppermute(block, axis, route)  28 us
    pallas_call x3, Pallas kernels, attend(): pl.pallas_call(functools.partial(attend_kernel, parts, part_rows, heads,...  26.5 us
    ppermute x14, waiting for transfers between devices, swap_pairs(): return lax.ppermute(block, axis, route)  12.2 us
    ppermute x6, starting transfers between devices, swap_flipped(): lax.ppermute(block, axis, [(i, i ^ flip) for i in range(lax.axis_size(axi...  10.3 us
    pallas_call x1, Pallas kernels, pack(): pl.pallas_call(functools.partial(pack_kernel, stride, jobs), out_shape=[j...  3.17 us
  transfers between devices with their start and end apart: 20, of which 8 were waited for; matrix products, arithmetic and copies ran while one was open for 1% of the time, Pallas kernels for 16%

profile of v10, /device:TPU:3, one launch (start us, length us, event | category | flops | bytes accessed | tf_op | source)
XLA Modules:
  0.0 128.8 jit_solution(9098672139557247418)
XLA Ops:
  0.6 3.2 %shard_map.84 = (bf16[4,64,768]{2,1,0:T(8,128)(2,1)}, bf16[4,64,1536]{2,1,0:T(8,128)(2,1)}, bf16[4,64,1536]{2,1,0:T(8,128)(2,1)}, bf16[4,64,768]{2,1,0:T(8,128)(...) custom-call(bf16[64,6144]{1,0:T(8,128)(2,1)} %refs_0_.1, ...), custom_call_target="tpu_custom_call" | custom-call | flops 1 | bytes 1 | tf_op jit(solution)/shard_map/pallas_call | solution.py:86
  3.8 0.7 collective-permute-start.3
  4.5 2.3 %collective-permute-start.1 = (bf16[4,64,768]{2,1,0:T(8,128)(2,1)}, bf16[4,64,768]{2,1,0:T(8,128)(2,1)}, u32[]{:S(2)}, u32[]{:S(2)}) collective-permute-start(bf16[4,64,768]{2,1,0:T(8,128)(2,1)} %get-tuple-element.22), channel_id=1, source_target_pairs={{0,2},{1,3},{2,0},{3,1},{4,6},{5,7},{6,4},{7,5},{8,10},{9,11},{10,... | collective-permute-start | bytes 1179656 | tf_op jit(solution)/shard_map/ppermute | solution.py:37
  6.9 3.3 %collective-permute-start.5 = (bf16[4,64,1536]{2,1,0:T(8,128)(2,1)}, bf16[4,64,1536]{2,1,0:T(8,128)(2,1)}, u32[]{:S(2)}, u32[]{:S(2)}) collective-permute-start(bf16[4,64,1536]{2,1,0:T(8,128)(2,1)} %get-tuple-element.19.refs_1_), channel_id=1, source_target_pairs={{4,8},{8,4},{12,16},{16,12},{20,24},{24,20},{5,9},{9,5},{13,17},{1... | collective-permute-start | bytes 2359304 | tf_op jit(solution)/shard_map/ppermute | solution.py:33
  10.2 14.7 %collective-permute-done.1.refs_1_.refs_0_ = bf16[4,64,768]{2,1,0:T(8,128)(2,1)} collective-permute-done((bf16[4,64,768]{2,1,0:T(8,128)(2,1)}, bf16[4,64,768]{2,1,0:T(8,128)(2,1)}, u32[]{:S(2)}, u32[]{:S(2)}) %collective-permute-start.1) | collective-permute-done | bytes 393248 | tf_op jit(solution)/shard_map/ppermute | solution.py:37
  24.9 3.9 %collective-permute-start = (bf16[4,64,1536]{2,1,0:T(8,128)(2,1)}, bf16[4,64,1536]{2,1,0:T(8,128)(2,1)}, u32[]{:S(2)}, u32[]{:S(2)}) collective-permute-start(bf16[4,64,1536]{2,1,0:T(8,128)(2,1)} %get-tuple-element.20), channel_id=1, source_target_pairs={{0,1},{1,0},{2,3},{3,2},{4,5},{5,4},{6,7},{7,6},{8,9},{9,8},{10,11... | collective-permute-start | bytes 2359304 | tf_op jit(solution)/shard_map/ppermute | solution.py:37
  28.8 1.0 collective-permute-start.4
  29.8 3.0 %collective-permute-start.7 = (bf16[4,64,768]{2,1,0:T(8,128)(2,1)}, bf16[4,64,768]{2,1,0:T(8,128)(2,1)}, u32[]{:S(2)}, u32[]{:S(2)}) collective-permute-start(bf16[4,64,768]{2,1,0:T(8,128)(2,1)} %shard_map.86.refs_3_), channel_id=1, source_target_pairs={{4,8},{8,4},{12,16},{16,12},{20,24},{24,20},{5,9},{9,5},{13,17},{1... | collective-permute-start | bytes 1179656 | tf_op jit(solution)/shard_map/ppermute | solution.py:33
  32.8 11.6 %collective-permute-done.2.refs_1_.refs_0_ = bf16[4,64,768]{2,1,0:T(8,128)(2,1)} collective-permute-done((bf16[4,64,768]{2,1,0:T(8,128)(2,1)}, bf16[4,64,768]{2,1,0:T(8,128)(2,1)}, u32[]{:S(2)}, u32[]{:S(2)}) %collective-permute-start.2) | collective-permute-done | bytes 393248 | tf_op jit(solution)/shard_map/ppermute | solution.py:37
  44.4 1.9 %collective-permute-start.6 = (bf16[4,64,768]{2,1,0:T(8,128)(2,1)}, bf16[4,64,768]{2,1,0:T(8,128)(2,1)}, u32[]{:S(2)}, u32[]{:S(2)}) collective-permute-start(bf16[4,64,768]{2,1,0:T(8,128)(2,1)} %shard_map.88.refs_3_), channel_id=1, source_target_pairs={{0,4},{4,0},{8,12},{12,8},{16,20},{20,16},{24,28},{28,24},{1,5},{5... | collective-permute-start | bytes 1179656 | tf_op jit(solution)/shard_map/ppermute | solution.py:33
  46.2 7.1 %collective-permute-done.refs_0_ = bf16[4,64,1536]{2,1,0:T(8,128)(2,1)} collective-permute-done((bf16[4,64,1536]{2,1,0:T(8,128)(2,1)}, bf16[4,64,1536]{2,1,0:T(8,128)(2,1)}, u32[]{:S(2)}, u32[]{:S(2)}) %collective-permute-start) | collective-permute-done | bytes 786464 | tf_op jit(solution)/shard_map/ppermute | solution.py:37
  53.4 1.3 %collective-permute-start.11 = (bf16[4,64,1536]{2,1,0:T(8,128)(2,1)}, bf16[4,64,1536]{2,1,0:T(8,128)(2,1)}, u32[]{:S(2)}, u32[]{:S(2)}) collective-permute-start(bf16[4,64,1536]{2,1,0:T(8,128)(2,1)} %shard_map.89.refs_2_), channel_id=1, source_target_pairs={{0,4},{4,0},{8,12},{12,8},{16,20},{20,16},{24,28},{28,24},{1,5},{5... | collective-permute-start | bytes 2359304 | tf_op jit(solution)/shard_map/ppermute | solution.py:33
  54.7 2.6 %collective-permute-start.8 = (bf16[4,64,768]{2,1,0:T(8,128)(2,1)}, bf16[4,64,768]{2,1,0:T(8,128)(2,1)}, u32[]{:S(2)}, u32[]{:S(2)}) collective-permute-start(bf16[4,64,768]{2,1,0:T(8,128)(2,1)} %shard_map.87.refs_3_), channel_id=1, source_target_pairs={{0,3},{1,2},{2,1},{3,0},{4,7},{5,6},{6,5},{7,4},{8,11},{9,10},{10,... | collective-permute-start | bytes 1179656 | tf_op jit(solution)/shard_map/ppermute | solution.py:37
  57.3 3.3 %collective-permute-start.12 = (bf16[4,64,768]{2,1,0:T(8,128)(2,1)}, bf16[4,64,768]{2,1,0:T(8,128)(2,1)}, u32[]{:S(2)}, u32[]{:S(2)}) collective-permute-start(bf16[4,64,768]{2,1,0:T(8,128)(2,1)} %shard_map.88.refs_3_), channel_id=1, source_target_pairs={{4,8},{8,4},{12,16},{16,12},{20,24},{24,20},{5,9},{9,5},{13,17},{1... | collective-permute-start | bytes 1179656 | tf_op jit(solution)/shard_map/ppermute | solution.py:33
  60.6 3.1 %collective-permute-start.14 = (bf16[4,64,1536]{2,1,0:T(8,128)(2,1)}, bf16[4,64,1536]{2,1,0:T(8,128)(2,1)}, u32[]{:S(2)}, u32[]{:S(2)}) collective-permute-start(bf16[4,64,1536]{2,1,0:T(8,128)(2,1)} %shard_map.89.refs_2_), channel_id=1, source_target_pairs={{4,8},{8,4},{12,16},{16,12},{20,24},{24,20},{5,9},{9,5},{13,17},{1... | collective-permute-start | bytes 2359304 | tf_op jit(solution)/shard_map/ppermute | solution.py:33
  63.8 3.8 %collective-permute-done.8.refs_1_.refs_0_ = bf16[4,64,768]{2,1,0:T(8,128)(2,1)} collective-permute-done((bf16[4,64,768]{2,1,0:T(8,128)(2,1)}, bf16[4,64,768]{2,1,0:T(8,128)(2,1)}, u32[]{:S(2)}, u32[]{:S(2)}) %collective-permute-start.8) | collective-permute-done | bytes 393248 | tf_op jit(solution)/shard_map/ppermute | solution.py:37
  67.6 4.2 %collective-permute-done.12.refs_2_.refs_11_ = bf16[4,64,768]{2,1,0:T(8,128)(2,1)} collective-permute-done((bf16[4,64,768]{2,1,0:T(8,128)(2,1)}, bf16[4,64,768]{2,1,0:T(8,128)(2,1)}, u32[]{:S(2)}, u32[]{:S(2)}) %collective-permute-start.12) | collective-permute-done | bytes 393248 | tf_op jit(solution)/shard_map/ppermute | solution.py:33
  71.8 3.3 %collective-permute-start.16 = (bf16[4,64,768]{2,1,0:T(8,128)(2,1)}, bf16[4,64,768]{2,1,0:T(8,128)(2,1)}, u32[]{:S(2)}, u32[]{:S(2)}) collective-permute-start(bf16[4,64,768]{2,1,0:T(8,128)(2,1)} %shard_map.92.refs_4_), channel_id=1, source_target_pairs={{4,8},{8,4},{12,16},{16,12},{20,24},{24,20},{5,9},{9,5},{13,17},{1... | collective-permute-start | bytes 1179656 | tf_op jit(solution)/shard_map/ppermute | solution.py:33
  75.1 0.8 collective-permute-start.9
  75.9 0.8 slice.3
  76.8 0.6 pad_add_fusion.refs_0_
  77.4 7.6 %collective-permute-done.9.refs_1_.refs_0_ = bf16[4,64,512]{2,1,0:T(8,128)(2,1)} collective-permute-done((bf16[4,64,512]{2,1,0:T(8,128)(2,1)}, bf16[4,64,512]{2,1,0:T(8,128)(2,1)}, u32[]{:S(2)}, u32[]{:S(2)}) %collective-permute-start.9) | collective-permute-done | bytes 262176 | tf_op jit(solution)/shard_map/ppermute | solution.py:37
  85.0 0.7 collective-permute-start.10
  85.7 2.9 %collective-permute-done.14.refs_2_.refs_10_ = bf16[4,64,1536]{2,1,0:T(8,128)(2,1)} collective-permute-done((bf16[4,64,1536]{2,1,0:T(8,128)(2,1)}, bf16[4,64,1536]{2,1,0:T(8,128)(2,1)}, u32[]{:S(2)}, u32[]{:S(2)}) %collective-permute-start.14) | collective-permute-done | bytes 786464 | tf_op jit(solution)/shard_map/ppermute | solution.py:33
  88.7 3.3 %collective-permute-start.19 = (bf16[4,64,512]{2,1,0:T(8,128)(2,1)}, bf16[4,64,512]{2,1,0:T(8,128)(2,1)}, u32[]{:S(2)}, u32[]{:S(2)}) collective-permute-start(bf16[4,64,512]{2,1,0:T(8,128)(2,1)} %shard_map.93.refs_4_), channel_id=1, source_target_pairs={{4,8},{8,4},{12,16},{16,12},{20,24},{24,20},{5,9},{9,5},{13,17},{1... | collective-permute-start | bytes 786440 | tf_op jit(solution)/shard_map/ppermute | solution.py:33
  92.0 5.0 %collective-permute-done.16.refs_2_.refs_12_ = bf16[4,64,768]{2,1,0:T(8,128)(2,1)} collective-permute-done((bf16[4,64,768]{2,1,0:T(8,128)(2,1)}, bf16[4,64,768]{2,1,0:T(8,128)(2,1)}, u32[]{:S(2)}, u32[]{:S(2)}) %collective-permute-start.16) | collective-permute-done | bytes 393248 | tf_op jit(solution)/shard_map/ppermute | solution.py:33
  97.1 12.0 %shard_map.95 = (bf16[256,1536]{1,0:T(8,128)(2,1)}, bf16[256,1536]{1,0:T(8,128)(2,1)}, bf16[256,1536]{1,0:T(8,128)(2,1)}, bf16[256,1536]{1,0:T(8,128)(2,1)}) custom-call(s32[3,4]{1,0:T(4,128)} %pad_add_fusion.refs_0_, bf16[4,64,1536]{2,1,0:T(8,128)(2,1)} %get-tuple-element.19.refs_1_, bf16[4,64,1536]{2,1,0:T(8,128)(2,1)} %shard_map.89.refs_2_, ...), custom_call_target="tpu_custom_call" | custom-call | flops 8999999488 | bytes 1 | tf_op jit(solution)/shard_map/pallas_call | solution.py:242
  109.1 0.6 copy-done
  109.8 3.6 %collective-permute-start.18 = (bf16[4,64,256]{2,1,0:T(8,128)(2,1)}, bf16[4,64,256]{2,1,0:T(8,128)(2,1)S(1)}, u32[]{:S(2)}, u32[]{:S(2)}) collective-permute-start(bf16[4,64,256]{2,1,0:T(8,128)(2,1)} %shard_map.94.refs_4_), channel_id=1, source_target_pairs={{4,8},{8,4},{12,16},{16,12},{20,24},{24,20},{5,9},{9,5},{13,17},{1... | collective-permute-start | bytes 393224 | tf_op jit(solution)/shard_map/ppermute | solution.py:33
  113.4 8.9 %shard_map.96 = (bf16[256,1536]{1,0:T(8,128)(2,1)}, bf16[256,1536]{1,0:T(8,128)(2,1)}, bf16[256,1536]{1,0:T(8,128)(2,1)}, bf16[256,1536]{1,0:T(8,128)(2,1)}) custom-call(s32[3,4]{1,0:T(4,128)} %pad_add_fusion.refs_0_, bf16[4,64,1536]{2,1,0:T(8,128)(2,1)} %get-tuple-element.19.refs_1_, ...), custom_call_target="tpu_custom_call", output_to_operand_aliasing={{0}: (13, {}), {1}: (14, {}), {2}: (15, {}), {3}: (16, {})} | custom-call | flops 6000000000 | bytes 1 | tf_op jit(solution)/shard_map/pallas_call | solution.py:242
  122.4 0.6 copy-done.1
  123.0 5.6 %shard_map.97 = (bf16[256,1536]{1,0:T(8,128)(2,1)}, bf16[256,1536]{1,0:T(8,128)(2,1)}, bf16[256,1536]{1,0:T(8,128)(2,1)}, bf16[256,1536]{1,0:T(8,128)(2,1)}) custom-call(s32[3,4]{1,0:T(4,128)} %pad_add_fusion.refs_0_, bf16[4,64,1536]{2,1,0:T(8,128)(2,1)} %get-tuple-element.19.refs_1_, ...), custom_call_target="tpu_custom_call", output_to_operand_aliasing={{0}: (13, {}), {1}: (14, {}), {2}: (15, {}), {3}: (16, {})} | custom-call | flops 3000000000 | bytes 1 | tf_op jit(solution)/shard_map/pallas_call | solution.py:242
  (29 shorter events, 0.3 us)
Async XLA Ops:
  3.8 25.0 %collective-permute-start.3 = (bf16[4,64,1536]{2,1,0:T(8,128)(2,1)}, bf16[4,64,1536]{2,1,0:T(8,128)(2,1)}, u32[]{:S(2)}, u32[]{:S(2)}) collective-permute-start(bf16[4,64,1536]{2,1,0:T(8,128)(2,1)} %get-tuple-element.19.refs_1_), channel_id=1, source_target_pairs={{0,4},{4,0},{8,12},{12,8},{16,20},{20,16},{24,28},{28,24},{1,5},{5... | collective-permute-start | bytes 2359304 | tf_op jit(solution)/shard_map/ppermute | solution.py:33
  4.5 20.3 %collective-permute-start.1 = (bf16[4,64,768]{2,1,0:T(8,128)(2,1)}, bf16[4,64,768]{2,1,0:T(8,128)(2,1)}, u32[]{:S(2)}, u32[]{:S(2)}) collective-permute-start(bf16[4,64,768]{2,1,0:T(8,128)(2,1)} %get-tuple-element.22), channel_id=1, source_target_pairs={{0,2},{1,3},{2,0},{3,1},{4,6},{5,7},{6,4},{7,5},{8,10},{9,11},{10,... | collective-permute-start | bytes 1179656 | tf_op jit(solution)/shard_map/ppermute | solution.py:37
  6.9 37.5 %collective-permute-start.5 = (bf16[4,64,1536]{2,1,0:T(8,128)(2,1)}, bf16[4,64,1536]{2,1,0:T(8,128)(2,1)}, u32[]{:S(2)}, u32[]{:S(2)}) collective-permute-start(bf16[4,64,1536]{2,1,0:T(8,128)(2,1)} %get-tuple-element.19.refs_1_), channel_id=1, source_target_pairs={{4,8},{8,4},{12,16},{16,12},{20,24},{24,20},{5,9},{9,5},{13,17},{1... | collective-permute-start | bytes 2359304 | tf_op jit(solution)/shard_map/ppermute | solution.py:33
  24.9 19.5 %collective-permute-start.2 = (bf16[4,64,768]{2,1,0:T(8,128)(2,1)}, bf16[4,64,768]{2,1,0:T(8,128)(2,1)}, u32[]{:S(2)}, u32[]{:S(2)}) collective-permute-start(bf16[4,64,768]{2,1,0:T(8,128)(2,1)} %shard_map.85.refs_2_), channel_id=1, source_target_pairs={{0,2},{1,3},{2,0},{3,1},{4,6},{5,7},{6,4},{7,5},{8,10},{9,11},{10,... | collective-permute-start | bytes 1179656 | tf_op jit(solution)/shard_map/ppermute | solution.py:37
  24.9 28.5 %collective-permute-start = (bf16[4,64,1536]{2,1,0:T(8,128)(2,1)}, bf16[4,64,1536]{2,1,0:T(8,128)(2,1)}, u32[]{:S(2)}, u32[]{:S(2)}) collective-permute-start(bf16[4,64,1536]{2,1,0:T(8,128)(2,1)} %get-tuple-element.20), channel_id=1, source_target_pairs={{0,1},{1,0},{2,3},{3,2},{4,5},{5,4},{6,7},{7,6},{8,9},{9,8},{10,11... | collective-permute-start | bytes 2359304 | tf_op jit(solution)/shard_map/ppermute | solution.py:37
  28.8 15.6 %collective-permute-start.4 = (bf16[4,64,768]{2,1,0:T(8,128)(2,1)}, bf16[4,64,768]{2,1,0:T(8,128)(2,1)}, u32[]{:S(2)}, u32[]{:S(2)}) collective-permute-start(bf16[4,64,768]{2,1,0:T(8,128)(2,1)} %shard_map.86.refs_3_), channel_id=1, source_target_pairs={{0,4},{4,0},{8,12},{12,8},{16,20},{20,16},{24,28},{28,24},{1,5},{5... | collective-permute-start | bytes 1179656 | tf_op jit(solution)/shard_map/ppermute | solution.py:33
  29.8 23.6 %collective-permute-start.7 = (bf16[4,64,768]{2,1,0:T(8,128)(2,1)}, bf16[4,64,768]{2,1,0:T(8,128)(2,1)}, u32[]{:S(2)}, u32[]{:S(2)}) collective-permute-start(bf16[4,64,768]{2,1,0:T(8,128)(2,1)} %shard_map.86.refs_3_), channel_id=1, source_target_pairs={{4,8},{8,4},{12,16},{16,12},{20,24},{24,20},{5,9},{9,5},{13,17},{1... | collective-permute-start | bytes 1179656 | tf_op jit(solution)/shard_map/ppermute | solution.py:33
  44.4 9.0 %collective-permute-start.6 = (bf16[4,64,768]{2,1,0:T(8,128)(2,1)}, bf16[4,64,768]{2,1,0:T(8,128)(2,1)}, u32[]{:S(2)}, u32[]{:S(2)}) collective-permute-start(bf16[4,64,768]{2,1,0:T(8,128)(2,1)} %shard_map.88.refs_3_), channel_id=1, source_target_pairs={{0,4},{4,0},{8,12},{12,8},{16,20},{20,16},{24,28},{28,24},{1,5},{5... | collective-permute-start | bytes 1179656 | tf_op jit(solution)/shard_map/ppermute | solution.py:33
  53.4 18.4 %collective-permute-start.11 = (bf16[4,64,1536]{2,1,0:T(8,128)(2,1)}, bf16[4,64,1536]{2,1,0:T(8,128)(2,1)}, u32[]{:S(2)}, u32[]{:S(2)}) collective-permute-start(bf16[4,64,1536]{2,1,0:T(8,128)(2,1)} %shard_map.89.refs_2_), channel_id=1, source_target_pairs={{0,4},{4,0},{8,12},{12,8},{16,20},{20,16},{24,28},{28,24},{1,5},{5... | collective-permute-start | bytes 2359304 | tf_op jit(solution)/shard_map/ppermute | solution.py:33
  54.7 12.9 %collective-permute-start.8 = (bf16[4,64,768]{2,1,0:T(8,128)(2,1)}, bf16[4,64,768]{2,1,0:T(8,128)(2,1)}, u32[]{:S(2)}, u32[]{:S(2)}) collective-permute-start(bf16[4,64,768]{2,1,0:T(8,128)(2,1)} %shard_map.87.refs_3_), channel_id=1, source_target_pairs={{0,3},{1,2},{2,1},{3,0},{4,7},{5,6},{6,5},{7,4},{8,11},{9,10},{10,... | collective-permute-start | bytes 1179656 | tf_op jit(solution)/shard_map/ppermute | solution.py:37
  57.3 14.5 %collective-permute-start.12 = (bf16[4,64,768]{2,1,0:T(8,128)(2,1)}, bf16[4,64,768]{2,1,0:T(8,128)(2,1)}, u32[]{:S(2)}, u32[]{:S(2)}) collective-permute-start(bf16[4,64,768]{2,1,0:T(8,128)(2,1)} %shard_map.88.refs_3_), channel_id=1, source_target_pairs={{4,8},{8,4},{12,16},{16,12},{20,24},{24,20},{5,9},{9,5},{13,17},{1... | collective-permute-start | bytes 1179656 | tf_op jit(solution)/shard_map/ppermute | solution.py:33
  60.6 28.0 %collective-permute-start.14 = (bf16[4,64,1536]{2,1,0:T(8,128)(2,1)}, bf16[4,64,1536]{2,1,0:T(8,128)(2,1)}, u32[]{:S(2)}, u32[]{:S(2)}) collective-permute-start(bf16[4,64,1536]{2,1,0:T(8,128)(2,1)} %shard_map.89.refs_2_), channel_id=1, source_target_pairs={{4,8},{8,4},{12,16},{16,12},{20,24},{24,20},{5,9},{9,5},{13,17},{1... | collective-permute-start | bytes 2359304 | tf_op jit(solution)/shard_map/ppermute | solution.py:33
  71.8 16.9 %collective-permute-start.13 = (bf16[4,64,768]{2,1,0:T(8,128)(2,1)}, bf16[4,64,768]{2,1,0:T(8,128)(2,1)}, u32[]{:S(2)}, u32[]{:S(2)}) collective-permute-start(bf16[4,64,768]{2,1,0:T(8,128)(2,1)} %shard_map.92.refs_4_), channel_id=1, source_target_pairs={{0,4},{4,0},{8,12},{12,8},{16,20},{20,16},{24,28},{28,24},{1,5},{5... | collective-permute-start | bytes 1179656 | tf_op jit(solution)/shard_map/ppermute | solution.py:33
  71.8 25.3 %collective-permute-start.16 = (bf16[4,64,768]{2,1,0:T(8,128)(2,1)}, bf16[4,64,768]{2,1,0:T(8,128)(2,1)}, u32[]{:S(2)}, u32[]{:S(2)}) collective-permute-start(bf16[4,64,768]{2,1,0:T(8,128)(2,1)} %shard_map.92.refs_4_), channel_id=1, source_target_pairs={{4,8},{8,4},{12,16},{16,12},{20,24},{24,20},{5,9},{9,5},{13,17},{1... | collective-permute-start | bytes 1179656 | tf_op jit(solution)/shard_map/ppermute | solution.py:33
  75.1 9.9 %collective-permute-start.9 = (bf16[4,64,512]{2,1,0:T(8,128)(2,1)}, bf16[4,64,512]{2,1,0:T(8,128)(2,1)}, u32[]{:S(2)}, u32[]{:S(2)}) collective-permute-start(bf16[4,64,512]{2,1,0:T(8,128)(2,1)} %shard_map.90.refs_3_), channel_id=1, source_target_pairs={{0,3},{1,2},{2,1},{3,0},{4,7},{5,6},{6,5},{7,4},{8,11},{9,10},{10,... | collective-permute-start | bytes 786440 | tf_op jit(solution)/shard_map/ppermute | solution.py:37
  85.0 24.1 %collective-permute-start.10 = (bf16[4,64,256]{2,1,0:T(8,128)(2,1)}, bf16[4,64,256]{2,1,0:T(8,128)(2,1)S(1)}, u32[]{:S(2)}, u32[]{:S(2)}) collective-permute-start(bf16[4,64,256]{2,1,0:T(8,128)(2,1)} %shard_map.91.refs_3_), channel_id=1, source_target_pairs={{0,3},{1,2},{2,1},{3,0},{4,7},{5,6},{6,5},{7,4},{8,11},{9,10},{10,... | collective-permute-start | bytes 393224 | tf_op jit(solution)/shard_map/ppermute | solution.py:37
  88.7 24.8 %collective-permute-start.19 = (bf16[4,64,512]{2,1,0:T(8,128)(2,1)}, bf16[4,64,512]{2,1,0:T(8,128)(2,1)}, u32[]{:S(2)}, u32[]{:S(2)}) collective-permute-start(bf16[4,64,512]{2,1,0:T(8,128)(2,1)} %shard_map.93.refs_4_), channel_id=1, source_target_pairs={{4,8},{8,4},{12,16},{16,12},{20,24},{24,20},{5,9},{9,5},{13,17},{1... | collective-permute-start | bytes 786440 | tf_op jit(solution)/shard_map/ppermute | solution.py:33
  91.9 17.2 %collective-permute-start.15 = (bf16[4,64,512]{2,1,0:T(8,128)(2,1)}, bf16[4,64,512]{2,1,0:T(8,128)(2,1)}, u32[]{:S(2)}, u32[]{:S(2)}) collective-permute-start(bf16[4,64,512]{2,1,0:T(8,128)(2,1)} %shard_map.93.refs_4_), channel_id=1, source_target_pairs={{0,4},{4,0},{8,12},{12,8},{16,20},{20,16},{24,28},{28,24},{1,5},{5... | collective-permute-start | bytes 786440 | tf_op jit(solution)/shard_map/ppermute | solution.py:33
  109.1 0.7 copy-start
  109.8 12.6 %collective-permute-start.18 = (bf16[4,64,256]{2,1,0:T(8,128)(2,1)}, bf16[4,64,256]{2,1,0:T(8,128)(2,1)S(1)}, u32[]{:S(2)}, u32[]{:S(2)}) collective-permute-start(bf16[4,64,256]{2,1,0:T(8,128)(2,1)} %shard_map.94.refs_4_), channel_id=1, source_target_pairs={{4,8},{8,4},{12,16},{16,12},{20,24},{24,20},{5,9},{9,5},{13,17},{1... | collective-permute-start | bytes 393224 | tf_op jit(solution)/shard_map/ppermute | solution.py:33
  113.4 9.0 %collective-permute-start.17 = (bf16[4,64,256]{2,1,0:T(8,128)(2,1)}, bf16[4,64,256]{2,1,0:T(8,128)(2,1)}, u32[]{:S(2)}, u32[]{:S(2)}) collective-permute-start(bf16[4,64,256]{2,1,0:T(8,128)(2,1)} %shard_map.94.refs_4_), channel_id=1, source_target_pairs={{0,4},{4,0},{8,12},{12,8},{16,20},{20,16},{24,28},{28,24},{1,5},{5... | collective-permute-start | bytes 393224 | tf_op jit(solution)/shard_map/ppermute | solution.py:33
  122.3 0.7 copy-start.1

commit v11 on v10

v11 whole, which is shorter than its diff:
```python
import functools
import math

import jax
import jax.numpy as jnp
from jax import lax
from jax.experimental import pallas as pl
from jax.experimental.pallas import tpu as pltpu
from jax.sharding import PartitionSpec as P

HD = 128
SCALE = 1.0 / math.sqrt(HD)
EXP2_SCALE = SCALE * math.log2(math.e)
MASKED = -1e30
GROUPS = ((8,), (2, 2))
VMEM_LIMIT = 64 * 1024 * 1024 - 256 * 1024
ATTEND_FLOPS = 1_500_000_000
SMALL_COST = pl.CostEstimate(flops=1, bytes_accessed=1, transcendentals=0)


def split_counts(total, shares):
    whole = sum(shares)
    edges = [round(total * sum(shares[:i]) / whole) for i in range(len(shares) + 1)]
    return [(a, b - a) for a, b in zip(edges[:-1], edges[1:]) if b > a]


def swap_pairs(block, axis, first):
    count = lax.axis_size(axis)
    route = []
    for low in range(first, count - 1, 2):
        route += [(low, low + 1), (low + 1, low)]
    return lax.ppermute(block, axis, route)


def swap_flipped(block, axis, flip):
    return lax.ppermute(block, axis, [(i, i ^ flip) for i in range(lax.axis_size(axis))])


def nearby_ids(image_ids, parts, part_rows):
    shard = lax.axis_index("dp")
    padded = jnp.pad(image_ids[::part_rows], (parts, parts), constant_values=-1)
    odd = lax.rem(shard, 2)

    def ids_of(other):
        return lax.dynamic_slice_in_dim(padded, (other + 1) * parts, parts)

    return jnp.stack((ids_of(shard), ids_of(shard + 1 - 2 * odd), ids_of(shard - 1 + 2 * odd)))


def columns(array, part, stride, first, width):
    start = pl.multiple_of(part * stride + first, HD)
    return array.at[:, pl.ds(start, width)]


def pack_kernel(stride, jobs, *refs):
    arrays, packed, (stage, in_sems, out_sems) = refs[:4], refs[4:-3], refs[-3:]
    me = lax.axis_index("tensor")
    loads, stores = [], []
    for number, (flip, first, count) in enumerate(jobs):
        for index, array in enumerate(arrays):
            load = pltpu.make_async_copy(
                columns(array, me ^ flip, stride, first * HD, count * HD),
                stage.at[flip, index, :, pl.ds(first * HD, count * HD)],
                in_sems.at[number * 4 + index],
            )
            load.start()
            loads.append(load)
    for number, (flip, first, count) in enumerate(jobs):
        for load in loads[number * 4 : number * 4 + 4]:
            load.wait()
        store = pltpu.make_async_copy(
            stage.at[flip, :, :, pl.ds(first * HD, count * HD)],
            packed[number],
            out_sems.at[number],
        )
        store.start()
        stores.append(store)
    for store in stores:
        store.wait()


def pack(arrays, parts, jobs):
    rows, total = arrays[0].shape
    stride = total // parts
    return pl.pallas_call(
        functools.partial(pack_kernel, stride, jobs),
        out_shape=[
            jax.ShapeDtypeStruct((4, rows, count * HD), jnp.bfloat16) for _, _, count in jobs
        ],
        in_specs=[pl.BlockSpec(memory_space=pl.ANY)] * 4,
        out_specs=[pl.BlockSpec(memory_space=pl.ANY)] * len(jobs),
        scratch_shapes=[
            pltpu.VMEM((parts, 4, rows, stride), jnp.bfloat16),
            pltpu.SemaphoreType.DMA((4 * len(jobs),)),
            pltpu.SemaphoreType.DMA((len(jobs),)),
        ],
        compiler_params=pltpu.CompilerParams(vmem_limit_bytes=VMEM_LIMIT),
        cost_estimate=SMALL_COST,
    )(*arrays)


def join_kernel(pieces, *refs):
    received, (joined, stage, in_sems, out_sems) = refs[:pieces], refs[-4:]
    loads, stores = [], []
    for piece in range(pieces):
        load = pltpu.make_async_copy(received[piece], stage.at[piece], in_sems.at[piece])
        load.start()
        loads.append(load)
    for piece in range(pieces):
        loads[piece].wait()
        store = pltpu.make_async_copy(stage.at[piece], joined.at[piece], out_sems.at[piece])
        store.start()
        stores.append(store)
    for store in stores:
        store.wait()


def join(received, after):
    pieces = len(received)
    shape = (pieces,) + received[0].shape
    return pl.pallas_call(
        functools.partial(join_kernel, pieces),
        out_shape=jax.ShapeDtypeStruct(shape, jnp.bfloat16),
        in_specs=[pl.BlockSpec(memory_space=pl.ANY)] * (pieces + len(after)),
        out_specs=pl.BlockSpec(memory_space=pl.ANY),
        scratch_shapes=[
            pltpu.VMEM(shape, jnp.bfloat16),
            pltpu.SemaphoreType.DMA((pieces,)),
            pltpu.SemaphoreType.DMA((pieces,)),
        ],
        compiler_params=pltpu.CompilerParams(vmem_limit_bytes=VMEM_LIMIT),
        cost_estimate=SMALL_COST,
    )(*received, *after)


def hold(array, after):
    return pl.pallas_call(
        lambda *refs: None,
        out_shape=jax.ShapeDtypeStruct(array.shape, array.dtype),
        in_specs=[pl.BlockSpec(memory_space=pl.ANY)] * (1 + len(after)),
        out_specs=pl.BlockSpec(memory_space=pl.ANY),
        input_output_aliases={0: 0},
        compiler_params=pltpu.CompilerParams(vmem_limit_bytes=VMEM_LIMIT),
        cost_estimate=SMALL_COST,
    )(array, *after)


def dot_nt(a, b):
    return lax.dot_general(a, b, (((1,), (1,)), ((), ())), preferred_element_type=jnp.float32)


def dot_tn(a, b):
    return lax.dot_general(a, b, (((0,), (0,)), ((), ())), preferred_element_type=jnp.float32)


def dot_nn(a, b):
    return jnp.dot(a, b, preferred_element_type=jnp.float32)


def attend_head(values_of, slot_ids, lane_ids, part_rows, rows):
    queries, keys, values, grads = values_of
    size = keys.shape[0]
    slots = size // part_rows
    grad_k = grad_v = None

    def per_slot(array):
        return [array[slot * part_rows : (slot + 1) * part_rows] for slot in range(slots)]

    def over_slots(reduce, combine, arrays):
        total = reduce(arrays[0], axis=0, keepdims=True)
        for array in arrays[1:]:
            total = combine(total, reduce(array, axis=0, keepdims=True))
        return total

    for start in range(0, size, rows):
        tile = slice(start, start + rows)
        scores = [
            part + jnp.where(lane_ids[:, tile] == slot_id, 0.0, MASKED)
            for part, slot_id in zip(per_slot(dot_nt(keys, queries[tile])), slot_ids)
        ]
        row_max = over_slots(jnp.max, jnp.maximum, scores)
        weights = [jnp.exp2((part - row_max) * EXP2_SCALE) for part in scores]
        inverse = 1.0 / over_slots(jnp.sum, jnp.add, weights)
        probs = [part * inverse for part in weights]
        grad_probs = per_slot(dot_nt(values, grads[tile]))
        inner = over_slots(jnp.sum, jnp.add, [p * g for p, g in zip(probs, grad_probs)])
        low = jnp.concatenate([p.astype(jnp.bfloat16) for p in probs])
        grad_scores = jnp.concatenate(
            [(p * (g - inner)).astype(jnp.bfloat16) for p, g in zip(probs, grad_probs)]
        )
        tile_v = dot_nn(low[:rows], grads[tile])
        tile_k = dot_nn(grad_scores[:rows], queries[tile])
        if start == 0:
            attended = dot_tn(low, values)
            grad_q = dot_tn(grad_scores, keys)
            grad_k, grad_v = tile_k, tile_v
        else:
            grad_k, grad_v = grad_k + tile_k, grad_v + tile_v
    return attended, grad_q * SCALE, grad_k * SCALE, grad_v


def attend_kernel(parts, part_rows, steps, width, offsets, has_outs, *refs):
    image_ids, mine, sides = refs[0], refs[1:4], (refs[4:7], refs[7:10])
    refs = refs[10 + (4 if has_outs else 0) :]
    outs, (window, lane_ids, slot_of, table, sems) = refs[:4], refs[4:]
    rows = parts * part_rows
    most = 3 * rows
    last = parts - 1
    me = lax.axis_index("tensor")
    step = pl.program_id(0)

    def copy_of(group, flip, number, place, sem):
        kind = 0 if flip == 0 else 2 if flip == last else 1
        buffer = lax.rem(number, 2)
        start = pl.multiple_of(place * part_rows, part_rows)
        column = pl.multiple_of(number * width + offsets[kind] * HD, HD)
        source = group[kind].at[flip - 1] if kind == 1 else group[kind]
        return pltpu.make_async_copy(
            source.at[:, :, pl.ds(column, width)],
            window.at[buffer, :, pl.ds(start, part_rows), :],
            sems.at[buffer, sem],
        )

    def copies(number, act):
        for flip in range(parts):
            act(copy_of(mine, flip, number, me ^ flip, flip))
        for source in range(2 * parts):
            slot = slot_of[source]

            @pl.when(slot >= 0)
            def _():
                group = sides[source // parts]
                act(copy_of(group, source % parts, number, parts + slot, parts + source))

    @pl.when(step == 0)
    def _():
        count = jnp.int32(0)
        for slot in range(2 * parts):
            table[slot] = -2
        for source in range(2 * parts):
            side, flip = 1 + source // parts, source % parts
            other_id = image_ids[side, me ^ flip]
            shared = other_id == image_ids[0, 0]
            for part in range(1, parts):
                shared = shared | (other_id == image_ids[0, part])
            slot_of[source] = jnp.where(shared, count, -1)
            table[count] = jnp.where(shared, other_id, -2)
            count = count + shared.astype(jnp.int32)
        table[2 * parts] = count
        window[:, :, rows:] = jnp.zeros((2, 4, most - rows, width), window.dtype)
        copies(0, lambda copy: copy.start())
        place = lax.broadcasted_iota(jnp.int32, (8, most), 1)
        ids = jnp.full((8, most), -2, jnp.int32)
        for slot in range(3 * parts):
            slot_id = image_ids[0, slot] if slot < parts else table[slot - parts]
            inside = (place >= slot * part_rows) & (place < (slot + 1) * part_rows)
            ids = jnp.where(inside, slot_id, ids)
        lane_ids[...] = ids

    @pl.when(step + 1 < steps)
    def _():
        copies(step + 1, lambda copy: copy.start())

    copies(step, lambda copy: copy.wait())
    count = table[2 * parts]
    buffer = lax.rem(step, 2)
    for size in range(rows, most + 1, rows):
        slots = (size - rows) // part_rows

        @pl.when((count <= slots) & (count > slots - parts))
        def _():
            slot_ids = [image_ids[0, slot] for slot in range(parts)]
            slot_ids += [table[slot] for slot in range(slots)]
            for start in range(0, width, HD):
                head = slice(start, start + HD)
                values_of = [window[buffer, index, :size, head] for index in range(4)]
                results = attend_head(values_of, slot_ids, lane_ids[0:1], part_rows, rows)
                for out, result in zip(outs, results):
                    out[:, head] = result.astype(jnp.bfloat16)


def attend(image_ids, groups, offsets, outs, first_head, heads):
    _, part_rows, total = groups[0][0].shape
    parts = groups[0][1].shape[0] + 2
    rows = parts * part_rows
    width = HD * math.gcd(2, math.gcd(first_head, heads))
    steps = heads * HD // width
    first_block = first_head * HD // width
    out_spec = pl.BlockSpec((rows, width), lambda s: (0, s + first_block))
    has_outs = outs is not None
    pieces = [piece for group in groups for piece in group]
    aliases = {1 + len(pieces) + i: i for i in range(4)} if has_outs else {}
    return pl.pallas_call(
        functools.partial(
            attend_kernel, parts, part_rows, steps, width, offsets, has_outs
        ),
        grid=(steps,),
        out_shape=[jax.ShapeDtypeStruct((rows, total), jnp.bfloat16)] * 4,
        in_specs=[pl.BlockSpec(memory_space=pltpu.SMEM)]
        + [pl.BlockSpec(memory_space=pl.ANY)] * (len(pieces) + (4 if has_outs else 0)),
        out_specs=[out_spec] * 4,
        scratch_shapes=[
            pltpu.VMEM((2, 4, 3 * rows, width), jnp.bfloat16),
            pltpu.VMEM((8, 3 * rows), jnp.int32),
            pltpu.SMEM((2 * parts,), jnp.int32),
            pltpu.SMEM((2 * parts + 1,), jnp.int32),
            pltpu.SemaphoreType.DMA((2, 3 * parts)),
        ],
        input_output_aliases=aliases,
        compiler_params=pltpu.CompilerParams(
            dimension_semantics=("arbitrary",), vmem_limit_bytes=VMEM_LIMIT
        ),
        cost_estimate=pl.CostEstimate(
            flops=heads * ATTEND_FLOPS, bytes_accessed=1, transcendentals=0
        ),
    )(image_ids, *pieces, *(outs or ()))


def shards(queries, key_vectors, value_vectors, grad_output, image_ids):
    arrays = (queries, key_vectors, value_vectors, grad_output)
    parts = lax.axis_size("tensor")
    part_rows = queries.shape[0]
    head_total = queries.shape[1] // HD // parts
    near_ids = nearby_ids(image_ids, parts, part_rows)
    last = parts - 1
    spans = split_counts(head_total, [sum(shares) for shares in GROUPS])
    groups = []
    for (start, count), shares in zip(spans, GROUPS):
        groups.append([(start + first, size) for first, size in split_counts(count, shares)])

    jobs = []
    for span, chunks in zip(spans, groups):
        jobs += [(flip, *span) for flip in range(last - 1, 0, -1)]
        jobs += [(last, *chunk) for chunk in chunks]
    jobs.insert(last - 1, (0, 0, head_total))
    packed = dict(zip(jobs, pack(arrays, parts, jobs)))

    steps = []
    for span, chunks in zip(spans, groups):
        steps.append([(flip, *span) for flip in range(1, last)])
        steps += [[(last, *chunk)] for chunk in chunks]

    def cross(step, after):
        held = [hold(packed[job], after) if after else packed[job] for job in step]
        return held, [swap_flipped(piece, "tensor", job[0]) for job, piece in zip(step, held)]

    def spread(piece):
        return piece, swap_pairs(piece, "dp", 0), swap_pairs(piece, "dp", 1)

    _, crossed = cross(steps[0], [])
    sent = [spread(packed[(0, 0, head_total)])]
    outs, joined, number = None, None, 0
    for span, chunks in zip(spans, groups):
        for place in range(1 + len(chunks)):
            after = [sent[-1][1]] + [earlier[2] for earlier in sent[-2:-1]]
            received = crossed
            number += 1
            if number < len(steps):
                held, crossed = cross(steps[number], [received[-1]])
                after += held
            if place == 0:
                joined = spread(join(received, after))
                sent.append(joined)
                continue
            if outs is not None and place == len(chunks):
                after.append(outs[0])
            piece = spread(hold(received[0], after))
            sent.append(piece)
            first_head, count = chunks[place - 1]
            offsets = (first_head, first_head - span[0], 0)
            outs = attend(
                near_ids, list(zip(sent[0], joined, piece)), offsets, outs, first_head, count
            )
    return tuple(outs)


def solution(mesh):
    return jax.shard_map(
        shards,
        mesh=mesh,
        in_specs=(
            P(("dp", "tensor"), None),
            P(("dp", "tensor"), None),
            P(("dp", "tensor"), None),
            P(("dp", "tensor"), None),
            P(),
        ),
        out_specs=(P("dp", "tensor"), P("dp", "tensor"), P("dp", "tensor"), P("dp", "tensor")),
        check_vma=False,
    )
```

time: 130 us -> 136 us (1.046)
  starting transfers between devices: 38.3 us -> 42 us
  Pallas kernels: 29.7 us -> 32.3 us
    ppermute x6 -> x7, starting transfers between devices: 10.3 us -> 18.6 us  [swap_flipped(): lax.ppermute(block, axis, [(i, i ^ flip) for i in range(lax.axis_size(axi...]
    ppermute x14 -> x12, starting transfers between devices: 28 us -> 23.4 us  [swap_pairs(): return lax.ppermute(block, axis, route)]
    ppermute x14 -> x12, waiting for transfers between devices: 12.2 us -> 8.02 us  [swap_pairs(): return lax.ppermute(block, axis, route)]
    ppermute x6 -> x7, waiting for transfers between devices: 44.8 us -> 47.7 us  [swap_flipped(): lax.ppermute(block, axis, [(i, i ^ flip) for i in range(lax.axis_size(axi...]
    pallas_call x3 -> x5, Pallas kernels: 26.5 us -> 29.1 us  [the longest x3 25.3 us: attend(): pl.pallas_call(functools.partial(attend_kernel, parts, part_rows, steps,...]
  transfers between devices with their start and end apart: 20 -> 19, of which waited for: 8 -> 6; matrix products, arithmetic and copies ran while one was open for 1% -> 1% of each run, Pallas kernels for 16% -> 16%
where the time goes in v11:
time: 136 us; the launch traced here: 134 us
  waiting for transfers between devices  55.8 us (41%)
  starting transfers between devices  42 us (31%)
  Pallas kernels  32.3 us (24%)
  local copies, waits for them, and re-layouts  2.18 us (2%)
    ppermute x7, waiting for transfers between devices, swap_flipped(): lax.ppermute(block, axis, [(i, i ^ flip) for i in range(lax.axis_size(axi...  47.7 us
    pallas_call x3, Pallas kernels, attend(): pl.pallas_call(functools.partial(attend_kernel, parts, part_rows, steps,...  25.3 us
    ppermute x12, starting transfers between devices, swap_pairs(): return lax.ppermute(block, axis, route)  23.4 us
    ppermute x7, starting transfers between devices, swap_flipped(): lax.ppermute(block, axis, [(i, i ^ flip) for i in range(lax.axis_size(axi...  18.6 us
    ppermute x12, waiting for transfers between devices, swap_pairs(): return lax.ppermute(block, axis, route)  8.02 us
    pallas_call x2, Pallas kernels, join(): pl.pallas_call(functools.partial(join_kernel, pieces), out_shape=jax.Shap...  3.84 us
    pallas_call x1, Pallas kernels, pack(): pl.pallas_call(functools.partial(pack_kernel, stride, jobs), out_shape=[j...  3.19 us
  transfers between devices with their start and end apart: 19, of which 6 were waited for; matrix products, arithmetic and copies ran while one was open for 1% of the time, Pallas kernels for 16%

profile of v11, /device:TPU:3, one launch (start us, length us, event | category | flops | bytes accessed | tf_op | source)
XLA Modules:
  0.0 133.9 jit_solution(5963079298687743112)
XLA Ops:
  0.6 3.2 %shard_map.84 = (bf16[4,64,1024]{2,1,0:T(8,128)(2,1)}, bf16[4,64,1024]{2,1,0:T(8,128)(2,1)}, bf16[4,64,1536]{2,1,0:T(8,128)(2,1)}, bf16[4,64,1024]{2,1,0:T(8,128...) custom-call(bf16[64,6144]{1,0:T(8,128)(2,1)} %refs_0_.1, ...), custom_call_target="tpu_custom_call" | custom-call | flops 1 | bytes 1 | tf_op jit(solution)/shard_map/pallas_call | solution.py:85
  3.8 0.7 collective-permute-start.5
  4.6 2.3 %collective-permute-start = (bf16[4,64,1024]{2,1,0:T(8,128)(2,1)}, bf16[4,64,1024]{2,1,0:T(8,128)(2,1)}, u32[]{:S(2)}, u32[]{:S(2)}) collective-permute-start(bf16[4,64,1024]{2,1,0:T(8,128)(2,1)} %get-tuple-element.23), channel_id=1, source_target_pairs={{0,2},{1,3},{2,0},{3,1},{4,6},{5,7},{6,4},{7,5},{8,10},{9,11},{10,... | collective-permute-start | bytes 1572872 | tf_op jit(solution)/shard_map/ppermute | solution.py:36
  6.9 1.3 collective-permute-start.4
  8.2 22.4 %collective-permute-done.refs_1_ = bf16[4,64,1024]{2,1,0:T(8,128)(2,1)} collective-permute-done((bf16[4,64,1024]{2,1,0:T(8,128)(2,1)}, bf16[4,64,1024]{2,1,0:T(8,128)(2,1)}, u32[]{:S(2)}, u32[]{:S(2)}) %collective-permute-start) | collective-permute-done | bytes 524320 | tf_op jit(solution)/shard_map/ppermute | solution.py:36
  30.6 2.1 %shard_map.88.refs_2_ = bf16[2,4,64,1024]{3,2,1,0:T(8,128)(2,1)} custom-call(bf16[4,64,1024]{2,1,0:T(8,128)(2,1)} %collective-permute-done.4.refs_0_, bf16[4,64,1024]{2,1,0:T(8,128)(2,1)} %collective-permute-done.refs_1_, bf16[4,64,1536]{2,1,0:T(8,128)(2,1)} %collective-permute-done.5.refs_2_.refs_4_, bf16[4,64,1024]{2,1,0:T(8,128)(2,1)} %shard_map.85.refs_3_), custom_call_target="tpu_custom_call" | custom-call | flops 1 | bytes 1 | tf_op jit(solution)/shard_map/pallas_call | solution.py:121
  32.7 1.2 collective-permute-start.6
  33.8 3.0 %collective-permute-start.7 = (bf16[4,64,1536]{2,1,0:T(8,128)(2,1)}, bf16[4,64,1536]{2,1,0:T(8,128)(2,1)}, u32[]{:S(2)}, u32[]{:S(2)}) collective-permute-start(bf16[4,64,1536]{2,1,0:T(8,128)(2,1)} %get-tuple-element.20.refs_1_), channel_id=1, source_target_pairs={{4,8},{8,4},{12,16},{16,12},{20,24},{24,20},{5,9},{9,5},{13,17},{1... | collective-permute-start | bytes 2359304 | tf_op jit(solution)/shard_map/ppermute | solution.py:32
  36.9 3.0 %collective-permute-start.1 = (bf16[4,64,1024]{2,1,0:T(8,128)(2,1)}, bf16[4,64,1024]{2,1,0:T(8,128)(2,1)}, u32[]{:S(2)}, u32[]{:S(2)}) collective-permute-start(bf16[4,64,1024]{2,1,0:T(8,128)(2,1)} %shard_map.85.refs_3_), channel_id=1, source_target_pairs={{0,3},{1,2},{2,1},{3,0},{4,7},{5,6},{6,5},{7,4},{8,11},{9,10},{10,... | collective-permute-start | bytes 1572872 | tf_op jit(solution)/shard_map/ppermute | solution.py:36
  39.9 3.7 %collective-permute-start.9 = (bf16[2,4,64,1024]{3,2,1,0:T(8,128)(2,1)}, bf16[2,4,64,1024]{3,2,1,0:T(8,128)(2,1)}, u32[]{:S(2)}, u32[]{:S(2)}) collective-permute-start(bf16[2,4,64,1024]{3,2,1,0:T(8,128)(2,1)} %shard_map.88.refs_2_), channel_id=1, source_target_pairs={{4,8},{8,4},{12,16},{16,12},{20,24},{24,20},{5,9},{9,5},{13,17},{1... | collective-permute-start | bytes 3145736 | tf_op jit(solution)/shard_map/ppermute | solution.py:32
  43.5 9.3 %collective-permute-done.1.refs_1_.refs_0_ = bf16[4,64,1024]{2,1,0:T(8,128)(2,1)} collective-permute-done((bf16[4,64,1024]{2,1,0:T(8,128)(2,1)}, bf16[4,64,1024]{2,1,0:T(8,128)(2,1)}, u32[]{:S(2)}, u32[]{:S(2)}) %collective-permute-start.1) | collective-permute-done | bytes 524320 | tf_op jit(solution)/shard_map/ppermute | solution.py:36
  52.9 3.8 %collective-permute-done.7.refs_2_.refs_7_ = bf16[4,64,1536]{2,1,0:T(8,128)(2,1)} collective-permute-done((bf16[4,64,1536]{2,1,0:T(8,128)(2,1)}, bf16[4,64,1536]{2,1,0:T(8,128)(2,1)}, u32[]{:S(2)}, u32[]{:S(2)}) %collective-permute-start.7) | collective-permute-done | bytes 786464 | tf_op jit(solution)/shard_map/ppermute | solution.py:32
  56.7 7.2 %collective-permute-start.3 = (bf16[4,64,512]{2,1,0:T(8,128)(2,1)}, bf16[4,64,512]{2,1,0:T(8,128)(2,1)}, u32[]{:S(2)}, u32[]{:S(2)}) collective-permute-start(bf16[4,64,512]{2,1,0:T(8,128)(2,1)} %shard_map.87.refs_4_), channel_id=1, source_target_pairs={{0,2},{1,3},{2,0},{3,1},{4,6},{5,7},{6,4},{7,5},{8,10},{9,11},{10,... | collective-permute-start | bytes 786440 | tf_op jit(solution)/shard_map/ppermute | solution.py:36
  63.9 0.1 collective-permute-start.2
  64.0 12.4 %collective-permute-done.3.refs_1_ = bf16[4,64,512]{2,1,0:T(8,128)(2,1)} collective-permute-done((bf16[4,64,512]{2,1,0:T(8,128)(2,1)}, bf16[4,64,512]{2,1,0:T(8,128)(2,1)}, u32[]{:S(2)}, u32[]{:S(2)}) %collective-permute-start.3) | collective-permute-done | bytes 262176 | tf_op jit(solution)/shard_map/ppermute | solution.py:36
  76.4 3.7 %collective-permute-start.13 = (bf16[4,64,1024]{2,1,0:T(8,128)(2,1)}, bf16[4,64,1024]{2,1,0:T(8,128)(2,1)}, u32[]{:S(2)}, u32[]{:S(2)}) collective-permute-start(bf16[4,64,1024]{2,1,0:T(8,128)(2,1)} %shard_map.89.refs_3_), channel_id=1, source_target_pairs={{4,8},{8,4},{12,16},{16,12},{20,24},{24,20},{5,9},{9,5},{13,17},{1... | collective-permute-start | bytes 1572872 | tf_op jit(solution)/shard_map/ppermute | solution.py:32
  80.2 1.8 %shard_map.91.refs_2_ = bf16[2,4,64,512]{3,2,1,0:T(8,128)(2,1)} custom-call(bf16[4,64,512]{2,1,0:T(8,128)(2,1)} %collective-permute-done.2.refs_0_, bf16[4,64,512]{2,1,0:T(8,128)(2,1)} %collective-permute-done.3.refs_1_, bf16[4,64,1024]{2,1,0:T(8,128)(2,1)} %collective-permute-done.8.refs_2_.refs_6_, ...), custom_call_target="tpu_custom_call" | custom-call | flops 1 | bytes 1 | tf_op jit(solution)/shard_map/pallas_call | solution.py:121
  82.0 0.8 slice.3
  82.8 2.4 %collective-permute-start.10 = (bf16[4,64,256]{2,1,0:T(8,128)(2,1)}, bf16[4,64,256]{2,1,0:T(8,128)(2,1)S(1)}, u32[]{:S(2)}, u32[]{:S(2)}) collective-permute-start(bf16[4,64,256]{2,1,0:T(8,128)(2,1)} %shard_map.90.refs_4_), channel_id=1, source_target_pairs={{0,3},{1,2},{2,1},{3,0},{4,7},{5,6},{6,5},{7,4},{8,11},{9,10},{10,... | collective-permute-start | bytes 393224 | tf_op jit(solution)/shard_map/ppermute | solution.py:36
  85.2 0.1 dynamic-slice_bitcast_fusion.2
  85.3 0.6 pad_add_fusion.refs_0_
  85.9 3.7 %collective-permute-done.10.refs_1_.refs_0_ = bf16[4,64,256]{2,1,0:T(8,128)(2,1)S(1)} collective-permute-done((bf16[4,64,256]{2,1,0:T(8,128)(2,1)}, bf16[4,64,256]{2,1,0:T(8,128)(2,1)S(1)}, u32[]{:S(2)}, u32[]{:S(2)}) %collective-permute-start.10) | collective-permute-done | bytes 131104 | tf_op jit(solution)/shard_map/ppermute | solution.py:36
  89.6 0.6 copy-done
  90.2 2.3 %collective-permute-start.11 = (bf16[4,64,256]{2,1,0:T(8,128)(2,1)}, bf16[4,64,256]{2,1,0:T(8,128)(2,1)S(1)}, u32[]{:S(2)}, u32[]{:S(2)}) collective-permute-start(bf16[4,64,256]{2,1,0:T(8,128)(2,1)} %shard_map.92.refs_3_), channel_id=1, source_target_pairs={{0,3},{1,2},{2,1},{3,0},{4,7},{5,6},{6,5},{7,4},{8,11},{9,10},{10,... | collective-permute-start | bytes 393224 | tf_op jit(solution)/shard_map/ppermute | solution.py:36
  92.5 4.2 %collective-permute-start.15 = (bf16[2,4,64,512]{3,2,1,0:T(8,128)(2,1)}, bf16[2,4,64,512]{3,2,1,0:T(8,128)(2,1)}, u32[]{:S(2)}, u32[]{:S(2)}) collective-permute-start(bf16[2,4,64,512]{3,2,1,0:T(8,128)(2,1)} %shard_map.91.refs_2_), channel_id=1, source_target_pairs={{4,8},{8,4},{12,16},{16,12},{20,24},{24,20},{5,9},{9,5},{13,17},{1... | collective-permute-start | bytes 1572872 | tf_op jit(solution)/shard_map/ppermute | solution.py:32
  96.8 2.6 %collective-permute-start.16 = (bf16[4,64,256]{2,1,0:T(8,128)(2,1)}, bf16[4,64,256]{2,1,0:T(8,128)(2,1)}, u32[]{:S(2)}, u32[]{:S(2)}) collective-permute-start(bf16[4,64,256]{2,1,0:T(8,128)(2,1)} %shard_map.93.refs_3_), channel_id=1, source_target_pairs={{4,8},{8,4},{12,16},{16,12},{20,24},{24,20},{5,9},{9,5},{13,17},{1... | collective-permute-start | bytes 393224 | tf_op jit(solution)/shard_map/ppermute | solution.py:32
  99.5 14.0 %shard_map.94 = (bf16[256,1536]{1,0:T(8,128)(2,1)}, bf16[256,1536]{1,0:T(8,128)(2,1)}, bf16[256,1536]{1,0:T(8,128)(2,1)}, bf16[256,1536]{1,0:T(8,128)(2,1)}) custom-call(s32[3,4]{1,0:T(4,128)} %pad_add_fusion.refs_0_, bf16[4,64,1536]{2,1,0:T(8,128)(2,1)} %get-tuple-element.20.refs_1_, bf16[2,4,64,1024]{3,2,1,0:T(8,128)(2,1)} %shard_map.88.refs_2_, ...), custom_call_target="tpu_custom_call" | custom-call | flops 12000000000 | bytes 1 | tf_op jit(solution)/shard_map/pallas_call | solution.py:293
  113.5 5.5 %shard_map.95 = (bf16[256,1536]{1,0:T(8,128)(2,1)}, bf16[256,1536]{1,0:T(8,128)(2,1)}, bf16[256,1536]{1,0:T(8,128)(2,1)}, bf16[256,1536]{1,0:T(8,128)(2,1)}) custom-call(s32[3,4]{1,0:T(4,128)} %pad_add_fusion.refs_0_, bf16[4,64,1536]{2,1,0:T(8,128)(2,1)} %get-tuple-element.20.refs_1_, ...), custom_call_target="tpu_custom_call", output_to_operand_aliasing={{0}: (10, {}), {1}: (11, {}), {2}: (12, {}), {3}: (13, {})} | custom-call | flops 3000000000 | bytes 1 | tf_op jit(solution)/shard_map/pallas_call | solution.py:293
  119.1 0.6 copy-done.1
  119.7 4.1 %collective-permute-start.18 = (bf16[4,64,256]{2,1,0:T(8,128)(2,1)}, bf16[4,64,256]{2,1,0:T(8,128)(2,1)}, u32[]{:S(2)}, u32[]{:S(2)}) collective-permute-start(bf16[4,64,256]{2,1,0:T(8,128)(2,1)} %shard_map.96.refs_3_), channel_id=1, source_target_pairs={{4,8},{8,4},{12,16},{16,12},{20,24},{24,20},{5,9},{9,5},{13,17},{1... | collective-permute-start | bytes 393224 | tf_op jit(solution)/shard_map/ppermute | solution.py:32
  123.8 4.2 %collective-permute-done.18.refs_9_ = bf16[4,64,256]{2,1,0:T(8,128)(2,1)} collective-permute-done((bf16[4,64,256]{2,1,0:T(8,128)(2,1)}, bf16[4,64,256]{2,1,0:T(8,128)(2,1)}, u32[]{:S(2)}, u32[]{:S(2)}) %collective-permute-start.18) | collective-permute-done | bytes 131104 | tf_op jit(solution)/shard_map/ppermute | solution.py:32
  128.0 5.8 %shard_map.97 = (bf16[256,1536]{1,0:T(8,128)(2,1)}, bf16[256,1536]{1,0:T(8,128)(2,1)}, bf16[256,1536]{1,0:T(8,128)(2,1)}, bf16[256,1536]{1,0:T(8,128)(2,1)}) custom-call(s32[3,4]{1,0:T(4,128)} %pad_add_fusion.refs_0_, bf16[4,64,1536]{2,1,0:T(8,128)(2,1)} %get-tuple-element.20.refs_1_, ...), custom_call_target="tpu_custom_call", output_to_operand_aliasing={{0}: (10, {}), {1}: (11, {}), {2}: (12, {}), {3}: (13, {})} | custom-call | flops 3000000000 | bytes 1 | tf_op jit(solution)/shard_map/pallas_call | solution.py:293
  (29 shorter events, 0.2 us)
Async XLA Ops:
  3.8 26.7 %collective-permute-start.5 = (bf16[4,64,1536]{2,1,0:T(8,128)(2,1)}, bf16[4,64,1536]{2,1,0:T(8,128)(2,1)}, u32[]{:S(2)}, u32[]{:S(2)}) collective-permute-start(bf16[4,64,1536]{2,1,0:T(8,128)(2,1)} %get-tuple-element.20.refs_1_), channel_id=1, source_target_pairs={{0,4},{4,0},{8,12},{12,8},{16,20},{20,16},{24,28},{28,24},{1,5},{5... | collective-permute-start | bytes 2359304 | tf_op jit(solution)/shard_map/ppermute | solution.py:32
  4.6 26.0 %collective-permute-start = (bf16[4,64,1024]{2,1,0:T(8,128)(2,1)}, bf16[4,64,1024]{2,1,0:T(8,128)(2,1)}, u32[]{:S(2)}, u32[]{:S(2)}) collective-permute-start(bf16[4,64,1024]{2,1,0:T(8,128)(2,1)} %get-tuple-element.23), channel_id=1, source_target_pairs={{0,2},{1,3},{2,0},{3,1},{4,6},{5,7},{6,4},{7,5},{8,10},{9,11},{10,... | collective-permute-start | bytes 1572872 | tf_op jit(solution)/shard_map/ppermute | solution.py:36
  6.9 23.7 %collective-permute-start.4 = (bf16[4,64,1024]{2,1,0:T(8,128)(2,1)}, bf16[4,64,1024]{2,1,0:T(8,128)(2,1)}, u32[]{:S(2)}, u32[]{:S(2)}) collective-permute-start(bf16[4,64,1024]{2,1,0:T(8,128)(2,1)} %get-tuple-element.25), channel_id=1, source_target_pairs={{0,1},{1,0},{2,3},{3,2},{4,5},{5,4},{6,7},{7,6},{8,9},{9,8},{10,11... | collective-permute-start | bytes 1572872 | tf_op jit(solution)/shard_map/ppermute | solution.py:36
  32.7 24.0 %collective-permute-start.6 = (bf16[2,4,64,1024]{3,2,1,0:T(8,128)(2,1)}, bf16[2,4,64,1024]{3,2,1,0:T(8,128)(2,1)}, u32[]{:S(2)}, u32[]{:S(2)}) collective-permute-start(bf16[2,4,64,1024]{3,2,1,0:T(8,128)(2,1)} %shard_map.88.refs_2_), channel_id=1, source_target_pairs={{0,4},{4,0},{8,12},{12,8},{16,20},{20,16},{24,28},{28,24},{1,5},{5... | collective-permute-start | bytes 3145736 | tf_op jit(solution)/shard_map/ppermute | solution.py:32
  33.8 22.9 %collective-permute-start.7 = (bf16[4,64,1536]{2,1,0:T(8,128)(2,1)}, bf16[4,64,1536]{2,1,0:T(8,128)(2,1)}, u32[]{:S(2)}, u32[]{:S(2)}) collective-permute-start(bf16[4,64,1536]{2,1,0:T(8,128)(2,1)} %get-tuple-element.20.refs_1_), channel_id=1, source_target_pairs={{4,8},{8,4},{12,16},{16,12},{20,24},{24,20},{5,9},{9,5},{13,17},{1... | collective-permute-start | bytes 2359304 | tf_op jit(solution)/shard_map/ppermute | solution.py:32
  36.9 16.0 %collective-permute-start.1 = (bf16[4,64,1024]{2,1,0:T(8,128)(2,1)}, bf16[4,64,1024]{2,1,0:T(8,128)(2,1)}, u32[]{:S(2)}, u32[]{:S(2)}) collective-permute-start(bf16[4,64,1024]{2,1,0:T(8,128)(2,1)} %shard_map.85.refs_3_), channel_id=1, source_target_pairs={{0,3},{1,2},{2,1},{3,0},{4,7},{5,6},{6,5},{7,4},{8,11},{9,10},{10,... | collective-permute-start | bytes 1572872 | tf_op jit(solution)/shard_map/ppermute | solution.py:36
  39.9 40.3 %collective-permute-start.9 = (bf16[2,4,64,1024]{3,2,1,0:T(8,128)(2,1)}, bf16[2,4,64,1024]{3,2,1,0:T(8,128)(2,1)}, u32[]{:S(2)}, u32[]{:S(2)}) collective-permute-start(bf16[2,4,64,1024]{3,2,1,0:T(8,128)(2,1)} %shard_map.88.refs_2_), channel_id=1, source_target_pairs={{4,8},{8,4},{12,16},{16,12},{20,24},{24,20},{5,9},{9,5},{13,17},{1... | collective-permute-start | bytes 3145736 | tf_op jit(solution)/shard_map/ppermute | solution.py:32
  56.7 23.4 %collective-permute-start.8 = (bf16[4,64,1024]{2,1,0:T(8,128)(2,1)}, bf16[4,64,1024]{2,1,0:T(8,128)(2,1)}, u32[]{:S(2)}, u32[]{:S(2)}) collective-permute-start(bf16[4,64,1024]{2,1,0:T(8,128)(2,1)} %shard_map.89.refs_3_), channel_id=1, source_target_pairs={{0,4},{4,0},{8,12},{12,8},{16,20},{20,16},{24,28},{28,24},{1,5},{5... | collective-permute-start | bytes 1572872 | tf_op jit(solution)/shard_map/ppermute | solution.py:32
  56.7 19.7 %collective-permute-start.3 = (bf16[4,64,512]{2,1,0:T(8,128)(2,1)}, bf16[4,64,512]{2,1,0:T(8,128)(2,1)}, u32[]{:S(2)}, u32[]{:S(2)}) collective-permute-start(bf16[4,64,512]{2,1,0:T(8,128)(2,1)} %shard_map.87.refs_4_), channel_id=1, source_target_pairs={{0,2},{1,3},{2,0},{3,1},{4,6},{5,7},{6,4},{7,5},{8,10},{9,11},{10,... | collective-permute-start | bytes 786440 | tf_op jit(solution)/shard_map/ppermute | solution.py:36
  63.9 16.2 %collective-permute-start.2 = (bf16[4,64,512]{2,1,0:T(8,128)(2,1)}, bf16[4,64,512]{2,1,0:T(8,128)(2,1)}, u32[]{:S(2)}, u32[]{:S(2)}) collective-permute-start(bf16[4,64,512]{2,1,0:T(8,128)(2,1)} %shard_map.86.refs_3_), channel_id=1, source_target_pairs={{0,1},{1,0},{2,3},{3,2},{4,5},{5,4},{6,7},{7,6},{8,9},{9,8},{10,11... | collective-permute-start | bytes 786440 | tf_op jit(solution)/shard_map/ppermute | solution.py:36
  76.4 20.3 %collective-permute-start.13 = (bf16[4,64,1024]{2,1,0:T(8,128)(2,1)}, bf16[4,64,1024]{2,1,0:T(8,128)(2,1)}, u32[]{:S(2)}, u32[]{:S(2)}) collective-permute-start(bf16[4,64,1024]{2,1,0:T(8,128)(2,1)} %shard_map.89.refs_3_), channel_id=1, source_target_pairs={{4,8},{8,4},{12,16},{16,12},{20,24},{24,20},{5,9},{9,5},{13,17},{1... | collective-permute-start | bytes 1572872 | tf_op jit(solution)/shard_map/ppermute | solution.py:32
  81.9 14.8 %collective-permute-start.12 = (bf16[2,4,64,512]{3,2,1,0:T(8,128)(2,1)}, bf16[2,4,64,512]{3,2,1,0:T(8,128)(2,1)}, u32[]{:S(2)}, u32[]{:S(2)}) collective-permute-start(bf16[2,4,64,512]{3,2,1,0:T(8,128)(2,1)} %shard_map.91.refs_2_), channel_id=1, source_target_pairs={{0,4},{4,0},{8,12},{12,8},{16,20},{20,16},{24,28},{28,24},{1,5},{5... | collective-permute-start | bytes 1572872 | tf_op jit(solution)/shard_map/ppermute | solution.py:32
  82.8 6.7 %collective-permute-start.10 = (bf16[4,64,256]{2,1,0:T(8,128)(2,1)}, bf16[4,64,256]{2,1,0:T(8,128)(2,1)S(1)}, u32[]{:S(2)}, u32[]{:S(2)}) collective-permute-start(bf16[4,64,256]{2,1,0:T(8,128)(2,1)} %shard_map.90.refs_4_), channel_id=1, source_target_pairs={{0,3},{1,2},{2,1},{3,0},{4,7},{5,6},{6,5},{7,4},{8,11},{9,10},{10,... | collective-permute-start | bytes 393224 | tf_op jit(solution)/shard_map/ppermute | solution.py:36
  89.6 0.7 copy-start
  90.2 28.8 %collective-permute-start.11 = (bf16[4,64,256]{2,1,0:T(8,128)(2,1)}, bf16[4,64,256]{2,1,0:T(8,128)(2,1)S(1)}, u32[]{:S(2)}, u32[]{:S(2)}) collective-permute-start(bf16[4,64,256]{2,1,0:T(8,128)(2,1)} %shard_map.92.refs_3_), channel_id=1, source_target_pairs={{0,3},{1,2},{2,1},{3,0},{4,7},{5,6},{6,5},{7,4},{8,11},{9,10},{10,... | collective-permute-start | bytes 393224 | tf_op jit(solution)/shard_map/ppermute | solution.py:36
  92.5 21.0 %collective-permute-start.15 = (bf16[2,4,64,512]{3,2,1,0:T(8,128)(2,1)}, bf16[2,4,64,512]{3,2,1,0:T(8,128)(2,1)}, u32[]{:S(2)}, u32[]{:S(2)}) collective-permute-start(bf16[2,4,64,512]{3,2,1,0:T(8,128)(2,1)} %shard_map.91.refs_2_), channel_id=1, source_target_pairs={{4,8},{8,4},{12,16},{16,12},{20,24},{24,20},{5,9},{9,5},{13,17},{1... | collective-permute-start | bytes 1572872 | tf_op jit(solution)/shard_map/ppermute | solution.py:32
  96.7 16.7 %collective-permute-start.14 = (bf16[4,64,256]{2,1,0:T(8,128)(2,1)}, bf16[4,64,256]{2,1,0:T(8,128)(2,1)}, u32[]{:S(2)}, u32[]{:S(2)}) collective-permute-start(bf16[4,64,256]{2,1,0:T(8,128)(2,1)} %shard_map.93.refs_3_), channel_id=1, source_target_pairs={{0,4},{4,0},{8,12},{12,8},{16,20},{20,16},{24,28},{28,24},{1,5},{5... | collective-permute-start | bytes 393224 | tf_op jit(solution)/shard_map/ppermute | solution.py:32
  96.8 16.7 %collective-permute-start.16 = (bf16[4,64,256]{2,1,0:T(8,128)(2,1)}, bf16[4,64,256]{2,1,0:T(8,128)(2,1)}, u32[]{:S(2)}, u32[]{:S(2)}) collective-permute-start(bf16[4,64,256]{2,1,0:T(8,128)(2,1)} %shard_map.93.refs_3_), channel_id=1, source_target_pairs={{4,8},{8,4},{12,16},{16,12},{20,24},{24,20},{5,9},{9,5},{13,17},{1... | collective-permute-start | bytes 393224 | tf_op jit(solution)/shard_map/ppermute | solution.py:32
  119.0 0.6 copy-start.1
  119.7 4.1 %collective-permute-start.17 = (bf16[4,64,256]{2,1,0:T(8,128)(2,1)}, bf16[4,64,256]{2,1,0:T(8,128)(2,1)S(1)}, u32[]{:S(2)}, u32[]{:S(2)}) collective-permute-start(bf16[4,64,256]{2,1,0:T(8,128)(2,1)} %shard_map.96.refs_3_), channel_id=1, source_target_pairs={{0,4},{4,0},{8,12},{12,8},{16,20},{20,16},{24,28},{28,24},{1,5},{5... | collective-permute-start | bytes 393224 | tf_op jit(solution)/shard_map/ppermute | solution.py:32
  119.7 8.3 %collective-permute-start.18 = (bf16[4,64,256]{2,1,0:T(8,128)(2,1)}, bf16[4,64,256]{2,1,0:T(8,128)(2,1)}, u32[]{:S(2)}, u32[]{:S(2)}) collective-permute-start(bf16[4,64,256]{2,1,0:T(8,128)(2,1)} %shard_map.96.refs_3_), channel_id=1, source_target_pairs={{4,8},{8,4},{12,16},{16,12},{20,24},{24,20},{5,9},{9,5},{13,17},{1... | collective-permute-start | bytes 393224 | tf_op jit(solution)/shard_map/ppermute | solution.py:32
  123.8 4.2 %copy-start.2 = (bf16[4,64,256]{2,1,0:T(8,128)(2,1)}, bf16[4,64,256]{2,1,0:T(8,128)(2,1)S(1)}, u32[]{:S(2)}) copy-start(bf16[4,64,256]{2,1,0:T(8,128)(2,1)S(1)} %collective-permute-done.17.refs_6_) | copy-start | bytes 393220

commit v12 on v11

--- a/solution.py
+++ b/solution.py
@@ -12,7 +12,7 @@
 SCALE = 1.0 / math.sqrt(HD)
 EXP2_SCALE = SCALE * math.log2(math.e)
 MASKED = -1e30
-GROUPS = ((8,), (2, 2))
+GROUPS = ((8,), (4,))
 VMEM_LIMIT = 64 * 1024 * 1024 - 256 * 1024
 ATTEND_FLOPS = 1_500_000_000
 SMALL_COST = pl.CostEstimate(flops=1, bytes_accessed=1, transcendentals=0)
@@ -352,7 +352,7 @@
     outs, joined, number = None, None, 0
     for span, chunks in zip(spans, groups):
         for place in range(1 + len(chunks)):
-            after = [sent[-1][1]] + [earlier[2] for earlier in sent[-2:-1]]
+            after = list(sent[-1][1:])
             received = crossed
             number += 1
             if number < len(steps):
@@ -362,8 +362,6 @@
                 joined = spread(join(received, after))
                 sent.append(joined)
                 continue
-            if outs is not None and place == len(chunks):
-                after.append(outs[0])
             piece = spread(hold(received[0], after))
             sent.append(piece)
             first_head, count = chunks[place - 1]

time: 136 us -> 128 us (0.941)
  starting transfers between devices: 42 us -> 33.4 us
  waiting for transfers between devices: 55.8 us -> 61.6 us
  Pallas kernels: 32.3 us -> 29.5 us
    ppermute x7 -> x6, starting transfers between devices: 18.6 us -> 13.6 us  [swap_flipped(): lax.ppermute(block, axis, [(i, i ^ flip) for i in range(lax.axis_size(axi...]
    ppermute x12 -> x10, starting transfers between devices: 23.4 us -> 19.8 us  [swap_pairs(): return lax.ppermute(block, axis, route)]
    ppermute x12 -> x10, waiting for transfers between devices: 8.02 us -> 11.6 us  [swap_pairs(): return lax.ppermute(block, axis, route)]
    pallas_call x3 -> x2, Pallas kernels: 25.3 us -> 22.5 us  [attend(): pl.pallas_call(functools.partial(attend_kernel, parts, part_rows, steps,...]
    ppermute x7 -> x6, waiting for transfers between devices: 47.7 us -> 50 us  [swap_flipped(): lax.ppermute(block, axis, [(i, i ^ flip) for i in range(lax.axis_size(axi...]
  transfers between devices with their start and end apart: 19 -> 16, of which waited for: 6 -> 6; matrix products, arithmetic and copies ran while one was open for 1% -> 1% of each run, Pallas kernels for 16% -> 11%
where the time goes in v12:
time: 128 us; the launch traced here: 127 us
  waiting for transfers between devices  61.6 us (48%)
  starting transfers between devices  33.4 us (26%)
  Pallas kernels  29.5 us (23%)
    ppermute x6, waiting for transfers between devices, swap_flipped(): lax.ppermute(block, axis, [(i, i ^ flip) for i in range(lax.axis_size(axi...  50 us
    pallas_call x2, Pallas kernels, attend(): pl.pallas_call(functools.partial(attend_kernel, parts, part_rows, steps,...  22.5 us
    ppermute x10, starting transfers between devices, swap_pairs(): return lax.ppermute(block, axis, route)  19.8 us
    ppermute x6, starting transfers between devices, swap_flipped(): lax.ppermute(block, axis, [(i, i ^ flip) for i in range(lax.axis_size(axi...  13.6 us
    ppermute x10, waiting for transfers between devices, swap_pairs(): return lax.ppermute(block, axis, route)  11.6 us
    pallas_call x2, Pallas kernels, join(): pl.pallas_call(functools.partial(join_kernel, pieces), out_shape=jax.Shap...  3.85 us
    pallas_call x1, Pallas kernels, pack(): pl.pallas_call(functools.partial(pack_kernel, stride, jobs), out_shape=[j...  3.16 us
  transfers between devices with their start and end apart: 16, of which 6 were waited for; matrix products, arithmetic and copies ran while one was open for 1% of the time, Pallas kernels for 11%

profile of v12, /device:TPU:3, one launch (start us, length us, event | category | flops | bytes accessed | tf_op | source)
XLA Modules:
  0.0 126.9 jit_solution(17256780891929854589)
XLA Ops:
  0.6 3.2 %shard_map.84 = (bf16[4,64,1024]{2,1,0:T(8,128)(2,1)}, bf16[4,64,1024]{2,1,0:T(8,128)(2,1)}, bf16[4,64,1536]{2,1,0:T(8,128)(2,1)}, bf16[4,64,1024]{2,1,0:T(8,128...) custom-call(bf16[64,6144]{1,0:T(8,128)(2,1)} %refs_0_.1, ...), custom_call_target="tpu_custom_call" | custom-call | flops 1 | bytes 1 | tf_op jit(solution)/shard_map/pallas_call | solution.py:85
  3.8 0.7 collective-permute-start.5
  4.5 3.0 %collective-permute-start.6 = (bf16[4,64,1536]{2,1,0:T(8,128)(2,1)}, bf16[4,64,1536]{2,1,0:T(8,128)(2,1)}, u32[]{:S(2)}, u32[]{:S(2)}) collective-permute-start(bf16[4,64,1536]{2,1,0:T(8,128)(2,1)} %get-tuple-element.15.refs_1_), channel_id=1, source_target_pairs={{4,8},{8,4},{12,16},{16,12},{20,24},{24,20},{5,9},{9,5},{13,17},{1... | collective-permute-start | bytes 2359304 | tf_op jit(solution)/shard_map/ppermute | solution.py:32
  7.6 2.4 %collective-permute-start = (bf16[4,64,1024]{2,1,0:T(8,128)(2,1)}, bf16[4,64,1024]{2,1,0:T(8,128)(2,1)}, u32[]{:S(2)}, u32[]{:S(2)}) collective-permute-start(bf16[4,64,1024]{2,1,0:T(8,128)(2,1)} %get-tuple-element.18), channel_id=1, source_target_pairs={{0,2},{1,3},{2,0},{3,1},{4,6},{5,7},{6,4},{7,5},{8,10},{9,11},{10,... | collective-permute-start | bytes 1572872 | tf_op jit(solution)/shard_map/ppermute | solution.py:36
  9.9 1.3 %collective-permute-start.4 = (bf16[4,64,1024]{2,1,0:T(8,128)(2,1)}, bf16[4,64,1024]{2,1,0:T(8,128)(2,1)}, u32[]{:S(2)}, u32[]{:S(2)}) collective-permute-start(bf16[4,64,1024]{2,1,0:T(8,128)(2,1)} %get-tuple-element.20), channel_id=1, source_target_pairs={{0,1},{1,0},{2,3},{3,2},{4,5},{5,4},{6,7},{7,6},{8,9},{9,8},{10,11... | collective-permute-start | bytes 1572872 | tf_op jit(solution)/shard_map/ppermute | solution.py:36
  11.2 22.3 %collective-permute-done.refs_1_ = bf16[4,64,1024]{2,1,0:T(8,128)(2,1)} collective-permute-done((bf16[4,64,1024]{2,1,0:T(8,128)(2,1)}, bf16[4,64,1024]{2,1,0:T(8,128)(2,1)}, u32[]{:S(2)}, u32[]{:S(2)}) %collective-permute-start) | collective-permute-done | bytes 524320 | tf_op jit(solution)/shard_map/ppermute | solution.py:36
  33.5 0.0 collective-permute-done.4.refs_0_
  33.5 0.0 collective-permute-done.5.refs_2_.refs_4_
  33.5 2.1 %shard_map.88.refs_2_ = bf16[2,4,64,1024]{3,2,1,0:T(8,128)(2,1)} custom-call(bf16[4,64,1024]{2,1,0:T(8,128)(2,1)} %collective-permute-done.4.refs_0_, bf16[4,64,1024]{2,1,0:T(8,128)(2,1)} %collective-permute-done.refs_1_, bf16[4,64,1536]{2,1,0:T(8,128)(2,1)} %collective-permute-done.5.refs_2_.refs_4_, ...), custom_call_target="tpu_custom_call" | custom-call | flops 1 | bytes 1 | tf_op jit(solution)/shard_map/pallas_call | solution.py:121
  35.6 0.9 collective-permute-start.7
  36.5 3.3 %collective-permute-start.8 = (bf16[2,4,64,1024]{3,2,1,0:T(8,128)(2,1)}, bf16[2,4,64,1024]{3,2,1,0:T(8,128)(2,1)}, u32[]{:S(2)}, u32[]{:S(2)}) collective-permute-start(bf16[2,4,64,1024]{3,2,1,0:T(8,128)(2,1)} %shard_map.88.refs_2_), channel_id=1, source_target_pairs={{4,8},{8,4},{12,16},{16,12},{20,24},{24,20},{5,9},{9,5},{13,17},{1... | collective-permute-start | bytes 3145736 | tf_op jit(solution)/shard_map/ppermute | solution.py:32
  39.9 3.0 %collective-permute-start.1 = (bf16[4,64,1024]{2,1,0:T(8,128)(2,1)}, bf16[4,64,1024]{2,1,0:T(8,128)(2,1)}, u32[]{:S(2)}, u32[]{:S(2)}) collective-permute-start(bf16[4,64,1024]{2,1,0:T(8,128)(2,1)} %shard_map.85.refs_4_), channel_id=1, source_target_pairs={{0,3},{1,2},{2,1},{3,0},{4,7},{5,6},{6,5},{7,4},{8,11},{9,10},{10,... | collective-permute-start | bytes 1572872 | tf_op jit(solution)/shard_map/ppermute | solution.py:36
  42.9 12.0 %collective-permute-done.1.refs_1_.refs_0_ = bf16[4,64,1024]{2,1,0:T(8,128)(2,1)} collective-permute-done((bf16[4,64,1024]{2,1,0:T(8,128)(2,1)}, bf16[4,64,1024]{2,1,0:T(8,128)(2,1)}, u32[]{:S(2)}, u32[]{:S(2)}) %collective-permute-start.1) | collective-permute-done | bytes 524320 | tf_op jit(solution)/shard_map/ppermute | solution.py:36
  54.9 0.0 collective-permute-done.7.refs_1_.refs_5_
  54.9 8.8 %collective-permute-done.8.refs_2_.refs_8_ = bf16[2,4,64,1024]{3,2,1,0:T(8,128)(2,1)} collective-permute-done((bf16[2,4,64,1024]{3,2,1,0:T(8,128)(2,1)}, bf16[2,4,64,1024]{3,2,1,0:T(8,128)(2,1)}, u32[]{:S(2)}, u32[]{:S(2)}) %collective-permute-start.8) | collective-permute-done | bytes 1048608 | tf_op jit(solution)/shard_map/ppermute | solution.py:32
  63.7 3.5 %collective-permute-start.10 = (bf16[4,64,1024]{2,1,0:T(8,128)(2,1)}, bf16[4,64,1024]{2,1,0:T(8,128)(2,1)}, u32[]{:S(2)}, u32[]{:S(2)}) collective-permute-start(bf16[4,64,1024]{2,1,0:T(8,128)(2,1)} %shard_map.89.refs_3_), channel_id=1, source_target_pairs={{4,8},{8,4},{12,16},{16,12},{20,24},{24,20},{5,9},{9,5},{13,17},{1... | collective-permute-start | bytes 1572872 | tf_op jit(solution)/shard_map/ppermute | solution.py:32
  67.2 0.1 collective-permute-start.9
  67.3 1.7 %collective-permute-start.3 = (bf16[4,64,512]{2,1,0:T(8,128)(2,1)}, bf16[4,64,512]{2,1,0:T(8,128)(2,1)}, u32[]{:S(2)}, u32[]{:S(2)}) collective-permute-start(bf16[4,64,512]{2,1,0:T(8,128)(2,1)} %shard_map.87.refs_4_), channel_id=1, source_target_pairs={{0,2},{1,3},{2,0},{3,1},{4,6},{5,7},{6,4},{7,5},{8,10},{9,11},{10,... | collective-permute-start | bytes 786440 | tf_op jit(solution)/shard_map/ppermute | solution.py:36
  69.0 2.0 %collective-permute-start.2 = (bf16[4,64,512]{2,1,0:T(8,128)(2,1)}, bf16[4,64,512]{2,1,0:T(8,128)(2,1)}, u32[]{:S(2)}, u32[]{:S(2)}) collective-permute-start(bf16[4,64,512]{2,1,0:T(8,128)(2,1)} %shard_map.86.refs_3_), channel_id=1, source_target_pairs={{0,1},{1,0},{2,3},{3,2},{4,5},{5,4},{6,7},{7,6},{8,9},{9,8},{10,11... | collective-permute-start | bytes 786440 | tf_op jit(solution)/shard_map/ppermute | solution.py:36
  71.0 10.7 %collective-permute-done.3.refs_1_ = bf16[4,64,512]{2,1,0:T(8,128)(2,1)} collective-permute-done((bf16[4,64,512]{2,1,0:T(8,128)(2,1)}, bf16[4,64,512]{2,1,0:T(8,128)(2,1)}, u32[]{:S(2)}, u32[]{:S(2)}) %collective-permute-start.3) | collective-permute-done | bytes 262176 | tf_op jit(solution)/shard_map/ppermute | solution.py:36
  81.7 1.8 %shard_map.91.refs_2_ = bf16[2,4,64,512]{3,2,1,0:T(8,128)(2,1)} custom-call(bf16[4,64,512]{2,1,0:T(8,128)(2,1)} %collective-permute-done.2.refs_0_, bf16[4,64,512]{2,1,0:T(8,128)(2,1)} %collective-permute-done.3.refs_1_, bf16[4,64,1024]{2,1,0:T(8,128)(2,1)} %collective-permute-done.9.refs_2_.refs_6_, ...), custom_call_target="tpu_custom_call" | custom-call | flops 1 | bytes 1 | tf_op jit(solution)/shard_map/pallas_call | solution.py:121
  83.5 1.3 %collective-permute-start.12 = (bf16[2,4,64,512]{3,2,1,0:T(8,128)(2,1)}, bf16[2,4,64,512]{3,2,1,0:T(8,128)(2,1)}, u32[]{:S(2)}, u32[]{:S(2)}) collective-permute-start(bf16[2,4,64,512]{3,2,1,0:T(8,128)(2,1)} %shard_map.91.refs_2_), channel_id=1, source_target_pairs={{0,4},{4,0},{8,12},{12,8},{16,20},{20,16},{24,28},{28,24},{1,5},{5... | collective-permute-start | bytes 1572872 | tf_op jit(solution)/shard_map/ppermute | solution.py:32
  84.8 2.9 %collective-permute-start.13 = (bf16[2,4,64,512]{3,2,1,0:T(8,128)(2,1)}, bf16[2,4,64,512]{3,2,1,0:T(8,128)(2,1)}, u32[]{:S(2)}, u32[]{:S(2)}) collective-permute-start(bf16[2,4,64,512]{3,2,1,0:T(8,128)(2,1)} %shard_map.91.refs_2_), channel_id=1, source_target_pairs={{4,8},{8,4},{12,16},{16,12},{20,24},{24,20},{5,9},{9,5},{13,17},{1... | collective-permute-start | bytes 1572872 | tf_op jit(solution)/shard_map/ppermute | solution.py:32
  87.7 3.3 %collective-permute-start.11 = (bf16[4,64,512]{2,1,0:T(8,128)(2,1)}, bf16[4,64,512]{2,1,0:T(8,128)(2,1)}, u32[]{:S(2)}, u32[]{:S(2)}) collective-permute-start(bf16[4,64,512]{2,1,0:T(8,128)(2,1)} %shard_map.90.refs_4_), channel_id=1, source_target_pairs={{0,3},{1,2},{2,1},{3,0},{4,7},{5,6},{6,5},{7,4},{8,11},{9,10},{10,... | collective-permute-start | bytes 786440 | tf_op jit(solution)/shard_map/ppermute | solution.py:36
  91.0 0.8 slice.3
  91.8 0.1 dynamic-slice_bitcast_fusion.2
  91.9 0.6 pad_add_fusion.refs_0_
  92.5 5.0 %collective-permute-done.11.refs_0_ = bf16[4,64,512]{2,1,0:T(8,128)(2,1)} collective-permute-done((bf16[4,64,512]{2,1,0:T(8,128)(2,1)}, bf16[4,64,512]{2,1,0:T(8,128)(2,1)}, u32[]{:S(2)}, u32[]{:S(2)}) %collective-permute-start.11) | collective-permute-done | bytes 262176 | tf_op jit(solution)/shard_map/ppermute | solution.py:36
  97.5 2.8 %collective-permute-done.13.refs_2_.refs_8_ = bf16[2,4,64,512]{3,2,1,0:T(8,128)(2,1)} collective-permute-done((bf16[2,4,64,512]{3,2,1,0:T(8,128)(2,1)}, bf16[2,4,64,512]{3,2,1,0:T(8,128)(2,1)}, u32[]{:S(2)}, u32[]{:S(2)}) %collective-permute-start.13) | collective-permute-done | bytes 524320 | tf_op jit(solution)/shard_map/ppermute | solution.py:32
  100.3 4.0 %collective-permute-start.15 = (bf16[4,64,512]{2,1,0:T(8,128)(2,1)}, bf16[4,64,512]{2,1,0:T(8,128)(2,1)}, u32[]{:S(2)}, u32[]{:S(2)}) collective-permute-start(bf16[4,64,512]{2,1,0:T(8,128)(2,1)} %shard_map.92.refs_3_), channel_id=1, source_target_pairs={{4,8},{8,4},{12,16},{16,12},{20,24},{24,20},{5,9},{9,5},{13,17},{1... | collective-permute-start | bytes 786440 | tf_op jit(solution)/shard_map/ppermute | solution.py:32
  104.2 14.0 %shard_map.93 = (bf16[256,1536]{1,0:T(8,128)(2,1)}, bf16[256,1536]{1,0:T(8,128)(2,1)}, bf16[256,1536]{1,0:T(8,128)(2,1)}, bf16[256,1536]{1,0:T(8,128)(2,1)}) custom-call(s32[3,4]{1,0:T(4,128)} %pad_add_fusion.refs_0_, bf16[4,64,1536]{2,1,0:T(8,128)(2,1)} %get-tuple-element.15.refs_1_, bf16[2,4,64,1024]{3,2,1,0:T(8,128)(2,1)} %shard_map.88.refs_2_, ...), custom_call_target="tpu_custom_call" | custom-call | flops 12000000000 | bytes 1 | tf_op jit(solution)/shard_map/pallas_call | solution.py:293
  118.2 8.5 %shard_map.94 = (bf16[256,1536]{1,0:T(8,128)(2,1)}, bf16[256,1536]{1,0:T(8,128)(2,1)}, bf16[256,1536]{1,0:T(8,128)(2,1)}, bf16[256,1536]{1,0:T(8,128)(2,1)}) custom-call(s32[3,4]{1,0:T(4,128)} %pad_add_fusion.refs_0_, bf16[4,64,1536]{2,1,0:T(8,128)(2,1)} %get-tuple-element.15.refs_1_, ...), custom_call_target="tpu_custom_call", output_to_operand_aliasing={{0}: (10, {}), {1}: (11, {}), {2}: (12, {}), {3}: (13, {})} | custom-call | flops 6000000000 | bytes 1 | tf_op jit(solution)/shard_map/pallas_call | solution.py:293
  (14 shorter events, 0.0 us)
Async XLA Ops:
  3.8 29.7 %collective-permute-start.5 = (bf16[4,64,1536]{2,1,0:T(8,128)(2,1)}, bf16[4,64,1536]{2,1,0:T(8,128)(2,1)}, u32[]{:S(2)}, u32[]{:S(2)}) collective-permute-start(bf16[4,64,1536]{2,1,0:T(8,128)(2,1)} %get-tuple-element.15.refs_1_), channel_id=1, source_target_pairs={{0,4},{4,0},{8,12},{12,8},{16,20},{20,16},{24,28},{28,24},{1,5},{5... | collective-permute-start | bytes 2359304 | tf_op jit(solution)/shard_map/ppermute | solution.py:32
  4.5 29.0 %collective-permute-start.6 = (bf16[4,64,1536]{2,1,0:T(8,128)(2,1)}, bf16[4,64,1536]{2,1,0:T(8,128)(2,1)}, u32[]{:S(2)}, u32[]{:S(2)}) collective-permute-start(bf16[4,64,1536]{2,1,0:T(8,128)(2,1)} %get-tuple-element.15.refs_1_), channel_id=1, source_target_pairs={{4,8},{8,4},{12,16},{16,12},{20,24},{24,20},{5,9},{9,5},{13,17},{1... | collective-permute-start | bytes 2359304 | tf_op jit(solution)/shard_map/ppermute | solution.py:32
  7.6 25.9 %collective-permute-start = (bf16[4,64,1024]{2,1,0:T(8,128)(2,1)}, bf16[4,64,1024]{2,1,0:T(8,128)(2,1)}, u32[]{:S(2)}, u32[]{:S(2)}) collective-permute-start(bf16[4,64,1024]{2,1,0:T(8,128)(2,1)} %get-tuple-element.18), channel_id=1, source_target_pairs={{0,2},{1,3},{2,0},{3,1},{4,6},{5,7},{6,4},{7,5},{8,10},{9,11},{10,... | collective-permute-start | bytes 1572872 | tf_op jit(solution)/shard_map/ppermute | solution.py:36
  9.9 23.6 %collective-permute-start.4 = (bf16[4,64,1024]{2,1,0:T(8,128)(2,1)}, bf16[4,64,1024]{2,1,0:T(8,128)(2,1)}, u32[]{:S(2)}, u32[]{:S(2)}) collective-permute-start(bf16[4,64,1024]{2,1,0:T(8,128)(2,1)} %get-tuple-element.20), channel_id=1, source_target_pairs={{0,1},{1,0},{2,3},{3,2},{4,5},{5,4},{6,7},{7,6},{8,9},{9,8},{10,11... | collective-permute-start | bytes 1572872 | tf_op jit(solution)/shard_map/ppermute | solution.py:36
  35.6 19.3 %collective-permute-start.7 = (bf16[2,4,64,1024]{3,2,1,0:T(8,128)(2,1)}, bf16[2,4,64,1024]{3,2,1,0:T(8,128)(2,1)}, u32[]{:S(2)}, u32[]{:S(2)}) collective-permute-start(bf16[2,4,64,1024]{3,2,1,0:T(8,128)(2,1)} %shard_map.88.refs_2_), channel_id=1, source_target_pairs={{0,4},{4,0},{8,12},{12,8},{16,20},{20,16},{24,28},{28,24},{1,5},{5... | collective-permute-start | bytes 3145736 | tf_op jit(solution)/shard_map/ppermute | solution.py:32
  36.5 27.2 %collective-permute-start.8 = (bf16[2,4,64,1024]{3,2,1,0:T(8,128)(2,1)}, bf16[2,4,64,1024]{3,2,1,0:T(8,128)(2,1)}, u32[]{:S(2)}, u32[]{:S(2)}) collective-permute-start(bf16[2,4,64,1024]{3,2,1,0:T(8,128)(2,1)} %shard_map.88.refs_2_), channel_id=1, source_target_pairs={{4,8},{8,4},{12,16},{16,12},{20,24},{24,20},{5,9},{9,5},{13,17},{1... | collective-permute-start | bytes 3145736 | tf_op jit(solution)/shard_map/ppermute | solution.py:32
  39.9 15.0 %collective-permute-start.1 = (bf16[4,64,1024]{2,1,0:T(8,128)(2,1)}, bf16[4,64,1024]{2,1,0:T(8,128)(2,1)}, u32[]{:S(2)}, u32[]{:S(2)}) collective-permute-start(bf16[4,64,1024]{2,1,0:T(8,128)(2,1)} %shard_map.85.refs_4_), channel_id=1, source_target_pairs={{0,3},{1,2},{2,1},{3,0},{4,7},{5,6},{6,5},{7,4},{8,11},{9,10},{10,... | collective-permute-start | bytes 1572872 | tf_op jit(solution)/shard_map/ppermute | solution.py:36
  63.7 17.9 %collective-permute-start.10 = (bf16[4,64,1024]{2,1,0:T(8,128)(2,1)}, bf16[4,64,1024]{2,1,0:T(8,128)(2,1)}, u32[]{:S(2)}, u32[]{:S(2)}) collective-permute-start(bf16[4,64,1024]{2,1,0:T(8,128)(2,1)} %shard_map.89.refs_3_), channel_id=1, source_target_pairs={{4,8},{8,4},{12,16},{16,12},{20,24},{24,20},{5,9},{9,5},{13,17},{1... | collective-permute-start | bytes 1572872 | tf_op jit(solution)/shard_map/ppermute | solution.py:32
  67.2 14.4 %collective-permute-start.9 = (bf16[4,64,1024]{2,1,0:T(8,128)(2,1)}, bf16[4,64,1024]{2,1,0:T(8,128)(2,1)}, u32[]{:S(2)}, u32[]{:S(2)}) collective-permute-start(bf16[4,64,1024]{2,1,0:T(8,128)(2,1)} %shard_map.89.refs_3_), channel_id=1, source_target_pairs={{0,4},{4,0},{8,12},{12,8},{16,20},{20,16},{24,28},{28,24},{1,5},{5... | collective-permute-start | bytes 1572872 | tf_op jit(solution)/shard_map/ppermute | solution.py:32
  67.3 14.3 %collective-permute-start.3 = (bf16[4,64,512]{2,1,0:T(8,128)(2,1)}, bf16[4,64,512]{2,1,0:T(8,128)(2,1)}, u32[]{:S(2)}, u32[]{:S(2)}) collective-permute-start(bf16[4,64,512]{2,1,0:T(8,128)(2,1)} %shard_map.87.refs_4_), channel_id=1, source_target_pairs={{0,2},{1,3},{2,0},{3,1},{4,6},{5,7},{6,4},{7,5},{8,10},{9,11},{10,... | collective-permute-start | bytes 786440 | tf_op jit(solution)/shard_map/ppermute | solution.py:36
  69.0 12.7 %collective-permute-start.2 = (bf16[4,64,512]{2,1,0:T(8,128)(2,1)}, bf16[4,64,512]{2,1,0:T(8,128)(2,1)}, u32[]{:S(2)}, u32[]{:S(2)}) collective-permute-start(bf16[4,64,512]{2,1,0:T(8,128)(2,1)} %shard_map.86.refs_3_), channel_id=1, source_target_pairs={{0,1},{1,0},{2,3},{3,2},{4,5},{5,4},{6,7},{7,6},{8,9},{9,8},{10,11... | collective-permute-start | bytes 786440 | tf_op jit(solution)/shard_map/ppermute | solution.py:36
  83.5 14.1 %collective-permute-start.12 = (bf16[2,4,64,512]{3,2,1,0:T(8,128)(2,1)}, bf16[2,4,64,512]{3,2,1,0:T(8,128)(2,1)}, u32[]{:S(2)}, u32[]{:S(2)}) collective-permute-start(bf16[2,4,64,512]{3,2,1,0:T(8,128)(2,1)} %shard_map.91.refs_2_), channel_id=1, source_target_pairs={{0,4},{4,0},{8,12},{12,8},{16,20},{20,16},{24,28},{28,24},{1,5},{5... | collective-permute-start | bytes 1572872 | tf_op jit(solution)/shard_map/ppermute | solution.py:32
  84.8 15.5 %collective-permute-start.13 = (bf16[2,4,64,512]{3,2,1,0:T(8,128)(2,1)}, bf16[2,4,64,512]{3,2,1,0:T(8,128)(2,1)}, u32[]{:S(2)}, u32[]{:S(2)}) collective-permute-start(bf16[2,4,64,512]{3,2,1,0:T(8,128)(2,1)} %shard_map.91.refs_2_), channel_id=1, source_target_pairs={{4,8},{8,4},{12,16},{16,12},{20,24},{24,20},{5,9},{9,5},{13,17},{1... | collective-permute-start | bytes 1572872 | tf_op jit(solution)/shard_map/ppermute | solution.py:32
  87.7 9.8 %collective-permute-start.11 = (bf16[4,64,512]{2,1,0:T(8,128)(2,1)}, bf16[4,64,512]{2,1,0:T(8,128)(2,1)}, u32[]{:S(2)}, u32[]{:S(2)}) collective-permute-start(bf16[4,64,512]{2,1,0:T(8,128)(2,1)} %shard_map.90.refs_4_), channel_id=1, source_target_pairs={{0,3},{1,2},{2,1},{3,0},{4,7},{5,6},{6,5},{7,4},{8,11},{9,10},{10,... | collective-permute-start | bytes 786440 | tf_op jit(solution)/shard_map/ppermute | solution.py:36
  100.3 18.0 %collective-permute-start.14 = (bf16[4,64,512]{2,1,0:T(8,128)(2,1)}, bf16[4,64,512]{2,1,0:T(8,128)(2,1)}, u32[]{:S(2)}, u32[]{:S(2)}) collective-permute-start(bf16[4,64,512]{2,1,0:T(8,128)(2,1)} %shard_map.92.refs_3_), channel_id=1, source_target_pairs={{0,4},{4,0},{8,12},{12,8},{16,20},{20,16},{24,28},{28,24},{1,5},{5... | collective-permute-start | bytes 786440 | tf_op jit(solution)/shard_map/ppermute | solution.py:32
  100.3 18.0 %collective-permute-start.15 = (bf16[4,64,512]{2,1,0:T(8,128)(2,1)}, bf16[4,64,512]{2,1,0:T(8,128)(2,1)}, u32[]{:S(2)}, u32[]{:S(2)}) collective-permute-start(bf16[4,64,512]{2,1,0:T(8,128)(2,1)} %shard_map.92.refs_3_), channel_id=1, source_target_pairs={{4,8},{8,4},{12,16},{16,12},{20,24},{24,20},{5,9},{9,5},{13,17},{1... | collective-permute-start | bytes 786440 | tf_op jit(solution)/shard_map/ppermute | solution.py:32

commit v13 on v12

--- a/solution.py
+++ b/solution.py
@@ -15,6 +15,7 @@
 GROUPS = ((8,), (4,))
 VMEM_LIMIT = 64 * 1024 * 1024 - 256 * 1024
 ATTEND_FLOPS = 1_500_000_000
+LARGE_COST = pl.CostEstimate(flops=40_000_000_000, bytes_accessed=1, transcendentals=0)
 SMALL_COST = pl.CostEstimate(flops=1, bytes_accessed=1, transcendentals=0)
 
 
@@ -129,11 +130,11 @@
             pltpu.SemaphoreType.DMA((pieces,)),
         ],
         compiler_params=pltpu.CompilerParams(vmem_limit_bytes=VMEM_LIMIT),
-        cost_estimate=SMALL_COST,
+        cost_estimate=LARGE_COST,
     )(*received, *after)
 
 
-def hold(array, after):
+def hold(array, after, cost=SMALL_COST):
     return pl.pallas_call(
         lambda *refs: None,
         out_shape=jax.ShapeDtypeStruct(array.shape, array.dtype),
@@ -141,7 +142,7 @@
         out_specs=pl.BlockSpec(memory_space=pl.ANY),
         input_output_aliases={0: 0},
         compiler_params=pltpu.CompilerParams(vmem_limit_bytes=VMEM_LIMIT),
-        cost_estimate=SMALL_COST,
+        cost_estimate=cost,
     )(array, *after)
 
 
@@ -157,11 +158,9 @@
     return jnp.dot(a, b, preferred_element_type=jnp.float32)
 
 
-def attend_head(values_of, slot_ids, lane_ids, part_rows, rows):
-    queries, keys, values, grads = values_of
-    size = keys.shape[0]
+def attend_heads(heads, slot_ids, lane_ids, part_rows, rows):
+    size = heads[0][0].shape[0]
     slots = size // part_rows
-    grad_k = grad_v = None
 
     def per_slot(array):
         return [array[slot * part_rows : (slot + 1) * part_rows] for slot in range(slots)]
@@ -172,31 +171,50 @@
             total = combine(total, reduce(array, axis=0, keepdims=True))
         return total
 
-    for start in range(0, size, rows):
+    def products(head, start):
+        queries, keys, values, grads = heads[head]
         tile = slice(start, start + rows)
+        return dot_nt(keys, queries[tile]), dot_nt(values, grads[tile])
+
+    def weigh(scores, grad_probs, start):
+        lanes = lane_ids[:, start : start + rows]
         scores = [
-            part + jnp.where(lane_ids[:, tile] == slot_id, 0.0, MASKED)
-            for part, slot_id in zip(per_slot(dot_nt(keys, queries[tile])), slot_ids)
+            part + jnp.where(lanes == slot_id, 0.0, MASKED)
+            for part, slot_id in zip(per_slot(scores), slot_ids)
         ]
         row_max = over_slots(jnp.max, jnp.maximum, scores)
         weights = [jnp.exp2((part - row_max) * EXP2_SCALE) for part in scores]
         inverse = 1.0 / over_slots(jnp.sum, jnp.add, weights)
         probs = [part * inverse for part in weights]
-        grad_probs = per_slot(dot_nt(values, grads[tile]))
+        grad_probs = per_slot(grad_probs)
         inner = over_slots(jnp.sum, jnp.add, [p * g for p, g in zip(probs, grad_probs)])
         low = jnp.concatenate([p.astype(jnp.bfloat16) for p in probs])
-        grad_scores = jnp.concatenate(
-            [(p * (g - inner)).astype(jnp.bfloat16) for p, g in zip(probs, grad_probs)]
-        )
-        tile_v = dot_nn(low[:rows], grads[tile])
-        tile_k = dot_nn(grad_scores[:rows], queries[tile])
+        grad_scores = [(p * (g - inner)).astype(jnp.bfloat16) for p, g in zip(probs, grad_probs)]
+        return low, jnp.concatenate(grad_scores)
+
+    def finish(head, low, grad_scores, start):
+        queries, keys, values, grads = heads[head]
+        tile = slice(start, start + rows)
+        result = results[head]
         if start == 0:
-            attended = dot_tn(low, values)
-            grad_q = dot_tn(grad_scores, keys)
-            grad_k, grad_v = tile_k, tile_v
-        else:
-            grad_k, grad_v = grad_k + tile_k, grad_v + tile_v
-    return attended, grad_q * SCALE, grad_k * SCALE, grad_v
+            result[0] = dot_tn(values, low).astype(jnp.bfloat16).T
+            result[1] = (dot_tn(keys, grad_scores) * SCALE).astype(jnp.bfloat16).T
+            result[2] = result[3] = 0.0
+        result[2] += dot_nn(grad_scores[:rows], queries[tile])
+        result[3] += dot_nn(low[:rows], grads[tile])
+
+    results = [[None] * 4 for _ in heads]
+    work = [(head, start) for head in range(len(heads)) for start in range(0, size, rows)]
+    ahead = products(*work[0])
+    for number, (head, start) in enumerate(work):
+        scores, grad_probs = ahead
+        if number + 1 < len(work):
+            ahead = products(*work[number + 1])
+        finish(head, *weigh(scores, grad_probs, start), start)
+    for result in results:
+        result[2] = (result[2] * SCALE).astype(jnp.bfloat16)
+        result[3] = result[3].astype(jnp.bfloat16)
+    return results
 
 
 def attend_kernel(parts, part_rows, steps, width, offsets, has_outs, *refs):
@@ -271,12 +289,12 @@
         def _():
             slot_ids = [image_ids[0, slot] for slot in range(parts)]
             slot_ids += [table[slot] for slot in range(slots)]
-            for start in range(0, width, HD):
-                head = slice(start, start + HD)
-                values_of = [window[buffer, index, :size, head] for index in range(4)]
-                results = attend_head(values_of, slot_ids, lane_ids[0:1], part_rows, rows)
-                for out, result in zip(outs, results):
-                    out[:, head] = result.astype(jnp.bfloat16)
+            spans = [slice(start, start + HD) for start in range(0, width, HD)]
+            heads = [[window[buffer, i, :size, span] for i in range(4)] for span in spans]
+            results = attend_heads(heads, slot_ids, lane_ids[0:1], part_rows, rows)
+            for span, result in zip(spans, results):
+                for out, part in zip(outs, result):
+                    out[:, span] = part
 
 
 def attend(image_ids, groups, offsets, outs, first_head, heads):
@@ -353,16 +371,17 @@
     for span, chunks in zip(spans, groups):
         for place in range(1 + len(chunks)):
             after = list(sent[-1][1:])
-            received = crossed
+            received, held = crossed, []
             number += 1
             if number < len(steps):
                 held, crossed = cross(steps[number], [received[-1]])
-                after += held
+            elif outs is not None:
+                after.append(outs[0])
             if place == 0:
-                joined = spread(join(received, after))
+                joined = spread(hold(join(received, held), after))
                 sent.append(joined)
                 continue
-            piece = spread(hold(received[0], after))
+            piece = spread(hold(hold(received[0], held, LARGE_COST), after))
             sent.append(piece)
             first_head, count = chunks[place - 1]
             offsets = (first_head, first_head - span[0], 0)

time: 128 us -> 126 us (0.984)
  starting transfers between devices: 33.4 us -> 44.9 us
  waiting for transfers between devices: 61.6 us -> 53.1 us
  Pallas kernels: 29.5 us -> 24.9 us
    ppermute x6, waiting for transfers between devices: 50 us -> 31.9 us  [swap_flipped(): lax.ppermute(block, axis, [(i, i ^ flip) for i in range(lax.axis_size(axi...]
    ppermute x10, waiting for transfers between devices: 11.6 us -> 21.3 us  [swap_pairs(): return lax.ppermute(block, axis, route)]
    ppermute x6, starting transfers between devices: 13.6 us -> 19.4 us  [swap_flipped(): lax.ppermute(block, axis, [(i, i ^ flip) for i in range(lax.axis_size(axi...]
    ppermute x10, starting transfers between devices: 19.8 us -> 25.4 us  [swap_pairs(): return lax.ppermute(block, axis, route)]
    pallas_call x2, Pallas kernels: 22.5 us -> 17.9 us  [attend(): pl.pallas_call(functools.partial(attend_kernel, parts, part_rows, steps,...]
  transfers between devices with their start and end apart: 16 -> 16, of which waited for: 6 -> 6; matrix products, arithmetic and copies ran while one was open for 1% -> 1% of each run, Pallas kernels for 11% -> 12%
where the time goes in v13:
time: 126 us; the launch traced here: 125 us
  waiting for transfers between devices  53.1 us (42%)
  starting transfers between devices  44.9 us (36%)
  Pallas kernels  24.9 us (20%)
    ppermute x6, waiting for transfers between devices, swap_flipped(): lax.ppermute(block, axis, [(i, i ^ flip) for i in range(lax.axis_size(axi...  31.9 us
    ppermute x10, starting transfers between devices, swap_pairs(): return lax.ppermute(block, axis, route)  25.4 us
    ppermute x10, waiting for transfers between devices, swap_pairs(): return lax.ppermute(block, axis, route)  21.3 us
    ppermute x6, starting transfers between devices, swap_flipped(): lax.ppermute(block, axis, [(i, i ^ flip) for i in range(lax.axis_size(axi...  19.4 us
    pallas_call x2, Pallas kernels, attend(): pl.pallas_call(functools.partial(attend_kernel, parts, part_rows, steps,...  17.9 us
    pallas_call x2, Pallas kernels, join(): pl.pallas_call(functools.partial(join_kernel, pieces), out_shape=jax.Shap...  3.88 us
    pallas_call x1, Pallas kernels, pack(): pl.pallas_call(functools.partial(pack_kernel, stride, jobs), out_shape=[j...  3.16 us
  transfers between devices with their start and end apart: 16, of which 6 were waited for; matrix products, arithmetic and copies ran while one was open for 1% of the time, Pallas kernels for 12%

profile of v13, /device:TPU:3, one launch (start us, length us, event | category | flops | bytes accessed | tf_op | source)
XLA Modules:
  0.0 125.4 jit_solution(5073189735751631996)
XLA Ops:
  0.6 3.2 %shard_map.84 = (bf16[4,64,1024]{2,1,0:T(8,128)(2,1)}, bf16[4,64,1024]{2,1,0:T(8,128)(2,1)}, bf16[4,64,1536]{2,1,0:T(8,128)(2,1)}, bf16[4,64,1024]{2,1,0:T(8,128...) custom-call(bf16[64,6144]{1,0:T(8,128)(2,1)} %refs_0_.1, ...), custom_call_target="tpu_custom_call" | custom-call | flops 1 | bytes 1 | tf_op jit(solution)/shard_map/pallas_call | solution.py:86
  3.8 2.4 %collective-permute-start = (bf16[4,64,1024]{2,1,0:T(8,128)(2,1)}, bf16[4,64,1024]{2,1,0:T(8,128)(2,1)}, u32[]{:S(2)}, u32[]{:S(2)}) collective-permute-start(bf16[4,64,1024]{2,1,0:T(8,128)(2,1)} %get-tuple-element.18), channel_id=1, source_target_pairs={{0,2},{1,3},{2,0},{3,1},{4,6},{5,7},{6,4},{7,5},{8,10},{9,11},{10,... | collective-permute-start | bytes 1572872 | tf_op jit(solution)/shard_map/ppermute | solution.py:37
  6.2 1.3 %collective-permute-start.4 = (bf16[4,64,1024]{2,1,0:T(8,128)(2,1)}, bf16[4,64,1024]{2,1,0:T(8,128)(2,1)}, u32[]{:S(2)}, u32[]{:S(2)}) collective-permute-start(bf16[4,64,1024]{2,1,0:T(8,128)(2,1)} %get-tuple-element.21), channel_id=1, source_target_pairs={{0,1},{1,0},{2,3},{3,2},{4,5},{5,4},{6,7},{7,6},{8,9},{9,8},{10,11... | collective-permute-start | bytes 1572872 | tf_op jit(solution)/shard_map/ppermute | solution.py:37
  7.5 4.2 %collective-permute-start.6 = (bf16[4,64,1536]{2,1,0:T(8,128)(2,1)}, bf16[4,64,1536]{2,1,0:T(8,128)(2,1)}, u32[]{:S(2)}, u32[]{:S(2)}) collective-permute-start(bf16[4,64,1536]{2,1,0:T(8,128)(2,1)} %get-tuple-element.15.refs_1_), channel_id=1, source_target_pairs={{4,8},{8,4},{12,16},{16,12},{20,24},{24,20},{5,9},{9,5},{13,17},{1... | collective-permute-start | bytes 2359304 | tf_op jit(solution)/shard_map/ppermute | solution.py:33
  11.7 0.1 collective-permute-start.5
  11.8 0.8 slice.3
  12.6 0.1 dynamic-slice_bitcast_fusion.2
  12.7 0.6 pad_add_fusion.refs_0_
  13.3 15.9 %collective-permute-done.refs_1_ = bf16[4,64,1024]{2,1,0:T(8,128)(2,1)} collective-permute-done((bf16[4,64,1024]{2,1,0:T(8,128)(2,1)}, bf16[4,64,1024]{2,1,0:T(8,128)(2,1)}, u32[]{:S(2)}, u32[]{:S(2)}) %collective-permute-start) | collective-permute-done | bytes 524320 | tf_op jit(solution)/shard_map/ppermute | solution.py:37
  29.2 4.2 %collective-permute-start.1 = (bf16[4,64,1024]{2,1,0:T(8,128)(2,1)}, bf16[4,64,1024]{2,1,0:T(8,128)(2,1)}, u32[]{:S(2)}, u32[]{:S(2)}) collective-permute-start(bf16[4,64,1024]{2,1,0:T(8,128)(2,1)} %shard_map.85.refs_2_), channel_id=1, source_target_pairs={{0,3},{1,2},{2,1},{3,0},{4,7},{5,6},{6,5},{7,4},{8,11},{9,10},{10,... | collective-permute-start | bytes 1572872 | tf_op jit(solution)/shard_map/ppermute | solution.py:37
  33.4 2.0 %shard_map.91.refs_0_ = bf16[2,4,64,1024]{3,2,1,0:T(8,128)(2,1)} custom-call(bf16[4,64,1024]{2,1,0:T(8,128)(2,1)} %collective-permute-done.4.refs_0_, bf16[4,64,1024]{2,1,0:T(8,128)(2,1)} %collective-permute-done.refs_1_, bf16[4,64,1024]{2,1,0:T(8,128)(2,1)} %shard_map.85.refs_2_), custom_call_target="tpu_custom_call" | custom-call | flops 40000000000 | bytes 1 | tf_op jit(solution)/shard_map/pallas_call | solution.py:122
  35.4 0.0 collective-permute-done.6.refs_2_.refs_7_
  35.5 3.8 %collective-permute-start.8 = (bf16[2,4,64,1024]{3,2,1,0:T(8,128)(2,1)}, bf16[2,4,64,1024]{3,2,1,0:T(8,128)(2,1)}, u32[]{:S(2)}, u32[]{:S(2)}) collective-permute-start(bf16[2,4,64,1024]{3,2,1,0:T(8,128)(2,1)} %shard_map.92.refs_2_), channel_id=1, source_target_pairs={{4,8},{8,4},{12,16},{16,12},{20,24},{24,20},{5,9},{9,5},{13,17},{1... | collective-permute-start | bytes 3145736 | tf_op jit(solution)/shard_map/ppermute | solution.py:33
  39.2 0.1 collective-permute-start.7
  39.3 5.8 %collective-permute-done.1.refs_1_.refs_0_ = bf16[4,64,1024]{2,1,0:T(8,128)(2,1)} collective-permute-done((bf16[4,64,1024]{2,1,0:T(8,128)(2,1)}, bf16[4,64,1024]{2,1,0:T(8,128)(2,1)}, u32[]{:S(2)}, u32[]{:S(2)}) %collective-permute-start.1) | collective-permute-done | bytes 524320 | tf_op jit(solution)/shard_map/ppermute | solution.py:37
  45.1 10.0 %collective-permute-start.2 = (bf16[4,64,512]{2,1,0:T(8,128)(2,1)}, bf16[4,64,512]{2,1,0:T(8,128)(2,1)}, u32[]{:S(2)}, u32[]{:S(2)}) collective-permute-start(bf16[4,64,512]{2,1,0:T(8,128)(2,1)} %shard_map.86.refs_1_), channel_id=1, source_target_pairs={{0,1},{1,0},{2,3},{3,2},{4,5},{5,4},{6,7},{7,6},{8,9},{9,8},{10,11... | collective-permute-start | bytes 786440 | tf_op jit(solution)/shard_map/ppermute | solution.py:37
  55.1 0.0 collective-permute-start.3
  55.2 10.2 %collective-permute-done.3.refs_1_ = bf16[4,64,512]{2,1,0:T(8,128)(2,1)} collective-permute-done((bf16[4,64,512]{2,1,0:T(8,128)(2,1)}, bf16[4,64,512]{2,1,0:T(8,128)(2,1)}, u32[]{:S(2)}, u32[]{:S(2)}) %collective-permute-start.3) | collective-permute-done | bytes 262176 | tf_op jit(solution)/shard_map/ppermute | solution.py:37
  65.4 1.5 %collective-permute-start.11 = (bf16[4,64,512]{2,1,0:T(8,128)(2,1)}, bf16[4,64,512]{2,1,0:T(8,128)(2,1)}, u32[]{:S(2)}, u32[]{:S(2)}) collective-permute-start(bf16[4,64,512]{2,1,0:T(8,128)(2,1)} %shard_map.88.refs_2_), channel_id=1, source_target_pairs={{0,3},{1,2},{2,1},{3,0},{4,7},{5,6},{6,5},{7,4},{8,11},{9,10},{10,... | collective-permute-start | bytes 786440 | tf_op jit(solution)/shard_map/ppermute | solution.py:37
  66.9 0.0 collective-permute-done.2.refs_0_
  66.9 1.8 %shard_map.89.refs_0_ = bf16[2,4,64,512]{3,2,1,0:T(8,128)(2,1)} custom-call(bf16[4,64,512]{2,1,0:T(8,128)(2,1)} %collective-permute-done.2.refs_0_, bf16[4,64,512]{2,1,0:T(8,128)(2,1)} %collective-permute-done.3.refs_1_, bf16[4,64,512]{2,1,0:T(8,128)(2,1)} %shard_map.88.refs_2_), custom_call_target="tpu_custom_call" | custom-call | flops 40000000000 | bytes 1 | tf_op jit(solution)/shard_map/pallas_call | solution.py:122
  68.8 9.6 %collective-permute-start.10 = (bf16[4,64,1024]{2,1,0:T(8,128)(2,1)}, bf16[4,64,1024]{2,1,0:T(8,128)(2,1)}, u32[]{:S(2)}, u32[]{:S(2)}) collective-permute-start(bf16[4,64,1024]{2,1,0:T(8,128)(2,1)} %shard_map.93.refs_3_), channel_id=1, source_target_pairs={{4,8},{8,4},{12,16},{16,12},{20,24},{24,20},{5,9},{9,5},{13,17},{1... | collective-permute-start | bytes 1572872 | tf_op jit(solution)/shard_map/ppermute | solution.py:33
  78.4 0.1 collective-permute-start.9
  78.5 11.8 %collective-permute-done.10.refs_2_.refs_9_ = bf16[4,64,1024]{2,1,0:T(8,128)(2,1)} collective-permute-done((bf16[4,64,1024]{2,1,0:T(8,128)(2,1)}, bf16[4,64,1024]{2,1,0:T(8,128)(2,1)}, u32[]{:S(2)}, u32[]{:S(2)}) %collective-permute-start.10) | collective-permute-done | bytes 524320 | tf_op jit(solution)/shard_map/ppermute | solution.py:33
  90.3 4.5 %collective-permute-start.13 = (bf16[2,4,64,512]{3,2,1,0:T(8,128)(2,1)}, bf16[2,4,64,512]{3,2,1,0:T(8,128)(2,1)}, u32[]{:S(2)}, u32[]{:S(2)}) collective-permute-start(bf16[2,4,64,512]{3,2,1,0:T(8,128)(2,1)} %shard_map.94.refs_2_), channel_id=1, source_target_pairs={{4,8},{8,4},{12,16},{16,12},{20,24},{24,20},{5,9},{9,5},{13,17},{1... | collective-permute-start | bytes 1572872 | tf_op jit(solution)/shard_map/ppermute | solution.py:33
  94.8 0.1 collective-permute-start.12
  94.9 11.0 %shard_map.96 = (bf16[256,1536]{1,0:T(8,128)(2,1)}, bf16[256,1536]{1,0:T(8,128)(2,1)}, bf16[256,1536]{1,0:T(8,128)(2,1)}, bf16[256,1536]{1,0:T(8,128)(2,1)}) custom-call(s32[3,4]{1,0:T(4,128)} %pad_add_fusion.refs_0_, bf16[4,64,1536]{2,1,0:T(8,128)(2,1)} %get-tuple-element.15.refs_1_, bf16[2,4,64,1024]{3,2,1,0:T(8,128)(2,1)} %shard_map.92.refs_2_, ...), custom_call_target="tpu_custom_call" | custom-call | flops 12000000000 | bytes 1 | tf_op jit(solution)/shard_map/pallas_call | solution.py:311
  106.0 1.7 %collective-permute-done.13.refs_2_.refs_8_ = bf16[2,4,64,512]{3,2,1,0:T(8,128)(2,1)} collective-permute-done((bf16[2,4,64,512]{3,2,1,0:T(8,128)(2,1)}, bf16[2,4,64,512]{3,2,1,0:T(8,128)(2,1)}, u32[]{:S(2)}, u32[]{:S(2)}) %collective-permute-start.13) | collective-permute-done | bytes 524320 | tf_op jit(solution)/shard_map/ppermute | solution.py:33
  107.6 2.9 %collective-permute-start.15 = (bf16[4,64,512]{2,1,0:T(8,128)(2,1)}, bf16[4,64,512]{2,1,0:T(8,128)(2,1)}, u32[]{:S(2)}, u32[]{:S(2)}) collective-permute-start(bf16[4,64,512]{2,1,0:T(8,128)(2,1)} %shard_map.97.refs_3_), channel_id=1, source_target_pairs={{4,8},{8,4},{12,16},{16,12},{20,24},{24,20},{5,9},{9,5},{13,17},{1... | collective-permute-start | bytes 786440 | tf_op jit(solution)/shard_map/ppermute | solution.py:33
  110.6 0.1 collective-permute-start.14
  110.6 7.8 %collective-permute-done.15.refs_9_ = bf16[4,64,512]{2,1,0:T(8,128)(2,1)} collective-permute-done((bf16[4,64,512]{2,1,0:T(8,128)(2,1)}, bf16[4,64,512]{2,1,0:T(8,128)(2,1)}, u32[]{:S(2)}, u32[]{:S(2)}) %collective-permute-start.15) | collective-permute-done | bytes 262176 | tf_op jit(solution)/shard_map/ppermute | solution.py:33
  118.4 6.8 %shard_map.98 = (bf16[256,1536]{1,0:T(8,128)(2,1)}, bf16[256,1536]{1,0:T(8,128)(2,1)}, bf16[256,1536]{1,0:T(8,128)(2,1)}, bf16[256,1536]{1,0:T(8,128)(2,1)}) custom-call(s32[3,4]{1,0:T(4,128)} %pad_add_fusion.refs_0_, bf16[4,64,1536]{2,1,0:T(8,128)(2,1)} %get-tuple-element.15.refs_1_, ...), custom_call_target="tpu_custom_call", output_to_operand_aliasing={{0}: (10, {}), {1}: (11, {}), {2}: (12, {}), {3}: (13, {})} | custom-call | flops 6000000000 | bytes 1 | tf_op jit(solution)/shard_map/pallas_call | solution.py:311
  (18 shorter events, 0.0 us)
Async XLA Ops:
  3.8 25.4 %collective-permute-start = (bf16[4,64,1024]{2,1,0:T(8,128)(2,1)}, bf16[4,64,1024]{2,1,0:T(8,128)(2,1)}, u32[]{:S(2)}, u32[]{:S(2)}) collective-permute-start(bf16[4,64,1024]{2,1,0:T(8,128)(2,1)} %get-tuple-element.18), channel_id=1, source_target_pairs={{0,2},{1,3},{2,0},{3,1},{4,6},{5,7},{6,4},{7,5},{8,10},{9,11},{10,... | collective-permute-start | bytes 1572872 | tf_op jit(solution)/shard_map/ppermute | solution.py:37
  6.2 27.2 %collective-permute-start.4 = (bf16[4,64,1024]{2,1,0:T(8,128)(2,1)}, bf16[4,64,1024]{2,1,0:T(8,128)(2,1)}, u32[]{:S(2)}, u32[]{:S(2)}) collective-permute-start(bf16[4,64,1024]{2,1,0:T(8,128)(2,1)} %get-tuple-element.21), channel_id=1, source_target_pairs={{0,1},{1,0},{2,3},{3,2},{4,5},{5,4},{6,7},{7,6},{8,9},{9,8},{10,11... | collective-permute-start | bytes 1572872 | tf_op jit(solution)/shard_map/ppermute | solution.py:37
  7.5 28.0 %collective-permute-start.6 = (bf16[4,64,1536]{2,1,0:T(8,128)(2,1)}, bf16[4,64,1536]{2,1,0:T(8,128)(2,1)}, u32[]{:S(2)}, u32[]{:S(2)}) collective-permute-start(bf16[4,64,1536]{2,1,0:T(8,128)(2,1)} %get-tuple-element.15.refs_1_), channel_id=1, source_target_pairs={{4,8},{8,4},{12,16},{16,12},{20,24},{24,20},{5,9},{9,5},{13,17},{1... | collective-permute-start | bytes 2359304 | tf_op jit(solution)/shard_map/ppermute | solution.py:33
  11.7 23.7 %collective-permute-start.5 = (bf16[4,64,1536]{2,1,0:T(8,128)(2,1)}, bf16[4,64,1536]{2,1,0:T(8,128)(2,1)}, u32[]{:S(2)}, u32[]{:S(2)}) collective-permute-start(bf16[4,64,1536]{2,1,0:T(8,128)(2,1)} %get-tuple-element.15.refs_1_), channel_id=1, source_target_pairs={{0,4},{4,0},{8,12},{12,8},{16,20},{20,16},{24,28},{28,24},{1,5},{5... | collective-permute-start | bytes 2359304 | tf_op jit(solution)/shard_map/ppermute | solution.py:33
  29.2 16.0 %collective-permute-start.1 = (bf16[4,64,1024]{2,1,0:T(8,128)(2,1)}, bf16[4,64,1024]{2,1,0:T(8,128)(2,1)}, u32[]{:S(2)}, u32[]{:S(2)}) collective-permute-start(bf16[4,64,1024]{2,1,0:T(8,128)(2,1)} %shard_map.85.refs_2_), channel_id=1, source_target_pairs={{0,3},{1,2},{2,1},{3,0},{4,7},{5,6},{6,5},{7,4},{8,11},{9,10},{10,... | collective-permute-start | bytes 1572872 | tf_op jit(solution)/shard_map/ppermute | solution.py:37
  35.5 33.3 %collective-permute-start.8 = (bf16[2,4,64,1024]{3,2,1,0:T(8,128)(2,1)}, bf16[2,4,64,1024]{3,2,1,0:T(8,128)(2,1)}, u32[]{:S(2)}, u32[]{:S(2)}) collective-permute-start(bf16[2,4,64,1024]{3,2,1,0:T(8,128)(2,1)} %shard_map.92.refs_2_), channel_id=1, source_target_pairs={{4,8},{8,4},{12,16},{16,12},{20,24},{24,20},{5,9},{9,5},{13,17},{1... | collective-permute-start | bytes 3145736 | tf_op jit(solution)/shard_map/ppermute | solution.py:33
  39.2 29.5 %collective-permute-start.7 = (bf16[2,4,64,1024]{3,2,1,0:T(8,128)(2,1)}, bf16[2,4,64,1024]{3,2,1,0:T(8,128)(2,1)}, u32[]{:S(2)}, u32[]{:S(2)}) collective-permute-start(bf16[2,4,64,1024]{3,2,1,0:T(8,128)(2,1)} %shard_map.92.refs_2_), channel_id=1, source_target_pairs={{0,4},{4,0},{8,12},{12,8},{16,20},{20,16},{24,28},{28,24},{1,5},{5... | collective-permute-start | bytes 3145736 | tf_op jit(solution)/shard_map/ppermute | solution.py:33
  45.1 21.7 %collective-permute-start.2 = (bf16[4,64,512]{2,1,0:T(8,128)(2,1)}, bf16[4,64,512]{2,1,0:T(8,128)(2,1)}, u32[]{:S(2)}, u32[]{:S(2)}) collective-permute-start(bf16[4,64,512]{2,1,0:T(8,128)(2,1)} %shard_map.86.refs_1_), channel_id=1, source_target_pairs={{0,1},{1,0},{2,3},{3,2},{4,5},{5,4},{6,7},{7,6},{8,9},{9,8},{10,11... | collective-permute-start | bytes 786440 | tf_op jit(solution)/shard_map/ppermute | solution.py:37
  55.1 10.2 %collective-permute-start.3 = (bf16[4,64,512]{2,1,0:T(8,128)(2,1)}, bf16[4,64,512]{2,1,0:T(8,128)(2,1)}, u32[]{:S(2)}, u32[]{:S(2)}) collective-permute-start(bf16[4,64,512]{2,1,0:T(8,128)(2,1)} %shard_map.87.refs_2_), channel_id=1, source_target_pairs={{0,2},{1,3},{2,0},{3,1},{4,6},{5,7},{6,4},{7,5},{8,10},{9,11},{10,... | collective-permute-start | bytes 786440 | tf_op jit(solution)/shard_map/ppermute | solution.py:37
  65.4 13.1 %collective-permute-start.11 = (bf16[4,64,512]{2,1,0:T(8,128)(2,1)}, bf16[4,64,512]{2,1,0:T(8,128)(2,1)}, u32[]{:S(2)}, u32[]{:S(2)}) collective-permute-start(bf16[4,64,512]{2,1,0:T(8,128)(2,1)} %shard_map.88.refs_2_), channel_id=1, source_target_pairs={{0,3},{1,2},{2,1},{3,0},{4,7},{5,6},{6,5},{7,4},{8,11},{9,10},{10,... | collective-permute-start | bytes 786440 | tf_op jit(solution)/shard_map/ppermute | solution.py:37
  68.8 21.5 %collective-permute-start.10 = (bf16[4,64,1024]{2,1,0:T(8,128)(2,1)}, bf16[4,64,1024]{2,1,0:T(8,128)(2,1)}, u32[]{:S(2)}, u32[]{:S(2)}) collective-permute-start(bf16[4,64,1024]{2,1,0:T(8,128)(2,1)} %shard_map.93.refs_3_), channel_id=1, source_target_pairs={{4,8},{8,4},{12,16},{16,12},{20,24},{24,20},{5,9},{9,5},{13,17},{1... | collective-permute-start | bytes 1572872 | tf_op jit(solution)/shard_map/ppermute | solution.py:33
  78.4 11.9 %collective-permute-start.9 = (bf16[4,64,1024]{2,1,0:T(8,128)(2,1)}, bf16[4,64,1024]{2,1,0:T(8,128)(2,1)}, u32[]{:S(2)}, u32[]{:S(2)}) collective-permute-start(bf16[4,64,1024]{2,1,0:T(8,128)(2,1)} %shard_map.93.refs_3_), channel_id=1, source_target_pairs={{0,4},{4,0},{8,12},{12,8},{16,20},{20,16},{24,28},{28,24},{1,5},{5... | collective-permute-start | bytes 1572872 | tf_op jit(solution)/shard_map/ppermute | solution.py:33
  90.3 17.3 %collective-permute-start.13 = (bf16[2,4,64,512]{3,2,1,0:T(8,128)(2,1)}, bf16[2,4,64,512]{3,2,1,0:T(8,128)(2,1)}, u32[]{:S(2)}, u32[]{:S(2)}) collective-permute-start(bf16[2,4,64,512]{3,2,1,0:T(8,128)(2,1)} %shard_map.94.refs_2_), channel_id=1, source_target_pairs={{4,8},{8,4},{12,16},{16,12},{20,24},{24,20},{5,9},{9,5},{13,17},{1... | collective-permute-start | bytes 1572872 | tf_op jit(solution)/shard_map/ppermute | solution.py:33
  94.8 12.8 %collective-permute-start.12 = (bf16[2,4,64,512]{3,2,1,0:T(8,128)(2,1)}, bf16[2,4,64,512]{3,2,1,0:T(8,128)(2,1)}, u32[]{:S(2)}, u32[]{:S(2)}) collective-permute-start(bf16[2,4,64,512]{3,2,1,0:T(8,128)(2,1)} %shard_map.94.refs_2_), channel_id=1, source_target_pairs={{0,4},{4,0},{8,12},{12,8},{16,20},{20,16},{24,28},{28,24},{1,5},{5... | collective-permute-start | bytes 1572872 | tf_op jit(solution)/shard_map/ppermute | solution.py:33
  107.6 10.8 %collective-permute-start.15 = (bf16[4,64,512]{2,1,0:T(8,128)(2,1)}, bf16[4,64,512]{2,1,0:T(8,128)(2,1)}, u32[]{:S(2)}, u32[]{:S(2)}) collective-permute-start(bf16[4,64,512]{2,1,0:T(8,128)(2,1)} %shard_map.97.refs_3_), channel_id=1, source_target_pairs={{4,8},{8,4},{12,16},{16,12},{20,24},{24,20},{5,9},{9,5},{13,17},{1... | collective-permute-start | bytes 786440 | tf_op jit(solution)/shard_map/ppermute | solution.py:33
  110.6 7.9 %collective-permute-start.14 = (bf16[4,64,512]{2,1,0:T(8,128)(2,1)}, bf16[4,64,512]{2,1,0:T(8,128)(2,1)}, u32[]{:S(2)}, u32[]{:S(2)}) collective-permute-start(bf16[4,64,512]{2,1,0:T(8,128)(2,1)} %shard_map.97.refs_3_), channel_id=1, source_target_pairs={{0,4},{4,0},{8,12},{12,8},{16,20},{20,16},{24,28},{28,24},{1,5},{5... | collective-permute-start | bytes 786440 | tf_op jit(solution)/shard_map/ppermute | solution.py:33

commit v14 on v13

--- a/solution.py
+++ b/solution.py
@@ -15,7 +15,7 @@
 GROUPS = ((8,), (4,))
 VMEM_LIMIT = 64 * 1024 * 1024 - 256 * 1024
 ATTEND_FLOPS = 1_500_000_000
-LARGE_COST = pl.CostEstimate(flops=40_000_000_000, bytes_accessed=1, transcendentals=0)
+FLOPS_PER_BYTE = 62_500
 SMALL_COST = pl.CostEstimate(flops=1, bytes_accessed=1, transcendentals=0)
 
 
@@ -116,7 +116,7 @@
         store.wait()
 
 
-def join(received, after):
+def join(received, after, cost):
     pieces = len(received)
     shape = (pieces,) + received[0].shape
     return pl.pallas_call(
@@ -130,7 +130,7 @@
             pltpu.SemaphoreType.DMA((pieces,)),
         ],
         compiler_params=pltpu.CompilerParams(vmem_limit_bytes=VMEM_LIMIT),
-        cost_estimate=LARGE_COST,
+        cost_estimate=cost,
     )(*received, *after)
 
 
@@ -334,6 +334,11 @@
     )(image_ids, *pieces, *(outs or ()))
 
 
+def between(sent, received):
+    size = 2 * sent.size - received.size
+    return pl.CostEstimate(flops=FLOPS_PER_BYTE * size, bytes_accessed=1, transcendentals=0)
+
+
 def shards(queries, key_vectors, value_vectors, grad_output, image_ids):
     arrays = (queries, key_vectors, value_vectors, grad_output)
     parts = lax.axis_size("tensor")
@@ -377,11 +382,12 @@
                 held, crossed = cross(steps[number], [received[-1]])
             elif outs is not None:
                 after.append(outs[0])
+            cost = between(sent[-1][0], received[0])
             if place == 0:
-                joined = spread(hold(join(received, held), after))
+                joined = spread(hold(join(received, held, cost), after))
                 sent.append(joined)
                 continue
-            piece = spread(hold(hold(received[0], held, LARGE_COST), after))
+            piece = spread(hold(hold(received[0], held, cost), after))
             sent.append(piece)
             first_head, count = chunks[place - 1]
             offsets = (first_head, first_head - span[0], 0)

time: 126 us -> 126 us (level)
  no operation moved by 1% of the time
where the time goes in v14:
time: 126 us; the launch traced here: 125 us
  waiting for transfers between devices  53.2 us (42%)
  starting transfers between devices  44.9 us (36%)
  Pallas kernels  24.9 us (20%)
    ppermute x6, waiting for transfers between devices, swap_flipped(): lax.ppermute(block, axis, [(i, i ^ flip) for i in range(lax.axis_size(axi...  31.9 us
    ppermute x10, starting transfers between devices, swap_pairs(): return lax.ppermute(block, axis, route)  25.4 us
    ppermute x10, waiting for transfers between devices, swap_pairs(): return lax.ppermute(block, axis, route)  21.3 us
    ppermute x6, starting transfers between devices, swap_flipped(): lax.ppermute(block, axis, [(i, i ^ flip) for i in range(lax.axis_size(axi...  19.4 us
    pallas_call x2, Pallas kernels, attend(): pl.pallas_call(functools.partial(attend_kernel, parts, part_rows, steps,...  17.8 us
    pallas_call x2, Pallas kernels, join(): pl.pallas_call(functools.partial(join_kernel, pieces), out_shape=jax.Shap...  3.88 us
    pallas_call x1, Pallas kernels, pack(): pl.pallas_call(functools.partial(pack_kernel, stride, jobs), out_shape=[j...  3.16 us
  transfers between devices with their start and end apart: 16, of which 6 were waited for; matrix products, arithmetic and copies ran while one was open for 1% of the time, Pallas kernels for 12%

profile of v14, /device:TPU:3, one launch (start us, length us, event | category | flops | bytes accessed | tf_op | source)
XLA Modules:
  0.0 125.4 jit_solution(5073189735751631996)
XLA Ops:
  0.6 3.2 %shard_map.84 = (bf16[4,64,1024]{2,1,0:T(8,128)(2,1)}, bf16[4,64,1024]{2,1,0:T(8,128)(2,1)}, bf16[4,64,1536]{2,1,0:T(8,128)(2,1)}, bf16[4,64,1024]{2,1,0:T(8,128...) custom-call(bf16[64,6144]{1,0:T(8,128)(2,1)} %refs_0_.1, ...), custom_call_target="tpu_custom_call" | custom-call | flops 1 | bytes 1 | tf_op jit(solution)/shard_map/pallas_call | solution.py:86
  3.8 2.4 %collective-permute-start = (bf16[4,64,1024]{2,1,0:T(8,128)(2,1)}, bf16[4,64,1024]{2,1,0:T(8,128)(2,1)}, u32[]{:S(2)}, u32[]{:S(2)}) collective-permute-start(bf16[4,64,1024]{2,1,0:T(8,128)(2,1)} %get-tuple-element.18), channel_id=1, source_target_pairs={{0,2},{1,3},{2,0},{3,1},{4,6},{5,7},{6,4},{7,5},{8,10},{9,11},{10,... | collective-permute-start | bytes 1572872 | tf_op jit(solution)/shard_map/ppermute | solution.py:37
  6.2 1.3 %collective-permute-start.4 = (bf16[4,64,1024]{2,1,0:T(8,128)(2,1)}, bf16[4,64,1024]{2,1,0:T(8,128)(2,1)}, u32[]{:S(2)}, u32[]{:S(2)}) collective-permute-start(bf16[4,64,1024]{2,1,0:T(8,128)(2,1)} %get-tuple-element.21), channel_id=1, source_target_pairs={{0,1},{1,0},{2,3},{3,2},{4,5},{5,4},{6,7},{7,6},{8,9},{9,8},{10,11... | collective-permute-start | bytes 1572872 | tf_op jit(solution)/shard_map/ppermute | solution.py:37
  7.5 4.2 %collective-permute-start.6 = (bf16[4,64,1536]{2,1,0:T(8,128)(2,1)}, bf16[4,64,1536]{2,1,0:T(8,128)(2,1)}, u32[]{:S(2)}, u32[]{:S(2)}) collective-permute-start(bf16[4,64,1536]{2,1,0:T(8,128)(2,1)} %get-tuple-element.15.refs_1_), channel_id=1, source_target_pairs={{4,8},{8,4},{12,16},{16,12},{20,24},{24,20},{5,9},{9,5},{13,17},{1... | collective-permute-start | bytes 2359304 | tf_op jit(solution)/shard_map/ppermute | solution.py:33
  11.7 0.1 collective-permute-start.5
  11.8 0.8 slice.3
  12.6 0.1 dynamic-slice_bitcast_fusion.2
  12.7 0.6 pad_add_fusion.refs_0_
  13.3 15.9 %collective-permute-done.refs_1_ = bf16[4,64,1024]{2,1,0:T(8,128)(2,1)} collective-permute-done((bf16[4,64,1024]{2,1,0:T(8,128)(2,1)}, bf16[4,64,1024]{2,1,0:T(8,128)(2,1)}, u32[]{:S(2)}, u32[]{:S(2)}) %collective-permute-start) | collective-permute-done | bytes 524320 | tf_op jit(solution)/shard_map/ppermute | solution.py:37
  29.2 4.2 %collective-permute-start.1 = (bf16[4,64,1024]{2,1,0:T(8,128)(2,1)}, bf16[4,64,1024]{2,1,0:T(8,128)(2,1)}, u32[]{:S(2)}, u32[]{:S(2)}) collective-permute-start(bf16[4,64,1024]{2,1,0:T(8,128)(2,1)} %shard_map.85.refs_2_), channel_id=1, source_target_pairs={{0,3},{1,2},{2,1},{3,0},{4,7},{5,6},{6,5},{7,4},{8,11},{9,10},{10,... | collective-permute-start | bytes 1572872 | tf_op jit(solution)/shard_map/ppermute | solution.py:37
  33.4 0.0 collective-permute-done.4.refs_0_
  33.4 2.0 %shard_map.91.refs_0_ = bf16[2,4,64,1024]{3,2,1,0:T(8,128)(2,1)} custom-call(bf16[4,64,1024]{2,1,0:T(8,128)(2,1)} %collective-permute-done.4.refs_0_, bf16[4,64,1024]{2,1,0:T(8,128)(2,1)} %collective-permute-done.refs_1_, bf16[4,64,1024]{2,1,0:T(8,128)(2,1)} %shard_map.85.refs_2_), custom_call_target="tpu_custom_call" | custom-call | flops 32768000000 | bytes 1 | tf_op jit(solution)/shard_map/pallas_call | solution.py:122
  35.4 0.0 collective-permute-done.6.refs_2_.refs_7_
  35.5 3.8 %collective-permute-start.8 = (bf16[2,4,64,1024]{3,2,1,0:T(8,128)(2,1)}, bf16[2,4,64,1024]{3,2,1,0:T(8,128)(2,1)}, u32[]{:S(2)}, u32[]{:S(2)}) collective-permute-start(bf16[2,4,64,1024]{3,2,1,0:T(8,128)(2,1)} %shard_map.92.refs_2_), channel_id=1, source_target_pairs={{4,8},{8,4},{12,16},{16,12},{20,24},{24,20},{5,9},{9,5},{13,17},{1... | collective-permute-start | bytes 3145736 | tf_op jit(solution)/shard_map/ppermute | solution.py:33
  39.2 0.1 collective-permute-start.7
  39.3 5.8 %collective-permute-done.1.refs_1_.refs_0_ = bf16[4,64,1024]{2,1,0:T(8,128)(2,1)} collective-permute-done((bf16[4,64,1024]{2,1,0:T(8,128)(2,1)}, bf16[4,64,1024]{2,1,0:T(8,128)(2,1)}, u32[]{:S(2)}, u32[]{:S(2)}) %collective-permute-start.1) | collective-permute-done | bytes 524320 | tf_op jit(solution)/shard_map/ppermute | solution.py:37
  45.1 10.0 %collective-permute-start.2 = (bf16[4,64,512]{2,1,0:T(8,128)(2,1)}, bf16[4,64,512]{2,1,0:T(8,128)(2,1)}, u32[]{:S(2)}, u32[]{:S(2)}) collective-permute-start(bf16[4,64,512]{2,1,0:T(8,128)(2,1)} %shard_map.86.refs_1_), channel_id=1, source_target_pairs={{0,1},{1,0},{2,3},{3,2},{4,5},{5,4},{6,7},{7,6},{8,9},{9,8},{10,11... | collective-permute-start | bytes 786440 | tf_op jit(solution)/shard_map/ppermute | solution.py:37
  55.1 0.0 collective-permute-start.3
  55.2 10.2 %collective-permute-done.3.refs_1_ = bf16[4,64,512]{2,1,0:T(8,128)(2,1)} collective-permute-done((bf16[4,64,512]{2,1,0:T(8,128)(2,1)}, bf16[4,64,512]{2,1,0:T(8,128)(2,1)}, u32[]{:S(2)}, u32[]{:S(2)}) %collective-permute-start.3) | collective-permute-done | bytes 262176 | tf_op jit(solution)/shard_map/ppermute | solution.py:37
  65.4 1.5 %collective-permute-start.11 = (bf16[4,64,512]{2,1,0:T(8,128)(2,1)}, bf16[4,64,512]{2,1,0:T(8,128)(2,1)}, u32[]{:S(2)}, u32[]{:S(2)}) collective-permute-start(bf16[4,64,512]{2,1,0:T(8,128)(2,1)} %shard_map.88.refs_2_), channel_id=1, source_target_pairs={{0,3},{1,2},{2,1},{3,0},{4,7},{5,6},{6,5},{7,4},{8,11},{9,10},{10,... | collective-permute-start | bytes 786440 | tf_op jit(solution)/shard_map/ppermute | solution.py:37
  66.9 1.8 %shard_map.89.refs_0_ = bf16[2,4,64,512]{3,2,1,0:T(8,128)(2,1)} custom-call(bf16[4,64,512]{2,1,0:T(8,128)(2,1)} %collective-permute-done.2.refs_0_, bf16[4,64,512]{2,1,0:T(8,128)(2,1)} %collective-permute-done.3.refs_1_, bf16[4,64,512]{2,1,0:T(8,128)(2,1)} %shard_map.88.refs_2_), custom_call_target="tpu_custom_call" | custom-call | flops 24576000000 | bytes 1 | tf_op jit(solution)/shard_map/pallas_call | solution.py:122
  68.8 9.6 %collective-permute-start.10 = (bf16[4,64,1024]{2,1,0:T(8,128)(2,1)}, bf16[4,64,1024]{2,1,0:T(8,128)(2,1)}, u32[]{:S(2)}, u32[]{:S(2)}) collective-permute-start(bf16[4,64,1024]{2,1,0:T(8,128)(2,1)} %shard_map.93.refs_3_), channel_id=1, source_target_pairs={{4,8},{8,4},{12,16},{16,12},{20,24},{24,20},{5,9},{9,5},{13,17},{1... | collective-permute-start | bytes 1572872 | tf_op jit(solution)/shard_map/ppermute | solution.py:33
  78.4 0.1 collective-permute-start.9
  78.5 11.8 %collective-permute-done.10.refs_2_.refs_9_ = bf16[4,64,1024]{2,1,0:T(8,128)(2,1)} collective-permute-done((bf16[4,64,1024]{2,1,0:T(8,128)(2,1)}, bf16[4,64,1024]{2,1,0:T(8,128)(2,1)}, u32[]{:S(2)}, u32[]{:S(2)}) %collective-permute-start.10) | collective-permute-done | bytes 524320 | tf_op jit(solution)/shard_map/ppermute | solution.py:33
  90.3 4.5 %collective-permute-start.13 = (bf16[2,4,64,512]{3,2,1,0:T(8,128)(2,1)}, bf16[2,4,64,512]{3,2,1,0:T(8,128)(2,1)}, u32[]{:S(2)}, u32[]{:S(2)}) collective-permute-start(bf16[2,4,64,512]{3,2,1,0:T(8,128)(2,1)} %shard_map.94.refs_2_), channel_id=1, source_target_pairs={{4,8},{8,4},{12,16},{16,12},{20,24},{24,20},{5,9},{9,5},{13,17},{1... | collective-permute-start | bytes 1572872 | tf_op jit(solution)/shard_map/ppermute | solution.py:33
  94.8 0.1 collective-permute-start.12
  94.9 11.0 %shard_map.96 = (bf16[256,1536]{1,0:T(8,128)(2,1)}, bf16[256,1536]{1,0:T(8,128)(2,1)}, bf16[256,1536]{1,0:T(8,128)(2,1)}, bf16[256,1536]{1,0:T(8,128)(2,1)}) custom-call(s32[3,4]{1,0:T(4,128)} %pad_add_fusion.refs_0_, bf16[4,64,1536]{2,1,0:T(8,128)(2,1)} %get-tuple-element.15.refs_1_, bf16[2,4,64,1024]{3,2,1,0:T(8,128)(2,1)} %shard_map.92.refs_2_, ...), custom_call_target="tpu_custom_call" | custom-call | flops 12000000000 | bytes 1 | tf_op jit(solution)/shard_map/pallas_call | solution.py:311
  105.9 1.7 %collective-permute-done.13.refs_2_.refs_8_ = bf16[2,4,64,512]{3,2,1,0:T(8,128)(2,1)} collective-permute-done((bf16[2,4,64,512]{3,2,1,0:T(8,128)(2,1)}, bf16[2,4,64,512]{3,2,1,0:T(8,128)(2,1)}, u32[]{:S(2)}, u32[]{:S(2)}) %collective-permute-start.13) | collective-permute-done | bytes 524320 | tf_op jit(solution)/shard_map/ppermute | solution.py:33
  107.6 2.9 %collective-permute-start.15 = (bf16[4,64,512]{2,1,0:T(8,128)(2,1)}, bf16[4,64,512]{2,1,0:T(8,128)(2,1)}, u32[]{:S(2)}, u32[]{:S(2)}) collective-permute-start(bf16[4,64,512]{2,1,0:T(8,128)(2,1)} %shard_map.97.refs_3_), channel_id=1, source_target_pairs={{4,8},{8,4},{12,16},{16,12},{20,24},{24,20},{5,9},{9,5},{13,17},{1... | collective-permute-start | bytes 786440 | tf_op jit(solution)/shard_map/ppermute | solution.py:33
  110.6 0.1 collective-permute-start.14
  110.6 7.8 %collective-permute-done.15.refs_9_ = bf16[4,64,512]{2,1,0:T(8,128)(2,1)} collective-permute-done((bf16[4,64,512]{2,1,0:T(8,128)(2,1)}, bf16[4,64,512]{2,1,0:T(8,128)(2,1)}, u32[]{:S(2)}, u32[]{:S(2)}) %collective-permute-start.15) | collective-permute-done | bytes 262176 | tf_op jit(solution)/shard_map/ppermute | solution.py:33
  118.4 6.8 %shard_map.98 = (bf16[256,1536]{1,0:T(8,128)(2,1)}, bf16[256,1536]{1,0:T(8,128)(2,1)}, bf16[256,1536]{1,0:T(8,128)(2,1)}, bf16[256,1536]{1,0:T(8,128)(2,1)}) custom-call(s32[3,4]{1,0:T(4,128)} %pad_add_fusion.refs_0_, bf16[4,64,1536]{2,1,0:T(8,128)(2,1)} %get-tuple-element.15.refs_1_, ...), custom_call_target="tpu_custom_call", output_to_operand_aliasing={{0}: (10, {}), {1}: (11, {}), {2}: (12, {}), {3}: (13, {})} | custom-call | flops 6000000000 | bytes 1 | tf_op jit(solution)/shard_map/pallas_call | solution.py:311
  (18 shorter events, 0.0 us)
Async XLA Ops:
  3.8 25.4 %collective-permute-start = (bf16[4,64,1024]{2,1,0:T(8,128)(2,1)}, bf16[4,64,1024]{2,1,0:T(8,128)(2,1)}, u32[]{:S(2)}, u32[]{:S(2)}) collective-permute-start(bf16[4,64,1024]{2,1,0:T(8,128)(2,1)} %get-tuple-element.18), channel_id=1, source_target_pairs={{0,2},{1,3},{2,0},{3,1},{4,6},{5,7},{6,4},{7,5},{8,10},{9,11},{10,... | collective-permute-start | bytes 1572872 | tf_op jit(solution)/shard_map/ppermute | solution.py:37
  6.2 27.2 %collective-permute-start.4 = (bf16[4,64,1024]{2,1,0:T(8,128)(2,1)}, bf16[4,64,1024]{2,1,0:T(8,128)(2,1)}, u32[]{:S(2)}, u32[]{:S(2)}) collective-permute-start(bf16[4,64,1024]{2,1,0:T(8,128)(2,1)} %get-tuple-element.21), channel_id=1, source_target_pairs={{0,1},{1,0},{2,3},{3,2},{4,5},{5,4},{6,7},{7,6},{8,9},{9,8},{10,11... | collective-permute-start | bytes 1572872 | tf_op jit(solution)/shard_map/ppermute | solution.py:37
  7.5 28.0 %collective-permute-start.6 = (bf16[4,64,1536]{2,1,0:T(8,128)(2,1)}, bf16[4,64,1536]{2,1,0:T(8,128)(2,1)}, u32[]{:S(2)}, u32[]{:S(2)}) collective-permute-start(bf16[4,64,1536]{2,1,0:T(8,128)(2,1)} %get-tuple-element.15.refs_1_), channel_id=1, source_target_pairs={{4,8},{8,4},{12,16},{16,12},{20,24},{24,20},{5,9},{9,5},{13,17},{1... | collective-permute-start | bytes 2359304 | tf_op jit(solution)/shard_map/ppermute | solution.py:33
  11.7 23.7 %collective-permute-start.5 = (bf16[4,64,1536]{2,1,0:T(8,128)(2,1)}, bf16[4,64,1536]{2,1,0:T(8,128)(2,1)}, u32[]{:S(2)}, u32[]{:S(2)}) collective-permute-start(bf16[4,64,1536]{2,1,0:T(8,128)(2,1)} %get-tuple-element.15.refs_1_), channel_id=1, source_target_pairs={{0,4},{4,0},{8,12},{12,8},{16,20},{20,16},{24,28},{28,24},{1,5},{5... | collective-permute-start | bytes 2359304 | tf_op jit(solution)/shard_map/ppermute | solution.py:33
  29.2 16.0 %collective-permute-start.1 = (bf16[4,64,1024]{2,1,0:T(8,128)(2,1)}, bf16[4,64,1024]{2,1,0:T(8,128)(2,1)}, u32[]{:S(2)}, u32[]{:S(2)}) collective-permute-start(bf16[4,64,1024]{2,1,0:T(8,128)(2,1)} %shard_map.85.refs_2_), channel_id=1, source_target_pairs={{0,3},{1,2},{2,1},{3,0},{4,7},{5,6},{6,5},{7,4},{8,11},{9,10},{10,... | collective-permute-start | bytes 1572872 | tf_op jit(solution)/shard_map/ppermute | solution.py:37
  35.5 33.3 %collective-permute-start.8 = (bf16[2,4,64,1024]{3,2,1,0:T(8,128)(2,1)}, bf16[2,4,64,1024]{3,2,1,0:T(8,128)(2,1)}, u32[]{:S(2)}, u32[]{:S(2)}) collective-permute-start(bf16[2,4,64,1024]{3,2,1,0:T(8,128)(2,1)} %shard_map.92.refs_2_), channel_id=1, source_target_pairs={{4,8},{8,4},{12,16},{16,12},{20,24},{24,20},{5,9},{9,5},{13,17},{1... | collective-permute-start | bytes 3145736 | tf_op jit(solution)/shard_map/ppermute | solution.py:33
  39.2 29.5 %collective-permute-start.7 = (bf16[2,4,64,1024]{3,2,1,0:T(8,128)(2,1)}, bf16[2,4,64,1024]{3,2,1,0:T(8,128)(2,1)}, u32[]{:S(2)}, u32[]{:S(2)}) collective-permute-start(bf16[2,4,64,1024]{3,2,1,0:T(8,128)(2,1)} %shard_map.92.refs_2_), channel_id=1, source_target_pairs={{0,4},{4,0},{8,12},{12,8},{16,20},{20,16},{24,28},{28,24},{1,5},{5... | collective-permute-start | bytes 3145736 | tf_op jit(solution)/shard_map/ppermute | solution.py:33
  45.1 21.7 %collective-permute-start.2 = (bf16[4,64,512]{2,1,0:T(8,128)(2,1)}, bf16[4,64,512]{2,1,0:T(8,128)(2,1)}, u32[]{:S(2)}, u32[]{:S(2)}) collective-permute-start(bf16[4,64,512]{2,1,0:T(8,128)(2,1)} %shard_map.86.refs_1_), channel_id=1, source_target_pairs={{0,1},{1,0},{2,3},{3,2},{4,5},{5,4},{6,7},{7,6},{8,9},{9,8},{10,11... | collective-permute-start | bytes 786440 | tf_op jit(solution)/shard_map/ppermute | solution.py:37
  55.1 10.2 %collective-permute-start.3 = (bf16[4,64,512]{2,1,0:T(8,128)(2,1)}, bf16[4,64,512]{2,1,0:T(8,128)(2,1)}, u32[]{:S(2)}, u32[]{:S(2)}) collective-permute-start(bf16[4,64,512]{2,1,0:T(8,128)(2,1)} %shard_map.87.refs_2_), channel_id=1, source_target_pairs={{0,2},{1,3},{2,0},{3,1},{4,6},{5,7},{6,4},{7,5},{8,10},{9,11},{10,... | collective-permute-start | bytes 786440 | tf_op jit(solution)/shard_map/ppermute | solution.py:37
  65.4 13.1 %collective-permute-start.11 = (bf16[4,64,512]{2,1,0:T(8,128)(2,1)}, bf16[4,64,512]{2,1,0:T(8,128)(2,1)}, u32[]{:S(2)}, u32[]{:S(2)}) collective-permute-start(bf16[4,64,512]{2,1,0:T(8,128)(2,1)} %shard_map.88.refs_2_), channel_id=1, source_target_pairs={{0,3},{1,2},{2,1},{3,0},{4,7},{5,6},{6,5},{7,4},{8,11},{9,10},{10,... | collective-permute-start | bytes 786440 | tf_op jit(solution)/shard_map/ppermute | solution.py:37
  68.8 21.5 %collective-permute-start.10 = (bf16[4,64,1024]{2,1,0:T(8,128)(2,1)}, bf16[4,64,1024]{2,1,0:T(8,128)(2,1)}, u32[]{:S(2)}, u32[]{:S(2)}) collective-permute-start(bf16[4,64,1024]{2,1,0:T(8,128)(2,1)} %shard_map.93.refs_3_), channel_id=1, source_target_pairs={{4,8},{8,4},{12,16},{16,12},{20,24},{24,20},{5,9},{9,5},{13,17},{1... | collective-permute-start | bytes 1572872 | tf_op jit(solution)/shard_map/ppermute | solution.py:33
  78.4 11.9 %collective-permute-start.9 = (bf16[4,64,1024]{2,1,0:T(8,128)(2,1)}, bf16[4,64,1024]{2,1,0:T(8,128)(2,1)}, u32[]{:S(2)}, u32[]{:S(2)}) collective-permute-start(bf16[4,64,1024]{2,1,0:T(8,128)(2,1)} %shard_map.93.refs_3_), channel_id=1, source_target_pairs={{0,4},{4,0},{8,12},{12,8},{16,20},{20,16},{24,28},{28,24},{1,5},{5... | collective-permute-start | bytes 1572872 | tf_op jit(solution)/shard_map/ppermute | solution.py:33
  90.3 17.3 %collective-permute-start.13 = (bf16[2,4,64,512]{3,2,1,0:T(8,128)(2,1)}, bf16[2,4,64,512]{3,2,1,0:T(8,128)(2,1)}, u32[]{:S(2)}, u32[]{:S(2)}) collective-permute-start(bf16[2,4,64,512]{3,2,1,0:T(8,128)(2,1)} %shard_map.94.refs_2_), channel_id=1, source_target_pairs={{4,8},{8,4},{12,16},{16,12},{20,24},{24,20},{5,9},{9,5},{13,17},{1... | collective-permute-start | bytes 1572872 | tf_op jit(solution)/shard_map/ppermute | solution.py:33
  94.8 12.8 %collective-permute-start.12 = (bf16[2,4,64,512]{3,2,1,0:T(8,128)(2,1)}, bf16[2,4,64,512]{3,2,1,0:T(8,128)(2,1)}, u32[]{:S(2)}, u32[]{:S(2)}) collective-permute-start(bf16[2,4,64,512]{3,2,1,0:T(8,128)(2,1)} %shard_map.94.refs_2_), channel_id=1, source_target_pairs={{0,4},{4,0},{8,12},{12,8},{16,20},{20,16},{24,28},{28,24},{1,5},{5... | collective-permute-start | bytes 1572872 | tf_op jit(solution)/shard_map/ppermute | solution.py:33
  107.6 10.8 %collective-permute-start.15 = (bf16[4,64,512]{2,1,0:T(8,128)(2,1)}, bf16[4,64,512]{2,1,0:T(8,128)(2,1)}, u32[]{:S(2)}, u32[]{:S(2)}) collective-permute-start(bf16[4,64,512]{2,1,0:T(8,128)(2,1)} %shard_map.97.refs_3_), channel_id=1, source_target_pairs={{4,8},{8,4},{12,16},{16,12},{20,24},{24,20},{5,9},{9,5},{13,17},{1... | collective-permute-start | bytes 786440 | tf_op jit(solution)/shard_map/ppermute | solution.py:33
  110.6 7.9 %collective-permute-start.14 = (bf16[4,64,512]{2,1,0:T(8,128)(2,1)}, bf16[4,64,512]{2,1,0:T(8,128)(2,1)}, u32[]{:S(2)}, u32[]{:S(2)}) collective-permute-start(bf16[4,64,512]{2,1,0:T(8,128)(2,1)} %shard_map.97.refs_3_), channel_id=1, source_target_pairs={{0,4},{4,0},{8,12},{12,8},{16,20},{20,16},{24,28},{28,24},{1,5},{5... | collective-permute-start | bytes 786440 | tf_op jit(solution)/shard_map/ppermute | solution.py:33

commit v15 on v14

--- a/solution.py
+++ b/solution.py
@@ -383,6 +383,7 @@
             elif outs is not None:
                 after.append(outs[0])
             cost = between(sent[-1][0], received[0])
+            held.append(sent[-1][0])
             if place == 0:
                 joined = spread(hold(join(received, held, cost), after))
                 sent.append(joined)

time: 126 us -> 124 us (0.984)
  waiting for transfers between devices: 53.2 us -> 51.3 us
    ppermute x10, waiting for transfers between devices: 21.3 us -> 19.4 us  [swap_pairs(): return lax.ppermute(block, axis, route)]
where the time goes in v15:
time: 124 us
  waiting for transfers between devices  51.3 us (41%)
  starting transfers between devices  44.9 us (36%)
  Pallas kernels  24.9 us (20%)
    ppermute x6, waiting for transfers between devices, swap_flipped(): lax.ppermute(block, axis, [(i, i ^ flip) for i in range(lax.axis_size(axi...  31.9 us
    ppermute x10, starting transfers between devices, swap_pairs(): return lax.ppermute(block, axis, route)  25.5 us
    ppermute x6, starting transfers between devices, swap_flipped(): lax.ppermute(block, axis, [(i, i ^ flip) for i in range(lax.axis_size(axi...  19.4 us
    ppermute x10, waiting for transfers between devices, swap_pairs(): return lax.ppermute(block, axis, route)  19.4 us
    pallas_call x2, Pallas kernels, attend(): pl.pallas_call(functools.partial(attend_kernel, parts, part_rows, steps,...  17.9 us
    pallas_call x2, Pallas kernels, join(): pl.pallas_call(functools.partial(join_kernel, pieces), out_shape=jax.Shap...  3.88 us
    pallas_call x1, Pallas kernels, pack(): pl.pallas_call(functools.partial(pack_kernel, stride, jobs), out_shape=[j...  3.16 us
  transfers between devices with their start and end apart: 16, of which 6 were waited for; matrix products, arithmetic and copies ran while one was open for 1% of the time, Pallas kernels for 12%

profile of v15, /device:TPU:3, one launch (start us, length us, event | category | flops | bytes accessed | tf_op | source)
XLA Modules:
  0.0 123.6 jit_solution(15533378374472220904)
XLA Ops:
  0.6 3.2 %shard_map.84 = (bf16[4,64,1024]{2,1,0:T(8,128)(2,1)}, bf16[4,64,1024]{2,1,0:T(8,128)(2,1)}, bf16[4,64,1536]{2,1,0:T(8,128)(2,1)}, bf16[4,64,1024]{2,1,0:T(8,128...) custom-call(bf16[64,6144]{1,0:T(8,128)(2,1)} %refs_0_.1, ...), custom_call_target="tpu_custom_call" | custom-call | flops 1 | bytes 1 | tf_op jit(solution)/shard_map/pallas_call | solution.py:86
  3.8 2.4 %collective-permute-start = (bf16[4,64,1024]{2,1,0:T(8,128)(2,1)}, bf16[4,64,1024]{2,1,0:T(8,128)(2,1)}, u32[]{:S(2)}, u32[]{:S(2)}) collective-permute-start(bf16[4,64,1024]{2,1,0:T(8,128)(2,1)} %get-tuple-element.18), channel_id=1, source_target_pairs={{0,2},{1,3},{2,0},{3,1},{4,6},{5,7},{6,4},{7,5},{8,10},{9,11},{10,... | collective-permute-start | bytes 1572872 | tf_op jit(solution)/shard_map/ppermute | solution.py:37
  6.2 1.3 %collective-permute-start.4 = (bf16[4,64,1024]{2,1,0:T(8,128)(2,1)}, bf16[4,64,1024]{2,1,0:T(8,128)(2,1)}, u32[]{:S(2)}, u32[]{:S(2)}) collective-permute-start(bf16[4,64,1024]{2,1,0:T(8,128)(2,1)} %get-tuple-element.21), channel_id=1, source_target_pairs={{0,1},{1,0},{2,3},{3,2},{4,5},{5,4},{6,7},{7,6},{8,9},{9,8},{10,11... | collective-permute-start | bytes 1572872 | tf_op jit(solution)/shard_map/ppermute | solution.py:37
  7.5 4.2 %collective-permute-start.6 = (bf16[4,64,1536]{2,1,0:T(8,128)(2,1)}, bf16[4,64,1536]{2,1,0:T(8,128)(2,1)}, u32[]{:S(2)}, u32[]{:S(2)}) collective-permute-start(bf16[4,64,1536]{2,1,0:T(8,128)(2,1)} %get-tuple-element.15.refs_3_.refs_1_), channel_id=1, source_target_pairs={{4,8},{8,4},{12,16},{16,12},{20,24},{24,20},{5,9},{9,5},{13,17},{1... | collective-permute-start | bytes 2359304 | tf_op jit(solution)/shard_map/ppermute | solution.py:33
  11.7 0.1 collective-permute-start.5
  11.8 0.8 slice.3
  12.6 0.1 dynamic-slice_bitcast_fusion.2
  12.7 0.6 pad_add_fusion.refs_0_
  13.3 15.9 %collective-permute-done.refs_1_ = bf16[4,64,1024]{2,1,0:T(8,128)(2,1)} collective-permute-done((bf16[4,64,1024]{2,1,0:T(8,128)(2,1)}, bf16[4,64,1024]{2,1,0:T(8,128)(2,1)}, u32[]{:S(2)}, u32[]{:S(2)}) %collective-permute-start) | collective-permute-done | bytes 524320 | tf_op jit(solution)/shard_map/ppermute | solution.py:37
  29.2 4.2 %collective-permute-start.1 = (bf16[4,64,1024]{2,1,0:T(8,128)(2,1)}, bf16[4,64,1024]{2,1,0:T(8,128)(2,1)}, u32[]{:S(2)}, u32[]{:S(2)}) collective-permute-start(bf16[4,64,1024]{2,1,0:T(8,128)(2,1)} %shard_map.85.refs_2_), channel_id=1, source_target_pairs={{0,3},{1,2},{2,1},{3,0},{4,7},{5,6},{6,5},{7,4},{8,11},{9,10},{10,... | collective-permute-start | bytes 1572872 | tf_op jit(solution)/shard_map/ppermute | solution.py:37
  33.4 0.0 collective-permute-done.4.refs_0_
  33.4 2.0 %shard_map.89.refs_0_ = bf16[2,4,64,1024]{3,2,1,0:T(8,128)(2,1)} custom-call(bf16[4,64,1024]{2,1,0:T(8,128)(2,1)} %collective-permute-done.4.refs_0_, bf16[4,64,1024]{2,1,0:T(8,128)(2,1)} %collective-permute-done.refs_1_, bf16[4,64,1024]{2,1,0:T(8,128)(2,1)} %shard_map.85.refs_2_, bf16[4,64,1536]{2,1,0:T(8,128)(2,1)} %get-tuple-element.15.refs_3_.refs_1_), custom_call_target="tpu_custom_call" | custom-call | flops 32768000000 | bytes 1 | tf_op jit(solution)/shard_map/pallas_call | solution.py:122
  35.4 0.0 collective-permute-done.6.refs_2_.refs_7_
  35.5 3.8 %collective-permute-start.8 = (bf16[2,4,64,1024]{3,2,1,0:T(8,128)(2,1)}, bf16[2,4,64,1024]{3,2,1,0:T(8,128)(2,1)}, u32[]{:S(2)}, u32[]{:S(2)}) collective-permute-start(bf16[2,4,64,1024]{3,2,1,0:T(8,128)(2,1)} %shard_map.90.refs_3_.refs_2_), channel_id=1, source_target_pairs={{4,8},{8,4},{12,16},{16,12},{20,24},{24,20},{5,9},{9,5},{13,17},{1... | collective-permute-start | bytes 3145736 | tf_op jit(solution)/shard_map/ppermute | solution.py:33
  39.2 0.1 collective-permute-start.7
  39.3 5.8 %collective-permute-done.1.refs_1_.refs_0_ = bf16[4,64,1024]{2,1,0:T(8,128)(2,1)} collective-permute-done((bf16[4,64,1024]{2,1,0:T(8,128)(2,1)}, bf16[4,64,1024]{2,1,0:T(8,128)(2,1)}, u32[]{:S(2)}, u32[]{:S(2)}) %collective-permute-start.1) | collective-permute-done | bytes 524320 | tf_op jit(solution)/shard_map/ppermute | solution.py:37
  45.1 10.0 %collective-permute-start.2 = (bf16[4,64,512]{2,1,0:T(8,128)(2,1)}, bf16[4,64,512]{2,1,0:T(8,128)(2,1)}, u32[]{:S(2)}, u32[]{:S(2)}) collective-permute-start(bf16[4,64,512]{2,1,0:T(8,128)(2,1)} %shard_map.86.refs_1_), channel_id=1, source_target_pairs={{0,1},{1,0},{2,3},{3,2},{4,5},{5,4},{6,7},{7,6},{8,9},{9,8},{10,11... | collective-permute-start | bytes 786440 | tf_op jit(solution)/shard_map/ppermute | solution.py:37
  55.1 0.0 collective-permute-start.3
  55.2 10.2 %collective-permute-done.3.refs_1_ = bf16[4,64,512]{2,1,0:T(8,128)(2,1)} collective-permute-done((bf16[4,64,512]{2,1,0:T(8,128)(2,1)}, bf16[4,64,512]{2,1,0:T(8,128)(2,1)}, u32[]{:S(2)}, u32[]{:S(2)}) %collective-permute-start.3) | collective-permute-done | bytes 262176 | tf_op jit(solution)/shard_map/ppermute | solution.py:37
  65.4 1.5 %collective-permute-start.11 = (bf16[4,64,512]{2,1,0:T(8,128)(2,1)}, bf16[4,64,512]{2,1,0:T(8,128)(2,1)}, u32[]{:S(2)}, u32[]{:S(2)}) collective-permute-start(bf16[4,64,512]{2,1,0:T(8,128)(2,1)} %shard_map.88.refs_2_), channel_id=1, source_target_pairs={{0,3},{1,2},{2,1},{3,0},{4,7},{5,6},{6,5},{7,4},{8,11},{9,10},{10,... | collective-permute-start | bytes 786440 | tf_op jit(solution)/shard_map/ppermute | solution.py:37
  66.9 9.7 %collective-permute-start.10 = (bf16[4,64,1024]{2,1,0:T(8,128)(2,1)}, bf16[4,64,1024]{2,1,0:T(8,128)(2,1)}, u32[]{:S(2)}, u32[]{:S(2)}) collective-permute-start(bf16[4,64,1024]{2,1,0:T(8,128)(2,1)} %shard_map.92.refs_3_), channel_id=1, source_target_pairs={{4,8},{8,4},{12,16},{16,12},{20,24},{24,20},{5,9},{9,5},{13,17},{1... | collective-permute-start | bytes 1572872 | tf_op jit(solution)/shard_map/ppermute | solution.py:33
  76.6 0.1 collective-permute-start.9
  76.6 1.8 %shard_map.93.refs_0_ = bf16[2,4,64,512]{3,2,1,0:T(8,128)(2,1)} custom-call(bf16[4,64,512]{2,1,0:T(8,128)(2,1)} %collective-permute-done.2.refs_0_, bf16[4,64,512]{2,1,0:T(8,128)(2,1)} %collective-permute-done.3.refs_1_, bf16[4,64,512]{2,1,0:T(8,128)(2,1)} %shard_map.88.refs_2_, bf16[4,64,1024]{2,1,0:T(8,128)(2,1)} %shard_map.92.refs_3_), custom_call_target="tpu_custom_call" | custom-call | flops 24576000000 | bytes 1 | tf_op jit(solution)/shard_map/pallas_call | solution.py:122
  78.5 10.0 %collective-permute-done.10.refs_2_.refs_9_ = bf16[4,64,1024]{2,1,0:T(8,128)(2,1)} collective-permute-done((bf16[4,64,1024]{2,1,0:T(8,128)(2,1)}, bf16[4,64,1024]{2,1,0:T(8,128)(2,1)}, u32[]{:S(2)}, u32[]{:S(2)}) %collective-permute-start.10) | collective-permute-done | bytes 524320 | tf_op jit(solution)/shard_map/ppermute | solution.py:33
  88.5 4.5 %collective-permute-start.13 = (bf16[2,4,64,512]{3,2,1,0:T(8,128)(2,1)}, bf16[2,4,64,512]{3,2,1,0:T(8,128)(2,1)}, u32[]{:S(2)}, u32[]{:S(2)}) collective-permute-start(bf16[2,4,64,512]{3,2,1,0:T(8,128)(2,1)} %shard_map.94.refs_1_.refs_2_), channel_id=1, source_target_pairs={{4,8},{8,4},{12,16},{16,12},{20,24},{24,20},{5,9},{9,5},{13,17},{1... | collective-permute-start | bytes 1572872 | tf_op jit(solution)/shard_map/ppermute | solution.py:33
  93.0 0.1 collective-permute-start.12
  93.1 11.0 %shard_map.96 = (bf16[256,1536]{1,0:T(8,128)(2,1)}, bf16[256,1536]{1,0:T(8,128)(2,1)}, bf16[256,1536]{1,0:T(8,128)(2,1)}, bf16[256,1536]{1,0:T(8,128)(2,1)}) custom-call(s32[3,4]{1,0:T(4,128)} %pad_add_fusion.refs_0_, bf16[4,64,1536]{2,1,0:T(8,128)(2,1)} %get-tuple-element.15.refs_3_.refs_1_, bf16[2,4,64,1024]{3,2,1,0:T(8,128)(2,1)} %shard_map.90.refs_3_.refs_2_, ...), custom_call_target="tpu_custom_call" | custom-call | flops 12000000000 | bytes 1 | tf_op jit(solution)/shard_map/pallas_call | solution.py:311
  104.1 1.6 %collective-permute-done.13.refs_2_.refs_8_ = bf16[2,4,64,512]{3,2,1,0:T(8,128)(2,1)} collective-permute-done((bf16[2,4,64,512]{3,2,1,0:T(8,128)(2,1)}, bf16[2,4,64,512]{3,2,1,0:T(8,128)(2,1)}, u32[]{:S(2)}, u32[]{:S(2)}) %collective-permute-start.13) | collective-permute-done | bytes 524320 | tf_op jit(solution)/shard_map/ppermute | solution.py:33
  105.8 2.9 %collective-permute-start.15 = (bf16[4,64,512]{2,1,0:T(8,128)(2,1)}, bf16[4,64,512]{2,1,0:T(8,128)(2,1)}, u32[]{:S(2)}, u32[]{:S(2)}) collective-permute-start(bf16[4,64,512]{2,1,0:T(8,128)(2,1)} %shard_map.97.refs_3_), channel_id=1, source_target_pairs={{4,8},{8,4},{12,16},{16,12},{20,24},{24,20},{5,9},{9,5},{13,17},{1... | collective-permute-start | bytes 786440 | tf_op jit(solution)/shard_map/ppermute | solution.py:33
  108.7 0.1 collective-permute-start.14
  108.8 7.8 %collective-permute-done.15.refs_9_ = bf16[4,64,512]{2,1,0:T(8,128)(2,1)} collective-permute-done((bf16[4,64,512]{2,1,0:T(8,128)(2,1)}, bf16[4,64,512]{2,1,0:T(8,128)(2,1)}, u32[]{:S(2)}, u32[]{:S(2)}) %collective-permute-start.15) | collective-permute-done | bytes 262176 | tf_op jit(solution)/shard_map/ppermute | solution.py:33
  116.6 6.8 %shard_map.98 = (bf16[256,1536]{1,0:T(8,128)(2,1)}, bf16[256,1536]{1,0:T(8,128)(2,1)}, bf16[256,1536]{1,0:T(8,128)(2,1)}, bf16[256,1536]{1,0:T(8,128)(2,1)}) custom-call(s32[3,4]{1,0:T(4,128)} %pad_add_fusion.refs_0_, ...), custom_call_target="tpu_custom_call", output_to_operand_aliasing={{0}: (10, {}), {1}: (11, {}), {2}: (12, {}), {3}: (13, {})} | custom-call | flops 6000000000 | bytes 1 | tf_op jit(solution)/shard_map/pallas_call | solution.py:311
  (18 shorter events, 0.0 us)
Async XLA Ops:
  3.8 25.4 %collective-permute-start = (bf16[4,64,1024]{2,1,0:T(8,128)(2,1)}, bf16[4,64,1024]{2,1,0:T(8,128)(2,1)}, u32[]{:S(2)}, u32[]{:S(2)}) collective-permute-start(bf16[4,64,1024]{2,1,0:T(8,128)(2,1)} %get-tuple-element.18), channel_id=1, source_target_pairs={{0,2},{1,3},{2,0},{3,1},{4,6},{5,7},{6,4},{7,5},{8,10},{9,11},{10,... | collective-permute-start | bytes 1572872 | tf_op jit(solution)/shard_map/ppermute | solution.py:37
  6.2 27.2 %collective-permute-start.4 = (bf16[4,64,1024]{2,1,0:T(8,128)(2,1)}, bf16[4,64,1024]{2,1,0:T(8,128)(2,1)}, u32[]{:S(2)}, u32[]{:S(2)}) collective-permute-start(bf16[4,64,1024]{2,1,0:T(8,128)(2,1)} %get-tuple-element.21), channel_id=1, source_target_pairs={{0,1},{1,0},{2,3},{3,2},{4,5},{5,4},{6,7},{7,6},{8,9},{9,8},{10,11... | collective-permute-start | bytes 1572872 | tf_op jit(solution)/shard_map/ppermute | solution.py:37
  7.5 28.0 %collective-permute-start.6 = (bf16[4,64,1536]{2,1,0:T(8,128)(2,1)}, bf16[4,64,1536]{2,1,0:T(8,128)(2,1)}, u32[]{:S(2)}, u32[]{:S(2)}) collective-permute-start(bf16[4,64,1536]{2,1,0:T(8,128)(2,1)} %get-tuple-element.15.refs_3_.refs_1_), channel_id=1, source_target_pairs={{4,8},{8,4},{12,16},{16,12},{20,24},{24,20},{5,9},{9,5},{13,17},{1... | collective-permute-start | bytes 2359304 | tf_op jit(solution)/shard_map/ppermute | solution.py:33
  11.7 23.7 %collective-permute-start.5 = (bf16[4,64,1536]{2,1,0:T(8,128)(2,1)}, bf16[4,64,1536]{2,1,0:T(8,128)(2,1)}, u32[]{:S(2)}, u32[]{:S(2)}) collective-permute-start(bf16[4,64,1536]{2,1,0:T(8,128)(2,1)} %get-tuple-element.15.refs_3_.refs_1_), channel_id=1, source_target_pairs={{0,4},{4,0},{8,12},{12,8},{16,20},{20,16},{24,28},{28,24},{1,5},{5... | collective-permute-start | bytes 2359304 | tf_op jit(solution)/shard_map/ppermute | solution.py:33
  29.2 16.0 %collective-permute-start.1 = (bf16[4,64,1024]{2,1,0:T(8,128)(2,1)}, bf16[4,64,1024]{2,1,0:T(8,128)(2,1)}, u32[]{:S(2)}, u32[]{:S(2)}) collective-permute-start(bf16[4,64,1024]{2,1,0:T(8,128)(2,1)} %shard_map.85.refs_2_), channel_id=1, source_target_pairs={{0,3},{1,2},{2,1},{3,0},{4,7},{5,6},{6,5},{7,4},{8,11},{9,10},{10,... | collective-permute-start | bytes 1572872 | tf_op jit(solution)/shard_map/ppermute | solution.py:37
  35.5 31.4 %collective-permute-start.8 = (bf16[2,4,64,1024]{3,2,1,0:T(8,128)(2,1)}, bf16[2,4,64,1024]{3,2,1,0:T(8,128)(2,1)}, u32[]{:S(2)}, u32[]{:S(2)}) collective-permute-start(bf16[2,4,64,1024]{3,2,1,0:T(8,128)(2,1)} %shard_map.90.refs_3_.refs_2_), channel_id=1, source_target_pairs={{4,8},{8,4},{12,16},{16,12},{20,24},{24,20},{5,9},{9,5},{13,17},{1... | collective-permute-start | bytes 3145736 | tf_op jit(solution)/shard_map/ppermute | solution.py:33
  39.2 27.6 %collective-permute-start.7 = (bf16[2,4,64,1024]{3,2,1,0:T(8,128)(2,1)}, bf16[2,4,64,1024]{3,2,1,0:T(8,128)(2,1)}, u32[]{:S(2)}, u32[]{:S(2)}) collective-permute-start(bf16[2,4,64,1024]{3,2,1,0:T(8,128)(2,1)} %shard_map.90.refs_3_.refs_2_), channel_id=1, source_target_pairs={{0,4},{4,0},{8,12},{12,8},{16,20},{20,16},{24,28},{28,24},{1,5},{5... | collective-permute-start | bytes 3145736 | tf_op jit(solution)/shard_map/ppermute | solution.py:33
  45.1 31.5 %collective-permute-start.2 = (bf16[4,64,512]{2,1,0:T(8,128)(2,1)}, bf16[4,64,512]{2,1,0:T(8,128)(2,1)}, u32[]{:S(2)}, u32[]{:S(2)}) collective-permute-start(bf16[4,64,512]{2,1,0:T(8,128)(2,1)} %shard_map.86.refs_1_), channel_id=1, source_target_pairs={{0,1},{1,0},{2,3},{3,2},{4,5},{5,4},{6,7},{7,6},{8,9},{9,8},{10,11... | collective-permute-start | bytes 786440 | tf_op jit(solution)/shard_map/ppermute | solution.py:37
  55.1 10.2 %collective-permute-start.3 = (bf16[4,64,512]{2,1,0:T(8,128)(2,1)}, bf16[4,64,512]{2,1,0:T(8,128)(2,1)}, u32[]{:S(2)}, u32[]{:S(2)}) collective-permute-start(bf16[4,64,512]{2,1,0:T(8,128)(2,1)} %shard_map.87.refs_2_), channel_id=1, source_target_pairs={{0,2},{1,3},{2,0},{3,1},{4,6},{5,7},{6,4},{7,5},{8,10},{9,11},{10,... | collective-permute-start | bytes 786440 | tf_op jit(solution)/shard_map/ppermute | solution.py:37
  65.4 27.7 %collective-permute-start.11 = (bf16[4,64,512]{2,1,0:T(8,128)(2,1)}, bf16[4,64,512]{2,1,0:T(8,128)(2,1)}, u32[]{:S(2)}, u32[]{:S(2)}) collective-permute-start(bf16[4,64,512]{2,1,0:T(8,128)(2,1)} %shard_map.88.refs_2_), channel_id=1, source_target_pairs={{0,3},{1,2},{2,1},{3,0},{4,7},{5,6},{6,5},{7,4},{8,11},{9,10},{10,... | collective-permute-start | bytes 786440 | tf_op jit(solution)/shard_map/ppermute | solution.py:37
  66.9 21.6 %collective-permute-start.10 = (bf16[4,64,1024]{2,1,0:T(8,128)(2,1)}, bf16[4,64,1024]{2,1,0:T(8,128)(2,1)}, u32[]{:S(2)}, u32[]{:S(2)}) collective-permute-start(bf16[4,64,1024]{2,1,0:T(8,128)(2,1)} %shard_map.92.refs_3_), channel_id=1, source_target_pairs={{4,8},{8,4},{12,16},{16,12},{20,24},{24,20},{5,9},{9,5},{13,17},{1... | collective-permute-start | bytes 1572872 | tf_op jit(solution)/shard_map/ppermute | solution.py:33
  76.6 11.9 %collective-permute-start.9 = (bf16[4,64,1024]{2,1,0:T(8,128)(2,1)}, bf16[4,64,1024]{2,1,0:T(8,128)(2,1)}, u32[]{:S(2)}, u32[]{:S(2)}) collective-permute-start(bf16[4,64,1024]{2,1,0:T(8,128)(2,1)} %shard_map.92.refs_3_), channel_id=1, source_target_pairs={{0,4},{4,0},{8,12},{12,8},{16,20},{20,16},{24,28},{28,24},{1,5},{5... | collective-permute-start | bytes 1572872 | tf_op jit(solution)/shard_map/ppermute | solution.py:33
  88.5 17.3 %collective-permute-start.13 = (bf16[2,4,64,512]{3,2,1,0:T(8,128)(2,1)}, bf16[2,4,64,512]{3,2,1,0:T(8,128)(2,1)}, u32[]{:S(2)}, u32[]{:S(2)}) collective-permute-start(bf16[2,4,64,512]{3,2,1,0:T(8,128)(2,1)} %shard_map.94.refs_1_.refs_2_), channel_id=1, source_target_pairs={{4,8},{8,4},{12,16},{16,12},{20,24},{24,20},{5,9},{9,5},{13,17},{1... | collective-permute-start | bytes 1572872 | tf_op jit(solution)/shard_map/ppermute | solution.py:33
  93.0 12.8 %collective-permute-start.12 = (bf16[2,4,64,512]{3,2,1,0:T(8,128)(2,1)}, bf16[2,4,64,512]{3,2,1,0:T(8,128)(2,1)}, u32[]{:S(2)}, u32[]{:S(2)}) collective-permute-start(bf16[2,4,64,512]{3,2,1,0:T(8,128)(2,1)} %shard_map.94.refs_1_.refs_2_), channel_id=1, source_target_pairs={{0,4},{4,0},{8,12},{12,8},{16,20},{20,16},{24,28},{28,24},{1,5},{5... | collective-permute-start | bytes 1572872 | tf_op jit(solution)/shard_map/ppermute | solution.py:33
  105.8 10.8 %collective-permute-start.15 = (bf16[4,64,512]{2,1,0:T(8,128)(2,1)}, bf16[4,64,512]{2,1,0:T(8,128)(2,1)}, u32[]{:S(2)}, u32[]{:S(2)}) collective-permute-start(bf16[4,64,512]{2,1,0:T(8,128)(2,1)} %shard_map.97.refs_3_), channel_id=1, source_target_pairs={{4,8},{8,4},{12,16},{16,12},{20,24},{24,20},{5,9},{9,5},{13,17},{1... | collective-permute-start | bytes 786440 | tf_op jit(solution)/shard_map/ppermute | solution.py:33
  108.7 7.9 %collective-permute-start.14 = (bf16[4,64,512]{2,1,0:T(8,128)(2,1)}, bf16[4,64,512]{2,1,0:T(8,128)(2,1)}, u32[]{:S(2)}, u32[]{:S(2)}) collective-permute-start(bf16[4,64,512]{2,1,0:T(8,128)(2,1)} %shard_map.97.refs_3_), channel_id=1, source_target_pairs={{0,4},{4,0},{8,12},{12,8},{16,20},{20,16},{24,28},{28,24},{1,5},{5... | collective-permute-start | bytes 786440 | tf_op jit(solution)/shard_map/ppermute | solution.py:33

commit v16 on v15

--- a/solution.py
+++ b/solution.py
@@ -334,9 +334,9 @@
     )(image_ids, *pieces, *(outs or ()))
 
 
-def between(sent, received):
-    size = 2 * sent.size - received.size
-    return pl.CostEstimate(flops=FLOPS_PER_BYTE * size, bytes_accessed=1, transcendentals=0)
+def between(sent, received, divisor):
+    flops = FLOPS_PER_BYTE * (2 * sent.size - received.size) // divisor
+    return pl.CostEstimate(flops=flops, bytes_accessed=1, transcendentals=0)
 
 
 def shards(queries, key_vectors, value_vectors, grad_output, image_ids):
@@ -382,7 +382,7 @@
                 held, crossed = cross(steps[number], [received[-1]])
             elif outs is not None:
                 after.append(outs[0])
-            cost = between(sent[-1][0], received[0])
+            cost = between(sent[-1][0], received[0], 1 if span is spans[0] else 2)
             held.append(sent[-1][0])
             if place == 0:
                 joined = spread(hold(join(received, held, cost), after))

time: 124 us -> 124 us (level)
  no operation moved by 1% of the time
where the time goes in v16:
time: 124 us
  waiting for transfers between devices  51.3 us (41%)
  starting transfers between devices  44.9 us (36%)
  Pallas kernels  24.9 us (20%)
    ppermute x6, waiting for transfers between devices, swap_flipped(): lax.ppermute(block, axis, [(i, i ^ flip) for i in range(lax.axis_size(axi...  31.9 us
    ppermute x10, starting transfers between devices, swap_pairs(): return lax.ppermute(block, axis, route)  25.5 us
    ppermute x10, waiting for transfers between devices, swap_pairs(): return lax.ppermute(block, axis, route)  19.4 us
    ppermute x6, starting transfers between devices, swap_flipped(): lax.ppermute(block, axis, [(i, i ^ flip) for i in range(lax.axis_size(axi...  19.4 us
    pallas_call x2, Pallas kernels, attend(): pl.pallas_call(functools.partial(attend_kernel, parts, part_rows, steps,...  17.8 us
    pallas_call x2, Pallas kernels, join(): pl.pallas_call(functools.partial(join_kernel, pieces), out_shape=jax.Shap...  3.88 us
    pallas_call x1, Pallas kernels, pack(): pl.pallas_call(functools.partial(pack_kernel, stride, jobs), out_shape=[j...  3.16 us
  transfers between devices with their start and end apart: 16, of which 6 were waited for; matrix products, arithmetic and copies ran while one was open for 1% of the time, Pallas kernels for 12%

profile of v16, /device:TPU:3, one launch (start us, length us, event | category | flops | bytes accessed | tf_op | source)
XLA Modules:
  0.0 123.5 jit_solution(15533378374472220904)
XLA Ops:
  0.6 3.2 %shard_map.84 = (bf16[4,64,1024]{2,1,0:T(8,128)(2,1)}, bf16[4,64,1024]{2,1,0:T(8,128)(2,1)}, bf16[4,64,1536]{2,1,0:T(8,128)(2,1)}, bf16[4,64,1024]{2,1,0:T(8,128...) custom-call(bf16[64,6144]{1,0:T(8,128)(2,1)} %refs_0_.1, ...), custom_call_target="tpu_custom_call" | custom-call | flops 1 | bytes 1 | tf_op jit(solution)/shard_map/pallas_call | solution.py:86
  3.8 2.4 %collective-permute-start = (bf16[4,64,1024]{2,1,0:T(8,128)(2,1)}, bf16[4,64,1024]{2,1,0:T(8,128)(2,1)}, u32[]{:S(2)}, u32[]{:S(2)}) collective-permute-start(bf16[4,64,1024]{2,1,0:T(8,128)(2,1)} %get-tuple-element.18), channel_id=1, source_target_pairs={{0,2},{1,3},{2,0},{3,1},{4,6},{5,7},{6,4},{7,5},{8,10},{9,11},{10,... | collective-permute-start | bytes 1572872 | tf_op jit(solution)/shard_map/ppermute | solution.py:37
  6.2 1.3 %collective-permute-start.4 = (bf16[4,64,1024]{2,1,0:T(8,128)(2,1)}, bf16[4,64,1024]{2,1,0:T(8,128)(2,1)}, u32[]{:S(2)}, u32[]{:S(2)}) collective-permute-start(bf16[4,64,1024]{2,1,0:T(8,128)(2,1)} %get-tuple-element.21), channel_id=1, source_target_pairs={{0,1},{1,0},{2,3},{3,2},{4,5},{5,4},{6,7},{7,6},{8,9},{9,8},{10,11... | collective-permute-start | bytes 1572872 | tf_op jit(solution)/shard_map/ppermute | solution.py:37
  7.5 4.2 %collective-permute-start.6 = (bf16[4,64,1536]{2,1,0:T(8,128)(2,1)}, bf16[4,64,1536]{2,1,0:T(8,128)(2,1)}, u32[]{:S(2)}, u32[]{:S(2)}) collective-permute-start(bf16[4,64,1536]{2,1,0:T(8,128)(2,1)} %get-tuple-element.15.refs_3_.refs_1_), channel_id=1, source_target_pairs={{4,8},{8,4},{12,16},{16,12},{20,24},{24,20},{5,9},{9,5},{13,17},{1... | collective-permute-start | bytes 2359304 | tf_op jit(solution)/shard_map/ppermute | solution.py:33
  11.7 0.1 collective-permute-start.5
  11.8 0.8 slice.3
  12.6 0.1 dynamic-slice_bitcast_fusion.2
  12.7 0.6 pad_add_fusion.refs_0_
  13.3 15.9 %collective-permute-done.refs_1_ = bf16[4,64,1024]{2,1,0:T(8,128)(2,1)} collective-permute-done((bf16[4,64,1024]{2,1,0:T(8,128)(2,1)}, bf16[4,64,1024]{2,1,0:T(8,128)(2,1)}, u32[]{:S(2)}, u32[]{:S(2)}) %collective-permute-start) | collective-permute-done | bytes 524320 | tf_op jit(solution)/shard_map/ppermute | solution.py:37
  29.2 4.2 %collective-permute-start.1 = (bf16[4,64,1024]{2,1,0:T(8,128)(2,1)}, bf16[4,64,1024]{2,1,0:T(8,128)(2,1)}, u32[]{:S(2)}, u32[]{:S(2)}) collective-permute-start(bf16[4,64,1024]{2,1,0:T(8,128)(2,1)} %shard_map.85.refs_2_), channel_id=1, source_target_pairs={{0,3},{1,2},{2,1},{3,0},{4,7},{5,6},{6,5},{7,4},{8,11},{9,10},{10,... | collective-permute-start | bytes 1572872 | tf_op jit(solution)/shard_map/ppermute | solution.py:37
  33.4 0.0 collective-permute-done.4.refs_0_
  33.4 2.0 %shard_map.89.refs_0_ = bf16[2,4,64,1024]{3,2,1,0:T(8,128)(2,1)} custom-call(bf16[4,64,1024]{2,1,0:T(8,128)(2,1)} %collective-permute-done.4.refs_0_, bf16[4,64,1024]{2,1,0:T(8,128)(2,1)} %collective-permute-done.refs_1_, bf16[4,64,1024]{2,1,0:T(8,128)(2,1)} %shard_map.85.refs_2_, bf16[4,64,1536]{2,1,0:T(8,128)(2,1)} %get-tuple-element.15.refs_3_.refs_1_), custom_call_target="tpu_custom_call" | custom-call | flops 32768000000 | bytes 1 | tf_op jit(solution)/shard_map/pallas_call | solution.py:122
  35.4 0.0 collective-permute-done.6.refs_2_.refs_7_
  35.5 3.8 %collective-permute-start.8 = (bf16[2,4,64,1024]{3,2,1,0:T(8,128)(2,1)}, bf16[2,4,64,1024]{3,2,1,0:T(8,128)(2,1)}, u32[]{:S(2)}, u32[]{:S(2)}) collective-permute-start(bf16[2,4,64,1024]{3,2,1,0:T(8,128)(2,1)} %shard_map.90.refs_3_.refs_2_), channel_id=1, source_target_pairs={{4,8},{8,4},{12,16},{16,12},{20,24},{24,20},{5,9},{9,5},{13,17},{1... | collective-permute-start | bytes 3145736 | tf_op jit(solution)/shard_map/ppermute | solution.py:33
  39.2 0.1 collective-permute-start.7
  39.3 5.8 %collective-permute-done.1.refs_1_.refs_0_ = bf16[4,64,1024]{2,1,0:T(8,128)(2,1)} collective-permute-done((bf16[4,64,1024]{2,1,0:T(8,128)(2,1)}, bf16[4,64,1024]{2,1,0:T(8,128)(2,1)}, u32[]{:S(2)}, u32[]{:S(2)}) %collective-permute-start.1) | collective-permute-done | bytes 524320 | tf_op jit(solution)/shard_map/ppermute | solution.py:37
  45.1 10.0 %collective-permute-start.2 = (bf16[4,64,512]{2,1,0:T(8,128)(2,1)}, bf16[4,64,512]{2,1,0:T(8,128)(2,1)}, u32[]{:S(2)}, u32[]{:S(2)}) collective-permute-start(bf16[4,64,512]{2,1,0:T(8,128)(2,1)} %shard_map.86.refs_1_), channel_id=1, source_target_pairs={{0,1},{1,0},{2,3},{3,2},{4,5},{5,4},{6,7},{7,6},{8,9},{9,8},{10,11... | collective-permute-start | bytes 786440 | tf_op jit(solution)/shard_map/ppermute | solution.py:37
  55.1 0.0 collective-permute-start.3
  55.2 10.2 %collective-permute-done.3.refs_1_ = bf16[4,64,512]{2,1,0:T(8,128)(2,1)} collective-permute-done((bf16[4,64,512]{2,1,0:T(8,128)(2,1)}, bf16[4,64,512]{2,1,0:T(8,128)(2,1)}, u32[]{:S(2)}, u32[]{:S(2)}) %collective-permute-start.3) | collective-permute-done | bytes 262176 | tf_op jit(solution)/shard_map/ppermute | solution.py:37
  65.4 1.5 %collective-permute-start.11 = (bf16[4,64,512]{2,1,0:T(8,128)(2,1)}, bf16[4,64,512]{2,1,0:T(8,128)(2,1)}, u32[]{:S(2)}, u32[]{:S(2)}) collective-permute-start(bf16[4,64,512]{2,1,0:T(8,128)(2,1)} %shard_map.88.refs_2_), channel_id=1, source_target_pairs={{0,3},{1,2},{2,1},{3,0},{4,7},{5,6},{6,5},{7,4},{8,11},{9,10},{10,... | collective-permute-start | bytes 786440 | tf_op jit(solution)/shard_map/ppermute | solution.py:37
  66.9 9.7 %collective-permute-start.10 = (bf16[4,64,1024]{2,1,0:T(8,128)(2,1)}, bf16[4,64,1024]{2,1,0:T(8,128)(2,1)}, u32[]{:S(2)}, u32[]{:S(2)}) collective-permute-start(bf16[4,64,1024]{2,1,0:T(8,128)(2,1)} %shard_map.92.refs_3_), channel_id=1, source_target_pairs={{4,8},{8,4},{12,16},{16,12},{20,24},{24,20},{5,9},{9,5},{13,17},{1... | collective-permute-start | bytes 1572872 | tf_op jit(solution)/shard_map/ppermute | solution.py:33
  76.6 0.1 collective-permute-start.9
  76.6 1.8 %shard_map.93.refs_0_ = bf16[2,4,64,512]{3,2,1,0:T(8,128)(2,1)} custom-call(bf16[4,64,512]{2,1,0:T(8,128)(2,1)} %collective-permute-done.2.refs_0_, bf16[4,64,512]{2,1,0:T(8,128)(2,1)} %collective-permute-done.3.refs_1_, bf16[4,64,512]{2,1,0:T(8,128)(2,1)} %shard_map.88.refs_2_, bf16[4,64,1024]{2,1,0:T(8,128)(2,1)} %shard_map.92.refs_3_), custom_call_target="tpu_custom_call" | custom-call | flops 12288000000 | bytes 1 | tf_op jit(solution)/shard_map/pallas_call | solution.py:122
  78.5 10.0 %collective-permute-done.10.refs_2_.refs_9_ = bf16[4,64,1024]{2,1,0:T(8,128)(2,1)} collective-permute-done((bf16[4,64,1024]{2,1,0:T(8,128)(2,1)}, bf16[4,64,1024]{2,1,0:T(8,128)(2,1)}, u32[]{:S(2)}, u32[]{:S(2)}) %collective-permute-start.10) | collective-permute-done | bytes 524320 | tf_op jit(solution)/shard_map/ppermute | solution.py:33
  88.5 4.5 %collective-permute-start.13 = (bf16[2,4,64,512]{3,2,1,0:T(8,128)(2,1)}, bf16[2,4,64,512]{3,2,1,0:T(8,128)(2,1)}, u32[]{:S(2)}, u32[]{:S(2)}) collective-permute-start(bf16[2,4,64,512]{3,2,1,0:T(8,128)(2,1)} %shard_map.94.refs_1_.refs_2_), channel_id=1, source_target_pairs={{4,8},{8,4},{12,16},{16,12},{20,24},{24,20},{5,9},{9,5},{13,17},{1... | collective-permute-start | bytes 1572872 | tf_op jit(solution)/shard_map/ppermute | solution.py:33
  93.0 0.1 collective-permute-start.12
  93.1 11.0 %shard_map.96 = (bf16[256,1536]{1,0:T(8,128)(2,1)}, bf16[256,1536]{1,0:T(8,128)(2,1)}, bf16[256,1536]{1,0:T(8,128)(2,1)}, bf16[256,1536]{1,0:T(8,128)(2,1)}) custom-call(s32[3,4]{1,0:T(4,128)} %pad_add_fusion.refs_0_, bf16[4,64,1536]{2,1,0:T(8,128)(2,1)} %get-tuple-element.15.refs_3_.refs_1_, bf16[2,4,64,1024]{3,2,1,0:T(8,128)(2,1)} %shard_map.90.refs_3_.refs_2_, ...), custom_call_target="tpu_custom_call" | custom-call | flops 12000000000 | bytes 1 | tf_op jit(solution)/shard_map/pallas_call | solution.py:311
  104.1 1.7 %collective-permute-done.13.refs_2_.refs_8_ = bf16[2,4,64,512]{3,2,1,0:T(8,128)(2,1)} collective-permute-done((bf16[2,4,64,512]{3,2,1,0:T(8,128)(2,1)}, bf16[2,4,64,512]{3,2,1,0:T(8,128)(2,1)}, u32[]{:S(2)}, u32[]{:S(2)}) %collective-permute-start.13) | collective-permute-done | bytes 524320 | tf_op jit(solution)/shard_map/ppermute | solution.py:33
  105.8 2.9 %collective-permute-start.15 = (bf16[4,64,512]{2,1,0:T(8,128)(2,1)}, bf16[4,64,512]{2,1,0:T(8,128)(2,1)}, u32[]{:S(2)}, u32[]{:S(2)}) collective-permute-start(bf16[4,64,512]{2,1,0:T(8,128)(2,1)} %shard_map.97.refs_3_), channel_id=1, source_target_pairs={{4,8},{8,4},{12,16},{16,12},{20,24},{24,20},{5,9},{9,5},{13,17},{1... | collective-permute-start | bytes 786440 | tf_op jit(solution)/shard_map/ppermute | solution.py:33
  108.7 0.1 collective-permute-start.14
  108.8 7.8 %collective-permute-done.15.refs_9_ = bf16[4,64,512]{2,1,0:T(8,128)(2,1)} collective-permute-done((bf16[4,64,512]{2,1,0:T(8,128)(2,1)}, bf16[4,64,512]{2,1,0:T(8,128)(2,1)}, u32[]{:S(2)}, u32[]{:S(2)}) %collective-permute-start.15) | collective-permute-done | bytes 262176 | tf_op jit(solution)/shard_map/ppermute | solution.py:33
  116.6 6.8 %shard_map.98 = (bf16[256,1536]{1,0:T(8,128)(2,1)}, bf16[256,1536]{1,0:T(8,128)(2,1)}, bf16[256,1536]{1,0:T(8,128)(2,1)}, bf16[256,1536]{1,0:T(8,128)(2,1)}) custom-call(s32[3,4]{1,0:T(4,128)} %pad_add_fusion.refs_0_, ...), custom_call_target="tpu_custom_call", output_to_operand_aliasing={{0}: (10, {}), {1}: (11, {}), {2}: (12, {}), {3}: (13, {})} | custom-call | flops 6000000000 | bytes 1 | tf_op jit(solution)/shard_map/pallas_call | solution.py:311
  (18 shorter events, 0.0 us)
Async XLA Ops:
  3.8 25.4 %collective-permute-start = (bf16[4,64,1024]{2,1,0:T(8,128)(2,1)}, bf16[4,64,1024]{2,1,0:T(8,128)(2,1)}, u32[]{:S(2)}, u32[]{:S(2)}) collective-permute-start(bf16[4,64,1024]{2,1,0:T(8,128)(2,1)} %get-tuple-element.18), channel_id=1, source_target_pairs={{0,2},{1,3},{2,0},{3,1},{4,6},{5,7},{6,4},{7,5},{8,10},{9,11},{10,... | collective-permute-start | bytes 1572872 | tf_op jit(solution)/shard_map/ppermute | solution.py:37
  6.2 27.2 %collective-permute-start.4 = (bf16[4,64,1024]{2,1,0:T(8,128)(2,1)}, bf16[4,64,1024]{2,1,0:T(8,128)(2,1)}, u32[]{:S(2)}, u32[]{:S(2)}) collective-permute-start(bf16[4,64,1024]{2,1,0:T(8,128)(2,1)} %get-tuple-element.21), channel_id=1, source_target_pairs={{0,1},{1,0},{2,3},{3,2},{4,5},{5,4},{6,7},{7,6},{8,9},{9,8},{10,11... | collective-permute-start | bytes 1572872 | tf_op jit(solution)/shard_map/ppermute | solution.py:37
  7.5 28.0 %collective-permute-start.6 = (bf16[4,64,1536]{2,1,0:T(8,128)(2,1)}, bf16[4,64,1536]{2,1,0:T(8,128)(2,1)}, u32[]{:S(2)}, u32[]{:S(2)}) collective-permute-start(bf16[4,64,1536]{2,1,0:T(8,128)(2,1)} %get-tuple-element.15.refs_3_.refs_1_), channel_id=1, source_target_pairs={{4,8},{8,4},{12,16},{16,12},{20,24},{24,20},{5,9},{9,5},{13,17},{1... | collective-permute-start | bytes 2359304 | tf_op jit(solution)/shard_map/ppermute | solution.py:33
  11.7 23.7 %collective-permute-start.5 = (bf16[4,64,1536]{2,1,0:T(8,128)(2,1)}, bf16[4,64,1536]{2,1,0:T(8,128)(2,1)}, u32[]{:S(2)}, u32[]{:S(2)}) collective-permute-start(bf16[4,64,1536]{2,1,0:T(8,128)(2,1)} %get-tuple-element.15.refs_3_.refs_1_), channel_id=1, source_target_pairs={{0,4},{4,0},{8,12},{12,8},{16,20},{20,16},{24,28},{28,24},{1,5},{5... | collective-permute-start | bytes 2359304 | tf_op jit(solution)/shard_map/ppermute | solution.py:33
  29.2 16.0 %collective-permute-start.1 = (bf16[4,64,1024]{2,1,0:T(8,128)(2,1)}, bf16[4,64,1024]{2,1,0:T(8,128)(2,1)}, u32[]{:S(2)}, u32[]{:S(2)}) collective-permute-start(bf16[4,64,1024]{2,1,0:T(8,128)(2,1)} %shard_map.85.refs_2_), channel_id=1, source_target_pairs={{0,3},{1,2},{2,1},{3,0},{4,7},{5,6},{6,5},{7,4},{8,11},{9,10},{10,... | collective-permute-start | bytes 1572872 | tf_op jit(solution)/shard_map/ppermute | solution.py:37
  35.5 31.4 %collective-permute-start.8 = (bf16[2,4,64,1024]{3,2,1,0:T(8,128)(2,1)}, bf16[2,4,64,1024]{3,2,1,0:T(8,128)(2,1)}, u32[]{:S(2)}, u32[]{:S(2)}) collective-permute-start(bf16[2,4,64,1024]{3,2,1,0:T(8,128)(2,1)} %shard_map.90.refs_3_.refs_2_), channel_id=1, source_target_pairs={{4,8},{8,4},{12,16},{16,12},{20,24},{24,20},{5,9},{9,5},{13,17},{1... | collective-permute-start | bytes 3145736 | tf_op jit(solution)/shard_map/ppermute | solution.py:33
  39.2 27.6 %collective-permute-start.7 = (bf16[2,4,64,1024]{3,2,1,0:T(8,128)(2,1)}, bf16[2,4,64,1024]{3,2,1,0:T(8,128)(2,1)}, u32[]{:S(2)}, u32[]{:S(2)}) collective-permute-start(bf16[2,4,64,1024]{3,2,1,0:T(8,128)(2,1)} %shard_map.90.refs_3_.refs_2_), channel_id=1, source_target_pairs={{0,4},{4,0},{8,12},{12,8},{16,20},{20,16},{24,28},{28,24},{1,5},{5... | collective-permute-start | bytes 3145736 | tf_op jit(solution)/shard_map/ppermute | solution.py:33
  45.1 31.5 %collective-permute-start.2 = (bf16[4,64,512]{2,1,0:T(8,128)(2,1)}, bf16[4,64,512]{2,1,0:T(8,128)(2,1)}, u32[]{:S(2)}, u32[]{:S(2)}) collective-permute-start(bf16[4,64,512]{2,1,0:T(8,128)(2,1)} %shard_map.86.refs_1_), channel_id=1, source_target_pairs={{0,1},{1,0},{2,3},{3,2},{4,5},{5,4},{6,7},{7,6},{8,9},{9,8},{10,11... | collective-permute-start | bytes 786440 | tf_op jit(solution)/shard_map/ppermute | solution.py:37
  55.1 10.2 %collective-permute-start.3 = (bf16[4,64,512]{2,1,0:T(8,128)(2,1)}, bf16[4,64,512]{2,1,0:T(8,128)(2,1)}, u32[]{:S(2)}, u32[]{:S(2)}) collective-permute-start(bf16[4,64,512]{2,1,0:T(8,128)(2,1)} %shard_map.87.refs_2_), channel_id=1, source_target_pairs={{0,2},{1,3},{2,0},{3,1},{4,6},{5,7},{6,4},{7,5},{8,10},{9,11},{10,... | collective-permute-start | bytes 786440 | tf_op jit(solution)/shard_map/ppermute | solution.py:37
  65.4 27.7 %collective-permute-start.11 = (bf16[4,64,512]{2,1,0:T(8,128)(2,1)}, bf16[4,64,512]{2,1,0:T(8,128)(2,1)}, u32[]{:S(2)}, u32[]{:S(2)}) collective-permute-start(bf16[4,64,512]{2,1,0:T(8,128)(2,1)} %shard_map.88.refs_2_), channel_id=1, source_target_pairs={{0,3},{1,2},{2,1},{3,0},{4,7},{5,6},{6,5},{7,4},{8,11},{9,10},{10,... | collective-permute-start | bytes 786440 | tf_op jit(solution)/shard_map/ppermute | solution.py:37
  66.9 21.6 %collective-permute-start.10 = (bf16[4,64,1024]{2,1,0:T(8,128)(2,1)}, bf16[4,64,1024]{2,1,0:T(8,128)(2,1)}, u32[]{:S(2)}, u32[]{:S(2)}) collective-permute-start(bf16[4,64,1024]{2,1,0:T(8,128)(2,1)} %shard_map.92.refs_3_), channel_id=1, source_target_pairs={{4,8},{8,4},{12,16},{16,12},{20,24},{24,20},{5,9},{9,5},{13,17},{1... | collective-permute-start | bytes 1572872 | tf_op jit(solution)/shard_map/ppermute | solution.py:33
  76.6 11.9 %collective-permute-start.9 = (bf16[4,64,1024]{2,1,0:T(8,128)(2,1)}, bf16[4,64,1024]{2,1,0:T(8,128)(2,1)}, u32[]{:S(2)}, u32[]{:S(2)}) collective-permute-start(bf16[4,64,1024]{2,1,0:T(8,128)(2,1)} %shard_map.92.refs_3_), channel_id=1, source_target_pairs={{0,4},{4,0},{8,12},{12,8},{16,20},{20,16},{24,28},{28,24},{1,5},{5... | collective-permute-start | bytes 1572872 | tf_op jit(solution)/shard_map/ppermute | solution.py:33
  88.5 17.3 %collective-permute-start.13 = (bf16[2,4,64,512]{3,2,1,0:T(8,128)(2,1)}, bf16[2,4,64,512]{3,2,1,0:T(8,128)(2,1)}, u32[]{:S(2)}, u32[]{:S(2)}) collective-permute-start(bf16[2,4,64,512]{3,2,1,0:T(8,128)(2,1)} %shard_map.94.refs_1_.refs_2_), channel_id=1, source_target_pairs={{4,8},{8,4},{12,16},{16,12},{20,24},{24,20},{5,9},{9,5},{13,17},{1... | collective-permute-start | bytes 1572872 | tf_op jit(solution)/shard_map/ppermute | solution.py:33
  93.0 12.8 %collective-permute-start.12 = (bf16[2,4,64,512]{3,2,1,0:T(8,128)(2,1)}, bf16[2,4,64,512]{3,2,1,0:T(8,128)(2,1)}, u32[]{:S(2)}, u32[]{:S(2)}) collective-permute-start(bf16[2,4,64,512]{3,2,1,0:T(8,128)(2,1)} %shard_map.94.refs_1_.refs_2_), channel_id=1, source_target_pairs={{0,4},{4,0},{8,12},{12,8},{16,20},{20,16},{24,28},{28,24},{1,5},{5... | collective-permute-start | bytes 1572872 | tf_op jit(solution)/shard_map/ppermute | solution.py:33
  105.8 10.8 %collective-permute-start.15 = (bf16[4,64,512]{2,1,0:T(8,128)(2,1)}, bf16[4,64,512]{2,1,0:T(8,128)(2,1)}, u32[]{:S(2)}, u32[]{:S(2)}) collective-permute-start(bf16[4,64,512]{2,1,0:T(8,128)(2,1)} %shard_map.97.refs_3_), channel_id=1, source_target_pairs={{4,8},{8,4},{12,16},{16,12},{20,24},{24,20},{5,9},{9,5},{13,17},{1... | collective-permute-start | bytes 786440 | tf_op jit(solution)/shard_map/ppermute | solution.py:33
  108.7 7.9 %collective-permute-start.14 = (bf16[4,64,512]{2,1,0:T(8,128)(2,1)}, bf16[4,64,512]{2,1,0:T(8,128)(2,1)}, u32[]{:S(2)}, u32[]{:S(2)}) collective-permute-start(bf16[4,64,512]{2,1,0:T(8,128)(2,1)} %shard_map.97.refs_3_), channel_id=1, source_target_pairs={{0,4},{4,0},{8,12},{12,8},{16,20},{20,16},{24,28},{28,24},{1,5},{5... | collective-permute-start | bytes 786440 | tf_op jit(solution)/shard_map/ppermute | solution.py:33

commit v17 on v15

--- a/solution.py
+++ b/solution.py
@@ -15,7 +15,7 @@
 GROUPS = ((8,), (4,))
 VMEM_LIMIT = 64 * 1024 * 1024 - 256 * 1024
 ATTEND_FLOPS = 1_500_000_000
-FLOPS_PER_BYTE = 62_500
+FLOPS_PER_BYTE = 52_000
 SMALL_COST = pl.CostEstimate(flops=1, bytes_accessed=1, transcendentals=0)
 
 
@@ -335,8 +335,8 @@
 
 
 def between(sent, received):
-    size = 2 * sent.size - received.size
-    return pl.CostEstimate(flops=FLOPS_PER_BYTE * size, bytes_accessed=1, transcendentals=0)
+    flops = FLOPS_PER_BYTE * (2 * sent.size - received.size)
+    return pl.CostEstimate(flops=flops, bytes_accessed=1, transcendentals=0)
 
 
 def shards(queries, key_vectors, value_vectors, grad_output, image_ids):
@@ -363,8 +363,9 @@
         steps.append([(flip, *span) for flip in range(1, last)])
         steps += [[(last, *chunk)] for chunk in chunks]
 
-    def cross(step, after):
-        held = [hold(packed[job], after) if after else packed[job] for job in step]
+    def cross(step, after, cost=SMALL_COST, late=()):
+        held = [hold(packed[job], after, cost) if after else packed[job] for job in step]
+        held = [hold(piece, late) if late else piece for piece in held]
         return held, [swap_flipped(piece, "tensor", job[0]) for job, piece in zip(step, held)]
 
     def spread(piece):
@@ -379,7 +380,9 @@
             received, held = crossed, []
             number += 1
             if number < len(steps):
-                held, crossed = cross(steps[number], [received[-1]])
+                late = sent[-1][1:] if number > 1 and place == 0 else ()
+                cost = between(sent[-1][0], received[0]) if late else SMALL_COST
+                held, crossed = cross(steps[number], [received[-1]], cost, late)
             elif outs is not None:
                 after.append(outs[0])
             cost = between(sent[-1][0], received[0])

time: 124 us -> 115 us (0.927)
  starting transfers between devices: 44.9 us -> 33.8 us
  waiting for transfers between devices: 51.3 us -> 53.2 us
    ppermute x10, waiting for transfers between devices: 19.4 us -> 31.5 us  [swap_pairs(): return lax.ppermute(block, axis, route)]
    ppermute x6, waiting for transfers between devices: 31.9 us -> 21.7 us  [swap_flipped(): lax.ppermute(block, axis, [(i, i ^ flip) for i in range(lax.axis_size(axi...]
    ppermute x10, starting transfers between devices: 25.5 us -> 15.9 us  [swap_pairs(): return lax.ppermute(block, axis, route)]
    ppermute x6, starting transfers between devices: 19.4 us -> 17.9 us  [swap_flipped(): lax.ppermute(block, axis, [(i, i ^ flip) for i in range(lax.axis_size(axi...]
  transfers between devices with their start and end apart: 16 -> 16, of which waited for: 6 -> 6; matrix products, arithmetic and copies ran while one was open for 1% -> 1% of each run, Pallas kernels for 12% -> 11%
where the time goes in v17:
time: 115 us; the launch traced here: 114 us
  waiting for transfers between devices  53.2 us (46%)
  starting transfers between devices  33.8 us (29%)
  Pallas kernels  24.9 us (22%)
    ppermute x10, waiting for transfers between devices, swap_pairs(): return lax.ppermute(block, axis, route)  31.5 us
    ppermute x6, waiting for transfers between devices, swap_flipped(): lax.ppermute(block, axis, [(i, i ^ flip) for i in range(lax.axis_size(axi...  21.7 us
    ppermute x6, starting transfers between devices, swap_flipped(): lax.ppermute(block, axis, [(i, i ^ flip) for i in range(lax.axis_size(axi...  17.9 us
    pallas_call x2, Pallas kernels, attend(): pl.pallas_call(functools.partial(attend_kernel, parts, part_rows, steps,...  17.8 us
    ppermute x10, starting transfers between devices, swap_pairs(): return lax.ppermute(block, axis, route)  15.9 us
    pallas_call x2, Pallas kernels, join(): pl.pallas_call(functools.partial(join_kernel, pieces), out_shape=jax.Shap...  3.88 us
    pallas_call x1, Pallas kernels, pack(): pl.pallas_call(functools.partial(pack_kernel, stride, jobs), out_shape=[j...  3.16 us
  transfers between devices with their start and end apart: 16, of which 6 were waited for; matrix products, arithmetic and copies ran while one was open for 1% of the time, Pallas kernels for 11%

profile of v17, /device:TPU:3, one launch (start us, length us, event | category | flops | bytes accessed | tf_op | source)
XLA Modules:
  0.0 114.4 jit_solution(1437390625526276798)
XLA Ops:
  0.6 3.2 %shard_map.84 = (bf16[4,64,1024]{2,1,0:T(8,128)(2,1)}, bf16[4,64,1024]{2,1,0:T(8,128)(2,1)}, bf16[4,64,1536]{2,1,0:T(8,128)(2,1)}, bf16[4,64,1024]{2,1,0:T(8,128...) custom-call(bf16[64,6144]{1,0:T(8,128)(2,1)} %refs_0_.1, ...), custom_call_target="tpu_custom_call" | custom-call | flops 1 | bytes 1 | tf_op jit(solution)/shard_map/pallas_call | solution.py:86
  3.8 2.4 %collective-permute-start = (bf16[4,64,1024]{2,1,0:T(8,128)(2,1)}, bf16[4,64,1024]{2,1,0:T(8,128)(2,1)}, u32[]{:S(2)}, u32[]{:S(2)}) collective-permute-start(bf16[4,64,1024]{2,1,0:T(8,128)(2,1)} %get-tuple-element.18), channel_id=1, source_target_pairs={{0,2},{1,3},{2,0},{3,1},{4,6},{5,7},{6,4},{7,5},{8,10},{9,11},{10,... | collective-permute-start | bytes 1572872 | tf_op jit(solution)/shard_map/ppermute | solution.py:37
  6.2 1.3 %collective-permute-start.4 = (bf16[4,64,1024]{2,1,0:T(8,128)(2,1)}, bf16[4,64,1024]{2,1,0:T(8,128)(2,1)}, u32[]{:S(2)}, u32[]{:S(2)}) collective-permute-start(bf16[4,64,1024]{2,1,0:T(8,128)(2,1)} %get-tuple-element.21), channel_id=1, source_target_pairs={{0,1},{1,0},{2,3},{3,2},{4,5},{5,4},{6,7},{7,6},{8,9},{9,8},{10,11... | collective-permute-start | bytes 1572872 | tf_op jit(solution)/shard_map/ppermute | solution.py:37
  7.5 4.2 %collective-permute-start.6 = (bf16[4,64,1536]{2,1,0:T(8,128)(2,1)}, bf16[4,64,1536]{2,1,0:T(8,128)(2,1)}, u32[]{:S(2)}, u32[]{:S(2)}) collective-permute-start(bf16[4,64,1536]{2,1,0:T(8,128)(2,1)} %get-tuple-element.15.refs_3_.refs_1_), channel_id=1, source_target_pairs={{4,8},{8,4},{12,16},{16,12},{20,24},{24,20},{5,9},{9,5},{13,17},{1... | collective-permute-start | bytes 2359304 | tf_op jit(solution)/shard_map/ppermute | solution.py:33
  11.7 0.1 collective-permute-start.5
  11.8 0.8 slice.3
  12.6 0.1 dynamic-slice_bitcast_fusion.2
  12.7 0.6 pad_add_fusion.refs_0_
  13.3 15.9 %collective-permute-done.refs_1_ = bf16[4,64,1024]{2,1,0:T(8,128)(2,1)} collective-permute-done((bf16[4,64,1024]{2,1,0:T(8,128)(2,1)}, bf16[4,64,1024]{2,1,0:T(8,128)(2,1)}, u32[]{:S(2)}, u32[]{:S(2)}) %collective-permute-start) | collective-permute-done | bytes 524320 | tf_op jit(solution)/shard_map/ppermute | solution.py:37
  29.2 4.2 %collective-permute-start.1 = (bf16[4,64,1024]{2,1,0:T(8,128)(2,1)}, bf16[4,64,1024]{2,1,0:T(8,128)(2,1)}, u32[]{:S(2)}, u32[]{:S(2)}) collective-permute-start(bf16[4,64,1024]{2,1,0:T(8,128)(2,1)} %shard_map.85.refs_2_), channel_id=1, source_target_pairs={{0,3},{1,2},{2,1},{3,0},{4,7},{5,6},{6,5},{7,4},{8,11},{9,10},{10,... | collective-permute-start | bytes 1572872 | tf_op jit(solution)/shard_map/ppermute | solution.py:37
  33.4 2.0 %shard_map.89.refs_0_ = bf16[2,4,64,1024]{3,2,1,0:T(8,128)(2,1)} custom-call(bf16[4,64,1024]{2,1,0:T(8,128)(2,1)} %collective-permute-done.4.refs_0_, bf16[4,64,1024]{2,1,0:T(8,128)(2,1)} %collective-permute-done.refs_1_, bf16[4,64,1024]{2,1,0:T(8,128)(2,1)} %shard_map.85.refs_2_, bf16[4,64,1536]{2,1,0:T(8,128)(2,1)} %get-tuple-element.15.refs_3_.refs_1_), custom_call_target="tpu_custom_call" | custom-call | flops 27262976000 | bytes 1 | tf_op jit(solution)/shard_map/pallas_call | solution.py:122
  35.4 0.0 collective-permute-done.6.refs_2_.refs_7_
  35.5 3.8 %collective-permute-start.8 = (bf16[2,4,64,1024]{3,2,1,0:T(8,128)(2,1)}, bf16[2,4,64,1024]{3,2,1,0:T(8,128)(2,1)}, u32[]{:S(2)}, u32[]{:S(2)}) collective-permute-start(bf16[2,4,64,1024]{3,2,1,0:T(8,128)(2,1)} %shard_map.90.refs_3_.refs_2_), channel_id=1, source_target_pairs={{4,8},{8,4},{12,16},{16,12},{20,24},{24,20},{5,9},{9,5},{13,17},{1... | collective-permute-start | bytes 3145736 | tf_op jit(solution)/shard_map/ppermute | solution.py:33
  39.2 0.1 collective-permute-start.7
  39.3 5.8 %collective-permute-done.1.refs_1_.refs_0_ = bf16[4,64,1024]{2,1,0:T(8,128)(2,1)} collective-permute-done((bf16[4,64,1024]{2,1,0:T(8,128)(2,1)}, bf16[4,64,1024]{2,1,0:T(8,128)(2,1)}, u32[]{:S(2)}, u32[]{:S(2)}) %collective-permute-start.1) | collective-permute-done | bytes 524320 | tf_op jit(solution)/shard_map/ppermute | solution.py:37
  45.1 10.0 %collective-permute-start.2 = (bf16[4,64,512]{2,1,0:T(8,128)(2,1)}, bf16[4,64,512]{2,1,0:T(8,128)(2,1)}, u32[]{:S(2)}, u32[]{:S(2)}) collective-permute-start(bf16[4,64,512]{2,1,0:T(8,128)(2,1)} %shard_map.86.refs_1_), channel_id=1, source_target_pairs={{0,1},{1,0},{2,3},{3,2},{4,5},{5,4},{6,7},{7,6},{8,9},{9,8},{10,11... | collective-permute-start | bytes 786440 | tf_op jit(solution)/shard_map/ppermute | solution.py:37
  55.1 0.0 collective-permute-start.3
  55.2 9.0 %collective-permute-done.8.refs_2_.refs_8_ = bf16[2,4,64,1024]{3,2,1,0:T(8,128)(2,1)} collective-permute-done((bf16[2,4,64,1024]{3,2,1,0:T(8,128)(2,1)}, bf16[2,4,64,1024]{3,2,1,0:T(8,128)(2,1)}, u32[]{:S(2)}, u32[]{:S(2)}) %collective-permute-start.8) | collective-permute-done | bytes 1048608 | tf_op jit(solution)/shard_map/ppermute | solution.py:33
  64.2 0.0 collective-permute-done.7.refs_1_.refs_5_
  64.2 2.7 %collective-permute-start.10 = (bf16[4,64,1024]{2,1,0:T(8,128)(2,1)}, bf16[4,64,1024]{2,1,0:T(8,128)(2,1)}, u32[]{:S(2)}, u32[]{:S(2)}) collective-permute-start(bf16[4,64,1024]{2,1,0:T(8,128)(2,1)} %shard_map.92.refs_3_), channel_id=1, source_target_pairs={{4,8},{8,4},{12,16},{16,12},{20,24},{24,20},{5,9},{9,5},{13,17},{1... | collective-permute-start | bytes 1572872 | tf_op jit(solution)/shard_map/ppermute | solution.py:33
  66.9 0.1 collective-permute-start.9
  67.0 13.5 %collective-permute-done.10.refs_2_.refs_9_ = bf16[4,64,1024]{2,1,0:T(8,128)(2,1)} collective-permute-done((bf16[4,64,1024]{2,1,0:T(8,128)(2,1)}, bf16[4,64,1024]{2,1,0:T(8,128)(2,1)}, u32[]{:S(2)}, u32[]{:S(2)}) %collective-permute-start.10) | collective-permute-done | bytes 524320 | tf_op jit(solution)/shard_map/ppermute | solution.py:33
  80.5 1.8 %shard_map.94.refs_0_ = bf16[2,4,64,512]{3,2,1,0:T(8,128)(2,1)} custom-call(bf16[4,64,512]{2,1,0:T(8,128)(2,1)} %collective-permute-done.2.refs_0_, bf16[4,64,512]{2,1,0:T(8,128)(2,1)} %collective-permute-done.3.refs_1_, bf16[4,64,512]{2,1,0:T(8,128)(2,1)} %shard_map.93.refs_2_, bf16[4,64,1024]{2,1,0:T(8,128)(2,1)} %shard_map.92.refs_3_), custom_call_target="tpu_custom_call" | custom-call | flops 20447232000 | bytes 1 | tf_op jit(solution)/shard_map/pallas_call | solution.py:122
  82.3 0.1 collective-permute-start.11
  82.4 2.7 %collective-permute-start.13 = (bf16[2,4,64,512]{3,2,1,0:T(8,128)(2,1)}, bf16[2,4,64,512]{3,2,1,0:T(8,128)(2,1)}, u32[]{:S(2)}, u32[]{:S(2)}) collective-permute-start(bf16[2,4,64,512]{3,2,1,0:T(8,128)(2,1)} %shard_map.95.refs_1_.refs_2_), channel_id=1, source_target_pairs={{4,8},{8,4},{12,16},{16,12},{20,24},{24,20},{5,9},{9,5},{13,17},{1... | collective-permute-start | bytes 1572872 | tf_op jit(solution)/shard_map/ppermute | solution.py:33
  85.1 0.1 collective-permute-start.12
  85.2 11.0 %shard_map.97 = (bf16[256,1536]{1,0:T(8,128)(2,1)}, bf16[256,1536]{1,0:T(8,128)(2,1)}, bf16[256,1536]{1,0:T(8,128)(2,1)}, bf16[256,1536]{1,0:T(8,128)(2,1)}) custom-call(s32[3,4]{1,0:T(4,128)} %pad_add_fusion.refs_0_, bf16[4,64,1536]{2,1,0:T(8,128)(2,1)} %get-tuple-element.15.refs_3_.refs_1_, bf16[2,4,64,1024]{3,2,1,0:T(8,128)(2,1)} %shard_map.90.refs_3_.refs_2_, ...), custom_call_target="tpu_custom_call" | custom-call | flops 12000000000 | bytes 1 | tf_op jit(solution)/shard_map/pallas_call | solution.py:311
  96.2 2.0 %collective-permute-done.13.refs_2_.refs_8_ = bf16[2,4,64,512]{3,2,1,0:T(8,128)(2,1)} collective-permute-done((bf16[2,4,64,512]{3,2,1,0:T(8,128)(2,1)}, bf16[2,4,64,512]{3,2,1,0:T(8,128)(2,1)}, u32[]{:S(2)}, u32[]{:S(2)}) %collective-permute-start.13) | collective-permute-done | bytes 524320 | tf_op jit(solution)/shard_map/ppermute | solution.py:33
  98.2 2.1 %collective-permute-start.15 = (bf16[4,64,512]{2,1,0:T(8,128)(2,1)}, bf16[4,64,512]{2,1,0:T(8,128)(2,1)}, u32[]{:S(2)}, u32[]{:S(2)}) collective-permute-start(bf16[4,64,512]{2,1,0:T(8,128)(2,1)} %shard_map.98.refs_3_), channel_id=1, source_target_pairs={{4,8},{8,4},{12,16},{16,12},{20,24},{24,20},{5,9},{9,5},{13,17},{1... | collective-permute-start | bytes 786440 | tf_op jit(solution)/shard_map/ppermute | solution.py:33
  100.3 0.1 collective-permute-start.14
  100.4 7.0 %collective-permute-done.15.refs_9_ = bf16[4,64,512]{2,1,0:T(8,128)(2,1)} collective-permute-done((bf16[4,64,512]{2,1,0:T(8,128)(2,1)}, bf16[4,64,512]{2,1,0:T(8,128)(2,1)}, u32[]{:S(2)}, u32[]{:S(2)}) %collective-permute-start.15) | collective-permute-done | bytes 262176 | tf_op jit(solution)/shard_map/ppermute | solution.py:33
  107.4 6.8 %shard_map.99 = (bf16[256,1536]{1,0:T(8,128)(2,1)}, bf16[256,1536]{1,0:T(8,128)(2,1)}, bf16[256,1536]{1,0:T(8,128)(2,1)}, bf16[256,1536]{1,0:T(8,128)(2,1)}) custom-call(s32[3,4]{1,0:T(4,128)} %pad_add_fusion.refs_0_, ...), custom_call_target="tpu_custom_call", output_to_operand_aliasing={{0}: (10, {}), {1}: (11, {}), {2}: (12, {}), {3}: (13, {})} | custom-call | flops 6000000000 | bytes 1 | tf_op jit(solution)/shard_map/pallas_call | solution.py:311
  (19 shorter events, 0.0 us)
Async XLA Ops:
  3.8 25.4 %collective-permute-start = (bf16[4,64,1024]{2,1,0:T(8,128)(2,1)}, bf16[4,64,1024]{2,1,0:T(8,128)(2,1)}, u32[]{:S(2)}, u32[]{:S(2)}) collective-permute-start(bf16[4,64,1024]{2,1,0:T(8,128)(2,1)} %get-tuple-element.18), channel_id=1, source_target_pairs={{0,2},{1,3},{2,0},{3,1},{4,6},{5,7},{6,4},{7,5},{8,10},{9,11},{10,... | collective-permute-start | bytes 1572872 | tf_op jit(solution)/shard_map/ppermute | solution.py:37
  6.2 27.2 %collective-permute-start.4 = (bf16[4,64,1024]{2,1,0:T(8,128)(2,1)}, bf16[4,64,1024]{2,1,0:T(8,128)(2,1)}, u32[]{:S(2)}, u32[]{:S(2)}) collective-permute-start(bf16[4,64,1024]{2,1,0:T(8,128)(2,1)} %get-tuple-element.21), channel_id=1, source_target_pairs={{0,1},{1,0},{2,3},{3,2},{4,5},{5,4},{6,7},{7,6},{8,9},{9,8},{10,11... | collective-permute-start | bytes 1572872 | tf_op jit(solution)/shard_map/ppermute | solution.py:37
  7.5 28.0 %collective-permute-start.6 = (bf16[4,64,1536]{2,1,0:T(8,128)(2,1)}, bf16[4,64,1536]{2,1,0:T(8,128)(2,1)}, u32[]{:S(2)}, u32[]{:S(2)}) collective-permute-start(bf16[4,64,1536]{2,1,0:T(8,128)(2,1)} %get-tuple-element.15.refs_3_.refs_1_), channel_id=1, source_target_pairs={{4,8},{8,4},{12,16},{16,12},{20,24},{24,20},{5,9},{9,5},{13,17},{1... | collective-permute-start | bytes 2359304 | tf_op jit(solution)/shard_map/ppermute | solution.py:33
  11.7 23.7 %collective-permute-start.5 = (bf16[4,64,1536]{2,1,0:T(8,128)(2,1)}, bf16[4,64,1536]{2,1,0:T(8,128)(2,1)}, u32[]{:S(2)}, u32[]{:S(2)}) collective-permute-start(bf16[4,64,1536]{2,1,0:T(8,128)(2,1)} %get-tuple-element.15.refs_3_.refs_1_), channel_id=1, source_target_pairs={{0,4},{4,0},{8,12},{12,8},{16,20},{20,16},{24,28},{28,24},{1,5},{5... | collective-permute-start | bytes 2359304 | tf_op jit(solution)/shard_map/ppermute | solution.py:33
  29.2 16.0 %collective-permute-start.1 = (bf16[4,64,1024]{2,1,0:T(8,128)(2,1)}, bf16[4,64,1024]{2,1,0:T(8,128)(2,1)}, u32[]{:S(2)}, u32[]{:S(2)}) collective-permute-start(bf16[4,64,1024]{2,1,0:T(8,128)(2,1)} %shard_map.85.refs_2_), channel_id=1, source_target_pairs={{0,3},{1,2},{2,1},{3,0},{4,7},{5,6},{6,5},{7,4},{8,11},{9,10},{10,... | collective-permute-start | bytes 1572872 | tf_op jit(solution)/shard_map/ppermute | solution.py:37
  35.5 28.7 %collective-permute-start.8 = (bf16[2,4,64,1024]{3,2,1,0:T(8,128)(2,1)}, bf16[2,4,64,1024]{3,2,1,0:T(8,128)(2,1)}, u32[]{:S(2)}, u32[]{:S(2)}) collective-permute-start(bf16[2,4,64,1024]{3,2,1,0:T(8,128)(2,1)} %shard_map.90.refs_3_.refs_2_), channel_id=1, source_target_pairs={{4,8},{8,4},{12,16},{16,12},{20,24},{24,20},{5,9},{9,5},{13,17},{1... | collective-permute-start | bytes 3145736 | tf_op jit(solution)/shard_map/ppermute | solution.py:33
  39.2 24.9 %collective-permute-start.7 = (bf16[2,4,64,1024]{3,2,1,0:T(8,128)(2,1)}, bf16[2,4,64,1024]{3,2,1,0:T(8,128)(2,1)}, u32[]{:S(2)}, u32[]{:S(2)}) collective-permute-start(bf16[2,4,64,1024]{3,2,1,0:T(8,128)(2,1)} %shard_map.90.refs_3_.refs_2_), channel_id=1, source_target_pairs={{0,4},{4,0},{8,12},{12,8},{16,20},{20,16},{24,28},{28,24},{1,5},{5... | collective-permute-start | bytes 3145736 | tf_op jit(solution)/shard_map/ppermute | solution.py:33
  45.1 35.3 %collective-permute-start.2 = (bf16[4,64,512]{2,1,0:T(8,128)(2,1)}, bf16[4,64,512]{2,1,0:T(8,128)(2,1)}, u32[]{:S(2)}, u32[]{:S(2)}) collective-permute-start(bf16[4,64,512]{2,1,0:T(8,128)(2,1)} %shard_map.86.refs_1_), channel_id=1, source_target_pairs={{0,1},{1,0},{2,3},{3,2},{4,5},{5,4},{6,7},{7,6},{8,9},{9,8},{10,11... | collective-permute-start | bytes 786440 | tf_op jit(solution)/shard_map/ppermute | solution.py:37
  55.1 11.9 %collective-permute-start.3 = (bf16[4,64,512]{2,1,0:T(8,128)(2,1)}, bf16[4,64,512]{2,1,0:T(8,128)(2,1)}, u32[]{:S(2)}, u32[]{:S(2)}) collective-permute-start(bf16[4,64,512]{2,1,0:T(8,128)(2,1)} %shard_map.87.refs_2_), channel_id=1, source_target_pairs={{0,2},{1,3},{2,0},{3,1},{4,6},{5,7},{6,4},{7,5},{8,10},{9,11},{10,... | collective-permute-start | bytes 786440 | tf_op jit(solution)/shard_map/ppermute | solution.py:37
  64.2 16.3 %collective-permute-start.10 = (bf16[4,64,1024]{2,1,0:T(8,128)(2,1)}, bf16[4,64,1024]{2,1,0:T(8,128)(2,1)}, u32[]{:S(2)}, u32[]{:S(2)}) collective-permute-start(bf16[4,64,1024]{2,1,0:T(8,128)(2,1)} %shard_map.92.refs_3_), channel_id=1, source_target_pairs={{4,8},{8,4},{12,16},{16,12},{20,24},{24,20},{5,9},{9,5},{13,17},{1... | collective-permute-start | bytes 1572872 | tf_op jit(solution)/shard_map/ppermute | solution.py:33
  66.9 13.6 %collective-permute-start.9 = (bf16[4,64,1024]{2,1,0:T(8,128)(2,1)}, bf16[4,64,1024]{2,1,0:T(8,128)(2,1)}, u32[]{:S(2)}, u32[]{:S(2)}) collective-permute-start(bf16[4,64,1024]{2,1,0:T(8,128)(2,1)} %shard_map.92.refs_3_), channel_id=1, source_target_pairs={{0,4},{4,0},{8,12},{12,8},{16,20},{20,16},{24,28},{28,24},{1,5},{5... | collective-permute-start | bytes 1572872 | tf_op jit(solution)/shard_map/ppermute | solution.py:33
  82.3 13.9 %collective-permute-start.11 = (bf16[4,64,512]{2,1,0:T(8,128)(2,1)}, bf16[4,64,512]{2,1,0:T(8,128)(2,1)}, u32[]{:S(2)}, u32[]{:S(2)}) collective-permute-start(bf16[4,64,512]{2,1,0:T(8,128)(2,1)} %shard_map.93.refs_2_), channel_id=1, source_target_pairs={{0,3},{1,2},{2,1},{3,0},{4,7},{5,6},{6,5},{7,4},{8,11},{9,10},{10,... | collective-permute-start | bytes 786440 | tf_op jit(solution)/shard_map/ppermute | solution.py:37
  82.4 15.8 %collective-permute-start.13 = (bf16[2,4,64,512]{3,2,1,0:T(8,128)(2,1)}, bf16[2,4,64,512]{3,2,1,0:T(8,128)(2,1)}, u32[]{:S(2)}, u32[]{:S(2)}) collective-permute-start(bf16[2,4,64,512]{3,2,1,0:T(8,128)(2,1)} %shard_map.95.refs_1_.refs_2_), channel_id=1, source_target_pairs={{4,8},{8,4},{12,16},{16,12},{20,24},{24,20},{5,9},{9,5},{13,17},{1... | collective-permute-start | bytes 1572872 | tf_op jit(solution)/shard_map/ppermute | solution.py:33
  85.1 13.1 %collective-permute-start.12 = (bf16[2,4,64,512]{3,2,1,0:T(8,128)(2,1)}, bf16[2,4,64,512]{3,2,1,0:T(8,128)(2,1)}, u32[]{:S(2)}, u32[]{:S(2)}) collective-permute-start(bf16[2,4,64,512]{3,2,1,0:T(8,128)(2,1)} %shard_map.95.refs_1_.refs_2_), channel_id=1, source_target_pairs={{0,4},{4,0},{8,12},{12,8},{16,20},{20,16},{24,28},{28,24},{1,5},{5... | collective-permute-start | bytes 1572872 | tf_op jit(solution)/shard_map/ppermute | solution.py:33
  98.2 9.2 %collective-permute-start.15 = (bf16[4,64,512]{2,1,0:T(8,128)(2,1)}, bf16[4,64,512]{2,1,0:T(8,128)(2,1)}, u32[]{:S(2)}, u32[]{:S(2)}) collective-permute-start(bf16[4,64,512]{2,1,0:T(8,128)(2,1)} %shard_map.98.refs_3_), channel_id=1, source_target_pairs={{4,8},{8,4},{12,16},{16,12},{20,24},{24,20},{5,9},{9,5},{13,17},{1... | collective-permute-start | bytes 786440 | tf_op jit(solution)/shard_map/ppermute | solution.py:33
  100.3 7.1 %collective-permute-start.14 = (bf16[4,64,512]{2,1,0:T(8,128)(2,1)}, bf16[4,64,512]{2,1,0:T(8,128)(2,1)}, u32[]{:S(2)}, u32[]{:S(2)}) collective-permute-start(bf16[4,64,512]{2,1,0:T(8,128)(2,1)} %shard_map.98.refs_3_), channel_id=1, source_target_pairs={{0,4},{4,0},{8,12},{12,8},{16,20},{20,16},{24,28},{28,24},{1,5},{5... | collective-permute-start | bytes 786440 | tf_op jit(solution)/shard_map/ppermute | solution.py:33

commit v18 on v17

--- a/solution.py
+++ b/solution.py
@@ -12,7 +12,7 @@
 SCALE = 1.0 / math.sqrt(HD)
 EXP2_SCALE = SCALE * math.log2(math.e)
 MASKED = -1e30
-GROUPS = ((8,), (4,))
+GROUPS = ((6,), (6,))
 VMEM_LIMIT = 64 * 1024 * 1024 - 256 * 1024
 ATTEND_FLOPS = 1_500_000_000
 FLOPS_PER_BYTE = 52_000
@@ -356,7 +356,9 @@
         jobs += [(flip, *span) for flip in range(last - 1, 0, -1)]
         jobs += [(last, *chunk) for chunk in chunks]
     jobs.insert(last - 1, (0, 0, head_total))
-    packed = dict(zip(jobs, pack(arrays, parts, jobs)))
+    soon, later = jobs[: last - 1], jobs[last - 1 :]
+    packed = dict(zip(soon, pack(arrays, parts, soon)))
+    packed.update(zip(later, pack(arrays, parts, later)))
 
     steps = []
     for span, chunks in zip(spans, groups):

time: 115 us -> 111 us (0.965)
  starting transfers between devices: 33.8 us -> 30.5 us
  waiting for transfers between devices: 53.2 us -> 51.1 us
  Pallas kernels: 24.9 us -> 26.7 us
    ppermute x6, waiting for transfers between devices: 21.7 us -> 9.07 us  [swap_flipped(): lax.ppermute(block, axis, [(i, i ^ flip) for i in range(lax.axis_size(axi...]
    ppermute x10, waiting for transfers between devices: 31.5 us -> 42 us  [swap_pairs(): return lax.ppermute(block, axis, route)]
    ppermute x6, starting transfers between devices: 17.9 us -> 15.4 us  [swap_flipped(): lax.ppermute(block, axis, [(i, i ^ flip) for i in range(lax.axis_size(axi...]
    pallas_call x1 -> x2, Pallas kernels: 3.16 us -> 4.89 us  [pack(): pl.pallas_call(functools.partial(pack_kernel, stride, jobs), out_shape=[j...]
  transfers between devices with their start and end apart: 16 -> 16, of which waited for: 6 -> 7; matrix products, arithmetic and copies ran while one was open for 1% -> 1% of each run, Pallas kernels for 11% -> 12%
where the time goes in v18:
time: 111 us
  waiting for transfers between devices  51.1 us (46%)
  starting transfers between devices  30.5 us (27%)
  Pallas kernels  26.7 us (24%)
    ppermute x10, waiting for transfers between devices, swap_pairs(): return lax.ppermute(block, axis, route)  42 us
    pallas_call x2, Pallas kernels, attend(): pl.pallas_call(functools.partial(attend_kernel, parts, part_rows, steps,...  17.9 us
    ppermute x6, starting transfers between devices, swap_flipped(): lax.ppermute(block, axis, [(i, i ^ flip) for i in range(lax.axis_size(axi...  15.4 us
    ppermute x10, starting transfers between devices, swap_pairs(): return lax.ppermute(block, axis, route)  15.1 us
    ppermute x6, waiting for transfers between devices, swap_flipped(): lax.ppermute(block, axis, [(i, i ^ flip) for i in range(lax.axis_size(axi...  9.07 us
    pallas_call x2, Pallas kernels, pack(): pl.pallas_call(functools.partial(pack_kernel, stride, jobs), out_shape=[j...  4.89 us
    pallas_call x2, Pallas kernels, join(): pl.pallas_call(functools.partial(join_kernel, pieces), out_shape=jax.Shap...  3.88 us
  transfers between devices with their start and end apart: 16, of which 7 were waited for; matrix products, arithmetic and copies ran while one was open for 1% of the time, Pallas kernels for 12%

profile of v18, /device:TPU:3, one launch (start us, length us, event | category | flops | bytes accessed | tf_op | source)
XLA Modules:
  0.0 110.8 jit_solution(9593090159452994618)
XLA Ops:
  0.6 2.1 %shard_map.85 = (bf16[4,64,768]{2,1,0:T(8,128)(2,1)}, bf16[4,64,768]{2,1,0:T(8,128)(2,1)}) custom-call(bf16[64,6144]{1,0:T(8,128)(2,1)} %refs_0_.3, bf16[64,6144]{1,0:T(8,128)(2,1)} %refs_1_.3, bf16[64,6144]{1,0:T(8,128)(2,1)} %refs_2_.3, bf16[64,6144]{1,0:T(8,128)(2,1)} %refs_3_.3), custom_call_target="tpu_custom_call" | custom-call | flops 1 | bytes 1 | tf_op jit(solution)/shard_map/pallas_call | solution.py:86
  2.7 2.4 %collective-permute-start = (bf16[4,64,768]{2,1,0:T(8,128)(2,1)}, bf16[4,64,768]{2,1,0:T(8,128)(2,1)}, u32[]{:S(2)}, u32[]{:S(2)}) collective-permute-start(bf16[4,64,768]{2,1,0:T(8,128)(2,1)} %get-tuple-element.18), channel_id=1, source_target_pairs={{0,2},{1,3},{2,0},{3,1},{4,6},{5,7},{6,4},{7,5},{8,10},{9,11},{10,... | collective-permute-start | bytes 1179656 | tf_op jit(solution)/shard_map/ppermute | solution.py:37
  5.1 1.3 %collective-permute-start.4 = (bf16[4,64,768]{2,1,0:T(8,128)(2,1)}, bf16[4,64,768]{2,1,0:T(8,128)(2,1)}, u32[]{:S(2)}, u32[]{:S(2)}) collective-permute-start(bf16[4,64,768]{2,1,0:T(8,128)(2,1)} %get-tuple-element.21), channel_id=1, source_target_pairs={{0,1},{1,0},{2,3},{3,2},{4,5},{5,4},{6,7},{7,6},{8,9},{9,8},{10,11... | collective-permute-start | bytes 1179656 | tf_op jit(solution)/shard_map/ppermute | solution.py:37
  6.4 2.8 %shard_map.84 = (bf16[4,64,1536]{2,1,0:T(8,128)(2,1)}, bf16[4,64,768]{2,1,0:T(8,128)(2,1)}, bf16[4,64,768]{2,1,0:T(8,128)(2,1)}, bf16[4,64,768]{2,1,0:T(8,128)(2,1)}, bf16[4,64,768]{2,1,0:T(8,128)(2,1)}) custom-call(bf16[64,6144]{1,0:T(8,128)(2,1)} %refs_0_.3, bf16[64,6144]{1,0:T(8,128)(2,1)} %refs_1_.3, bf16[64,6144]{1,0:T(8,128)(2,1)} %refs_2_.3, ...), custom_call_target="tpu_custom_call" | custom-call | flops 1 | bytes 1 | tf_op jit(solution)/shard_map/pallas_call | solution.py:86
  9.2 4.2 %collective-permute-start.6 = (bf16[4,64,1536]{2,1,0:T(8,128)(2,1)}, bf16[4,64,1536]{2,1,0:T(8,128)(2,1)}, u32[]{:S(2)}, u32[]{:S(2)}) collective-permute-start(bf16[4,64,1536]{2,1,0:T(8,128)(2,1)} %get-tuple-element.15.refs_3_.refs_1_), channel_id=1, source_target_pairs={{4,8},{8,4},{12,16},{16,12},{20,24},{24,20},{5,9},{9,5},{13,17},{1... | collective-permute-start | bytes 2359304 | tf_op jit(solution)/shard_map/ppermute | solution.py:33
  13.5 0.1 collective-permute-start.5
  13.5 0.8 slice.3
  14.4 0.1 dynamic-slice_bitcast_fusion.2
  14.5 0.6 pad_add_fusion.refs_0_
  15.1 7.4 %collective-permute-done.refs_1_ = bf16[4,64,768]{2,1,0:T(8,128)(2,1)} collective-permute-done((bf16[4,64,768]{2,1,0:T(8,128)(2,1)}, bf16[4,64,768]{2,1,0:T(8,128)(2,1)}, u32[]{:S(2)}, u32[]{:S(2)}) %collective-permute-start) | collective-permute-done | bytes 393248 | tf_op jit(solution)/shard_map/ppermute | solution.py:37
  22.5 4.2 %collective-permute-start.1 = (bf16[4,64,768]{2,1,0:T(8,128)(2,1)}, bf16[4,64,768]{2,1,0:T(8,128)(2,1)}, u32[]{:S(2)}, u32[]{:S(2)}) collective-permute-start(bf16[4,64,768]{2,1,0:T(8,128)(2,1)} %shard_map.86.refs_2_), channel_id=1, source_target_pairs={{0,3},{1,2},{2,1},{3,0},{4,7},{5,6},{6,5},{7,4},{8,11},{9,10},{10,... | collective-permute-start | bytes 1179656 | tf_op jit(solution)/shard_map/ppermute | solution.py:37
  26.7 2.0 %shard_map.90.refs_0_ = bf16[2,4,64,768]{3,2,1,0:T(8,128)(2,1)} custom-call(bf16[4,64,768]{2,1,0:T(8,128)(2,1)} %collective-permute-done.4.refs_0_, bf16[4,64,768]{2,1,0:T(8,128)(2,1)} %collective-permute-done.refs_1_, bf16[4,64,768]{2,1,0:T(8,128)(2,1)} %shard_map.86.refs_2_, bf16[4,64,1536]{2,1,0:T(8,128)(2,1)} %get-tuple-element.15.refs_3_.refs_1_), custom_call_target="tpu_custom_call" | custom-call | flops 30670848000 | bytes 1 | tf_op jit(solution)/shard_map/pallas_call | solution.py:122
  28.6 3.3 %collective-permute-done.6.refs_2_.refs_7_ = bf16[4,64,1536]{2,1,0:T(8,128)(2,1)} collective-permute-done((bf16[4,64,1536]{2,1,0:T(8,128)(2,1)}, bf16[4,64,1536]{2,1,0:T(8,128)(2,1)}, u32[]{:S(2)}, u32[]{:S(2)}) %collective-permute-start.6) | collective-permute-done | bytes 786464 | tf_op jit(solution)/shard_map/ppermute | solution.py:33
  31.9 3.6 %collective-permute-start.8 = (bf16[2,4,64,768]{3,2,1,0:T(8,128)(2,1)}, bf16[2,4,64,768]{3,2,1,0:T(8,128)(2,1)}, u32[]{:S(2)}, u32[]{:S(2)}) collective-permute-start(bf16[2,4,64,768]{3,2,1,0:T(8,128)(2,1)} %shard_map.91.refs_3_.refs_2_), channel_id=1, source_target_pairs={{4,8},{8,4},{12,16},{16,12},{20,24},{24,20},{5,9},{9,5},{13,17},{1... | collective-permute-start | bytes 2359304 | tf_op jit(solution)/shard_map/ppermute | solution.py:33
  35.5 0.1 collective-permute-start.7
  35.6 0.0 collective-permute-done.1.refs_1_.refs_0_
  35.6 7.2 %collective-permute-start.2 = (bf16[4,64,768]{2,1,0:T(8,128)(2,1)}, bf16[4,64,768]{2,1,0:T(8,128)(2,1)}, u32[]{:S(2)}, u32[]{:S(2)}) collective-permute-start(bf16[4,64,768]{2,1,0:T(8,128)(2,1)} %shard_map.87.refs_1_), channel_id=1, source_target_pairs={{0,1},{1,0},{2,3},{3,2},{4,5},{5,4},{6,7},{7,6},{8,9},{9,8},{10,11... | collective-permute-start | bytes 1179656 | tf_op jit(solution)/shard_map/ppermute | solution.py:37
  42.8 11.7 %collective-permute-done.8.refs_2_.refs_8_ = bf16[2,4,64,768]{3,2,1,0:T(8,128)(2,1)} collective-permute-done((bf16[2,4,64,768]{3,2,1,0:T(8,128)(2,1)}, bf16[2,4,64,768]{3,2,1,0:T(8,128)(2,1)}, u32[]{:S(2)}, u32[]{:S(2)}) %collective-permute-start.8) | collective-permute-done | bytes 786464 | tf_op jit(solution)/shard_map/ppermute | solution.py:33
  54.5 2.4 %collective-permute-start.10 = (bf16[4,64,768]{2,1,0:T(8,128)(2,1)}, bf16[4,64,768]{2,1,0:T(8,128)(2,1)}, u32[]{:S(2)}, u32[]{:S(2)}) collective-permute-start(bf16[4,64,768]{2,1,0:T(8,128)(2,1)} %shard_map.93.refs_3_), channel_id=1, source_target_pairs={{4,8},{8,4},{12,16},{16,12},{20,24},{24,20},{5,9},{9,5},{13,17},{1... | collective-permute-start | bytes 1179656 | tf_op jit(solution)/shard_map/ppermute | solution.py:33
  56.9 0.1 collective-permute-start.9
  57.0 1.6 %collective-permute-done.3.refs_1_ = bf16[4,64,768]{2,1,0:T(8,128)(2,1)} collective-permute-done((bf16[4,64,768]{2,1,0:T(8,128)(2,1)}, bf16[4,64,768]{2,1,0:T(8,128)(2,1)}, u32[]{:S(2)}, u32[]{:S(2)}) %collective-permute-start.3) | collective-permute-done | bytes 393248 | tf_op jit(solution)/shard_map/ppermute | solution.py:37
  58.6 8.6 %collective-permute-done.10.refs_2_.refs_9_ = bf16[4,64,768]{2,1,0:T(8,128)(2,1)} collective-permute-done((bf16[4,64,768]{2,1,0:T(8,128)(2,1)}, bf16[4,64,768]{2,1,0:T(8,128)(2,1)}, u32[]{:S(2)}, u32[]{:S(2)}) %collective-permute-start.10) | collective-permute-done | bytes 393248 | tf_op jit(solution)/shard_map/ppermute | solution.py:33
  67.2 1.9 %shard_map.95.refs_0_ = bf16[2,4,64,768]{3,2,1,0:T(8,128)(2,1)} custom-call(bf16[4,64,768]{2,1,0:T(8,128)(2,1)} %collective-permute-done.2.refs_0_, bf16[4,64,768]{2,1,0:T(8,128)(2,1)} %collective-permute-done.3.refs_1_, bf16[4,64,768]{2,1,0:T(8,128)(2,1)} %shard_map.94.refs_2_, bf16[4,64,768]{2,1,0:T(8,128)(2,1)} %shard_map.93.refs_3_), custom_call_target="tpu_custom_call" | custom-call | flops 10223616000 | bytes 1 | tf_op jit(solution)/shard_map/pallas_call | solution.py:122
  69.2 0.3 collective-permute-start.11
  69.5 2.0 %collective-permute-start.13 = (bf16[2,4,64,768]{3,2,1,0:T(8,128)(2,1)}, bf16[2,4,64,768]{3,2,1,0:T(8,128)(2,1)}, u32[]{:S(2)}, u32[]{:S(2)}) collective-permute-start(bf16[2,4,64,768]{3,2,1,0:T(8,128)(2,1)} %shard_map.96.refs_1_.refs_2_), channel_id=1, source_target_pairs={{4,8},{8,4},{12,16},{16,12},{20,24},{24,20},{5,9},{9,5},{13,17},{1... | collective-permute-start | bytes 2359304 | tf_op jit(solution)/shard_map/ppermute | solution.py:33
  71.5 0.1 collective-permute-start.12
  71.6 9.0 %shard_map.98 = (bf16[256,1536]{1,0:T(8,128)(2,1)}, bf16[256,1536]{1,0:T(8,128)(2,1)}, bf16[256,1536]{1,0:T(8,128)(2,1)}, bf16[256,1536]{1,0:T(8,128)(2,1)}) custom-call(s32[3,4]{1,0:T(4,128)} %pad_add_fusion.refs_0_, bf16[4,64,1536]{2,1,0:T(8,128)(2,1)} %get-tuple-element.15.refs_3_.refs_1_, bf16[2,4,64,768]{3,2,1,0:T(8,128)(2,1)} %shard_map.91.refs_3_.refs_2_, ...), custom_call_target="tpu_custom_call" | custom-call | flops 8999999488 | bytes 1 | tf_op jit(solution)/shard_map/pallas_call | solution.py:311
  80.6 9.7 %collective-permute-done.13.refs_2_.refs_8_ = bf16[2,4,64,768]{3,2,1,0:T(8,128)(2,1)} collective-permute-done((bf16[2,4,64,768]{3,2,1,0:T(8,128)(2,1)}, bf16[2,4,64,768]{3,2,1,0:T(8,128)(2,1)}, u32[]{:S(2)}, u32[]{:S(2)}) %collective-permute-start.13) | collective-permute-done | bytes 786464 | tf_op jit(solution)/shard_map/ppermute | solution.py:33
  90.3 2.5 %collective-permute-start.15 = (bf16[4,64,768]{2,1,0:T(8,128)(2,1)}, bf16[4,64,768]{2,1,0:T(8,128)(2,1)}, u32[]{:S(2)}, u32[]{:S(2)}) collective-permute-start(bf16[4,64,768]{2,1,0:T(8,128)(2,1)} %shard_map.99.refs_3_), channel_id=1, source_target_pairs={{4,8},{8,4},{12,16},{16,12},{20,24},{24,20},{5,9},{9,5},{13,17},{1... | collective-permute-start | bytes 1179656 | tf_op jit(solution)/shard_map/ppermute | solution.py:33
  92.8 0.1 collective-permute-start.14
  92.8 8.8 %collective-permute-done.15.refs_9_ = bf16[4,64,768]{2,1,0:T(8,128)(2,1)} collective-permute-done((bf16[4,64,768]{2,1,0:T(8,128)(2,1)}, bf16[4,64,768]{2,1,0:T(8,128)(2,1)}, u32[]{:S(2)}, u32[]{:S(2)}) %collective-permute-start.15) | collective-permute-done | bytes 393248 | tf_op jit(solution)/shard_map/ppermute | solution.py:33
  101.7 8.9 %shard_map.100 = (bf16[256,1536]{1,0:T(8,128)(2,1)}, bf16[256,1536]{1,0:T(8,128)(2,1)}, bf16[256,1536]{1,0:T(8,128)(2,1)}, bf16[256,1536]{1,0:T(8,128)(2,1)}) custom-call(s32[3,4]{1,0:T(4,128)} %pad_add_fusion.refs_0_, ...), custom_call_target="tpu_custom_call", output_to_operand_aliasing={{0}: (10, {}), {1}: (11, {}), {2}: (12, {}), {3}: (13, {})} | custom-call | flops 8999999488 | bytes 1 | tf_op jit(solution)/shard_map/pallas_call | solution.py:311
  (20 shorter events, 0.1 us)
Async XLA Ops:
  2.7 19.8 %collective-permute-start = (bf16[4,64,768]{2,1,0:T(8,128)(2,1)}, bf16[4,64,768]{2,1,0:T(8,128)(2,1)}, u32[]{:S(2)}, u32[]{:S(2)}) collective-permute-start(bf16[4,64,768]{2,1,0:T(8,128)(2,1)} %get-tuple-element.18), channel_id=1, source_target_pairs={{0,2},{1,3},{2,0},{3,1},{4,6},{5,7},{6,4},{7,5},{8,10},{9,11},{10,... | collective-permute-start | bytes 1179656 | tf_op jit(solution)/shard_map/ppermute | solution.py:37
  5.1 21.6 %collective-permute-start.4 = (bf16[4,64,768]{2,1,0:T(8,128)(2,1)}, bf16[4,64,768]{2,1,0:T(8,128)(2,1)}, u32[]{:S(2)}, u32[]{:S(2)}) collective-permute-start(bf16[4,64,768]{2,1,0:T(8,128)(2,1)} %get-tuple-element.21), channel_id=1, source_target_pairs={{0,1},{1,0},{2,3},{3,2},{4,5},{5,4},{6,7},{7,6},{8,9},{9,8},{10,11... | collective-permute-start | bytes 1179656 | tf_op jit(solution)/shard_map/ppermute | solution.py:37
  9.2 22.7 %collective-permute-start.6 = (bf16[4,64,1536]{2,1,0:T(8,128)(2,1)}, bf16[4,64,1536]{2,1,0:T(8,128)(2,1)}, u32[]{:S(2)}, u32[]{:S(2)}) collective-permute-start(bf16[4,64,1536]{2,1,0:T(8,128)(2,1)} %get-tuple-element.15.refs_3_.refs_1_), channel_id=1, source_target_pairs={{4,8},{8,4},{12,16},{16,12},{20,24},{24,20},{5,9},{9,5},{13,17},{1... | collective-permute-start | bytes 2359304 | tf_op jit(solution)/shard_map/ppermute | solution.py:33
  13.5 18.5 %collective-permute-start.5 = (bf16[4,64,1536]{2,1,0:T(8,128)(2,1)}, bf16[4,64,1536]{2,1,0:T(8,128)(2,1)}, u32[]{:S(2)}, u32[]{:S(2)}) collective-permute-start(bf16[4,64,1536]{2,1,0:T(8,128)(2,1)} %get-tuple-element.15.refs_3_.refs_1_), channel_id=1, source_target_pairs={{0,4},{4,0},{8,12},{12,8},{16,20},{20,16},{24,28},{28,24},{1,5},{5... | collective-permute-start | bytes 2359304 | tf_op jit(solution)/shard_map/ppermute | solution.py:33
  22.5 13.2 %collective-permute-start.1 = (bf16[4,64,768]{2,1,0:T(8,128)(2,1)}, bf16[4,64,768]{2,1,0:T(8,128)(2,1)}, u32[]{:S(2)}, u32[]{:S(2)}) collective-permute-start(bf16[4,64,768]{2,1,0:T(8,128)(2,1)} %shard_map.86.refs_2_), channel_id=1, source_target_pairs={{0,3},{1,2},{2,1},{3,0},{4,7},{5,6},{6,5},{7,4},{8,11},{9,10},{10,... | collective-permute-start | bytes 1179656 | tf_op jit(solution)/shard_map/ppermute | solution.py:37
  31.9 22.6 %collective-permute-start.8 = (bf16[2,4,64,768]{3,2,1,0:T(8,128)(2,1)}, bf16[2,4,64,768]{3,2,1,0:T(8,128)(2,1)}, u32[]{:S(2)}, u32[]{:S(2)}) collective-permute-start(bf16[2,4,64,768]{3,2,1,0:T(8,128)(2,1)} %shard_map.91.refs_3_.refs_2_), channel_id=1, source_target_pairs={{4,8},{8,4},{12,16},{16,12},{20,24},{24,20},{5,9},{9,5},{13,17},{1... | collective-permute-start | bytes 2359304 | tf_op jit(solution)/shard_map/ppermute | solution.py:33
  35.5 19.0 %collective-permute-start.7 = (bf16[2,4,64,768]{3,2,1,0:T(8,128)(2,1)}, bf16[2,4,64,768]{3,2,1,0:T(8,128)(2,1)}, u32[]{:S(2)}, u32[]{:S(2)}) collective-permute-start(bf16[2,4,64,768]{3,2,1,0:T(8,128)(2,1)} %shard_map.91.refs_3_.refs_2_), channel_id=1, source_target_pairs={{0,4},{4,0},{8,12},{12,8},{16,20},{20,16},{24,28},{28,24},{1,5},{5... | collective-permute-start | bytes 2359304 | tf_op jit(solution)/shard_map/ppermute | solution.py:33
  35.6 31.6 %collective-permute-start.2 = (bf16[4,64,768]{2,1,0:T(8,128)(2,1)}, bf16[4,64,768]{2,1,0:T(8,128)(2,1)}, u32[]{:S(2)}, u32[]{:S(2)}) collective-permute-start(bf16[4,64,768]{2,1,0:T(8,128)(2,1)} %shard_map.87.refs_1_), channel_id=1, source_target_pairs={{0,1},{1,0},{2,3},{3,2},{4,5},{5,4},{6,7},{7,6},{8,9},{9,8},{10,11... | collective-permute-start | bytes 1179656 | tf_op jit(solution)/shard_map/ppermute | solution.py:37
  42.8 15.9 %collective-permute-start.3 = (bf16[4,64,768]{2,1,0:T(8,128)(2,1)}, bf16[4,64,768]{2,1,0:T(8,128)(2,1)}, u32[]{:S(2)}, u32[]{:S(2)}) collective-permute-start(bf16[4,64,768]{2,1,0:T(8,128)(2,1)} %shard_map.88.refs_2_), channel_id=1, source_target_pairs={{0,2},{1,3},{2,0},{3,1},{4,6},{5,7},{6,4},{7,5},{8,10},{9,11},{10,... | collective-permute-start | bytes 1179656 | tf_op jit(solution)/shard_map/ppermute | solution.py:37
  54.5 12.7 %collective-permute-start.10 = (bf16[4,64,768]{2,1,0:T(8,128)(2,1)}, bf16[4,64,768]{2,1,0:T(8,128)(2,1)}, u32[]{:S(2)}, u32[]{:S(2)}) collective-permute-start(bf16[4,64,768]{2,1,0:T(8,128)(2,1)} %shard_map.93.refs_3_), channel_id=1, source_target_pairs={{4,8},{8,4},{12,16},{16,12},{20,24},{24,20},{5,9},{9,5},{13,17},{1... | collective-permute-start | bytes 1179656 | tf_op jit(solution)/shard_map/ppermute | solution.py:33
  56.9 10.3 %collective-permute-start.9 = (bf16[4,64,768]{2,1,0:T(8,128)(2,1)}, bf16[4,64,768]{2,1,0:T(8,128)(2,1)}, u32[]{:S(2)}, u32[]{:S(2)}) collective-permute-start(bf16[4,64,768]{2,1,0:T(8,128)(2,1)} %shard_map.93.refs_3_), channel_id=1, source_target_pairs={{0,4},{4,0},{8,12},{12,8},{16,20},{20,16},{24,28},{28,24},{1,5},{5... | collective-permute-start | bytes 1179656 | tf_op jit(solution)/shard_map/ppermute | solution.py:33
  69.2 11.4 %collective-permute-start.11 = (bf16[4,64,768]{2,1,0:T(8,128)(2,1)}, bf16[4,64,768]{2,1,0:T(8,128)(2,1)}, u32[]{:S(2)}, u32[]{:S(2)}) collective-permute-start(bf16[4,64,768]{2,1,0:T(8,128)(2,1)} %shard_map.94.refs_2_), channel_id=1, source_target_pairs={{0,3},{1,2},{2,1},{3,0},{4,7},{5,6},{6,5},{7,4},{8,11},{9,10},{10,... | collective-permute-start | bytes 1179656 | tf_op jit(solution)/shard_map/ppermute | solution.py:37
  69.5 20.8 %collective-permute-start.13 = (bf16[2,4,64,768]{3,2,1,0:T(8,128)(2,1)}, bf16[2,4,64,768]{3,2,1,0:T(8,128)(2,1)}, u32[]{:S(2)}, u32[]{:S(2)}) collective-permute-start(bf16[2,4,64,768]{3,2,1,0:T(8,128)(2,1)} %shard_map.96.refs_1_.refs_2_), channel_id=1, source_target_pairs={{4,8},{8,4},{12,16},{16,12},{20,24},{24,20},{5,9},{9,5},{13,17},{1... | collective-permute-start | bytes 2359304 | tf_op jit(solution)/shard_map/ppermute | solution.py:33
  71.5 18.7 %collective-permute-start.12 = (bf16[2,4,64,768]{3,2,1,0:T(8,128)(2,1)}, bf16[2,4,64,768]{3,2,1,0:T(8,128)(2,1)}, u32[]{:S(2)}, u32[]{:S(2)}) collective-permute-start(bf16[2,4,64,768]{3,2,1,0:T(8,128)(2,1)} %shard_map.96.refs_1_.refs_2_), channel_id=1, source_target_pairs={{0,4},{4,0},{8,12},{12,8},{16,20},{20,16},{24,28},{28,24},{1,5},{5... | collective-permute-start | bytes 2359304 | tf_op jit(solution)/shard_map/ppermute | solution.py:33
  90.3 11.4 %collective-permute-start.15 = (bf16[4,64,768]{2,1,0:T(8,128)(2,1)}, bf16[4,64,768]{2,1,0:T(8,128)(2,1)}, u32[]{:S(2)}, u32[]{:S(2)}) collective-permute-start(bf16[4,64,768]{2,1,0:T(8,128)(2,1)} %shard_map.99.refs_3_), channel_id=1, source_target_pairs={{4,8},{8,4},{12,16},{16,12},{20,24},{24,20},{5,9},{9,5},{13,17},{1... | collective-permute-start | bytes 1179656 | tf_op jit(solution)/shard_map/ppermute | solution.py:33
  92.8 8.9 %collective-permute-start.14 = (bf16[4,64,768]{2,1,0:T(8,128)(2,1)}, bf16[4,64,768]{2,1,0:T(8,128)(2,1)}, u32[]{:S(2)}, u32[]{:S(2)}) collective-permute-start(bf16[4,64,768]{2,1,0:T(8,128)(2,1)} %shard_map.99.refs_3_), channel_id=1, source_target_pairs={{0,4},{4,0},{8,12},{12,8},{16,20},{20,16},{24,28},{28,24},{1,5},{5... | collective-permute-start | bytes 1179656 | tf_op jit(solution)/shard_map/ppermute | solution.py:33

commit v19 on v18

--- a/solution.py
+++ b/solution.py
@@ -356,7 +356,7 @@
         jobs += [(flip, *span) for flip in range(last - 1, 0, -1)]
         jobs += [(last, *chunk) for chunk in chunks]
     jobs.insert(last - 1, (0, 0, head_total))
-    soon, later = jobs[: last - 1], jobs[last - 1 :]
+    soon, later = jobs[:last], jobs[last:]
     packed = dict(zip(soon, pack(arrays, parts, soon)))
     packed.update(zip(later, pack(arrays, parts, later)))
 
@@ -378,16 +378,16 @@
     outs, joined, number = None, None, 0
     for span, chunks in zip(spans, groups):
         for place in range(1 + len(chunks)):
-            after = list(sent[-1][1:])
+            after = list(sent[-1][1 : 3 if place == 0 else 2])
             received, held = crossed, []
             number += 1
             if number < len(steps):
-                late = sent[-1][1:] if number > 1 and place == 0 else ()
+                late = [*sent[-1][1:], sent[-2][2]] if number > 1 and place == 0 else ()
                 cost = between(sent[-1][0], received[0]) if late else SMALL_COST
                 held, crossed = cross(steps[number], [received[-1]], cost, late)
             elif outs is not None:
                 after.append(outs[0])
-            cost = between(sent[-1][0], received[0])
+            cost = between(sent[-1][0], received[0]) if place == 0 else SMALL_COST
             held.append(sent[-1][0])
             if place == 0:
                 joined = spread(hold(join(received, held, cost), after))

time: 111 us -> 127 us (1.14)
  waiting for transfers between devices: 51.1 us -> 64.9 us
  starting transfers between devices: 30.5 us -> 32.1 us
    ppermute x6, waiting for transfers between devices: 9.07 us -> 29.3 us  [swap_flipped(): lax.ppermute(block, axis, [(i, i ^ flip) for i in range(lax.axis_size(axi...]
    ppermute x10, waiting for transfers between devices: 42 us -> 35.6 us  [swap_pairs(): return lax.ppermute(block, axis, route)]
    ppermute x10, starting transfers between devices: 15.1 us -> 18.9 us  [swap_pairs(): return lax.ppermute(block, axis, route)]
    ppermute x6, starting transfers between devices: 15.4 us -> 13.2 us  [swap_flipped(): lax.ppermute(block, axis, [(i, i ^ flip) for i in range(lax.axis_size(axi...]
  transfers between devices with their start and end apart: 16 -> 16, of which waited for: 7 -> 8; matrix products, arithmetic and copies ran while one was open for 1% -> 1% of each run, Pallas kernels for 12% -> 11%
where the time goes in v19:
time: 127 us; the launch traced here: 126 us
  waiting for transfers between devices  64.9 us (51%)
  starting transfers between devices  32.1 us (25%)
  Pallas kernels  26.6 us (21%)
    ppermute x10, waiting for transfers between devices, swap_pairs(): return lax.ppermute(block, axis, route)  35.6 us
    ppermute x6, waiting for transfers between devices, swap_flipped(): lax.ppermute(block, axis, [(i, i ^ flip) for i in range(lax.axis_size(axi...  29.3 us
    ppermute x10, starting transfers between devices, swap_pairs(): return lax.ppermute(block, axis, route)  18.9 us
    pallas_call x2, Pallas kernels, attend(): pl.pallas_call(functools.partial(attend_kernel, parts, part_rows, steps,...  17.8 us
    ppermute x6, starting transfers between devices, swap_flipped(): lax.ppermute(block, axis, [(i, i ^ flip) for i in range(lax.axis_size(axi...  13.2 us
    pallas_call x2, Pallas kernels, pack(): pl.pallas_call(functools.partial(pack_kernel, stride, jobs), out_shape=[j...  4.88 us
    pallas_call x2, Pallas kernels, join(): pl.pallas_call(functools.partial(join_kernel, pieces), out_shape=jax.Shap...  3.88 us
  transfers between devices with their start and end apart: 16, of which 8 were waited for; matrix products, arithmetic and copies ran while one was open for 1% of the time, Pallas kernels for 11%

profile of v19, /device:TPU:3, one launch (start us, length us, event | category | flops | bytes accessed | tf_op | source)
XLA Modules:
  0.0 126.0 jit_solution(47315923804689210)
XLA Ops:
  0.6 2.5 %shard_map.84 = (bf16[4,64,768]{2,1,0:T(8,128)(2,1)}, bf16[4,64,768]{2,1,0:T(8,128)(2,1)}, bf16[4,64,1536]{2,1,0:T(8,128)(2,1)}) custom-call(bf16[64,6144]{1,0:T(8,128)(2,1)} %refs_0_.3, bf16[64,6144]{1,0:T(8,128)(2,1)} %refs_1_.3, bf16[64,6144]{1,0:T(8,128)(2,1)} %refs_2_.3, bf16[64,6144]{1,0:T(8,128)(2,1)} %refs_3_.3), custom_call_target="tpu_custom_call" | custom-call | flops 1 | bytes 1 | tf_op jit(solution)/shard_map/pallas_call | solution.py:86
  3.1 2.4 %collective-permute-start = (bf16[4,64,768]{2,1,0:T(8,128)(2,1)}, bf16[4,64,768]{2,1,0:T(8,128)(2,1)}, u32[]{:S(2)}, u32[]{:S(2)}) collective-permute-start(bf16[4,64,768]{2,1,0:T(8,128)(2,1)} %get-tuple-element.18), channel_id=1, source_target_pairs={{0,2},{1,3},{2,0},{3,1},{4,6},{5,7},{6,4},{7,5},{8,10},{9,11},{10,... | collective-permute-start | bytes 1179656 | tf_op jit(solution)/shard_map/ppermute | solution.py:37
  5.5 1.3 %collective-permute-start.4 = (bf16[4,64,768]{2,1,0:T(8,128)(2,1)}, bf16[4,64,768]{2,1,0:T(8,128)(2,1)}, u32[]{:S(2)}, u32[]{:S(2)}) collective-permute-start(bf16[4,64,768]{2,1,0:T(8,128)(2,1)} %get-tuple-element.21), channel_id=1, source_target_pairs={{0,1},{1,0},{2,3},{3,2},{4,5},{5,4},{6,7},{7,6},{8,9},{9,8},{10,11... | collective-permute-start | bytes 1179656 | tf_op jit(solution)/shard_map/ppermute | solution.py:37
  6.8 4.2 %collective-permute-start.6 = (bf16[4,64,1536]{2,1,0:T(8,128)(2,1)}, bf16[4,64,1536]{2,1,0:T(8,128)(2,1)}, u32[]{:S(2)}, u32[]{:S(2)}) collective-permute-start(bf16[4,64,1536]{2,1,0:T(8,128)(2,1)} %get-tuple-element.15.refs_3_.refs_1_), channel_id=1, source_target_pairs={{4,8},{8,4},{12,16},{16,12},{20,24},{24,20},{5,9},{9,5},{13,17},{1... | collective-permute-start | bytes 2359304 | tf_op jit(solution)/shard_map/ppermute | solution.py:33
  11.0 0.1 collective-permute-start.5
  11.1 2.4 %shard_map.85 = (bf16[4,64,768]{2,1,0:T(8,128)(2,1)}, bf16[4,64,768]{2,1,0:T(8,128)(2,1)}, bf16[4,64,768]{2,1,0:T(8,128)(2,1)}, bf16[4,64,768]{2,1,0:T(8,128)(2,1)}) custom-call(bf16[64,6144]{1,0:T(8,128)(2,1)} %refs_0_.3, bf16[64,6144]{1,0:T(8,128)(2,1)} %refs_1_.3, bf16[64,6144]{1,0:T(8,128)(2,1)} %refs_2_.3, bf16[64,6144]{1,0:T(8,128)(2,1)} %refs_3_.3), custom_call_target="tpu_custom_call" | custom-call | flops 1 | bytes 1 | tf_op jit(solution)/shard_map/pallas_call | solution.py:86
  13.5 9.4 %collective-permute-done.refs_1_ = bf16[4,64,768]{2,1,0:T(8,128)(2,1)} collective-permute-done((bf16[4,64,768]{2,1,0:T(8,128)(2,1)}, bf16[4,64,768]{2,1,0:T(8,128)(2,1)}, u32[]{:S(2)}, u32[]{:S(2)}) %collective-permute-start) | collective-permute-done | bytes 393248 | tf_op jit(solution)/shard_map/ppermute | solution.py:37
  22.9 2.0 %shard_map.90.refs_0_ = bf16[2,4,64,768]{3,2,1,0:T(8,128)(2,1)} custom-call(bf16[4,64,768]{2,1,0:T(8,128)(2,1)} %collective-permute-done.4.refs_0_, bf16[4,64,768]{2,1,0:T(8,128)(2,1)} %collective-permute-done.refs_1_, bf16[4,64,768]{2,1,0:T(8,128)(2,1)} %shard_map.86.refs_2_, bf16[4,64,1536]{2,1,0:T(8,128)(2,1)} %get-tuple-element.15.refs_3_.refs_1_), custom_call_target="tpu_custom_call" | custom-call | flops 30670848000 | bytes 1 | tf_op jit(solution)/shard_map/pallas_call | solution.py:122
  24.8 4.3 %collective-permute-done.6.refs_2_.refs_7_ = bf16[4,64,1536]{2,1,0:T(8,128)(2,1)} collective-permute-done((bf16[4,64,1536]{2,1,0:T(8,128)(2,1)}, bf16[4,64,1536]{2,1,0:T(8,128)(2,1)}, u32[]{:S(2)}, u32[]{:S(2)}) %collective-permute-start.6) | collective-permute-done | bytes 786464 | tf_op jit(solution)/shard_map/ppermute | solution.py:33
  29.2 0.4 collective-permute-start.1
  29.6 12.0 %collective-permute-done.1.refs_1_.refs_0_ = bf16[4,64,768]{2,1,0:T(8,128)(2,1)} collective-permute-done((bf16[4,64,768]{2,1,0:T(8,128)(2,1)}, bf16[4,64,768]{2,1,0:T(8,128)(2,1)}, u32[]{:S(2)}, u32[]{:S(2)}) %collective-permute-start.1) | collective-permute-done | bytes 393248 | tf_op jit(solution)/shard_map/ppermute | solution.py:37
  41.7 6.7 %collective-permute-start.3 = (bf16[4,64,768]{2,1,0:T(8,128)(2,1)}, bf16[4,64,768]{2,1,0:T(8,128)(2,1)}, u32[]{:S(2)}, u32[]{:S(2)}) collective-permute-start(bf16[4,64,768]{2,1,0:T(8,128)(2,1)} %shard_map.88.refs_2_), channel_id=1, source_target_pairs={{0,2},{1,3},{2,0},{3,1},{4,6},{5,7},{6,4},{7,5},{8,10},{9,11},{10,... | collective-permute-start | bytes 1179656 | tf_op jit(solution)/shard_map/ppermute | solution.py:37
  48.3 0.8 slice.3
  49.2 0.1 dynamic-slice_bitcast_fusion.2
  49.3 0.6 pad_add_fusion.refs_0_
  49.9 5.3 %collective-permute-start.10 = (bf16[2,4,64,768]{3,2,1,0:T(8,128)(2,1)}, bf16[2,4,64,768]{3,2,1,0:T(8,128)(2,1)}, u32[]{:S(2)}, u32[]{:S(2)}) collective-permute-start(bf16[2,4,64,768]{3,2,1,0:T(8,128)(2,1)} %shard_map.91.refs_3_.refs_2_), channel_id=1, source_target_pairs={{4,8},{8,4},{12,16},{16,12},{20,24},{24,20},{5,9},{9,5},{13,17},{1... | collective-permute-start | bytes 2359304 | tf_op jit(solution)/shard_map/ppermute | solution.py:33
  55.2 0.1 collective-permute-start.2
  55.3 2.0 %collective-permute-start.9 = (bf16[4,64,768]{2,1,0:T(8,128)(2,1)}, bf16[4,64,768]{2,1,0:T(8,128)(2,1)}, u32[]{:S(2)}, u32[]{:S(2)}) collective-permute-start(bf16[4,64,768]{2,1,0:T(8,128)(2,1)} %shard_map.93.refs_3_), channel_id=1, source_target_pairs={{4,8},{8,4},{12,16},{16,12},{20,24},{24,20},{5,9},{9,5},{13,17},{1... | collective-permute-start | bytes 1179656 | tf_op jit(solution)/shard_map/ppermute | solution.py:33
  57.3 0.1 collective-permute-start.8
  57.4 7.9 %collective-permute-done.3.refs_1_ = bf16[4,64,768]{2,1,0:T(8,128)(2,1)} collective-permute-done((bf16[4,64,768]{2,1,0:T(8,128)(2,1)}, bf16[4,64,768]{2,1,0:T(8,128)(2,1)}, u32[]{:S(2)}, u32[]{:S(2)}) %collective-permute-start.3) | collective-permute-done | bytes 393248 | tf_op jit(solution)/shard_map/ppermute | solution.py:37
  65.3 8.0 %collective-permute-done.10.refs_3_.refs_8_ = bf16[2,4,64,768]{3,2,1,0:T(8,128)(2,1)} collective-permute-done((bf16[2,4,64,768]{3,2,1,0:T(8,128)(2,1)}, bf16[2,4,64,768]{3,2,1,0:T(8,128)(2,1)}, u32[]{:S(2)}, u32[]{:S(2)}) %collective-permute-start.10) | collective-permute-done | bytes 786464 | tf_op jit(solution)/shard_map/ppermute | solution.py:33
  73.3 8.4 %collective-permute-done.9.refs_2_.refs_9_ = bf16[4,64,768]{2,1,0:T(8,128)(2,1)} collective-permute-done((bf16[4,64,768]{2,1,0:T(8,128)(2,1)}, bf16[4,64,768]{2,1,0:T(8,128)(2,1)}, u32[]{:S(2)}, u32[]{:S(2)}) %collective-permute-start.9) | collective-permute-done | bytes 393248 | tf_op jit(solution)/shard_map/ppermute | solution.py:33
  81.7 1.9 %shard_map.95.refs_0_ = bf16[2,4,64,768]{3,2,1,0:T(8,128)(2,1)} custom-call(bf16[4,64,768]{2,1,0:T(8,128)(2,1)} %collective-permute-done.2.refs_0_, bf16[4,64,768]{2,1,0:T(8,128)(2,1)} %collective-permute-done.3.refs_1_, bf16[4,64,768]{2,1,0:T(8,128)(2,1)} %shard_map.94.refs_2_, bf16[4,64,768]{2,1,0:T(8,128)(2,1)} %shard_map.93.refs_3_), custom_call_target="tpu_custom_call" | custom-call | flops 10223616000 | bytes 1 | tf_op jit(solution)/shard_map/pallas_call | solution.py:122
  83.6 2.3 %collective-permute-start.11 = (bf16[4,64,768]{2,1,0:T(8,128)(2,1)}, bf16[4,64,768]{2,1,0:T(8,128)(2,1)}, u32[]{:S(2)}, u32[]{:S(2)}) collective-permute-start(bf16[4,64,768]{2,1,0:T(8,128)(2,1)} %shard_map.94.refs_2_), channel_id=1, source_target_pairs={{0,3},{1,2},{2,1},{3,0},{4,7},{5,6},{6,5},{7,4},{8,11},{9,10},{10,... | collective-permute-start | bytes 1179656 | tf_op jit(solution)/shard_map/ppermute | solution.py:37
  85.9 3.4 %collective-permute-start.14 = (bf16[2,4,64,768]{3,2,1,0:T(8,128)(2,1)}, bf16[2,4,64,768]{3,2,1,0:T(8,128)(2,1)}, u32[]{:S(2)}, u32[]{:S(2)}) collective-permute-start(bf16[2,4,64,768]{3,2,1,0:T(8,128)(2,1)} %shard_map.96.refs_1_.refs_2_), channel_id=1, source_target_pairs={{4,8},{8,4},{12,16},{16,12},{20,24},{24,20},{5,9},{9,5},{13,17},{1... | collective-permute-start | bytes 2359304 | tf_op jit(solution)/shard_map/ppermute | solution.py:33
  89.3 0.1 collective-permute-start.12
  89.4 8.9 %shard_map.98 = (bf16[256,1536]{1,0:T(8,128)(2,1)}, bf16[256,1536]{1,0:T(8,128)(2,1)}, bf16[256,1536]{1,0:T(8,128)(2,1)}, bf16[256,1536]{1,0:T(8,128)(2,1)}) custom-call(s32[3,4]{1,0:T(4,128)} %pad_add_fusion.refs_0_, bf16[4,64,1536]{2,1,0:T(8,128)(2,1)} %get-tuple-element.15.refs_3_.refs_1_, bf16[2,4,64,768]{3,2,1,0:T(8,128)(2,1)} %shard_map.91.refs_3_.refs_2_, ...), custom_call_target="tpu_custom_call" | custom-call | flops 8999999488 | bytes 1 | tf_op jit(solution)/shard_map/pallas_call | solution.py:311
  98.4 3.7 %collective-permute-start.15 = (bf16[4,64,768]{2,1,0:T(8,128)(2,1)}, bf16[4,64,768]{2,1,0:T(8,128)(2,1)}, u32[]{:S(2)}, u32[]{:S(2)}) collective-permute-start(bf16[4,64,768]{2,1,0:T(8,128)(2,1)} %shard_map.99.refs_3_), channel_id=1, source_target_pairs={{4,8},{8,4},{12,16},{16,12},{20,24},{24,20},{5,9},{9,5},{13,17},{1... | collective-permute-start | bytes 1179656 | tf_op jit(solution)/shard_map/ppermute | solution.py:33
  102.1 0.1 collective-permute-start.13
  102.2 6.7 %collective-permute-done.14.refs_8_ = bf16[2,4,64,768]{3,2,1,0:T(8,128)(2,1)} collective-permute-done((bf16[2,4,64,768]{3,2,1,0:T(8,128)(2,1)}, bf16[2,4,64,768]{3,2,1,0:T(8,128)(2,1)}, u32[]{:S(2)}, u32[]{:S(2)}) %collective-permute-start.14) | collective-permute-done | bytes 786464 | tf_op jit(solution)/shard_map/ppermute | solution.py:33
  108.9 8.1 %collective-permute-done.15.refs_9_ = bf16[4,64,768]{2,1,0:T(8,128)(2,1)} collective-permute-done((bf16[4,64,768]{2,1,0:T(8,128)(2,1)}, bf16[4,64,768]{2,1,0:T(8,128)(2,1)}, u32[]{:S(2)}, u32[]{:S(2)}) %collective-permute-start.15) | collective-permute-done | bytes 393248 | tf_op jit(solution)/shard_map/ppermute | solution.py:33
  117.0 8.9 %shard_map.100 = (bf16[256,1536]{1,0:T(8,128)(2,1)}, bf16[256,1536]{1,0:T(8,128)(2,1)}, bf16[256,1536]{1,0:T(8,128)(2,1)}, bf16[256,1536]{1,0:T(8,128)(2,1)}) custom-call(s32[3,4]{1,0:T(4,128)} %pad_add_fusion.refs_0_, ...), custom_call_target="tpu_custom_call", output_to_operand_aliasing={{0}: (10, {}), {1}: (11, {}), {2}: (12, {}), {3}: (13, {})} | custom-call | flops 8999999488 | bytes 1 | tf_op jit(solution)/shard_map/pallas_call | solution.py:311
  (20 shorter events, 0.0 us)
Async XLA Ops:
  3.1 19.8 %collective-permute-start = (bf16[4,64,768]{2,1,0:T(8,128)(2,1)}, bf16[4,64,768]{2,1,0:T(8,128)(2,1)}, u32[]{:S(2)}, u32[]{:S(2)}) collective-permute-start(bf16[4,64,768]{2,1,0:T(8,128)(2,1)} %get-tuple-element.18), channel_id=1, source_target_pairs={{0,2},{1,3},{2,0},{3,1},{4,6},{5,7},{6,4},{7,5},{8,10},{9,11},{10,... | collective-permute-start | bytes 1179656 | tf_op jit(solution)/shard_map/ppermute | solution.py:37
  5.5 17.4 %collective-permute-start.4 = (bf16[4,64,768]{2,1,0:T(8,128)(2,1)}, bf16[4,64,768]{2,1,0:T(8,128)(2,1)}, u32[]{:S(2)}, u32[]{:S(2)}) collective-permute-start(bf16[4,64,768]{2,1,0:T(8,128)(2,1)} %get-tuple-element.21), channel_id=1, source_target_pairs={{0,1},{1,0},{2,3},{3,2},{4,5},{5,4},{6,7},{7,6},{8,9},{9,8},{10,11... | collective-permute-start | bytes 1179656 | tf_op jit(solution)/shard_map/ppermute | solution.py:37
  6.8 22.4 %collective-permute-start.6 = (bf16[4,64,1536]{2,1,0:T(8,128)(2,1)}, bf16[4,64,1536]{2,1,0:T(8,128)(2,1)}, u32[]{:S(2)}, u32[]{:S(2)}) collective-permute-start(bf16[4,64,1536]{2,1,0:T(8,128)(2,1)} %get-tuple-element.15.refs_3_.refs_1_), channel_id=1, source_target_pairs={{4,8},{8,4},{12,16},{16,12},{20,24},{24,20},{5,9},{9,5},{13,17},{1... | collective-permute-start | bytes 2359304 | tf_op jit(solution)/shard_map/ppermute | solution.py:33
  11.0 18.2 %collective-permute-start.5 = (bf16[4,64,1536]{2,1,0:T(8,128)(2,1)}, bf16[4,64,1536]{2,1,0:T(8,128)(2,1)}, u32[]{:S(2)}, u32[]{:S(2)}) collective-permute-start(bf16[4,64,1536]{2,1,0:T(8,128)(2,1)} %get-tuple-element.15.refs_3_.refs_1_), channel_id=1, source_target_pairs={{0,4},{4,0},{8,12},{12,8},{16,20},{20,16},{24,28},{28,24},{1,5},{5... | collective-permute-start | bytes 2359304 | tf_op jit(solution)/shard_map/ppermute | solution.py:33
  29.2 26.1 %collective-permute-start.7 = (bf16[2,4,64,768]{3,2,1,0:T(8,128)(2,1)}, bf16[2,4,64,768]{3,2,1,0:T(8,128)(2,1)}, u32[]{:S(2)}, u32[]{:S(2)}) collective-permute-start(bf16[2,4,64,768]{3,2,1,0:T(8,128)(2,1)} %shard_map.91.refs_3_.refs_2_), channel_id=1, source_target_pairs={{0,4},{4,0},{8,12},{12,8},{16,20},{20,16},{24,28},{28,24},{1,5},{5... | collective-permute-start | bytes 2359304 | tf_op jit(solution)/shard_map/ppermute | solution.py:33
  29.2 12.5 %collective-permute-start.1 = (bf16[4,64,768]{2,1,0:T(8,128)(2,1)}, bf16[4,64,768]{2,1,0:T(8,128)(2,1)}, u32[]{:S(2)}, u32[]{:S(2)}) collective-permute-start(bf16[4,64,768]{2,1,0:T(8,128)(2,1)} %shard_map.86.refs_2_), channel_id=1, source_target_pairs={{0,3},{1,2},{2,1},{3,0},{4,7},{5,6},{6,5},{7,4},{8,11},{9,10},{10,... | collective-permute-start | bytes 1179656 | tf_op jit(solution)/shard_map/ppermute | solution.py:37
  41.7 23.6 %collective-permute-start.3 = (bf16[4,64,768]{2,1,0:T(8,128)(2,1)}, bf16[4,64,768]{2,1,0:T(8,128)(2,1)}, u32[]{:S(2)}, u32[]{:S(2)}) collective-permute-start(bf16[4,64,768]{2,1,0:T(8,128)(2,1)} %shard_map.88.refs_2_), channel_id=1, source_target_pairs={{0,2},{1,3},{2,0},{3,1},{4,6},{5,7},{6,4},{7,5},{8,10},{9,11},{10,... | collective-permute-start | bytes 1179656 | tf_op jit(solution)/shard_map/ppermute | solution.py:37
  49.9 23.4 %collective-permute-start.10 = (bf16[2,4,64,768]{3,2,1,0:T(8,128)(2,1)}, bf16[2,4,64,768]{3,2,1,0:T(8,128)(2,1)}, u32[]{:S(2)}, u32[]{:S(2)}) collective-permute-start(bf16[2,4,64,768]{3,2,1,0:T(8,128)(2,1)} %shard_map.91.refs_3_.refs_2_), channel_id=1, source_target_pairs={{4,8},{8,4},{12,16},{16,12},{20,24},{24,20},{5,9},{9,5},{13,17},{1... | collective-permute-start | bytes 2359304 | tf_op jit(solution)/shard_map/ppermute | solution.py:33
  55.2 26.5 %collective-permute-start.2 = (bf16[4,64,768]{2,1,0:T(8,128)(2,1)}, bf16[4,64,768]{2,1,0:T(8,128)(2,1)}, u32[]{:S(2)}, u32[]{:S(2)}) collective-permute-start(bf16[4,64,768]{2,1,0:T(8,128)(2,1)} %shard_map.87.refs_1_), channel_id=1, source_target_pairs={{0,1},{1,0},{2,3},{3,2},{4,5},{5,4},{6,7},{7,6},{8,9},{9,8},{10,11... | collective-permute-start | bytes 1179656 | tf_op jit(solution)/shard_map/ppermute | solution.py:37
  55.3 26.4 %collective-permute-start.9 = (bf16[4,64,768]{2,1,0:T(8,128)(2,1)}, bf16[4,64,768]{2,1,0:T(8,128)(2,1)}, u32[]{:S(2)}, u32[]{:S(2)}) collective-permute-start(bf16[4,64,768]{2,1,0:T(8,128)(2,1)} %shard_map.93.refs_3_), channel_id=1, source_target_pairs={{4,8},{8,4},{12,16},{16,12},{20,24},{24,20},{5,9},{9,5},{13,17},{1... | collective-permute-start | bytes 1179656 | tf_op jit(solution)/shard_map/ppermute | solution.py:33
  57.3 24.4 %collective-permute-start.8 = (bf16[4,64,768]{2,1,0:T(8,128)(2,1)}, bf16[4,64,768]{2,1,0:T(8,128)(2,1)}, u32[]{:S(2)}, u32[]{:S(2)}) collective-permute-start(bf16[4,64,768]{2,1,0:T(8,128)(2,1)} %shard_map.93.refs_3_), channel_id=1, source_target_pairs={{0,4},{4,0},{8,12},{12,8},{16,20},{20,16},{24,28},{28,24},{1,5},{5... | collective-permute-start | bytes 1179656 | tf_op jit(solution)/shard_map/ppermute | solution.py:33
  83.6 14.7 %collective-permute-start.11 = (bf16[4,64,768]{2,1,0:T(8,128)(2,1)}, bf16[4,64,768]{2,1,0:T(8,128)(2,1)}, u32[]{:S(2)}, u32[]{:S(2)}) collective-permute-start(bf16[4,64,768]{2,1,0:T(8,128)(2,1)} %shard_map.94.refs_2_), channel_id=1, source_target_pairs={{0,3},{1,2},{2,1},{3,0},{4,7},{5,6},{6,5},{7,4},{8,11},{9,10},{10,... | collective-permute-start | bytes 1179656 | tf_op jit(solution)/shard_map/ppermute | solution.py:37
  85.9 22.9 %collective-permute-start.14 = (bf16[2,4,64,768]{3,2,1,0:T(8,128)(2,1)}, bf16[2,4,64,768]{3,2,1,0:T(8,128)(2,1)}, u32[]{:S(2)}, u32[]{:S(2)}) collective-permute-start(bf16[2,4,64,768]{3,2,1,0:T(8,128)(2,1)} %shard_map.96.refs_1_.refs_2_), channel_id=1, source_target_pairs={{4,8},{8,4},{12,16},{16,12},{20,24},{24,20},{5,9},{9,5},{13,17},{1... | collective-permute-start | bytes 2359304 | tf_op jit(solution)/shard_map/ppermute | solution.py:33
  89.3 9.0 %collective-permute-start.12 = (bf16[2,4,64,768]{3,2,1,0:T(8,128)(2,1)}, bf16[2,4,64,768]{3,2,1,0:T(8,128)(2,1)}, u32[]{:S(2)}, u32[]{:S(2)}) collective-permute-start(bf16[2,4,64,768]{3,2,1,0:T(8,128)(2,1)} %shard_map.96.refs_1_.refs_2_), channel_id=1, source_target_pairs={{0,4},{4,0},{8,12},{12,8},{16,20},{20,16},{24,28},{28,24},{1,5},{5... | collective-permute-start | bytes 2359304 | tf_op jit(solution)/shard_map/ppermute | solution.py:33
  98.4 18.6 %collective-permute-start.15 = (bf16[4,64,768]{2,1,0:T(8,128)(2,1)}, bf16[4,64,768]{2,1,0:T(8,128)(2,1)}, u32[]{:S(2)}, u32[]{:S(2)}) collective-permute-start(bf16[4,64,768]{2,1,0:T(8,128)(2,1)} %shard_map.99.refs_3_), channel_id=1, source_target_pairs={{4,8},{8,4},{12,16},{16,12},{20,24},{24,20},{5,9},{9,5},{13,17},{1... | collective-permute-start | bytes 1179656 | tf_op jit(solution)/shard_map/ppermute | solution.py:33
  102.1 14.9 %collective-permute-start.13 = (bf16[4,64,768]{2,1,0:T(8,128)(2,1)}, bf16[4,64,768]{2,1,0:T(8,128)(2,1)}, u32[]{:S(2)}, u32[]{:S(2)}) collective-permute-start(bf16[4,64,768]{2,1,0:T(8,128)(2,1)} %shard_map.99.refs_3_), channel_id=1, source_target_pairs={{0,4},{4,0},{8,12},{12,8},{16,20},{20,16},{24,28},{28,24},{1,5},{5... | collective-permute-start | bytes 1179656 | tf_op jit(solution)/shard_map/ppermute | solution.py:33

commit v20 on v19

--- a/solution.py
+++ b/solution.py
@@ -378,16 +378,16 @@
     outs, joined, number = None, None, 0
     for span, chunks in zip(spans, groups):
         for place in range(1 + len(chunks)):
-            after = list(sent[-1][1 : 3 if place == 0 else 2])
+            after = list(sent[-1][1 : 3 if number + 1 < len(steps) else 2])
             received, held = crossed, []
             number += 1
             if number < len(steps):
-                late = [*sent[-1][1:], sent[-2][2]] if number > 1 and place == 0 else ()
+                late = sent[-1][1:] if number > 1 and place == 0 else ()
                 cost = between(sent[-1][0], received[0]) if late else SMALL_COST
                 held, crossed = cross(steps[number], [received[-1]], cost, late)
             elif outs is not None:
                 after.append(outs[0])
-            cost = between(sent[-1][0], received[0]) if place == 0 else SMALL_COST
+            cost = between(sent[-1][0], received[0]) if number < len(steps) else SMALL_COST
             held.append(sent[-1][0])
             if place == 0:
                 joined = spread(hold(join(received, held, cost), after))

time: 127 us -> 108 us (0.85)
  waiting for transfers between devices: 64.9 us -> 45.7 us
    ppermute x6, waiting for transfers between devices: 29.3 us -> 14.8 us  [swap_flipped(): lax.ppermute(block, axis, [(i, i ^ flip) for i in range(lax.axis_size(axi...]
    ppermute x10, waiting for transfers between devices: 35.6 us -> 30.9 us  [swap_pairs(): return lax.ppermute(block, axis, route)]
    ppermute x6, starting transfers between devices: 13.2 us -> 15.1 us  [swap_flipped(): lax.ppermute(block, axis, [(i, i ^ flip) for i in range(lax.axis_size(axi...]
  transfers between devices with their start and end apart: 16 -> 16, of which waited for: 8 -> 8; matrix products, arithmetic and copies ran while one was open for 1% -> 1% of each run, Pallas kernels for 11% -> 12%
where the time goes in v20:
time: 108 us
  waiting for transfers between devices  45.7 us (42%)
  starting transfers between devices  33 us (31%)
  Pallas kernels  26.6 us (25%)
    ppermute x10, waiting for transfers between devices, swap_pairs(): return lax.ppermute(block, axis, route)  30.9 us
    ppermute x10, starting transfers between devices, swap_pairs(): return lax.ppermute(block, axis, route)  17.8 us
    pallas_call x2, Pallas kernels, attend(): pl.pallas_call(functools.partial(attend_kernel, parts, part_rows, steps,...  17.8 us
    ppermute x6, starting transfers between devices, swap_flipped(): lax.ppermute(block, axis, [(i, i ^ flip) for i in range(lax.axis_size(axi...  15.1 us
    ppermute x6, waiting for transfers between devices, swap_flipped(): lax.ppermute(block, axis, [(i, i ^ flip) for i in range(lax.axis_size(axi...  14.8 us
    pallas_call x2, Pallas kernels, pack(): pl.pallas_call(functools.partial(pack_kernel, stride, jobs), out_shape=[j...  4.88 us
    pallas_call x2, Pallas kernels, join(): pl.pallas_call(functools.partial(join_kernel, pieces), out_shape=jax.Shap...  3.88 us
  transfers between devices with their start and end apart: 16, of which 8 were waited for; matrix products, arithmetic and copies ran while one was open for 1% of the time, Pallas kernels for 12%

profile of v20, /device:TPU:3, one launch (start us, length us, event | category | flops | bytes accessed | tf_op | source)
XLA Modules:
  0.0 107.7 jit_solution(10890480529340321865)
XLA Ops:
  0.6 2.5 %shard_map.84 = (bf16[4,64,768]{2,1,0:T(8,128)(2,1)}, bf16[4,64,768]{2,1,0:T(8,128)(2,1)}, bf16[4,64,1536]{2,1,0:T(8,128)(2,1)}) custom-call(bf16[64,6144]{1,0:T(8,128)(2,1)} %refs_0_.3, bf16[64,6144]{1,0:T(8,128)(2,1)} %refs_1_.3, bf16[64,6144]{1,0:T(8,128)(2,1)} %refs_2_.3, bf16[64,6144]{1,0:T(8,128)(2,1)} %refs_3_.3), custom_call_target="tpu_custom_call" | custom-call | flops 1 | bytes 1 | tf_op jit(solution)/shard_map/pallas_call | solution.py:86
  3.1 2.4 %collective-permute-start = (bf16[4,64,768]{2,1,0:T(8,128)(2,1)}, bf16[4,64,768]{2,1,0:T(8,128)(2,1)}, u32[]{:S(2)}, u32[]{:S(2)}) collective-permute-start(bf16[4,64,768]{2,1,0:T(8,128)(2,1)} %get-tuple-element.18), channel_id=1, source_target_pairs={{0,2},{1,3},{2,0},{3,1},{4,6},{5,7},{6,4},{7,5},{8,10},{9,11},{10,... | collective-permute-start | bytes 1179656 | tf_op jit(solution)/shard_map/ppermute | solution.py:37
  5.5 1.3 %collective-permute-start.4 = (bf16[4,64,768]{2,1,0:T(8,128)(2,1)}, bf16[4,64,768]{2,1,0:T(8,128)(2,1)}, u32[]{:S(2)}, u32[]{:S(2)}) collective-permute-start(bf16[4,64,768]{2,1,0:T(8,128)(2,1)} %get-tuple-element.21), channel_id=1, source_target_pairs={{0,1},{1,0},{2,3},{3,2},{4,5},{5,4},{6,7},{7,6},{8,9},{9,8},{10,11... | collective-permute-start | bytes 1179656 | tf_op jit(solution)/shard_map/ppermute | solution.py:37
  6.8 4.2 %collective-permute-start.6 = (bf16[4,64,1536]{2,1,0:T(8,128)(2,1)}, bf16[4,64,1536]{2,1,0:T(8,128)(2,1)}, u32[]{:S(2)}, u32[]{:S(2)}) collective-permute-start(bf16[4,64,1536]{2,1,0:T(8,128)(2,1)} %get-tuple-element.15.refs_3_.refs_1_), channel_id=1, source_target_pairs={{4,8},{8,4},{12,16},{16,12},{20,24},{24,20},{5,9},{9,5},{13,17},{1... | collective-permute-start | bytes 2359304 | tf_op jit(solution)/shard_map/ppermute | solution.py:33
  11.0 0.1 collective-permute-start.5
  11.1 2.4 %shard_map.85 = (bf16[4,64,768]{2,1,0:T(8,128)(2,1)}, bf16[4,64,768]{2,1,0:T(8,128)(2,1)}, bf16[4,64,768]{2,1,0:T(8,128)(2,1)}, bf16[4,64,768]{2,1,0:T(8,128)(2,1)}) custom-call(bf16[64,6144]{1,0:T(8,128)(2,1)} %refs_0_.3, bf16[64,6144]{1,0:T(8,128)(2,1)} %refs_1_.3, bf16[64,6144]{1,0:T(8,128)(2,1)} %refs_2_.3, bf16[64,6144]{1,0:T(8,128)(2,1)} %refs_3_.3), custom_call_target="tpu_custom_call" | custom-call | flops 1 | bytes 1 | tf_op jit(solution)/shard_map/pallas_call | solution.py:86
  13.5 0.8 slice.3
  14.3 0.1 dynamic-slice_bitcast_fusion.2
  14.4 0.6 pad_add_fusion.refs_0_
  15.1 7.8 %collective-permute-done.refs_1_ = bf16[4,64,768]{2,1,0:T(8,128)(2,1)} collective-permute-done((bf16[4,64,768]{2,1,0:T(8,128)(2,1)}, bf16[4,64,768]{2,1,0:T(8,128)(2,1)}, u32[]{:S(2)}, u32[]{:S(2)}) %collective-permute-start) | collective-permute-done | bytes 393248 | tf_op jit(solution)/shard_map/ppermute | solution.py:37
  22.9 4.2 %collective-permute-start.1 = (bf16[4,64,768]{2,1,0:T(8,128)(2,1)}, bf16[4,64,768]{2,1,0:T(8,128)(2,1)}, u32[]{:S(2)}, u32[]{:S(2)}) collective-permute-start(bf16[4,64,768]{2,1,0:T(8,128)(2,1)} %shard_map.86.refs_2_), channel_id=1, source_target_pairs={{0,3},{1,2},{2,1},{3,0},{4,7},{5,6},{6,5},{7,4},{8,11},{9,10},{10,... | collective-permute-start | bytes 1179656 | tf_op jit(solution)/shard_map/ppermute | solution.py:37
  27.1 2.0 %shard_map.90.refs_0_ = bf16[2,4,64,768]{3,2,1,0:T(8,128)(2,1)} custom-call(bf16[4,64,768]{2,1,0:T(8,128)(2,1)} %collective-permute-done.4.refs_0_, bf16[4,64,768]{2,1,0:T(8,128)(2,1)} %collective-permute-done.refs_1_, bf16[4,64,768]{2,1,0:T(8,128)(2,1)} %shard_map.86.refs_2_, bf16[4,64,1536]{2,1,0:T(8,128)(2,1)} %get-tuple-element.15.refs_3_.refs_1_), custom_call_target="tpu_custom_call" | custom-call | flops 30670848000 | bytes 1 | tf_op jit(solution)/shard_map/pallas_call | solution.py:122
  29.0 0.1 collective-permute-done.6.refs_2_.refs_7_
  29.2 3.9 %collective-permute-start.8 = (bf16[2,4,64,768]{3,2,1,0:T(8,128)(2,1)}, bf16[2,4,64,768]{3,2,1,0:T(8,128)(2,1)}, u32[]{:S(2)}, u32[]{:S(2)}) collective-permute-start(bf16[2,4,64,768]{3,2,1,0:T(8,128)(2,1)} %shard_map.91.refs_3_.refs_2_), channel_id=1, source_target_pairs={{4,8},{8,4},{12,16},{16,12},{20,24},{24,20},{5,9},{9,5},{13,17},{1... | collective-permute-start | bytes 2359304 | tf_op jit(solution)/shard_map/ppermute | solution.py:33
  33.1 0.1 collective-permute-start.7
  33.2 2.9 %collective-permute-done.1.refs_1_.refs_0_ = bf16[4,64,768]{2,1,0:T(8,128)(2,1)} collective-permute-done((bf16[4,64,768]{2,1,0:T(8,128)(2,1)}, bf16[4,64,768]{2,1,0:T(8,128)(2,1)}, u32[]{:S(2)}, u32[]{:S(2)}) %collective-permute-start.1) | collective-permute-done | bytes 393248 | tf_op jit(solution)/shard_map/ppermute | solution.py:37
  36.0 7.2 %collective-permute-start.2 = (bf16[4,64,768]{2,1,0:T(8,128)(2,1)}, bf16[4,64,768]{2,1,0:T(8,128)(2,1)}, u32[]{:S(2)}, u32[]{:S(2)}) collective-permute-start(bf16[4,64,768]{2,1,0:T(8,128)(2,1)} %shard_map.87.refs_1_), channel_id=1, source_target_pairs={{0,1},{1,0},{2,3},{3,2},{4,5},{5,4},{6,7},{7,6},{8,9},{9,8},{10,11... | collective-permute-start | bytes 1179656 | tf_op jit(solution)/shard_map/ppermute | solution.py:37
  43.2 9.2 %collective-permute-done.8.refs_2_.refs_8_ = bf16[2,4,64,768]{3,2,1,0:T(8,128)(2,1)} collective-permute-done((bf16[2,4,64,768]{3,2,1,0:T(8,128)(2,1)}, bf16[2,4,64,768]{3,2,1,0:T(8,128)(2,1)}, u32[]{:S(2)}, u32[]{:S(2)}) %collective-permute-start.8) | collective-permute-done | bytes 786464 | tf_op jit(solution)/shard_map/ppermute | solution.py:33
  52.4 2.5 %collective-permute-start.10 = (bf16[4,64,768]{2,1,0:T(8,128)(2,1)}, bf16[4,64,768]{2,1,0:T(8,128)(2,1)}, u32[]{:S(2)}, u32[]{:S(2)}) collective-permute-start(bf16[4,64,768]{2,1,0:T(8,128)(2,1)} %shard_map.93.refs_3_), channel_id=1, source_target_pairs={{4,8},{8,4},{12,16},{16,12},{20,24},{24,20},{5,9},{9,5},{13,17},{1... | collective-permute-start | bytes 1179656 | tf_op jit(solution)/shard_map/ppermute | solution.py:33
  54.9 0.1 collective-permute-start.9
  55.0 4.1 %collective-permute-done.3.refs_1_ = bf16[4,64,768]{2,1,0:T(8,128)(2,1)} collective-permute-done((bf16[4,64,768]{2,1,0:T(8,128)(2,1)}, bf16[4,64,768]{2,1,0:T(8,128)(2,1)}, u32[]{:S(2)}, u32[]{:S(2)}) %collective-permute-start.3) | collective-permute-done | bytes 393248 | tf_op jit(solution)/shard_map/ppermute | solution.py:37
  59.1 6.7 %collective-permute-done.10.refs_2_.refs_9_ = bf16[4,64,768]{2,1,0:T(8,128)(2,1)} collective-permute-done((bf16[4,64,768]{2,1,0:T(8,128)(2,1)}, bf16[4,64,768]{2,1,0:T(8,128)(2,1)}, u32[]{:S(2)}, u32[]{:S(2)}) %collective-permute-start.10) | collective-permute-done | bytes 393248 | tf_op jit(solution)/shard_map/ppermute | solution.py:33
  65.8 1.9 %shard_map.95.refs_0_ = bf16[2,4,64,768]{3,2,1,0:T(8,128)(2,1)} custom-call(bf16[4,64,768]{2,1,0:T(8,128)(2,1)} %collective-permute-done.2.refs_0_, bf16[4,64,768]{2,1,0:T(8,128)(2,1)} %collective-permute-done.3.refs_1_, bf16[4,64,768]{2,1,0:T(8,128)(2,1)} %shard_map.94.refs_2_, bf16[4,64,768]{2,1,0:T(8,128)(2,1)} %shard_map.93.refs_3_), custom_call_target="tpu_custom_call" | custom-call | flops 10223616000 | bytes 1 | tf_op jit(solution)/shard_map/pallas_call | solution.py:122
  67.7 0.1 collective-permute-start.11
  67.8 3.1 %collective-permute-start.14 = (bf16[2,4,64,768]{3,2,1,0:T(8,128)(2,1)}, bf16[2,4,64,768]{3,2,1,0:T(8,128)(2,1)}, u32[]{:S(2)}, u32[]{:S(2)}) collective-permute-start(bf16[2,4,64,768]{3,2,1,0:T(8,128)(2,1)} %shard_map.96.refs_1_.refs_2_), channel_id=1, source_target_pairs={{4,8},{8,4},{12,16},{16,12},{20,24},{24,20},{5,9},{9,5},{13,17},{1... | collective-permute-start | bytes 2359304 | tf_op jit(solution)/shard_map/ppermute | solution.py:33
  70.9 0.1 collective-permute-start.12
  71.0 8.9 %shard_map.98 = (bf16[256,1536]{1,0:T(8,128)(2,1)}, bf16[256,1536]{1,0:T(8,128)(2,1)}, bf16[256,1536]{1,0:T(8,128)(2,1)}, bf16[256,1536]{1,0:T(8,128)(2,1)}) custom-call(s32[3,4]{1,0:T(4,128)} %pad_add_fusion.refs_0_, bf16[4,64,1536]{2,1,0:T(8,128)(2,1)} %get-tuple-element.15.refs_3_.refs_1_, bf16[2,4,64,768]{3,2,1,0:T(8,128)(2,1)} %shard_map.91.refs_3_.refs_2_, ...), custom_call_target="tpu_custom_call" | custom-call | flops 8999999488 | bytes 1 | tf_op jit(solution)/shard_map/pallas_call | solution.py:311
  80.0 3.7 %collective-permute-start.15 = (bf16[4,64,768]{2,1,0:T(8,128)(2,1)}, bf16[4,64,768]{2,1,0:T(8,128)(2,1)}, u32[]{:S(2)}, u32[]{:S(2)}) collective-permute-start(bf16[4,64,768]{2,1,0:T(8,128)(2,1)} %shard_map.99.refs_3_), channel_id=1, source_target_pairs={{4,8},{8,4},{12,16},{16,12},{20,24},{24,20},{5,9},{9,5},{13,17},{1... | collective-permute-start | bytes 1179656 | tf_op jit(solution)/shard_map/ppermute | solution.py:33
  83.7 0.1 collective-permute-start.13
  83.8 6.8 %collective-permute-done.14.refs_8_ = bf16[2,4,64,768]{3,2,1,0:T(8,128)(2,1)} collective-permute-done((bf16[2,4,64,768]{3,2,1,0:T(8,128)(2,1)}, bf16[2,4,64,768]{3,2,1,0:T(8,128)(2,1)}, u32[]{:S(2)}, u32[]{:S(2)}) %collective-permute-start.14) | collective-permute-done | bytes 786464 | tf_op jit(solution)/shard_map/ppermute | solution.py:33
  90.7 8.0 %collective-permute-done.15.refs_9_ = bf16[4,64,768]{2,1,0:T(8,128)(2,1)} collective-permute-done((bf16[4,64,768]{2,1,0:T(8,128)(2,1)}, bf16[4,64,768]{2,1,0:T(8,128)(2,1)}, u32[]{:S(2)}, u32[]{:S(2)}) %collective-permute-start.15) | collective-permute-done | bytes 393248 | tf_op jit(solution)/shard_map/ppermute | solution.py:33
  98.7 8.9 %shard_map.100 = (bf16[256,1536]{1,0:T(8,128)(2,1)}, bf16[256,1536]{1,0:T(8,128)(2,1)}, bf16[256,1536]{1,0:T(8,128)(2,1)}, bf16[256,1536]{1,0:T(8,128)(2,1)}) custom-call(s32[3,4]{1,0:T(4,128)} %pad_add_fusion.refs_0_, ...), custom_call_target="tpu_custom_call", output_to_operand_aliasing={{0}: (10, {}), {1}: (11, {}), {2}: (12, {}), {3}: (13, {})} | custom-call | flops 8999999488 | bytes 1 | tf_op jit(solution)/shard_map/pallas_call | solution.py:311
  (20 shorter events, 0.1 us)
Async XLA Ops:
  3.1 19.8 %collective-permute-start = (bf16[4,64,768]{2,1,0:T(8,128)(2,1)}, bf16[4,64,768]{2,1,0:T(8,128)(2,1)}, u32[]{:S(2)}, u32[]{:S(2)}) collective-permute-start(bf16[4,64,768]{2,1,0:T(8,128)(2,1)} %get-tuple-element.18), channel_id=1, source_target_pairs={{0,2},{1,3},{2,0},{3,1},{4,6},{5,7},{6,4},{7,5},{8,10},{9,11},{10,... | collective-permute-start | bytes 1179656 | tf_op jit(solution)/shard_map/ppermute | solution.py:37
  5.5 21.6 %collective-permute-start.4 = (bf16[4,64,768]{2,1,0:T(8,128)(2,1)}, bf16[4,64,768]{2,1,0:T(8,128)(2,1)}, u32[]{:S(2)}, u32[]{:S(2)}) collective-permute-start(bf16[4,64,768]{2,1,0:T(8,128)(2,1)} %get-tuple-element.21), channel_id=1, source_target_pairs={{0,1},{1,0},{2,3},{3,2},{4,5},{5,4},{6,7},{7,6},{8,9},{9,8},{10,11... | collective-permute-start | bytes 1179656 | tf_op jit(solution)/shard_map/ppermute | solution.py:37
  6.8 22.4 %collective-permute-start.6 = (bf16[4,64,1536]{2,1,0:T(8,128)(2,1)}, bf16[4,64,1536]{2,1,0:T(8,128)(2,1)}, u32[]{:S(2)}, u32[]{:S(2)}) collective-permute-start(bf16[4,64,1536]{2,1,0:T(8,128)(2,1)} %get-tuple-element.15.refs_3_.refs_1_), channel_id=1, source_target_pairs={{4,8},{8,4},{12,16},{16,12},{20,24},{24,20},{5,9},{9,5},{13,17},{1... | collective-permute-start | bytes 2359304 | tf_op jit(solution)/shard_map/ppermute | solution.py:33
  11.0 18.2 %collective-permute-start.5 = (bf16[4,64,1536]{2,1,0:T(8,128)(2,1)}, bf16[4,64,1536]{2,1,0:T(8,128)(2,1)}, u32[]{:S(2)}, u32[]{:S(2)}) collective-permute-start(bf16[4,64,1536]{2,1,0:T(8,128)(2,1)} %get-tuple-element.15.refs_3_.refs_1_), channel_id=1, source_target_pairs={{0,4},{4,0},{8,12},{12,8},{16,20},{20,16},{24,28},{28,24},{1,5},{5... | collective-permute-start | bytes 2359304 | tf_op jit(solution)/shard_map/ppermute | solution.py:33
  22.9 13.2 %collective-permute-start.1 = (bf16[4,64,768]{2,1,0:T(8,128)(2,1)}, bf16[4,64,768]{2,1,0:T(8,128)(2,1)}, u32[]{:S(2)}, u32[]{:S(2)}) collective-permute-start(bf16[4,64,768]{2,1,0:T(8,128)(2,1)} %shard_map.86.refs_2_), channel_id=1, source_target_pairs={{0,3},{1,2},{2,1},{3,0},{4,7},{5,6},{6,5},{7,4},{8,11},{9,10},{10,... | collective-permute-start | bytes 1179656 | tf_op jit(solution)/shard_map/ppermute | solution.py:37
  29.2 23.2 %collective-permute-start.8 = (bf16[2,4,64,768]{3,2,1,0:T(8,128)(2,1)}, bf16[2,4,64,768]{3,2,1,0:T(8,128)(2,1)}, u32[]{:S(2)}, u32[]{:S(2)}) collective-permute-start(bf16[2,4,64,768]{3,2,1,0:T(8,128)(2,1)} %shard_map.91.refs_3_.refs_2_), channel_id=1, source_target_pairs={{4,8},{8,4},{12,16},{16,12},{20,24},{24,20},{5,9},{9,5},{13,17},{1... | collective-permute-start | bytes 2359304 | tf_op jit(solution)/shard_map/ppermute | solution.py:33
  33.1 19.3 %collective-permute-start.7 = (bf16[2,4,64,768]{3,2,1,0:T(8,128)(2,1)}, bf16[2,4,64,768]{3,2,1,0:T(8,128)(2,1)}, u32[]{:S(2)}, u32[]{:S(2)}) collective-permute-start(bf16[2,4,64,768]{3,2,1,0:T(8,128)(2,1)} %shard_map.91.refs_3_.refs_2_), channel_id=1, source_target_pairs={{0,4},{4,0},{8,12},{12,8},{16,20},{20,16},{24,28},{28,24},{1,5},{5... | collective-permute-start | bytes 2359304 | tf_op jit(solution)/shard_map/ppermute | solution.py:33
  36.0 29.7 %collective-permute-start.2 = (bf16[4,64,768]{2,1,0:T(8,128)(2,1)}, bf16[4,64,768]{2,1,0:T(8,128)(2,1)}, u32[]{:S(2)}, u32[]{:S(2)}) collective-permute-start(bf16[4,64,768]{2,1,0:T(8,128)(2,1)} %shard_map.87.refs_1_), channel_id=1, source_target_pairs={{0,1},{1,0},{2,3},{3,2},{4,5},{5,4},{6,7},{7,6},{8,9},{9,8},{10,11... | collective-permute-start | bytes 1179656 | tf_op jit(solution)/shard_map/ppermute | solution.py:37
  43.2 15.9 %collective-permute-start.3 = (bf16[4,64,768]{2,1,0:T(8,128)(2,1)}, bf16[4,64,768]{2,1,0:T(8,128)(2,1)}, u32[]{:S(2)}, u32[]{:S(2)}) collective-permute-start(bf16[4,64,768]{2,1,0:T(8,128)(2,1)} %shard_map.88.refs_2_), channel_id=1, source_target_pairs={{0,2},{1,3},{2,0},{3,1},{4,6},{5,7},{6,4},{7,5},{8,10},{9,11},{10,... | collective-permute-start | bytes 1179656 | tf_op jit(solution)/shard_map/ppermute | solution.py:37
  52.4 13.4 %collective-permute-start.10 = (bf16[4,64,768]{2,1,0:T(8,128)(2,1)}, bf16[4,64,768]{2,1,0:T(8,128)(2,1)}, u32[]{:S(2)}, u32[]{:S(2)}) collective-permute-start(bf16[4,64,768]{2,1,0:T(8,128)(2,1)} %shard_map.93.refs_3_), channel_id=1, source_target_pairs={{4,8},{8,4},{12,16},{16,12},{20,24},{24,20},{5,9},{9,5},{13,17},{1... | collective-permute-start | bytes 1179656 | tf_op jit(solution)/shard_map/ppermute | solution.py:33
  54.9 10.9 %collective-permute-start.9 = (bf16[4,64,768]{2,1,0:T(8,128)(2,1)}, bf16[4,64,768]{2,1,0:T(8,128)(2,1)}, u32[]{:S(2)}, u32[]{:S(2)}) collective-permute-start(bf16[4,64,768]{2,1,0:T(8,128)(2,1)} %shard_map.93.refs_3_), channel_id=1, source_target_pairs={{0,4},{4,0},{8,12},{12,8},{16,20},{20,16},{24,28},{28,24},{1,5},{5... | collective-permute-start | bytes 1179656 | tf_op jit(solution)/shard_map/ppermute | solution.py:33
  67.7 12.3 %collective-permute-start.11 = (bf16[4,64,768]{2,1,0:T(8,128)(2,1)}, bf16[4,64,768]{2,1,0:T(8,128)(2,1)}, u32[]{:S(2)}, u32[]{:S(2)}) collective-permute-start(bf16[4,64,768]{2,1,0:T(8,128)(2,1)} %shard_map.94.refs_2_), channel_id=1, source_target_pairs={{0,3},{1,2},{2,1},{3,0},{4,7},{5,6},{6,5},{7,4},{8,11},{9,10},{10,... | collective-permute-start | bytes 1179656 | tf_op jit(solution)/shard_map/ppermute | solution.py:37
  67.8 22.9 %collective-permute-start.14 = (bf16[2,4,64,768]{3,2,1,0:T(8,128)(2,1)}, bf16[2,4,64,768]{3,2,1,0:T(8,128)(2,1)}, u32[]{:S(2)}, u32[]{:S(2)}) collective-permute-start(bf16[2,4,64,768]{3,2,1,0:T(8,128)(2,1)} %shard_map.96.refs_1_.refs_2_), channel_id=1, source_target_pairs={{4,8},{8,4},{12,16},{16,12},{20,24},{24,20},{5,9},{9,5},{13,17},{1... | collective-permute-start | bytes 2359304 | tf_op jit(solution)/shard_map/ppermute | solution.py:33
  70.9 9.0 %collective-permute-start.12 = (bf16[2,4,64,768]{3,2,1,0:T(8,128)(2,1)}, bf16[2,4,64,768]{3,2,1,0:T(8,128)(2,1)}, u32[]{:S(2)}, u32[]{:S(2)}) collective-permute-start(bf16[2,4,64,768]{3,2,1,0:T(8,128)(2,1)} %shard_map.96.refs_1_.refs_2_), channel_id=1, source_target_pairs={{0,4},{4,0},{8,12},{12,8},{16,20},{20,16},{24,28},{28,24},{1,5},{5... | collective-permute-start | bytes 2359304 | tf_op jit(solution)/shard_map/ppermute | solution.py:33
  80.0 18.7 %collective-permute-start.15 = (bf16[4,64,768]{2,1,0:T(8,128)(2,1)}, bf16[4,64,768]{2,1,0:T(8,128)(2,1)}, u32[]{:S(2)}, u32[]{:S(2)}) collective-permute-start(bf16[4,64,768]{2,1,0:T(8,128)(2,1)} %shard_map.99.refs_3_), channel_id=1, source_target_pairs={{4,8},{8,4},{12,16},{16,12},{20,24},{24,20},{5,9},{9,5},{13,17},{1... | collective-permute-start | bytes 1179656 | tf_op jit(solution)/shard_map/ppermute | solution.py:33
  83.7 14.9 %collective-permute-start.13 = (bf16[4,64,768]{2,1,0:T(8,128)(2,1)}, bf16[4,64,768]{2,1,0:T(8,128)(2,1)}, u32[]{:S(2)}, u32[]{:S(2)}) collective-permute-start(bf16[4,64,768]{2,1,0:T(8,128)(2,1)} %shard_map.99.refs_3_), channel_id=1, source_target_pairs={{0,4},{4,0},{8,12},{12,8},{16,20},{20,16},{24,28},{28,24},{1,5},{5... | collective-permute-start | bytes 1179656 | tf_op jit(solution)/shard_map/ppermute | solution.py:33

commit v21 on v20

--- a/solution.py
+++ b/solution.py
@@ -12,7 +12,7 @@
 SCALE = 1.0 / math.sqrt(HD)
 EXP2_SCALE = SCALE * math.log2(math.e)
 MASKED = -1e30
-GROUPS = ((6,), (6,))
+GROUPS = ((6,), (4, 2))
 VMEM_LIMIT = 64 * 1024 * 1024 - 256 * 1024
 ATTEND_FLOPS = 1_500_000_000
 FLOPS_PER_BYTE = 52_000
@@ -378,16 +378,17 @@
     outs, joined, number = None, None, 0
     for span, chunks in zip(spans, groups):
         for place in range(1 + len(chunks)):
-            after = list(sent[-1][1 : 3 if number + 1 < len(steps) else 2])
+            final = place >= 1 and span is spans[-1]
+            after = list(sent[-1][1 : 2 if final else 3])
             received, held = crossed, []
             number += 1
             if number < len(steps):
                 late = sent[-1][1:] if number > 1 and place == 0 else ()
                 cost = between(sent[-1][0], received[0]) if late else SMALL_COST
                 held, crossed = cross(steps[number], [received[-1]], cost, late)
-            elif outs is not None:
+            if final and place == 1 and outs is not None:
                 after.append(outs[0])
-            cost = between(sent[-1][0], received[0]) if number < len(steps) else SMALL_COST
+            cost = SMALL_COST if final else between(sent[-1][0], received[0])
             held.append(sent[-1][0])
             if place == 0:
                 joined = spread(hold(join(received, held, cost), after))

time: 108 us -> 113 us (1.046); the launches traced: 108 us -> 111 us
  waiting for transfers between devices: 45.7 us -> 40.2 us
  starting transfers between devices: 33 us -> 37.8 us
  Pallas kernels: 26.6 us -> 29.6 us
  local copies, waits for them, and re-layouts: 0.9 us -> 2.18 us
    ppermute x10 -> x12, waiting for transfers between devices: 30.9 us -> 16.1 us  [swap_pairs(): return lax.ppermute(block, axis, route)]
    ppermute x6 -> x7, waiting for transfers between devices: 14.8 us -> 24.1 us  [swap_flipped(): lax.ppermute(block, axis, [(i, i ^ flip) for i in range(lax.axis_size(axi...]
    ppermute x10 -> x12, starting transfers between devices: 17.8 us -> 21.2 us  [swap_pairs(): return lax.ppermute(block, axis, route)]
    pallas_call x2 -> x3, Pallas kernels: 17.8 us -> 20.8 us  [attend(): pl.pallas_call(functools.partial(attend_kernel, parts, part_rows, steps,...]
    ppermute x6 -> x7, starting transfers between devices: 15.1 us -> 16.6 us  [swap_flipped(): lax.ppermute(block, axis, [(i, i ^ flip) for i in range(lax.axis_size(axi...]
    unnamed x0 -> x4, local copies, waits for them, and re-layouts: none -> 1.27 us
  transfers between devices with their start and end apart: 16 -> 19, of which waited for: 8 -> 8; matrix products, arithmetic and copies ran while one was open for 1% -> 1% of each run, Pallas kernels for 12% -> 20%
where the time goes in v21:
time: 113 us; the launch traced here: 111 us
  waiting for transfers between devices  40.2 us (36%)
  starting transfers between devices  37.8 us (33%)
  Pallas kernels  29.6 us (26%)
  local copies, waits for them, and re-layouts  2.18 us (2%)
    ppermute x7, waiting for transfers between devices, swap_flipped(): lax.ppermute(block, axis, [(i, i ^ flip) for i in range(lax.axis_size(axi...  24.1 us
    ppermute x12, starting transfers between devices, swap_pairs(): return lax.ppermute(block, axis, route)  21.2 us
    pallas_call x3, Pallas kernels, attend(): pl.pallas_call(functools.partial(attend_kernel, parts, part_rows, steps,...  20.8 us
    ppermute x7, starting transfers between devices, swap_flipped(): lax.ppermute(block, axis, [(i, i ^ flip) for i in range(lax.axis_size(axi...  16.6 us
    ppermute x12, waiting for transfers between devices, swap_pairs(): return lax.ppermute(block, axis, route)  16.1 us
    pallas_call x2, Pallas kernels, pack(): pl.pallas_call(functools.partial(pack_kernel, stride, jobs), out_shape=[j...  4.92 us
    pallas_call x2, Pallas kernels, join(): pl.pallas_call(functools.partial(join_kernel, pieces), out_shape=jax.Shap...  3.85 us
  transfers between devices with their start and end apart: 19, of which 8 were waited for; matrix products, arithmetic and copies ran while one was open for 1% of the time, Pallas kernels for 20%

profile of v21, /device:TPU:3, one launch (start us, length us, event | category | flops | bytes accessed | tf_op | source)
XLA Modules:
  0.0 111.5 jit_solution(107386585261019016)
XLA Ops:
  0.6 2.5 %shard_map.84 = (bf16[4,64,768]{2,1,0:T(8,128)(2,1)}, bf16[4,64,768]{2,1,0:T(8,128)(2,1)}, bf16[4,64,1536]{2,1,0:T(8,128)(2,1)}) custom-call(bf16[64,6144]{1,0:T(8,128)(2,1)} %refs_0_.3, bf16[64,6144]{1,0:T(8,128)(2,1)} %refs_1_.3, bf16[64,6144]{1,0:T(8,128)(2,1)} %refs_2_.3, bf16[64,6144]{1,0:T(8,128)(2,1)} %refs_3_.3), custom_call_target="tpu_custom_call" | custom-call | flops 1 | bytes 1 | tf_op jit(solution)/shard_map/pallas_call | solution.py:86
  3.1 2.4 %collective-permute-start = (bf16[4,64,768]{2,1,0:T(8,128)(2,1)}, bf16[4,64,768]{2,1,0:T(8,128)(2,1)}, u32[]{:S(2)}, u32[]{:S(2)}) collective-permute-start(bf16[4,64,768]{2,1,0:T(8,128)(2,1)} %get-tuple-element.23), channel_id=1, source_target_pairs={{0,2},{1,3},{2,0},{3,1},{4,6},{5,7},{6,4},{7,5},{8,10},{9,11},{10,... | collective-permute-start | bytes 1179656 | tf_op jit(solution)/shard_map/ppermute | solution.py:37
  5.5 1.3 %collective-permute-start.4 = (bf16[4,64,768]{2,1,0:T(8,128)(2,1)}, bf16[4,64,768]{2,1,0:T(8,128)(2,1)}, u32[]{:S(2)}, u32[]{:S(2)}) collective-permute-start(bf16[4,64,768]{2,1,0:T(8,128)(2,1)} %get-tuple-element.26), channel_id=1, source_target_pairs={{0,1},{1,0},{2,3},{3,2},{4,5},{5,4},{6,7},{7,6},{8,9},{9,8},{10,11... | collective-permute-start | bytes 1179656 | tf_op jit(solution)/shard_map/ppermute | solution.py:37
  6.8 4.2 %collective-permute-start.6 = (bf16[4,64,1536]{2,1,0:T(8,128)(2,1)}, bf16[4,64,1536]{2,1,0:T(8,128)(2,1)}, u32[]{:S(2)}, u32[]{:S(2)}) collective-permute-start(bf16[4,64,1536]{2,1,0:T(8,128)(2,1)} %get-tuple-element.20.refs_3_.refs_1_), channel_id=1, source_target_pairs={{4,8},{8,4},{12,16},{16,12},{20,24},{24,20},{5,9},{9,5},{13,17},{1... | collective-permute-start | bytes 2359304 | tf_op jit(solution)/shard_map/ppermute | solution.py:33
  11.0 0.1 collective-permute-start.5
  11.1 2.4 %shard_map.85 = (bf16[4,64,768]{2,1,0:T(8,128)(2,1)}, bf16[4,64,768]{2,1,0:T(8,128)(2,1)}, bf16[4,64,768]{2,1,0:T(8,128)(2,1)}, bf16[4,64,512]{2,1,0:T(8,128)(2,1)}, bf16[4,64,256]{2,1,0:T(8,128)(2,1)}) custom-call(bf16[64,6144]{1,0:T(8,128)(2,1)} %refs_0_.3, bf16[64,6144]{1,0:T(8,128)(2,1)} %refs_1_.3, bf16[64,6144]{1,0:T(8,128)(2,1)} %refs_2_.3, ...), custom_call_target="tpu_custom_call" | custom-call | flops 1 | bytes 1 | tf_op jit(solution)/shard_map/pallas_call | solution.py:86
  13.6 0.8 slice.3
  14.4 0.1 dynamic-slice_bitcast_fusion.2
  14.5 8.4 %collective-permute-done.refs_1_ = bf16[4,64,768]{2,1,0:T(8,128)(2,1)} collective-permute-done((bf16[4,64,768]{2,1,0:T(8,128)(2,1)}, bf16[4,64,768]{2,1,0:T(8,128)(2,1)}, u32[]{:S(2)}, u32[]{:S(2)}) %collective-permute-start) | collective-permute-done | bytes 393248 | tf_op jit(solution)/shard_map/ppermute | solution.py:37
  22.9 4.2 %collective-permute-start.1 = (bf16[4,64,768]{2,1,0:T(8,128)(2,1)}, bf16[4,64,768]{2,1,0:T(8,128)(2,1)}, u32[]{:S(2)}, u32[]{:S(2)}) collective-permute-start(bf16[4,64,768]{2,1,0:T(8,128)(2,1)} %shard_map.86.refs_2_), channel_id=1, source_target_pairs={{0,3},{1,2},{2,1},{3,0},{4,7},{5,6},{6,5},{7,4},{8,11},{9,10},{10,... | collective-permute-start | bytes 1179656 | tf_op jit(solution)/shard_map/ppermute | solution.py:37
  27.1 1.9 %shard_map.90.refs_0_ = bf16[2,4,64,768]{3,2,1,0:T(8,128)(2,1)} custom-call(bf16[4,64,768]{2,1,0:T(8,128)(2,1)} %collective-permute-done.4.refs_0_, bf16[4,64,768]{2,1,0:T(8,128)(2,1)} %collective-permute-done.refs_1_, bf16[4,64,768]{2,1,0:T(8,128)(2,1)} %shard_map.86.refs_2_, bf16[4,64,1536]{2,1,0:T(8,128)(2,1)} %get-tuple-element.20.refs_3_.refs_1_), custom_call_target="tpu_custom_call" | custom-call | flops 30670848000 | bytes 1 | tf_op jit(solution)/shard_map/pallas_call | solution.py:122
  29.0 0.2 collective-permute-done.6.refs_2_.refs_7_
  29.2 3.9 %collective-permute-start.8 = (bf16[2,4,64,768]{3,2,1,0:T(8,128)(2,1)}, bf16[2,4,64,768]{3,2,1,0:T(8,128)(2,1)}, u32[]{:S(2)}, u32[]{:S(2)}) collective-permute-start(bf16[2,4,64,768]{3,2,1,0:T(8,128)(2,1)} %shard_map.91.refs_3_.refs_2_), channel_id=1, source_target_pairs={{4,8},{8,4},{12,16},{16,12},{20,24},{24,20},{5,9},{9,5},{13,17},{1... | collective-permute-start | bytes 2359304 | tf_op jit(solution)/shard_map/ppermute | solution.py:33
  33.1 2.9 %collective-permute-done.1.refs_1_.refs_0_ = bf16[4,64,768]{2,1,0:T(8,128)(2,1)} collective-permute-done((bf16[4,64,768]{2,1,0:T(8,128)(2,1)}, bf16[4,64,768]{2,1,0:T(8,128)(2,1)}, u32[]{:S(2)}, u32[]{:S(2)}) %collective-permute-start.1) | collective-permute-done | bytes 393248 | tf_op jit(solution)/shard_map/ppermute | solution.py:37
  36.0 7.2 %collective-permute-start.2 = (bf16[4,64,768]{2,1,0:T(8,128)(2,1)}, bf16[4,64,768]{2,1,0:T(8,128)(2,1)}, u32[]{:S(2)}, u32[]{:S(2)}) collective-permute-start(bf16[4,64,768]{2,1,0:T(8,128)(2,1)} %shard_map.87.refs_1_), channel_id=1, source_target_pairs={{0,1},{1,0},{2,3},{3,2},{4,5},{5,4},{6,7},{7,6},{8,9},{9,8},{10,11... | collective-permute-start | bytes 1179656 | tf_op jit(solution)/shard_map/ppermute | solution.py:37
  43.2 9.2 %collective-permute-done.8.refs_2_.refs_8_ = bf16[2,4,64,768]{3,2,1,0:T(8,128)(2,1)} collective-permute-done((bf16[2,4,64,768]{3,2,1,0:T(8,128)(2,1)}, bf16[2,4,64,768]{3,2,1,0:T(8,128)(2,1)}, u32[]{:S(2)}, u32[]{:S(2)}) %collective-permute-start.8) | collective-permute-done | bytes 786464 | tf_op jit(solution)/shard_map/ppermute | solution.py:33
  52.4 2.4 %collective-permute-start.10 = (bf16[4,64,768]{2,1,0:T(8,128)(2,1)}, bf16[4,64,768]{2,1,0:T(8,128)(2,1)}, u32[]{:S(2)}, u32[]{:S(2)}) collective-permute-start(bf16[4,64,768]{2,1,0:T(8,128)(2,1)} %shard_map.93.refs_3_), channel_id=1, source_target_pairs={{4,8},{8,4},{12,16},{16,12},{20,24},{24,20},{5,9},{9,5},{13,17},{1... | collective-permute-start | bytes 1179656 | tf_op jit(solution)/shard_map/ppermute | solution.py:33
  54.9 4.1 %collective-permute-done.3.refs_1_ = bf16[4,64,768]{2,1,0:T(8,128)(2,1)} collective-permute-done((bf16[4,64,768]{2,1,0:T(8,128)(2,1)}, bf16[4,64,768]{2,1,0:T(8,128)(2,1)}, u32[]{:S(2)}, u32[]{:S(2)}) %collective-permute-start.3) | collective-permute-done | bytes 393248 | tf_op jit(solution)/shard_map/ppermute | solution.py:37
  59.0 6.7 %collective-permute-done.10.refs_2_.refs_9_ = bf16[4,64,768]{2,1,0:T(8,128)(2,1)} collective-permute-done((bf16[4,64,768]{2,1,0:T(8,128)(2,1)}, bf16[4,64,768]{2,1,0:T(8,128)(2,1)}, u32[]{:S(2)}, u32[]{:S(2)}) %collective-permute-start.10) | collective-permute-done | bytes 393248 | tf_op jit(solution)/shard_map/ppermute | solution.py:33
  65.8 1.9 %shard_map.95.refs_0_ = bf16[2,4,64,768]{3,2,1,0:T(8,128)(2,1)} custom-call(bf16[4,64,768]{2,1,0:T(8,128)(2,1)} %collective-permute-done.2.refs_0_, bf16[4,64,768]{2,1,0:T(8,128)(2,1)} %collective-permute-done.3.refs_1_, bf16[4,64,512]{2,1,0:T(8,128)(2,1)} %shard_map.94.refs_2_, bf16[4,64,768]{2,1,0:T(8,128)(2,1)} %shard_map.93.refs_3_), custom_call_target="tpu_custom_call" | custom-call | flops 10223616000 | bytes 1 | tf_op jit(solution)/shard_map/pallas_call | solution.py:122
  67.7 0.6 pad_add_fusion.refs_0_
  68.3 3.2 %collective-permute-start.16 = (bf16[2,4,64,768]{3,2,1,0:T(8,128)(2,1)}, bf16[2,4,64,768]{3,2,1,0:T(8,128)(2,1)}, u32[]{:S(2)}, u32[]{:S(2)}) collective-permute-start(bf16[2,4,64,768]{3,2,1,0:T(8,128)(2,1)} %shard_map.96.refs_2_), channel_id=1, source_target_pairs={{4,8},{8,4},{12,16},{16,12},{20,24},{24,20},{5,9},{9,5},{13,17},{1... | collective-permute-start | bytes 2359304 | tf_op jit(solution)/shard_map/ppermute | solution.py:33
  71.6 3.6 %collective-permute-done.11.refs_1_.refs_0_ = bf16[4,64,512]{2,1,0:T(8,128)(2,1)} collective-permute-done((bf16[4,64,512]{2,1,0:T(8,128)(2,1)}, bf16[4,64,512]{2,1,0:T(8,128)(2,1)}, u32[]{:S(2)}, u32[]{:S(2)}) %collective-permute-start.11) | collective-permute-done | bytes 262176 | tf_op jit(solution)/shard_map/ppermute | solution.py:37
  75.2 8.9 %shard_map.99 = (bf16[256,1536]{1,0:T(8,128)(2,1)}, bf16[256,1536]{1,0:T(8,128)(2,1)}, bf16[256,1536]{1,0:T(8,128)(2,1)}, bf16[256,1536]{1,0:T(8,128)(2,1)}) custom-call(s32[3,4]{1,0:T(4,128)} %pad_add_fusion.refs_0_, bf16[4,64,1536]{2,1,0:T(8,128)(2,1)} %get-tuple-element.20.refs_3_.refs_1_, bf16[2,4,64,768]{3,2,1,0:T(8,128)(2,1)} %shard_map.91.refs_3_.refs_2_, ...), custom_call_target="tpu_custom_call" | custom-call | flops 8999999488 | bytes 1 | tf_op jit(solution)/shard_map/pallas_call | solution.py:311
  84.2 1.9 %collective-permute-start.18 = (bf16[4,64,512]{2,1,0:T(8,128)(2,1)}, bf16[4,64,512]{2,1,0:T(8,128)(2,1)}, u32[]{:S(2)}, u32[]{:S(2)}) collective-permute-start(bf16[4,64,512]{2,1,0:T(8,128)(2,1)} %shard_map.100.refs_1_.refs_3_), channel_id=1, source_target_pairs={{4,8},{8,4},{12,16},{16,12},{20,24},{24,20},{5,9},{9,5},{13,17},{1... | collective-permute-start | bytes 786440 | tf_op jit(solution)/shard_map/ppermute | solution.py:33
  86.2 1.5 %collective-permute-start.12 = (bf16[4,64,256]{2,1,0:T(8,128)(2,1)}, bf16[4,64,256]{2,1,0:T(8,128)(2,1)S(1)}, u32[]{:S(2)}, u32[]{:S(2)}) collective-permute-start(bf16[4,64,256]{2,1,0:T(8,128)(2,1)} %shard_map.97.refs_1_), channel_id=1, source_target_pairs={{0,3},{1,2},{2,1},{3,0},{4,7},{5,6},{6,5},{7,4},{8,11},{9,10},{10,... | collective-permute-start | bytes 393224 | tf_op jit(solution)/shard_map/ppermute | solution.py:37
  87.7 5.1 %collective-permute-done.12.refs_0_ = bf16[4,64,256]{2,1,0:T(8,128)(2,1)S(1)} collective-permute-done((bf16[4,64,256]{2,1,0:T(8,128)(2,1)}, bf16[4,64,256]{2,1,0:T(8,128)(2,1)S(1)}, u32[]{:S(2)}, u32[]{:S(2)}) %collective-permute-start.12) | collective-permute-done | bytes 131104 | tf_op jit(solution)/shard_map/ppermute | solution.py:37
  92.8 0.6 copy-done
  93.5 5.1 %collective-permute-start.17 = (bf16[4,64,256]{2,1,0:T(8,128)(2,1)}, bf16[4,64,256]{2,1,0:T(8,128)(2,1)S(1)}, u32[]{:S(2)}, u32[]{:S(2)}) collective-permute-start(bf16[4,64,256]{2,1,0:T(8,128)(2,1)} %shard_map.102.refs_3_), channel_id=1, source_target_pairs={{4,8},{8,4},{12,16},{16,12},{20,24},{24,20},{5,9},{9,5},{13,17},{1... | collective-permute-start | bytes 393224 | tf_op jit(solution)/shard_map/ppermute | solution.py:33
  98.7 6.9 %shard_map.103 = (bf16[256,1536]{1,0:T(8,128)(2,1)}, bf16[256,1536]{1,0:T(8,128)(2,1)}, bf16[256,1536]{1,0:T(8,128)(2,1)}, bf16[256,1536]{1,0:T(8,128)(2,1)}) custom-call(s32[3,4]{1,0:T(4,128)} %pad_add_fusion.refs_0_, ...), custom_call_target="tpu_custom_call", output_to_operand_aliasing={{0}: (10, {}), {1}: (11, {}), {2}: (12, {}), {3}: (13, {})} | custom-call | flops 6000000000 | bytes 1 | tf_op jit(solution)/shard_map/pallas_call | solution.py:311
  105.6 0.6 copy-done.1
  106.3 5.0 %shard_map.104 = (bf16[256,1536]{1,0:T(8,128)(2,1)}, bf16[256,1536]{1,0:T(8,128)(2,1)}, bf16[256,1536]{1,0:T(8,128)(2,1)}, bf16[256,1536]{1,0:T(8,128)(2,1)}) custom-call(s32[3,4]{1,0:T(4,128)} %pad_add_fusion.refs_0_, ...), custom_call_target="tpu_custom_call", output_to_operand_aliasing={{0}: (10, {}), {1}: (11, {}), {2}: (12, {}), {3}: (13, {})} | custom-call | flops 3000000000 | bytes 1 | tf_op jit(solution)/shard_map/pallas_call | solution.py:311
  (34 shorter events, 0.4 us)
Async XLA Ops:
  3.1 19.8 %collective-permute-start = (bf16[4,64,768]{2,1,0:T(8,128)(2,1)}, bf16[4,64,768]{2,1,0:T(8,128)(2,1)}, u32[]{:S(2)}, u32[]{:S(2)}) collective-permute-start(bf16[4,64,768]{2,1,0:T(8,128)(2,1)} %get-tuple-element.23), channel_id=1, source_target_pairs={{0,2},{1,3},{2,0},{3,1},{4,6},{5,7},{6,4},{7,5},{8,10},{9,11},{10,... | collective-permute-start | bytes 1179656 | tf_op jit(solution)/shard_map/ppermute | solution.py:37
  5.5 21.6 %collective-permute-start.4 = (bf16[4,64,768]{2,1,0:T(8,128)(2,1)}, bf16[4,64,768]{2,1,0:T(8,128)(2,1)}, u32[]{:S(2)}, u32[]{:S(2)}) collective-permute-start(bf16[4,64,768]{2,1,0:T(8,128)(2,1)} %get-tuple-element.26), channel_id=1, source_target_pairs={{0,1},{1,0},{2,3},{3,2},{4,5},{5,4},{6,7},{7,6},{8,9},{9,8},{10,11... | collective-permute-start | bytes 1179656 | tf_op jit(solution)/shard_map/ppermute | solution.py:37
  6.8 22.4 %collective-permute-start.6 = (bf16[4,64,1536]{2,1,0:T(8,128)(2,1)}, bf16[4,64,1536]{2,1,0:T(8,128)(2,1)}, u32[]{:S(2)}, u32[]{:S(2)}) collective-permute-start(bf16[4,64,1536]{2,1,0:T(8,128)(2,1)} %get-tuple-element.20.refs_3_.refs_1_), channel_id=1, source_target_pairs={{4,8},{8,4},{12,16},{16,12},{20,24},{24,20},{5,9},{9,5},{13,17},{1... | collective-permute-start | bytes 2359304 | tf_op jit(solution)/shard_map/ppermute | solution.py:33
  11.0 18.2 %collective-permute-start.5 = (bf16[4,64,1536]{2,1,0:T(8,128)(2,1)}, bf16[4,64,1536]{2,1,0:T(8,128)(2,1)}, u32[]{:S(2)}, u32[]{:S(2)}) collective-permute-start(bf16[4,64,1536]{2,1,0:T(8,128)(2,1)} %get-tuple-element.20.refs_3_.refs_1_), channel_id=1, source_target_pairs={{0,4},{4,0},{8,12},{12,8},{16,20},{20,16},{24,28},{28,24},{1,5},{5... | collective-permute-start | bytes 2359304 | tf_op jit(solution)/shard_map/ppermute | solution.py:33
  22.9 13.2 %collective-permute-start.1 = (bf16[4,64,768]{2,1,0:T(8,128)(2,1)}, bf16[4,64,768]{2,1,0:T(8,128)(2,1)}, u32[]{:S(2)}, u32[]{:S(2)}) collective-permute-start(bf16[4,64,768]{2,1,0:T(8,128)(2,1)} %shard_map.86.refs_2_), channel_id=1, source_target_pairs={{0,3},{1,2},{2,1},{3,0},{4,7},{5,6},{6,5},{7,4},{8,11},{9,10},{10,... | collective-permute-start | bytes 1179656 | tf_op jit(solution)/shard_map/ppermute | solution.py:37
  29.2 23.2 %collective-permute-start.8 = (bf16[2,4,64,768]{3,2,1,0:T(8,128)(2,1)}, bf16[2,4,64,768]{3,2,1,0:T(8,128)(2,1)}, u32[]{:S(2)}, u32[]{:S(2)}) collective-permute-start(bf16[2,4,64,768]{3,2,1,0:T(8,128)(2,1)} %shard_map.91.refs_3_.refs_2_), channel_id=1, source_target_pairs={{4,8},{8,4},{12,16},{16,12},{20,24},{24,20},{5,9},{9,5},{13,17},{1... | collective-permute-start | bytes 2359304 | tf_op jit(solution)/shard_map/ppermute | solution.py:33
  33.1 19.4 %collective-permute-start.7 = (bf16[2,4,64,768]{3,2,1,0:T(8,128)(2,1)}, bf16[2,4,64,768]{3,2,1,0:T(8,128)(2,1)}, u32[]{:S(2)}, u32[]{:S(2)}) collective-permute-start(bf16[2,4,64,768]{3,2,1,0:T(8,128)(2,1)} %shard_map.91.refs_3_.refs_2_), channel_id=1, source_target_pairs={{0,4},{4,0},{8,12},{12,8},{16,20},{20,16},{24,28},{28,24},{1,5},{5... | collective-permute-start | bytes 2359304 | tf_op jit(solution)/shard_map/ppermute | solution.py:33
  36.0 29.7 %collective-permute-start.2 = (bf16[4,64,768]{2,1,0:T(8,128)(2,1)}, bf16[4,64,768]{2,1,0:T(8,128)(2,1)}, u32[]{:S(2)}, u32[]{:S(2)}) collective-permute-start(bf16[4,64,768]{2,1,0:T(8,128)(2,1)} %shard_map.87.refs_1_), channel_id=1, source_target_pairs={{0,1},{1,0},{2,3},{3,2},{4,5},{5,4},{6,7},{7,6},{8,9},{9,8},{10,11... | collective-permute-start | bytes 1179656 | tf_op jit(solution)/shard_map/ppermute | solution.py:37
  43.2 15.9 %collective-permute-start.3 = (bf16[4,64,768]{2,1,0:T(8,128)(2,1)}, bf16[4,64,768]{2,1,0:T(8,128)(2,1)}, u32[]{:S(2)}, u32[]{:S(2)}) collective-permute-start(bf16[4,64,768]{2,1,0:T(8,128)(2,1)} %shard_map.88.refs_2_), channel_id=1, source_target_pairs={{0,2},{1,3},{2,0},{3,1},{4,6},{5,7},{6,4},{7,5},{8,10},{9,11},{10,... | collective-permute-start | bytes 1179656 | tf_op jit(solution)/shard_map/ppermute | solution.py:37
  52.4 13.3 %collective-permute-start.10 = (bf16[4,64,768]{2,1,0:T(8,128)(2,1)}, bf16[4,64,768]{2,1,0:T(8,128)(2,1)}, u32[]{:S(2)}, u32[]{:S(2)}) collective-permute-start(bf16[4,64,768]{2,1,0:T(8,128)(2,1)} %shard_map.93.refs_3_), channel_id=1, source_target_pairs={{4,8},{8,4},{12,16},{16,12},{20,24},{24,20},{5,9},{9,5},{13,17},{1... | collective-permute-start | bytes 1179656 | tf_op jit(solution)/shard_map/ppermute | solution.py:33
  54.9 10.9 %collective-permute-start.9 = (bf16[4,64,768]{2,1,0:T(8,128)(2,1)}, bf16[4,64,768]{2,1,0:T(8,128)(2,1)}, u32[]{:S(2)}, u32[]{:S(2)}) collective-permute-start(bf16[4,64,768]{2,1,0:T(8,128)(2,1)} %shard_map.93.refs_3_), channel_id=1, source_target_pairs={{0,4},{4,0},{8,12},{12,8},{16,20},{20,16},{24,28},{28,24},{1,5},{5... | collective-permute-start | bytes 1179656 | tf_op jit(solution)/shard_map/ppermute | solution.py:33
  65.8 9.4 %collective-permute-start.11 = (bf16[4,64,512]{2,1,0:T(8,128)(2,1)}, bf16[4,64,512]{2,1,0:T(8,128)(2,1)}, u32[]{:S(2)}, u32[]{:S(2)}) collective-permute-start(bf16[4,64,512]{2,1,0:T(8,128)(2,1)} %shard_map.94.refs_2_), channel_id=1, source_target_pairs={{0,3},{1,2},{2,1},{3,0},{4,7},{5,6},{6,5},{7,4},{8,11},{9,10},{10,... | collective-permute-start | bytes 786440 | tf_op jit(solution)/shard_map/ppermute | solution.py:37
  68.3 30.4 %collective-permute-start.16 = (bf16[2,4,64,768]{3,2,1,0:T(8,128)(2,1)}, bf16[2,4,64,768]{3,2,1,0:T(8,128)(2,1)}, u32[]{:S(2)}, u32[]{:S(2)}) collective-permute-start(bf16[2,4,64,768]{3,2,1,0:T(8,128)(2,1)} %shard_map.96.refs_2_), channel_id=1, source_target_pairs={{4,8},{8,4},{12,16},{16,12},{20,24},{24,20},{5,9},{9,5},{13,17},{1... | collective-permute-start | bytes 2359304 | tf_op jit(solution)/shard_map/ppermute | solution.py:33
  71.5 12.6 %collective-permute-start.13 = (bf16[2,4,64,768]{3,2,1,0:T(8,128)(2,1)}, bf16[2,4,64,768]{3,2,1,0:T(8,128)(2,1)}, u32[]{:S(2)}, u32[]{:S(2)}) collective-permute-start(bf16[2,4,64,768]{3,2,1,0:T(8,128)(2,1)} %shard_map.96.refs_2_), channel_id=1, source_target_pairs={{0,4},{4,0},{8,12},{12,8},{16,20},{20,16},{24,28},{28,24},{1,5},{5... | collective-permute-start | bytes 2359304 | tf_op jit(solution)/shard_map/ppermute | solution.py:33
  84.2 9.3 %collective-permute-start.14 = (bf16[4,64,512]{2,1,0:T(8,128)(2,1)}, bf16[4,64,512]{2,1,0:T(8,128)(2,1)}, u32[]{:S(2)}, u32[]{:S(2)}) collective-permute-start(bf16[4,64,512]{2,1,0:T(8,128)(2,1)} %shard_map.100.refs_1_.refs_3_), channel_id=1, source_target_pairs={{0,4},{4,0},{8,12},{12,8},{16,20},{20,16},{24,28},{28,24},{1,5},{5... | collective-permute-start | bytes 786440 | tf_op jit(solution)/shard_map/ppermute | solution.py:33
  84.2 14.5 %collective-permute-start.18 = (bf16[4,64,512]{2,1,0:T(8,128)(2,1)}, bf16[4,64,512]{2,1,0:T(8,128)(2,1)}, u32[]{:S(2)}, u32[]{:S(2)}) collective-permute-start(bf16[4,64,512]{2,1,0:T(8,128)(2,1)} %shard_map.100.refs_1_.refs_3_), channel_id=1, source_target_pairs={{4,8},{8,4},{12,16},{16,12},{20,24},{24,20},{5,9},{9,5},{13,17},{1... | collective-permute-start | bytes 786440 | tf_op jit(solution)/shard_map/ppermute | solution.py:33
  86.2 6.7 %collective-permute-start.12 = (bf16[4,64,256]{2,1,0:T(8,128)(2,1)}, bf16[4,64,256]{2,1,0:T(8,128)(2,1)S(1)}, u32[]{:S(2)}, u32[]{:S(2)}) collective-permute-start(bf16[4,64,256]{2,1,0:T(8,128)(2,1)} %shard_map.97.refs_1_), channel_id=1, source_target_pairs={{0,3},{1,2},{2,1},{3,0},{4,7},{5,6},{6,5},{7,4},{8,11},{9,10},{10,... | collective-permute-start | bytes 393224 | tf_op jit(solution)/shard_map/ppermute | solution.py:37
  92.8 0.6 copy-start
  93.5 12.1 %collective-permute-start.17 = (bf16[4,64,256]{2,1,0:T(8,128)(2,1)}, bf16[4,64,256]{2,1,0:T(8,128)(2,1)S(1)}, u32[]{:S(2)}, u32[]{:S(2)}) collective-permute-start(bf16[4,64,256]{2,1,0:T(8,128)(2,1)} %shard_map.102.refs_3_), channel_id=1, source_target_pairs={{4,8},{8,4},{12,16},{16,12},{20,24},{24,20},{5,9},{9,5},{13,17},{1... | collective-permute-start | bytes 393224 | tf_op jit(solution)/shard_map/ppermute | solution.py:33
  98.6 7.0 %collective-permute-start.15 = (bf16[4,64,256]{2,1,0:T(8,128)(2,1)}, bf16[4,64,256]{2,1,0:T(8,128)(2,1)}, u32[]{:S(2)}, u32[]{:S(2)}) collective-permute-start(bf16[4,64,256]{2,1,0:T(8,128)(2,1)} %shard_map.102.refs_3_), channel_id=1, source_target_pairs={{0,4},{4,0},{8,12},{12,8},{16,20},{20,16},{24,28},{28,24},{1,5},{5... | collective-permute-start | bytes 393224 | tf_op jit(solution)/shard_map/ppermute | solution.py:33
  105.6 0.6 copy-start.1

commit v22 on v20

--- a/solution.py
+++ b/solution.py
@@ -205,12 +205,15 @@
 
     results = [[None] * 4 for _ in heads]
     work = [(head, start) for head in range(len(heads)) for start in range(0, size, rows)]
-    ahead = products(*work[0])
+    ahead, behind = products(*work[0]), None
     for number, (head, start) in enumerate(work):
         scores, grad_probs = ahead
         if number + 1 < len(work):
             ahead = products(*work[number + 1])
-        finish(head, *weigh(scores, grad_probs, start), start)
+        if behind is not None:
+            finish(*behind)
+        behind = (head, *weigh(scores, grad_probs, start), start)
+    finish(*behind)
     for result in results:
         result[2] = (result[2] * SCALE).astype(jnp.bfloat16)
         result[3] = result[3].astype(jnp.bfloat16)
@@ -239,9 +242,11 @@
             sems.at[buffer, sem],
         )
 
-    def copies(number, act):
+    def own_copies(number, act):
         for flip in range(parts):
             act(copy_of(mine, flip, number, me ^ flip, flip))
+
+    def other_copies(number, act):
         for source in range(2 * parts):
             slot = slot_of[source]
 
@@ -252,6 +257,7 @@
 
     @pl.when(step == 0)
     def _():
+        own_copies(0, lambda copy: copy.start())
         count = jnp.int32(0)
         for slot in range(2 * parts):
             table[slot] = -2
@@ -265,8 +271,14 @@
             table[count] = jnp.where(shared, other_id, -2)
             count = count + shared.astype(jnp.int32)
         table[2 * parts] = count
-        window[:, :, rows:] = jnp.zeros((2, 4, most - rows, width), window.dtype)
-        copies(0, lambda copy: copy.start())
+        other_copies(0, lambda copy: copy.start())
+        for slot in range(2 * parts):
+
+            @pl.when((slot >= count) & (slot < (count + parts - 1) // parts * parts))
+            def _():
+                place = slice(rows + slot * part_rows, rows + (slot + 1) * part_rows)
+                window[:, :, place] = jnp.zeros((2, 4, part_rows, width), window.dtype)
+
         place = lax.broadcasted_iota(jnp.int32, (8, most), 1)
         ids = jnp.full((8, most), -2, jnp.int32)
         for slot in range(3 * parts):
@@ -277,9 +289,11 @@
 
     @pl.when(step + 1 < steps)
     def _():
-        copies(step + 1, lambda copy: copy.start())
-
-    copies(step, lambda copy: copy.wait())
+        own_copies(step + 1, lambda copy: copy.start())
+        other_copies(step + 1, lambda copy: copy.start())
+
+    own_copies(step, lambda copy: copy.wait())
+    other_copies(step, lambda copy: copy.wait())
     count = table[2 * parts]
     buffer = lax.rem(step, 2)
     for size in range(rows, most + 1, rows):

time: 108 us -> 108 us (level)
  transfers between devices with their start and end apart: 16 -> 16, of which waited for: 8 -> 9; matrix products, arithmetic and copies ran while one was open for 1% -> 1% of each run, Pallas kernels for 12% -> 12%
where the time goes in v22:
time: 108 us
  waiting for transfers between devices  45.8 us (42%)
  starting transfers between devices  33 us (31%)
  Pallas kernels  26.4 us (24%)
    ppermute x10, waiting for transfers between devices, swap_pairs(): return lax.ppermute(block, axis, route)  30.9 us
    ppermute x10, starting transfers between devices, swap_pairs(): return lax.ppermute(block, axis, route)  17.8 us
    pallas_call x2, Pallas kernels, attend(): pl.pallas_call(functools.partial(attend_kernel, parts, part_rows, steps,...  17.7 us
    ppermute x6, starting transfers between devices, swap_flipped(): lax.ppermute(block, axis, [(i, i ^ flip) for i in range(lax.axis_size(axi...  15.1 us
    ppermute x6, waiting for transfers between devices, swap_flipped(): lax.ppermute(block, axis, [(i, i ^ flip) for i in range(lax.axis_size(axi...  14.9 us
    pallas_call x2, Pallas kernels, pack(): pl.pallas_call(functools.partial(pack_kernel, stride, jobs), out_shape=[j...  4.88 us
    pallas_call x2, Pallas kernels, join(): pl.pallas_call(functools.partial(join_kernel, pieces), out_shape=jax.Shap...  3.88 us
  transfers between devices with their start and end apart: 16, of which 9 were waited for; matrix products, arithmetic and copies ran while one was open for 1% of the time, Pallas kernels for 12%

profile of v22, /device:TPU:3, one launch (start us, length us, event | category | flops | bytes accessed | tf_op | source)
XLA Modules:
  0.0 107.7 jit_solution(16652555027342603643)
XLA Ops:
  0.6 2.5 %shard_map.84 = (bf16[4,64,768]{2,1,0:T(8,128)(2,1)}, bf16[4,64,768]{2,1,0:T(8,128)(2,1)}, bf16[4,64,1536]{2,1,0:T(8,128)(2,1)}) custom-call(bf16[64,6144]{1,0:T(8,128)(2,1)} %refs_0_.3, bf16[64,6144]{1,0:T(8,128)(2,1)} %refs_1_.3, bf16[64,6144]{1,0:T(8,128)(2,1)} %refs_2_.3, bf16[64,6144]{1,0:T(8,128)(2,1)} %refs_3_.3), custom_call_target="tpu_custom_call" | custom-call | flops 1 | bytes 1 | tf_op jit(solution)/shard_map/pallas_call | solution.py:86
  3.1 2.4 %collective-permute-start = (bf16[4,64,768]{2,1,0:T(8,128)(2,1)}, bf16[4,64,768]{2,1,0:T(8,128)(2,1)}, u32[]{:S(2)}, u32[]{:S(2)}) collective-permute-start(bf16[4,64,768]{2,1,0:T(8,128)(2,1)} %get-tuple-element.18), channel_id=1, source_target_pairs={{0,2},{1,3},{2,0},{3,1},{4,6},{5,7},{6,4},{7,5},{8,10},{9,11},{10,... | collective-permute-start | bytes 1179656 | tf_op jit(solution)/shard_map/ppermute | solution.py:37
  5.5 1.3 %collective-permute-start.4 = (bf16[4,64,768]{2,1,0:T(8,128)(2,1)}, bf16[4,64,768]{2,1,0:T(8,128)(2,1)}, u32[]{:S(2)}, u32[]{:S(2)}) collective-permute-start(bf16[4,64,768]{2,1,0:T(8,128)(2,1)} %get-tuple-element.21), channel_id=1, source_target_pairs={{0,1},{1,0},{2,3},{3,2},{4,5},{5,4},{6,7},{7,6},{8,9},{9,8},{10,11... | collective-permute-start | bytes 1179656 | tf_op jit(solution)/shard_map/ppermute | solution.py:37
  6.8 4.2 %collective-permute-start.6 = (bf16[4,64,1536]{2,1,0:T(8,128)(2,1)}, bf16[4,64,1536]{2,1,0:T(8,128)(2,1)}, u32[]{:S(2)}, u32[]{:S(2)}) collective-permute-start(bf16[4,64,1536]{2,1,0:T(8,128)(2,1)} %get-tuple-element.15.refs_3_.refs_1_), channel_id=1, source_target_pairs={{4,8},{8,4},{12,16},{16,12},{20,24},{24,20},{5,9},{9,5},{13,17},{1... | collective-permute-start | bytes 2359304 | tf_op jit(solution)/shard_map/ppermute | solution.py:33
  11.0 0.1 collective-permute-start.5
  11.1 2.4 %shard_map.85 = (bf16[4,64,768]{2,1,0:T(8,128)(2,1)}, bf16[4,64,768]{2,1,0:T(8,128)(2,1)}, bf16[4,64,768]{2,1,0:T(8,128)(2,1)}, bf16[4,64,768]{2,1,0:T(8,128)(2,1)}) custom-call(bf16[64,6144]{1,0:T(8,128)(2,1)} %refs_0_.3, bf16[64,6144]{1,0:T(8,128)(2,1)} %refs_1_.3, bf16[64,6144]{1,0:T(8,128)(2,1)} %refs_2_.3, bf16[64,6144]{1,0:T(8,128)(2,1)} %refs_3_.3), custom_call_target="tpu_custom_call" | custom-call | flops 1 | bytes 1 | tf_op jit(solution)/shard_map/pallas_call | solution.py:86
  13.5 0.8 slice.3
  14.3 0.1 dynamic-slice_bitcast_fusion.2
  14.4 0.6 pad_add_fusion.refs_0_
  15.1 7.8 %collective-permute-done.refs_1_ = bf16[4,64,768]{2,1,0:T(8,128)(2,1)} collective-permute-done((bf16[4,64,768]{2,1,0:T(8,128)(2,1)}, bf16[4,64,768]{2,1,0:T(8,128)(2,1)}, u32[]{:S(2)}, u32[]{:S(2)}) %collective-permute-start) | collective-permute-done | bytes 393248 | tf_op jit(solution)/shard_map/ppermute | solution.py:37
  22.9 4.2 %collective-permute-start.1 = (bf16[4,64,768]{2,1,0:T(8,128)(2,1)}, bf16[4,64,768]{2,1,0:T(8,128)(2,1)}, u32[]{:S(2)}, u32[]{:S(2)}) collective-permute-start(bf16[4,64,768]{2,1,0:T(8,128)(2,1)} %shard_map.86.refs_2_), channel_id=1, source_target_pairs={{0,3},{1,2},{2,1},{3,0},{4,7},{5,6},{6,5},{7,4},{8,11},{9,10},{10,... | collective-permute-start | bytes 1179656 | tf_op jit(solution)/shard_map/ppermute | solution.py:37
  27.1 2.0 %shard_map.90.refs_0_ = bf16[2,4,64,768]{3,2,1,0:T(8,128)(2,1)} custom-call(bf16[4,64,768]{2,1,0:T(8,128)(2,1)} %collective-permute-done.4.refs_0_, bf16[4,64,768]{2,1,0:T(8,128)(2,1)} %collective-permute-done.refs_1_, bf16[4,64,768]{2,1,0:T(8,128)(2,1)} %shard_map.86.refs_2_, bf16[4,64,1536]{2,1,0:T(8,128)(2,1)} %get-tuple-element.15.refs_3_.refs_1_), custom_call_target="tpu_custom_call" | custom-call | flops 30670848000 | bytes 1 | tf_op jit(solution)/shard_map/pallas_call | solution.py:122
  29.0 0.1 collective-permute-done.6.refs_2_.refs_7_
  29.2 3.9 %collective-permute-start.8 = (bf16[2,4,64,768]{3,2,1,0:T(8,128)(2,1)}, bf16[2,4,64,768]{3,2,1,0:T(8,128)(2,1)}, u32[]{:S(2)}, u32[]{:S(2)}) collective-permute-start(bf16[2,4,64,768]{3,2,1,0:T(8,128)(2,1)} %shard_map.91.refs_3_.refs_2_), channel_id=1, source_target_pairs={{4,8},{8,4},{12,16},{16,12},{20,24},{24,20},{5,9},{9,5},{13,17},{1... | collective-permute-start | bytes 2359304 | tf_op jit(solution)/shard_map/ppermute | solution.py:33
  33.1 0.1 collective-permute-start.7
  33.2 2.9 %collective-permute-done.1.refs_1_.refs_0_ = bf16[4,64,768]{2,1,0:T(8,128)(2,1)} collective-permute-done((bf16[4,64,768]{2,1,0:T(8,128)(2,1)}, bf16[4,64,768]{2,1,0:T(8,128)(2,1)}, u32[]{:S(2)}, u32[]{:S(2)}) %collective-permute-start.1) | collective-permute-done | bytes 393248 | tf_op jit(solution)/shard_map/ppermute | solution.py:37
  36.0 7.2 %collective-permute-start.2 = (bf16[4,64,768]{2,1,0:T(8,128)(2,1)}, bf16[4,64,768]{2,1,0:T(8,128)(2,1)}, u32[]{:S(2)}, u32[]{:S(2)}) collective-permute-start(bf16[4,64,768]{2,1,0:T(8,128)(2,1)} %shard_map.87.refs_1_), channel_id=1, source_target_pairs={{0,1},{1,0},{2,3},{3,2},{4,5},{5,4},{6,7},{7,6},{8,9},{9,8},{10,11... | collective-permute-start | bytes 1179656 | tf_op jit(solution)/shard_map/ppermute | solution.py:37
  43.2 9.2 %collective-permute-done.8.refs_2_.refs_8_ = bf16[2,4,64,768]{3,2,1,0:T(8,128)(2,1)} collective-permute-done((bf16[2,4,64,768]{3,2,1,0:T(8,128)(2,1)}, bf16[2,4,64,768]{3,2,1,0:T(8,128)(2,1)}, u32[]{:S(2)}, u32[]{:S(2)}) %collective-permute-start.8) | collective-permute-done | bytes 786464 | tf_op jit(solution)/shard_map/ppermute | solution.py:33
  52.4 2.5 %collective-permute-start.10 = (bf16[4,64,768]{2,1,0:T(8,128)(2,1)}, bf16[4,64,768]{2,1,0:T(8,128)(2,1)}, u32[]{:S(2)}, u32[]{:S(2)}) collective-permute-start(bf16[4,64,768]{2,1,0:T(8,128)(2,1)} %shard_map.93.refs_3_), channel_id=1, source_target_pairs={{4,8},{8,4},{12,16},{16,12},{20,24},{24,20},{5,9},{9,5},{13,17},{1... | collective-permute-start | bytes 1179656 | tf_op jit(solution)/shard_map/ppermute | solution.py:33
  54.9 0.1 collective-permute-start.9
  55.0 4.1 %collective-permute-done.3.refs_1_ = bf16[4,64,768]{2,1,0:T(8,128)(2,1)} collective-permute-done((bf16[4,64,768]{2,1,0:T(8,128)(2,1)}, bf16[4,64,768]{2,1,0:T(8,128)(2,1)}, u32[]{:S(2)}, u32[]{:S(2)}) %collective-permute-start.3) | collective-permute-done | bytes 393248 | tf_op jit(solution)/shard_map/ppermute | solution.py:37
  59.1 6.7 %collective-permute-done.10.refs_2_.refs_9_ = bf16[4,64,768]{2,1,0:T(8,128)(2,1)} collective-permute-done((bf16[4,64,768]{2,1,0:T(8,128)(2,1)}, bf16[4,64,768]{2,1,0:T(8,128)(2,1)}, u32[]{:S(2)}, u32[]{:S(2)}) %collective-permute-start.10) | collective-permute-done | bytes 393248 | tf_op jit(solution)/shard_map/ppermute | solution.py:33
  65.8 1.9 %shard_map.95.refs_0_ = bf16[2,4,64,768]{3,2,1,0:T(8,128)(2,1)} custom-call(bf16[4,64,768]{2,1,0:T(8,128)(2,1)} %collective-permute-done.2.refs_0_, bf16[4,64,768]{2,1,0:T(8,128)(2,1)} %collective-permute-done.3.refs_1_, bf16[4,64,768]{2,1,0:T(8,128)(2,1)} %shard_map.94.refs_2_, bf16[4,64,768]{2,1,0:T(8,128)(2,1)} %shard_map.93.refs_3_), custom_call_target="tpu_custom_call" | custom-call | flops 10223616000 | bytes 1 | tf_op jit(solution)/shard_map/pallas_call | solution.py:122
  67.7 0.1 collective-permute-start.11
  67.8 3.1 %collective-permute-start.14 = (bf16[2,4,64,768]{3,2,1,0:T(8,128)(2,1)}, bf16[2,4,64,768]{3,2,1,0:T(8,128)(2,1)}, u32[]{:S(2)}, u32[]{:S(2)}) collective-permute-start(bf16[2,4,64,768]{3,2,1,0:T(8,128)(2,1)} %shard_map.96.refs_1_.refs_2_), channel_id=1, source_target_pairs={{4,8},{8,4},{12,16},{16,12},{20,24},{24,20},{5,9},{9,5},{13,17},{1... | collective-permute-start | bytes 2359304 | tf_op jit(solution)/shard_map/ppermute | solution.py:33
  70.9 0.1 collective-permute-start.12
  71.0 8.9 %shard_map.98 = (bf16[256,1536]{1,0:T(8,128)(2,1)}, bf16[256,1536]{1,0:T(8,128)(2,1)}, bf16[256,1536]{1,0:T(8,128)(2,1)}, bf16[256,1536]{1,0:T(8,128)(2,1)}) custom-call(s32[3,4]{1,0:T(4,128)} %pad_add_fusion.refs_0_, bf16[4,64,1536]{2,1,0:T(8,128)(2,1)} %get-tuple-element.15.refs_3_.refs_1_, bf16[2,4,64,768]{3,2,1,0:T(8,128)(2,1)} %shard_map.91.refs_3_.refs_2_, ...), custom_call_target="tpu_custom_call" | custom-call | flops 8999999488 | bytes 1 | tf_op jit(solution)/shard_map/pallas_call | solution.py:325
  79.9 0.1 collective-permute-done.11.refs_0_
  80.0 3.7 %collective-permute-start.15 = (bf16[4,64,768]{2,1,0:T(8,128)(2,1)}, bf16[4,64,768]{2,1,0:T(8,128)(2,1)}, u32[]{:S(2)}, u32[]{:S(2)}) collective-permute-start(bf16[4,64,768]{2,1,0:T(8,128)(2,1)} %shard_map.99.refs_3_), channel_id=1, source_target_pairs={{4,8},{8,4},{12,16},{16,12},{20,24},{24,20},{5,9},{9,5},{13,17},{1... | collective-permute-start | bytes 1179656 | tf_op jit(solution)/shard_map/ppermute | solution.py:33
  83.8 6.9 %collective-permute-done.14.refs_8_ = bf16[2,4,64,768]{3,2,1,0:T(8,128)(2,1)} collective-permute-done((bf16[2,4,64,768]{3,2,1,0:T(8,128)(2,1)}, bf16[2,4,64,768]{3,2,1,0:T(8,128)(2,1)}, u32[]{:S(2)}, u32[]{:S(2)}) %collective-permute-start.14) | collective-permute-done | bytes 786464 | tf_op jit(solution)/shard_map/ppermute | solution.py:33
  90.7 8.0 %collective-permute-done.15.refs_9_ = bf16[4,64,768]{2,1,0:T(8,128)(2,1)} collective-permute-done((bf16[4,64,768]{2,1,0:T(8,128)(2,1)}, bf16[4,64,768]{2,1,0:T(8,128)(2,1)}, u32[]{:S(2)}, u32[]{:S(2)}) %collective-permute-start.15) | collective-permute-done | bytes 393248 | tf_op jit(solution)/shard_map/ppermute | solution.py:33
  98.7 8.8 %shard_map.100 = (bf16[256,1536]{1,0:T(8,128)(2,1)}, bf16[256,1536]{1,0:T(8,128)(2,1)}, bf16[256,1536]{1,0:T(8,128)(2,1)}, bf16[256,1536]{1,0:T(8,128)(2,1)}) custom-call(s32[3,4]{1,0:T(4,128)} %pad_add_fusion.refs_0_, ...), custom_call_target="tpu_custom_call", output_to_operand_aliasing={{0}: (10, {}), {1}: (11, {}), {2}: (12, {}), {3}: (13, {})} | custom-call | flops 8999999488 | bytes 1 | tf_op jit(solution)/shard_map/pallas_call | solution.py:325
  (20 shorter events, 0.1 us)
Async XLA Ops:
  3.1 19.8 %collective-permute-start = (bf16[4,64,768]{2,1,0:T(8,128)(2,1)}, bf16[4,64,768]{2,1,0:T(8,128)(2,1)}, u32[]{:S(2)}, u32[]{:S(2)}) collective-permute-start(bf16[4,64,768]{2,1,0:T(8,128)(2,1)} %get-tuple-element.18), channel_id=1, source_target_pairs={{0,2},{1,3},{2,0},{3,1},{4,6},{5,7},{6,4},{7,5},{8,10},{9,11},{10,... | collective-permute-start | bytes 1179656 | tf_op jit(solution)/shard_map/ppermute | solution.py:37
  5.5 21.6 %collective-permute-start.4 = (bf16[4,64,768]{2,1,0:T(8,128)(2,1)}, bf16[4,64,768]{2,1,0:T(8,128)(2,1)}, u32[]{:S(2)}, u32[]{:S(2)}) collective-permute-start(bf16[4,64,768]{2,1,0:T(8,128)(2,1)} %get-tuple-element.21), channel_id=1, source_target_pairs={{0,1},{1,0},{2,3},{3,2},{4,5},{5,4},{6,7},{7,6},{8,9},{9,8},{10,11... | collective-permute-start | bytes 1179656 | tf_op jit(solution)/shard_map/ppermute | solution.py:37
  6.8 22.4 %collective-permute-start.6 = (bf16[4,64,1536]{2,1,0:T(8,128)(2,1)}, bf16[4,64,1536]{2,1,0:T(8,128)(2,1)}, u32[]{:S(2)}, u32[]{:S(2)}) collective-permute-start(bf16[4,64,1536]{2,1,0:T(8,128)(2,1)} %get-tuple-element.15.refs_3_.refs_1_), channel_id=1, source_target_pairs={{4,8},{8,4},{12,16},{16,12},{20,24},{24,20},{5,9},{9,5},{13,17},{1... | collective-permute-start | bytes 2359304 | tf_op jit(solution)/shard_map/ppermute | solution.py:33
  11.0 18.2 %collective-permute-start.5 = (bf16[4,64,1536]{2,1,0:T(8,128)(2,1)}, bf16[4,64,1536]{2,1,0:T(8,128)(2,1)}, u32[]{:S(2)}, u32[]{:S(2)}) collective-permute-start(bf16[4,64,1536]{2,1,0:T(8,128)(2,1)} %get-tuple-element.15.refs_3_.refs_1_), channel_id=1, source_target_pairs={{0,4},{4,0},{8,12},{12,8},{16,20},{20,16},{24,28},{28,24},{1,5},{5... | collective-permute-start | bytes 2359304 | tf_op jit(solution)/shard_map/ppermute | solution.py:33
  22.9 13.2 %collective-permute-start.1 = (bf16[4,64,768]{2,1,0:T(8,128)(2,1)}, bf16[4,64,768]{2,1,0:T(8,128)(2,1)}, u32[]{:S(2)}, u32[]{:S(2)}) collective-permute-start(bf16[4,64,768]{2,1,0:T(8,128)(2,1)} %shard_map.86.refs_2_), channel_id=1, source_target_pairs={{0,3},{1,2},{2,1},{3,0},{4,7},{5,6},{6,5},{7,4},{8,11},{9,10},{10,... | collective-permute-start | bytes 1179656 | tf_op jit(solution)/shard_map/ppermute | solution.py:37
  29.2 23.2 %collective-permute-start.8 = (bf16[2,4,64,768]{3,2,1,0:T(8,128)(2,1)}, bf16[2,4,64,768]{3,2,1,0:T(8,128)(2,1)}, u32[]{:S(2)}, u32[]{:S(2)}) collective-permute-start(bf16[2,4,64,768]{3,2,1,0:T(8,128)(2,1)} %shard_map.91.refs_3_.refs_2_), channel_id=1, source_target_pairs={{4,8},{8,4},{12,16},{16,12},{20,24},{24,20},{5,9},{9,5},{13,17},{1... | collective-permute-start | bytes 2359304 | tf_op jit(solution)/shard_map/ppermute | solution.py:33
  33.1 19.3 %collective-permute-start.7 = (bf16[2,4,64,768]{3,2,1,0:T(8,128)(2,1)}, bf16[2,4,64,768]{3,2,1,0:T(8,128)(2,1)}, u32[]{:S(2)}, u32[]{:S(2)}) collective-permute-start(bf16[2,4,64,768]{3,2,1,0:T(8,128)(2,1)} %shard_map.91.refs_3_.refs_2_), channel_id=1, source_target_pairs={{0,4},{4,0},{8,12},{12,8},{16,20},{20,16},{24,28},{28,24},{1,5},{5... | collective-permute-start | bytes 2359304 | tf_op jit(solution)/shard_map/ppermute | solution.py:33
  36.0 29.7 %collective-permute-start.2 = (bf16[4,64,768]{2,1,0:T(8,128)(2,1)}, bf16[4,64,768]{2,1,0:T(8,128)(2,1)}, u32[]{:S(2)}, u32[]{:S(2)}) collective-permute-start(bf16[4,64,768]{2,1,0:T(8,128)(2,1)} %shard_map.87.refs_1_), channel_id=1, source_target_pairs={{0,1},{1,0},{2,3},{3,2},{4,5},{5,4},{6,7},{7,6},{8,9},{9,8},{10,11... | collective-permute-start | bytes 1179656 | tf_op jit(solution)/shard_map/ppermute | solution.py:37
  43.2 15.9 %collective-permute-start.3 = (bf16[4,64,768]{2,1,0:T(8,128)(2,1)}, bf16[4,64,768]{2,1,0:T(8,128)(2,1)}, u32[]{:S(2)}, u32[]{:S(2)}) collective-permute-start(bf16[4,64,768]{2,1,0:T(8,128)(2,1)} %shard_map.88.refs_2_), channel_id=1, source_target_pairs={{0,2},{1,3},{2,0},{3,1},{4,6},{5,7},{6,4},{7,5},{8,10},{9,11},{10,... | collective-permute-start | bytes 1179656 | tf_op jit(solution)/shard_map/ppermute | solution.py:37
  52.4 13.4 %collective-permute-start.10 = (bf16[4,64,768]{2,1,0:T(8,128)(2,1)}, bf16[4,64,768]{2,1,0:T(8,128)(2,1)}, u32[]{:S(2)}, u32[]{:S(2)}) collective-permute-start(bf16[4,64,768]{2,1,0:T(8,128)(2,1)} %shard_map.93.refs_3_), channel_id=1, source_target_pairs={{4,8},{8,4},{12,16},{16,12},{20,24},{24,20},{5,9},{9,5},{13,17},{1... | collective-permute-start | bytes 1179656 | tf_op jit(solution)/shard_map/ppermute | solution.py:33
  54.9 10.9 %collective-permute-start.9 = (bf16[4,64,768]{2,1,0:T(8,128)(2,1)}, bf16[4,64,768]{2,1,0:T(8,128)(2,1)}, u32[]{:S(2)}, u32[]{:S(2)}) collective-permute-start(bf16[4,64,768]{2,1,0:T(8,128)(2,1)} %shard_map.93.refs_3_), channel_id=1, source_target_pairs={{0,4},{4,0},{8,12},{12,8},{16,20},{20,16},{24,28},{28,24},{1,5},{5... | collective-permute-start | bytes 1179656 | tf_op jit(solution)/shard_map/ppermute | solution.py:33
  67.7 12.3 %collective-permute-start.11 = (bf16[4,64,768]{2,1,0:T(8,128)(2,1)}, bf16[4,64,768]{2,1,0:T(8,128)(2,1)}, u32[]{:S(2)}, u32[]{:S(2)}) collective-permute-start(bf16[4,64,768]{2,1,0:T(8,128)(2,1)} %shard_map.94.refs_2_), channel_id=1, source_target_pairs={{0,3},{1,2},{2,1},{3,0},{4,7},{5,6},{6,5},{7,4},{8,11},{9,10},{10,... | collective-permute-start | bytes 1179656 | tf_op jit(solution)/shard_map/ppermute | solution.py:37
  67.8 22.9 %collective-permute-start.14 = (bf16[2,4,64,768]{3,2,1,0:T(8,128)(2,1)}, bf16[2,4,64,768]{3,2,1,0:T(8,128)(2,1)}, u32[]{:S(2)}, u32[]{:S(2)}) collective-permute-start(bf16[2,4,64,768]{3,2,1,0:T(8,128)(2,1)} %shard_map.96.refs_1_.refs_2_), channel_id=1, source_target_pairs={{4,8},{8,4},{12,16},{16,12},{20,24},{24,20},{5,9},{9,5},{13,17},{1... | collective-permute-start | bytes 2359304 | tf_op jit(solution)/shard_map/ppermute | solution.py:33
  70.9 9.0 %collective-permute-start.12 = (bf16[2,4,64,768]{3,2,1,0:T(8,128)(2,1)}, bf16[2,4,64,768]{3,2,1,0:T(8,128)(2,1)}, u32[]{:S(2)}, u32[]{:S(2)}) collective-permute-start(bf16[2,4,64,768]{3,2,1,0:T(8,128)(2,1)} %shard_map.96.refs_1_.refs_2_), channel_id=1, source_target_pairs={{0,4},{4,0},{8,12},{12,8},{16,20},{20,16},{24,28},{28,24},{1,5},{5... | collective-permute-start | bytes 2359304 | tf_op jit(solution)/shard_map/ppermute | solution.py:33
  80.0 18.7 %collective-permute-start.15 = (bf16[4,64,768]{2,1,0:T(8,128)(2,1)}, bf16[4,64,768]{2,1,0:T(8,128)(2,1)}, u32[]{:S(2)}, u32[]{:S(2)}) collective-permute-start(bf16[4,64,768]{2,1,0:T(8,128)(2,1)} %shard_map.99.refs_3_), channel_id=1, source_target_pairs={{4,8},{8,4},{12,16},{16,12},{20,24},{24,20},{5,9},{9,5},{13,17},{1... | collective-permute-start | bytes 1179656 | tf_op jit(solution)/shard_map/ppermute | solution.py:33
  83.7 15.0 %collective-permute-start.13 = (bf16[4,64,768]{2,1,0:T(8,128)(2,1)}, bf16[4,64,768]{2,1,0:T(8,128)(2,1)}, u32[]{:S(2)}, u32[]{:S(2)}) collective-permute-start(bf16[4,64,768]{2,1,0:T(8,128)(2,1)} %shard_map.99.refs_3_), channel_id=1, source_target_pairs={{0,4},{4,0},{8,12},{12,8},{16,20},{20,16},{24,28},{28,24},{1,5},{5... | collective-permute-start | bytes 1179656 | tf_op jit(solution)/shard_map/ppermute | solution.py:33

commit v23 on v22

--- a/solution.py
+++ b/solution.py
@@ -102,14 +102,19 @@
 
 def join_kernel(pieces, *refs):
     received, (joined, stage, in_sems, out_sems) = refs[:pieces], refs[-4:]
+    places = [(piece, index) for piece in range(pieces) for index in range(4)]
     loads, stores = [], []
-    for piece in range(pieces):
-        load = pltpu.make_async_copy(received[piece], stage.at[piece], in_sems.at[piece])
+    for piece, index in places:
+        load = pltpu.make_async_copy(
+            received[piece].at[index], stage.at[piece, index], in_sems.at[piece * 4 + index]
+        )
         load.start()
         loads.append(load)
-    for piece in range(pieces):
-        loads[piece].wait()
-        store = pltpu.make_async_copy(stage.at[piece], joined.at[piece], out_sems.at[piece])
+    for load, (piece, index) in zip(loads, places):
+        load.wait()
+        store = pltpu.make_async_copy(
+            stage.at[piece, index], joined.at[piece, index], out_sems.at[piece * 4 + index]
+        )
         store.start()
         stores.append(store)
     for store in stores:
@@ -126,8 +131,8 @@
         out_specs=pl.BlockSpec(memory_space=pl.ANY),
         scratch_shapes=[
             pltpu.VMEM(shape, jnp.bfloat16),
-            pltpu.SemaphoreType.DMA((pieces,)),
-            pltpu.SemaphoreType.DMA((pieces,)),
+            pltpu.SemaphoreType.DMA((pieces * 4,)),
+            pltpu.SemaphoreType.DMA((pieces * 4,)),
         ],
         compiler_params=pltpu.CompilerParams(vmem_limit_bytes=VMEM_LIMIT),
         cost_estimate=cost,

time: 108 us -> 108 us (level)
  transfers between devices with their start and end apart: 16 -> 16, of which waited for: 9 -> 8; matrix products, arithmetic and copies ran while one was open for 1% -> 1% of each run, Pallas kernels for 12% -> 12%
where the time goes in v23:
time: 108 us
  waiting for transfers between devices  45.6 us (42%)
  starting transfers between devices  33.1 us (31%)
  Pallas kernels  26.7 us (25%)
    ppermute x10, waiting for transfers between devices, swap_pairs(): return lax.ppermute(block, axis, route)  30.8 us
    ppermute x10, starting transfers between devices, swap_pairs(): return lax.ppermute(block, axis, route)  17.9 us
    pallas_call x2, Pallas kernels, attend(): pl.pallas_call(functools.partial(attend_kernel, parts, part_rows, steps,...  17.8 us
    ppermute x6, starting transfers between devices, swap_flipped(): lax.ppermute(block, axis, [(i, i ^ flip) for i in range(lax.axis_size(axi...  15.1 us
    ppermute x6, waiting for transfers between devices, swap_flipped(): lax.ppermute(block, axis, [(i, i ^ flip) for i in range(lax.axis_size(axi...  14.8 us
    pallas_call x2, Pallas kernels, pack(): pl.pallas_call(functools.partial(pack_kernel, stride, jobs), out_shape=[j...  4.88 us
    pallas_call x2, Pallas kernels, join(): pl.pallas_call(functools.partial(join_kernel, pieces), out_shape=jax.Shap...  4 us
  transfers between devices with their start and end apart: 16, of which 8 were waited for; matrix products, arithmetic and copies ran while one was open for 1% of the time, Pallas kernels for 12%

profile of v23, /device:TPU:3, one launch (start us, length us, event | category | flops | bytes accessed | tf_op | source)
XLA Modules:
  0.0 107.8 jit_solution(4543307002669112487)
XLA Ops:
  0.6 2.5 %shard_map.84 = (bf16[4,64,768]{2,1,0:T(8,128)(2,1)}, bf16[4,64,768]{2,1,0:T(8,128)(2,1)}, bf16[4,64,1536]{2,1,0:T(8,128)(2,1)}) custom-call(bf16[64,6144]{1,0:T(8,128)(2,1)} %refs_0_.3, bf16[64,6144]{1,0:T(8,128)(2,1)} %refs_1_.3, bf16[64,6144]{1,0:T(8,128)(2,1)} %refs_2_.3, bf16[64,6144]{1,0:T(8,128)(2,1)} %refs_3_.3), custom_call_target="tpu_custom_call" | custom-call | flops 1 | bytes 1 | tf_op jit(solution)/shard_map/pallas_call | solution.py:86
  3.1 2.4 %collective-permute-start = (bf16[4,64,768]{2,1,0:T(8,128)(2,1)}, bf16[4,64,768]{2,1,0:T(8,128)(2,1)}, u32[]{:S(2)}, u32[]{:S(2)}) collective-permute-start(bf16[4,64,768]{2,1,0:T(8,128)(2,1)} %get-tuple-element.18), channel_id=1, source_target_pairs={{0,2},{1,3},{2,0},{3,1},{4,6},{5,7},{6,4},{7,5},{8,10},{9,11},{10,... | collective-permute-start | bytes 1179656 | tf_op jit(solution)/shard_map/ppermute | solution.py:37
  5.5 1.3 %collective-permute-start.4 = (bf16[4,64,768]{2,1,0:T(8,128)(2,1)}, bf16[4,64,768]{2,1,0:T(8,128)(2,1)}, u32[]{:S(2)}, u32[]{:S(2)}) collective-permute-start(bf16[4,64,768]{2,1,0:T(8,128)(2,1)} %get-tuple-element.21), channel_id=1, source_target_pairs={{0,1},{1,0},{2,3},{3,2},{4,5},{5,4},{6,7},{7,6},{8,9},{9,8},{10,11... | collective-permute-start | bytes 1179656 | tf_op jit(solution)/shard_map/ppermute | solution.py:37
  6.8 4.2 %collective-permute-start.6 = (bf16[4,64,1536]{2,1,0:T(8,128)(2,1)}, bf16[4,64,1536]{2,1,0:T(8,128)(2,1)}, u32[]{:S(2)}, u32[]{:S(2)}) collective-permute-start(bf16[4,64,1536]{2,1,0:T(8,128)(2,1)} %get-tuple-element.15.refs_3_.refs_1_), channel_id=1, source_target_pairs={{4,8},{8,4},{12,16},{16,12},{20,24},{24,20},{5,9},{9,5},{13,17},{1... | collective-permute-start | bytes 2359304 | tf_op jit(solution)/shard_map/ppermute | solution.py:33
  11.0 0.1 collective-permute-start.5
  11.1 2.4 %shard_map.85 = (bf16[4,64,768]{2,1,0:T(8,128)(2,1)}, bf16[4,64,768]{2,1,0:T(8,128)(2,1)}, bf16[4,64,768]{2,1,0:T(8,128)(2,1)}, bf16[4,64,768]{2,1,0:T(8,128)(2,1)}) custom-call(bf16[64,6144]{1,0:T(8,128)(2,1)} %refs_0_.3, bf16[64,6144]{1,0:T(8,128)(2,1)} %refs_1_.3, bf16[64,6144]{1,0:T(8,128)(2,1)} %refs_2_.3, bf16[64,6144]{1,0:T(8,128)(2,1)} %refs_3_.3), custom_call_target="tpu_custom_call" | custom-call | flops 1 | bytes 1 | tf_op jit(solution)/shard_map/pallas_call | solution.py:86
  13.5 0.8 slice.3
  14.3 0.1 dynamic-slice_bitcast_fusion.2
  14.4 0.6 pad_add_fusion.refs_0_
  15.1 7.8 %collective-permute-done.refs_1_ = bf16[4,64,768]{2,1,0:T(8,128)(2,1)} collective-permute-done((bf16[4,64,768]{2,1,0:T(8,128)(2,1)}, bf16[4,64,768]{2,1,0:T(8,128)(2,1)}, u32[]{:S(2)}, u32[]{:S(2)}) %collective-permute-start) | collective-permute-done | bytes 393248 | tf_op jit(solution)/shard_map/ppermute | solution.py:37
  22.9 4.2 %collective-permute-start.1 = (bf16[4,64,768]{2,1,0:T(8,128)(2,1)}, bf16[4,64,768]{2,1,0:T(8,128)(2,1)}, u32[]{:S(2)}, u32[]{:S(2)}) collective-permute-start(bf16[4,64,768]{2,1,0:T(8,128)(2,1)} %shard_map.86.refs_2_), channel_id=1, source_target_pairs={{0,3},{1,2},{2,1},{3,0},{4,7},{5,6},{6,5},{7,4},{8,11},{9,10},{10,... | collective-permute-start | bytes 1179656 | tf_op jit(solution)/shard_map/ppermute | solution.py:37
  27.1 2.0 %shard_map.90.refs_0_ = bf16[2,4,64,768]{3,2,1,0:T(8,128)(2,1)} custom-call(bf16[4,64,768]{2,1,0:T(8,128)(2,1)} %collective-permute-done.4.refs_0_, bf16[4,64,768]{2,1,0:T(8,128)(2,1)} %collective-permute-done.refs_1_, bf16[4,64,768]{2,1,0:T(8,128)(2,1)} %shard_map.86.refs_2_, bf16[4,64,1536]{2,1,0:T(8,128)(2,1)} %get-tuple-element.15.refs_3_.refs_1_), custom_call_target="tpu_custom_call" | custom-call | flops 30670848000 | bytes 1 | tf_op jit(solution)/shard_map/pallas_call | solution.py:127
  29.1 0.1 collective-permute-done.6.refs_2_.refs_7_
  29.2 3.9 %collective-permute-start.8 = (bf16[2,4,64,768]{3,2,1,0:T(8,128)(2,1)}, bf16[2,4,64,768]{3,2,1,0:T(8,128)(2,1)}, u32[]{:S(2)}, u32[]{:S(2)}) collective-permute-start(bf16[2,4,64,768]{3,2,1,0:T(8,128)(2,1)} %shard_map.91.refs_3_.refs_2_), channel_id=1, source_target_pairs={{4,8},{8,4},{12,16},{16,12},{20,24},{24,20},{5,9},{9,5},{13,17},{1... | collective-permute-start | bytes 2359304 | tf_op jit(solution)/shard_map/ppermute | solution.py:33
  33.1 0.1 collective-permute-start.7
  33.2 2.9 %collective-permute-done.1.refs_1_.refs_0_ = bf16[4,64,768]{2,1,0:T(8,128)(2,1)} collective-permute-done((bf16[4,64,768]{2,1,0:T(8,128)(2,1)}, bf16[4,64,768]{2,1,0:T(8,128)(2,1)}, u32[]{:S(2)}, u32[]{:S(2)}) %collective-permute-start.1) | collective-permute-done | bytes 393248 | tf_op jit(solution)/shard_map/ppermute | solution.py:37
  36.0 7.2 %collective-permute-start.2 = (bf16[4,64,768]{2,1,0:T(8,128)(2,1)}, bf16[4,64,768]{2,1,0:T(8,128)(2,1)}, u32[]{:S(2)}, u32[]{:S(2)}) collective-permute-start(bf16[4,64,768]{2,1,0:T(8,128)(2,1)} %shard_map.87.refs_1_), channel_id=1, source_target_pairs={{0,1},{1,0},{2,3},{3,2},{4,5},{5,4},{6,7},{7,6},{8,9},{9,8},{10,11... | collective-permute-start | bytes 1179656 | tf_op jit(solution)/shard_map/ppermute | solution.py:37
  43.2 9.1 %collective-permute-done.8.refs_2_.refs_8_ = bf16[2,4,64,768]{3,2,1,0:T(8,128)(2,1)} collective-permute-done((bf16[2,4,64,768]{3,2,1,0:T(8,128)(2,1)}, bf16[2,4,64,768]{3,2,1,0:T(8,128)(2,1)}, u32[]{:S(2)}, u32[]{:S(2)}) %collective-permute-start.8) | collective-permute-done | bytes 786464 | tf_op jit(solution)/shard_map/ppermute | solution.py:33
  52.4 2.6 %collective-permute-start.10 = (bf16[4,64,768]{2,1,0:T(8,128)(2,1)}, bf16[4,64,768]{2,1,0:T(8,128)(2,1)}, u32[]{:S(2)}, u32[]{:S(2)}) collective-permute-start(bf16[4,64,768]{2,1,0:T(8,128)(2,1)} %shard_map.93.refs_3_), channel_id=1, source_target_pairs={{4,8},{8,4},{12,16},{16,12},{20,24},{24,20},{5,9},{9,5},{13,17},{1... | collective-permute-start | bytes 1179656 | tf_op jit(solution)/shard_map/ppermute | solution.py:33
  55.0 0.1 collective-permute-start.9
  55.0 4.0 %collective-permute-done.3.refs_1_ = bf16[4,64,768]{2,1,0:T(8,128)(2,1)} collective-permute-done((bf16[4,64,768]{2,1,0:T(8,128)(2,1)}, bf16[4,64,768]{2,1,0:T(8,128)(2,1)}, u32[]{:S(2)}, u32[]{:S(2)}) %collective-permute-start.3) | collective-permute-done | bytes 393248 | tf_op jit(solution)/shard_map/ppermute | solution.py:37
  59.1 6.7 %collective-permute-done.10.refs_2_.refs_9_ = bf16[4,64,768]{2,1,0:T(8,128)(2,1)} collective-permute-done((bf16[4,64,768]{2,1,0:T(8,128)(2,1)}, bf16[4,64,768]{2,1,0:T(8,128)(2,1)}, u32[]{:S(2)}, u32[]{:S(2)}) %collective-permute-start.10) | collective-permute-done | bytes 393248 | tf_op jit(solution)/shard_map/ppermute | solution.py:33
  65.8 2.0 %shard_map.95.refs_0_ = bf16[2,4,64,768]{3,2,1,0:T(8,128)(2,1)} custom-call(bf16[4,64,768]{2,1,0:T(8,128)(2,1)} %collective-permute-done.2.refs_0_, bf16[4,64,768]{2,1,0:T(8,128)(2,1)} %collective-permute-done.3.refs_1_, bf16[4,64,768]{2,1,0:T(8,128)(2,1)} %shard_map.94.refs_2_, bf16[4,64,768]{2,1,0:T(8,128)(2,1)} %shard_map.93.refs_3_), custom_call_target="tpu_custom_call" | custom-call | flops 10223616000 | bytes 1 | tf_op jit(solution)/shard_map/pallas_call | solution.py:127
  67.8 0.1 collective-permute-start.11
  67.9 3.1 %collective-permute-start.14 = (bf16[2,4,64,768]{3,2,1,0:T(8,128)(2,1)}, bf16[2,4,64,768]{3,2,1,0:T(8,128)(2,1)}, u32[]{:S(2)}, u32[]{:S(2)}) collective-permute-start(bf16[2,4,64,768]{3,2,1,0:T(8,128)(2,1)} %shard_map.96.refs_1_.refs_2_), channel_id=1, source_target_pairs={{4,8},{8,4},{12,16},{16,12},{20,24},{24,20},{5,9},{9,5},{13,17},{1... | collective-permute-start | bytes 2359304 | tf_op jit(solution)/shard_map/ppermute | solution.py:33
  71.0 0.1 collective-permute-start.12
  71.1 8.9 %shard_map.98 = (bf16[256,1536]{1,0:T(8,128)(2,1)}, bf16[256,1536]{1,0:T(8,128)(2,1)}, bf16[256,1536]{1,0:T(8,128)(2,1)}, bf16[256,1536]{1,0:T(8,128)(2,1)}) custom-call(s32[3,4]{1,0:T(4,128)} %pad_add_fusion.refs_0_, bf16[4,64,1536]{2,1,0:T(8,128)(2,1)} %get-tuple-element.15.refs_3_.refs_1_, bf16[2,4,64,768]{3,2,1,0:T(8,128)(2,1)} %shard_map.91.refs_3_.refs_2_, ...), custom_call_target="tpu_custom_call" | custom-call | flops 8999999488 | bytes 1 | tf_op jit(solution)/shard_map/pallas_call | solution.py:330
  80.1 3.7 %collective-permute-start.15 = (bf16[4,64,768]{2,1,0:T(8,128)(2,1)}, bf16[4,64,768]{2,1,0:T(8,128)(2,1)}, u32[]{:S(2)}, u32[]{:S(2)}) collective-permute-start(bf16[4,64,768]{2,1,0:T(8,128)(2,1)} %shard_map.99.refs_3_), channel_id=1, source_target_pairs={{4,8},{8,4},{12,16},{16,12},{20,24},{24,20},{5,9},{9,5},{13,17},{1... | collective-permute-start | bytes 1179656 | tf_op jit(solution)/shard_map/ppermute | solution.py:33
  83.8 0.1 collective-permute-start.13
  83.8 6.9 %collective-permute-done.14.refs_8_ = bf16[2,4,64,768]{3,2,1,0:T(8,128)(2,1)} collective-permute-done((bf16[2,4,64,768]{3,2,1,0:T(8,128)(2,1)}, bf16[2,4,64,768]{3,2,1,0:T(8,128)(2,1)}, u32[]{:S(2)}, u32[]{:S(2)}) %collective-permute-start.14) | collective-permute-done | bytes 786464 | tf_op jit(solution)/shard_map/ppermute | solution.py:33
  90.7 8.0 %collective-permute-done.15.refs_9_ = bf16[4,64,768]{2,1,0:T(8,128)(2,1)} collective-permute-done((bf16[4,64,768]{2,1,0:T(8,128)(2,1)}, bf16[4,64,768]{2,1,0:T(8,128)(2,1)}, u32[]{:S(2)}, u32[]{:S(2)}) %collective-permute-start.15) | collective-permute-done | bytes 393248 | tf_op jit(solution)/shard_map/ppermute | solution.py:33
  98.7 8.8 %shard_map.100 = (bf16[256,1536]{1,0:T(8,128)(2,1)}, bf16[256,1536]{1,0:T(8,128)(2,1)}, bf16[256,1536]{1,0:T(8,128)(2,1)}, bf16[256,1536]{1,0:T(8,128)(2,1)}) custom-call(s32[3,4]{1,0:T(4,128)} %pad_add_fusion.refs_0_, ...), custom_call_target="tpu_custom_call", output_to_operand_aliasing={{0}: (10, {}), {1}: (11, {}), {2}: (12, {}), {3}: (13, {})} | custom-call | flops 8999999488 | bytes 1 | tf_op jit(solution)/shard_map/pallas_call | solution.py:330
  (20 shorter events, 0.1 us)
Async XLA Ops:
  3.1 19.8 %collective-permute-start = (bf16[4,64,768]{2,1,0:T(8,128)(2,1)}, bf16[4,64,768]{2,1,0:T(8,128)(2,1)}, u32[]{:S(2)}, u32[]{:S(2)}) collective-permute-start(bf16[4,64,768]{2,1,0:T(8,128)(2,1)} %get-tuple-element.18), channel_id=1, source_target_pairs={{0,2},{1,3},{2,0},{3,1},{4,6},{5,7},{6,4},{7,5},{8,10},{9,11},{10,... | collective-permute-start | bytes 1179656 | tf_op jit(solution)/shard_map/ppermute | solution.py:37
  5.5 21.6 %collective-permute-start.4 = (bf16[4,64,768]{2,1,0:T(8,128)(2,1)}, bf16[4,64,768]{2,1,0:T(8,128)(2,1)}, u32[]{:S(2)}, u32[]{:S(2)}) collective-permute-start(bf16[4,64,768]{2,1,0:T(8,128)(2,1)} %get-tuple-element.21), channel_id=1, source_target_pairs={{0,1},{1,0},{2,3},{3,2},{4,5},{5,4},{6,7},{7,6},{8,9},{9,8},{10,11... | collective-permute-start | bytes 1179656 | tf_op jit(solution)/shard_map/ppermute | solution.py:37
  6.8 22.4 %collective-permute-start.6 = (bf16[4,64,1536]{2,1,0:T(8,128)(2,1)}, bf16[4,64,1536]{2,1,0:T(8,128)(2,1)}, u32[]{:S(2)}, u32[]{:S(2)}) collective-permute-start(bf16[4,64,1536]{2,1,0:T(8,128)(2,1)} %get-tuple-element.15.refs_3_.refs_1_), channel_id=1, source_target_pairs={{4,8},{8,4},{12,16},{16,12},{20,24},{24,20},{5,9},{9,5},{13,17},{1... | collective-permute-start | bytes 2359304 | tf_op jit(solution)/shard_map/ppermute | solution.py:33
  11.0 18.2 %collective-permute-start.5 = (bf16[4,64,1536]{2,1,0:T(8,128)(2,1)}, bf16[4,64,1536]{2,1,0:T(8,128)(2,1)}, u32[]{:S(2)}, u32[]{:S(2)}) collective-permute-start(bf16[4,64,1536]{2,1,0:T(8,128)(2,1)} %get-tuple-element.15.refs_3_.refs_1_), channel_id=1, source_target_pairs={{0,4},{4,0},{8,12},{12,8},{16,20},{20,16},{24,28},{28,24},{1,5},{5... | collective-permute-start | bytes 2359304 | tf_op jit(solution)/shard_map/ppermute | solution.py:33
  22.9 13.2 %collective-permute-start.1 = (bf16[4,64,768]{2,1,0:T(8,128)(2,1)}, bf16[4,64,768]{2,1,0:T(8,128)(2,1)}, u32[]{:S(2)}, u32[]{:S(2)}) collective-permute-start(bf16[4,64,768]{2,1,0:T(8,128)(2,1)} %shard_map.86.refs_2_), channel_id=1, source_target_pairs={{0,3},{1,2},{2,1},{3,0},{4,7},{5,6},{6,5},{7,4},{8,11},{9,10},{10,... | collective-permute-start | bytes 1179656 | tf_op jit(solution)/shard_map/ppermute | solution.py:37
  29.2 23.1 %collective-permute-start.8 = (bf16[2,4,64,768]{3,2,1,0:T(8,128)(2,1)}, bf16[2,4,64,768]{3,2,1,0:T(8,128)(2,1)}, u32[]{:S(2)}, u32[]{:S(2)}) collective-permute-start(bf16[2,4,64,768]{3,2,1,0:T(8,128)(2,1)} %shard_map.91.refs_3_.refs_2_), channel_id=1, source_target_pairs={{4,8},{8,4},{12,16},{16,12},{20,24},{24,20},{5,9},{9,5},{13,17},{1... | collective-permute-start | bytes 2359304 | tf_op jit(solution)/shard_map/ppermute | solution.py:33
  33.1 19.3 %collective-permute-start.7 = (bf16[2,4,64,768]{3,2,1,0:T(8,128)(2,1)}, bf16[2,4,64,768]{3,2,1,0:T(8,128)(2,1)}, u32[]{:S(2)}, u32[]{:S(2)}) collective-permute-start(bf16[2,4,64,768]{3,2,1,0:T(8,128)(2,1)} %shard_map.91.refs_3_.refs_2_), channel_id=1, source_target_pairs={{0,4},{4,0},{8,12},{12,8},{16,20},{20,16},{24,28},{28,24},{1,5},{5... | collective-permute-start | bytes 2359304 | tf_op jit(solution)/shard_map/ppermute | solution.py:33
  36.0 29.7 %collective-permute-start.2 = (bf16[4,64,768]{2,1,0:T(8,128)(2,1)}, bf16[4,64,768]{2,1,0:T(8,128)(2,1)}, u32[]{:S(2)}, u32[]{:S(2)}) collective-permute-start(bf16[4,64,768]{2,1,0:T(8,128)(2,1)} %shard_map.87.refs_1_), channel_id=1, source_target_pairs={{0,1},{1,0},{2,3},{3,2},{4,5},{5,4},{6,7},{7,6},{8,9},{9,8},{10,11... | collective-permute-start | bytes 1179656 | tf_op jit(solution)/shard_map/ppermute | solution.py:37
  43.2 15.9 %collective-permute-start.3 = (bf16[4,64,768]{2,1,0:T(8,128)(2,1)}, bf16[4,64,768]{2,1,0:T(8,128)(2,1)}, u32[]{:S(2)}, u32[]{:S(2)}) collective-permute-start(bf16[4,64,768]{2,1,0:T(8,128)(2,1)} %shard_map.88.refs_2_), channel_id=1, source_target_pairs={{0,2},{1,3},{2,0},{3,1},{4,6},{5,7},{6,4},{7,5},{8,10},{9,11},{10,... | collective-permute-start | bytes 1179656 | tf_op jit(solution)/shard_map/ppermute | solution.py:37
  52.4 13.4 %collective-permute-start.10 = (bf16[4,64,768]{2,1,0:T(8,128)(2,1)}, bf16[4,64,768]{2,1,0:T(8,128)(2,1)}, u32[]{:S(2)}, u32[]{:S(2)}) collective-permute-start(bf16[4,64,768]{2,1,0:T(8,128)(2,1)} %shard_map.93.refs_3_), channel_id=1, source_target_pairs={{4,8},{8,4},{12,16},{16,12},{20,24},{24,20},{5,9},{9,5},{13,17},{1... | collective-permute-start | bytes 1179656 | tf_op jit(solution)/shard_map/ppermute | solution.py:33
  55.0 10.8 %collective-permute-start.9 = (bf16[4,64,768]{2,1,0:T(8,128)(2,1)}, bf16[4,64,768]{2,1,0:T(8,128)(2,1)}, u32[]{:S(2)}, u32[]{:S(2)}) collective-permute-start(bf16[4,64,768]{2,1,0:T(8,128)(2,1)} %shard_map.93.refs_3_), channel_id=1, source_target_pairs={{0,4},{4,0},{8,12},{12,8},{16,20},{20,16},{24,28},{28,24},{1,5},{5... | collective-permute-start | bytes 1179656 | tf_op jit(solution)/shard_map/ppermute | solution.py:33
  67.8 12.3 %collective-permute-start.11 = (bf16[4,64,768]{2,1,0:T(8,128)(2,1)}, bf16[4,64,768]{2,1,0:T(8,128)(2,1)}, u32[]{:S(2)}, u32[]{:S(2)}) collective-permute-start(bf16[4,64,768]{2,1,0:T(8,128)(2,1)} %shard_map.94.refs_2_), channel_id=1, source_target_pairs={{0,3},{1,2},{2,1},{3,0},{4,7},{5,6},{6,5},{7,4},{8,11},{9,10},{10,... | collective-permute-start | bytes 1179656 | tf_op jit(solution)/shard_map/ppermute | solution.py:37
  67.9 22.9 %collective-permute-start.14 = (bf16[2,4,64,768]{3,2,1,0:T(8,128)(2,1)}, bf16[2,4,64,768]{3,2,1,0:T(8,128)(2,1)}, u32[]{:S(2)}, u32[]{:S(2)}) collective-permute-start(bf16[2,4,64,768]{3,2,1,0:T(8,128)(2,1)} %shard_map.96.refs_1_.refs_2_), channel_id=1, source_target_pairs={{4,8},{8,4},{12,16},{16,12},{20,24},{24,20},{5,9},{9,5},{13,17},{1... | collective-permute-start | bytes 2359304 | tf_op jit(solution)/shard_map/ppermute | solution.py:33
  71.0 9.0 %collective-permute-start.12 = (bf16[2,4,64,768]{3,2,1,0:T(8,128)(2,1)}, bf16[2,4,64,768]{3,2,1,0:T(8,128)(2,1)}, u32[]{:S(2)}, u32[]{:S(2)}) collective-permute-start(bf16[2,4,64,768]{3,2,1,0:T(8,128)(2,1)} %shard_map.96.refs_1_.refs_2_), channel_id=1, source_target_pairs={{0,4},{4,0},{8,12},{12,8},{16,20},{20,16},{24,28},{28,24},{1,5},{5... | collective-permute-start | bytes 2359304 | tf_op jit(solution)/shard_map/ppermute | solution.py:33
  80.1 18.7 %collective-permute-start.15 = (bf16[4,64,768]{2,1,0:T(8,128)(2,1)}, bf16[4,64,768]{2,1,0:T(8,128)(2,1)}, u32[]{:S(2)}, u32[]{:S(2)}) collective-permute-start(bf16[4,64,768]{2,1,0:T(8,128)(2,1)} %shard_map.99.refs_3_), channel_id=1, source_target_pairs={{4,8},{8,4},{12,16},{16,12},{20,24},{24,20},{5,9},{9,5},{13,17},{1... | collective-permute-start | bytes 1179656 | tf_op jit(solution)/shard_map/ppermute | solution.py:33
  83.8 15.0 %collective-permute-start.13 = (bf16[4,64,768]{2,1,0:T(8,128)(2,1)}, bf16[4,64,768]{2,1,0:T(8,128)(2,1)}, u32[]{:S(2)}, u32[]{:S(2)}) collective-permute-start(bf16[4,64,768]{2,1,0:T(8,128)(2,1)} %shard_map.99.refs_3_), channel_id=1, source_target_pairs={{0,4},{4,0},{8,12},{12,8},{16,20},{20,16},{24,28},{28,24},{1,5},{5... | collective-permute-start | bytes 1179656 | tf_op jit(solution)/shard_map/ppermute | solution.py:33

commit v24 on v22

--- a/solution.py
+++ b/solution.py
@@ -382,7 +382,10 @@
     def cross(step, after, cost=SMALL_COST, late=()):
         held = [hold(packed[job], after, cost) if after else packed[job] for job in step]
         held = [hold(piece, late) if late else piece for piece in held]
-        return held, [swap_flipped(piece, "tensor", job[0]) for job, piece in zip(step, held)]
+        order = list(zip(step, held))
+        order = order[::-1] if after else order
+        crossed = [swap_flipped(piece, "tensor", job[0]) for job, piece in order]
+        return held, crossed[::-1] if after else crossed
 
     def spread(piece):
         return piece, swap_pairs(piece, "dp", 0), swap_pairs(piece, "dp", 1)

time: 108 us -> 108 us (level)
  transfers between devices with their start and end apart: 16 -> 16, of which waited for: 9 -> 8; matrix products, arithmetic and copies ran while one was open for 1% -> 1% of each run, Pallas kernels for 12% -> 12%
where the time goes in v24:
time: 108 us
  waiting for transfers between devices  45.7 us (42%)
  starting transfers between devices  32.9 us (30%)
  Pallas kernels  26.5 us (25%)
    ppermute x10, waiting for transfers between devices, swap_pairs(): return lax.ppermute(block, axis, route)  30.9 us
    ppermute x10, starting transfers between devices, swap_pairs(): return lax.ppermute(block, axis, route)  17.8 us
    pallas_call x2, Pallas kernels, attend(): pl.pallas_call(functools.partial(attend_kernel, parts, part_rows, steps,...  17.7 us
    ppermute x6, starting transfers between devices, swap_flipped(): lax.ppermute(block, axis, [(i, i ^ flip) for i in range(lax.axis_size(axi...  15.1 us
    ppermute x6, waiting for transfers between devices, swap_flipped(): lax.ppermute(block, axis, [(i, i ^ flip) for i in range(lax.axis_size(axi...  14.8 us
    pallas_call x2, Pallas kernels, pack(): pl.pallas_call(functools.partial(pack_kernel, stride, jobs), out_shape=[j...  4.88 us
    pallas_call x2, Pallas kernels, join(): pl.pallas_call(functools.partial(join_kernel, pieces), out_shape=jax.Shap...  3.88 us
  transfers between devices with their start and end apart: 16, of which 8 were waited for; matrix products, arithmetic and copies ran while one was open for 1% of the time, Pallas kernels for 12%

profile of v24, /device:TPU:3, one launch (start us, length us, event | category | flops | bytes accessed | tf_op | source)
XLA Modules:
  0.0 107.7 jit_solution(16652555027342603643)
XLA Ops:
  0.6 2.5 %shard_map.84 = (bf16[4,64,768]{2,1,0:T(8,128)(2,1)}, bf16[4,64,768]{2,1,0:T(8,128)(2,1)}, bf16[4,64,1536]{2,1,0:T(8,128)(2,1)}) custom-call(bf16[64,6144]{1,0:T(8,128)(2,1)} %refs_0_.3, bf16[64,6144]{1,0:T(8,128)(2,1)} %refs_1_.3, bf16[64,6144]{1,0:T(8,128)(2,1)} %refs_2_.3, bf16[64,6144]{1,0:T(8,128)(2,1)} %refs_3_.3), custom_call_target="tpu_custom_call" | custom-call | flops 1 | bytes 1 | tf_op jit(solution)/shard_map/pallas_call | solution.py:86
  3.1 2.4 %collective-permute-start = (bf16[4,64,768]{2,1,0:T(8,128)(2,1)}, bf16[4,64,768]{2,1,0:T(8,128)(2,1)}, u32[]{:S(2)}, u32[]{:S(2)}) collective-permute-start(bf16[4,64,768]{2,1,0:T(8,128)(2,1)} %get-tuple-element.18), channel_id=1, source_target_pairs={{0,2},{1,3},{2,0},{3,1},{4,6},{5,7},{6,4},{7,5},{8,10},{9,11},{10,... | collective-permute-start | bytes 1179656 | tf_op jit(solution)/shard_map/ppermute | solution.py:37
  5.5 1.3 %collective-permute-start.4 = (bf16[4,64,768]{2,1,0:T(8,128)(2,1)}, bf16[4,64,768]{2,1,0:T(8,128)(2,1)}, u32[]{:S(2)}, u32[]{:S(2)}) collective-permute-start(bf16[4,64,768]{2,1,0:T(8,128)(2,1)} %get-tuple-element.21), channel_id=1, source_target_pairs={{0,1},{1,0},{2,3},{3,2},{4,5},{5,4},{6,7},{7,6},{8,9},{9,8},{10,11... | collective-permute-start | bytes 1179656 | tf_op jit(solution)/shard_map/ppermute | solution.py:37
  6.8 4.2 %collective-permute-start.6 = (bf16[4,64,1536]{2,1,0:T(8,128)(2,1)}, bf16[4,64,1536]{2,1,0:T(8,128)(2,1)}, u32[]{:S(2)}, u32[]{:S(2)}) collective-permute-start(bf16[4,64,1536]{2,1,0:T(8,128)(2,1)} %get-tuple-element.15.refs_3_.refs_1_), channel_id=1, source_target_pairs={{4,8},{8,4},{12,16},{16,12},{20,24},{24,20},{5,9},{9,5},{13,17},{1... | collective-permute-start | bytes 2359304 | tf_op jit(solution)/shard_map/ppermute | solution.py:33
  11.0 0.1 collective-permute-start.5
  11.1 2.4 %shard_map.85 = (bf16[4,64,768]{2,1,0:T(8,128)(2,1)}, bf16[4,64,768]{2,1,0:T(8,128)(2,1)}, bf16[4,64,768]{2,1,0:T(8,128)(2,1)}, bf16[4,64,768]{2,1,0:T(8,128)(2,1)}) custom-call(bf16[64,6144]{1,0:T(8,128)(2,1)} %refs_0_.3, bf16[64,6144]{1,0:T(8,128)(2,1)} %refs_1_.3, bf16[64,6144]{1,0:T(8,128)(2,1)} %refs_2_.3, bf16[64,6144]{1,0:T(8,128)(2,1)} %refs_3_.3), custom_call_target="tpu_custom_call" | custom-call | flops 1 | bytes 1 | tf_op jit(solution)/shard_map/pallas_call | solution.py:86
  13.5 0.8 slice.3
  14.3 0.1 dynamic-slice_bitcast_fusion.2
  14.4 0.6 pad_add_fusion.refs_0_
  15.1 7.8 %collective-permute-done.refs_1_ = bf16[4,64,768]{2,1,0:T(8,128)(2,1)} collective-permute-done((bf16[4,64,768]{2,1,0:T(8,128)(2,1)}, bf16[4,64,768]{2,1,0:T(8,128)(2,1)}, u32[]{:S(2)}, u32[]{:S(2)}) %collective-permute-start) | collective-permute-done | bytes 393248 | tf_op jit(solution)/shard_map/ppermute | solution.py:37
  22.9 4.2 %collective-permute-start.1 = (bf16[4,64,768]{2,1,0:T(8,128)(2,1)}, bf16[4,64,768]{2,1,0:T(8,128)(2,1)}, u32[]{:S(2)}, u32[]{:S(2)}) collective-permute-start(bf16[4,64,768]{2,1,0:T(8,128)(2,1)} %shard_map.86.refs_2_), channel_id=1, source_target_pairs={{0,3},{1,2},{2,1},{3,0},{4,7},{5,6},{6,5},{7,4},{8,11},{9,10},{10,... | collective-permute-start | bytes 1179656 | tf_op jit(solution)/shard_map/ppermute | solution.py:37
  27.1 2.0 %shard_map.90.refs_0_ = bf16[2,4,64,768]{3,2,1,0:T(8,128)(2,1)} custom-call(bf16[4,64,768]{2,1,0:T(8,128)(2,1)} %collective-permute-done.4.refs_0_, bf16[4,64,768]{2,1,0:T(8,128)(2,1)} %collective-permute-done.refs_1_, bf16[4,64,768]{2,1,0:T(8,128)(2,1)} %shard_map.86.refs_2_, bf16[4,64,1536]{2,1,0:T(8,128)(2,1)} %get-tuple-element.15.refs_3_.refs_1_), custom_call_target="tpu_custom_call" | custom-call | flops 30670848000 | bytes 1 | tf_op jit(solution)/shard_map/pallas_call | solution.py:122
  29.0 0.1 collective-permute-done.6.refs_2_.refs_7_
  29.2 3.9 %collective-permute-start.8 = (bf16[2,4,64,768]{3,2,1,0:T(8,128)(2,1)}, bf16[2,4,64,768]{3,2,1,0:T(8,128)(2,1)}, u32[]{:S(2)}, u32[]{:S(2)}) collective-permute-start(bf16[2,4,64,768]{3,2,1,0:T(8,128)(2,1)} %shard_map.91.refs_3_.refs_2_), channel_id=1, source_target_pairs={{4,8},{8,4},{12,16},{16,12},{20,24},{24,20},{5,9},{9,5},{13,17},{1... | collective-permute-start | bytes 2359304 | tf_op jit(solution)/shard_map/ppermute | solution.py:33
  33.1 0.1 collective-permute-start.7
  33.2 2.9 %collective-permute-done.1.refs_1_.refs_0_ = bf16[4,64,768]{2,1,0:T(8,128)(2,1)} collective-permute-done((bf16[4,64,768]{2,1,0:T(8,128)(2,1)}, bf16[4,64,768]{2,1,0:T(8,128)(2,1)}, u32[]{:S(2)}, u32[]{:S(2)}) %collective-permute-start.1) | collective-permute-done | bytes 393248 | tf_op jit(solution)/shard_map/ppermute | solution.py:37
  36.0 7.2 %collective-permute-start.2 = (bf16[4,64,768]{2,1,0:T(8,128)(2,1)}, bf16[4,64,768]{2,1,0:T(8,128)(2,1)}, u32[]{:S(2)}, u32[]{:S(2)}) collective-permute-start(bf16[4,64,768]{2,1,0:T(8,128)(2,1)} %shard_map.87.refs_1_), channel_id=1, source_target_pairs={{0,1},{1,0},{2,3},{3,2},{4,5},{5,4},{6,7},{7,6},{8,9},{9,8},{10,11... | collective-permute-start | bytes 1179656 | tf_op jit(solution)/shard_map/ppermute | solution.py:37
  43.2 9.2 %collective-permute-done.8.refs_2_.refs_8_ = bf16[2,4,64,768]{3,2,1,0:T(8,128)(2,1)} collective-permute-done((bf16[2,4,64,768]{3,2,1,0:T(8,128)(2,1)}, bf16[2,4,64,768]{3,2,1,0:T(8,128)(2,1)}, u32[]{:S(2)}, u32[]{:S(2)}) %collective-permute-start.8) | collective-permute-done | bytes 786464 | tf_op jit(solution)/shard_map/ppermute | solution.py:33
  52.4 2.5 %collective-permute-start.10 = (bf16[4,64,768]{2,1,0:T(8,128)(2,1)}, bf16[4,64,768]{2,1,0:T(8,128)(2,1)}, u32[]{:S(2)}, u32[]{:S(2)}) collective-permute-start(bf16[4,64,768]{2,1,0:T(8,128)(2,1)} %shard_map.93.refs_3_), channel_id=1, source_target_pairs={{4,8},{8,4},{12,16},{16,12},{20,24},{24,20},{5,9},{9,5},{13,17},{1... | collective-permute-start | bytes 1179656 | tf_op jit(solution)/shard_map/ppermute | solution.py:33
  54.9 0.1 collective-permute-start.9
  55.0 4.1 %collective-permute-done.3.refs_1_ = bf16[4,64,768]{2,1,0:T(8,128)(2,1)} collective-permute-done((bf16[4,64,768]{2,1,0:T(8,128)(2,1)}, bf16[4,64,768]{2,1,0:T(8,128)(2,1)}, u32[]{:S(2)}, u32[]{:S(2)}) %collective-permute-start.3) | collective-permute-done | bytes 393248 | tf_op jit(solution)/shard_map/ppermute | solution.py:37
  59.1 6.7 %collective-permute-done.10.refs_2_.refs_9_ = bf16[4,64,768]{2,1,0:T(8,128)(2,1)} collective-permute-done((bf16[4,64,768]{2,1,0:T(8,128)(2,1)}, bf16[4,64,768]{2,1,0:T(8,128)(2,1)}, u32[]{:S(2)}, u32[]{:S(2)}) %collective-permute-start.10) | collective-permute-done | bytes 393248 | tf_op jit(solution)/shard_map/ppermute | solution.py:33
  65.8 1.9 %shard_map.95.refs_0_ = bf16[2,4,64,768]{3,2,1,0:T(8,128)(2,1)} custom-call(bf16[4,64,768]{2,1,0:T(8,128)(2,1)} %collective-permute-done.2.refs_0_, bf16[4,64,768]{2,1,0:T(8,128)(2,1)} %collective-permute-done.3.refs_1_, bf16[4,64,768]{2,1,0:T(8,128)(2,1)} %shard_map.94.refs_2_, bf16[4,64,768]{2,1,0:T(8,128)(2,1)} %shard_map.93.refs_3_), custom_call_target="tpu_custom_call" | custom-call | flops 10223616000 | bytes 1 | tf_op jit(solution)/shard_map/pallas_call | solution.py:122
  67.7 0.1 collective-permute-start.11
  67.8 3.1 %collective-permute-start.14 = (bf16[2,4,64,768]{3,2,1,0:T(8,128)(2,1)}, bf16[2,4,64,768]{3,2,1,0:T(8,128)(2,1)}, u32[]{:S(2)}, u32[]{:S(2)}) collective-permute-start(bf16[2,4,64,768]{3,2,1,0:T(8,128)(2,1)} %shard_map.96.refs_1_.refs_2_), channel_id=1, source_target_pairs={{4,8},{8,4},{12,16},{16,12},{20,24},{24,20},{5,9},{9,5},{13,17},{1... | collective-permute-start | bytes 2359304 | tf_op jit(solution)/shard_map/ppermute | solution.py:33
  70.9 0.1 collective-permute-start.12
  71.0 8.9 %shard_map.98 = (bf16[256,1536]{1,0:T(8,128)(2,1)}, bf16[256,1536]{1,0:T(8,128)(2,1)}, bf16[256,1536]{1,0:T(8,128)(2,1)}, bf16[256,1536]{1,0:T(8,128)(2,1)}) custom-call(s32[3,4]{1,0:T(4,128)} %pad_add_fusion.refs_0_, bf16[4,64,1536]{2,1,0:T(8,128)(2,1)} %get-tuple-element.15.refs_3_.refs_1_, bf16[2,4,64,768]{3,2,1,0:T(8,128)(2,1)} %shard_map.91.refs_3_.refs_2_, ...), custom_call_target="tpu_custom_call" | custom-call | flops 8999999488 | bytes 1 | tf_op jit(solution)/shard_map/pallas_call | solution.py:325
  80.0 3.7 %collective-permute-start.15 = (bf16[4,64,768]{2,1,0:T(8,128)(2,1)}, bf16[4,64,768]{2,1,0:T(8,128)(2,1)}, u32[]{:S(2)}, u32[]{:S(2)}) collective-permute-start(bf16[4,64,768]{2,1,0:T(8,128)(2,1)} %shard_map.99.refs_3_), channel_id=1, source_target_pairs={{4,8},{8,4},{12,16},{16,12},{20,24},{24,20},{5,9},{9,5},{13,17},{1... | collective-permute-start | bytes 1179656 | tf_op jit(solution)/shard_map/ppermute | solution.py:33
  83.7 0.1 collective-permute-start.13
  83.8 6.9 %collective-permute-done.14.refs_8_ = bf16[2,4,64,768]{3,2,1,0:T(8,128)(2,1)} collective-permute-done((bf16[2,4,64,768]{3,2,1,0:T(8,128)(2,1)}, bf16[2,4,64,768]{3,2,1,0:T(8,128)(2,1)}, u32[]{:S(2)}, u32[]{:S(2)}) %collective-permute-start.14) | collective-permute-done | bytes 786464 | tf_op jit(solution)/shard_map/ppermute | solution.py:33
  90.7 8.0 %collective-permute-done.15.refs_9_ = bf16[4,64,768]{2,1,0:T(8,128)(2,1)} collective-permute-done((bf16[4,64,768]{2,1,0:T(8,128)(2,1)}, bf16[4,64,768]{2,1,0:T(8,128)(2,1)}, u32[]{:S(2)}, u32[]{:S(2)}) %collective-permute-start.15) | collective-permute-done | bytes 393248 | tf_op jit(solution)/shard_map/ppermute | solution.py:33
  98.7 8.8 %shard_map.100 = (bf16[256,1536]{1,0:T(8,128)(2,1)}, bf16[256,1536]{1,0:T(8,128)(2,1)}, bf16[256,1536]{1,0:T(8,128)(2,1)}, bf16[256,1536]{1,0:T(8,128)(2,1)}) custom-call(s32[3,4]{1,0:T(4,128)} %pad_add_fusion.refs_0_, ...), custom_call_target="tpu_custom_call", output_to_operand_aliasing={{0}: (10, {}), {1}: (11, {}), {2}: (12, {}), {3}: (13, {})} | custom-call | flops 8999999488 | bytes 1 | tf_op jit(solution)/shard_map/pallas_call | solution.py:325
  (20 shorter events, 0.1 us)
Async XLA Ops:
  3.1 19.8 %collective-permute-start = (bf16[4,64,768]{2,1,0:T(8,128)(2,1)}, bf16[4,64,768]{2,1,0:T(8,128)(2,1)}, u32[]{:S(2)}, u32[]{:S(2)}) collective-permute-start(bf16[4,64,768]{2,1,0:T(8,128)(2,1)} %get-tuple-element.18), channel_id=1, source_target_pairs={{0,2},{1,3},{2,0},{3,1},{4,6},{5,7},{6,4},{7,5},{8,10},{9,11},{10,... | collective-permute-start | bytes 1179656 | tf_op jit(solution)/shard_map/ppermute | solution.py:37
  5.5 21.6 %collective-permute-start.4 = (bf16[4,64,768]{2,1,0:T(8,128)(2,1)}, bf16[4,64,768]{2,1,0:T(8,128)(2,1)}, u32[]{:S(2)}, u32[]{:S(2)}) collective-permute-start(bf16[4,64,768]{2,1,0:T(8,128)(2,1)} %get-tuple-element.21), channel_id=1, source_target_pairs={{0,1},{1,0},{2,3},{3,2},{4,5},{5,4},{6,7},{7,6},{8,9},{9,8},{10,11... | collective-permute-start | bytes 1179656 | tf_op jit(solution)/shard_map/ppermute | solution.py:37
  6.8 22.4 %collective-permute-start.6 = (bf16[4,64,1536]{2,1,0:T(8,128)(2,1)}, bf16[4,64,1536]{2,1,0:T(8,128)(2,1)}, u32[]{:S(2)}, u32[]{:S(2)}) collective-permute-start(bf16[4,64,1536]{2,1,0:T(8,128)(2,1)} %get-tuple-element.15.refs_3_.refs_1_), channel_id=1, source_target_pairs={{4,8},{8,4},{12,16},{16,12},{20,24},{24,20},{5,9},{9,5},{13,17},{1... | collective-permute-start | bytes 2359304 | tf_op jit(solution)/shard_map/ppermute | solution.py:33
  11.0 18.2 %collective-permute-start.5 = (bf16[4,64,1536]{2,1,0:T(8,128)(2,1)}, bf16[4,64,1536]{2,1,0:T(8,128)(2,1)}, u32[]{:S(2)}, u32[]{:S(2)}) collective-permute-start(bf16[4,64,1536]{2,1,0:T(8,128)(2,1)} %get-tuple-element.15.refs_3_.refs_1_), channel_id=1, source_target_pairs={{0,4},{4,0},{8,12},{12,8},{16,20},{20,16},{24,28},{28,24},{1,5},{5... | collective-permute-start | bytes 2359304 | tf_op jit(solution)/shard_map/ppermute | solution.py:33
  22.9 13.2 %collective-permute-start.1 = (bf16[4,64,768]{2,1,0:T(8,128)(2,1)}, bf16[4,64,768]{2,1,0:T(8,128)(2,1)}, u32[]{:S(2)}, u32[]{:S(2)}) collective-permute-start(bf16[4,64,768]{2,1,0:T(8,128)(2,1)} %shard_map.86.refs_2_), channel_id=1, source_target_pairs={{0,3},{1,2},{2,1},{3,0},{4,7},{5,6},{6,5},{7,4},{8,11},{9,10},{10,... | collective-permute-start | bytes 1179656 | tf_op jit(solution)/shard_map/ppermute | solution.py:37
  29.2 23.2 %collective-permute-start.8 = (bf16[2,4,64,768]{3,2,1,0:T(8,128)(2,1)}, bf16[2,4,64,768]{3,2,1,0:T(8,128)(2,1)}, u32[]{:S(2)}, u32[]{:S(2)}) collective-permute-start(bf16[2,4,64,768]{3,2,1,0:T(8,128)(2,1)} %shard_map.91.refs_3_.refs_2_), channel_id=1, source_target_pairs={{4,8},{8,4},{12,16},{16,12},{20,24},{24,20},{5,9},{9,5},{13,17},{1... | collective-permute-start | bytes 2359304 | tf_op jit(solution)/shard_map/ppermute | solution.py:33
  33.1 19.3 %collective-permute-start.7 = (bf16[2,4,64,768]{3,2,1,0:T(8,128)(2,1)}, bf16[2,4,64,768]{3,2,1,0:T(8,128)(2,1)}, u32[]{:S(2)}, u32[]{:S(2)}) collective-permute-start(bf16[2,4,64,768]{3,2,1,0:T(8,128)(2,1)} %shard_map.91.refs_3_.refs_2_), channel_id=1, source_target_pairs={{0,4},{4,0},{8,12},{12,8},{16,20},{20,16},{24,28},{28,24},{1,5},{5... | collective-permute-start | bytes 2359304 | tf_op jit(solution)/shard_map/ppermute | solution.py:33
  36.0 29.7 %collective-permute-start.2 = (bf16[4,64,768]{2,1,0:T(8,128)(2,1)}, bf16[4,64,768]{2,1,0:T(8,128)(2,1)}, u32[]{:S(2)}, u32[]{:S(2)}) collective-permute-start(bf16[4,64,768]{2,1,0:T(8,128)(2,1)} %shard_map.87.refs_1_), channel_id=1, source_target_pairs={{0,1},{1,0},{2,3},{3,2},{4,5},{5,4},{6,7},{7,6},{8,9},{9,8},{10,11... | collective-permute-start | bytes 1179656 | tf_op jit(solution)/shard_map/ppermute | solution.py:37
  43.2 15.9 %collective-permute-start.3 = (bf16[4,64,768]{2,1,0:T(8,128)(2,1)}, bf16[4,64,768]{2,1,0:T(8,128)(2,1)}, u32[]{:S(2)}, u32[]{:S(2)}) collective-permute-start(bf16[4,64,768]{2,1,0:T(8,128)(2,1)} %shard_map.88.refs_2_), channel_id=1, source_target_pairs={{0,2},{1,3},{2,0},{3,1},{4,6},{5,7},{6,4},{7,5},{8,10},{9,11},{10,... | collective-permute-start | bytes 1179656 | tf_op jit(solution)/shard_map/ppermute | solution.py:37
  52.4 13.4 %collective-permute-start.10 = (bf16[4,64,768]{2,1,0:T(8,128)(2,1)}, bf16[4,64,768]{2,1,0:T(8,128)(2,1)}, u32[]{:S(2)}, u32[]{:S(2)}) collective-permute-start(bf16[4,64,768]{2,1,0:T(8,128)(2,1)} %shard_map.93.refs_3_), channel_id=1, source_target_pairs={{4,8},{8,4},{12,16},{16,12},{20,24},{24,20},{5,9},{9,5},{13,17},{1... | collective-permute-start | bytes 1179656 | tf_op jit(solution)/shard_map/ppermute | solution.py:33
  54.9 10.9 %collective-permute-start.9 = (bf16[4,64,768]{2,1,0:T(8,128)(2,1)}, bf16[4,64,768]{2,1,0:T(8,128)(2,1)}, u32[]{:S(2)}, u32[]{:S(2)}) collective-permute-start(bf16[4,64,768]{2,1,0:T(8,128)(2,1)} %shard_map.93.refs_3_), channel_id=1, source_target_pairs={{0,4},{4,0},{8,12},{12,8},{16,20},{20,16},{24,28},{28,24},{1,5},{5... | collective-permute-start | bytes 1179656 | tf_op jit(solution)/shard_map/ppermute | solution.py:33
  67.7 12.3 %collective-permute-start.11 = (bf16[4,64,768]{2,1,0:T(8,128)(2,1)}, bf16[4,64,768]{2,1,0:T(8,128)(2,1)}, u32[]{:S(2)}, u32[]{:S(2)}) collective-permute-start(bf16[4,64,768]{2,1,0:T(8,128)(2,1)} %shard_map.94.refs_2_), channel_id=1, source_target_pairs={{0,3},{1,2},{2,1},{3,0},{4,7},{5,6},{6,5},{7,4},{8,11},{9,10},{10,... | collective-permute-start | bytes 1179656 | tf_op jit(solution)/shard_map/ppermute | solution.py:37
  67.8 22.9 %collective-permute-start.14 = (bf16[2,4,64,768]{3,2,1,0:T(8,128)(2,1)}, bf16[2,4,64,768]{3,2,1,0:T(8,128)(2,1)}, u32[]{:S(2)}, u32[]{:S(2)}) collective-permute-start(bf16[2,4,64,768]{3,2,1,0:T(8,128)(2,1)} %shard_map.96.refs_1_.refs_2_), channel_id=1, source_target_pairs={{4,8},{8,4},{12,16},{16,12},{20,24},{24,20},{5,9},{9,5},{13,17},{1... | collective-permute-start | bytes 2359304 | tf_op jit(solution)/shard_map/ppermute | solution.py:33
  70.9 9.0 %collective-permute-start.12 = (bf16[2,4,64,768]{3,2,1,0:T(8,128)(2,1)}, bf16[2,4,64,768]{3,2,1,0:T(8,128)(2,1)}, u32[]{:S(2)}, u32[]{:S(2)}) collective-permute-start(bf16[2,4,64,768]{3,2,1,0:T(8,128)(2,1)} %shard_map.96.refs_1_.refs_2_), channel_id=1, source_target_pairs={{0,4},{4,0},{8,12},{12,8},{16,20},{20,16},{24,28},{28,24},{1,5},{5... | collective-permute-start | bytes 2359304 | tf_op jit(solution)/shard_map/ppermute | solution.py:33
  80.0 18.7 %collective-permute-start.15 = (bf16[4,64,768]{2,1,0:T(8,128)(2,1)}, bf16[4,64,768]{2,1,0:T(8,128)(2,1)}, u32[]{:S(2)}, u32[]{:S(2)}) collective-permute-start(bf16[4,64,768]{2,1,0:T(8,128)(2,1)} %shard_map.99.refs_3_), channel_id=1, source_target_pairs={{4,8},{8,4},{12,16},{16,12},{20,24},{24,20},{5,9},{9,5},{13,17},{1... | collective-permute-start | bytes 1179656 | tf_op jit(solution)/shard_map/ppermute | solution.py:33
  83.7 15.0 %collective-permute-start.13 = (bf16[4,64,768]{2,1,0:T(8,128)(2,1)}, bf16[4,64,768]{2,1,0:T(8,128)(2,1)}, u32[]{:S(2)}, u32[]{:S(2)}) collective-permute-start(bf16[4,64,768]{2,1,0:T(8,128)(2,1)} %shard_map.99.refs_3_), channel_id=1, source_target_pairs={{0,4},{4,0},{8,12},{12,8},{16,20},{20,16},{24,28},{28,24},{1,5},{5... | collective-permute-start | bytes 1179656 | tf_op jit(solution)/shard_map/ppermute | solution.py:33

commit v25 on v22

--- a/solution.py
+++ b/solution.py
@@ -315,7 +315,8 @@
     _, part_rows, total = groups[0][0].shape
     parts = groups[0][1].shape[0] + 2
     rows = parts * part_rows
-    width = HD * math.gcd(2, math.gcd(first_head, heads))
+    shared = math.gcd(first_head, heads)
+    width = HD * next(count for count in (3, 2, 1) if shared % count == 0)
     steps = heads * HD // width
     first_block = first_head * HD // width
     out_spec = pl.BlockSpec((rows, width), lambda s: (0, s + first_block))

time: 108 us -> 108 us (level)
  no operation moved by 1% of the time
where the time goes in v25:
time: 108 us; the launch traced here: 107 us
  waiting for transfers between devices  46.3 us (43%)
  starting transfers between devices  32.7 us (30%)
  Pallas kernels  25.9 us (24%)
    ppermute x10, waiting for transfers between devices, swap_pairs(): return lax.ppermute(block, axis, route)  31.2 us
    ppermute x10, starting transfers between devices, swap_pairs(): return lax.ppermute(block, axis, route)  17.6 us
    pallas_call x2, Pallas kernels, attend(): pl.pallas_call(functools.partial(attend_kernel, parts, part_rows, steps,...  17.2 us
    ppermute x6, starting transfers between devices, swap_flipped(): lax.ppermute(block, axis, [(i, i ^ flip) for i in range(lax.axis_size(axi...  15.1 us
    ppermute x6, waiting for transfers between devices, swap_flipped(): lax.ppermute(block, axis, [(i, i ^ flip) for i in range(lax.axis_size(axi...  15.1 us
    pallas_call x2, Pallas kernels, pack(): pl.pallas_call(functools.partial(pack_kernel, stride, jobs), out_shape=[j...  4.88 us
    pallas_call x2, Pallas kernels, join(): pl.pallas_call(functools.partial(join_kernel, pieces), out_shape=jax.Shap...  3.88 us
  transfers between devices with their start and end apart: 16, of which 9 were waited for; matrix products, arithmetic and copies ran while one was open for 1% of the time, Pallas kernels for 12%

profile of v25, /device:TPU:3, one launch (start us, length us, event | category | flops | bytes accessed | tf_op | source)
XLA Modules:
  0.0 107.4 jit_solution(14404846066021129959)
XLA Ops:
  0.6 2.5 %shard_map.84 = (bf16[4,64,768]{2,1,0:T(8,128)(2,1)}, bf16[4,64,768]{2,1,0:T(8,128)(2,1)}, bf16[4,64,1536]{2,1,0:T(8,128)(2,1)}) custom-call(bf16[64,6144]{1,0:T(8,128)(2,1)} %refs_0_.3, bf16[64,6144]{1,0:T(8,128)(2,1)} %refs_1_.3, bf16[64,6144]{1,0:T(8,128)(2,1)} %refs_2_.3, bf16[64,6144]{1,0:T(8,128)(2,1)} %refs_3_.3), custom_call_target="tpu_custom_call" | custom-call | flops 1 | bytes 1 | tf_op jit(solution)/shard_map/pallas_call | solution.py:86
  3.1 2.4 %collective-permute-start = (bf16[4,64,768]{2,1,0:T(8,128)(2,1)}, bf16[4,64,768]{2,1,0:T(8,128)(2,1)}, u32[]{:S(2)}, u32[]{:S(2)}) collective-permute-start(bf16[4,64,768]{2,1,0:T(8,128)(2,1)} %get-tuple-element.18), channel_id=1, source_target_pairs={{0,2},{1,3},{2,0},{3,1},{4,6},{5,7},{6,4},{7,5},{8,10},{9,11},{10,... | collective-permute-start | bytes 1179656 | tf_op jit(solution)/shard_map/ppermute | solution.py:37
  5.5 1.3 %collective-permute-start.4 = (bf16[4,64,768]{2,1,0:T(8,128)(2,1)}, bf16[4,64,768]{2,1,0:T(8,128)(2,1)}, u32[]{:S(2)}, u32[]{:S(2)}) collective-permute-start(bf16[4,64,768]{2,1,0:T(8,128)(2,1)} %get-tuple-element.21), channel_id=1, source_target_pairs={{0,1},{1,0},{2,3},{3,2},{4,5},{5,4},{6,7},{7,6},{8,9},{9,8},{10,11... | collective-permute-start | bytes 1179656 | tf_op jit(solution)/shard_map/ppermute | solution.py:37
  6.8 4.2 %collective-permute-start.6 = (bf16[4,64,1536]{2,1,0:T(8,128)(2,1)}, bf16[4,64,1536]{2,1,0:T(8,128)(2,1)}, u32[]{:S(2)}, u32[]{:S(2)}) collective-permute-start(bf16[4,64,1536]{2,1,0:T(8,128)(2,1)} %get-tuple-element.15.refs_3_.refs_1_), channel_id=1, source_target_pairs={{4,8},{8,4},{12,16},{16,12},{20,24},{24,20},{5,9},{9,5},{13,17},{1... | collective-permute-start | bytes 2359304 | tf_op jit(solution)/shard_map/ppermute | solution.py:33
  11.0 0.1 collective-permute-start.5
  11.1 2.4 %shard_map.85 = (bf16[4,64,768]{2,1,0:T(8,128)(2,1)}, bf16[4,64,768]{2,1,0:T(8,128)(2,1)}, bf16[4,64,768]{2,1,0:T(8,128)(2,1)}, bf16[4,64,768]{2,1,0:T(8,128)(2,1)}) custom-call(bf16[64,6144]{1,0:T(8,128)(2,1)} %refs_0_.3, bf16[64,6144]{1,0:T(8,128)(2,1)} %refs_1_.3, bf16[64,6144]{1,0:T(8,128)(2,1)} %refs_2_.3, bf16[64,6144]{1,0:T(8,128)(2,1)} %refs_3_.3), custom_call_target="tpu_custom_call" | custom-call | flops 1 | bytes 1 | tf_op jit(solution)/shard_map/pallas_call | solution.py:86
  13.5 0.8 slice.3
  14.3 0.1 dynamic-slice_bitcast_fusion.2
  14.4 0.6 pad_add_fusion.refs_0_
  15.1 7.8 %collective-permute-done.refs_1_ = bf16[4,64,768]{2,1,0:T(8,128)(2,1)} collective-permute-done((bf16[4,64,768]{2,1,0:T(8,128)(2,1)}, bf16[4,64,768]{2,1,0:T(8,128)(2,1)}, u32[]{:S(2)}, u32[]{:S(2)}) %collective-permute-start) | collective-permute-done | bytes 393248 | tf_op jit(solution)/shard_map/ppermute | solution.py:37
  22.9 4.2 %collective-permute-start.1 = (bf16[4,64,768]{2,1,0:T(8,128)(2,1)}, bf16[4,64,768]{2,1,0:T(8,128)(2,1)}, u32[]{:S(2)}, u32[]{:S(2)}) collective-permute-start(bf16[4,64,768]{2,1,0:T(8,128)(2,1)} %shard_map.86.refs_2_), channel_id=1, source_target_pairs={{0,3},{1,2},{2,1},{3,0},{4,7},{5,6},{6,5},{7,4},{8,11},{9,10},{10,... | collective-permute-start | bytes 1179656 | tf_op jit(solution)/shard_map/ppermute | solution.py:37
  27.1 2.0 %shard_map.90.refs_0_ = bf16[2,4,64,768]{3,2,1,0:T(8,128)(2,1)} custom-call(bf16[4,64,768]{2,1,0:T(8,128)(2,1)} %collective-permute-done.4.refs_0_, bf16[4,64,768]{2,1,0:T(8,128)(2,1)} %collective-permute-done.refs_1_, bf16[4,64,768]{2,1,0:T(8,128)(2,1)} %shard_map.86.refs_2_, bf16[4,64,1536]{2,1,0:T(8,128)(2,1)} %get-tuple-element.15.refs_3_.refs_1_), custom_call_target="tpu_custom_call" | custom-call | flops 30670848000 | bytes 1 | tf_op jit(solution)/shard_map/pallas_call | solution.py:122
  29.0 0.1 collective-permute-done.6.refs_2_.refs_7_
  29.2 3.9 %collective-permute-start.8 = (bf16[2,4,64,768]{3,2,1,0:T(8,128)(2,1)}, bf16[2,4,64,768]{3,2,1,0:T(8,128)(2,1)}, u32[]{:S(2)}, u32[]{:S(2)}) collective-permute-start(bf16[2,4,64,768]{3,2,1,0:T(8,128)(2,1)} %shard_map.91.refs_3_.refs_2_), channel_id=1, source_target_pairs={{4,8},{8,4},{12,16},{16,12},{20,24},{24,20},{5,9},{9,5},{13,17},{1... | collective-permute-start | bytes 2359304 | tf_op jit(solution)/shard_map/ppermute | solution.py:33
  33.1 0.1 collective-permute-start.7
  33.2 2.9 %collective-permute-done.1.refs_1_.refs_0_ = bf16[4,64,768]{2,1,0:T(8,128)(2,1)} collective-permute-done((bf16[4,64,768]{2,1,0:T(8,128)(2,1)}, bf16[4,64,768]{2,1,0:T(8,128)(2,1)}, u32[]{:S(2)}, u32[]{:S(2)}) %collective-permute-start.1) | collective-permute-done | bytes 393248 | tf_op jit(solution)/shard_map/ppermute | solution.py:37
  36.0 7.2 %collective-permute-start.2 = (bf16[4,64,768]{2,1,0:T(8,128)(2,1)}, bf16[4,64,768]{2,1,0:T(8,128)(2,1)}, u32[]{:S(2)}, u32[]{:S(2)}) collective-permute-start(bf16[4,64,768]{2,1,0:T(8,128)(2,1)} %shard_map.87.refs_1_), channel_id=1, source_target_pairs={{0,1},{1,0},{2,3},{3,2},{4,5},{5,4},{6,7},{7,6},{8,9},{9,8},{10,11... | collective-permute-start | bytes 1179656 | tf_op jit(solution)/shard_map/ppermute | solution.py:37
  43.2 9.2 %collective-permute-done.8.refs_2_.refs_8_ = bf16[2,4,64,768]{3,2,1,0:T(8,128)(2,1)} collective-permute-done((bf16[2,4,64,768]{3,2,1,0:T(8,128)(2,1)}, bf16[2,4,64,768]{3,2,1,0:T(8,128)(2,1)}, u32[]{:S(2)}, u32[]{:S(2)}) %collective-permute-start.8) | collective-permute-done | bytes 786464 | tf_op jit(solution)/shard_map/ppermute | solution.py:33
  52.4 2.5 %collective-permute-start.10 = (bf16[4,64,768]{2,1,0:T(8,128)(2,1)}, bf16[4,64,768]{2,1,0:T(8,128)(2,1)}, u32[]{:S(2)}, u32[]{:S(2)}) collective-permute-start(bf16[4,64,768]{2,1,0:T(8,128)(2,1)} %shard_map.93.refs_3_), channel_id=1, source_target_pairs={{4,8},{8,4},{12,16},{16,12},{20,24},{24,20},{5,9},{9,5},{13,17},{1... | collective-permute-start | bytes 1179656 | tf_op jit(solution)/shard_map/ppermute | solution.py:33
  54.9 0.1 collective-permute-start.9
  55.0 4.1 %collective-permute-done.3.refs_1_ = bf16[4,64,768]{2,1,0:T(8,128)(2,1)} collective-permute-done((bf16[4,64,768]{2,1,0:T(8,128)(2,1)}, bf16[4,64,768]{2,1,0:T(8,128)(2,1)}, u32[]{:S(2)}, u32[]{:S(2)}) %collective-permute-start.3) | collective-permute-done | bytes 393248 | tf_op jit(solution)/shard_map/ppermute | solution.py:37
  59.1 6.7 %collective-permute-done.10.refs_2_.refs_9_ = bf16[4,64,768]{2,1,0:T(8,128)(2,1)} collective-permute-done((bf16[4,64,768]{2,1,0:T(8,128)(2,1)}, bf16[4,64,768]{2,1,0:T(8,128)(2,1)}, u32[]{:S(2)}, u32[]{:S(2)}) %collective-permute-start.10) | collective-permute-done | bytes 393248 | tf_op jit(solution)/shard_map/ppermute | solution.py:33
  65.8 1.9 %shard_map.95.refs_0_ = bf16[2,4,64,768]{3,2,1,0:T(8,128)(2,1)} custom-call(bf16[4,64,768]{2,1,0:T(8,128)(2,1)} %collective-permute-done.2.refs_0_, bf16[4,64,768]{2,1,0:T(8,128)(2,1)} %collective-permute-done.3.refs_1_, bf16[4,64,768]{2,1,0:T(8,128)(2,1)} %shard_map.94.refs_2_, bf16[4,64,768]{2,1,0:T(8,128)(2,1)} %shard_map.93.refs_3_), custom_call_target="tpu_custom_call" | custom-call | flops 10223616000 | bytes 1 | tf_op jit(solution)/shard_map/pallas_call | solution.py:122
  67.7 0.1 collective-permute-start.11
  67.8 3.1 %collective-permute-start.14 = (bf16[2,4,64,768]{3,2,1,0:T(8,128)(2,1)}, bf16[2,4,64,768]{3,2,1,0:T(8,128)(2,1)}, u32[]{:S(2)}, u32[]{:S(2)}) collective-permute-start(bf16[2,4,64,768]{3,2,1,0:T(8,128)(2,1)} %shard_map.96.refs_1_.refs_2_), channel_id=1, source_target_pairs={{4,8},{8,4},{12,16},{16,12},{20,24},{24,20},{5,9},{9,5},{13,17},{1... | collective-permute-start | bytes 2359304 | tf_op jit(solution)/shard_map/ppermute | solution.py:33
  70.9 0.1 collective-permute-start.12
  71.0 8.6 %shard_map.98 = (bf16[256,1536]{1,0:T(8,128)(2,1)}, bf16[256,1536]{1,0:T(8,128)(2,1)}, bf16[256,1536]{1,0:T(8,128)(2,1)}, bf16[256,1536]{1,0:T(8,128)(2,1)}) custom-call(s32[3,4]{1,0:T(4,128)} %pad_add_fusion.refs_0_, bf16[4,64,1536]{2,1,0:T(8,128)(2,1)} %get-tuple-element.15.refs_3_.refs_1_, bf16[2,4,64,768]{3,2,1,0:T(8,128)(2,1)} %shard_map.91.refs_3_.refs_2_, ...), custom_call_target="tpu_custom_call" | custom-call | flops 8999999488 | bytes 1 | tf_op jit(solution)/shard_map/pallas_call | solution.py:326
  79.6 0.3 collective-permute-done.11.refs_0_
  80.0 3.5 %collective-permute-start.15 = (bf16[4,64,768]{2,1,0:T(8,128)(2,1)}, bf16[4,64,768]{2,1,0:T(8,128)(2,1)}, u32[]{:S(2)}, u32[]{:S(2)}) collective-permute-start(bf16[4,64,768]{2,1,0:T(8,128)(2,1)} %shard_map.99.refs_3_), channel_id=1, source_target_pairs={{4,8},{8,4},{12,16},{16,12},{20,24},{24,20},{5,9},{9,5},{13,17},{1... | collective-permute-start | bytes 1179656 | tf_op jit(solution)/shard_map/ppermute | solution.py:33
  83.5 7.1 %collective-permute-done.14.refs_8_ = bf16[2,4,64,768]{3,2,1,0:T(8,128)(2,1)} collective-permute-done((bf16[2,4,64,768]{3,2,1,0:T(8,128)(2,1)}, bf16[2,4,64,768]{3,2,1,0:T(8,128)(2,1)}, u32[]{:S(2)}, u32[]{:S(2)}) %collective-permute-start.14) | collective-permute-done | bytes 786464 | tf_op jit(solution)/shard_map/ppermute | solution.py:33
  90.7 8.0 %collective-permute-done.15.refs_9_ = bf16[4,64,768]{2,1,0:T(8,128)(2,1)} collective-permute-done((bf16[4,64,768]{2,1,0:T(8,128)(2,1)}, bf16[4,64,768]{2,1,0:T(8,128)(2,1)}, u32[]{:S(2)}, u32[]{:S(2)}) %collective-permute-start.15) | collective-permute-done | bytes 393248 | tf_op jit(solution)/shard_map/ppermute | solution.py:33
  98.7 8.6 %shard_map.100 = (bf16[256,1536]{1,0:T(8,128)(2,1)}, bf16[256,1536]{1,0:T(8,128)(2,1)}, bf16[256,1536]{1,0:T(8,128)(2,1)}, bf16[256,1536]{1,0:T(8,128)(2,1)}) custom-call(s32[3,4]{1,0:T(4,128)} %pad_add_fusion.refs_0_, ...), custom_call_target="tpu_custom_call", output_to_operand_aliasing={{0}: (10, {}), {1}: (11, {}), {2}: (12, {}), {3}: (13, {})} | custom-call | flops 8999999488 | bytes 1 | tf_op jit(solution)/shard_map/pallas_call | solution.py:326
  (20 shorter events, 0.1 us)
Async XLA Ops:
  3.1 19.8 %collective-permute-start = (bf16[4,64,768]{2,1,0:T(8,128)(2,1)}, bf16[4,64,768]{2,1,0:T(8,128)(2,1)}, u32[]{:S(2)}, u32[]{:S(2)}) collective-permute-start(bf16[4,64,768]{2,1,0:T(8,128)(2,1)} %get-tuple-element.18), channel_id=1, source_target_pairs={{0,2},{1,3},{2,0},{3,1},{4,6},{5,7},{6,4},{7,5},{8,10},{9,11},{10,... | collective-permute-start | bytes 1179656 | tf_op jit(solution)/shard_map/ppermute | solution.py:37
  5.5 21.6 %collective-permute-start.4 = (bf16[4,64,768]{2,1,0:T(8,128)(2,1)}, bf16[4,64,768]{2,1,0:T(8,128)(2,1)}, u32[]{:S(2)}, u32[]{:S(2)}) collective-permute-start(bf16[4,64,768]{2,1,0:T(8,128)(2,1)} %get-tuple-element.21), channel_id=1, source_target_pairs={{0,1},{1,0},{2,3},{3,2},{4,5},{5,4},{6,7},{7,6},{8,9},{9,8},{10,11... | collective-permute-start | bytes 1179656 | tf_op jit(solution)/shard_map/ppermute | solution.py:37
  6.8 22.4 %collective-permute-start.6 = (bf16[4,64,1536]{2,1,0:T(8,128)(2,1)}, bf16[4,64,1536]{2,1,0:T(8,128)(2,1)}, u32[]{:S(2)}, u32[]{:S(2)}) collective-permute-start(bf16[4,64,1536]{2,1,0:T(8,128)(2,1)} %get-tuple-element.15.refs_3_.refs_1_), channel_id=1, source_target_pairs={{4,8},{8,4},{12,16},{16,12},{20,24},{24,20},{5,9},{9,5},{13,17},{1... | collective-permute-start | bytes 2359304 | tf_op jit(solution)/shard_map/ppermute | solution.py:33
  11.0 18.2 %collective-permute-start.5 = (bf16[4,64,1536]{2,1,0:T(8,128)(2,1)}, bf16[4,64,1536]{2,1,0:T(8,128)(2,1)}, u32[]{:S(2)}, u32[]{:S(2)}) collective-permute-start(bf16[4,64,1536]{2,1,0:T(8,128)(2,1)} %get-tuple-element.15.refs_3_.refs_1_), channel_id=1, source_target_pairs={{0,4},{4,0},{8,12},{12,8},{16,20},{20,16},{24,28},{28,24},{1,5},{5... | collective-permute-start | bytes 2359304 | tf_op jit(solution)/shard_map/ppermute | solution.py:33
  22.9 13.2 %collective-permute-start.1 = (bf16[4,64,768]{2,1,0:T(8,128)(2,1)}, bf16[4,64,768]{2,1,0:T(8,128)(2,1)}, u32[]{:S(2)}, u32[]{:S(2)}) collective-permute-start(bf16[4,64,768]{2,1,0:T(8,128)(2,1)} %shard_map.86.refs_2_), channel_id=1, source_target_pairs={{0,3},{1,2},{2,1},{3,0},{4,7},{5,6},{6,5},{7,4},{8,11},{9,10},{10,... | collective-permute-start | bytes 1179656 | tf_op jit(solution)/shard_map/ppermute | solution.py:37
  29.2 23.2 %collective-permute-start.8 = (bf16[2,4,64,768]{3,2,1,0:T(8,128)(2,1)}, bf16[2,4,64,768]{3,2,1,0:T(8,128)(2,1)}, u32[]{:S(2)}, u32[]{:S(2)}) collective-permute-start(bf16[2,4,64,768]{3,2,1,0:T(8,128)(2,1)} %shard_map.91.refs_3_.refs_2_), channel_id=1, source_target_pairs={{4,8},{8,4},{12,16},{16,12},{20,24},{24,20},{5,9},{9,5},{13,17},{1... | collective-permute-start | bytes 2359304 | tf_op jit(solution)/shard_map/ppermute | solution.py:33
  33.1 19.3 %collective-permute-start.7 = (bf16[2,4,64,768]{3,2,1,0:T(8,128)(2,1)}, bf16[2,4,64,768]{3,2,1,0:T(8,128)(2,1)}, u32[]{:S(2)}, u32[]{:S(2)}) collective-permute-start(bf16[2,4,64,768]{3,2,1,0:T(8,128)(2,1)} %shard_map.91.refs_3_.refs_2_), channel_id=1, source_target_pairs={{0,4},{4,0},{8,12},{12,8},{16,20},{20,16},{24,28},{28,24},{1,5},{5... | collective-permute-start | bytes 2359304 | tf_op jit(solution)/shard_map/ppermute | solution.py:33
  36.0 29.7 %collective-permute-start.2 = (bf16[4,64,768]{2,1,0:T(8,128)(2,1)}, bf16[4,64,768]{2,1,0:T(8,128)(2,1)}, u32[]{:S(2)}, u32[]{:S(2)}) collective-permute-start(bf16[4,64,768]{2,1,0:T(8,128)(2,1)} %shard_map.87.refs_1_), channel_id=1, source_target_pairs={{0,1},{1,0},{2,3},{3,2},{4,5},{5,4},{6,7},{7,6},{8,9},{9,8},{10,11... | collective-permute-start | bytes 1179656 | tf_op jit(solution)/shard_map/ppermute | solution.py:37
  43.2 15.9 %collective-permute-start.3 = (bf16[4,64,768]{2,1,0:T(8,128)(2,1)}, bf16[4,64,768]{2,1,0:T(8,128)(2,1)}, u32[]{:S(2)}, u32[]{:S(2)}) collective-permute-start(bf16[4,64,768]{2,1,0:T(8,128)(2,1)} %shard_map.88.refs_2_), channel_id=1, source_target_pairs={{0,2},{1,3},{2,0},{3,1},{4,6},{5,7},{6,4},{7,5},{8,10},{9,11},{10,... | collective-permute-start | bytes 1179656 | tf_op jit(solution)/shard_map/ppermute | solution.py:37
  52.4 13.4 %collective-permute-start.10 = (bf16[4,64,768]{2,1,0:T(8,128)(2,1)}, bf16[4,64,768]{2,1,0:T(8,128)(2,1)}, u32[]{:S(2)}, u32[]{:S(2)}) collective-permute-start(bf16[4,64,768]{2,1,0:T(8,128)(2,1)} %shard_map.93.refs_3_), channel_id=1, source_target_pairs={{4,8},{8,4},{12,16},{16,12},{20,24},{24,20},{5,9},{9,5},{13,17},{1... | collective-permute-start | bytes 1179656 | tf_op jit(solution)/shard_map/ppermute | solution.py:33
  54.9 10.9 %collective-permute-start.9 = (bf16[4,64,768]{2,1,0:T(8,128)(2,1)}, bf16[4,64,768]{2,1,0:T(8,128)(2,1)}, u32[]{:S(2)}, u32[]{:S(2)}) collective-permute-start(bf16[4,64,768]{2,1,0:T(8,128)(2,1)} %shard_map.93.refs_3_), channel_id=1, source_target_pairs={{0,4},{4,0},{8,12},{12,8},{16,20},{20,16},{24,28},{28,24},{1,5},{5... | collective-permute-start | bytes 1179656 | tf_op jit(solution)/shard_map/ppermute | solution.py:33
  67.7 12.3 %collective-permute-start.11 = (bf16[4,64,768]{2,1,0:T(8,128)(2,1)}, bf16[4,64,768]{2,1,0:T(8,128)(2,1)}, u32[]{:S(2)}, u32[]{:S(2)}) collective-permute-start(bf16[4,64,768]{2,1,0:T(8,128)(2,1)} %shard_map.94.refs_2_), channel_id=1, source_target_pairs={{0,3},{1,2},{2,1},{3,0},{4,7},{5,6},{6,5},{7,4},{8,11},{9,10},{10,... | collective-permute-start | bytes 1179656 | tf_op jit(solution)/shard_map/ppermute | solution.py:37
  67.8 22.9 %collective-permute-start.14 = (bf16[2,4,64,768]{3,2,1,0:T(8,128)(2,1)}, bf16[2,4,64,768]{3,2,1,0:T(8,128)(2,1)}, u32[]{:S(2)}, u32[]{:S(2)}) collective-permute-start(bf16[2,4,64,768]{3,2,1,0:T(8,128)(2,1)} %shard_map.96.refs_1_.refs_2_), channel_id=1, source_target_pairs={{4,8},{8,4},{12,16},{16,12},{20,24},{24,20},{5,9},{9,5},{13,17},{1... | collective-permute-start | bytes 2359304 | tf_op jit(solution)/shard_map/ppermute | solution.py:33
  70.9 9.0 %collective-permute-start.12 = (bf16[2,4,64,768]{3,2,1,0:T(8,128)(2,1)}, bf16[2,4,64,768]{3,2,1,0:T(8,128)(2,1)}, u32[]{:S(2)}, u32[]{:S(2)}) collective-permute-start(bf16[2,4,64,768]{3,2,1,0:T(8,128)(2,1)} %shard_map.96.refs_1_.refs_2_), channel_id=1, source_target_pairs={{0,4},{4,0},{8,12},{12,8},{16,20},{20,16},{24,28},{28,24},{1,5},{5... | collective-permute-start | bytes 2359304 | tf_op jit(solution)/shard_map/ppermute | solution.py:33
  80.0 18.7 %collective-permute-start.15 = (bf16[4,64,768]{2,1,0:T(8,128)(2,1)}, bf16[4,64,768]{2,1,0:T(8,128)(2,1)}, u32[]{:S(2)}, u32[]{:S(2)}) collective-permute-start(bf16[4,64,768]{2,1,0:T(8,128)(2,1)} %shard_map.99.refs_3_), channel_id=1, source_target_pairs={{4,8},{8,4},{12,16},{16,12},{20,24},{24,20},{5,9},{9,5},{13,17},{1... | collective-permute-start | bytes 1179656 | tf_op jit(solution)/shard_map/ppermute | solution.py:33
  83.5 15.2 %collective-permute-start.13 = (bf16[4,64,768]{2,1,0:T(8,128)(2,1)}, bf16[4,64,768]{2,1,0:T(8,128)(2,1)}, u32[]{:S(2)}, u32[]{:S(2)}) collective-permute-start(bf16[4,64,768]{2,1,0:T(8,128)(2,1)} %shard_map.99.refs_3_), channel_id=1, source_target_pairs={{0,4},{4,0},{8,12},{12,8},{16,20},{20,16},{24,28},{28,24},{1,5},{5... | collective-permute-start | bytes 1179656 | tf_op jit(solution)/shard_map/ppermute | solution.py:33
